TPU v7x, 32 devices: a whole 2x2x4 slice. The times are simulated.
32 devices in a mesh: ctx: 8 (over z, y), mp: 4 (over x, core).
Axes of the slice: x: 2, y: 2, z: 4, core: 2. Of those that a mesh axis runs over, the one named last changes fastest.
Arguments:
- projected: bfloat16 [1024, 3, 8192], P('ctx', None, 'mp'), may hold values from -6 to 6
- short_weight: float32 [3, 3, 8192], P(None, None, 'mp'), may hold values from -3 to 3
- filter_taps: float32 [64, 512], P('mp'), may hold values from -1 to 1
- tap_blocks: int32 [64, 4], P('mp'), may hold values 0 or 1
- skip_bias: float32 [8192], P('mp'), may hold values from -3 to 3
- norm_gain: float32 [8192], P('mp'), may hold values from 0.1 to 1.9
- seq_lengths: int32 [32], replicated, may hold values from 1 to 512, 1024 in all
Outputs:
- output: bfloat16 [1024, 8192], P('ctx', 'mp')
Inputs may be any that keep to these rules, and one draw needn't show every extreme that they name: `seq_lengths`: sum to 1024; the longest is exactly 512.
All inputs are finite; a program needn't handle non-finite values. No bound on the sum of `tap_blocks` on one device may be relied on, other than what follows from the above.
Results may differ from a plain program's by a relative error of at most 0.0075.
Values may be sent and summed in bfloat16 or wider, within the bound.
No kernel may reach another device: no remote copies, remote signals or barrier semaphores. Data moves between devices by JAX's collectives and lax.ppermute only.
A program may use at most 64 MiB of HBM per device.

v0:
```python
import functools

import jax
import jax.numpy as jnp
from jax import lax
from jax.experimental import pallas as pl
from jax.experimental.pallas import tpu as pltpu
from jax.sharding import Mesh, PartitionSpec as P

GROUP = 128
BLK = 128
norm_eps = 1e-06

VMEM = pl.BlockSpec(memory_space=pltpu.VMEM)
SMEM = pl.BlockSpec(memory_space=pltpu.SMEM)
SPOTS = ("blk", "half")


def moved(block, pairs):
    return lax.ppermute(block, SPOTS, pairs)


def boundaries(seq_ref, t):
    def step(k, carry):
        end, first, second = carry
        end = end + seq_ref[k]
        return end, first | (t == end).astype(jnp.int32), second | (t - 1 == end).astype(jnp.int32)

    first = (t == 0).astype(jnp.int32)
    second = (t == 1).astype(jnp.int32)
    _, first, second = lax.fori_loop(0, seq_ref.shape[0], step, (jnp.int32(0), first, second))
    return first, second


def counted(seq_ref, t):
    def step(k, carry):
        end, total = carry
        end = end + seq_ref[k]
        return end, total + (end <= t).astype(jnp.int32)

    _, total = lax.fori_loop(
        0, seq_ref.shape[0], step, (jnp.int32(0), jnp.zeros(t.shape, jnp.int32))
    )
    return jnp.where(t >= 0, total, -1)


def products_kernel(
    seq_ref, proj_ref, edge_ref, w_ref, sent_ref, kept_ref, qsent_ref, qkept_ref, x_ref, m1_ref, m2_ref
):
    rows = proj_ref.shape[1]
    width = sent_ref.shape[1]
    half = lax.axis_index("half")
    shard = lax.axis_index("blk") * 2 + half
    t = shard * rows + lax.broadcasted_iota(jnp.int32, (rows, GROUP), 0)
    first, second = boundaries(seq_ref, t)
    m1_ref[...] = 1.0 - first.astype(jnp.float32)
    m2_ref[...] = 1.0 - (first | second).astype(jnp.float32)

    def feature(panel, lanes):
        x = proj_ref[panel, :, lanes].astype(jnp.float32)
        x_ref[panel, 6:8, :] = edge_ref[panel, :, lanes].astype(jnp.float32)
        x_ref[panel, 8:, :] = x
        w = w_ref[panel, :, lanes]
        return (
            w[0:1] * x
            + w[1:2] * x_ref[panel, 7 : rows + 7, :] * m1_ref[...]
            + w[2:3] * x_ref[panel, 6 : rows + 6, :] * m2_ref[...]
        )

    def chunk(c, _):
        there = pl.ds(pl.multiple_of(c * GROUP, GROUP), GROUP)
        for which, p_ref, q_ref in ((1 - half, sent_ref, qsent_ref), (half, kept_ref, qkept_ref)):
            lanes = pl.ds(pl.multiple_of(which * width + c * GROUP, GROUP), GROUP)
            product = feature(1, lanes) * feature(2, lanes)
            p_ref[:, there] = product.astype(p_ref.dtype)
            q_ref[:, there] = feature(0, lanes).astype(q_ref.dtype)
        return 0

    lax.fori_loop(0, width // GROUP, chunk, 0)


def tables_kernel(seq_ref, taps_ref, out_ref, rev_ref, m_ref):
    groups = out_ref.shape[0]
    taps = taps_ref.shape[1]
    span = rev_ref.shape[1]
    width = out_ref.shape[3]
    half = lax.axis_index("half")
    start = lax.axis_index("blk") * (2 * BLK)
    turn = lax.broadcasted_iota(jnp.int32, (taps, span), 0) + lax.broadcasted_iota(
        jnp.int32, (taps, span), 1
    )
    turn = (turn == taps).astype(jnp.bfloat16)
    rev_ref[...] = jnp.dot(taps_ref[...], turn, preferred_element_type=jnp.float32)
    for part in range(2):
        t_in = start - taps + part * BLK + lax.broadcasted_iota(jnp.int32, (8, width), 1)
        t_out = start + part * BLK + lax.broadcasted_iota(jnp.int32, (BLK, GROUP), 0)
        seg_in = counted(seq_ref, t_in)[0:1]
        seg_out = counted(seq_ref, t_out)[:, 0:1]
        m_ref[part] = (seg_in == seg_out).astype(jnp.float32)

    def one(g, _):
        row = rev_ref[pl.ds(half * groups + g, 1), :]
        table = pltpu.roll(
            jnp.broadcast_to(row, (BLK, span)), 0, 1, stride=1, stride_axis=0
        )[:, :width]
        for part in range(2):
            out_ref[g, part] = (table * m_ref[part]).astype(out_ref.dtype)
        return 0

    lax.fori_loop(0, groups, one, 0)


def near_kernel(table_ref, own_ref, pair_ref, back_own_ref, back_pair_ref, bias_ref, acc_ref, win_ref):
    groups = table_ref.shape[0]
    half = lax.axis_index("half")
    own = pl.multiple_of(half * BLK, BLK)
    pair = pl.multiple_of((1 - half) * BLK, BLK)
    win_ref[pl.ds(own, BLK), :] = back_own_ref[...]
    win_ref[pl.ds(pair, BLK), :] = back_pair_ref[...]
    win_ref[pl.ds(2 * BLK + own, BLK), :] = own_ref[...]
    win_ref[pl.ds(2 * BLK + pair, BLK), :] = pair_ref[...]
    for g in range(groups):
        lanes = slice(g * GROUP, (g + 1) * GROUP)
        bias = bias_ref[:, pl.ds(pl.multiple_of(half * groups * GROUP + g * GROUP, GROUP), GROUP)]
        for part in range(2):
            total = jnp.dot(
                table_ref[g, part, :, (2 - part) * BLK :],
                win_ref[: (3 + part) * BLK, lanes],
                preferred_element_type=jnp.float32,
            )
            here = win_ref[(2 + part) * BLK : (3 + part) * BLK, lanes].astype(jnp.float32)
            acc_ref[part * BLK : (part + 1) * BLK, lanes] = total + bias * here


def far_kernel(
    table_ref, acc_ref, far_own_ref, far_pair_ref, qkept_ref, qgot_ref, kept_ref, sent_ref, power_ref, win_ref, sq_ref
):
    groups = table_ref.shape[0]
    half = lax.axis_index("half")
    own = pl.multiple_of(half * BLK, BLK)
    pair = pl.multiple_of((1 - half) * BLK, BLK)
    win_ref[pl.ds(own, BLK), :] = far_own_ref[...]
    win_ref[pl.ds(pair, BLK), :] = far_pair_ref[...]
    for g in range(groups):
        lanes = slice(g * GROUP, (g + 1) * GROUP)
        for part in range(2):
            rows = slice(part * BLK, (part + 1) * BLK)
            acc_ref[rows, lanes] += jnp.dot(
                table_ref[g, part, :, : (2 - part) * BLK],
                win_ref[part * BLK :, lanes],
                preferred_element_type=jnp.float32,
            )
    for spot, q_ref, out_ref in ((own, qkept_ref, kept_ref), (pair, qgot_ref, sent_ref)):
        squares = jnp.zeros((BLK, GROUP), jnp.float32)
        for g in range(groups):
            lanes = slice(g * GROUP, (g + 1) * GROUP)
            gated = q_ref[:, lanes].astype(jnp.float32) * acc_ref[pl.ds(spot, BLK), lanes]
            out_ref[:, lanes] = gated.astype(out_ref.dtype)
            squares = squares + gated * gated
        sq_ref[pl.ds(spot, BLK), :] = squares
    power_ref[...] = lax.dot_general(
        jnp.ones((8, GROUP), jnp.float32),
        sq_ref[...],
        (((1,), (1,)), ((), ())),
        precision=lax.Precision.HIGHEST,
        preferred_element_type=jnp.float32,
    )[0:1]


def norm_kernel(channels, power_ref, kept_ref, got_ref, gain_ref, out_ref):
    half = lax.axis_index("half")
    width = kept_ref.shape[1]
    power = power_ref[:, pl.ds(pl.multiple_of(half * BLK, BLK), BLK)]
    scale = lax.rsqrt(power / channels + norm_eps)
    diagonal = lax.broadcasted_iota(jnp.int32, (BLK, BLK), 0) == lax.broadcasted_iota(
        jnp.int32, (BLK, BLK), 1
    )
    column = jnp.sum(jnp.where(diagonal, scale, 0.0), axis=1, keepdims=True)
    for which, part_ref in ((half, kept_ref), (1 - half, got_ref)):
        for c in range(0, width, GROUP):
            lanes = pl.ds(pl.multiple_of(which * width + c, GROUP), GROUP)
            out_ref[:, lanes] = (
                part_ref[:, c : c + GROUP].astype(jnp.float32) * column * gain_ref[:, lanes]
            ).astype(out_ref.dtype)


def kernel_call(body, outs, in_specs, scratch, flops, moved_bytes):
    return pl.pallas_call(
        body,
        out_shape=outs,
        in_specs=in_specs,
        out_specs=jax.tree.map(lambda _: VMEM, outs),
        scratch_shapes=scratch,
        compiler_params=pltpu.CompilerParams(vmem_limit_bytes=24 << 20),
        cost_estimate=pl.CostEstimate(flops=flops, bytes_accessed=moved_bytes, transcendentals=0),
    )


def shards(blocks, channels, projected, short_weight, filter_taps, tap_blocks, skip_bias, norm_gain, seq_lengths):
    rows = projected.shape[0]
    width = projected.shape[2] // 2
    groups = width // GROUP
    taps = filter_taps.shape[1]
    shape = jax.ShapeDtypeStruct
    half_shape = shape((rows, width), jnp.bfloat16)
    half_wide = shape((rows, width), jnp.float32)

    spots = range(2 * blocks)
    to_next = [(i, i + 1) for i in spots if i + 1 < 2 * blocks]
    to_pair = [(i, i ^ 1) for i in spots]
    ahead = [(i, i + 2) for i in spots if i + 2 < 2 * blocks]
    ahead_pair = [(i, (i ^ 1) + 2) for i in spots if (i ^ 1) + 2 < 2 * blocks]

    panels = jnp.transpose(projected, (1, 0, 2))
    edge = moved(panels[:, rows - 2 :], to_next)

    sent, kept, qsent, qkept = kernel_call(
        products_kernel,
        (half_shape, half_shape, half_shape, half_wide),
        [SMEM, VMEM, VMEM, VMEM],
        [
            pltpu.VMEM((3, rows + 8, GROUP), jnp.float32),
            pltpu.VMEM((rows, GROUP), jnp.float32),
            pltpu.VMEM((rows, GROUP), jnp.float32),
        ],
        60 * rows * width,
        16 * rows * width,
    )(seq_lengths, panels, edge, short_weight)

    pair = moved(sent, to_pair)
    back_own = moved(kept, ahead)
    back_pair = moved(sent, ahead_pair)
    qgot = moved(qsent, to_pair)

    scaled = (filter_taps * jnp.repeat(tap_blocks.astype(jnp.float32), BLK, axis=1)).astype(jnp.bfloat16)
    table = kernel_call(
        tables_kernel,
        shape((groups, 2, BLK, taps + BLK), jnp.bfloat16),
        [SMEM, VMEM],
        [pltpu.VMEM((2 * groups, taps + 2 * BLK), jnp.float32), pltpu.VMEM((2, BLK, taps + BLK), jnp.float32)],
        40 * groups * BLK * taps,
        8 * groups * BLK * taps,
    )(seq_lengths, scaled)

    acc = kernel_call(
        near_kernel,
        shape((2 * rows, width), jnp.float32),
        [VMEM] * 6,
        [pltpu.VMEM((4 * rows, width), jnp.bfloat16)],
        2 * 7 * rows * BLK * width,
        16 * rows * width,
    )(table, kept, pair, back_own, back_pair, skip_bias.reshape(1, -1))

    far_own = moved(back_own, ahead)
    far_pair = moved(back_pair, ahead)
    done, send, power = kernel_call(
        far_kernel,
        (half_wide, half_shape, shape((1, 2 * rows), jnp.float32)),
        [VMEM] * 6,
        [pltpu.VMEM((2 * rows, width), jnp.bfloat16), pltpu.VMEM((2 * rows, GROUP), jnp.float32)],
        2 * 3 * rows * BLK * width,
        24 * rows * width,
    )(table, acc, far_own, far_pair, qkept, qgot)

    back = moved(send, to_pair)
    power = lax.psum(power, ("half", "mp"))
    return kernel_call(
        functools.partial(norm_kernel, channels),
        shape((rows, 2 * width), jnp.bfloat16),
        [VMEM] * 4,
        [],
        8 * rows * width,
        10 * rows * width,
    )(power, done, back, norm_gain.reshape(1, -1))


def solution(mesh):
    blocks = mesh.shape["ctx"] // 2
    grid = Mesh(mesh.devices.reshape(blocks, 2, mesh.shape["mp"]), ("blk", "half", "mp"))
    in_specs = (
        P(SPOTS, None, "mp"),
        P(None, None, "mp"),
        P("mp", None),
        P("mp", None),
        P("mp"),
        P("mp"),
        P(),
    )

    def program(projected, *rest):
        body = functools.partial(shards, blocks, projected.shape[2])
        return jax.shard_map(
            body, mesh=grid, in_specs=in_specs, out_specs=P(SPOTS, "mp"), check_vma=False
        )(projected, *rest)

    return program
```

profile of v0, /device:TPU:0, one launch (start us, length us, event | category | flops | bytes accessed | tf_op | source)
XLA Modules:
  0.0 57.5 jit_solution(11248773661843153144)
XLA Ops:
  0.0 0.0 copy-start.2
  0.0 0.9 %slice.4 = bf16[3,2,2048]{2,1,0:T(2,128)(2,1)S(1)} slice(bf16[3,128,2048]{2,1,0:T(8,128)(2,1)} %bitcast.8), slice={[0:3], [126:128], [0:2048]} | slice | bytes 49152 | tf_op jit(solution)/shard_map/slice | solution.py:215
  0.9 4.9 %collective-permute-start = (bf16[3,2,2048]{2,1,0:T(2,128)(2,1)S(1)}, bf16[3,2,2048]{2,1,0:T(2,128)(2,1)S(1)}, u32[]{:S(2)}, u32[]{:S(2)}) collective-permute-start(bf16[3,2,2048]{2,1,0:T(2,128)(2,1)S(1)} %slice.4), channel_id=1, source_target_pairs={{0,4},{4,8},{8,12},{12,16},{16,20},{20,24},{24,28},{1,5},{5,9},{9,... | collective-permute-start | bytes 73736 | tf_op jit(solution)/shard_map/ppermute | solution.py:20
  5.8 1.5 %collective-permute-done.edge_ref = bf16[3,2,2048]{2,1,0:T(2,128)(2,1)S(1)} collective-permute-done((bf16[3,2,2048]{2,1,0:T(2,128)(2,1)S(1)}, bf16[3,2,2048]{2,1,0:T(2,128)(2,1)S(1)}, u32[]{:S(2)}, u32[]{:S(2)}) %collective-permute-start) | collective-permute-done | bytes 24608 | tf_op jit(solution)/shard_map/ppermute | solution.py:20
  7.3 0.0 copy-start
  7.3 1.4 %copy-done = bf16[128,3,2048]{2,0,1:T(8,128)(2,1)S(1)} copy-done((bf16[128,3,2048]{2,0,1:T(8,128)(2,1)S(1)}, bf16[128,3,2048]{2,0,1:T(8,128)(2,1)}, u32[]{:S(2)}) %copy-start) | copy-done | bytes 1572888
  8.7 0.0 copy-start.1
  8.7 0.9 %copy-done.1 = f32[3,3,2048]{2,1,0:T(4,128)S(1)} copy-done((f32[3,3,2048]{2,1,0:T(4,128)S(1)}, f32[3,3,2048]{2,1,0:T(4,128)}, u32[]{:S(2)}) %copy-start.1) | copy-done | bytes 73752
  9.6 0.0 copy-start.4
  9.6 0.7 %copy-done.4 = s32[32]{0:T(128)S(1)} copy-done((s32[32]{0:T(128)S(1)}, s32[32]{0:T(128)}, u32[]{:S(2)}) %copy-start.4) | copy-done | bytes 152
  10.3 2.9 %shard_map.74 = (bf16[128,1024]{1,0:T(8,128)(2,1)S(1)}, bf16[128,1024]{1,0:T(8,128)(2,1)S(1)}, bf16[128,1024]{1,0:T(8,128)(2,1)S(1)}, f32[128,1024]{1,0:T(8,128)S(1)}) custom-call(s32[32]{0:T(128)S(1)} %copy-done.4, bf16[3,128,2048]{2,1,0:T(8,128)(2,1)S(1)} %bitcast.9, bf16[3,2,2048]{2,1,0:T(2,128)(2,1)S(1)} %collective-permute-done.edge_ref, ...), custom_call_target="tpu_custom_call" | custom-call | flops 7864320 | bytes 2097152 | tf_op jit(solution)/shard_map/pallas_call | solution.py:217
  13.2 5.2 %collective-permute-start.2 = (bf16[128,1024]{1,0:T(8,128)(2,1)S(1)}, bf16[128,1024]{1,0:T(8,128)(2,1)S(1)}, u32[]{:S(2)}, u32[]{:S(2)}) collective-permute-start(bf16[128,1024]{1,0:T(8,128)(2,1)S(1)} %get-tuple-element.12.own_ref), channel_id=1, source_target_pairs={{0,8},{4,12},{8,16},{12,20},{16,24},{20,28},{1,9},{5,13},{9,17},{1... | collective-permute-start | bytes 786440 | tf_op jit(solution)/shard_map/ppermute | solution.py:20
  18.4 3.5 %collective-permute-start.3 = (bf16[128,1024]{1,0:T(8,128)(2,1)S(1)}, bf16[128,1024]{1,0:T(8,128)(2,1)S(1)}, u32[]{:S(2)}, u32[]{:S(2)}) collective-permute-start(bf16[128,1024]{1,0:T(8,128)(2,1)S(1)} %get-tuple-element.13), channel_id=1, source_target_pairs={{0,12},{4,8},{8,20},{12,16},{16,28},{20,24},{1,13},{5,9},{9,21},{1... | collective-permute-start | bytes 786440 | tf_op jit(solution)/shard_map/ppermute | solution.py:20
  21.9 1.5 %collective-permute-start.1 = (bf16[128,1024]{1,0:T(8,128)(2,1)S(1)}, bf16[128,1024]{1,0:T(8,128)(2,1)S(1)}, u32[]{:S(2)}, u32[]{:S(2)}) collective-permute-start(bf16[128,1024]{1,0:T(8,128)(2,1)S(1)} %get-tuple-element.13), channel_id=1, source_target_pairs={{0,4},{4,0},{8,12},{12,8},{16,20},{20,16},{24,28},{28,24},{1,5},{5... | collective-permute-start | bytes 786440 | tf_op jit(solution)/shard_map/ppermute | solution.py:20
  23.4 0.6 %collective-permute-start.6 = (bf16[128,1024]{1,0:T(8,128)(2,1)S(1)}, bf16[128,1024]{1,0:T(8,128)(2,1)S(1)}, u32[]{:S(2)}, u32[]{:S(2)}) collective-permute-start(bf16[128,1024]{1,0:T(8,128)(2,1)S(1)} %get-tuple-element.15), channel_id=1, source_target_pairs={{0,4},{4,0},{8,12},{12,8},{16,20},{20,16},{24,28},{28,24},{1,5},{5... | collective-permute-start | bytes 786440 | tf_op jit(solution)/shard_map/ppermute | solution.py:20
  24.0 1.1 %collective-permute-done.2.back_own_ref = bf16[128,1024]{1,0:T(8,128)(2,1)S(1)} collective-permute-done((bf16[128,1024]{1,0:T(8,128)(2,1)S(1)}, bf16[128,1024]{1,0:T(8,128)(2,1)S(1)}, u32[]{:S(2)}, u32[]{:S(2)}) %collective-permute-start.2) | collective-permute-done | bytes 262176 | tf_op jit(solution)/shard_map/ppermute | solution.py:20
  25.1 4.4 %collective-permute-start.4 = (bf16[128,1024]{1,0:T(8,128)(2,1)S(1)}, bf16[128,1024]{1,0:T(8,128)(2,1)S(1)}, u32[]{:S(2)}, u32[]{:S(2)}) collective-permute-start(bf16[128,1024]{1,0:T(8,128)(2,1)S(1)} %collective-permute-done.2.back_own_ref), channel_id=1, source_target_pairs={{0,8},{4,12},{8,16},{12,20},{16,24},{20,28},{1,9},{5,13},{9,17},{1... | collective-permute-start | bytes 786440 | tf_op jit(solution)/shard_map/ppermute | solution.py:20
  29.5 1.2 %collective-permute-done.3.back_pair_ref = bf16[128,1024]{1,0:T(8,128)(2,1)S(1)} collective-permute-done((bf16[128,1024]{1,0:T(8,128)(2,1)S(1)}, bf16[128,1024]{1,0:T(8,128)(2,1)S(1)}, u32[]{:S(2)}, u32[]{:S(2)}) %collective-permute-start.3) | collective-permute-done | bytes 262176 | tf_op jit(solution)/shard_map/ppermute | solution.py:20
  30.7 3.6 %collective-permute-start.5 = (bf16[128,1024]{1,0:T(8,128)(2,1)S(1)}, bf16[128,1024]{1,0:T(8,128)(2,1)S(1)}, u32[]{:S(2)}, u32[]{:S(2)}) collective-permute-start(bf16[128,1024]{1,0:T(8,128)(2,1)S(1)} %collective-permute-done.3.back_pair_ref), channel_id=1, source_target_pairs={{0,8},{4,12},{8,16},{12,20},{16,24},{20,28},{1,9},{5,13},{9,17},{1... | collective-permute-start | bytes 786440 | tf_op jit(solution)/shard_map/ppermute | solution.py:20
  34.4 0.7 %convert_element_type.6 = f32[16,4]{0,1:T(4,128)S(1)} convert(s32[16,4]{0,1:T(4,128)} %param.10) | non-fusion elementwise | flops 64 | bytes 512 | tf_op jit(solution)/shard_map/convert_element_type | solution.py:235
  35.1 0.1 copy.8
  35.1 0.1 broadcast_in_dim.3
  35.2 0.8 %fusion.taps_ref = bf16[16,512]{1,0:T(8,128)(2,1)S(1)} fusion(f32[16,512]{1,0:T(8,128)} %param.9, f32[2,8,4,128]{3,2,1,0:T(4,128)S(1)} %bitcast.12), kind=kLoop, calls=%fused_computation.1 | loop fusion | flops 16384 | bytes 81920 | tf_op jit(solution)/shard_map/convert_element_type | solution.py:235
  36.0 0.0 copy-start.5
  36.0 0.7 %copy-done.5 = s32[32]{0:T(128)S(1)} copy-done((s32[32]{0:T(128)S(1)}, s32[32]{0:T(128)}, u32[]{:S(2)}) %copy-start.5) | copy-done | bytes 152
  36.7 3.6 %shard_map.73.table_ref = bf16[8,2,128,640]{3,2,1,0:T(8,128)(2,1)S(1)} custom-call(s32[32]{0:T(128)S(1)} %copy-done.5, bf16[16,512]{1,0:T(8,128)(2,1)S(1)} %fusion.taps_ref), custom_call_target="tpu_custom_call" | custom-call | flops 20971520 | bytes 4194304 | tf_op jit(solution)/shard_map/pallas_call | solution.py:236
  40.2 0.0 collective-permute-done.1.pair_ref
  40.2 0.0 copy-done.2
  40.2 0.9 %shard_map.75.acc_ref = f32[256,1024]{1,0:T(8,128)S(1)} custom-call(bf16[8,2,128,640]{3,2,1,0:T(8,128)(2,1)S(1)} %shard_map.73.table_ref, bf16[128,1024]{1,0:T(8,128)(2,1)S(1)} %get-tuple-element.12.own_ref, bf16[128,1024]{1,0:T(8,128)(2,1)S(1)} %collective-permute-done.1.pair_ref, bf16[128,1024]{1,0:T(8,128)(2,1)S(1)} %collective-permute-done.2.back_own_ref, ...), custom_call_target="tpu_custom_call" | custom-call | flops 234881024 | bytes 2097152 | tf_op jit(solution)/shard_map/pallas_call | solution.py:245
  41.1 0.0 copy-start.3
  41.2 0.0 collective-permute-done.6.qgot_ref
  41.2 0.0 collective-permute-done.4.far_own_ref
  41.2 0.0 collective-permute-done.5.far_pair_ref
  41.2 1.1 %shard_map.76 = (f32[128,1024]{1,0:T(8,128)S(1)}, bf16[128,1024]{1,0:T(8,128)(2,1)S(1)}, f32[1,256]{1,0:T(1,128)S(1)}) custom-call(bf16[8,2,128,640]{3,2,1,0:T(8,128)(2,1)S(1)} %shard_map.73.table_ref, f32[256,1024]{1,0:T(8,128)S(1)} %shard_map.75.acc_ref, bf16[128,1024]{1,0:T(8,128)(2,1)S(1)} %collective-permute-done.4.far_own_ref, ...), custom_call_target="tpu_custom_call" | custom-call | flops 100663296 | bytes 3145728 | tf_op jit(solution)/shard_map/pallas_call | solution.py:256
  42.3 2.3 %collective-permute-start.7 = (bf16[128,1024]{1,0:T(8,128)(2,1)S(1)}, bf16[128,1024]{1,0:T(8,128)(2,1)S(1)}, u32[]{:S(2)}, u32[]{:S(2)}) collective-permute-start(bf16[128,1024]{1,0:T(8,128)(2,1)S(1)} %get-tuple-element.18), channel_id=1, source_target_pairs={{0,4},{4,0},{8,12},{12,8},{16,20},{20,16},{24,28},{28,24},{1,5},{5... | collective-permute-start | bytes 786440 | tf_op jit(solution)/shard_map/ppermute | solution.py:20
  44.6 11.9 %psum.7.power_ref = f32[1,256]{1,0:T(1,128)S(1)} all-reduce(f32[1,256]{1,0:T(1,128)S(1)} %get-tuple-element.16), channel_id=1, replica_groups=mesh['blk'=4,'half'=2,'mp'=4] {'half','mp'}, use_global_device_ids=true, to_apply=%region_0.0 | all-reduce | flops 256 | bytes 2048 | tf_op jit(solution)/shard_map/psum | solution.py:266
  56.5 0.0 collective-permute-done.7.got_ref
  56.5 0.0 copy-done.3
  56.5 1.1 %shard_map.77 = bf16[128,2048]{1,0:T(8,128)(2,1)} custom-call(f32[1,256]{1,0:T(1,128)S(1)} %psum.7.power_ref, f32[128,1024]{1,0:T(8,128)S(1)} %get-tuple-element.17.kept_ref, bf16[128,1024]{1,0:T(8,128)(2,1)S(1)} %collective-permute-done.7.got_ref, f32[1,2048]{1,0:T(1,128)S(1)} %bitcast.11), custom_call_target="tpu_custom_call" | custom-call | flops 1048576 | bytes 1310720 | tf_op jit(solution)/shard_map/pallas_call | solution.py:267
Async XLA Ops:
  0.0 40.2 %copy-start.2 = (f32[2048]{0:T(1024)S(1)}, f32[2048]{0:T(1024)}, u32[]{:S(2)}) copy-start(f32[2048]{0:T(1024)} %param.11) | copy-start | bytes 24580
  0.9 6.4 %collective-permute-start = (bf16[3,2,2048]{2,1,0:T(2,128)(2,1)S(1)}, bf16[3,2,2048]{2,1,0:T(2,128)(2,1)S(1)}, u32[]{:S(2)}, u32[]{:S(2)}) collective-permute-start(bf16[3,2,2048]{2,1,0:T(2,128)(2,1)S(1)} %slice.4), channel_id=1, source_target_pairs={{0,4},{4,8},{8,12},{12,16},{16,20},{20,24},{24,28},{1,5},{5,9},{9,... | collective-permute-start | bytes 73736 | tf_op jit(solution)/shard_map/ppermute | solution.py:20
  7.3 1.4 %copy-start = (bf16[128,3,2048]{2,0,1:T(8,128)(2,1)S(1)}, bf16[128,3,2048]{2,0,1:T(8,128)(2,1)}, u32[]{:S(2)}) copy-start(bf16[128,3,2048]{2,0,1:T(8,128)(2,1)} %param.7) | copy-start | bytes 4718596
  8.7 0.9 %copy-start.1 = (f32[3,3,2048]{2,1,0:T(4,128)S(1)}, f32[3,3,2048]{2,1,0:T(4,128)}, u32[]{:S(2)}) copy-start(f32[3,3,2048]{2,1,0:T(4,128)} %w_ref.1) | copy-start | bytes 221188
  9.6 0.7 %copy-start.4 = (s32[32]{0:T(128)S(1)}, s32[32]{0:T(128)}, u32[]{:S(2)}) copy-start(s32[32]{0:T(128)} %seq_ref.3) | copy-start | bytes 388
  13.2 11.9 %collective-permute-start.2 = (bf16[128,1024]{1,0:T(8,128)(2,1)S(1)}, bf16[128,1024]{1,0:T(8,128)(2,1)S(1)}, u32[]{:S(2)}, u32[]{:S(2)}) collective-permute-start(bf16[128,1024]{1,0:T(8,128)(2,1)S(1)} %get-tuple-element.12.own_ref), channel_id=1, source_target_pairs={{0,8},{4,12},{8,16},{12,20},{16,24},{20,28},{1,9},{5,13},{9,17},{1... | collective-permute-start | bytes 786440 | tf_op jit(solution)/shard_map/ppermute | solution.py:20
  18.4 12.3 %collective-permute-start.3 = (bf16[128,1024]{1,0:T(8,128)(2,1)S(1)}, bf16[128,1024]{1,0:T(8,128)(2,1)S(1)}, u32[]{:S(2)}, u32[]{:S(2)}) collective-permute-start(bf16[128,1024]{1,0:T(8,128)(2,1)S(1)} %get-tuple-element.13), channel_id=1, source_target_pairs={{0,12},{4,8},{8,20},{12,16},{16,28},{20,24},{1,13},{5,9},{9,21},{1... | collective-permute-start | bytes 786440 | tf_op jit(solution)/shard_map/ppermute | solution.py:20
  21.9 18.3 %collective-permute-start.1 = (bf16[128,1024]{1,0:T(8,128)(2,1)S(1)}, bf16[128,1024]{1,0:T(8,128)(2,1)S(1)}, u32[]{:S(2)}, u32[]{:S(2)}) collective-permute-start(bf16[128,1024]{1,0:T(8,128)(2,1)S(1)} %get-tuple-element.13), channel_id=1, source_target_pairs={{0,4},{4,0},{8,12},{12,8},{16,20},{20,16},{24,28},{28,24},{1,5},{5... | collective-permute-start | bytes 786440 | tf_op jit(solution)/shard_map/ppermute | solution.py:20
  23.4 17.7 %collective-permute-start.6 = (bf16[128,1024]{1,0:T(8,128)(2,1)S(1)}, bf16[128,1024]{1,0:T(8,128)(2,1)S(1)}, u32[]{:S(2)}, u32[]{:S(2)}) collective-permute-start(bf16[128,1024]{1,0:T(8,128)(2,1)S(1)} %get-tuple-element.15), channel_id=1, source_target_pairs={{0,4},{4,0},{8,12},{12,8},{16,20},{20,16},{24,28},{28,24},{1,5},{5... | collective-permute-start | bytes 786440 | tf_op jit(solution)/shard_map/ppermute | solution.py:20
  25.1 16.0 %collective-permute-start.4 = (bf16[128,1024]{1,0:T(8,128)(2,1)S(1)}, bf16[128,1024]{1,0:T(8,128)(2,1)S(1)}, u32[]{:S(2)}, u32[]{:S(2)}) collective-permute-start(bf16[128,1024]{1,0:T(8,128)(2,1)S(1)} %collective-permute-done.2.back_own_ref), channel_id=1, source_target_pairs={{0,8},{4,12},{8,16},{12,20},{16,24},{20,28},{1,9},{5,13},{9,17},{1... | collective-permute-start | bytes 786440 | tf_op jit(solution)/shard_map/ppermute | solution.py:20
  30.7 10.4 %collective-permute-start.5 = (bf16[128,1024]{1,0:T(8,128)(2,1)S(1)}, bf16[128,1024]{1,0:T(8,128)(2,1)S(1)}, u32[]{:S(2)}, u32[]{:S(2)}) collective-permute-start(bf16[128,1024]{1,0:T(8,128)(2,1)S(1)} %collective-permute-done.3.back_pair_ref), channel_id=1, source_target_pairs={{0,8},{4,12},{8,16},{12,20},{16,24},{20,28},{1,9},{5,13},{9,17},{1... | collective-permute-start | bytes 786440 | tf_op jit(solution)/shard_map/ppermute | solution.py:20
  36.0 0.7 %copy-start.5 = (s32[32]{0:T(128)S(1)}, s32[32]{0:T(128)}, u32[]{:S(2)}) copy-start(s32[32]{0:T(128)} %seq_ref.3) | copy-start | bytes 388
  41.1 15.3 %copy-start.3 = (f32[2048]{0:T(1024)S(1)}, f32[2048]{0:T(1024)}, u32[]{:S(2)}) copy-start(f32[2048]{0:T(1024)} %param.12) | copy-start | bytes 24580
  42.3 14.1 %collective-permute-start.7 = (bf16[128,1024]{1,0:T(8,128)(2,1)S(1)}, bf16[128,1024]{1,0:T(8,128)(2,1)S(1)}, u32[]{:S(2)}, u32[]{:S(2)}) collective-permute-start(bf16[128,1024]{1,0:T(8,128)(2,1)S(1)} %get-tuple-element.18), channel_id=1, source_target_pairs={{0,4},{4,0},{8,12},{12,8},{16,20},{20,16},{24,28},{28,24},{1,5},{5... | collective-permute-start | bytes 786440 | tf_op jit(solution)/shard_map/ppermute | solution.py:20
where the time goes:
time: 57.9 us; the launch traced here: 57.5 us
  starting transfers between devices  25.9 us (45%)
  blocking collectives  11.9 us (21%)
  Pallas kernels  9.56 us (17%)
  local copies, waits for them, and re-layouts  4.71 us (8%)
  waiting for transfers between devices  3.83 us (7%)
  other arithmetic  1.46 us (3%)
    ppermute x8, starting transfers between devices, moved(): return lax.ppermute(block, SPOTS, pairs)  25.9 us
    psum x1, blocking collectives, shards(): power = lax.psum(power, ('half', 'mp'))  11.9 us
    ppermute x8, waiting for transfers between devices, moved(): return lax.ppermute(block, SPOTS, pairs)  3.83 us
    unnamed x12, local copies, waits for them, and re-layouts  3.62 us
    pallas_call x1, Pallas kernels, shards(): kernel_call(tables_kernel, shape((groups, 2, BLK, taps + BLK), jnp.bfloat...  3.56 us
    pallas_call x1, Pallas kernels, shards(): kernel_call(products_kernel, (half_shape, half_shape, half_shape, half_wi...  2.92 us
  transfers between devices with their start and end apart: 8, of which 3 were waited for; matrix products, arithmetic and copies ran while one was open for 3% of the time, Pallas kernels for 8%

commit v1 on v0

--- a/solution.py
+++ b/solution.py
@@ -133,7 +133,7 @@
 
 
 def far_kernel(
-    table_ref, acc_ref, far_own_ref, far_pair_ref, qkept_ref, qgot_ref, kept_ref, sent_ref, power_ref, win_ref, sq_ref
+    table_ref, acc_ref, far_own_ref, far_pair_ref, qkept_ref, qgot_ref, kept_ref, sent_ref, pkept_ref, psent_ref, win_ref, sq_ref
 ):
     groups = table_ref.shape[0]
     half = lax.axis_index("half")
@@ -158,19 +158,20 @@
             out_ref[:, lanes] = gated.astype(out_ref.dtype)
             squares = squares + gated * gated
         sq_ref[pl.ds(spot, BLK), :] = squares
-    power_ref[...] = lax.dot_general(
-        jnp.ones((8, GROUP), jnp.float32),
-        sq_ref[...],
-        (((1,), (1,)), ((), ())),
-        precision=lax.Precision.HIGHEST,
-        preferred_element_type=jnp.float32,
-    )[0:1]
-
-
-def norm_kernel(channels, power_ref, kept_ref, got_ref, gain_ref, out_ref):
+    for spot, out_ref in ((own, pkept_ref), (pair, psent_ref)):
+        out_ref[...] = lax.dot_general(
+            jnp.ones((8, GROUP), jnp.float32),
+            sq_ref[pl.ds(spot, BLK), :],
+            (((1,), (1,)), ((), ())),
+            precision=lax.Precision.HIGHEST,
+            preferred_element_type=jnp.float32,
+        )[0:1]
+
+
+def norm_kernel(channels, p0_ref, p1_ref, p2_ref, p3_ref, kept_ref, got_ref, gain_ref, out_ref):
     half = lax.axis_index("half")
     width = kept_ref.shape[1]
-    power = power_ref[:, pl.ds(pl.multiple_of(half * BLK, BLK), BLK)]
+    power = (p0_ref[...] + p1_ref[...]) + (p2_ref[...] + p3_ref[...])
     scale = lax.rsqrt(power / channels + norm_eps)
     diagonal = lax.broadcasted_iota(jnp.int32, (BLK, BLK), 0) == lax.broadcasted_iota(
         jnp.int32, (BLK, BLK), 1
@@ -206,10 +207,10 @@
     half_wide = shape((rows, width), jnp.float32)
 
     spots = range(2 * blocks)
-    to_next = [(i, i + 1) for i in spots if i + 1 < 2 * blocks]
+    to_next = [(i, (i + 1) % (2 * blocks)) for i in spots]
     to_pair = [(i, i ^ 1) for i in spots]
-    ahead = [(i, i + 2) for i in spots if i + 2 < 2 * blocks]
-    ahead_pair = [(i, (i ^ 1) + 2) for i in spots if (i ^ 1) + 2 < 2 * blocks]
+    ahead = [(i, (i + 2) % (2 * blocks)) for i in spots]
+    ahead_pair = [(i, ((i ^ 1) + 2) % (2 * blocks)) for i in spots]
 
     panels = jnp.transpose(projected, (1, 0, 2))
     edge = moved(panels[:, rows - 2 :], to_next)
@@ -253,25 +254,26 @@
 
     far_own = moved(back_own, ahead)
     far_pair = moved(back_pair, ahead)
-    done, send, power = kernel_call(
+    done, send, pkept, psent = kernel_call(
         far_kernel,
-        (half_wide, half_shape, shape((1, 2 * rows), jnp.float32)),
+        (half_wide, half_shape, shape((1, rows), jnp.float32), shape((1, rows), jnp.float32)),
         [VMEM] * 6,
         [pltpu.VMEM((2 * rows, width), jnp.bfloat16), pltpu.VMEM((2 * rows, GROUP), jnp.float32)],
         2 * 3 * rows * BLK * width,
         24 * rows * width,
     )(table, acc, far_own, far_pair, qkept, qgot)
 
+    power = pkept + moved(psent, to_pair)
+    powers = [power] + [lax.ppermute(power, "mp", [(i, i ^ k) for i in range(4)]) for k in (1, 2, 3)]
     back = moved(send, to_pair)
-    power = lax.psum(power, ("half", "mp"))
     return kernel_call(
         functools.partial(norm_kernel, channels),
         shape((rows, 2 * width), jnp.bfloat16),
-        [VMEM] * 4,
+        [VMEM] * 7,
         [],
         8 * rows * width,
         10 * rows * width,
-    )(power, done, back, norm_gain.reshape(1, -1))
+    )(*powers, done, back, norm_gain.reshape(1, -1))
 
 
 def solution(mesh):

time: 57.9 us -> 54.7 us (0.945)
  waiting for transfers between devices: 3.83 us -> 27.8 us
  starting transfers between devices: 25.9 us -> 10.8 us
  blocking collectives: 11.9 us -> 0 us
    ppermute x8 -> x9, waiting for transfers between devices: 3.83 us -> 24.8 us  [moved(): return lax.ppermute(block, SPOTS, pairs)]
    ppermute x8 -> x9, starting transfers between devices: 25.9 us -> 8.7 us  [moved(): return lax.ppermute(block, SPOTS, pairs)]
    psum x1 -> x0, blocking collectives: 11.9 us -> none  [shards(): power = lax.psum(power, ('half', 'mp'))]
    ppermute x0 -> x3, waiting for transfers between devices: none -> 3 us  [shards(): lax.ppermute(power, 'mp', [(i, i ^ k) for i in range(4)])]
    ppermute x0 -> x3, starting transfers between devices: none -> 2.14 us  [shards(): lax.ppermute(power, 'mp', [(i, i ^ k) for i in range(4)])]
  transfers between devices with their start and end apart: 8 -> 12, of which waited for: 3 -> 8; matrix products, arithmetic and copies ran while one was open for 3% -> 3% of each run, Pallas kernels for 8% -> 8%
where the time goes in v1:
time: 54.7 us; the launch traced here: 54.4 us
  waiting for transfers between devices  27.8 us (51%)
  starting transfers between devices  10.8 us (20%)
  Pallas kernels  9.5 us (17%)
  local copies, waits for them, and re-layouts  4.72 us (9%)
  other arithmetic  1.46 us (3%)
    ppermute x9, waiting for transfers between devices, moved(): return lax.ppermute(block, SPOTS, pairs)  24.8 us
    ppermute x9, starting transfers between devices, moved(): return lax.ppermute(block, SPOTS, pairs)  8.7 us
    unnamed x12, local copies, waits for them, and re-layouts  3.62 us
    pallas_call x1, Pallas kernels, shards(): kernel_call(tables_kernel, shape((groups, 2, BLK, taps + BLK), jnp.bfloat...  3.56 us
    ppermute x3, waiting for transfers between devices, shards(): lax.ppermute(power, 'mp', [(i, i ^ k) for i in range(4)])  3 us
    pallas_call x1, Pallas kernels, shards(): kernel_call(products_kernel, (half_shape, half_shape, half_shape, half_wi...  2.92 us
    ppermute x3, starting transfers between devices, shards(): lax.ppermute(power, 'mp', [(i, i ^ k) for i in range(4)])  2.14 us
  transfers between devices with their start and end apart: 12, of which 8 were waited for; matrix products, arithmetic and copies ran while one was open for 3% of the time, Pallas kernels for 8%

profile of v1, /device:TPU:0, one launch (start us, length us, event | category | flops | bytes accessed | tf_op | source)
XLA Modules:
  0.0 54.4 jit_solution(10469033448094910739)
XLA Ops:
  0.0 0.0 copy-start.2
  0.0 0.9 %slice.4 = bf16[3,2,2048]{2,1,0:T(2,128)(2,1)S(1)} slice(bf16[3,128,2048]{2,1,0:T(8,128)(2,1)} %bitcast.8), slice={[0:3], [126:128], [0:2048]} | slice | bytes 49152 | tf_op jit(solution)/shard_map/slice | solution.py:216
  0.9 3.0 %collective-permute-start = (bf16[3,2,2048]{2,1,0:T(2,128)(2,1)S(1)}, bf16[3,2,2048]{2,1,0:T(2,128)(2,1)S(1)}, u32[]{:S(2)}, u32[]{:S(2)}) collective-permute-start(bf16[3,2,2048]{2,1,0:T(2,128)(2,1)S(1)} %slice.4), channel_id=1, source_target_pairs={{0,4},{4,8},{8,12},{12,16},{16,20},{20,24},{24,28},{28,0},{1,5},{5... | collective-permute-start | bytes 73736 | tf_op jit(solution)/shard_map/ppermute | solution.py:20
  4.0 4.8 %collective-permute-done.edge_ref = bf16[3,2,2048]{2,1,0:T(2,128)(2,1)S(1)} collective-permute-done((bf16[3,2,2048]{2,1,0:T(2,128)(2,1)S(1)}, bf16[3,2,2048]{2,1,0:T(2,128)(2,1)S(1)}, u32[]{:S(2)}, u32[]{:S(2)}) %collective-permute-start) | collective-permute-done | bytes 24608 | tf_op jit(solution)/shard_map/ppermute | solution.py:20
  8.8 0.0 copy-start
  8.8 1.4 %copy-done = bf16[128,3,2048]{2,0,1:T(8,128)(2,1)S(1)} copy-done((bf16[128,3,2048]{2,0,1:T(8,128)(2,1)S(1)}, bf16[128,3,2048]{2,0,1:T(8,128)(2,1)}, u32[]{:S(2)}) %copy-start) | copy-done | bytes 1572888
  10.2 0.0 copy-start.1
  10.2 0.9 %copy-done.1 = f32[3,3,2048]{2,1,0:T(4,128)S(1)} copy-done((f32[3,3,2048]{2,1,0:T(4,128)S(1)}, f32[3,3,2048]{2,1,0:T(4,128)}, u32[]{:S(2)}) %copy-start.1) | copy-done | bytes 73752
  11.1 0.0 copy-start.4
  11.1 0.7 %copy-done.4 = s32[32]{0:T(128)S(1)} copy-done((s32[32]{0:T(128)S(1)}, s32[32]{0:T(128)}, u32[]{:S(2)}) %copy-start.4) | copy-done | bytes 152
  11.8 2.9 %shard_map.74 = (bf16[128,1024]{1,0:T(8,128)(2,1)S(1)}, bf16[128,1024]{1,0:T(8,128)(2,1)S(1)}, bf16[128,1024]{1,0:T(8,128)(2,1)S(1)}, f32[128,1024]{1,0:T(8,128)S(1)}) custom-call(s32[32]{0:T(128)S(1)} %copy-done.4, bf16[3,128,2048]{2,1,0:T(8,128)(2,1)S(1)} %bitcast.9, bf16[3,2,2048]{2,1,0:T(2,128)(2,1)S(1)} %collective-permute-done.edge_ref, ...), custom_call_target="tpu_custom_call" | custom-call | flops 7864320 | bytes 2097152 | tf_op jit(solution)/shard_map/pallas_call | solution.py:218
  14.7 0.1 collective-permute-start.2
  14.8 1.5 %collective-permute-start.3 = (bf16[128,1024]{1,0:T(8,128)(2,1)S(1)}, bf16[128,1024]{1,0:T(8,128)(2,1)S(1)}, u32[]{:S(2)}, u32[]{:S(2)}) collective-permute-start(bf16[128,1024]{1,0:T(8,128)(2,1)S(1)} %get-tuple-element.14), channel_id=1, source_target_pairs={{0,12},{4,8},{8,20},{12,16},{16,28},{20,24},{24,4},{28,0},{1,13},{... | collective-permute-start | bytes 786440 | tf_op jit(solution)/shard_map/ppermute | solution.py:20
  16.3 1.4 %collective-permute-start.1 = (bf16[128,1024]{1,0:T(8,128)(2,1)S(1)}, bf16[128,1024]{1,0:T(8,128)(2,1)S(1)}, u32[]{:S(2)}, u32[]{:S(2)}) collective-permute-start(bf16[128,1024]{1,0:T(8,128)(2,1)S(1)} %get-tuple-element.14), channel_id=1, source_target_pairs={{0,4},{4,0},{8,12},{12,8},{16,20},{20,16},{24,28},{28,24},{1,5},{5... | collective-permute-start | bytes 786440 | tf_op jit(solution)/shard_map/ppermute | solution.py:20
  17.7 0.6 %collective-permute-start.6 = (bf16[128,1024]{1,0:T(8,128)(2,1)S(1)}, bf16[128,1024]{1,0:T(8,128)(2,1)S(1)}, u32[]{:S(2)}, u32[]{:S(2)}) collective-permute-start(bf16[128,1024]{1,0:T(8,128)(2,1)S(1)} %get-tuple-element.16), channel_id=1, source_target_pairs={{0,4},{4,0},{8,12},{12,8},{16,20},{20,16},{24,28},{28,24},{1,5},{5... | collective-permute-start | bytes 786440 | tf_op jit(solution)/shard_map/ppermute | solution.py:20
  18.3 7.5 %collective-permute-done.2.back_own_ref = bf16[128,1024]{1,0:T(8,128)(2,1)S(1)} collective-permute-done((bf16[128,1024]{1,0:T(8,128)(2,1)S(1)}, bf16[128,1024]{1,0:T(8,128)(2,1)S(1)}, u32[]{:S(2)}, u32[]{:S(2)}) %collective-permute-start.2) | collective-permute-done | bytes 262176 | tf_op jit(solution)/shard_map/ppermute | solution.py:20
  25.8 0.0 collective-permute-start.4
  25.8 4.1 %collective-permute-done.3.back_pair_ref = bf16[128,1024]{1,0:T(8,128)(2,1)S(1)} collective-permute-done((bf16[128,1024]{1,0:T(8,128)(2,1)S(1)}, bf16[128,1024]{1,0:T(8,128)(2,1)S(1)}, u32[]{:S(2)}, u32[]{:S(2)}) %collective-permute-start.3) | collective-permute-done | bytes 262176 | tf_op jit(solution)/shard_map/ppermute | solution.py:20
  29.9 0.0 collective-permute-start.5
  29.9 0.7 %convert_element_type.6 = f32[16,4]{0,1:T(4,128)S(1)} convert(s32[16,4]{0,1:T(4,128)} %param.10) | non-fusion elementwise | flops 64 | bytes 512 | tf_op jit(solution)/shard_map/convert_element_type | solution.py:236
  30.5 0.1 copy.8
  30.6 0.1 broadcast_in_dim.3
  30.7 0.8 %fusion.taps_ref = bf16[16,512]{1,0:T(8,128)(2,1)S(1)} fusion(f32[16,512]{1,0:T(8,128)} %param.9, f32[2,8,4,128]{3,2,1,0:T(4,128)S(1)} %bitcast.12), kind=kLoop, calls=%fused_computation.1 | loop fusion | flops 16384 | bytes 81920 | tf_op jit(solution)/shard_map/convert_element_type | solution.py:236
  31.5 0.0 copy-start.5
  31.5 0.7 %copy-done.5 = s32[32]{0:T(128)S(1)} copy-done((s32[32]{0:T(128)S(1)}, s32[32]{0:T(128)}, u32[]{:S(2)}) %copy-start.5) | copy-done | bytes 152
  32.1 3.6 %shard_map.73.table_ref = bf16[8,2,128,640]{3,2,1,0:T(8,128)(2,1)S(1)} custom-call(s32[32]{0:T(128)S(1)} %copy-done.5, bf16[16,512]{1,0:T(8,128)(2,1)S(1)} %fusion.taps_ref), custom_call_target="tpu_custom_call" | custom-call | flops 20971520 | bytes 4194304 | tf_op jit(solution)/shard_map/pallas_call | solution.py:237
  35.7 0.0 collective-permute-done.1.pair_ref
  35.7 0.0 copy-done.2
  35.7 0.9 %shard_map.75.acc_ref = f32[256,1024]{1,0:T(8,128)S(1)} custom-call(bf16[8,2,128,640]{3,2,1,0:T(8,128)(2,1)S(1)} %shard_map.73.table_ref, bf16[128,1024]{1,0:T(8,128)(2,1)S(1)} %get-tuple-element.13.own_ref, bf16[128,1024]{1,0:T(8,128)(2,1)S(1)} %collective-permute-done.1.pair_ref, bf16[128,1024]{1,0:T(8,128)(2,1)S(1)} %collective-permute-done.2.back_own_ref, ...), custom_call_target="tpu_custom_call" | custom-call | flops 234881024 | bytes 2097152 | tf_op jit(solution)/shard_map/pallas_call | solution.py:246
  36.6 0.0 copy-start.3
  36.6 0.0 collective-permute-done.6.qgot_ref
  36.6 0.4 collective-permute-done.4.far_own_ref
  37.1 3.5 %collective-permute-done.5.far_pair_ref = bf16[128,1024]{1,0:T(8,128)(2,1)S(1)} collective-permute-done((bf16[128,1024]{1,0:T(8,128)(2,1)S(1)}, bf16[128,1024]{1,0:T(8,128)(2,1)S(1)}, u32[]{:S(2)}, u32[]{:S(2)}) %collective-permute-start.5) | collective-permute-done | bytes 262176 | tf_op jit(solution)/shard_map/ppermute | solution.py:20
  40.6 1.1 %shard_map.76 = (f32[128,1024]{1,0:T(8,128)S(1)}, bf16[128,1024]{1,0:T(8,128)(2,1)S(1)}, f32[1,128]{1,0:T(1,128)S(1)}, f32[1,128]{1,0:T(1,128)S(1)}) custom-call(bf16[8,2,128,640]{3,2,1,0:T(8,128)(2,1)S(1)} %shard_map.73.table_ref, f32[256,1024]{1,0:T(8,128)S(1)} %shard_map.75.acc_ref, bf16[128,1024]{1,0:T(8,128)(2,1)S(1)} %collective-permute-done.4.far_own_ref, ...), custom_call_target="tpu_custom_call" | custom-call | flops 100663296 | bytes 3145728 | tf_op jit(solution)/shard_map/pallas_call | solution.py:257
  41.7 0.5 collective-permute-start.11
  42.2 1.6 %collective-permute-start.7 = (f32[1,128]{1,0:T(1,128)S(1)}, f32[1,128]{1,0:T(1,128)S(1)}, u32[]{:S(2)}, u32[]{:S(2)}) collective-permute-start(f32[1,128]{1,0:T(1,128)S(1)} %get-tuple-element.18), channel_id=1, source_target_pairs={{0,4},{4,0},{8,12},{12,8},{16,20},{20,16},{24,28},{28,24},{1,5},{5... | collective-permute-start | bytes 1544 | tf_op jit(solution)/shard_map/ppermute | solution.py:20
  43.7 4.4 %collective-permute-done.7 = f32[1,128]{1,0:T(1,128)S(1)} collective-permute-done((f32[1,128]{1,0:T(1,128)S(1)}, f32[1,128]{1,0:T(1,128)S(1)}, u32[]{:S(2)}, u32[]{:S(2)}) %collective-permute-start.7) | collective-permute-done | bytes 544 | tf_op jit(solution)/shard_map/ppermute | solution.py:20
  48.2 0.0 collective-permute-start.10
  48.2 1.6 %collective-permute-start.8 = (f32[1,128]{1,0:T(1,128)S(1)}, f32[1,128]{1,0:T(1,128)S(1)}, u32[]{:S(2)}, u32[]{:S(2)}) collective-permute-start(f32[1,128]{1,0:T(1,128)S(1)} %add.3.p0_ref), channel_id=1, source_target_pairs={{0,1},{1,0},{2,3},{3,2},{4,5},{5,4},{6,7},{7,6},{8,9},{9,8},{10,11... | collective-permute-start | bytes 1544 | tf_op jit(solution)/shard_map/ppermute | solution.py:267
  49.8 0.5 collective-permute-start.9
  50.3 0.8 %collective-permute-done.10.p3_ref = f32[1,128]{1,0:T(1,128)S(1)} collective-permute-done((f32[1,128]{1,0:T(1,128)S(1)}, f32[1,128]{1,0:T(1,128)S(1)}, u32[]{:S(2)}, u32[]{:S(2)}) %collective-permute-start.10) | collective-permute-done | bytes 544 | tf_op jit(solution)/shard_map/ppermute | solution.py:267
  51.1 0.0 collective-permute-done.8.p1_ref
  51.1 2.2 %collective-permute-done.9.p2_ref = f32[1,128]{1,0:T(1,128)S(1)} collective-permute-done((f32[1,128]{1,0:T(1,128)S(1)}, f32[1,128]{1,0:T(1,128)S(1)}, u32[]{:S(2)}, u32[]{:S(2)}) %collective-permute-start.9) | collective-permute-done | bytes 544 | tf_op jit(solution)/shard_map/ppermute | solution.py:267
  53.3 0.0 collective-permute-done.11.got_ref
  53.3 0.0 copy-done.3
  53.3 1.0 %shard_map.77 = bf16[128,2048]{1,0:T(8,128)(2,1)} custom-call(f32[1,128]{1,0:T(1,128)S(1)} %add.3.p0_ref, f32[1,128]{1,0:T(1,128)S(1)} %collective-permute-done.8.p1_ref, f32[1,128]{1,0:T(1,128)S(1)} %collective-permute-done.9.p2_ref, f32[1,128]{1,0:T(1,128)S(1)} %collective-permute-done.10.p3_ref, f32[128,1024]{1,0:T(8,128)S(1)} %get-tuple-element.19.kept_ref, ...), custom_call_target="tpu_custom_call" | custom-call | flops 1048576 | bytes 1310720 | tf_op jit(solution)/shard_map/pallas_call | solution.py:269
  (1 shorter events, 0.0 us)
Async XLA Ops:
  0.0 35.7 %copy-start.2 = (f32[2048]{0:T(1024)S(1)}, f32[2048]{0:T(1024)}, u32[]{:S(2)}) copy-start(f32[2048]{0:T(1024)} %param.11) | copy-start | bytes 24580
  0.9 7.9 %collective-permute-start = (bf16[3,2,2048]{2,1,0:T(2,128)(2,1)S(1)}, bf16[3,2,2048]{2,1,0:T(2,128)(2,1)S(1)}, u32[]{:S(2)}, u32[]{:S(2)}) collective-permute-start(bf16[3,2,2048]{2,1,0:T(2,128)(2,1)S(1)} %slice.4), channel_id=1, source_target_pairs={{0,4},{4,8},{8,12},{12,16},{16,20},{20,24},{24,28},{28,0},{1,5},{5... | collective-permute-start | bytes 73736 | tf_op jit(solution)/shard_map/ppermute | solution.py:20
  8.8 1.4 %copy-start = (bf16[128,3,2048]{2,0,1:T(8,128)(2,1)S(1)}, bf16[128,3,2048]{2,0,1:T(8,128)(2,1)}, u32[]{:S(2)}) copy-start(bf16[128,3,2048]{2,0,1:T(8,128)(2,1)} %param.7) | copy-start | bytes 4718596
  10.2 0.9 %copy-start.1 = (f32[3,3,2048]{2,1,0:T(4,128)S(1)}, f32[3,3,2048]{2,1,0:T(4,128)}, u32[]{:S(2)}) copy-start(f32[3,3,2048]{2,1,0:T(4,128)} %w_ref.1) | copy-start | bytes 221188
  11.1 0.7 %copy-start.4 = (s32[32]{0:T(128)S(1)}, s32[32]{0:T(128)}, u32[]{:S(2)}) copy-start(s32[32]{0:T(128)} %seq_ref.3) | copy-start | bytes 388
  14.7 11.1 %collective-permute-start.2 = (bf16[128,1024]{1,0:T(8,128)(2,1)S(1)}, bf16[128,1024]{1,0:T(8,128)(2,1)S(1)}, u32[]{:S(2)}, u32[]{:S(2)}) collective-permute-start(bf16[128,1024]{1,0:T(8,128)(2,1)S(1)} %get-tuple-element.13.own_ref), channel_id=1, source_target_pairs={{0,8},{4,12},{8,16},{12,20},{16,24},{20,28},{24,0},{28,4},{1,9},{5... | collective-permute-start | bytes 786440 | tf_op jit(solution)/shard_map/ppermute | solution.py:20
  14.8 15.1 %collective-permute-start.3 = (bf16[128,1024]{1,0:T(8,128)(2,1)S(1)}, bf16[128,1024]{1,0:T(8,128)(2,1)S(1)}, u32[]{:S(2)}, u32[]{:S(2)}) collective-permute-start(bf16[128,1024]{1,0:T(8,128)(2,1)S(1)} %get-tuple-element.14), channel_id=1, source_target_pairs={{0,12},{4,8},{8,20},{12,16},{16,28},{20,24},{24,4},{28,0},{1,13},{... | collective-permute-start | bytes 786440 | tf_op jit(solution)/shard_map/ppermute | solution.py:20
  16.3 19.4 %collective-permute-start.1 = (bf16[128,1024]{1,0:T(8,128)(2,1)S(1)}, bf16[128,1024]{1,0:T(8,128)(2,1)S(1)}, u32[]{:S(2)}, u32[]{:S(2)}) collective-permute-start(bf16[128,1024]{1,0:T(8,128)(2,1)S(1)} %get-tuple-element.14), channel_id=1, source_target_pairs={{0,4},{4,0},{8,12},{12,8},{16,20},{20,16},{24,28},{28,24},{1,5},{5... | collective-permute-start | bytes 786440 | tf_op jit(solution)/shard_map/ppermute | solution.py:20
  17.7 18.9 %collective-permute-start.6 = (bf16[128,1024]{1,0:T(8,128)(2,1)S(1)}, bf16[128,1024]{1,0:T(8,128)(2,1)S(1)}, u32[]{:S(2)}, u32[]{:S(2)}) collective-permute-start(bf16[128,1024]{1,0:T(8,128)(2,1)S(1)} %get-tuple-element.16), channel_id=1, source_target_pairs={{0,4},{4,0},{8,12},{12,8},{16,20},{20,16},{24,28},{28,24},{1,5},{5... | collective-permute-start | bytes 786440 | tf_op jit(solution)/shard_map/ppermute | solution.py:20
  25.8 11.3 %collective-permute-start.4 = (bf16[128,1024]{1,0:T(8,128)(2,1)S(1)}, bf16[128,1024]{1,0:T(8,128)(2,1)S(1)}, u32[]{:S(2)}, u32[]{:S(2)}) collective-permute-start(bf16[128,1024]{1,0:T(8,128)(2,1)S(1)} %collective-permute-done.2.back_own_ref), channel_id=1, source_target_pairs={{0,8},{4,12},{8,16},{12,20},{16,24},{20,28},{24,0},{28,4},{1,9},{5... | collective-permute-start | bytes 786440 | tf_op jit(solution)/shard_map/ppermute | solution.py:20
  29.9 10.8 %collective-permute-start.5 = (bf16[128,1024]{1,0:T(8,128)(2,1)S(1)}, bf16[128,1024]{1,0:T(8,128)(2,1)S(1)}, u32[]{:S(2)}, u32[]{:S(2)}) collective-permute-start(bf16[128,1024]{1,0:T(8,128)(2,1)S(1)} %collective-permute-done.3.back_pair_ref), channel_id=1, source_target_pairs={{0,8},{4,12},{8,16},{12,20},{16,24},{20,28},{24,0},{28,4},{1,9},{5... | collective-permute-start | bytes 786440 | tf_op jit(solution)/shard_map/ppermute | solution.py:20
  31.5 0.7 %copy-start.5 = (s32[32]{0:T(128)S(1)}, s32[32]{0:T(128)}, u32[]{:S(2)}) copy-start(s32[32]{0:T(128)} %seq_ref.3) | copy-start | bytes 388
  36.6 16.7 %copy-start.3 = (f32[2048]{0:T(1024)S(1)}, f32[2048]{0:T(1024)}, u32[]{:S(2)}) copy-start(f32[2048]{0:T(1024)} %param.12) | copy-start | bytes 24580
  41.7 11.6 %collective-permute-start.11 = (bf16[128,1024]{1,0:T(8,128)(2,1)S(1)}, bf16[128,1024]{1,0:T(8,128)(2,1)S(1)}, u32[]{:S(2)}, u32[]{:S(2)}) collective-permute-start(bf16[128,1024]{1,0:T(8,128)(2,1)S(1)} %get-tuple-element.20), channel_id=1, source_target_pairs={{0,4},{4,0},{8,12},{12,8},{16,20},{20,16},{24,28},{28,24},{1,5},{5... | collective-permute-start | bytes 786440 | tf_op jit(solution)/shard_map/ppermute | solution.py:20
  42.2 6.0 %collective-permute-start.7 = (f32[1,128]{1,0:T(1,128)S(1)}, f32[1,128]{1,0:T(1,128)S(1)}, u32[]{:S(2)}, u32[]{:S(2)}) collective-permute-start(f32[1,128]{1,0:T(1,128)S(1)} %get-tuple-element.18), channel_id=1, source_target_pairs={{0,4},{4,0},{8,12},{12,8},{16,20},{20,16},{24,28},{28,24},{1,5},{5... | collective-permute-start | bytes 1544 | tf_op jit(solution)/shard_map/ppermute | solution.py:20
  48.2 3.0 %collective-permute-start.10 = (f32[1,128]{1,0:T(1,128)S(1)}, f32[1,128]{1,0:T(1,128)S(1)}, u32[]{:S(2)}, u32[]{:S(2)}) collective-permute-start(f32[1,128]{1,0:T(1,128)S(1)} %add.3.p0_ref), channel_id=1, source_target_pairs={{0,3},{1,2},{2,1},{3,0},{4,7},{5,6},{6,5},{7,4},{8,11},{9,10},{10,... | collective-permute-start | bytes 1544 | tf_op jit(solution)/shard_map/ppermute | solution.py:267
  48.2 3.0 %collective-permute-start.8 = (f32[1,128]{1,0:T(1,128)S(1)}, f32[1,128]{1,0:T(1,128)S(1)}, u32[]{:S(2)}, u32[]{:S(2)}) collective-permute-start(f32[1,128]{1,0:T(1,128)S(1)} %add.3.p0_ref), channel_id=1, source_target_pairs={{0,1},{1,0},{2,3},{3,2},{4,5},{5,4},{6,7},{7,6},{8,9},{9,8},{10,11... | collective-permute-start | bytes 1544 | tf_op jit(solution)/shard_map/ppermute | solution.py:267
  49.8 3.5 %collective-permute-start.9 = (f32[1,128]{1,0:T(1,128)S(1)}, f32[1,128]{1,0:T(1,128)S(1)}, u32[]{:S(2)}, u32[]{:S(2)}) collective-permute-start(f32[1,128]{1,0:T(1,128)S(1)} %add.3.p0_ref), channel_id=1, source_target_pairs={{0,2},{1,3},{2,0},{3,1},{4,6},{5,7},{6,4},{7,5},{8,10},{9,11},{10,... | collective-permute-start | bytes 1544 | tf_op jit(solution)/shard_map/ppermute | solution.py:267

commit v2 on v0

v2 whole, which is shorter than its diff:
```python
import functools

import jax
import jax.numpy as jnp
from jax import lax
from jax.experimental import pallas as pl
from jax.experimental.pallas import tpu as pltpu
from jax.sharding import Mesh, PartitionSpec as P

GROUP = 128
BLK = 128
norm_eps = 1e-06

VMEM = pl.BlockSpec(memory_space=pltpu.VMEM)
SMEM = pl.BlockSpec(memory_space=pltpu.SMEM)
SPOTS = ("blk", "half")


def moved(block, pairs):
    return lax.ppermute(block, SPOTS, pairs)


def boundaries(seq_ref, t):
    def step(k, carry):
        end, first, second = carry
        end = end + seq_ref[k]
        return end, first | (t == end).astype(jnp.int32), second | (t - 1 == end).astype(jnp.int32)

    first = (t == 0).astype(jnp.int32)
    second = (t == 1).astype(jnp.int32)
    _, first, second = lax.fori_loop(0, seq_ref.shape[0], step, (jnp.int32(0), first, second))
    return first, first | second


def row_masks(seq_ref, start, m1_ref, m2_ref):
    rows = lax.broadcasted_iota(jnp.int32, (BLK, GROUP), 0)
    diagonal = rows == lax.broadcasted_iota(jnp.int32, (BLK, GROUP), 1)
    marks = boundaries(seq_ref, start + lax.broadcasted_iota(jnp.int32, (8, GROUP), 1))
    for mark, m_ref in zip(marks, (m1_ref, m2_ref)):
        keep = 1.0 - mark.astype(jnp.float32)[0:1]
        column = jnp.sum(jnp.where(diagonal, keep, 0.0), axis=1, keepdims=True)
        m_ref[...] = jnp.broadcast_to(column, (BLK, GROUP))


def counted(seq_ref, t):
    def step(k, carry):
        end, total = carry
        end = end + seq_ref[k]
        return end, total + (end <= t).astype(jnp.int32)

    _, total = lax.fori_loop(
        0, seq_ref.shape[0], step, (jnp.int32(0), jnp.zeros(t.shape, jnp.int32))
    )
    return jnp.where(t >= 0, total, -1)


def feature(x, x_ref, w, m1_ref, m2_ref):
    rows = x.shape[0]
    return (
        w[0:1] * x
        + w[1:2] * x_ref[7 : rows + 7, :] * m1_ref[...]
        + w[2:3] * x_ref[6 : rows + 6, :] * m2_ref[...]
    )


def products_kernel(
    seq_hbm, panels_hbm, w_hbm, sent_ref, kept_ref, qsent_ref, qkept_ref,
    seq_ref, kv_ref, w_ref, x_ref, m1_ref, m2_ref, sems,
):
    rows, width = qsent_ref.shape
    pieces = kv_ref.shape[0]
    piece = kv_ref.shape[3]
    half = lax.axis_index("half")
    shard = lax.axis_index("blk") * 2 + half
    keep_at = pl.multiple_of(half * width, width)
    send_at = pl.multiple_of((1 - half) * width, width)

    loads = [
        pltpu.make_async_copy(seq_hbm, seq_ref, sems.at[0]),
        pltpu.make_async_copy(w_hbm, w_ref, sems.at[1]),
    ]
    for p in range(pieces):
        at = keep_at if p < pieces // 2 else send_at
        lanes = pl.ds(pl.multiple_of(at + (p % (pieces // 2)) * piece, piece), piece)
        loads.append(pltpu.make_async_copy(panels_hbm.at[1:3, :, lanes], kv_ref.at[p], sems.at[2 + p]))
    asides = [
        pltpu.make_async_copy(panels_hbm.at[0, :, pl.ds(keep_at, width)], qkept_ref, sems.at[2 + pieces]),
        pltpu.make_async_copy(panels_hbm.at[0, :, pl.ds(send_at, width)], qsent_ref, sems.at[3 + pieces]),
    ]
    for load in loads + asides:
        load.start()
    loads[0].wait()
    row_masks(seq_ref, shard * rows, m1_ref, m2_ref)
    x_ref[:, 0:8, :] = jnp.zeros((x_ref.shape[0], 8, GROUP), jnp.float32)
    loads[1].wait()
    asides[0].wait()
    asides[1].wait()
    for p in range(pieces):
        loads[2 + p].wait()
        kept = p < pieces // 2
        out_ref, q_ref, at = (kept_ref, qkept_ref, keep_at) if kept else (sent_ref, qsent_ref, send_at)
        for c in range(0, piece, GROUP):
            base = (p % (pieces // 2)) * piece + c
            there = slice(base, base + GROUP)
            w_lanes = pl.ds(pl.multiple_of(at + base, GROUP), GROUP)
            slot = (c // GROUP) % (x_ref.shape[0] // 2) * 2
            heads, tails, made = [], [], []
            for i in range(2):
                x = kv_ref[p, i, :, c : c + GROUP].astype(jnp.float32)
                x_ref[slot + i, 8:, :] = x
                made.append(feature(x, x_ref.at[slot + i], w_ref[1 + i, :, w_lanes], m1_ref, m2_ref))
                heads.append(x[0:2])
                tails.append(x[rows - 2 :])
            out_ref[:rows, there] = (made[0] * made[1]).astype(out_ref.dtype)
            tails.append(q_ref[rows - 16 :, there].astype(jnp.float32)[14:])
            extra = jnp.concatenate(heads + tails + [jnp.zeros((6, GROUP), jnp.float32)], 0)
            out_ref[rows:, there] = extra.astype(out_ref.dtype)


def edge_marks(seq_ref):
    t = (
        (lax.axis_index("blk") - 2) * (2 * BLK)
        + lax.broadcasted_iota(jnp.int32, (8, GROUP), 1) * BLK
        + lax.broadcasted_iota(jnp.int32, (8, GROUP), 0)
    )
    return [1.0 - mark.astype(jnp.float32) for mark in boundaries(seq_ref, t)]


def first_rows(now, ahead, w_ref, lanes, marks, spot):
    m1, m2 = [mark[:, spot : spot + 1] for mark in marks]
    top = lax.broadcasted_iota(jnp.int32, now.shape, 0) == 0
    made = []
    for i in range(2):
        x0 = pltpu.roll(now, (8 - 2 * i) % 8, 0) if i else now
        x1 = jnp.where(top, pltpu.roll(ahead, 3 - 2 * i, 0), pltpu.roll(now, (9 - 2 * i) % 8, 0))
        x2 = pltpu.roll(ahead, 4 - 2 * i, 0)
        w = w_ref[1 + i, :, lanes]
        made.append(w[0:1] * x0 + w[1:2] * x1 * m1 + w[2:3] * x2 * m2)
    return made[0] * made[1]


def put_first_rows(win_ref, at, rows):
    old = win_ref[at : at + 16, :].astype(jnp.float32)
    new = jnp.concatenate([rows, rows], 0)
    first = lax.broadcasted_iota(jnp.int32, old.shape, 0) < 2
    win_ref[at : at + 16, :] = jnp.where(first, new, old).astype(win_ref.dtype)


def tables_kernel(seq_ref, taps_ref, out_ref, rev_ref, m_ref):
    groups = out_ref.shape[0]
    taps = taps_ref.shape[1]
    span = rev_ref.shape[1]
    width = out_ref.shape[3]
    half = lax.axis_index("half")
    start = lax.axis_index("blk") * (2 * BLK)
    turn = lax.broadcasted_iota(jnp.int32, (taps, span), 0) + lax.broadcasted_iota(
        jnp.int32, (taps, span), 1
    )
    turn = (turn == taps).astype(jnp.bfloat16)
    rev_ref[...] = jnp.dot(taps_ref[...], turn, preferred_element_type=jnp.float32)
    for part in range(2):
        t_in = start - taps + part * BLK + lax.broadcasted_iota(jnp.int32, (8, width), 1)
        t_out = start + part * BLK + lax.broadcasted_iota(jnp.int32, (BLK, GROUP), 0)
        seg_in = counted(seq_ref, t_in)[0:1]
        seg_out = counted(seq_ref, t_out)[:, 0:1]
        m_ref[part] = (seg_in == seg_out).astype(jnp.float32)

    def one(g, _):
        row = rev_ref[pl.ds(half * groups + g, 1), :]
        table = pltpu.roll(
            jnp.broadcast_to(row, (BLK, span)), 0, 1, stride=1, stride_axis=0
        )[:, :width]
        for part in range(2):
            out_ref[g, part] = (table * m_ref[part]).astype(out_ref.dtype)
        return 0

    lax.fori_loop(0, groups, one, 0)


def near_kernel(
    seq_ref, table_ref, own_ref, pair_ref, back_own_ref, back_pair_ref, qkept_ref, qgot_ref, w_ref, bias_ref,
    acc_ref, q_ref, win_ref, extra_ref, x_ref, m1_ref, m2_ref,
):
    groups = table_ref.shape[0]
    width = groups * GROUP
    half = lax.axis_index("half")
    start = lax.axis_index("blk") * (2 * BLK)
    half_lanes = pl.ds(pl.multiple_of(half * width, width), width)
    for spot, message in ((half, back_own_ref), (1 - half, back_pair_ref), (2 + half, own_ref), (3 - half, pair_ref)):
        win_ref[pl.ds(pl.multiple_of(spot * BLK, BLK), BLK), :] = message[:BLK]
        extra_ref[spot] = message[BLK:].astype(jnp.float32)
    marks = edge_marks(seq_ref)
    for spot in (1, 2, 3):
        rows = first_rows(extra_ref[spot, :8], extra_ref[spot - 1, :8], w_ref, half_lanes, marks, spot + 2)
        put_first_rows(win_ref, spot * BLK, rows)
    for g in range(groups):
        lanes = slice(g * GROUP, (g + 1) * GROUP)
        bias = bias_ref[:, pl.ds(pl.multiple_of(half * width + g * GROUP, GROUP), GROUP)]
        for part in range(2):
            total = jnp.dot(
                table_ref[g, part, :, (3 - part) * BLK :],
                win_ref[BLK : (3 + part) * BLK, lanes],
                preferred_element_type=jnp.float32,
            )
            here = win_ref[(2 + part) * BLK : (3 + part) * BLK, lanes].astype(jnp.float32)
            acc_ref[part * BLK : (part + 1) * BLK, lanes] = total + bias * here
    for part, raw_ref in ((half, qkept_ref), (1 - half, qgot_ref)):
        row_masks(seq_ref, start + part * BLK, m1_ref, m2_ref)
        for g in range(groups):
            lanes = slice(g * GROUP, (g + 1) * GROUP)
            w = w_ref[0, :, pl.ds(pl.multiple_of(half * width + g * GROUP, GROUP), GROUP)]
            x = raw_ref[:, lanes].astype(jnp.float32)
            slot = g % 2
            x_ref[slot, 6:8, :] = extra_ref[1 + part, 8:10, lanes]
            x_ref[slot, 8:, :] = x
            q_ref[pl.ds(pl.multiple_of(part * BLK, BLK), BLK), lanes] = feature(
                x, x_ref.at[slot], w, m1_ref, m2_ref
            )


def far_kernel(deep, seq_ref, table_ref, acc_ref, q_ref, w_ref, *refs):
    messages, refs = refs[: 4 + deep], refs[4 + deep :]
    back_own_ref, back_pair_ref, far_own_ref, far_pair_ref = messages[:4]
    kept_ref, sent_ref, power_ref, win_ref, extra_ref, sq_ref = refs
    groups = table_ref.shape[0]
    width = groups * GROUP
    half = lax.axis_index("half")
    half_lanes = pl.ds(pl.multiple_of(half * width, width), width)
    for spot, message in (
        (half, far_own_ref), (1 - half, far_pair_ref), (2 + half, back_own_ref), (3 - half, back_pair_ref)
    ):
        win_ref[pl.ds(pl.multiple_of(spot * BLK, BLK), BLK), :] = message[:BLK]
        extra_ref[spot] = message[BLK:].astype(jnp.float32)
    marks = edge_marks(seq_ref)
    for spot in (1, 2):
        rows = first_rows(extra_ref[spot, :8], extra_ref[spot - 1, :8], w_ref, half_lanes, marks, spot)
        put_first_rows(win_ref, spot * BLK, rows)
    if deep:
        ahead = messages[4][...].astype(jnp.float32)[:8]
        put_first_rows(win_ref, 0, first_rows(extra_ref[0, :8], ahead, w_ref, half_lanes, marks, 0))
    for part in range(2):
        squares = jnp.zeros((BLK, GROUP), jnp.float32)
        rows = slice(part * BLK, (part + 1) * BLK)
        for g in range(groups):
            lanes = slice(g * GROUP, (g + 1) * GROUP)
            filtered = acc_ref[rows, lanes] + jnp.dot(
                table_ref[g, part, :, : (3 - part) * BLK],
                win_ref[part * BLK : 3 * BLK, lanes],
                preferred_element_type=jnp.float32,
            )
            gated = q_ref[rows, lanes] * filtered
            squares = squares + gated * gated

            @pl.when(half == part)
            def _():
                kept_ref[:, lanes] = gated

            @pl.when(half != part)
            def _():
                sent_ref[:, lanes] = gated.astype(sent_ref.dtype)

        sq_ref[rows, :] = squares
    power_ref[...] = lax.dot_general(
        jnp.ones((8, GROUP), jnp.float32),
        sq_ref[...],
        (((1,), (1,)), ((), ())),
        precision=lax.Precision.HIGHEST,
        preferred_element_type=jnp.float32,
    )[0:1]


def norm_kernel(channels, power_ref, power_got_ref, kept_ref, got_ref, gain_ref, out_ref):
    half = lax.axis_index("half")
    width = kept_ref.shape[1]
    mine = pl.ds(pl.multiple_of(half * BLK, BLK), BLK)
    power = power_ref[:, mine] + power_got_ref[:, mine]
    scale = lax.rsqrt(power / channels + norm_eps)
    diagonal = lax.broadcasted_iota(jnp.int32, (BLK, BLK), 0) == lax.broadcasted_iota(
        jnp.int32, (BLK, BLK), 1
    )
    column = jnp.sum(jnp.where(diagonal, scale, 0.0), axis=1, keepdims=True)
    for which, part_ref in ((half, kept_ref), (1 - half, got_ref)):
        for c in range(0, width, GROUP):
            lanes = pl.ds(pl.multiple_of(which * width + c, GROUP), GROUP)
            out_ref[:, lanes] = (
                part_ref[:, c : c + GROUP].astype(jnp.float32) * column * gain_ref[:, lanes]
            ).astype(out_ref.dtype)


def kernel_call(body, outs, in_specs, scratch, flops, moved_bytes):
    return pl.pallas_call(
        body,
        out_shape=outs,
        in_specs=in_specs,
        out_specs=jax.tree.map(lambda _: VMEM, outs),
        scratch_shapes=scratch,
        compiler_params=pltpu.CompilerParams(vmem_limit_bytes=24 << 20),
        cost_estimate=pl.CostEstimate(flops=flops, bytes_accessed=moved_bytes, transcendentals=0),
    )


def shards(blocks, whole_tokens, channels, projected, short_weight, filter_taps, tap_blocks, skip_bias, norm_gain, seq_lengths):
    rows = projected.shape[0]
    width = projected.shape[2] // 2
    groups = width // GROUP
    taps = filter_taps.shape[1]
    shape = jax.ShapeDtypeStruct
    half_shape = shape((rows, width), jnp.bfloat16)
    half_wide = shape((rows, width), jnp.float32)

    spots = range(2 * blocks)
    to_pair = [(i, i ^ 1) for i in spots]
    ahead = [(i, (i + 2) % (2 * blocks)) for i in spots]
    ahead_pair = [(i, ((i ^ 1) + 2) % (2 * blocks)) for i in spots]

    panels = jnp.transpose(projected, (1, 0, 2))
    message = shape((rows + 16, width), jnp.bfloat16)
    any_space = pl.BlockSpec(memory_space=pl.ANY)
    pieces = 4
    row_mask = pltpu.VMEM((rows, GROUP), jnp.float32)

    sent, kept, qsent, qkept = kernel_call(
        products_kernel,
        (message, message, half_shape, half_shape),
        [any_space] * 3,
        [
            pltpu.SMEM(seq_lengths.shape, jnp.int32),
            pltpu.VMEM((pieces, 2, rows, 2 * width // pieces), jnp.bfloat16),
            pltpu.VMEM(short_weight.shape, jnp.float32),
            pltpu.VMEM((4, rows + 8, GROUP), jnp.float32),
            row_mask,
            row_mask,
            pltpu.SemaphoreType.DMA((4 + pieces,)),
        ],
        40 * rows * width,
        16 * rows * width,
    )(seq_lengths, panels, short_weight)

    back_own = moved(kept, ahead)
    back_pair = moved(sent, ahead_pair)

    filter_taps, _ = lax.optimization_barrier((filter_taps, kept))
    scaled = (filter_taps * jnp.repeat(tap_blocks.astype(jnp.float32), BLK, axis=1)).astype(jnp.bfloat16)
    table = kernel_call(
        tables_kernel,
        shape((groups, 2, BLK, taps + BLK), jnp.bfloat16),
        [SMEM, VMEM],
        [pltpu.VMEM((2 * groups, taps + 2 * BLK), jnp.float32), pltpu.VMEM((2, BLK, taps + BLK), jnp.float32)],
        40 * groups * BLK * taps,
        8 * groups * BLK * taps,
    )(seq_lengths, scaled)

    table, back_own = lax.optimization_barrier((table, back_own))
    far_own = moved(back_own, ahead)
    far_pair = moved(back_pair, ahead)
    sent_late, qsent, back_pair = lax.optimization_barrier((sent, qsent, back_pair))
    pair = moved(sent_late, to_pair)
    qgot = moved(qsent, to_pair)
    extras = ()
    if whole_tokens // 2 > taps:
        half = lax.axis_index("half")
        straight = moved(kept[rows:], [(i, (i + 6) % (2 * blocks)) for i in spots])
        across = moved(sent[rows:], [(i, ((i ^ 1) + 6) % (2 * blocks)) for i in spots])
        extras = (jnp.where(half == 1, straight, across),)

    acc, q = kernel_call(
        near_kernel,
        (shape((2 * rows, width), jnp.float32), shape((2 * rows, width), jnp.float32)),
        [SMEM] + [VMEM] * 9,
        [
            pltpu.VMEM((4 * rows, width), jnp.bfloat16),
            pltpu.VMEM((4, 16, width), jnp.float32),
            pltpu.VMEM((2, rows + 8, GROUP), jnp.float32),
            row_mask,
            row_mask,
        ],
        2 * 5 * rows * BLK * width,
        16 * rows * width,
    )(seq_lengths, table, kept, pair, back_own, back_pair, qkept, qgot, short_weight, skip_bias.reshape(1, -1))

    done, send, power = kernel_call(
        functools.partial(far_kernel, len(extras)),
        (half_wide, half_shape, shape((1, 2 * rows), jnp.float32)),
        [SMEM] + [VMEM] * (8 + len(extras)),
        [
            pltpu.VMEM((4 * rows, width), jnp.bfloat16),
            pltpu.VMEM((4, 16, width), jnp.float32),
            pltpu.VMEM((2 * rows, GROUP), jnp.float32),
        ],
        2 * 5 * rows * BLK * width,
        24 * rows * width,
    )(seq_lengths, table, acc, q, short_weight, back_own, back_pair, far_own, far_pair, *extras)

    back = moved(send, to_pair)
    peers = lax.axis_size("mp")
    shares = [lax.ppermute(power, "mp", [(i, i ^ k) for i in range(peers)]) for k in range(1, peers)]
    power = sum(shares, power)
    return kernel_call(
        functools.partial(norm_kernel, channels),
        shape((rows, 2 * width), jnp.bfloat16),
        [VMEM] * 5,
        [],
        8 * rows * width,
        10 * rows * width,
    )(power, moved(power, to_pair), done, back, norm_gain.reshape(1, -1))


def solution(mesh):
    blocks = mesh.shape["ctx"] // 2
    grid = Mesh(mesh.devices.reshape(blocks, 2, mesh.shape["mp"]), ("blk", "half", "mp"))
    in_specs = (
        P(SPOTS, None, "mp"),
        P(None, None, "mp"),
        P("mp", None),
        P("mp", None),
        P("mp"),
        P("mp"),
        P(),
    )

    def program(projected, *rest):
        body = functools.partial(shards, blocks, projected.shape[0], projected.shape[2])
        return jax.shard_map(
            body, mesh=grid, in_specs=in_specs, out_specs=P(SPOTS, "mp"), check_vma=False
        )(projected, *rest)

    return program
```

time: 57.9 us -> 54.5 us (0.941)
  waiting for transfers between devices: 3.83 us -> 22.4 us
  starting transfers between devices: 25.9 us -> 13.3 us
  blocking collectives: 11.9 us -> 0 us
  Pallas kernels: 9.56 us -> 13.2 us
  local copies, waits for them, and re-layouts: 4.71 us -> 3.78 us
    ppermute x8, waiting for transfers between devices: 3.83 us -> 20 us  [moved(): return lax.ppermute(block, SPOTS, pairs)]
    ppermute x8, starting transfers between devices: 25.9 us -> 11.5 us  [moved(): return lax.ppermute(block, SPOTS, pairs)]
    psum x1 -> x0, blocking collectives: 11.9 us -> none  [shards(): power = lax.psum(power, ('half', 'mp'))]
    pallas_call x3, Pallas kernels: 4.94 us -> 8.58 us  [the longest x1 4.21 us: shards(): kernel_call(functools.partial(far_kernel, len(extras)), (half_wide, half_...]
    ppermute x0 -> x3, waiting for transfers between devices: none -> 2.44 us  [shards(): lax.ppermute(power, 'mp', [(i, i ^ k) for i in range(peers)])]
    ppermute x0 -> x3, starting transfers between devices: none -> 1.86 us  [shards(): lax.ppermute(power, 'mp', [(i, i ^ k) for i in range(peers)])]
    slice x1 -> x0, local copies, waits for them, and re-layouts: 0.93 us -> none  [shards(): edge = moved(panels[:, rows - 2:], to_next)]
    unnamed x12 -> x14, local copies, waits for them, and re-layouts: 3.62 us -> 3.62 us
  transfers between devices with their start and end apart: 8 -> 11, of which waited for: 3 -> 7; matrix products, arithmetic and copies ran while one was open for 3% -> 3% of each run, Pallas kernels for 8% -> 11%
where the time goes in v2:
time: 54.5 us; the launch traced here: 54.3 us
  waiting for transfers between devices  22.4 us (41%)
  starting transfers between devices  13.3 us (24%)
  Pallas kernels  13.2 us (24%)
  local copies, waits for them, and re-layouts  3.78 us (7%)
  other arithmetic  1.46 us (3%)
    ppermute x8, waiting for transfers between devices, moved(): return lax.ppermute(block, SPOTS, pairs)  20 us
    ppermute x8, starting transfers between devices, moved(): return lax.ppermute(block, SPOTS, pairs)  11.5 us
    pallas_call x1, Pallas kernels, shards(): kernel_call(functools.partial(far_kernel, len(extras)), (half_wide, half_...  4.21 us
    unnamed x14, local copies, waits for them, and re-layouts  3.62 us
    pallas_call x1, Pallas kernels, shards(): kernel_call(tables_kernel, shape((groups, 2, BLK, taps + BLK), jnp.bfloat...  3.56 us
    pallas_call x1, Pallas kernels, shards(): kernel_call(near_kernel, (shape((2 * rows, width), jnp.float32), shape((2...  2.52 us
    ppermute x3, waiting for transfers between devices, shards(): lax.ppermute(power, 'mp', [(i, i ^ k) for i in range(peers)])  2.44 us
    ppermute x3, starting transfers between devices, shards(): lax.ppermute(power, 'mp', [(i, i ^ k) for i in range(peers)])  1.86 us
  transfers between devices with their start and end apart: 11, of which 7 were waited for; matrix products, arithmetic and copies ran while one was open for 3% of the time, Pallas kernels for 11%

profile of v2, /device:TPU:0, one launch (start us, length us, event | category | flops | bytes accessed | tf_op | source)
XLA Modules:
  0.0 54.3 jit_solution(5621728266326240830)
XLA Ops:
  0.0 0.0 copy-start
  0.0 1.4 %copy-done = bf16[128,3,2048]{2,0,1:T(8,128)(2,1)S(1)} copy-done((bf16[128,3,2048]{2,0,1:T(8,128)(2,1)S(1)}, bf16[128,3,2048]{2,0,1:T(8,128)(2,1)}, u32[]{:S(2)}) %copy-start) | copy-done | bytes 1572888
  1.4 0.0 copy-start.1
  1.4 0.9 %copy-done.1 = f32[3,3,2048]{2,1,0:T(4,128)S(1)} copy-done((f32[3,3,2048]{2,1,0:T(4,128)S(1)}, f32[3,3,2048]{2,1,0:T(4,128)}, u32[]{:S(2)}) %copy-start.1) | copy-done | bytes 73752
  2.3 0.0 copy-start.5
  2.3 0.7 %copy-done.5 = s32[32]{0:T(128)S(1)} copy-done((s32[32]{0:T(128)S(1)}, s32[32]{0:T(128)}, u32[]{:S(2)}) %copy-start.5) | copy-done | bytes 152
  3.0 0.0 copy-start.2
  3.0 0.0 copy-start.3
  3.0 1.8 %shard_map.73 = (bf16[144,1024]{1,0:T(8,128)(2,1)S(1)}, bf16[144,1024]{1,0:T(8,128)(2,1)S(1)}, bf16[128,1024]{1,0:T(8,128)(2,1)S(1)}, bf16[128,1024]{1,0:T(8,128)(2,1)S(1)}) custom-call(s32[32]{0:T(128)S(1)} %copy-done.5, bf16[3,128,2048]{2,1,0:T(8,128)(2,1)S(1)} %bitcast.8, f32[3,3,2048]{2,1,0:T(4,128)S(1)} %copy-done.1), custom_call_target="tpu_custom_call" | custom-call | flops 5242880 | bytes 2097152 | tf_op jit(solution)/shard_map/pallas_call | solution.py:322
  4.8 4.0 %collective-permute-start.1 = (bf16[144,1024]{1,0:T(8,128)(2,1)S(1)}, bf16[144,1024]{1,0:T(8,128)(2,1)S(1)}, u32[]{:S(2)}, u32[]{:S(2)}) collective-permute-start(bf16[144,1024]{1,0:T(8,128)(2,1)S(1)} %get-tuple-element.25), channel_id=1, source_target_pairs={{0,12},{4,8},{8,20},{12,16},{16,28},{20,24},{24,4},{28,0},{1,13},{... | collective-permute-start | bytes 884744 | tf_op jit(solution)/shard_map/ppermute | solution.py:20
  8.9 1.6 %collective-permute-start = (bf16[144,1024]{1,0:T(8,128)(2,1)S(1)}, bf16[144,1024]{1,0:T(8,128)(2,1)S(1)}, u32[]{:S(2)}, u32[]{:S(2)}) collective-permute-start(bf16[144,1024]{1,0:T(8,128)(2,1)S(1)} %get-tuple-element.20.own_ref), channel_id=1, source_target_pairs={{0,8},{4,12},{8,16},{12,20},{16,24},{20,28},{24,0},{28,4},{1,9},{5... | collective-permute-start | bytes 884744 | tf_op jit(solution)/shard_map/ppermute | solution.py:20
  10.4 0.7 %convert_element_type.6 = f32[16,4]{0,1:T(4,128)S(1)} convert(s32[16,4]{0,1:T(4,128)} %param.10) | non-fusion elementwise | flops 64 | bytes 512 | tf_op jit(solution)/shard_map/convert_element_type | solution.py:343
  11.1 0.1 copy.8
  11.2 7.5 %collective-permute-done.1.back_pair_ref.refs_1_ = bf16[144,1024]{1,0:T(8,128)(2,1)S(1)} collective-permute-done((bf16[144,1024]{1,0:T(8,128)(2,1)S(1)}, bf16[144,1024]{1,0:T(8,128)(2,1)S(1)}, u32[]{:S(2)}, u32[]{:S(2)}) %collective-permute-start.1) | collective-permute-done | bytes 294944 | tf_op jit(solution)/shard_map/ppermute | solution.py:20
  18.7 1.7 %collective-permute-start.2 = (bf16[144,1024]{1,0:T(8,128)(2,1)S(1)}, bf16[144,1024]{1,0:T(8,128)(2,1)S(1)}, u32[]{:S(2)}, u32[]{:S(2)}) collective-permute-start(bf16[144,1024]{1,0:T(8,128)(2,1)S(1)} %get-tuple-element.25), channel_id=1, source_target_pairs={{0,4},{4,0},{8,12},{12,8},{16,20},{20,16},{24,28},{28,24},{1,5},{5... | collective-permute-start | bytes 884744 | tf_op jit(solution)/shard_map/ppermute | solution.py:20
  20.4 0.1 broadcast_in_dim.3
  20.5 0.8 %fusion.taps_ref = bf16[16,512]{1,0:T(8,128)(2,1)S(1)} fusion(f32[16,512]{1,0:T(8,128)} %param.9, f32[2,8,4,128]{3,2,1,0:T(4,128)S(1)} %bitcast.11), kind=kLoop, calls=%fused_computation.1 | loop fusion | flops 16384 | bytes 81920 | tf_op jit(solution)/shard_map/convert_element_type | solution.py:343
  21.3 0.0 copy-start.6
  21.3 0.7 %copy-done.6 = s32[32]{0:T(128)S(1)} copy-done((s32[32]{0:T(128)S(1)}, s32[32]{0:T(128)}, u32[]{:S(2)}) %copy-start.6) | copy-done | bytes 152
  21.9 3.6 %shard_map.74.table_ref = bf16[8,2,128,640]{3,2,1,0:T(8,128)(2,1)S(1)} custom-call(s32[32]{0:T(128)S(1)} %copy-done.6, bf16[16,512]{1,0:T(8,128)(2,1)S(1)} %fusion.taps_ref), custom_call_target="tpu_custom_call" | custom-call | flops 20971520 | bytes 4194304 | tf_op jit(solution)/shard_map/pallas_call | solution.py:344
  25.5 0.0 collective-permute-done.back_own_ref.refs_0_
  25.5 0.1 collective-permute-start.4
  25.6 1.3 %collective-permute-start.5 = (bf16[144,1024]{1,0:T(8,128)(2,1)S(1)}, bf16[144,1024]{1,0:T(8,128)(2,1)S(1)}, u32[]{:S(2)}, u32[]{:S(2)}) collective-permute-start(bf16[144,1024]{1,0:T(8,128)(2,1)S(1)} %collective-permute-done.1.back_pair_ref.refs_1_), channel_id=1, source_target_pairs={{0,8},{4,12},{8,16},{12,20},{16,24},{20,28},{24,0},{28,4},{1,9},{5... | collective-permute-start | bytes 884744 | tf_op jit(solution)/shard_map/ppermute | solution.py:20
  26.9 0.5 collective-permute-start.3
  27.4 5.9 %collective-permute-done.3.qgot_ref = bf16[128,1024]{1,0:T(8,128)(2,1)S(1)} collective-permute-done((bf16[128,1024]{1,0:T(8,128)(2,1)S(1)}, bf16[128,1024]{1,0:T(8,128)(2,1)S(1)}, u32[]{:S(2)}, u32[]{:S(2)}) %collective-permute-start.3) | collective-permute-done | bytes 262176 | tf_op jit(solution)/shard_map/ppermute | solution.py:20
  33.3 0.0 collective-permute-done.2.pair_ref
  33.3 0.0 copy-done.2
  33.3 0.0 copy-done.3
  33.3 2.5 %shard_map.75 = (f32[256,1024]{1,0:T(8,128)S(1)}, f32[256,1024]{1,0:T(8,128)S(1)}) custom-call(s32[32]{0:T(128)S(1)} %copy-done.6, bf16[8,2,128,640]{3,2,1,0:T(8,128)(2,1)S(1)} %shard_map.74.table_ref, bf16[144,1024]{1,0:T(8,128)(2,1)S(1)} %get-tuple-element.20.own_ref, bf16[144,1024]{1,0:T(8,128)(2,1)S(1)} %collective-permute-done.2.pair_ref, ...), custom_call_target="tpu_custom_call" | custom-call | flops 167772160 | bytes 2097152 | tf_op jit(solution)/shard_map/pallas_call | solution.py:366
  35.8 1.1 %collective-permute-done.4.refs_2_ = bf16[144,1024]{1,0:T(8,128)(2,1)S(1)} collective-permute-done((bf16[144,1024]{1,0:T(8,128)(2,1)S(1)}, bf16[144,1024]{1,0:T(8,128)(2,1)S(1)}, u32[]{:S(2)}, u32[]{:S(2)}) %collective-permute-start.4) | collective-permute-done | bytes 294944 | tf_op jit(solution)/shard_map/ppermute | solution.py:20
  37.0 3.2 %collective-permute-done.5.refs_3_ = bf16[144,1024]{1,0:T(8,128)(2,1)S(1)} collective-permute-done((bf16[144,1024]{1,0:T(8,128)(2,1)S(1)}, bf16[144,1024]{1,0:T(8,128)(2,1)S(1)}, u32[]{:S(2)}, u32[]{:S(2)}) %collective-permute-start.5) | collective-permute-done | bytes 294944 | tf_op jit(solution)/shard_map/ppermute | solution.py:20
  40.1 0.0 copy-start.4
  40.1 4.2 %shard_map.76 = (f32[128,1024]{1,0:T(8,128)S(1)}, bf16[128,1024]{1,0:T(8,128)(2,1)S(1)}, f32[1,256]{1,0:T(1,128)S(1)}) custom-call(s32[32]{0:T(128)S(1)} %copy-done.6, bf16[8,2,128,640]{3,2,1,0:T(8,128)(2,1)S(1)} %shard_map.74.table_ref, f32[256,1024]{1,0:T(8,128)S(1)} %get-tuple-element.30.acc_ref, f32[256,1024]{1,0:T(8,128)S(1)} %get-tuple-element.31.q_ref, ...), custom_call_target="tpu_custom_call" | custom-call | flops 167772160 | bytes 3145728 | tf_op jit(solution)/shard_map/pallas_call | solution.py:381
  44.4 1.0 %collective-permute-start.10 = (bf16[128,1024]{1,0:T(8,128)(2,1)S(1)}, bf16[128,1024]{1,0:T(8,128)(2,1)S(1)}, u32[]{:S(2)}, u32[]{:S(2)}) collective-permute-start(bf16[128,1024]{1,0:T(8,128)(2,1)S(1)} %get-tuple-element.34), channel_id=1, source_target_pairs={{0,4},{4,0},{8,12},{12,8},{16,20},{20,16},{24,28},{28,24},{1,5},{5... | collective-permute-start | bytes 786440 | tf_op jit(solution)/shard_map/ppermute | solution.py:20
  45.3 0.0 collective-permute-start.6
  45.3 1.3 %collective-permute-start.7 = (f32[1,256]{1,0:T(1,128)S(1)}, f32[1,256]{1,0:T(1,128)S(1)}, u32[]{:S(2)}, u32[]{:S(2)}) collective-permute-start(f32[1,256]{1,0:T(1,128)S(1)} %get-tuple-element.32), channel_id=1, source_target_pairs={{0,2},{1,3},{2,0},{3,1},{4,6},{5,7},{6,4},{7,5},{8,10},{9,11},{10,... | collective-permute-start | bytes 3080 | tf_op jit(solution)/shard_map/ppermute | solution.py:396
  46.6 0.6 %collective-permute-start.8 = (f32[1,256]{1,0:T(1,128)S(1)}, f32[1,256]{1,0:T(1,128)S(1)}, u32[]{:S(2)}, u32[]{:S(2)}) collective-permute-start(f32[1,256]{1,0:T(1,128)S(1)} %get-tuple-element.32), channel_id=1, source_target_pairs={{0,3},{1,2},{2,1},{3,0},{4,7},{5,6},{6,5},{7,4},{8,11},{9,10},{10,... | collective-permute-start | bytes 3080 | tf_op jit(solution)/shard_map/ppermute | solution.py:396
  47.2 0.0 collective-permute-done.6
  47.2 1.7 %collective-permute-done.7 = f32[1,256]{1,0:T(1,128)S(1)} collective-permute-done((f32[1,256]{1,0:T(1,128)S(1)}, f32[1,256]{1,0:T(1,128)S(1)}, u32[]{:S(2)}, u32[]{:S(2)}) %collective-permute-start.7) | collective-permute-done | bytes 1056 | tf_op jit(solution)/shard_map/ppermute | solution.py:396
  48.9 0.7 %collective-permute-done.8 = f32[1,256]{1,0:T(1,128)S(1)} collective-permute-done((f32[1,256]{1,0:T(1,128)S(1)}, f32[1,256]{1,0:T(1,128)S(1)}, u32[]{:S(2)}, u32[]{:S(2)}) %collective-permute-start.8) | collective-permute-done | bytes 1056 | tf_op jit(solution)/shard_map/ppermute | solution.py:396
  49.6 1.3 %collective-permute-start.9 = (f32[1,256]{1,0:T(1,128)S(1)}, f32[1,256]{1,0:T(1,128)S(1)}, u32[]{:S(2)}, u32[]{:S(2)}) collective-permute-start(f32[1,256]{1,0:T(1,128)S(1)} %add_add_fusion.power_ref), channel_id=1, source_target_pairs={{0,4},{4,0},{8,12},{12,8},{16,20},{20,16},{24,28},{28,24},{1,5},{5... | collective-permute-start | bytes 3080 | tf_op jit(solution)/shard_map/ppermute | solution.py:20
  50.9 2.3 %collective-permute-done.9.power_got_ref = f32[1,256]{1,0:T(1,128)S(1)} collective-permute-done((f32[1,256]{1,0:T(1,128)S(1)}, f32[1,256]{1,0:T(1,128)S(1)}, u32[]{:S(2)}, u32[]{:S(2)}) %collective-permute-start.9) | collective-permute-done | bytes 1056 | tf_op jit(solution)/shard_map/ppermute | solution.py:20
  53.2 0.0 collective-permute-done.10.got_ref
  53.2 0.0 copy-done.4
  53.2 1.1 %shard_map.77 = bf16[128,2048]{1,0:T(8,128)(2,1)} custom-call(f32[1,256]{1,0:T(1,128)S(1)} %add_add_fusion.power_ref, f32[1,256]{1,0:T(1,128)S(1)} %collective-permute-done.9.power_got_ref, f32[128,1024]{1,0:T(8,128)S(1)} %get-tuple-element.33.kept_ref, bf16[128,1024]{1,0:T(8,128)(2,1)S(1)} %collective-permute-done.10.got_ref, f32[1,2048]{1,0:T(1,128)S(1)} %bitcast.10), custom_call_target="tpu_custom_call" | custom-call | flops 1048576 | bytes 1310720 | tf_op jit(solution)/shard_map/pallas_call | solution.py:398
  (1 shorter events, 0.0 us)
Async XLA Ops:
  0.0 1.4 %copy-start = (bf16[128,3,2048]{2,0,1:T(8,128)(2,1)S(1)}, bf16[128,3,2048]{2,0,1:T(8,128)(2,1)}, u32[]{:S(2)}) copy-start(bf16[128,3,2048]{2,0,1:T(8,128)(2,1)} %param.7) | copy-start | bytes 4718596
  1.4 0.9 %copy-start.1 = (f32[3,3,2048]{2,1,0:T(4,128)S(1)}, f32[3,3,2048]{2,1,0:T(4,128)}, u32[]{:S(2)}) copy-start(f32[3,3,2048]{2,1,0:T(4,128)} %w_ref.3) | copy-start | bytes 221188
  2.3 0.7 %copy-start.5 = (s32[32]{0:T(128)S(1)}, s32[32]{0:T(128)}, u32[]{:S(2)}) copy-start(s32[32]{0:T(128)} %seq_ref.5) | copy-start | bytes 388
  3.0 30.3 %copy-start.2 = (f32[3,3,2048]{2,1,0:T(4,128)S(1)}, f32[3,3,2048]{2,1,0:T(4,128)}, u32[]{:S(2)}) copy-start(f32[3,3,2048]{2,1,0:T(4,128)} %w_ref.3) | copy-start | bytes 221188
  3.0 30.3 %copy-start.3 = (f32[2048]{0:T(1024)S(1)}, f32[2048]{0:T(1024)}, u32[]{:S(2)}) copy-start(f32[2048]{0:T(1024)} %param.11) | copy-start | bytes 24580
  4.8 13.9 %collective-permute-start.1 = (bf16[144,1024]{1,0:T(8,128)(2,1)S(1)}, bf16[144,1024]{1,0:T(8,128)(2,1)S(1)}, u32[]{:S(2)}, u32[]{:S(2)}) collective-permute-start(bf16[144,1024]{1,0:T(8,128)(2,1)S(1)} %get-tuple-element.25), channel_id=1, source_target_pairs={{0,12},{4,8},{8,20},{12,16},{16,28},{20,24},{24,4},{28,0},{1,13},{... | collective-permute-start | bytes 884744 | tf_op jit(solution)/shard_map/ppermute | solution.py:20
  8.9 16.7 %collective-permute-start = (bf16[144,1024]{1,0:T(8,128)(2,1)S(1)}, bf16[144,1024]{1,0:T(8,128)(2,1)S(1)}, u32[]{:S(2)}, u32[]{:S(2)}) collective-permute-start(bf16[144,1024]{1,0:T(8,128)(2,1)S(1)} %get-tuple-element.20.own_ref), channel_id=1, source_target_pairs={{0,8},{4,12},{8,16},{12,20},{16,24},{20,28},{24,0},{28,4},{1,9},{5... | collective-permute-start | bytes 884744 | tf_op jit(solution)/shard_map/ppermute | solution.py:20
  18.7 14.6 %collective-permute-start.2 = (bf16[144,1024]{1,0:T(8,128)(2,1)S(1)}, bf16[144,1024]{1,0:T(8,128)(2,1)S(1)}, u32[]{:S(2)}, u32[]{:S(2)}) collective-permute-start(bf16[144,1024]{1,0:T(8,128)(2,1)S(1)} %get-tuple-element.25), channel_id=1, source_target_pairs={{0,4},{4,0},{8,12},{12,8},{16,20},{20,16},{24,28},{28,24},{1,5},{5... | collective-permute-start | bytes 884744 | tf_op jit(solution)/shard_map/ppermute | solution.py:20
  21.3 0.7 %copy-start.6 = (s32[32]{0:T(128)S(1)}, s32[32]{0:T(128)}, u32[]{:S(2)}) copy-start(s32[32]{0:T(128)} %seq_ref.5) | copy-start | bytes 388
  25.5 11.5 %collective-permute-start.4 = (bf16[144,1024]{1,0:T(8,128)(2,1)S(1)}, bf16[144,1024]{1,0:T(8,128)(2,1)S(1)}, u32[]{:S(2)}, u32[]{:S(2)}) collective-permute-start(bf16[144,1024]{1,0:T(8,128)(2,1)S(1)} %collective-permute-done.back_own_ref.refs_0_), channel_id=1, source_target_pairs={{0,8},{4,12},{8,16},{12,20},{16,24},{20,28},{24,0},{28,4},{1,9},{5... | collective-permute-start | bytes 884744 | tf_op jit(solution)/shard_map/ppermute | solution.py:20
  25.6 14.6 %collective-permute-start.5 = (bf16[144,1024]{1,0:T(8,128)(2,1)S(1)}, bf16[144,1024]{1,0:T(8,128)(2,1)S(1)}, u32[]{:S(2)}, u32[]{:S(2)}) collective-permute-start(bf16[144,1024]{1,0:T(8,128)(2,1)S(1)} %collective-permute-done.1.back_pair_ref.refs_1_), channel_id=1, source_target_pairs={{0,8},{4,12},{8,16},{12,20},{16,24},{20,28},{24,0},{28,4},{1,9},{5... | collective-permute-start | bytes 884744 | tf_op jit(solution)/shard_map/ppermute | solution.py:20
  26.9 6.4 %collective-permute-start.3 = (bf16[128,1024]{1,0:T(8,128)(2,1)S(1)}, bf16[128,1024]{1,0:T(8,128)(2,1)S(1)}, u32[]{:S(2)}, u32[]{:S(2)}) collective-permute-start(bf16[128,1024]{1,0:T(8,128)(2,1)S(1)} %get-tuple-element.29), channel_id=1, source_target_pairs={{0,4},{4,0},{8,12},{12,8},{16,20},{20,16},{24,28},{28,24},{1,5},{5... | collective-permute-start | bytes 786440 | tf_op jit(solution)/shard_map/ppermute | solution.py:20
  40.1 13.1 %copy-start.4 = (f32[2048]{0:T(1024)S(1)}, f32[2048]{0:T(1024)}, u32[]{:S(2)}) copy-start(f32[2048]{0:T(1024)} %param.12) | copy-start | bytes 24580
  44.4 8.9 %collective-permute-start.10 = (bf16[128,1024]{1,0:T(8,128)(2,1)S(1)}, bf16[128,1024]{1,0:T(8,128)(2,1)S(1)}, u32[]{:S(2)}, u32[]{:S(2)}) collective-permute-start(bf16[128,1024]{1,0:T(8,128)(2,1)S(1)} %get-tuple-element.34), channel_id=1, source_target_pairs={{0,4},{4,0},{8,12},{12,8},{16,20},{20,16},{24,28},{28,24},{1,5},{5... | collective-permute-start | bytes 786440 | tf_op jit(solution)/shard_map/ppermute | solution.py:20
  45.3 1.9 %collective-permute-start.6 = (f32[1,256]{1,0:T(1,128)S(1)}, f32[1,256]{1,0:T(1,128)S(1)}, u32[]{:S(2)}, u32[]{:S(2)}) collective-permute-start(f32[1,256]{1,0:T(1,128)S(1)} %get-tuple-element.32), channel_id=1, source_target_pairs={{0,1},{1,0},{2,3},{3,2},{4,5},{5,4},{6,7},{7,6},{8,9},{9,8},{10,11... | collective-permute-start | bytes 3080 | tf_op jit(solution)/shard_map/ppermute | solution.py:396
  45.3 3.6 %collective-permute-start.7 = (f32[1,256]{1,0:T(1,128)S(1)}, f32[1,256]{1,0:T(1,128)S(1)}, u32[]{:S(2)}, u32[]{:S(2)}) collective-permute-start(f32[1,256]{1,0:T(1,128)S(1)} %get-tuple-element.32), channel_id=1, source_target_pairs={{0,2},{1,3},{2,0},{3,1},{4,6},{5,7},{6,4},{7,5},{8,10},{9,11},{10,... | collective-permute-start | bytes 3080 | tf_op jit(solution)/shard_map/ppermute | solution.py:396
  46.6 3.0 %collective-permute-start.8 = (f32[1,256]{1,0:T(1,128)S(1)}, f32[1,256]{1,0:T(1,128)S(1)}, u32[]{:S(2)}, u32[]{:S(2)}) collective-permute-start(f32[1,256]{1,0:T(1,128)S(1)} %get-tuple-element.32), channel_id=1, source_target_pairs={{0,3},{1,2},{2,1},{3,0},{4,7},{5,6},{6,5},{7,4},{8,11},{9,10},{10,... | collective-permute-start | bytes 3080 | tf_op jit(solution)/shard_map/ppermute | solution.py:396
  49.6 3.6 %collective-permute-start.9 = (f32[1,256]{1,0:T(1,128)S(1)}, f32[1,256]{1,0:T(1,128)S(1)}, u32[]{:S(2)}, u32[]{:S(2)}) collective-permute-start(f32[1,256]{1,0:T(1,128)S(1)} %add_add_fusion.power_ref), channel_id=1, source_target_pairs={{0,4},{4,0},{8,12},{12,8},{16,20},{20,16},{24,28},{28,24},{1,5},{5... | collective-permute-start | bytes 3080 | tf_op jit(solution)/shard_map/ppermute | solution.py:20

commit v3 on v2

--- a/solution.py
+++ b/solution.py
@@ -28,7 +28,7 @@
 
     first = (t == 0).astype(jnp.int32)
     second = (t == 1).astype(jnp.int32)
-    _, first, second = lax.fori_loop(0, seq_ref.shape[0], step, (jnp.int32(0), first, second))
+    _, first, second = lax.fori_loop(0, seq_ref.shape[0], step, (jnp.int32(0), first, second), unroll=True)
     return first, first | second
 
 
@@ -49,7 +49,7 @@
         return end, total + (end <= t).astype(jnp.int32)
 
     _, total = lax.fori_loop(
-        0, seq_ref.shape[0], step, (jnp.int32(0), jnp.zeros(t.shape, jnp.int32))
+        0, seq_ref.shape[0], step, (jnp.int32(0), jnp.zeros(t.shape, jnp.int32)), unroll=True
     )
     return jnp.where(t >= 0, total, -1)
 
@@ -179,7 +179,7 @@
 
 def near_kernel(
     seq_ref, table_ref, own_ref, pair_ref, back_own_ref, back_pair_ref, qkept_ref, qgot_ref, w_ref, bias_ref,
-    acc_ref, q_ref, win_ref, extra_ref, x_ref, m1_ref, m2_ref,
+    acc_ref, q_ref, marks_ref, win_ref, extra_ref, x_ref, m1_ref, m2_ref,
 ):
     groups = table_ref.shape[0]
     width = groups * GROUP
@@ -190,6 +190,7 @@
         win_ref[pl.ds(pl.multiple_of(spot * BLK, BLK), BLK), :] = message[:BLK]
         extra_ref[spot] = message[BLK:].astype(jnp.float32)
     marks = edge_marks(seq_ref)
+    marks_ref[0], marks_ref[1] = marks
     for spot in (1, 2, 3):
         rows = first_rows(extra_ref[spot, :8], extra_ref[spot - 1, :8], w_ref, half_lanes, marks, spot + 2)
         put_first_rows(win_ref, spot * BLK, rows)
@@ -218,10 +219,10 @@
             )
 
 
-def far_kernel(deep, seq_ref, table_ref, acc_ref, q_ref, w_ref, *refs):
+def far_kernel(deep, table_ref, acc_ref, q_ref, w_ref, marks_ref, *refs):
     messages, refs = refs[: 4 + deep], refs[4 + deep :]
     back_own_ref, back_pair_ref, far_own_ref, far_pair_ref = messages[:4]
-    kept_ref, sent_ref, power_ref, win_ref, extra_ref, sq_ref = refs
+    kept_ref, sent_ref, power_ref, win_ref, extra_ref, gated_ref = refs
     groups = table_ref.shape[0]
     width = groups * GROUP
     half = lax.axis_index("half")
@@ -231,13 +232,14 @@
     ):
         win_ref[pl.ds(pl.multiple_of(spot * BLK, BLK), BLK), :] = message[:BLK]
         extra_ref[spot] = message[BLK:].astype(jnp.float32)
-    marks = edge_marks(seq_ref)
+    marks = [marks_ref[0], marks_ref[1]]
     for spot in (1, 2):
         rows = first_rows(extra_ref[spot, :8], extra_ref[spot - 1, :8], w_ref, half_lanes, marks, spot)
         put_first_rows(win_ref, spot * BLK, rows)
     if deep:
         ahead = messages[4][...].astype(jnp.float32)[:8]
         put_first_rows(win_ref, 0, first_rows(extra_ref[0, :8], ahead, w_ref, half_lanes, marks, 0))
+    power = []
     for part in range(2):
         squares = jnp.zeros((BLK, GROUP), jnp.float32)
         rows = slice(part * BLK, (part + 1) * BLK)
@@ -250,30 +252,27 @@
             )
             gated = q_ref[rows, lanes] * filtered
             squares = squares + gated * gated
-
-            @pl.when(half == part)
-            def _():
-                kept_ref[:, lanes] = gated
-
-            @pl.when(half != part)
-            def _():
-                sent_ref[:, lanes] = gated.astype(sent_ref.dtype)
-
-        sq_ref[rows, :] = squares
-    power_ref[...] = lax.dot_general(
-        jnp.ones((8, GROUP), jnp.float32),
-        sq_ref[...],
-        (((1,), (1,)), ((), ())),
-        precision=lax.Precision.HIGHEST,
-        preferred_element_type=jnp.float32,
-    )[0:1]
-
-
-def norm_kernel(channels, power_ref, power_got_ref, kept_ref, got_ref, gain_ref, out_ref):
+            gated_ref[rows, lanes] = gated
+        power.append(
+            lax.dot_general(
+                jnp.ones((8, GROUP), jnp.float32),
+                squares,
+                (((1,), (1,)), ((), ())),
+                precision=lax.Precision.HIGHEST,
+                preferred_element_type=jnp.float32,
+            )[0:1]
+        )
+    power_ref[...] = jnp.concatenate(power, 1)
+    kept_ref[...] = gated_ref[pl.ds(pl.multiple_of(half * BLK, BLK), BLK), :]
+    sent_ref[...] = gated_ref[pl.ds(pl.multiple_of((1 - half) * BLK, BLK), BLK), :].astype(sent_ref.dtype)
+
+
+def norm_kernel(channels, *refs):
     half = lax.axis_index("half")
+    *power_refs, kept_ref, got_ref, gain_ref, out_ref = refs
     width = kept_ref.shape[1]
     mine = pl.ds(pl.multiple_of(half * BLK, BLK), BLK)
-    power = power_ref[:, mine] + power_got_ref[:, mine]
+    power = sum(ref[:, mine] for ref in power_refs)
     scale = lax.rsqrt(power / channels + norm_eps)
     diagonal = lax.broadcasted_iota(jnp.int32, (BLK, BLK), 0) == lax.broadcasted_iota(
         jnp.int32, (BLK, BLK), 1
@@ -287,14 +286,14 @@
             ).astype(out_ref.dtype)
 
 
-def kernel_call(body, outs, in_specs, scratch, flops, moved_bytes):
+def kernel_call(body, outs, in_specs, scratch, flops, moved_bytes, vmem=24 << 20):
     return pl.pallas_call(
         body,
         out_shape=outs,
         in_specs=in_specs,
         out_specs=jax.tree.map(lambda _: VMEM, outs),
         scratch_shapes=scratch,
-        compiler_params=pltpu.CompilerParams(vmem_limit_bytes=24 << 20),
+        compiler_params=pltpu.CompilerParams(vmem_limit_bytes=vmem),
         cost_estimate=pl.CostEstimate(flops=flops, bytes_accessed=moved_bytes, transcendentals=0),
     )
 
@@ -315,14 +314,14 @@
 
     panels = jnp.transpose(projected, (1, 0, 2))
     message = shape((rows + 16, width), jnp.bfloat16)
-    any_space = pl.BlockSpec(memory_space=pl.ANY)
+    hbm = pl.BlockSpec(memory_space=pltpu.HBM)
     pieces = 4
     row_mask = pltpu.VMEM((rows, GROUP), jnp.float32)
 
     sent, kept, qsent, qkept = kernel_call(
         products_kernel,
         (message, message, half_shape, half_shape),
-        [any_space] * 3,
+        [hbm] * 3,
         [
             pltpu.SMEM(seq_lengths.shape, jnp.int32),
             pltpu.VMEM((pieces, 2, rows, 2 * width // pieces), jnp.bfloat16),
@@ -334,10 +333,12 @@
         ],
         40 * rows * width,
         16 * rows * width,
+        60 << 20,
     )(seq_lengths, panels, short_weight)
 
     back_own = moved(kept, ahead)
     back_pair = moved(sent, ahead_pair)
+    pair = moved(sent, to_pair)
 
     filter_taps, _ = lax.optimization_barrier((filter_taps, kept))
     scaled = (filter_taps * jnp.repeat(tap_blocks.astype(jnp.float32), BLK, axis=1)).astype(jnp.bfloat16)
@@ -352,9 +353,8 @@
 
     table, back_own = lax.optimization_barrier((table, back_own))
     far_own = moved(back_own, ahead)
+    table, back_pair, qsent = lax.optimization_barrier((table, back_pair, qsent))
     far_pair = moved(back_pair, ahead)
-    sent_late, qsent, back_pair = lax.optimization_barrier((sent, qsent, back_pair))
-    pair = moved(sent_late, to_pair)
     qgot = moved(qsent, to_pair)
     extras = ()
     if whole_tokens // 2 > taps:
@@ -363,9 +363,13 @@
         across = moved(sent[rows:], [(i, ((i ^ 1) + 6) % (2 * blocks)) for i in spots])
         extras = (jnp.where(half == 1, straight, across),)
 
-    acc, q = kernel_call(
+    acc, q, marks = kernel_call(
         near_kernel,
-        (shape((2 * rows, width), jnp.float32), shape((2 * rows, width), jnp.float32)),
+        (
+            shape((2 * rows, width), jnp.float32),
+            shape((2 * rows, width), jnp.float32),
+            shape((2, 8, GROUP), jnp.float32),
+        ),
         [SMEM] + [VMEM] * 9,
         [
             pltpu.VMEM((4 * rows, width), jnp.bfloat16),
@@ -381,28 +385,30 @@
     done, send, power = kernel_call(
         functools.partial(far_kernel, len(extras)),
         (half_wide, half_shape, shape((1, 2 * rows), jnp.float32)),
-        [SMEM] + [VMEM] * (8 + len(extras)),
+        [VMEM] * (9 + len(extras)),
         [
             pltpu.VMEM((4 * rows, width), jnp.bfloat16),
             pltpu.VMEM((4, 16, width), jnp.float32),
-            pltpu.VMEM((2 * rows, GROUP), jnp.float32),
+            pltpu.VMEM((2 * rows, width), jnp.float32),
         ],
         2 * 5 * rows * BLK * width,
         24 * rows * width,
-    )(seq_lengths, table, acc, q, short_weight, back_own, back_pair, far_own, far_pair, *extras)
+    )(table, acc, q, short_weight, marks, back_own, back_pair, far_own, far_pair, *extras)
 
     back = moved(send, to_pair)
     peers = lax.axis_size("mp")
-    shares = [lax.ppermute(power, "mp", [(i, i ^ k) for i in range(peers)]) for k in range(1, peers)]
-    power = sum(shares, power)
+    powers = [power] + [
+        lax.ppermute(power, SPOTS + ("mp",), [(i, i ^ k) for i in range(2 * blocks * peers)])
+        for k in range(1, 2 * peers)
+    ]
     return kernel_call(
         functools.partial(norm_kernel, channels),
         shape((rows, 2 * width), jnp.bfloat16),
-        [VMEM] * 5,
+        [VMEM] * (3 + len(powers)),
         [],
         8 * rows * width,
         10 * rows * width,
-    )(power, moved(power, to_pair), done, back, norm_gain.reshape(1, -1))
+    )(*powers, done, back, norm_gain.reshape(1, -1))
 
 
 def solution(mesh):

time: 54.5 us -> 53.2 us (0.976)
  Pallas kernels: 13.2 us -> 10.2 us
  starting transfers between devices: 13.3 us -> 16.3 us
  local copies, waits for them, and re-layouts: 3.78 us -> 0.84 us
  waiting for transfers between devices: 22.4 us -> 24.1 us
    ppermute x3 -> x7, starting transfers between devices: 1.86 us -> 7.56 us  [shards(): lax.ppermute(power, SPOTS + ('mp',), [(i, i ^ k) for i in range(2 * block...]
    unnamed x14, local copies, waits for them, and re-layouts: 3.62 us -> 0.68 us
    ppermute x8 -> x7, starting transfers between devices: 11.5 us -> 8.7 us  [moved(): return lax.ppermute(block, SPOTS, pairs)]
    pallas_call x1, Pallas kernels: 4.21 us -> 1.51 us  [shards(): kernel_call(functools.partial(far_kernel, len(extras)), (half_wide, half_...]
    pallas_call x1, Pallas kernels: 1.85 us -> 3.17 us  [shards(): kernel_call(products_kernel, (message, message, half_shape, half_shape),...]
    ppermute x8 -> x7, waiting for transfers between devices: 20 us -> 21 us  [moved(): return lax.ppermute(block, SPOTS, pairs)]
    pallas_call x1, Pallas kernels: 3.56 us -> 2.6 us  [shards(): kernel_call(tables_kernel, shape((groups, 2, BLK, taps + BLK), jnp.bfloat...]
    ppermute x3 -> x7, waiting for transfers between devices: 2.44 us -> 3.13 us  [shards(): lax.ppermute(power, SPOTS + ('mp',), [(i, i ^ k) for i in range(2 * block...]
  transfers between devices with their start and end apart: 11 -> 14, of which waited for: 7 -> 8; matrix products, arithmetic and copies ran while one was open for 3% -> 3% of each run, Pallas kernels for 11% -> 8%
where the time goes in v3:
time: 53.2 us; the launch traced here: 52.9 us
  waiting for transfers between devices  24.1 us (45%)
  starting transfers between devices  16.3 us (31%)
  Pallas kernels  10.2 us (19%)
  other arithmetic  1.46 us (3%)
  local copies, waits for them, and re-layouts  0.84 us (2%)
    ppermute x7, waiting for transfers between devices, moved(): return lax.ppermute(block, SPOTS, pairs)  21 us
    ppermute x7, starting transfers between devices, moved(): return lax.ppermute(block, SPOTS, pairs)  8.7 us
    ppermute x7, starting transfers between devices, shards(): lax.ppermute(power, SPOTS + ('mp',), [(i, i ^ k) for i in range(2 * block...  7.56 us
    pallas_call x1, Pallas kernels, shards(): kernel_call(products_kernel, (message, message, half_shape, half_shape),...  3.17 us
    ppermute x7, waiting for transfers between devices, shards(): lax.ppermute(power, SPOTS + ('mp',), [(i, i ^ k) for i in range(2 * block...  3.13 us
    pallas_call x1, Pallas kernels, shards(): kernel_call(tables_kernel, shape((groups, 2, BLK, taps + BLK), jnp.bfloat...  2.6 us
    pallas_call x1, Pallas kernels, shards(): kernel_call(near_kernel, (shape((2 * rows, width), jnp.float32), shape((2...  1.85 us
    pallas_call x1, Pallas kernels, shards(): kernel_call(functools.partial(far_kernel, len(extras)), (half_wide, half_...  1.51 us
  transfers between devices with their start and end apart: 14, of which 8 were waited for; matrix products, arithmetic and copies ran while one was open for 3% of the time, Pallas kernels for 8%

profile of v3, /device:TPU:0, one launch (start us, length us, event | category | flops | bytes accessed | tf_op | source)
XLA Modules:
  0.0 52.9 jit_solution(142903584189032389)
XLA Ops:
  0.0 0.0 copy-start
  0.0 0.0 copy-start.3
  0.0 3.2 %shard_map.73 = (bf16[144,1024]{1,0:T(8,128)(2,1)}, bf16[144,1024]{1,0:T(8,128)(2,1)}, bf16[128,1024]{1,0:T(8,128)(2,1)}, bf16[128,1024]{1,0:T(8,128)(2,1)}) custom-call(s32[32]{0:T(128)} %seq_ref.3, bf16[3,128,2048]{2,1,0:T(8,128)(2,1)} %bitcast.10, f32[3,3,2048]{2,1,0:T(4,128)} %w_ref.3), custom_call_target="tpu_custom_call" | custom-call | flops 5242880 | bytes 2097152 | tf_op jit(solution)/shard_map/pallas_call | solution.py:321
  3.2 0.0 copy-start.1
  3.2 0.0 copy-start.2
  3.2 3.1 %collective-permute-start = (bf16[144,1024]{1,0:T(8,128)(2,1)}, bf16[144,1024]{1,0:T(8,128)(2,1)S(1)}, u32[]{:S(2)}, u32[]{:S(2)}) collective-permute-start(bf16[144,1024]{1,0:T(8,128)(2,1)} %get-tuple-element.21.own_ref), channel_id=1, source_target_pairs={{0,8},{4,12},{8,16},{12,20},{16,24},{20,28},{24,0},{28,4},{1,9},{5... | collective-permute-start | bytes 884744 | tf_op jit(solution)/shard_map/ppermute | solution.py:20
  6.3 2.5 %collective-permute-start.1 = (bf16[144,1024]{1,0:T(8,128)(2,1)}, bf16[144,1024]{1,0:T(8,128)(2,1)S(1)}, u32[]{:S(2)}, u32[]{:S(2)}) collective-permute-start(bf16[144,1024]{1,0:T(8,128)(2,1)} %get-tuple-element.24), channel_id=1, source_target_pairs={{0,12},{4,8},{8,20},{12,16},{16,28},{20,24},{24,4},{28,0},{1,13},{... | collective-permute-start | bytes 884744 | tf_op jit(solution)/shard_map/ppermute | solution.py:20
  8.8 0.5 collective-permute-start.2
  9.3 0.7 %convert_element_type.6 = f32[16,4]{0,1:T(4,128)S(1)} convert(s32[16,4]{0,1:T(4,128)} %param.10) | non-fusion elementwise | flops 64 | bytes 512 | tf_op jit(solution)/shard_map/convert_element_type | solution.py:344
  10.0 0.1 copy.8
  10.1 0.1 broadcast_in_dim.3
  10.2 0.8 %fusion.taps_ref = bf16[16,512]{1,0:T(8,128)(2,1)S(1)} fusion(f32[16,512]{1,0:T(8,128)} %param.9, f32[2,8,4,128]{3,2,1,0:T(4,128)S(1)} %bitcast.11), kind=kLoop, calls=%fused_computation.1 | loop fusion | flops 16384 | bytes 81920 | tf_op jit(solution)/shard_map/convert_element_type | solution.py:344
  10.9 0.7 %copy-done.5 = s32[32]{0:T(128)S(1)} copy-done((s32[32]{0:T(128)S(1)}, s32[32]{0:T(128)}, u32[]{:S(2)}) %copy-start.5) | copy-done | bytes 152
  11.6 2.6 %shard_map.74.table_ref = bf16[8,2,128,640]{3,2,1,0:T(8,128)(2,1)S(1)} custom-call(s32[32]{0:T(128)S(1)} %copy-done.5, bf16[16,512]{1,0:T(8,128)(2,1)S(1)} %fusion.taps_ref), custom_call_target="tpu_custom_call" | custom-call | flops 20971520 | bytes 4194304 | tf_op jit(solution)/shard_map/pallas_call | solution.py:345
  14.2 2.1 %collective-permute-done.back_own_ref.refs_0_ = bf16[144,1024]{1,0:T(8,128)(2,1)S(1)} collective-permute-done((bf16[144,1024]{1,0:T(8,128)(2,1)}, bf16[144,1024]{1,0:T(8,128)(2,1)S(1)}, u32[]{:S(2)}, u32[]{:S(2)}) %collective-permute-start) | collective-permute-done | bytes 294944 | tf_op jit(solution)/shard_map/ppermute | solution.py:20
  16.3 6.6 %collective-permute-done.1.back_pair_ref.refs_1_ = bf16[144,1024]{1,0:T(8,128)(2,1)S(1)} collective-permute-done((bf16[144,1024]{1,0:T(8,128)(2,1)}, bf16[144,1024]{1,0:T(8,128)(2,1)S(1)}, u32[]{:S(2)}, u32[]{:S(2)}) %collective-permute-start.1) | collective-permute-done | bytes 294944 | tf_op jit(solution)/shard_map/ppermute | solution.py:20
  22.9 0.0 collective-permute-start.5
  22.9 1.3 %collective-permute-start.4 = (bf16[144,1024]{1,0:T(8,128)(2,1)S(1)}, bf16[144,1024]{1,0:T(8,128)(2,1)S(1)}, u32[]{:S(2)}, u32[]{:S(2)}) collective-permute-start(bf16[144,1024]{1,0:T(8,128)(2,1)S(1)} %collective-permute-done.back_own_ref.refs_0_), channel_id=1, source_target_pairs={{0,8},{4,12},{8,16},{12,20},{16,24},{20,28},{24,0},{28,4},{1,9},{5... | collective-permute-start | bytes 884744 | tf_op jit(solution)/shard_map/ppermute | solution.py:20
  24.2 0.0 copy-done.6
  24.2 0.5 collective-permute-start.3
  24.7 0.0 collective-permute-done.2.pair_ref
  24.7 6.0 %collective-permute-done.3.qgot_ref = bf16[128,1024]{1,0:T(8,128)(2,1)S(1)} collective-permute-done((bf16[128,1024]{1,0:T(8,128)(2,1)S(1)}, bf16[128,1024]{1,0:T(8,128)(2,1)S(1)}, u32[]{:S(2)}, u32[]{:S(2)}) %collective-permute-start.3) | collective-permute-done | bytes 262176 | tf_op jit(solution)/shard_map/ppermute | solution.py:20
  30.7 0.0 copy-done
  30.8 0.0 copy-done.3
  30.8 0.0 copy-done.1
  30.8 0.0 copy-done.2
  30.8 1.8 %shard_map.75 = (f32[256,1024]{1,0:T(8,128)S(1)}, f32[256,1024]{1,0:T(8,128)S(1)}, f32[2,8,128]{2,1,0:T(8,128)S(1)}) custom-call(s32[32]{0:T(128)S(1)} %copy-done.5, bf16[8,2,128,640]{3,2,1,0:T(8,128)(2,1)S(1)} %shard_map.74.table_ref, bf16[144,1024]{1,0:T(8,128)(2,1)S(1)} %copy-done.1, bf16[144,1024]{1,0:T(8,128)(2,1)S(1)} %collective-permute-done.2.pair_ref, ...), custom_call_target="tpu_custom_call" | custom-call | flops 167772160 | bytes 2097152 | tf_op jit(solution)/shard_map/pallas_call | solution.py:366
  32.6 2.0 %collective-permute-done.5.refs_3_ = bf16[144,1024]{1,0:T(8,128)(2,1)S(1)} collective-permute-done((bf16[144,1024]{1,0:T(8,128)(2,1)S(1)}, bf16[144,1024]{1,0:T(8,128)(2,1)S(1)}, u32[]{:S(2)}, u32[]{:S(2)}) %collective-permute-start.5) | collective-permute-done | bytes 294944 | tf_op jit(solution)/shard_map/ppermute | solution.py:20
  34.6 4.2 %collective-permute-done.4.refs_2_ = bf16[144,1024]{1,0:T(8,128)(2,1)S(1)} collective-permute-done((bf16[144,1024]{1,0:T(8,128)(2,1)S(1)}, bf16[144,1024]{1,0:T(8,128)(2,1)S(1)}, u32[]{:S(2)}, u32[]{:S(2)}) %collective-permute-start.4) | collective-permute-done | bytes 294944 | tf_op jit(solution)/shard_map/ppermute | solution.py:20
  38.9 1.5 %shard_map.76 = (f32[128,1024]{1,0:T(8,128)S(1)}, bf16[128,1024]{1,0:T(8,128)(2,1)S(1)}, f32[1,256]{1,0:T(1,128)S(1)}) custom-call(bf16[8,2,128,640]{3,2,1,0:T(8,128)(2,1)S(1)} %shard_map.74.table_ref, f32[256,1024]{1,0:T(8,128)S(1)} %get-tuple-element.31.acc_ref, f32[256,1024]{1,0:T(8,128)S(1)} %get-tuple-element.32.q_ref, f32[3,3,2048]{2,1,0:T(4,128)S(1)} %copy-done, ...), custom_call_target="tpu_custom_call" | custom-call | flops 167772160 | bytes 3145728 | tf_op jit(solution)/shard_map/pallas_call | solution.py:385
  40.4 0.8 %collective-permute-start.13 = (bf16[128,1024]{1,0:T(8,128)(2,1)S(1)}, bf16[128,1024]{1,0:T(8,128)(2,1)S(1)}, u32[]{:S(2)}, u32[]{:S(2)}) collective-permute-start(bf16[128,1024]{1,0:T(8,128)(2,1)S(1)} %get-tuple-element.36), channel_id=1, source_target_pairs={{0,4},{4,0},{8,12},{12,8},{16,20},{20,16},{24,28},{28,24},{1,5},{5... | collective-permute-start | bytes 786440 | tf_op jit(solution)/shard_map/ppermute | solution.py:20
  41.2 0.0 collective-permute-start.10
  41.2 2.2 %collective-permute-start.11 = (f32[1,256]{1,0:T(1,128)S(1)}, f32[1,256]{1,0:T(1,128)S(1)}, u32[]{:S(2)}, u32[]{:S(2)}) collective-permute-start(f32[1,256]{1,0:T(1,128)S(1)} %get-tuple-element.34.refs_0_), channel_id=1, source_target_pairs={{0,6},{1,7},{2,4},{3,5},{4,2},{5,3},{6,0},{7,1},{8,14},{9,15},{10,... | collective-permute-start | bytes 3080 | tf_op jit(solution)/shard_map/ppermute | solution.py:401
  43.4 1.4 %collective-permute-start.12 = (f32[1,256]{1,0:T(1,128)S(1)}, f32[1,256]{1,0:T(1,128)S(1)}, u32[]{:S(2)}, u32[]{:S(2)}) collective-permute-start(f32[1,256]{1,0:T(1,128)S(1)} %get-tuple-element.34.refs_0_), channel_id=1, source_target_pairs={{0,7},{1,6},{2,5},{3,4},{4,3},{5,2},{6,1},{7,0},{8,15},{9,14},{10,... | collective-permute-start | bytes 3080 | tf_op jit(solution)/shard_map/ppermute | solution.py:401
  44.8 0.0 collective-permute-start.6
  44.8 0.4 collective-permute-done.10.refs_5_
  45.2 1.2 %collective-permute-start.7 = (f32[1,256]{1,0:T(1,128)S(1)}, f32[1,256]{1,0:T(1,128)S(1)}, u32[]{:S(2)}, u32[]{:S(2)}) collective-permute-start(f32[1,256]{1,0:T(1,128)S(1)} %get-tuple-element.34.refs_0_), channel_id=1, source_target_pairs={{0,2},{1,3},{2,0},{3,1},{4,6},{5,7},{6,4},{7,5},{8,10},{9,11},{10,... | collective-permute-start | bytes 3080 | tf_op jit(solution)/shard_map/ppermute | solution.py:401
  46.4 0.0 collective-permute-done.11.refs_6_
  46.4 1.9 %collective-permute-start.8 = (f32[1,256]{1,0:T(1,128)S(1)}, f32[1,256]{1,0:T(1,128)S(1)}, u32[]{:S(2)}, u32[]{:S(2)}) collective-permute-start(f32[1,256]{1,0:T(1,128)S(1)} %get-tuple-element.34.refs_0_), channel_id=1, source_target_pairs={{0,3},{1,2},{2,1},{3,0},{4,7},{5,6},{6,5},{7,4},{8,11},{9,10},{10,... | collective-permute-start | bytes 3080 | tf_op jit(solution)/shard_map/ppermute | solution.py:401
  48.3 0.0 collective-permute-done.12.refs_7_
  48.3 0.8 %collective-permute-start.9 = (f32[1,256]{1,0:T(1,128)S(1)}, f32[1,256]{1,0:T(1,128)S(1)}, u32[]{:S(2)}, u32[]{:S(2)}) collective-permute-start(f32[1,256]{1,0:T(1,128)S(1)} %get-tuple-element.34.refs_0_), channel_id=1, source_target_pairs={{0,4},{1,5},{2,6},{3,7},{4,0},{5,1},{6,2},{7,3},{8,12},{9,13},{10,... | collective-permute-start | bytes 3080 | tf_op jit(solution)/shard_map/ppermute | solution.py:401
  49.1 0.0 collective-permute-done.6.refs_1_
  49.1 0.0 collective-permute-done.7.refs_2_
  49.1 0.4 collective-permute-done.8.refs_3_
  49.6 2.3 %collective-permute-done.9.refs_4_ = f32[1,256]{1,0:T(1,128)S(1)} collective-permute-done((f32[1,256]{1,0:T(1,128)S(1)}, f32[1,256]{1,0:T(1,128)S(1)}, u32[]{:S(2)}, u32[]{:S(2)}) %collective-permute-start.9) | collective-permute-done | bytes 1056 | tf_op jit(solution)/shard_map/ppermute | solution.py:401
  51.9 0.0 collective-permute-done.13.refs_9_
  51.9 0.0 copy-done.4
  51.9 1.1 %shard_map.77 = bf16[128,2048]{1,0:T(8,128)(2,1)} custom-call(f32[1,256]{1,0:T(1,128)S(1)} %get-tuple-element.34.refs_0_, f32[1,256]{1,0:T(1,128)S(1)} %collective-permute-done.6.refs_1_, f32[1,256]{1,0:T(1,128)S(1)} %collective-permute-done.7.refs_2_, f32[1,256]{1,0:T(1,128)S(1)} %collective-permute-done.8.refs_3_, ...), custom_call_target="tpu_custom_call" | custom-call | flops 1048576 | bytes 1310720 | tf_op jit(solution)/shard_map/pallas_call | solution.py:404
  (3 shorter events, 0.0 us)
Async XLA Ops:
  0.0 30.8 %copy-start = (f32[3,3,2048]{2,1,0:T(4,128)S(1)}, f32[3,3,2048]{2,1,0:T(4,128)}, u32[]{:S(2)}) copy-start(f32[3,3,2048]{2,1,0:T(4,128)} %w_ref.3) | copy-start | bytes 221188
  0.0 30.8 %copy-start.3 = (f32[2048]{0:T(1024)S(1)}, f32[2048]{0:T(1024)}, u32[]{:S(2)}) copy-start(f32[2048]{0:T(1024)} %param.11) | copy-start | bytes 24580
  3.2 27.6 %copy-start.1 = (bf16[144,1024]{1,0:T(8,128)(2,1)S(1)}, bf16[144,1024]{1,0:T(8,128)(2,1)}, u32[]{:S(2)}) copy-start(bf16[144,1024]{1,0:T(8,128)(2,1)} %get-tuple-element.21.own_ref) | copy-start | bytes 884740
  3.2 27.6 %copy-start.2 = (bf16[128,1024]{1,0:T(8,128)(2,1)S(1)}, bf16[128,1024]{1,0:T(8,128)(2,1)}, u32[]{:S(2)}) copy-start(bf16[128,1024]{1,0:T(8,128)(2,1)} %get-tuple-element.29.qkept_ref) | copy-start | bytes 786436
  3.2 13.1 %collective-permute-start = (bf16[144,1024]{1,0:T(8,128)(2,1)}, bf16[144,1024]{1,0:T(8,128)(2,1)S(1)}, u32[]{:S(2)}, u32[]{:S(2)}) collective-permute-start(bf16[144,1024]{1,0:T(8,128)(2,1)} %get-tuple-element.21.own_ref), channel_id=1, source_target_pairs={{0,8},{4,12},{8,16},{12,20},{16,24},{20,28},{24,0},{28,4},{1,9},{5... | collective-permute-start | bytes 884744 | tf_op jit(solution)/shard_map/ppermute | solution.py:20
  6.3 16.6 %collective-permute-start.1 = (bf16[144,1024]{1,0:T(8,128)(2,1)}, bf16[144,1024]{1,0:T(8,128)(2,1)S(1)}, u32[]{:S(2)}, u32[]{:S(2)}) collective-permute-start(bf16[144,1024]{1,0:T(8,128)(2,1)} %get-tuple-element.24), channel_id=1, source_target_pairs={{0,12},{4,8},{8,20},{12,16},{16,28},{20,24},{24,4},{28,0},{1,13},{... | collective-permute-start | bytes 884744 | tf_op jit(solution)/shard_map/ppermute | solution.py:20
  8.8 15.9 %collective-permute-start.2 = (bf16[144,1024]{1,0:T(8,128)(2,1)}, bf16[144,1024]{1,0:T(8,128)(2,1)S(1)}, u32[]{:S(2)}, u32[]{:S(2)}) collective-permute-start(bf16[144,1024]{1,0:T(8,128)(2,1)} %get-tuple-element.24), channel_id=1, source_target_pairs={{0,4},{4,0},{8,12},{12,8},{16,20},{20,16},{24,28},{28,24},{1,5},{5... | collective-permute-start | bytes 884744 | tf_op jit(solution)/shard_map/ppermute | solution.py:20
  10.9 0.7 %copy-start.5 = (s32[32]{0:T(128)S(1)}, s32[32]{0:T(128)}, u32[]{:S(2)}) copy-start(s32[32]{0:T(128)} %seq_ref.3) | copy-start | bytes 388
  11.6 12.6 %copy-start.6 = (bf16[128,1024]{1,0:T(8,128)(2,1)S(1)}, bf16[128,1024]{1,0:T(8,128)(2,1)}, u32[]{:S(2)}) copy-start(bf16[128,1024]{1,0:T(8,128)(2,1)} %get-tuple-element.30) | copy-start | bytes 786436
  22.9 11.7 %collective-permute-start.5 = (bf16[144,1024]{1,0:T(8,128)(2,1)S(1)}, bf16[144,1024]{1,0:T(8,128)(2,1)S(1)}, u32[]{:S(2)}, u32[]{:S(2)}) collective-permute-start(bf16[144,1024]{1,0:T(8,128)(2,1)S(1)} %collective-permute-done.1.back_pair_ref.refs_1_), channel_id=1, source_target_pairs={{0,8},{4,12},{8,16},{12,20},{16,24},{20,28},{24,0},{28,4},{1,9},{5... | collective-permute-start | bytes 884744 | tf_op jit(solution)/shard_map/ppermute | solution.py:20
  22.9 16.0 %collective-permute-start.4 = (bf16[144,1024]{1,0:T(8,128)(2,1)S(1)}, bf16[144,1024]{1,0:T(8,128)(2,1)S(1)}, u32[]{:S(2)}, u32[]{:S(2)}) collective-permute-start(bf16[144,1024]{1,0:T(8,128)(2,1)S(1)} %collective-permute-done.back_own_ref.refs_0_), channel_id=1, source_target_pairs={{0,8},{4,12},{8,16},{12,20},{16,24},{20,28},{24,0},{28,4},{1,9},{5... | collective-permute-start | bytes 884744 | tf_op jit(solution)/shard_map/ppermute | solution.py:20
  24.2 6.6 %collective-permute-start.3 = (bf16[128,1024]{1,0:T(8,128)(2,1)S(1)}, bf16[128,1024]{1,0:T(8,128)(2,1)S(1)}, u32[]{:S(2)}, u32[]{:S(2)}) collective-permute-start(bf16[128,1024]{1,0:T(8,128)(2,1)S(1)} %copy-done.6), channel_id=1, source_target_pairs={{0,4},{4,0},{8,12},{12,8},{16,20},{20,16},{24,28},{28,24},{1,5},{5... | collective-permute-start | bytes 786440 | tf_op jit(solution)/shard_map/ppermute | solution.py:20
  38.9 13.0 %copy-start.4 = (f32[2048]{0:T(1024)S(1)}, f32[2048]{0:T(1024)}, u32[]{:S(2)}) copy-start(f32[2048]{0:T(1024)} %param.12) | copy-start | bytes 24580
  40.4 11.5 %collective-permute-start.13 = (bf16[128,1024]{1,0:T(8,128)(2,1)S(1)}, bf16[128,1024]{1,0:T(8,128)(2,1)S(1)}, u32[]{:S(2)}, u32[]{:S(2)}) collective-permute-start(bf16[128,1024]{1,0:T(8,128)(2,1)S(1)} %get-tuple-element.36), channel_id=1, source_target_pairs={{0,4},{4,0},{8,12},{12,8},{16,20},{20,16},{24,28},{28,24},{1,5},{5... | collective-permute-start | bytes 786440 | tf_op jit(solution)/shard_map/ppermute | solution.py:20
  41.2 4.0 %collective-permute-start.10 = (f32[1,256]{1,0:T(1,128)S(1)}, f32[1,256]{1,0:T(1,128)S(1)}, u32[]{:S(2)}, u32[]{:S(2)}) collective-permute-start(f32[1,256]{1,0:T(1,128)S(1)} %get-tuple-element.34.refs_0_), channel_id=1, source_target_pairs={{0,5},{1,4},{2,7},{3,6},{4,1},{5,0},{6,3},{7,2},{8,13},{9,12},{10,... | collective-permute-start | bytes 3080 | tf_op jit(solution)/shard_map/ppermute | solution.py:401
  41.2 5.2 %collective-permute-start.11 = (f32[1,256]{1,0:T(1,128)S(1)}, f32[1,256]{1,0:T(1,128)S(1)}, u32[]{:S(2)}, u32[]{:S(2)}) collective-permute-start(f32[1,256]{1,0:T(1,128)S(1)} %get-tuple-element.34.refs_0_), channel_id=1, source_target_pairs={{0,6},{1,7},{2,4},{3,5},{4,2},{5,3},{6,0},{7,1},{8,14},{9,15},{10,... | collective-permute-start | bytes 3080 | tf_op jit(solution)/shard_map/ppermute | solution.py:401
  43.4 4.9 %collective-permute-start.12 = (f32[1,256]{1,0:T(1,128)S(1)}, f32[1,256]{1,0:T(1,128)S(1)}, u32[]{:S(2)}, u32[]{:S(2)}) collective-permute-start(f32[1,256]{1,0:T(1,128)S(1)} %get-tuple-element.34.refs_0_), channel_id=1, source_target_pairs={{0,7},{1,6},{2,5},{3,4},{4,3},{5,2},{6,1},{7,0},{8,15},{9,14},{10,... | collective-permute-start | bytes 3080 | tf_op jit(solution)/shard_map/ppermute | solution.py:401
  44.8 4.3 %collective-permute-start.6 = (f32[1,256]{1,0:T(1,128)S(1)}, f32[1,256]{1,0:T(1,128)S(1)}, u32[]{:S(2)}, u32[]{:S(2)}) collective-permute-start(f32[1,256]{1,0:T(1,128)S(1)} %get-tuple-element.34.refs_0_), channel_id=1, source_target_pairs={{0,1},{1,0},{2,3},{3,2},{4,5},{5,4},{6,7},{7,6},{8,9},{9,8},{10,11... | collective-permute-start | bytes 3080 | tf_op jit(solution)/shard_map/ppermute | solution.py:401
  45.2 3.9 %collective-permute-start.7 = (f32[1,256]{1,0:T(1,128)S(1)}, f32[1,256]{1,0:T(1,128)S(1)}, u32[]{:S(2)}, u32[]{:S(2)}) collective-permute-start(f32[1,256]{1,0:T(1,128)S(1)} %get-tuple-element.34.refs_0_), channel_id=1, source_target_pairs={{0,2},{1,3},{2,0},{3,1},{4,6},{5,7},{6,4},{7,5},{8,10},{9,11},{10,... | collective-permute-start | bytes 3080 | tf_op jit(solution)/shard_map/ppermute | solution.py:401
  46.4 3.2 %collective-permute-start.8 = (f32[1,256]{1,0:T(1,128)S(1)}, f32[1,256]{1,0:T(1,128)S(1)}, u32[]{:S(2)}, u32[]{:S(2)}) collective-permute-start(f32[1,256]{1,0:T(1,128)S(1)} %get-tuple-element.34.refs_0_), channel_id=1, source_target_pairs={{0,3},{1,2},{2,1},{3,0},{4,7},{5,6},{6,5},{7,4},{8,11},{9,10},{10,... | collective-permute-start | bytes 3080 | tf_op jit(solution)/shard_map/ppermute | solution.py:401
  48.3 3.6 %collective-permute-start.9 = (f32[1,256]{1,0:T(1,128)S(1)}, f32[1,256]{1,0:T(1,128)S(1)}, u32[]{:S(2)}, u32[]{:S(2)}) collective-permute-start(f32[1,256]{1,0:T(1,128)S(1)} %get-tuple-element.34.refs_0_), channel_id=1, source_target_pairs={{0,4},{1,5},{2,6},{3,7},{4,0},{5,1},{6,2},{7,3},{8,12},{9,13},{10,... | collective-permute-start | bytes 3080 | tf_op jit(solution)/shard_map/ppermute | solution.py:401

commit v4 on v3

--- a/solution.py
+++ b/solution.py
@@ -146,11 +146,22 @@
     win_ref[at : at + 16, :] = jnp.where(first, new, old).astype(win_ref.dtype)
 
 
-def tables_kernel(seq_ref, taps_ref, out_ref, rev_ref, m_ref):
+def reaches_past(seq_ref, block):
+    first = block * (2 * BLK)
+
+    def step(k, carry):
+        end, start = carry
+        end = end + seq_ref[k]
+        return end, jnp.where(end <= first, end, start)
+
+    _, start = lax.fori_loop(0, seq_ref.shape[0], step, (jnp.int32(0), jnp.int32(0)), unroll=True)
+    return first - 2 * BLK - start > BLK
+
+
+def tables_kernel(seq_ref, taps_ref, out_ref, next_ref, rev_ref, m_ref):
     groups = out_ref.shape[0]
     taps = taps_ref.shape[1]
-    span = rev_ref.shape[1]
-    width = out_ref.shape[3]
+    span = out_ref.shape[3]
     half = lax.axis_index("half")
     start = lax.axis_index("blk") * (2 * BLK)
     turn = lax.broadcasted_iota(jnp.int32, (taps, span), 0) + lax.broadcasted_iota(
@@ -158,39 +169,85 @@
     )
     turn = (turn == taps).astype(jnp.bfloat16)
     rev_ref[...] = jnp.dot(taps_ref[...], turn, preferred_element_type=jnp.float32)
-    for part in range(2):
-        t_in = start - taps + part * BLK + lax.broadcasted_iota(jnp.int32, (8, width), 1)
+    seg_in = counted(seq_ref, start - taps + lax.broadcasted_iota(jnp.int32, (8, span), 1))[0:1]
+    for part in range(3):
         t_out = start + part * BLK + lax.broadcasted_iota(jnp.int32, (BLK, GROUP), 0)
-        seg_in = counted(seq_ref, t_in)[0:1]
         seg_out = counted(seq_ref, t_out)[:, 0:1]
-        m_ref[part] = (seg_in == seg_out).astype(jnp.float32)
+        if part < 2:
+            m_ref[part] = (seg_in == seg_out).astype(jnp.float32)
+        else:
+            m_ref[2, :, : 2 * BLK] = (seg_in[:, 2 * BLK : 4 * BLK] == seg_out).astype(jnp.float32)
 
     def one(g, _):
         row = rev_ref[pl.ds(half * groups + g, 1), :]
-        table = pltpu.roll(
-            jnp.broadcast_to(row, (BLK, span)), 0, 1, stride=1, stride_axis=0
-        )[:, :width]
-        for part in range(2):
-            out_ref[g, part] = (table * m_ref[part]).astype(out_ref.dtype)
+        table = pltpu.roll(jnp.broadcast_to(row, (BLK, span)), 0, 1, stride=1, stride_axis=0)
+        out_ref[g, 0] = (table * m_ref[0]).astype(out_ref.dtype)
+        later = jnp.concatenate([table[:, span - BLK :], table[:, : span - BLK]], 1)
+        out_ref[g, 1] = (later * m_ref[1]).astype(out_ref.dtype)
+        next_ref[g] = (table[:, : 2 * BLK] * m_ref[2, :, : 2 * BLK]).astype(next_ref.dtype)
         return 0
 
     lax.fori_loop(0, groups, one, 0)
 
 
+def fill(win_ref, extra_ref, spot, message):
+    win_ref[pl.ds(pl.multiple_of(spot * BLK, BLK), BLK), :] = message[:BLK]
+    extra_ref[spot] = message[BLK:].astype(jnp.float32)
+
+
+def relay_kernel(seq_ref, next_ref, back_own_ref, back_pair_ref, w_ref, out_ref, win_ref, extra_ref):
+    groups = next_ref.shape[0]
+    width = groups * GROUP
+    half = lax.axis_index("half")
+    half_lanes = pl.ds(pl.multiple_of(half * width, width), width)
+    fill(win_ref, extra_ref, half, back_own_ref)
+    fill(win_ref, extra_ref, 1 - half, back_pair_ref)
+    marks = edge_marks(seq_ref)
+    rows = first_rows(extra_ref[1, :8], extra_ref[0, :8], w_ref, half_lanes, marks, 3)
+    put_first_rows(win_ref, BLK, rows)
+    out_ref[BLK:] = extra_ref[1].astype(out_ref.dtype)
+    summed = reaches_past(seq_ref, lax.axis_index("blk") + 1)
+
+    @pl.when(summed)
+    def _():
+        for g in range(groups):
+            lanes = slice(g * GROUP, (g + 1) * GROUP)
+            total = jnp.dot(next_ref[g], win_ref[:, lanes], preferred_element_type=jnp.float32)
+            out_ref[:BLK, lanes] = total.astype(out_ref.dtype)
+
+    @pl.when(jnp.logical_not(summed))
+    def _():
+        out_ref[:BLK] = win_ref[BLK:]
+
+
+def gate_rows(seq_ref, raw_ref, tail, w_ref, part, q_ref, x_ref, m1_ref, m2_ref):
+    width = raw_ref.shape[1]
+    half = lax.axis_index("half")
+    row_masks(seq_ref, lax.axis_index("blk") * (2 * BLK) + part * BLK, m1_ref, m2_ref)
+    for c in range(0, width, GROUP):
+        lanes = slice(c, c + GROUP)
+        w = w_ref[0, :, pl.ds(pl.multiple_of(half * width + c, GROUP), GROUP)]
+        x = raw_ref[:, lanes].astype(jnp.float32)
+        slot = (c // GROUP) % 2
+        x_ref[slot, 6:8, :] = tail(lanes)
+        x_ref[slot, 8:, :] = x
+        q_ref[:, lanes] = feature(x, x_ref.at[slot], w, m1_ref, m2_ref)
+
+
 def near_kernel(
-    seq_ref, table_ref, own_ref, pair_ref, back_own_ref, back_pair_ref, qkept_ref, qgot_ref, w_ref, bias_ref,
+    seq_ref, table_ref, own_ref, pair_ref, back_own_ref, back_pair_ref, qkept_ref, w_ref, bias_ref,
     acc_ref, q_ref, marks_ref, win_ref, extra_ref, x_ref, m1_ref, m2_ref,
 ):
     groups = table_ref.shape[0]
     width = groups * GROUP
     half = lax.axis_index("half")
-    start = lax.axis_index("blk") * (2 * BLK)
+    block = lax.axis_index("blk")
     half_lanes = pl.ds(pl.multiple_of(half * width, width), width)
     for spot, message in ((half, back_own_ref), (1 - half, back_pair_ref), (2 + half, own_ref), (3 - half, pair_ref)):
-        win_ref[pl.ds(pl.multiple_of(spot * BLK, BLK), BLK), :] = message[:BLK]
-        extra_ref[spot] = message[BLK:].astype(jnp.float32)
+        fill(win_ref, extra_ref, spot, message)
     marks = edge_marks(seq_ref)
     marks_ref[0], marks_ref[1] = marks
+    marks_ref[2] = jnp.full((8, GROUP), reaches_past(seq_ref, block).astype(jnp.float32))
     for spot in (1, 2, 3):
         rows = first_rows(extra_ref[spot, :8], extra_ref[spot - 1, :8], w_ref, half_lanes, marks, spot + 2)
         put_first_rows(win_ref, spot * BLK, rows)
@@ -199,60 +256,70 @@
         bias = bias_ref[:, pl.ds(pl.multiple_of(half * width + g * GROUP, GROUP), GROUP)]
         for part in range(2):
             total = jnp.dot(
-                table_ref[g, part, :, (3 - part) * BLK :],
+                table_ref[g, part, :, 3 * BLK : (5 + part) * BLK],
                 win_ref[BLK : (3 + part) * BLK, lanes],
                 preferred_element_type=jnp.float32,
             )
             here = win_ref[(2 + part) * BLK : (3 + part) * BLK, lanes].astype(jnp.float32)
             acc_ref[part * BLK : (part + 1) * BLK, lanes] = total + bias * here
-    for part, raw_ref in ((half, qkept_ref), (1 - half, qgot_ref)):
-        row_masks(seq_ref, start + part * BLK, m1_ref, m2_ref)
-        for g in range(groups):
-            lanes = slice(g * GROUP, (g + 1) * GROUP)
-            w = w_ref[0, :, pl.ds(pl.multiple_of(half * width + g * GROUP, GROUP), GROUP)]
-            x = raw_ref[:, lanes].astype(jnp.float32)
-            slot = g % 2
-            x_ref[slot, 6:8, :] = extra_ref[1 + part, 8:10, lanes]
-            x_ref[slot, 8:, :] = x
-            q_ref[pl.ds(pl.multiple_of(part * BLK, BLK), BLK), lanes] = feature(
-                x, x_ref.at[slot], w, m1_ref, m2_ref
-            )
-
-
-def far_kernel(deep, table_ref, acc_ref, q_ref, w_ref, marks_ref, *refs):
-    messages, refs = refs[: 4 + deep], refs[4 + deep :]
-    back_own_ref, back_pair_ref, far_own_ref, far_pair_ref = messages[:4]
-    kept_ref, sent_ref, power_ref, win_ref, extra_ref, gated_ref = refs
+    gate_rows(
+        seq_ref, qkept_ref, lambda lanes: extra_ref[1 + half, 8:10, lanes], w_ref, half, q_ref, x_ref, m1_ref, m2_ref
+    )
+
+
+def pair_gate_kernel(seq_ref, raw_ref, own_ref, back_own_ref, w_ref, q_ref, x_ref, m1_ref, m2_ref):
+    half = lax.axis_index("half")
+
+    def tail(lanes):
+        back = back_own_ref[BLK:, lanes].astype(jnp.float32)
+        own = own_ref[BLK:, lanes].astype(jnp.float32)
+        return jnp.where(half == 1, back, own)[8:10]
+
+    gate_rows(seq_ref, raw_ref, tail, w_ref, 1 - half, q_ref, x_ref, m1_ref, m2_ref)
+
+
+def far_kernel(short, table_ref, acc_ref, qown_ref, qpair_ref, w_ref, marks_ref, *refs):
+    *messages, kept_ref, sent_ref, power_ref, win_ref, extra_ref = refs
     groups = table_ref.shape[0]
     width = groups * GROUP
     half = lax.axis_index("half")
     half_lanes = pl.ds(pl.multiple_of(half * width, width), width)
-    for spot, message in (
-        (half, far_own_ref), (1 - half, far_pair_ref), (2 + half, back_own_ref), (3 - half, back_pair_ref)
-    ):
-        win_ref[pl.ds(pl.multiple_of(spot * BLK, BLK), BLK), :] = message[:BLK]
-        extra_ref[spot] = message[BLK:].astype(jnp.float32)
     marks = [marks_ref[0], marks_ref[1]]
-    for spot in (1, 2):
-        rows = first_rows(extra_ref[spot, :8], extra_ref[spot - 1, :8], w_ref, half_lanes, marks, spot)
-        put_first_rows(win_ref, spot * BLK, rows)
-    if deep:
-        ahead = messages[4][...].astype(jnp.float32)[:8]
+    back_own_ref, back_pair_ref, far_ref, *others = messages
+    low = 1 if short else 0
+    fill(win_ref, extra_ref, 2 + half, back_own_ref)
+    fill(win_ref, extra_ref, 3 - half, back_pair_ref)
+    if short:
+        summed = marks_ref[2, 0:1, 0:1]
+        payload = far_ref[:BLK].astype(jnp.float32)
+        win_ref[BLK : 2 * BLK, :] = (payload * (1.0 - summed)).astype(win_ref.dtype)
+        extra_ref[1] = far_ref[BLK:].astype(jnp.float32)
+    else:
+        fill(win_ref, extra_ref, half, far_ref)
+        fill(win_ref, extra_ref, 1 - half, others[0])
+        ahead = others[1][...].astype(jnp.float32)[:8]
         put_first_rows(win_ref, 0, first_rows(extra_ref[0, :8], ahead, w_ref, half_lanes, marks, 0))
+        rows = first_rows(extra_ref[1, :8], extra_ref[0, :8], w_ref, half_lanes, marks, 1)
+        put_first_rows(win_ref, BLK, rows)
+    rows = first_rows(extra_ref[2, :8], extra_ref[1, :8], w_ref, half_lanes, marks, 2)
+    put_first_rows(win_ref, 2 * BLK, rows)
     power = []
-    for part in range(2):
+    for part, q_ref, out_ref in ((half, qown_ref, kept_ref), (1 - half, qpair_ref, sent_ref)):
         squares = jnp.zeros((BLK, GROUP), jnp.float32)
-        rows = slice(part * BLK, (part + 1) * BLK)
+        rows = pl.ds(pl.multiple_of(part * BLK, BLK), BLK)
         for g in range(groups):
             lanes = slice(g * GROUP, (g + 1) * GROUP)
             filtered = acc_ref[rows, lanes] + jnp.dot(
-                table_ref[g, part, :, : (3 - part) * BLK],
-                win_ref[part * BLK : 3 * BLK, lanes],
+                table_ref[g, part, :, low * BLK : 3 * BLK],
+                win_ref[low * BLK : 3 * BLK, lanes],
                 preferred_element_type=jnp.float32,
             )
-            gated = q_ref[rows, lanes] * filtered
+            if short:
+                weight = summed * (part == 0).astype(jnp.float32)
+                filtered = filtered + weight * far_ref[:BLK, lanes].astype(jnp.float32)
+            gated = q_ref[:, lanes] * filtered
             squares = squares + gated * gated
-            gated_ref[rows, lanes] = gated
+            out_ref[:, lanes] = gated.astype(out_ref.dtype)
         power.append(
             lax.dot_general(
                 jnp.ones((8, GROUP), jnp.float32),
@@ -262,9 +329,9 @@
                 preferred_element_type=jnp.float32,
             )[0:1]
         )
-    power_ref[...] = jnp.concatenate(power, 1)
-    kept_ref[...] = gated_ref[pl.ds(pl.multiple_of(half * BLK, BLK), BLK), :]
-    sent_ref[...] = gated_ref[pl.ds(pl.multiple_of((1 - half) * BLK, BLK), BLK), :].astype(sent_ref.dtype)
+    own, pair = power
+    power_ref[:, :BLK] = jnp.where(half == 0, own, pair)
+    power_ref[:, BLK:] = jnp.where(half == 0, pair, own)
 
 
 def norm_kernel(channels, *refs):
@@ -342,73 +409,78 @@
 
     filter_taps, _ = lax.optimization_barrier((filter_taps, kept))
     scaled = (filter_taps * jnp.repeat(tap_blocks.astype(jnp.float32), BLK, axis=1)).astype(jnp.bfloat16)
-    table = kernel_call(
+    span = taps + 2 * BLK
+    table, table_next = kernel_call(
         tables_kernel,
-        shape((groups, 2, BLK, taps + BLK), jnp.bfloat16),
+        (shape((groups, 2, BLK, span), jnp.bfloat16), shape((groups, BLK, 2 * BLK), jnp.bfloat16)),
         [SMEM, VMEM],
-        [pltpu.VMEM((2 * groups, taps + 2 * BLK), jnp.float32), pltpu.VMEM((2, BLK, taps + BLK), jnp.float32)],
+        [pltpu.VMEM((2 * groups, span), jnp.float32), pltpu.VMEM((3, BLK, span), jnp.float32)],
         40 * groups * BLK * taps,
         8 * groups * BLK * taps,
     )(seq_lengths, scaled)
-
-    table, back_own = lax.optimization_barrier((table, back_own))
-    far_own = moved(back_own, ahead)
+    table, table_next, back_own = lax.optimization_barrier((table, table_next, back_own))
     table, back_pair, qsent = lax.optimization_barrier((table, back_pair, qsent))
-    far_pair = moved(back_pair, ahead)
     qgot = moved(qsent, to_pair)
-    extras = ()
-    if whole_tokens // 2 > taps:
-        half = lax.axis_index("half")
+
+    window = pltpu.VMEM((4 * rows, width), jnp.bfloat16)
+    extras = pltpu.VMEM((4, 16, width), jnp.float32)
+    shifted = pltpu.VMEM((2, rows + 8, GROUP), jnp.float32)
+    short = whole_tokens // 2 <= 4 * BLK
+    if short:
+        relayed = kernel_call(
+            relay_kernel,
+            message,
+            [SMEM] + [VMEM] * 4,
+            [pltpu.VMEM((2 * rows, width), jnp.bfloat16), pltpu.VMEM((2, 16, width), jnp.float32)],
+            2 * 2 * rows * BLK * width,
+            8 * rows * width,
+        )(seq_lengths, table_next, back_own, back_pair, short_weight)
+        far = (moved(relayed, ahead),)
+    else:
         straight = moved(kept[rows:], [(i, (i + 6) % (2 * blocks)) for i in spots])
         across = moved(sent[rows:], [(i, ((i ^ 1) + 6) % (2 * blocks)) for i in spots])
-        extras = (jnp.where(half == 1, straight, across),)
-
-    acc, q, marks = kernel_call(
+        deep = jnp.where(lax.axis_index("half") == 1, straight, across)
+        far = (moved(back_own, ahead), moved(back_pair, ahead), deep)
+
+    acc, qown, marks = kernel_call(
         near_kernel,
-        (
-            shape((2 * rows, width), jnp.float32),
-            shape((2 * rows, width), jnp.float32),
-            shape((2, 8, GROUP), jnp.float32),
-        ),
-        [SMEM] + [VMEM] * 9,
-        [
-            pltpu.VMEM((4 * rows, width), jnp.bfloat16),
-            pltpu.VMEM((4, 16, width), jnp.float32),
-            pltpu.VMEM((2, rows + 8, GROUP), jnp.float32),
-            row_mask,
-            row_mask,
-        ],
+        (shape((2 * rows, width), jnp.float32), half_wide, shape((3, 8, GROUP), jnp.float32)),
+        [SMEM] + [VMEM] * 8,
+        [window, extras, shifted, row_mask, row_mask],
         2 * 5 * rows * BLK * width,
         16 * rows * width,
-    )(seq_lengths, table, kept, pair, back_own, back_pair, qkept, qgot, short_weight, skip_bias.reshape(1, -1))
+    )(seq_lengths, table, kept, pair, back_own, back_pair, qkept, short_weight, skip_bias.reshape(1, -1))
+
+    qpair = kernel_call(
+        pair_gate_kernel,
+        half_wide,
+        [SMEM] + [VMEM] * 4,
+        [shifted, row_mask, row_mask],
+        10 * rows * width,
+        8 * rows * width,
+    )(seq_lengths, qgot, kept, back_own, short_weight)
 
     done, send, power = kernel_call(
-        functools.partial(far_kernel, len(extras)),
+        functools.partial(far_kernel, short),
         (half_wide, half_shape, shape((1, 2 * rows), jnp.float32)),
-        [VMEM] * (9 + len(extras)),
-        [
-            pltpu.VMEM((4 * rows, width), jnp.bfloat16),
-            pltpu.VMEM((4, 16, width), jnp.float32),
-            pltpu.VMEM((2 * rows, width), jnp.float32),
-        ],
+        [VMEM] * (8 + len(far)),
+        [window, extras],
         2 * 5 * rows * BLK * width,
         24 * rows * width,
-    )(table, acc, q, short_weight, marks, back_own, back_pair, far_own, far_pair, *extras)
+    )(table, acc, qown, qpair, short_weight, marks, back_own, back_pair, *far)
 
     back = moved(send, to_pair)
     peers = lax.axis_size("mp")
-    powers = [power] + [
-        lax.ppermute(power, SPOTS + ("mp",), [(i, i ^ k) for i in range(2 * blocks * peers)])
-        for k in range(1, 2 * peers)
-    ]
+    shares = [lax.ppermute(power, "mp", [(i, i ^ k) for i in range(peers)]) for k in range(1, peers)]
+    power = sum(shares, power)
     return kernel_call(
         functools.partial(norm_kernel, channels),
         shape((rows, 2 * width), jnp.bfloat16),
-        [VMEM] * (3 + len(powers)),
+        [VMEM] * 5,
         [],
         8 * rows * width,
         10 * rows * width,
-    )(*powers, done, back, norm_gain.reshape(1, -1))
+    )(power, moved(power, to_pair), done, back, norm_gain.reshape(1, -1))
 
 
 def solution(mesh):

time: 53.2 us -> 45.3 us (0.85)
  waiting for transfers between devices: 24.1 us -> 17.6 us
  starting transfers between devices: 16.3 us -> 10.9 us
  local copies, waits for them, and re-layouts: 0.84 us -> 3.63 us
  Pallas kernels: 10.2 us -> 11.3 us
    ppermute x7, waiting for transfers between devices: 21 us -> 15.2 us  [moved(): return lax.ppermute(block, SPOTS, pairs)]
    ppermute x7 -> x3, starting transfers between devices: 7.56 us -> 1.86 us  [shards(): lax.ppermute(power, 'mp', [(i, i ^ k) for i in range(peers)])]
    unnamed x14 -> x12, local copies, waits for them, and re-layouts: 0.68 us -> 3.47 us
    pallas_call x3 -> x5, Pallas kernels: 5.96 us -> 7.08 us  [the longest x1 2.81 us: shards(): kernel_call(tables_kernel, (shape((groups, 2, BLK, span), jnp.bfloat16),...]
    ppermute x7 -> x3, waiting for transfers between devices: 3.13 us -> 2.38 us  [shards(): lax.ppermute(power, 'mp', [(i, i ^ k) for i in range(peers)])]
  transfers between devices with their start and end apart: 14 -> 10, of which waited for: 8 -> 7; matrix products, arithmetic and copies ran while one was open for 3% -> 4% of each run, Pallas kernels for 8% -> 13%
where the time goes in v4:
time: 45.3 us; the launch traced here: 45 us
  waiting for transfers between devices  17.6 us (39%)
  Pallas kernels  11.3 us (25%)
  starting transfers between devices  10.9 us (24%)
  local copies, waits for them, and re-layouts  3.63 us (8%)
  other arithmetic  1.46 us (3%)
    ppermute x7, waiting for transfers between devices, moved(): return lax.ppermute(block, SPOTS, pairs)  15.2 us
    ppermute x7, starting transfers between devices, moved(): return lax.ppermute(block, SPOTS, pairs)  9.05 us
    unnamed x12, local copies, waits for them, and re-layouts  3.47 us
    pallas_call x1, Pallas kernels, shards(): kernel_call(products_kernel, (message, message, half_shape, half_shape),...  3.15 us
    pallas_call x1, Pallas kernels, shards(): kernel_call(tables_kernel, (shape((groups, 2, BLK, span), jnp.bfloat16),...  2.81 us
    ppermute x3, waiting for transfers between devices, shards(): lax.ppermute(power, 'mp', [(i, i ^ k) for i in range(peers)])  2.38 us
    ppermute x3, starting transfers between devices, shards(): lax.ppermute(power, 'mp', [(i, i ^ k) for i in range(peers)])  1.86 us
    pallas_call x1, Pallas kernels, shards(): kernel_call(near_kernel, (shape((2 * rows, width), jnp.float32), half_wid...  1.55 us
  transfers between devices with their start and end apart: 10, of which 7 were waited for; matrix products, arithmetic and copies ran while one was open for 4% of the time, Pallas kernels for 13%

profile of v4, /device:TPU:0, one launch (start us, length us, event | category | flops | bytes accessed | tf_op | source)
XLA Modules:
  0.0 45.0 jit_solution(11094162702660957821)
XLA Ops:
  0.0 0.0 copy-start.3
  0.0 3.1 %shard_map.73 = (bf16[144,1024]{1,0:T(8,128)(2,1)}, bf16[144,1024]{1,0:T(8,128)(2,1)}, bf16[128,1024]{1,0:T(8,128)(2,1)}, bf16[128,1024]{1,0:T(8,128)(2,1)}) custom-call(s32[32]{0:T(128)} %seq_ref.7, bf16[3,128,2048]{2,1,0:T(8,128)(2,1)} %bitcast.10, f32[3,3,2048]{2,1,0:T(4,128)} %w_ref.7), custom_call_target="tpu_custom_call" | custom-call | flops 5242880 | bytes 2097152 | tf_op jit(solution)/shard_map/pallas_call | solution.py:388
  3.2 3.1 %collective-permute-start = (bf16[144,1024]{1,0:T(8,128)(2,1)}, bf16[144,1024]{1,0:T(8,128)(2,1)S(1)}, u32[]{:S(2)}, u32[]{:S(2)}) collective-permute-start(bf16[144,1024]{1,0:T(8,128)(2,1)} %get-tuple-element.24.own_ref), channel_id=1, source_target_pairs={{0,8},{4,12},{8,16},{12,20},{16,24},{20,28},{24,0},{28,4},{1,9},{5... | collective-permute-start | bytes 884744 | tf_op jit(solution)/shard_map/ppermute | solution.py:20
  6.2 2.5 %collective-permute-start.1 = (bf16[144,1024]{1,0:T(8,128)(2,1)}, bf16[144,1024]{1,0:T(8,128)(2,1)S(1)}, u32[]{:S(2)}, u32[]{:S(2)}) collective-permute-start(bf16[144,1024]{1,0:T(8,128)(2,1)} %get-tuple-element.29), channel_id=1, source_target_pairs={{0,12},{4,8},{8,20},{12,16},{16,28},{20,24},{24,4},{28,0},{1,13},{... | collective-permute-start | bytes 884744 | tf_op jit(solution)/shard_map/ppermute | solution.py:20
  8.8 0.5 %collective-permute-start.2 = (bf16[144,1024]{1,0:T(8,128)(2,1)}, bf16[144,1024]{1,0:T(8,128)(2,1)S(1)}, u32[]{:S(2)}, u32[]{:S(2)}) collective-permute-start(bf16[144,1024]{1,0:T(8,128)(2,1)} %get-tuple-element.29), channel_id=1, source_target_pairs={{0,4},{4,0},{8,12},{12,8},{16,20},{20,16},{24,28},{28,24},{1,5},{5... | collective-permute-start | bytes 884744 | tf_op jit(solution)/shard_map/ppermute | solution.py:20
  9.3 0.7 %convert_element_type.6 = f32[16,4]{0,1:T(4,128)S(1)} convert(s32[16,4]{0,1:T(4,128)} %param.10) | non-fusion elementwise | flops 64 | bytes 512 | tf_op jit(solution)/shard_map/convert_element_type | solution.py:411
  10.0 0.1 copy.8
  10.0 0.1 broadcast_in_dim.3
  10.1 0.8 %fusion.taps_ref = bf16[16,512]{1,0:T(8,128)(2,1)S(1)} fusion(f32[16,512]{1,0:T(8,128)} %param.9, f32[2,8,4,128]{3,2,1,0:T(4,128)S(1)} %bitcast.11), kind=kLoop, calls=%fused_computation.1 | loop fusion | flops 16384 | bytes 81920 | tf_op jit(solution)/shard_map/convert_element_type | solution.py:411
  10.9 0.0 copy-start.5
  10.9 0.7 %copy-done.5 = s32[32]{0:T(128)S(1)} copy-done((s32[32]{0:T(128)S(1)}, s32[32]{0:T(128)}, u32[]{:S(2)}) %copy-start.5) | copy-done | bytes 152
  11.6 2.8 %shard_map.74 = (bf16[8,2,128,768]{3,2,1,0:T(8,128)(2,1)S(1)}, bf16[8,128,256]{2,1,0:T(8,128)(2,1)S(1)}) custom-call(s32[32]{0:T(128)S(1)} %copy-done.5, bf16[16,512]{1,0:T(8,128)(2,1)S(1)} %fusion.taps_ref), custom_call_target="tpu_custom_call" | custom-call | flops 20971520 | bytes 4194304 | tf_op jit(solution)/shard_map/pallas_call | solution.py:413
  14.4 1.9 %collective-permute-done.back_own_ref.refs_0_ = bf16[144,1024]{1,0:T(8,128)(2,1)S(1)} collective-permute-done((bf16[144,1024]{1,0:T(8,128)(2,1)}, bf16[144,1024]{1,0:T(8,128)(2,1)S(1)}, u32[]{:S(2)}, u32[]{:S(2)}) %collective-permute-start) | collective-permute-done | bytes 294944 | tf_op jit(solution)/shard_map/ppermute | solution.py:20
  16.3 6.6 %collective-permute-done.1.back_pair_ref.refs_1_ = bf16[144,1024]{1,0:T(8,128)(2,1)S(1)} collective-permute-done((bf16[144,1024]{1,0:T(8,128)(2,1)}, bf16[144,1024]{1,0:T(8,128)(2,1)S(1)}, u32[]{:S(2)}, u32[]{:S(2)}) %collective-permute-start.1) | collective-permute-done | bytes 294944 | tf_op jit(solution)/shard_map/ppermute | solution.py:20
  22.9 0.0 copy-start
  22.9 0.9 %copy-done = f32[3,3,2048]{2,1,0:T(4,128)S(1)} copy-done((f32[3,3,2048]{2,1,0:T(4,128)S(1)}, f32[3,3,2048]{2,1,0:T(4,128)}, u32[]{:S(2)}) %copy-start) | copy-done | bytes 73752
  23.8 0.7 %shard_map.77 = bf16[144,1024]{1,0:T(8,128)(2,1)S(1)} custom-call(s32[32]{0:T(128)S(1)} %copy-done.5, bf16[8,128,256]{2,1,0:T(8,128)(2,1)S(1)} %get-tuple-element.39.next_ref, bf16[144,1024]{1,0:T(8,128)(2,1)S(1)} %collective-permute-done.back_own_ref.refs_0_, bf16[144,1024]{1,0:T(8,128)(2,1)S(1)} %collective-permute-done.1.back_pair_ref.refs_1_, ...), custom_call_target="tpu_custom_call" | custom-call | flops 67108864 | bytes 1048576 | tf_op jit(solution)/shard_map/pallas_call | solution.py:430
  24.4 0.1 collective-permute-start.4
  24.5 0.6 %collective-permute-start.3 = (bf16[128,1024]{1,0:T(8,128)(2,1)}, bf16[128,1024]{1,0:T(8,128)(2,1)S(1)}, u32[]{:S(2)}, u32[]{:S(2)}) collective-permute-start(bf16[128,1024]{1,0:T(8,128)(2,1)} %get-tuple-element.37), channel_id=1, source_target_pairs={{0,4},{4,0},{8,12},{12,8},{16,20},{20,16},{24,28},{28,24},{1,5},{5... | collective-permute-start | bytes 786440 | tf_op jit(solution)/shard_map/ppermute | solution.py:20
  25.1 0.0 collective-permute-done.2.pair_ref
  25.1 0.0 copy-done.3
  25.1 0.0 copy-start.1
  25.1 1.0 %copy-done.1 = bf16[144,1024]{1,0:T(8,128)(2,1)S(1)} copy-done((bf16[144,1024]{1,0:T(8,128)(2,1)S(1)}, bf16[144,1024]{1,0:T(8,128)(2,1)}, u32[]{:S(2)}) %copy-start.1) | copy-done | bytes 294936
  26.1 0.0 copy-start.2
  26.1 0.9 %copy-done.2 = bf16[128,1024]{1,0:T(8,128)(2,1)S(1)} copy-done((bf16[128,1024]{1,0:T(8,128)(2,1)S(1)}, bf16[128,1024]{1,0:T(8,128)(2,1)}, u32[]{:S(2)}) %copy-start.2) | copy-done | bytes 262168
  27.0 1.6 %shard_map.75 = (f32[256,1024]{1,0:T(8,128)S(1)}, f32[128,1024]{1,0:T(8,128)S(1)}, f32[3,8,128]{2,1,0:T(8,128)S(1)}) custom-call(s32[32]{0:T(128)S(1)} %copy-done.5, bf16[8,2,128,768]{3,2,1,0:T(8,128)(2,1)S(1)} %get-tuple-element.31.table_ref, bf16[144,1024]{1,0:T(8,128)(2,1)S(1)} %copy-done.1, bf16[144,1024]{1,0:T(8,128)(2,1)S(1)} %collective-permute-done.2.pair_ref, ...), custom_call_target="tpu_custom_call" | custom-call | flops 167772160 | bytes 2097152 | tf_op jit(solution)/shard_map/pallas_call | solution.py:445
  28.6 3.4 %collective-permute-done.3.raw_ref = bf16[128,1024]{1,0:T(8,128)(2,1)S(1)} collective-permute-done((bf16[128,1024]{1,0:T(8,128)(2,1)}, bf16[128,1024]{1,0:T(8,128)(2,1)S(1)}, u32[]{:S(2)}, u32[]{:S(2)}) %collective-permute-start.3) | collective-permute-done | bytes 262176 | tf_op jit(solution)/shard_map/ppermute | solution.py:20
  31.9 0.9 %shard_map.76.qpair_ref = f32[128,1024]{1,0:T(8,128)S(1)} custom-call(s32[32]{0:T(128)S(1)} %copy-done.5, bf16[128,1024]{1,0:T(8,128)(2,1)S(1)} %collective-permute-done.3.raw_ref, bf16[144,1024]{1,0:T(8,128)(2,1)S(1)} %copy-done.1, bf16[144,1024]{1,0:T(8,128)(2,1)S(1)} %collective-permute-done.back_own_ref.refs_0_, f32[3,3,2048]{2,1,0:T(4,128)S(1)} %copy-done), custom_call_target="tpu_custom_call" | custom-call | flops 1310720 | bytes 1048576 | tf_op jit(solution)/shard_map/pallas_call | solution.py:454
  32.8 0.0 copy-start.4
  32.8 1.3 %collective-permute-done.4.refs_2_ = bf16[144,1024]{1,0:T(8,128)(2,1)S(1)} collective-permute-done((bf16[144,1024]{1,0:T(8,128)(2,1)S(1)}, bf16[144,1024]{1,0:T(8,128)(2,1)S(1)}, u32[]{:S(2)}, u32[]{:S(2)}) %collective-permute-start.4) | collective-permute-done | bytes 294944 | tf_op jit(solution)/shard_map/ppermute | solution.py:20
  34.1 1.2 %shard_map.78 = (f32[128,1024]{1,0:T(8,128)S(1)}, bf16[128,1024]{1,0:T(8,128)(2,1)S(1)}, f32[1,256]{1,0:T(1,128)S(1)}) custom-call(bf16[8,2,128,768]{3,2,1,0:T(8,128)(2,1)S(1)} %get-tuple-element.31.table_ref, f32[256,1024]{1,0:T(8,128)S(1)} %get-tuple-element.35.acc_ref, f32[128,1024]{1,0:T(8,128)S(1)} %get-tuple-element.36.qown_ref, ...), custom_call_target="tpu_custom_call" | custom-call | flops 167772160 | bytes 3145728 | tf_op jit(solution)/shard_map/pallas_call | solution.py:463
  35.3 0.8 %collective-permute-start.9 = (bf16[128,1024]{1,0:T(8,128)(2,1)S(1)}, bf16[128,1024]{1,0:T(8,128)(2,1)S(1)}, u32[]{:S(2)}, u32[]{:S(2)}) collective-permute-start(bf16[128,1024]{1,0:T(8,128)(2,1)S(1)} %get-tuple-element.42), channel_id=1, source_target_pairs={{0,4},{4,0},{8,12},{12,8},{16,20},{20,16},{24,28},{28,24},{1,5},{5... | collective-permute-start | bytes 786440 | tf_op jit(solution)/shard_map/ppermute | solution.py:20
  36.1 0.0 collective-permute-start.5
  36.1 1.2 %collective-permute-start.6 = (f32[1,256]{1,0:T(1,128)S(1)}, f32[1,256]{1,0:T(1,128)S(1)}, u32[]{:S(2)}, u32[]{:S(2)}) collective-permute-start(f32[1,256]{1,0:T(1,128)S(1)} %get-tuple-element.40), channel_id=1, source_target_pairs={{0,2},{1,3},{2,0},{3,1},{4,6},{5,7},{6,4},{7,5},{8,10},{9,11},{10,... | collective-permute-start | bytes 3080 | tf_op jit(solution)/shard_map/ppermute | solution.py:474
  37.3 0.6 %collective-permute-start.7 = (f32[1,256]{1,0:T(1,128)S(1)}, f32[1,256]{1,0:T(1,128)S(1)}, u32[]{:S(2)}, u32[]{:S(2)}) collective-permute-start(f32[1,256]{1,0:T(1,128)S(1)} %get-tuple-element.40), channel_id=1, source_target_pairs={{0,3},{1,2},{2,1},{3,0},{4,7},{5,6},{6,5},{7,4},{8,11},{9,10},{10,... | collective-permute-start | bytes 3080 | tf_op jit(solution)/shard_map/ppermute | solution.py:474
  38.0 0.0 collective-permute-done.5
  38.0 1.7 %collective-permute-done.6 = f32[1,256]{1,0:T(1,128)S(1)} collective-permute-done((f32[1,256]{1,0:T(1,128)S(1)}, f32[1,256]{1,0:T(1,128)S(1)}, u32[]{:S(2)}, u32[]{:S(2)}) %collective-permute-start.6) | collective-permute-done | bytes 1056 | tf_op jit(solution)/shard_map/ppermute | solution.py:474
  39.7 0.7 %collective-permute-done.7 = f32[1,256]{1,0:T(1,128)S(1)} collective-permute-done((f32[1,256]{1,0:T(1,128)S(1)}, f32[1,256]{1,0:T(1,128)S(1)}, u32[]{:S(2)}, u32[]{:S(2)}) %collective-permute-start.7) | collective-permute-done | bytes 1056 | tf_op jit(solution)/shard_map/ppermute | solution.py:474
  40.3 1.5 %collective-permute-start.8 = (f32[1,256]{1,0:T(1,128)S(1)}, f32[1,256]{1,0:T(1,128)S(1)}, u32[]{:S(2)}, u32[]{:S(2)}) collective-permute-start(f32[1,256]{1,0:T(1,128)S(1)} %add_add_fusion.refs_0_), channel_id=1, source_target_pairs={{0,4},{4,0},{8,12},{12,8},{16,20},{20,16},{24,28},{28,24},{1,5},{5... | collective-permute-start | bytes 3080 | tf_op jit(solution)/shard_map/ppermute | solution.py:20
  41.9 2.0 %collective-permute-done.8.refs_1_ = f32[1,256]{1,0:T(1,128)S(1)} collective-permute-done((f32[1,256]{1,0:T(1,128)S(1)}, f32[1,256]{1,0:T(1,128)S(1)}, u32[]{:S(2)}, u32[]{:S(2)}) %collective-permute-start.8) | collective-permute-done | bytes 1056 | tf_op jit(solution)/shard_map/ppermute | solution.py:20
  43.9 0.0 collective-permute-done.9.refs_3_
  43.9 0.0 copy-done.4
  43.9 1.1 %shard_map.79 = bf16[128,2048]{1,0:T(8,128)(2,1)} custom-call(f32[1,256]{1,0:T(1,128)S(1)} %add_add_fusion.refs_0_, f32[1,256]{1,0:T(1,128)S(1)} %collective-permute-done.8.refs_1_, f32[128,1024]{1,0:T(8,128)S(1)} %get-tuple-element.41.refs_2_, bf16[128,1024]{1,0:T(8,128)(2,1)S(1)} %collective-permute-done.9.refs_3_, f32[1,2048]{1,0:T(1,128)S(1)} %bitcast.9), custom_call_target="tpu_custom_call" | custom-call | flops 1048576 | bytes 1310720 | tf_op jit(solution)/shard_map/pallas_call | solution.py:476
  (1 shorter events, 0.0 us)
Async XLA Ops:
  0.0 25.1 %copy-start.3 = (f32[2048]{0:T(1024)S(1)}, f32[2048]{0:T(1024)}, u32[]{:S(2)}) copy-start(f32[2048]{0:T(1024)} %param.11) | copy-start | bytes 24580
  3.2 13.1 %collective-permute-start = (bf16[144,1024]{1,0:T(8,128)(2,1)}, bf16[144,1024]{1,0:T(8,128)(2,1)S(1)}, u32[]{:S(2)}, u32[]{:S(2)}) collective-permute-start(bf16[144,1024]{1,0:T(8,128)(2,1)} %get-tuple-element.24.own_ref), channel_id=1, source_target_pairs={{0,8},{4,12},{8,16},{12,20},{16,24},{20,28},{24,0},{28,4},{1,9},{5... | collective-permute-start | bytes 884744 | tf_op jit(solution)/shard_map/ppermute | solution.py:20
  6.2 16.6 %collective-permute-start.1 = (bf16[144,1024]{1,0:T(8,128)(2,1)}, bf16[144,1024]{1,0:T(8,128)(2,1)S(1)}, u32[]{:S(2)}, u32[]{:S(2)}) collective-permute-start(bf16[144,1024]{1,0:T(8,128)(2,1)} %get-tuple-element.29), channel_id=1, source_target_pairs={{0,12},{4,8},{8,20},{12,16},{16,28},{20,24},{24,4},{28,0},{1,13},{... | collective-permute-start | bytes 884744 | tf_op jit(solution)/shard_map/ppermute | solution.py:20
  8.8 16.3 %collective-permute-start.2 = (bf16[144,1024]{1,0:T(8,128)(2,1)}, bf16[144,1024]{1,0:T(8,128)(2,1)S(1)}, u32[]{:S(2)}, u32[]{:S(2)}) collective-permute-start(bf16[144,1024]{1,0:T(8,128)(2,1)} %get-tuple-element.29), channel_id=1, source_target_pairs={{0,4},{4,0},{8,12},{12,8},{16,20},{20,16},{24,28},{28,24},{1,5},{5... | collective-permute-start | bytes 884744 | tf_op jit(solution)/shard_map/ppermute | solution.py:20
  10.9 0.7 %copy-start.5 = (s32[32]{0:T(128)S(1)}, s32[32]{0:T(128)}, u32[]{:S(2)}) copy-start(s32[32]{0:T(128)} %seq_ref.7) | copy-start | bytes 388
  22.9 0.9 %copy-start = (f32[3,3,2048]{2,1,0:T(4,128)S(1)}, f32[3,3,2048]{2,1,0:T(4,128)}, u32[]{:S(2)}) copy-start(f32[3,3,2048]{2,1,0:T(4,128)} %w_ref.7) | copy-start | bytes 221188
  24.4 9.7 %collective-permute-start.4 = (bf16[144,1024]{1,0:T(8,128)(2,1)S(1)}, bf16[144,1024]{1,0:T(8,128)(2,1)S(1)}, u32[]{:S(2)}, u32[]{:S(2)}) collective-permute-start(bf16[144,1024]{1,0:T(8,128)(2,1)S(1)} %shard_map.77), channel_id=1, source_target_pairs={{0,8},{4,12},{8,16},{12,20},{16,24},{20,28},{24,0},{28,4},{1,9},{5... | collective-permute-start | bytes 884744 | tf_op jit(solution)/shard_map/ppermute | solution.py:20
  24.5 7.4 %collective-permute-start.3 = (bf16[128,1024]{1,0:T(8,128)(2,1)}, bf16[128,1024]{1,0:T(8,128)(2,1)S(1)}, u32[]{:S(2)}, u32[]{:S(2)}) collective-permute-start(bf16[128,1024]{1,0:T(8,128)(2,1)} %get-tuple-element.37), channel_id=1, source_target_pairs={{0,4},{4,0},{8,12},{12,8},{16,20},{20,16},{24,28},{28,24},{1,5},{5... | collective-permute-start | bytes 786440 | tf_op jit(solution)/shard_map/ppermute | solution.py:20
  25.1 1.0 %copy-start.1 = (bf16[144,1024]{1,0:T(8,128)(2,1)S(1)}, bf16[144,1024]{1,0:T(8,128)(2,1)}, u32[]{:S(2)}) copy-start(bf16[144,1024]{1,0:T(8,128)(2,1)} %get-tuple-element.24.own_ref) | copy-start | bytes 884740
  26.1 0.9 %copy-start.2 = (bf16[128,1024]{1,0:T(8,128)(2,1)S(1)}, bf16[128,1024]{1,0:T(8,128)(2,1)}, u32[]{:S(2)}) copy-start(bf16[128,1024]{1,0:T(8,128)(2,1)} %get-tuple-element.34.qkept_ref) | copy-start | bytes 786436
  32.8 11.1 %copy-start.4 = (f32[2048]{0:T(1024)S(1)}, f32[2048]{0:T(1024)}, u32[]{:S(2)}) copy-start(f32[2048]{0:T(1024)} %param.12) | copy-start | bytes 24580
  35.3 8.6 %collective-permute-start.9 = (bf16[128,1024]{1,0:T(8,128)(2,1)S(1)}, bf16[128,1024]{1,0:T(8,128)(2,1)S(1)}, u32[]{:S(2)}, u32[]{:S(2)}) collective-permute-start(bf16[128,1024]{1,0:T(8,128)(2,1)S(1)} %get-tuple-element.42), channel_id=1, source_target_pairs={{0,4},{4,0},{8,12},{12,8},{16,20},{20,16},{24,28},{28,24},{1,5},{5... | collective-permute-start | bytes 786440 | tf_op jit(solution)/shard_map/ppermute | solution.py:20
  36.1 1.9 %collective-permute-start.5 = (f32[1,256]{1,0:T(1,128)S(1)}, f32[1,256]{1,0:T(1,128)S(1)}, u32[]{:S(2)}, u32[]{:S(2)}) collective-permute-start(f32[1,256]{1,0:T(1,128)S(1)} %get-tuple-element.40), channel_id=1, source_target_pairs={{0,1},{1,0},{2,3},{3,2},{4,5},{5,4},{6,7},{7,6},{8,9},{9,8},{10,11... | collective-permute-start | bytes 3080 | tf_op jit(solution)/shard_map/ppermute | solution.py:474
  36.1 3.6 %collective-permute-start.6 = (f32[1,256]{1,0:T(1,128)S(1)}, f32[1,256]{1,0:T(1,128)S(1)}, u32[]{:S(2)}, u32[]{:S(2)}) collective-permute-start(f32[1,256]{1,0:T(1,128)S(1)} %get-tuple-element.40), channel_id=1, source_target_pairs={{0,2},{1,3},{2,0},{3,1},{4,6},{5,7},{6,4},{7,5},{8,10},{9,11},{10,... | collective-permute-start | bytes 3080 | tf_op jit(solution)/shard_map/ppermute | solution.py:474
  37.3 3.0 %collective-permute-start.7 = (f32[1,256]{1,0:T(1,128)S(1)}, f32[1,256]{1,0:T(1,128)S(1)}, u32[]{:S(2)}, u32[]{:S(2)}) collective-permute-start(f32[1,256]{1,0:T(1,128)S(1)} %get-tuple-element.40), channel_id=1, source_target_pairs={{0,3},{1,2},{2,1},{3,0},{4,7},{5,6},{6,5},{7,4},{8,11},{9,10},{10,... | collective-permute-start | bytes 3080 | tf_op jit(solution)/shard_map/ppermute | solution.py:474
  40.3 3.6 %collective-permute-start.8 = (f32[1,256]{1,0:T(1,128)S(1)}, f32[1,256]{1,0:T(1,128)S(1)}, u32[]{:S(2)}, u32[]{:S(2)}) collective-permute-start(f32[1,256]{1,0:T(1,128)S(1)} %add_add_fusion.refs_0_), channel_id=1, source_target_pairs={{0,4},{4,0},{8,12},{12,8},{16,20},{20,16},{24,28},{28,24},{1,5},{5... | collective-permute-start | bytes 3080 | tf_op jit(solution)/shard_map/ppermute | solution.py:20

commit v5 on v4

--- a/solution.py
+++ b/solution.py
@@ -64,10 +64,10 @@
 
 
 def products_kernel(
-    seq_hbm, panels_hbm, w_hbm, sent_ref, kept_ref, qsent_ref, qkept_ref,
-    seq_ref, kv_ref, w_ref, x_ref, m1_ref, m2_ref, sems,
+    seq_hbm, panels_hbm, w_hbm, sent_ref, kept_ref, seq_ref, kv_ref, q_ref, w_ref, x_ref, m1_ref, m2_ref, sems
 ):
-    rows, width = qsent_ref.shape
+    width = kept_ref.shape[1]
+    rows = kv_ref.shape[2]
     pieces = kv_ref.shape[0]
     piece = kv_ref.shape[3]
     half = lax.axis_index("half")
@@ -75,44 +75,37 @@
     keep_at = pl.multiple_of(half * width, width)
     send_at = pl.multiple_of((1 - half) * width, width)
 
-    loads = [
-        pltpu.make_async_copy(seq_hbm, seq_ref, sems.at[0]),
-        pltpu.make_async_copy(w_hbm, w_ref, sems.at[1]),
-    ]
+    loads = [pltpu.make_async_copy(seq_hbm, seq_ref, sems.at[0])]
     for p in range(pieces):
         at = keep_at if p < pieces // 2 else send_at
         lanes = pl.ds(pl.multiple_of(at + (p % (pieces // 2)) * piece, piece), piece)
-        loads.append(pltpu.make_async_copy(panels_hbm.at[1:3, :, lanes], kv_ref.at[p], sems.at[2 + p]))
-    asides = [
-        pltpu.make_async_copy(panels_hbm.at[0, :, pl.ds(keep_at, width)], qkept_ref, sems.at[2 + pieces]),
-        pltpu.make_async_copy(panels_hbm.at[0, :, pl.ds(send_at, width)], qsent_ref, sems.at[3 + pieces]),
-    ]
-    for load in loads + asides:
+        loads.append(pltpu.make_async_copy(panels_hbm.at[1:3, :, lanes], kv_ref.at[p], sems.at[1 + p]))
+    loads.append(pltpu.make_async_copy(w_hbm, w_ref, sems.at[1 + pieces]))
+    loads.append(pltpu.make_async_copy(panels_hbm.at[0, rows - 16 :, :], q_ref, sems.at[2 + pieces]))
+    for load in loads:
         load.start()
+    x_ref[:, 0:8, :] = jnp.zeros((x_ref.shape[0], 8, GROUP), jnp.float32)
     loads[0].wait()
     row_masks(seq_ref, shard * rows, m1_ref, m2_ref)
-    x_ref[:, 0:8, :] = jnp.zeros((x_ref.shape[0], 8, GROUP), jnp.float32)
-    loads[1].wait()
-    asides[0].wait()
-    asides[1].wait()
+    loads[1 + pieces].wait()
+    loads[2 + pieces].wait()
     for p in range(pieces):
-        loads[2 + p].wait()
-        kept = p < pieces // 2
-        out_ref, q_ref, at = (kept_ref, qkept_ref, keep_at) if kept else (sent_ref, qsent_ref, send_at)
+        loads[1 + p].wait()
+        out_ref, at = (kept_ref, keep_at) if p < pieces // 2 else (sent_ref, send_at)
         for c in range(0, piece, GROUP):
             base = (p % (pieces // 2)) * piece + c
             there = slice(base, base + GROUP)
-            w_lanes = pl.ds(pl.multiple_of(at + base, GROUP), GROUP)
+            lanes = pl.ds(pl.multiple_of(at + base, GROUP), GROUP)
             slot = (c // GROUP) % (x_ref.shape[0] // 2) * 2
             heads, tails, made = [], [], []
             for i in range(2):
                 x = kv_ref[p, i, :, c : c + GROUP].astype(jnp.float32)
                 x_ref[slot + i, 8:, :] = x
-                made.append(feature(x, x_ref.at[slot + i], w_ref[1 + i, :, w_lanes], m1_ref, m2_ref))
+                made.append(feature(x, x_ref.at[slot + i], w_ref[1 + i, :, lanes], m1_ref, m2_ref))
                 heads.append(x[0:2])
                 tails.append(x[rows - 2 :])
             out_ref[:rows, there] = (made[0] * made[1]).astype(out_ref.dtype)
-            tails.append(q_ref[rows - 16 :, there].astype(jnp.float32)[14:])
+            tails.append(q_ref[:, lanes].astype(jnp.float32)[14:])
             extra = jnp.concatenate(heads + tails + [jnp.zeros((6, GROUP), jnp.float32)], 0)
             out_ref[rows:, there] = extra.astype(out_ref.dtype)
 
@@ -126,7 +119,7 @@
     return [1.0 - mark.astype(jnp.float32) for mark in boundaries(seq_ref, t)]
 
 
-def first_rows(now, ahead, w_ref, lanes, marks, spot):
+def first_rows(now, ahead, w_ref, marks, spot):
     m1, m2 = [mark[:, spot : spot + 1] for mark in marks]
     top = lax.broadcasted_iota(jnp.int32, now.shape, 0) == 0
     made = []
@@ -134,7 +127,7 @@
         x0 = pltpu.roll(now, (8 - 2 * i) % 8, 0) if i else now
         x1 = jnp.where(top, pltpu.roll(ahead, 3 - 2 * i, 0), pltpu.roll(now, (9 - 2 * i) % 8, 0))
         x2 = pltpu.roll(ahead, 4 - 2 * i, 0)
-        w = w_ref[1 + i, :, lanes]
+        w = w_ref[1 + i]
         made.append(w[0:1] * x0 + w[1:2] * x1 * m1 + w[2:3] * x2 * m2)
     return made[0] * made[1]
 
@@ -158,12 +151,14 @@
     return first - 2 * BLK - start > BLK
 
 
-def tables_kernel(seq_ref, taps_ref, out_ref, next_ref, rev_ref, m_ref):
+def tables_kernel(seq_ref, taps_ref, w_ref, out_ref, next_ref, w_half_ref, rev_ref, m_ref):
     groups = out_ref.shape[0]
     taps = taps_ref.shape[1]
     span = out_ref.shape[3]
     half = lax.axis_index("half")
     start = lax.axis_index("blk") * (2 * BLK)
+    width = w_half_ref.shape[2]
+    w_half_ref[...] = w_ref[:, :, pl.ds(pl.multiple_of(half * width, width), width)]
     turn = lax.broadcasted_iota(jnp.int32, (taps, span), 0) + lax.broadcasted_iota(
         jnp.int32, (taps, span), 1
     )
@@ -199,11 +194,10 @@
     groups = next_ref.shape[0]
     width = groups * GROUP
     half = lax.axis_index("half")
-    half_lanes = pl.ds(pl.multiple_of(half * width, width), width)
     fill(win_ref, extra_ref, half, back_own_ref)
     fill(win_ref, extra_ref, 1 - half, back_pair_ref)
     marks = edge_marks(seq_ref)
-    rows = first_rows(extra_ref[1, :8], extra_ref[0, :8], w_ref, half_lanes, marks, 3)
+    rows = first_rows(extra_ref[1, :8], extra_ref[0, :8], w_ref, marks, 3)
     put_first_rows(win_ref, BLK, rows)
     out_ref[BLK:] = extra_ref[1].astype(out_ref.dtype)
     summed = reaches_past(seq_ref, lax.axis_index("blk") + 1)
@@ -222,11 +216,10 @@
 
 def gate_rows(seq_ref, raw_ref, tail, w_ref, part, q_ref, x_ref, m1_ref, m2_ref):
     width = raw_ref.shape[1]
-    half = lax.axis_index("half")
     row_masks(seq_ref, lax.axis_index("blk") * (2 * BLK) + part * BLK, m1_ref, m2_ref)
     for c in range(0, width, GROUP):
         lanes = slice(c, c + GROUP)
-        w = w_ref[0, :, pl.ds(pl.multiple_of(half * width + c, GROUP), GROUP)]
+        w = w_ref[0, :, lanes]
         x = raw_ref[:, lanes].astype(jnp.float32)
         slot = (c // GROUP) % 2
         x_ref[slot, 6:8, :] = tail(lanes)
@@ -242,14 +235,13 @@
     width = groups * GROUP
     half = lax.axis_index("half")
     block = lax.axis_index("blk")
-    half_lanes = pl.ds(pl.multiple_of(half * width, width), width)
     for spot, message in ((half, back_own_ref), (1 - half, back_pair_ref), (2 + half, own_ref), (3 - half, pair_ref)):
         fill(win_ref, extra_ref, spot, message)
     marks = edge_marks(seq_ref)
     marks_ref[0], marks_ref[1] = marks
     marks_ref[2] = jnp.full((8, GROUP), reaches_past(seq_ref, block).astype(jnp.float32))
     for spot in (1, 2, 3):
-        rows = first_rows(extra_ref[spot, :8], extra_ref[spot - 1, :8], w_ref, half_lanes, marks, spot + 2)
+        rows = first_rows(extra_ref[spot, :8], extra_ref[spot - 1, :8], w_ref, marks, spot + 2)
         put_first_rows(win_ref, spot * BLK, rows)
     for g in range(groups):
         lanes = slice(g * GROUP, (g + 1) * GROUP)
@@ -283,7 +275,6 @@
     groups = table_ref.shape[0]
     width = groups * GROUP
     half = lax.axis_index("half")
-    half_lanes = pl.ds(pl.multiple_of(half * width, width), width)
     marks = [marks_ref[0], marks_ref[1]]
     back_own_ref, back_pair_ref, far_ref, *others = messages
     low = 1 if short else 0
@@ -298,13 +289,12 @@
         fill(win_ref, extra_ref, half, far_ref)
         fill(win_ref, extra_ref, 1 - half, others[0])
         ahead = others[1][...].astype(jnp.float32)[:8]
-        put_first_rows(win_ref, 0, first_rows(extra_ref[0, :8], ahead, w_ref, half_lanes, marks, 0))
-        rows = first_rows(extra_ref[1, :8], extra_ref[0, :8], w_ref, half_lanes, marks, 1)
+        put_first_rows(win_ref, 0, first_rows(extra_ref[0, :8], ahead, w_ref, marks, 0))
+        rows = first_rows(extra_ref[1, :8], extra_ref[0, :8], w_ref, marks, 1)
         put_first_rows(win_ref, BLK, rows)
-    rows = first_rows(extra_ref[2, :8], extra_ref[1, :8], w_ref, half_lanes, marks, 2)
+    rows = first_rows(extra_ref[2, :8], extra_ref[1, :8], w_ref, marks, 2)
     put_first_rows(win_ref, 2 * BLK, rows)
-    power = []
-    for part, q_ref, out_ref in ((half, qown_ref, kept_ref), (1 - half, qpair_ref, sent_ref)):
+    for at, part, q_ref, out_ref in ((0, half, qown_ref, kept_ref), (BLK, 1 - half, qpair_ref, sent_ref)):
         squares = jnp.zeros((BLK, GROUP), jnp.float32)
         rows = pl.ds(pl.multiple_of(part * BLK, BLK), BLK)
         for g in range(groups):
@@ -320,26 +310,19 @@
             gated = q_ref[:, lanes] * filtered
             squares = squares + gated * gated
             out_ref[:, lanes] = gated.astype(out_ref.dtype)
-        power.append(
-            lax.dot_general(
-                jnp.ones((8, GROUP), jnp.float32),
-                squares,
-                (((1,), (1,)), ((), ())),
-                precision=lax.Precision.HIGHEST,
-                preferred_element_type=jnp.float32,
-            )[0:1]
-        )
-    own, pair = power
-    power_ref[:, :BLK] = jnp.where(half == 0, own, pair)
-    power_ref[:, BLK:] = jnp.where(half == 0, pair, own)
-
-
-def norm_kernel(channels, *refs):
-    half = lax.axis_index("half")
-    *power_refs, kept_ref, got_ref, gain_ref, out_ref = refs
+        power_ref[:, at : at + BLK] = lax.dot_general(
+            jnp.ones((8, GROUP), jnp.float32),
+            squares,
+            (((1,), (1,)), ((), ())),
+            precision=lax.Precision.HIGHEST,
+            preferred_element_type=jnp.float32,
+        )[0:1]
+
+
+def norm_kernel(channels, power_ref, power_got_ref, kept_ref, got_ref, gain_ref, out_ref):
+    half = lax.axis_index("half")
     width = kept_ref.shape[1]
-    mine = pl.ds(pl.multiple_of(half * BLK, BLK), BLK)
-    power = sum(ref[:, mine] for ref in power_refs)
+    power = power_ref[:, :BLK] + power_got_ref[:, BLK:]
     scale = lax.rsqrt(power / channels + norm_eps)
     diagonal = lax.broadcasted_iota(jnp.int32, (BLK, BLK), 0) == lax.broadcasted_iota(
         jnp.int32, (BLK, BLK), 1
@@ -385,18 +368,19 @@
     pieces = 4
     row_mask = pltpu.VMEM((rows, GROUP), jnp.float32)
 
-    sent, kept, qsent, qkept = kernel_call(
+    sent, kept = kernel_call(
         products_kernel,
-        (message, message, half_shape, half_shape),
+        (message, message),
         [hbm] * 3,
         [
             pltpu.SMEM(seq_lengths.shape, jnp.int32),
             pltpu.VMEM((pieces, 2, rows, 2 * width // pieces), jnp.bfloat16),
+            pltpu.VMEM((16, 2 * width), jnp.bfloat16),
             pltpu.VMEM(short_weight.shape, jnp.float32),
             pltpu.VMEM((4, rows + 8, GROUP), jnp.float32),
             row_mask,
             row_mask,
-            pltpu.SemaphoreType.DMA((4 + pieces,)),
+            pltpu.SemaphoreType.DMA((3 + pieces,)),
         ],
         40 * rows * width,
         16 * rows * width,
@@ -405,21 +389,28 @@
 
     back_own = moved(kept, ahead)
     back_pair = moved(sent, ahead_pair)
-    pair = moved(sent, to_pair)
-
-    filter_taps, _ = lax.optimization_barrier((filter_taps, kept))
+    filter_taps, query, _ = lax.optimization_barrier((filter_taps, panels[0], kept))
+    half = lax.axis_index("half")
+    qkept = lax.dynamic_slice_in_dim(query, half * width, width, 1)
+    qsent = lax.dynamic_slice_in_dim(query, (1 - half) * width, width, 1)
     scaled = (filter_taps * jnp.repeat(tap_blocks.astype(jnp.float32), BLK, axis=1)).astype(jnp.bfloat16)
+    scaled, sent_late = lax.optimization_barrier((scaled, sent))
+    pair = moved(sent_late, to_pair)
     span = taps + 2 * BLK
-    table, table_next = kernel_call(
+    table, table_next, w_half = kernel_call(
         tables_kernel,
-        (shape((groups, 2, BLK, span), jnp.bfloat16), shape((groups, BLK, 2 * BLK), jnp.bfloat16)),
-        [SMEM, VMEM],
+        (
+            shape((groups, 2, BLK, span), jnp.bfloat16),
+            shape((groups, BLK, 2 * BLK), jnp.bfloat16),
+            shape((3, 3, width), jnp.float32),
+        ),
+        [SMEM, VMEM, VMEM],
         [pltpu.VMEM((2 * groups, span), jnp.float32), pltpu.VMEM((3, BLK, span), jnp.float32)],
         40 * groups * BLK * taps,
         8 * groups * BLK * taps,
-    )(seq_lengths, scaled)
+    )(seq_lengths, scaled, short_weight)
     table, table_next, back_own = lax.optimization_barrier((table, table_next, back_own))
-    table, back_pair, qsent = lax.optimization_barrier((table, back_pair, qsent))
+    table, back_pair, qsent, qkept = lax.optimization_barrier((table, back_pair, qsent, qkept))
     qgot = moved(qsent, to_pair)
 
     window = pltpu.VMEM((4 * rows, width), jnp.bfloat16)
@@ -434,12 +425,12 @@
             [pltpu.VMEM((2 * rows, width), jnp.bfloat16), pltpu.VMEM((2, 16, width), jnp.float32)],
             2 * 2 * rows * BLK * width,
             8 * rows * width,
-        )(seq_lengths, table_next, back_own, back_pair, short_weight)
+        )(seq_lengths, table_next, back_own, back_pair, w_half)
         far = (moved(relayed, ahead),)
     else:
         straight = moved(kept[rows:], [(i, (i + 6) % (2 * blocks)) for i in spots])
         across = moved(sent[rows:], [(i, ((i ^ 1) + 6) % (2 * blocks)) for i in spots])
-        deep = jnp.where(lax.axis_index("half") == 1, straight, across)
+        deep = jnp.where(half == 1, straight, across)
         far = (moved(back_own, ahead), moved(back_pair, ahead), deep)
 
     acc, qown, marks = kernel_call(
@@ -449,7 +440,7 @@
         [window, extras, shifted, row_mask, row_mask],
         2 * 5 * rows * BLK * width,
         16 * rows * width,
-    )(seq_lengths, table, kept, pair, back_own, back_pair, qkept, short_weight, skip_bias.reshape(1, -1))
+    )(seq_lengths, table, kept, pair, back_own, back_pair, qkept, w_half, skip_bias.reshape(1, -1))
 
     qpair = kernel_call(
         pair_gate_kernel,
@@ -458,7 +449,7 @@
         [shifted, row_mask, row_mask],
         10 * rows * width,
         8 * rows * width,
-    )(seq_lengths, qgot, kept, back_own, short_weight)
+    )(seq_lengths, qgot, kept, back_own, w_half)
 
     done, send, power = kernel_call(
         functools.partial(far_kernel, short),
@@ -467,7 +458,7 @@
         [window, extras],
         2 * 5 * rows * BLK * width,
         24 * rows * width,
-    )(table, acc, qown, qpair, short_weight, marks, back_own, back_pair, *far)
+    )(table, acc, qown, qpair, w_half, marks, back_own, back_pair, *far)
 
     back = moved(send, to_pair)
     peers = lax.axis_size("mp")

time: 45.3 us -> 43.5 us (0.960)
  waiting for transfers between devices: 17.6 us -> 20 us
  local copies, waits for them, and re-layouts: 3.63 us -> 1.3 us
  other arithmetic: 1.46 us -> 0.02 us
    unnamed x12 -> x14, local copies, waits for them, and re-layouts: 3.47 us -> 0.03 us
    ppermute x7, waiting for transfers between devices: 15.2 us -> 18.3 us  [moved(): return lax.ppermute(block, SPOTS, pairs)]
    squeeze x0 -> x1, local copies, waits for them, and re-layouts: none -> 1.08 us  [shards(): panels[0]]
    convert_element_type x1, other arithmetic: 0.77 us -> 0.01 us  [shards(): (filter_taps * jnp.repeat(tap_blocks.astype(jnp.float32), BLK, axis=1)).a...]
    convert_element_type x1, other arithmetic: 0.68 us -> 0.01 us  [shards(): tap_blocks.astype(jnp.float32)]
    ppermute x3, waiting for transfers between devices: 2.38 us -> 1.74 us  [shards(): lax.ppermute(power, 'mp', [(i, i ^ k) for i in range(peers)])]
  transfers between devices with their start and end apart: 10 -> 10, of which waited for: 7 -> 8; matrix products, arithmetic and copies ran while one was open for 4% -> 3% of each run, Pallas kernels for 13% -> 14%
where the time goes in v5:
time: 43.5 us; the launch traced here: 43.3 us
  waiting for transfers between devices  20 us (46%)
  Pallas kernels  11.1 us (26%)
  starting transfers between devices  10.8 us (25%)
  local copies, waits for them, and re-layouts  1.3 us (3%)
    ppermute x7, waiting for transfers between devices, moved(): return lax.ppermute(block, SPOTS, pairs)  18.3 us
    ppermute x7, starting transfers between devices, moved(): return lax.ppermute(block, SPOTS, pairs)  8.95 us
    pallas_call x1, Pallas kernels, shards(): kernel_call(products_kernel, (message, message), [hbm] * 3, [pltpu.SMEM(s...  2.95 us
    pallas_call x1, Pallas kernels, shards(): kernel_call(tables_kernel, (shape((groups, 2, BLK, span), jnp.bfloat16),...  2.81 us
    ppermute x3, starting transfers between devices, shards(): lax.ppermute(power, 'mp', [(i, i ^ k) for i in range(peers)])  1.86 us
    ppermute x3, waiting for transfers between devices, shards(): lax.ppermute(power, 'mp', [(i, i ^ k) for i in range(peers)])  1.74 us
    pallas_call x1, Pallas kernels, shards(): kernel_call(near_kernel, (shape((2 * rows, width), jnp.float32), half_wid...  1.55 us
    pallas_call x1, Pallas kernels, shards(): kernel_call(functools.partial(far_kernel, short), (half_wide, half_shape,...  1.18 us
  transfers between devices with their start and end apart: 10, of which 8 were waited for; matrix products, arithmetic and copies ran while one was open for 3% of the time, Pallas kernels for 14%

profile of v5, /device:TPU:0, one launch (start us, length us, event | category | flops | bytes accessed | tf_op | source)
XLA Modules:
  0.0 43.3 jit_solution(14950570195046666378)
XLA Ops:
  0.0 0.0 copy-start.5
  0.0 0.0 copy-start.6
  0.0 0.0 copy-start.1
  0.0 0.0 copy-start.2
  0.0 2.9 %shard_map.73 = (bf16[144,1024]{1,0:T(8,128)(2,1)}, bf16[144,1024]{1,0:T(8,128)(2,1)}) custom-call(s32[32]{0:T(128)} %seq_ref.7, bf16[3,128,2048]{2,1,0:T(8,128)(2,1)} %bitcast.12, f32[3,3,2048]{2,1,0:T(4,128)} %w_ref.1), custom_call_target="tpu_custom_call" | custom-call | flops 5242880 | bytes 2097152 | tf_op jit(solution)/shard_map/pallas_call | solution.py:371
  3.0 3.1 %collective-permute-start = (bf16[144,1024]{1,0:T(8,128)(2,1)}, bf16[144,1024]{1,0:T(8,128)(2,1)S(1)}, u32[]{:S(2)}, u32[]{:S(2)}) collective-permute-start(bf16[144,1024]{1,0:T(8,128)(2,1)} %get-tuple-element.27.own_ref), channel_id=1, source_target_pairs={{0,8},{4,12},{8,16},{12,20},{16,24},{20,28},{24,0},{28,4},{1,9},{5... | collective-permute-start | bytes 884744 | tf_op jit(solution)/shard_map/ppermute | solution.py:20
  6.1 2.5 %collective-permute-start.1 = (bf16[144,1024]{1,0:T(8,128)(2,1)}, bf16[144,1024]{1,0:T(8,128)(2,1)S(1)}, u32[]{:S(2)}, u32[]{:S(2)}) collective-permute-start(bf16[144,1024]{1,0:T(8,128)(2,1)} %get-tuple-element.36), channel_id=1, source_target_pairs={{0,12},{4,8},{8,20},{12,16},{16,28},{20,24},{24,4},{28,0},{1,13},{... | collective-permute-start | bytes 884744 | tf_op jit(solution)/shard_map/ppermute | solution.py:20
  8.6 1.1 %slice_bitcast_fusion = bf16[128,2048]{1,0:T(8,128)(2,1)S(1)} fusion(bf16[3,128,2048]{2,1,0:T(8,128)(2,1)} %bitcast.13), kind=kLoop, calls=%fused_computation | loop fusion | bytes 1048576 | tf_op jit(solution)/shard_map/squeeze | solution.py:392
  9.7 0.0 copy-done.6
  9.7 0.0 copy-start
  9.7 0.0 copy-start.3
  9.7 0.1 copy.8
  9.8 0.1 broadcast_in_dim.3
  9.9 0.0 copy-done.5
  9.9 0.6 %collective-permute-start.2 = (bf16[144,1024]{1,0:T(8,128)(2,1)}, bf16[144,1024]{1,0:T(8,128)(2,1)S(1)}, u32[]{:S(2)}, u32[]{:S(2)}) collective-permute-start(bf16[144,1024]{1,0:T(8,128)(2,1)} %get-tuple-element.36), channel_id=1, source_target_pairs={{0,4},{4,0},{8,12},{12,8},{16,20},{20,16},{24,28},{28,24},{1,5},{5... | collective-permute-start | bytes 884744 | tf_op jit(solution)/shard_map/ppermute | solution.py:20
  10.5 0.0 copy-done.1
  10.5 0.0 copy-done.2
  10.5 2.8 %shard_map.74 = (bf16[8,2,128,768]{3,2,1,0:T(8,128)(2,1)S(1)}, bf16[8,128,256]{2,1,0:T(8,128)(2,1)S(1)}, f32[3,3,1024]{2,1,0:T(4,128)S(1)}) custom-call(s32[32]{0:T(128)S(1)} %copy-done.2, bf16[16,512]{1,0:T(8,128)(2,1)S(1)} %fusion.taps_ref, f32[3,3,2048]{2,1,0:T(4,128)S(1)} %copy-done.1), custom_call_target="tpu_custom_call" | custom-call | flops 20971520 | bytes 4194304 | tf_op jit(solution)/shard_map/pallas_call | solution.py:400
  13.4 2.8 %collective-permute-done.back_own_ref.refs_0_ = bf16[144,1024]{1,0:T(8,128)(2,1)S(1)} collective-permute-done((bf16[144,1024]{1,0:T(8,128)(2,1)}, bf16[144,1024]{1,0:T(8,128)(2,1)S(1)}, u32[]{:S(2)}, u32[]{:S(2)}) %collective-permute-start) | collective-permute-done | bytes 294944 | tf_op jit(solution)/shard_map/ppermute | solution.py:20
  16.1 6.6 %collective-permute-done.1.back_pair_ref.refs_1_ = bf16[144,1024]{1,0:T(8,128)(2,1)S(1)} collective-permute-done((bf16[144,1024]{1,0:T(8,128)(2,1)}, bf16[144,1024]{1,0:T(8,128)(2,1)S(1)}, u32[]{:S(2)}, u32[]{:S(2)}) %collective-permute-start.1) | collective-permute-done | bytes 294944 | tf_op jit(solution)/shard_map/ppermute | solution.py:20
  22.7 0.7 %shard_map.77 = bf16[144,1024]{1,0:T(8,128)(2,1)S(1)} custom-call(s32[32]{0:T(128)S(1)} %copy-done.2, bf16[8,128,256]{2,1,0:T(8,128)(2,1)S(1)} %get-tuple-element.45.next_ref, bf16[144,1024]{1,0:T(8,128)(2,1)S(1)} %collective-permute-done.back_own_ref.refs_0_, bf16[144,1024]{1,0:T(8,128)(2,1)S(1)} %collective-permute-done.1.back_pair_ref.refs_1_, ...), custom_call_target="tpu_custom_call" | custom-call | flops 67108864 | bytes 1048576 | tf_op jit(solution)/shard_map/pallas_call | solution.py:421
  23.4 0.1 collective-permute-start.4
  23.5 0.6 %collective-permute-start.3 = (bf16[128,1024]{1,0:T(8,128)(2,1)S(1)}, bf16[128,1024]{1,0:T(8,128)(2,1)S(1)}, u32[]{:S(2)}, u32[]{:S(2)}) collective-permute-start(bf16[128,1024]{1,0:T(8,128)(2,1)S(1)} %get-tuple-element.43), channel_id=1, source_target_pairs={{0,4},{4,0},{8,12},{12,8},{16,20},{20,16},{24,28},{28,24},{1,5},{5... | collective-permute-start | bytes 786440 | tf_op jit(solution)/shard_map/ppermute | solution.py:20
  24.0 0.7 %collective-permute-done.2.pair_ref = bf16[144,1024]{1,0:T(8,128)(2,1)S(1)} collective-permute-done((bf16[144,1024]{1,0:T(8,128)(2,1)}, bf16[144,1024]{1,0:T(8,128)(2,1)S(1)}, u32[]{:S(2)}, u32[]{:S(2)}) %collective-permute-start.2) | collective-permute-done | bytes 294944 | tf_op jit(solution)/shard_map/ppermute | solution.py:20
  24.7 0.0 copy-done
  24.7 0.0 copy-done.3
  24.7 1.6 %shard_map.75 = (f32[256,1024]{1,0:T(8,128)S(1)}, f32[128,1024]{1,0:T(8,128)S(1)}, f32[3,8,128]{2,1,0:T(8,128)S(1)}) custom-call(s32[32]{0:T(128)S(1)} %copy-done.2, bf16[8,2,128,768]{3,2,1,0:T(8,128)(2,1)S(1)} %get-tuple-element.35.table_ref, bf16[144,1024]{1,0:T(8,128)(2,1)S(1)} %copy-done, bf16[144,1024]{1,0:T(8,128)(2,1)S(1)} %collective-permute-done.2.pair_ref, ...), custom_call_target="tpu_custom_call" | custom-call | flops 167772160 | bytes 2097152 | tf_op jit(solution)/shard_map/pallas_call | solution.py:436
  26.3 4.4 %collective-permute-done.3.raw_ref = bf16[128,1024]{1,0:T(8,128)(2,1)S(1)} collective-permute-done((bf16[128,1024]{1,0:T(8,128)(2,1)S(1)}, bf16[128,1024]{1,0:T(8,128)(2,1)S(1)}, u32[]{:S(2)}, u32[]{:S(2)}) %collective-permute-start.3) | collective-permute-done | bytes 262176 | tf_op jit(solution)/shard_map/ppermute | solution.py:20
  30.7 0.9 %shard_map.76.qpair_ref = f32[128,1024]{1,0:T(8,128)S(1)} custom-call(s32[32]{0:T(128)S(1)} %copy-done.2, bf16[128,1024]{1,0:T(8,128)(2,1)S(1)} %collective-permute-done.3.raw_ref, bf16[144,1024]{1,0:T(8,128)(2,1)S(1)} %copy-done, bf16[144,1024]{1,0:T(8,128)(2,1)S(1)} %collective-permute-done.back_own_ref.refs_0_, f32[3,3,1024]{2,1,0:T(4,128)S(1)} %get-tuple-element.40.w_ref), custom_call_target="tpu_custom_call" | custom-call | flops 1310720 | bytes 1048576 | tf_op jit(solution)/shard_map/pallas_call | solution.py:445
  31.5 1.5 %collective-permute-done.4.refs_2_ = bf16[144,1024]{1,0:T(8,128)(2,1)S(1)} collective-permute-done((bf16[144,1024]{1,0:T(8,128)(2,1)S(1)}, bf16[144,1024]{1,0:T(8,128)(2,1)S(1)}, u32[]{:S(2)}, u32[]{:S(2)}) %collective-permute-start.4) | collective-permute-done | bytes 294944 | tf_op jit(solution)/shard_map/ppermute | solution.py:20
  33.1 0.0 copy-start.4
  33.1 1.2 %shard_map.78 = (f32[128,1024]{1,0:T(8,128)S(1)}, bf16[128,1024]{1,0:T(8,128)(2,1)S(1)}, f32[1,256]{1,0:T(1,128)S(1)}) custom-call(bf16[8,2,128,768]{3,2,1,0:T(8,128)(2,1)S(1)} %get-tuple-element.35.table_ref, f32[256,1024]{1,0:T(8,128)S(1)} %get-tuple-element.41.acc_ref, f32[128,1024]{1,0:T(8,128)S(1)} %get-tuple-element.42.qown_ref, ...), custom_call_target="tpu_custom_call" | custom-call | flops 167772160 | bytes 3145728 | tf_op jit(solution)/shard_map/pallas_call | solution.py:454
  34.3 0.8 %collective-permute-start.9 = (bf16[128,1024]{1,0:T(8,128)(2,1)S(1)}, bf16[128,1024]{1,0:T(8,128)(2,1)S(1)}, u32[]{:S(2)}, u32[]{:S(2)}) collective-permute-start(bf16[128,1024]{1,0:T(8,128)(2,1)S(1)} %get-tuple-element.48), channel_id=1, source_target_pairs={{0,4},{4,0},{8,12},{12,8},{16,20},{20,16},{24,28},{28,24},{1,5},{5... | collective-permute-start | bytes 786440 | tf_op jit(solution)/shard_map/ppermute | solution.py:20
  35.0 0.0 collective-permute-start.7
  35.0 1.3 %collective-permute-start.6 = (f32[1,256]{1,0:T(1,128)S(1)}, f32[1,256]{1,0:T(1,128)S(1)}, u32[]{:S(2)}, u32[]{:S(2)}) collective-permute-start(f32[1,256]{1,0:T(1,128)S(1)} %get-tuple-element.46), channel_id=1, source_target_pairs={{0,2},{1,3},{2,0},{3,1},{4,6},{5,7},{6,4},{7,5},{8,10},{9,11},{10,... | collective-permute-start | bytes 3080 | tf_op jit(solution)/shard_map/ppermute | solution.py:465
  36.3 0.6 %collective-permute-start.5 = (f32[1,256]{1,0:T(1,128)S(1)}, f32[1,256]{1,0:T(1,128)S(1)}, u32[]{:S(2)}, u32[]{:S(2)}) collective-permute-start(f32[1,256]{1,0:T(1,128)S(1)} %get-tuple-element.46), channel_id=1, source_target_pairs={{0,1},{1,0},{2,3},{3,2},{4,5},{5,4},{6,7},{7,6},{8,9},{9,8},{10,11... | collective-permute-start | bytes 3080 | tf_op jit(solution)/shard_map/ppermute | solution.py:465
  36.9 1.1 %collective-permute-done.7 = f32[1,256]{1,0:T(1,128)S(1)} collective-permute-done((f32[1,256]{1,0:T(1,128)S(1)}, f32[1,256]{1,0:T(1,128)S(1)}, u32[]{:S(2)}, u32[]{:S(2)}) %collective-permute-start.7) | collective-permute-done | bytes 1056 | tf_op jit(solution)/shard_map/ppermute | solution.py:465
  38.0 0.6 %collective-permute-done.6 = f32[1,256]{1,0:T(1,128)S(1)} collective-permute-done((f32[1,256]{1,0:T(1,128)S(1)}, f32[1,256]{1,0:T(1,128)S(1)}, u32[]{:S(2)}, u32[]{:S(2)}) %collective-permute-start.6) | collective-permute-done | bytes 1056 | tf_op jit(solution)/shard_map/ppermute | solution.py:465
  38.6 0.0 collective-permute-done.5
  38.7 1.3 %collective-permute-start.8 = (f32[1,256]{1,0:T(1,128)S(1)}, f32[1,256]{1,0:T(1,128)S(1)}, u32[]{:S(2)}, u32[]{:S(2)}) collective-permute-start(f32[1,256]{1,0:T(1,128)S(1)} %add_add_fusion.power_ref), channel_id=1, source_target_pairs={{0,4},{4,0},{8,12},{12,8},{16,20},{20,16},{24,28},{28,24},{1,5},{5... | collective-permute-start | bytes 3080 | tf_op jit(solution)/shard_map/ppermute | solution.py:20
  40.0 2.3 %collective-permute-done.8.power_got_ref = f32[1,256]{1,0:T(1,128)S(1)} collective-permute-done((f32[1,256]{1,0:T(1,128)S(1)}, f32[1,256]{1,0:T(1,128)S(1)}, u32[]{:S(2)}, u32[]{:S(2)}) %collective-permute-start.8) | collective-permute-done | bytes 1056 | tf_op jit(solution)/shard_map/ppermute | solution.py:20
  42.3 0.0 collective-permute-done.9.got_ref
  42.3 0.0 copy-done.4
  42.3 1.0 %shard_map.79 = bf16[128,2048]{1,0:T(8,128)(2,1)} custom-call(f32[1,256]{1,0:T(1,128)S(1)} %add_add_fusion.power_ref, f32[1,256]{1,0:T(1,128)S(1)} %collective-permute-done.8.power_got_ref, f32[128,1024]{1,0:T(8,128)S(1)} %get-tuple-element.47.kept_ref, bf16[128,1024]{1,0:T(8,128)(2,1)S(1)} %collective-permute-done.9.got_ref, f32[1,2048]{1,0:T(1,128)S(1)} %bitcast.11), custom_call_target="tpu_custom_call" | custom-call | flops 1048576 | bytes 1310720 | tf_op jit(solution)/shard_map/pallas_call | solution.py:467
  (4 shorter events, 0.1 us)
Async XLA Ops:
  0.0 9.9 %copy-start.5 = (f32[16,512]{1,0:T(8,128)S(1)}, f32[16,512]{1,0:T(8,128)}, u32[]{:S(2)}) copy-start(f32[16,512]{1,0:T(8,128)} %param.9) | copy-start | bytes 98308
  0.0 9.7 %copy-start.6 = (s32[16,4]{0,1:T(4,128)S(1)}, s32[16,4]{0,1:T(4,128)}, u32[]{:S(2)}) copy-start(s32[16,4]{0,1:T(4,128)} %param.10) | copy-start | bytes 772
  0.0 10.5 %copy-start.1 = (f32[3,3,2048]{2,1,0:T(4,128)S(1)}, f32[3,3,2048]{2,1,0:T(4,128)}, u32[]{:S(2)}) copy-start(f32[3,3,2048]{2,1,0:T(4,128)} %w_ref.1) | copy-start | bytes 221188
  0.0 10.5 %copy-start.2 = (s32[32]{0:T(128)S(1)}, s32[32]{0:T(128)}, u32[]{:S(2)}) copy-start(s32[32]{0:T(128)} %seq_ref.7) | copy-start | bytes 388
  3.0 13.2 %collective-permute-start = (bf16[144,1024]{1,0:T(8,128)(2,1)}, bf16[144,1024]{1,0:T(8,128)(2,1)S(1)}, u32[]{:S(2)}, u32[]{:S(2)}) collective-permute-start(bf16[144,1024]{1,0:T(8,128)(2,1)} %get-tuple-element.27.own_ref), channel_id=1, source_target_pairs={{0,8},{4,12},{8,16},{12,20},{16,24},{20,28},{24,0},{28,4},{1,9},{5... | collective-permute-start | bytes 884744 | tf_op jit(solution)/shard_map/ppermute | solution.py:20
  6.1 16.6 %collective-permute-start.1 = (bf16[144,1024]{1,0:T(8,128)(2,1)}, bf16[144,1024]{1,0:T(8,128)(2,1)S(1)}, u32[]{:S(2)}, u32[]{:S(2)}) collective-permute-start(bf16[144,1024]{1,0:T(8,128)(2,1)} %get-tuple-element.36), channel_id=1, source_target_pairs={{0,12},{4,8},{8,20},{12,16},{16,28},{20,24},{24,4},{28,0},{1,13},{... | collective-permute-start | bytes 884744 | tf_op jit(solution)/shard_map/ppermute | solution.py:20
  9.7 15.0 %copy-start = (bf16[144,1024]{1,0:T(8,128)(2,1)S(1)}, bf16[144,1024]{1,0:T(8,128)(2,1)}, u32[]{:S(2)}) copy-start(bf16[144,1024]{1,0:T(8,128)(2,1)} %get-tuple-element.27.own_ref) | copy-start | bytes 884740
  9.7 15.0 %copy-start.3 = (f32[2048]{0:T(1024)S(1)}, f32[2048]{0:T(1024)}, u32[]{:S(2)}) copy-start(f32[2048]{0:T(1024)} %param.11) | copy-start | bytes 24580
  9.9 14.8 %collective-permute-start.2 = (bf16[144,1024]{1,0:T(8,128)(2,1)}, bf16[144,1024]{1,0:T(8,128)(2,1)S(1)}, u32[]{:S(2)}, u32[]{:S(2)}) collective-permute-start(bf16[144,1024]{1,0:T(8,128)(2,1)} %get-tuple-element.36), channel_id=1, source_target_pairs={{0,4},{4,0},{8,12},{12,8},{16,20},{20,16},{24,28},{28,24},{1,5},{5... | collective-permute-start | bytes 884744 | tf_op jit(solution)/shard_map/ppermute | solution.py:20
  23.4 9.7 %collective-permute-start.4 = (bf16[144,1024]{1,0:T(8,128)(2,1)S(1)}, bf16[144,1024]{1,0:T(8,128)(2,1)S(1)}, u32[]{:S(2)}, u32[]{:S(2)}) collective-permute-start(bf16[144,1024]{1,0:T(8,128)(2,1)S(1)} %shard_map.77), channel_id=1, source_target_pairs={{0,8},{4,12},{8,16},{12,20},{16,24},{20,28},{24,0},{28,4},{1,9},{5... | collective-permute-start | bytes 884744 | tf_op jit(solution)/shard_map/ppermute | solution.py:20
  23.5 7.2 %collective-permute-start.3 = (bf16[128,1024]{1,0:T(8,128)(2,1)S(1)}, bf16[128,1024]{1,0:T(8,128)(2,1)S(1)}, u32[]{:S(2)}, u32[]{:S(2)}) collective-permute-start(bf16[128,1024]{1,0:T(8,128)(2,1)S(1)} %get-tuple-element.43), channel_id=1, source_target_pairs={{0,4},{4,0},{8,12},{12,8},{16,20},{20,16},{24,28},{28,24},{1,5},{5... | collective-permute-start | bytes 786440 | tf_op jit(solution)/shard_map/ppermute | solution.py:20
  33.1 9.2 %copy-start.4 = (f32[2048]{0:T(1024)S(1)}, f32[2048]{0:T(1024)}, u32[]{:S(2)}) copy-start(f32[2048]{0:T(1024)} %param.12) | copy-start | bytes 24580
  34.3 8.0 %collective-permute-start.9 = (bf16[128,1024]{1,0:T(8,128)(2,1)S(1)}, bf16[128,1024]{1,0:T(8,128)(2,1)S(1)}, u32[]{:S(2)}, u32[]{:S(2)}) collective-permute-start(bf16[128,1024]{1,0:T(8,128)(2,1)S(1)} %get-tuple-element.48), channel_id=1, source_target_pairs={{0,4},{4,0},{8,12},{12,8},{16,20},{20,16},{24,28},{28,24},{1,5},{5... | collective-permute-start | bytes 786440 | tf_op jit(solution)/shard_map/ppermute | solution.py:20
  35.0 3.0 %collective-permute-start.7 = (f32[1,256]{1,0:T(1,128)S(1)}, f32[1,256]{1,0:T(1,128)S(1)}, u32[]{:S(2)}, u32[]{:S(2)}) collective-permute-start(f32[1,256]{1,0:T(1,128)S(1)} %get-tuple-element.46), channel_id=1, source_target_pairs={{0,3},{1,2},{2,1},{3,0},{4,7},{5,6},{6,5},{7,4},{8,11},{9,10},{10,... | collective-permute-start | bytes 3080 | tf_op jit(solution)/shard_map/ppermute | solution.py:465
  35.0 3.6 %collective-permute-start.6 = (f32[1,256]{1,0:T(1,128)S(1)}, f32[1,256]{1,0:T(1,128)S(1)}, u32[]{:S(2)}, u32[]{:S(2)}) collective-permute-start(f32[1,256]{1,0:T(1,128)S(1)} %get-tuple-element.46), channel_id=1, source_target_pairs={{0,2},{1,3},{2,0},{3,1},{4,6},{5,7},{6,4},{7,5},{8,10},{9,11},{10,... | collective-permute-start | bytes 3080 | tf_op jit(solution)/shard_map/ppermute | solution.py:465
  36.3 2.3 %collective-permute-start.5 = (f32[1,256]{1,0:T(1,128)S(1)}, f32[1,256]{1,0:T(1,128)S(1)}, u32[]{:S(2)}, u32[]{:S(2)}) collective-permute-start(f32[1,256]{1,0:T(1,128)S(1)} %get-tuple-element.46), channel_id=1, source_target_pairs={{0,1},{1,0},{2,3},{3,2},{4,5},{5,4},{6,7},{7,6},{8,9},{9,8},{10,11... | collective-permute-start | bytes 3080 | tf_op jit(solution)/shard_map/ppermute | solution.py:465
  38.7 3.6 %collective-permute-start.8 = (f32[1,256]{1,0:T(1,128)S(1)}, f32[1,256]{1,0:T(1,128)S(1)}, u32[]{:S(2)}, u32[]{:S(2)}) collective-permute-start(f32[1,256]{1,0:T(1,128)S(1)} %add_add_fusion.power_ref), channel_id=1, source_target_pairs={{0,4},{4,0},{8,12},{12,8},{16,20},{20,16},{24,28},{28,24},{1,5},{5... | collective-permute-start | bytes 3080 | tf_op jit(solution)/shard_map/ppermute | solution.py:20

commit v6 on v5

--- a/solution.py
+++ b/solution.py
@@ -360,7 +360,6 @@
     spots = range(2 * blocks)
     to_pair = [(i, i ^ 1) for i in spots]
     ahead = [(i, (i + 2) % (2 * blocks)) for i in spots]
-    ahead_pair = [(i, ((i ^ 1) + 2) % (2 * blocks)) for i in spots]
 
     panels = jnp.transpose(projected, (1, 0, 2))
     message = shape((rows + 16, width), jnp.bfloat16)
@@ -387,15 +386,16 @@
         60 << 20,
     )(seq_lengths, panels, short_weight)
 
+    pair = moved(sent, to_pair)
     back_own = moved(kept, ahead)
-    back_pair = moved(sent, ahead_pair)
+    back_pair = moved(pair, ahead)
     filter_taps, query, _ = lax.optimization_barrier((filter_taps, panels[0], kept))
     half = lax.axis_index("half")
     qkept = lax.dynamic_slice_in_dim(query, half * width, width, 1)
     qsent = lax.dynamic_slice_in_dim(query, (1 - half) * width, width, 1)
     scaled = (filter_taps * jnp.repeat(tap_blocks.astype(jnp.float32), BLK, axis=1)).astype(jnp.bfloat16)
-    scaled, sent_late = lax.optimization_barrier((scaled, sent))
-    pair = moved(sent_late, to_pair)
+    pair, qsent = lax.optimization_barrier((pair, qsent))
+    qgot = moved(qsent, to_pair)
     span = taps + 2 * BLK
     table, table_next, w_half = kernel_call(
         tables_kernel,
@@ -410,8 +410,7 @@
         8 * groups * BLK * taps,
     )(seq_lengths, scaled, short_weight)
     table, table_next, back_own = lax.optimization_barrier((table, table_next, back_own))
-    table, back_pair, qsent, qkept = lax.optimization_barrier((table, back_pair, qsent, qkept))
-    qgot = moved(qsent, to_pair)
+    table, back_pair, qkept, qgot = lax.optimization_barrier((table, back_pair, qkept, qgot))
 
     window = pltpu.VMEM((4 * rows, width), jnp.bfloat16)
     extras = pltpu.VMEM((4, 16, width), jnp.float32)

time: 43.5 us -> 44.6 us (1.025)
  starting transfers between devices: 10.8 us -> 12.3 us
    ppermute x7, starting transfers between devices: 8.95 us -> 10.4 us  [moved(): return lax.ppermute(block, SPOTS, pairs)]
  transfers between devices with their start and end apart: 10 -> 10, of which waited for: 8 -> 7; matrix products, arithmetic and copies ran while one was open for 3% -> 3% of each run, Pallas kernels for 14% -> 12%
where the time goes in v6:
time: 44.6 us; the launch traced here: 44.4 us
  waiting for transfers between devices  19.6 us (44%)
  starting transfers between devices  12.3 us (28%)
  Pallas kernels  11.1 us (25%)
  local copies, waits for them, and re-layouts  1.3 us (3%)
    ppermute x7, waiting for transfers between devices, moved(): return lax.ppermute(block, SPOTS, pairs)  17.8 us
    ppermute x7, starting transfers between devices, moved(): return lax.ppermute(block, SPOTS, pairs)  10.4 us
    pallas_call x1, Pallas kernels, shards(): kernel_call(products_kernel, (message, message), [hbm] * 3, [pltpu.SMEM(s...  2.95 us
    pallas_call x1, Pallas kernels, shards(): kernel_call(tables_kernel, (shape((groups, 2, BLK, span), jnp.bfloat16),...  2.81 us
    ppermute x3, starting transfers between devices, shards(): lax.ppermute(power, 'mp', [(i, i ^ k) for i in range(peers)])  1.86 us
    ppermute x3, waiting for transfers between devices, shards(): lax.ppermute(power, 'mp', [(i, i ^ k) for i in range(peers)])  1.74 us
    pallas_call x1, Pallas kernels, shards(): kernel_call(near_kernel, (shape((2 * rows, width), jnp.float32), half_wid...  1.56 us
    pallas_call x1, Pallas kernels, shards(): kernel_call(functools.partial(far_kernel, short), (half_wide, half_shape,...  1.18 us
  transfers between devices with their start and end apart: 10, of which 7 were waited for; matrix products, arithmetic and copies ran while one was open for 3% of the time, Pallas kernels for 12%

profile of v6, /device:TPU:0, one launch (start us, length us, event | category | flops | bytes accessed | tf_op | source)
XLA Modules:
  0.0 44.4 jit_solution(16165424627381029957)
XLA Ops:
  0.0 0.0 copy-start.6
  0.0 0.0 copy-start.5
  0.0 0.0 copy-start.1
  0.0 0.0 copy-start.2
  0.0 2.9 %shard_map.73 = (bf16[144,1024]{1,0:T(8,128)(2,1)}, bf16[144,1024]{1,0:T(8,128)(2,1)}) custom-call(s32[32]{0:T(128)} %seq_ref.7, bf16[3,128,2048]{2,1,0:T(8,128)(2,1)} %bitcast.12, f32[3,3,2048]{2,1,0:T(4,128)} %w_ref.1), custom_call_target="tpu_custom_call" | custom-call | flops 5242880 | bytes 2097152 | tf_op jit(solution)/shard_map/pallas_call | solution.py:370
  3.0 3.1 %collective-permute-start = (bf16[144,1024]{1,0:T(8,128)(2,1)}, bf16[144,1024]{1,0:T(8,128)(2,1)S(1)}, u32[]{:S(2)}, u32[]{:S(2)}) collective-permute-start(bf16[144,1024]{1,0:T(8,128)(2,1)} %get-tuple-element.27.own_ref), channel_id=1, source_target_pairs={{0,8},{4,12},{8,16},{12,20},{16,24},{20,28},{24,0},{28,4},{1,9},{5... | collective-permute-start | bytes 884744 | tf_op jit(solution)/shard_map/ppermute | solution.py:20
  6.1 1.5 %collective-permute-start.1 = (bf16[144,1024]{1,0:T(8,128)(2,1)}, bf16[144,1024]{1,0:T(8,128)(2,1)S(1)}, u32[]{:S(2)}, u32[]{:S(2)}) collective-permute-start(bf16[144,1024]{1,0:T(8,128)(2,1)} %get-tuple-element.32), channel_id=1, source_target_pairs={{0,4},{4,0},{8,12},{12,8},{16,20},{20,16},{24,28},{28,24},{1,5},{5... | collective-permute-start | bytes 884744 | tf_op jit(solution)/shard_map/ppermute | solution.py:20
  7.6 1.1 %slice_bitcast_fusion = bf16[128,2048]{1,0:T(8,128)(2,1)S(1)} fusion(bf16[3,128,2048]{2,1,0:T(8,128)(2,1)} %bitcast.13), kind=kLoop, calls=%fused_computation | loop fusion | bytes 1048576 | tf_op jit(solution)/shard_map/squeeze | solution.py:392
  8.7 0.0 copy-start
  8.7 6.1 %collective-permute-done.1.pair_ref = bf16[144,1024]{1,0:T(8,128)(2,1)S(1)} collective-permute-done((bf16[144,1024]{1,0:T(8,128)(2,1)}, bf16[144,1024]{1,0:T(8,128)(2,1)S(1)}, u32[]{:S(2)}, u32[]{:S(2)}) %collective-permute-start.1) | collective-permute-done | bytes 294944 | tf_op jit(solution)/shard_map/ppermute | solution.py:20
  14.7 1.6 %collective-permute-start.2 = (bf16[144,1024]{1,0:T(8,128)(2,1)S(1)}, bf16[144,1024]{1,0:T(8,128)(2,1)S(1)}, u32[]{:S(2)}, u32[]{:S(2)}) collective-permute-start(bf16[144,1024]{1,0:T(8,128)(2,1)S(1)} %collective-permute-done.1.pair_ref), channel_id=1, source_target_pairs={{0,8},{4,12},{8,16},{12,20},{16,24},{20,28},{24,0},{28,4},{1,9},{5... | collective-permute-start | bytes 884744 | tf_op jit(solution)/shard_map/ppermute | solution.py:20
  16.4 1.6 %collective-permute-start.3 = (bf16[128,1024]{1,0:T(8,128)(2,1)S(1)}, bf16[128,1024]{1,0:T(8,128)(2,1)S(1)}, u32[]{:S(2)}, u32[]{:S(2)}) collective-permute-start(bf16[128,1024]{1,0:T(8,128)(2,1)S(1)} %get-tuple-element.34), channel_id=1, source_target_pairs={{0,4},{4,0},{8,12},{12,8},{16,20},{20,16},{24,28},{28,24},{1,5},{5... | collective-permute-start | bytes 786440 | tf_op jit(solution)/shard_map/ppermute | solution.py:20
  17.9 0.0 copy-done.6
  18.0 0.0 copy-start.3
  18.0 0.1 copy.8
  18.0 0.1 broadcast_in_dim.3
  18.1 0.0 copy-done.5
  18.1 0.0 copy-done.1
  18.2 0.0 copy-done.2
  18.2 2.8 %shard_map.74 = (bf16[8,2,128,768]{3,2,1,0:T(8,128)(2,1)S(1)}, bf16[8,128,256]{2,1,0:T(8,128)(2,1)S(1)}, f32[3,3,1024]{2,1,0:T(4,128)S(1)}) custom-call(s32[32]{0:T(128)S(1)} %copy-done.2, bf16[16,512]{1,0:T(8,128)(2,1)S(1)} %fusion.taps_ref, f32[3,3,2048]{2,1,0:T(4,128)S(1)} %copy-done.1), custom_call_target="tpu_custom_call" | custom-call | flops 20971520 | bytes 4194304 | tf_op jit(solution)/shard_map/pallas_call | solution.py:400
  21.0 0.0 collective-permute-done.back_own_ref.refs_0_
  21.0 2.0 %collective-permute-done.3.raw_ref = bf16[128,1024]{1,0:T(8,128)(2,1)S(1)} collective-permute-done((bf16[128,1024]{1,0:T(8,128)(2,1)S(1)}, bf16[128,1024]{1,0:T(8,128)(2,1)S(1)}, u32[]{:S(2)}, u32[]{:S(2)}) %collective-permute-start.3) | collective-permute-done | bytes 262176 | tf_op jit(solution)/shard_map/ppermute | solution.py:20
  23.0 1.1 %collective-permute-done.2.back_pair_ref.refs_1_ = bf16[144,1024]{1,0:T(8,128)(2,1)S(1)} collective-permute-done((bf16[144,1024]{1,0:T(8,128)(2,1)S(1)}, bf16[144,1024]{1,0:T(8,128)(2,1)S(1)}, u32[]{:S(2)}, u32[]{:S(2)}) %collective-permute-start.2) | collective-permute-done | bytes 294944 | tf_op jit(solution)/shard_map/ppermute | solution.py:20
  24.1 0.7 %shard_map.77 = bf16[144,1024]{1,0:T(8,128)(2,1)S(1)} custom-call(s32[32]{0:T(128)S(1)} %copy-done.2, bf16[8,128,256]{2,1,0:T(8,128)(2,1)S(1)} %get-tuple-element.45.next_ref, bf16[144,1024]{1,0:T(8,128)(2,1)S(1)} %collective-permute-done.back_own_ref.refs_0_, bf16[144,1024]{1,0:T(8,128)(2,1)S(1)} %collective-permute-done.2.back_pair_ref.refs_1_, ...), custom_call_target="tpu_custom_call" | custom-call | flops 67108864 | bytes 1048576 | tf_op jit(solution)/shard_map/pallas_call | solution.py:420
  24.8 0.5 %collective-permute-start.4 = (bf16[144,1024]{1,0:T(8,128)(2,1)S(1)}, bf16[144,1024]{1,0:T(8,128)(2,1)S(1)}, u32[]{:S(2)}, u32[]{:S(2)}) collective-permute-start(bf16[144,1024]{1,0:T(8,128)(2,1)S(1)} %shard_map.77), channel_id=1, source_target_pairs={{0,8},{4,12},{8,16},{12,20},{16,24},{20,28},{24,0},{28,4},{1,9},{5... | collective-permute-start | bytes 884744 | tf_op jit(solution)/shard_map/ppermute | solution.py:20
  25.3 0.0 copy-done
  25.3 0.9 %shard_map.76.qpair_ref = f32[128,1024]{1,0:T(8,128)S(1)} custom-call(s32[32]{0:T(128)S(1)} %copy-done.2, bf16[128,1024]{1,0:T(8,128)(2,1)S(1)} %collective-permute-done.3.raw_ref, bf16[144,1024]{1,0:T(8,128)(2,1)S(1)} %copy-done, bf16[144,1024]{1,0:T(8,128)(2,1)S(1)} %collective-permute-done.back_own_ref.refs_0_, f32[3,3,1024]{2,1,0:T(4,128)S(1)} %get-tuple-element.40.w_ref), custom_call_target="tpu_custom_call" | custom-call | flops 1310720 | bytes 1048576 | tf_op jit(solution)/shard_map/pallas_call | solution.py:444
  26.2 0.0 copy-done.3
  26.2 1.6 %shard_map.75 = (f32[256,1024]{1,0:T(8,128)S(1)}, f32[128,1024]{1,0:T(8,128)S(1)}, f32[3,8,128]{2,1,0:T(8,128)S(1)}) custom-call(s32[32]{0:T(128)S(1)} %copy-done.2, bf16[8,2,128,768]{3,2,1,0:T(8,128)(2,1)S(1)} %get-tuple-element.35.table_ref, bf16[144,1024]{1,0:T(8,128)(2,1)S(1)} %copy-done, bf16[144,1024]{1,0:T(8,128)(2,1)S(1)} %collective-permute-done.1.pair_ref, ...), custom_call_target="tpu_custom_call" | custom-call | flops 167772160 | bytes 2097152 | tf_op jit(solution)/shard_map/pallas_call | solution.py:435
  27.8 5.6 %collective-permute-done.4.refs_2_ = bf16[144,1024]{1,0:T(8,128)(2,1)S(1)} collective-permute-done((bf16[144,1024]{1,0:T(8,128)(2,1)S(1)}, bf16[144,1024]{1,0:T(8,128)(2,1)S(1)}, u32[]{:S(2)}, u32[]{:S(2)}) %collective-permute-start.4) | collective-permute-done | bytes 294944 | tf_op jit(solution)/shard_map/ppermute | solution.py:20
  33.4 0.0 copy-start.4
  33.4 1.2 %shard_map.78 = (f32[128,1024]{1,0:T(8,128)S(1)}, bf16[128,1024]{1,0:T(8,128)(2,1)S(1)}, f32[1,256]{1,0:T(1,128)S(1)}) custom-call(bf16[8,2,128,768]{3,2,1,0:T(8,128)(2,1)S(1)} %get-tuple-element.35.table_ref, f32[256,1024]{1,0:T(8,128)S(1)} %get-tuple-element.41.acc_ref, f32[128,1024]{1,0:T(8,128)S(1)} %get-tuple-element.42.qown_ref, ...), custom_call_target="tpu_custom_call" | custom-call | flops 167772160 | bytes 3145728 | tf_op jit(solution)/shard_map/pallas_call | solution.py:453
  34.6 1.5 %collective-permute-start.9 = (bf16[128,1024]{1,0:T(8,128)(2,1)S(1)}, bf16[128,1024]{1,0:T(8,128)(2,1)S(1)}, u32[]{:S(2)}, u32[]{:S(2)}) collective-permute-start(bf16[128,1024]{1,0:T(8,128)(2,1)S(1)} %get-tuple-element.48), channel_id=1, source_target_pairs={{0,4},{4,0},{8,12},{12,8},{16,20},{20,16},{24,28},{28,24},{1,5},{5... | collective-permute-start | bytes 786440 | tf_op jit(solution)/shard_map/ppermute | solution.py:20
  36.1 0.0 collective-permute-start.7
  36.1 1.5 %collective-permute-start.6 = (f32[1,256]{1,0:T(1,128)S(1)}, f32[1,256]{1,0:T(1,128)S(1)}, u32[]{:S(2)}, u32[]{:S(2)}) collective-permute-start(f32[1,256]{1,0:T(1,128)S(1)} %get-tuple-element.46), channel_id=1, source_target_pairs={{0,2},{1,3},{2,0},{3,1},{4,6},{5,7},{6,4},{7,5},{8,10},{9,11},{10,... | collective-permute-start | bytes 3080 | tf_op jit(solution)/shard_map/ppermute | solution.py:464
  37.6 0.3 collective-permute-start.5
  38.0 1.1 %collective-permute-done.7 = f32[1,256]{1,0:T(1,128)S(1)} collective-permute-done((f32[1,256]{1,0:T(1,128)S(1)}, f32[1,256]{1,0:T(1,128)S(1)}, u32[]{:S(2)}, u32[]{:S(2)}) %collective-permute-start.7) | collective-permute-done | bytes 1056 | tf_op jit(solution)/shard_map/ppermute | solution.py:464
  39.1 0.6 %collective-permute-done.6 = f32[1,256]{1,0:T(1,128)S(1)} collective-permute-done((f32[1,256]{1,0:T(1,128)S(1)}, f32[1,256]{1,0:T(1,128)S(1)}, u32[]{:S(2)}, u32[]{:S(2)}) %collective-permute-start.6) | collective-permute-done | bytes 1056 | tf_op jit(solution)/shard_map/ppermute | solution.py:464
  39.7 0.0 collective-permute-done.5
  39.7 0.6 %collective-permute-start.8 = (f32[1,256]{1,0:T(1,128)S(1)}, f32[1,256]{1,0:T(1,128)S(1)}, u32[]{:S(2)}, u32[]{:S(2)}) collective-permute-start(f32[1,256]{1,0:T(1,128)S(1)} %add_add_fusion.power_ref), channel_id=1, source_target_pairs={{0,4},{4,0},{8,12},{12,8},{16,20},{20,16},{24,28},{28,24},{1,5},{5... | collective-permute-start | bytes 3080 | tf_op jit(solution)/shard_map/ppermute | solution.py:20
  40.3 3.1 %collective-permute-done.8.power_got_ref = f32[1,256]{1,0:T(1,128)S(1)} collective-permute-done((f32[1,256]{1,0:T(1,128)S(1)}, f32[1,256]{1,0:T(1,128)S(1)}, u32[]{:S(2)}, u32[]{:S(2)}) %collective-permute-start.8) | collective-permute-done | bytes 1056 | tf_op jit(solution)/shard_map/ppermute | solution.py:20
  43.3 0.0 collective-permute-done.9.got_ref
  43.4 0.0 copy-done.4
  43.4 1.0 %shard_map.79 = bf16[128,2048]{1,0:T(8,128)(2,1)} custom-call(f32[1,256]{1,0:T(1,128)S(1)} %add_add_fusion.power_ref, f32[1,256]{1,0:T(1,128)S(1)} %collective-permute-done.8.power_got_ref, f32[128,1024]{1,0:T(8,128)S(1)} %get-tuple-element.47.kept_ref, bf16[128,1024]{1,0:T(8,128)(2,1)S(1)} %collective-permute-done.9.got_ref, f32[1,2048]{1,0:T(1,128)S(1)} %bitcast.11), custom_call_target="tpu_custom_call" | custom-call | flops 1048576 | bytes 1310720 | tf_op jit(solution)/shard_map/pallas_call | solution.py:466
  (4 shorter events, 0.1 us)
Async XLA Ops:
  0.0 17.9 %copy-start.6 = (s32[16,4]{0,1:T(4,128)S(1)}, s32[16,4]{0,1:T(4,128)}, u32[]{:S(2)}) copy-start(s32[16,4]{0,1:T(4,128)} %param.10) | copy-start | bytes 772
  0.0 18.1 %copy-start.5 = (f32[16,512]{1,0:T(8,128)S(1)}, f32[16,512]{1,0:T(8,128)}, u32[]{:S(2)}) copy-start(f32[16,512]{1,0:T(8,128)} %param.9) | copy-start | bytes 98308
  0.0 18.1 %copy-start.1 = (f32[3,3,2048]{2,1,0:T(4,128)S(1)}, f32[3,3,2048]{2,1,0:T(4,128)}, u32[]{:S(2)}) copy-start(f32[3,3,2048]{2,1,0:T(4,128)} %w_ref.1) | copy-start | bytes 221188
  0.0 18.1 %copy-start.2 = (s32[32]{0:T(128)S(1)}, s32[32]{0:T(128)}, u32[]{:S(2)}) copy-start(s32[32]{0:T(128)} %seq_ref.7) | copy-start | bytes 388
  3.0 18.0 %collective-permute-start = (bf16[144,1024]{1,0:T(8,128)(2,1)}, bf16[144,1024]{1,0:T(8,128)(2,1)S(1)}, u32[]{:S(2)}, u32[]{:S(2)}) collective-permute-start(bf16[144,1024]{1,0:T(8,128)(2,1)} %get-tuple-element.27.own_ref), channel_id=1, source_target_pairs={{0,8},{4,12},{8,16},{12,20},{16,24},{20,28},{24,0},{28,4},{1,9},{5... | collective-permute-start | bytes 884744 | tf_op jit(solution)/shard_map/ppermute | solution.py:20
  6.1 8.7 %collective-permute-start.1 = (bf16[144,1024]{1,0:T(8,128)(2,1)}, bf16[144,1024]{1,0:T(8,128)(2,1)S(1)}, u32[]{:S(2)}, u32[]{:S(2)}) collective-permute-start(bf16[144,1024]{1,0:T(8,128)(2,1)} %get-tuple-element.32), channel_id=1, source_target_pairs={{0,4},{4,0},{8,12},{12,8},{16,20},{20,16},{24,28},{28,24},{1,5},{5... | collective-permute-start | bytes 884744 | tf_op jit(solution)/shard_map/ppermute | solution.py:20
  8.7 16.7 %copy-start = (bf16[144,1024]{1,0:T(8,128)(2,1)S(1)}, bf16[144,1024]{1,0:T(8,128)(2,1)}, u32[]{:S(2)}) copy-start(bf16[144,1024]{1,0:T(8,128)(2,1)} %get-tuple-element.27.own_ref) | copy-start | bytes 884740
  14.7 9.4 %collective-permute-start.2 = (bf16[144,1024]{1,0:T(8,128)(2,1)S(1)}, bf16[144,1024]{1,0:T(8,128)(2,1)S(1)}, u32[]{:S(2)}, u32[]{:S(2)}) collective-permute-start(bf16[144,1024]{1,0:T(8,128)(2,1)S(1)} %collective-permute-done.1.pair_ref), channel_id=1, source_target_pairs={{0,8},{4,12},{8,16},{12,20},{16,24},{20,28},{24,0},{28,4},{1,9},{5... | collective-permute-start | bytes 884744 | tf_op jit(solution)/shard_map/ppermute | solution.py:20
  16.4 6.6 %collective-permute-start.3 = (bf16[128,1024]{1,0:T(8,128)(2,1)S(1)}, bf16[128,1024]{1,0:T(8,128)(2,1)S(1)}, u32[]{:S(2)}, u32[]{:S(2)}) collective-permute-start(bf16[128,1024]{1,0:T(8,128)(2,1)S(1)} %get-tuple-element.34), channel_id=1, source_target_pairs={{0,4},{4,0},{8,12},{12,8},{16,20},{20,16},{24,28},{28,24},{1,5},{5... | collective-permute-start | bytes 786440 | tf_op jit(solution)/shard_map/ppermute | solution.py:20
  18.0 8.3 %copy-start.3 = (f32[2048]{0:T(1024)S(1)}, f32[2048]{0:T(1024)}, u32[]{:S(2)}) copy-start(f32[2048]{0:T(1024)} %param.11) | copy-start | bytes 24580
  24.8 8.6 %collective-permute-start.4 = (bf16[144,1024]{1,0:T(8,128)(2,1)S(1)}, bf16[144,1024]{1,0:T(8,128)(2,1)S(1)}, u32[]{:S(2)}, u32[]{:S(2)}) collective-permute-start(bf16[144,1024]{1,0:T(8,128)(2,1)S(1)} %shard_map.77), channel_id=1, source_target_pairs={{0,8},{4,12},{8,16},{12,20},{16,24},{20,28},{24,0},{28,4},{1,9},{5... | collective-permute-start | bytes 884744 | tf_op jit(solution)/shard_map/ppermute | solution.py:20
  33.4 10.0 %copy-start.4 = (f32[2048]{0:T(1024)S(1)}, f32[2048]{0:T(1024)}, u32[]{:S(2)}) copy-start(f32[2048]{0:T(1024)} %param.12) | copy-start | bytes 24580
  34.6 8.8 %collective-permute-start.9 = (bf16[128,1024]{1,0:T(8,128)(2,1)S(1)}, bf16[128,1024]{1,0:T(8,128)(2,1)S(1)}, u32[]{:S(2)}, u32[]{:S(2)}) collective-permute-start(bf16[128,1024]{1,0:T(8,128)(2,1)S(1)} %get-tuple-element.48), channel_id=1, source_target_pairs={{0,4},{4,0},{8,12},{12,8},{16,20},{20,16},{24,28},{28,24},{1,5},{5... | collective-permute-start | bytes 786440 | tf_op jit(solution)/shard_map/ppermute | solution.py:20
  36.1 3.0 %collective-permute-start.7 = (f32[1,256]{1,0:T(1,128)S(1)}, f32[1,256]{1,0:T(1,128)S(1)}, u32[]{:S(2)}, u32[]{:S(2)}) collective-permute-start(f32[1,256]{1,0:T(1,128)S(1)} %get-tuple-element.46), channel_id=1, source_target_pairs={{0,3},{1,2},{2,1},{3,0},{4,7},{5,6},{6,5},{7,4},{8,11},{9,10},{10,... | collective-permute-start | bytes 3080 | tf_op jit(solution)/shard_map/ppermute | solution.py:464
  36.1 3.6 %collective-permute-start.6 = (f32[1,256]{1,0:T(1,128)S(1)}, f32[1,256]{1,0:T(1,128)S(1)}, u32[]{:S(2)}, u32[]{:S(2)}) collective-permute-start(f32[1,256]{1,0:T(1,128)S(1)} %get-tuple-element.46), channel_id=1, source_target_pairs={{0,2},{1,3},{2,0},{3,1},{4,6},{5,7},{6,4},{7,5},{8,10},{9,11},{10,... | collective-permute-start | bytes 3080 | tf_op jit(solution)/shard_map/ppermute | solution.py:464
  37.6 2.1 %collective-permute-start.5 = (f32[1,256]{1,0:T(1,128)S(1)}, f32[1,256]{1,0:T(1,128)S(1)}, u32[]{:S(2)}, u32[]{:S(2)}) collective-permute-start(f32[1,256]{1,0:T(1,128)S(1)} %get-tuple-element.46), channel_id=1, source_target_pairs={{0,1},{1,0},{2,3},{3,2},{4,5},{5,4},{6,7},{7,6},{8,9},{9,8},{10,11... | collective-permute-start | bytes 3080 | tf_op jit(solution)/shard_map/ppermute | solution.py:464
  39.7 3.6 %collective-permute-start.8 = (f32[1,256]{1,0:T(1,128)S(1)}, f32[1,256]{1,0:T(1,128)S(1)}, u32[]{:S(2)}, u32[]{:S(2)}) collective-permute-start(f32[1,256]{1,0:T(1,128)S(1)} %add_add_fusion.power_ref), channel_id=1, source_target_pairs={{0,4},{4,0},{8,12},{12,8},{16,20},{20,16},{24,28},{28,24},{1,5},{5... | collective-permute-start | bytes 3080 | tf_op jit(solution)/shard_map/ppermute | solution.py:20

commit v7 on v6

--- a/solution.py
+++ b/solution.py
@@ -425,7 +425,7 @@
             2 * 2 * rows * BLK * width,
             8 * rows * width,
         )(seq_lengths, table_next, back_own, back_pair, w_half)
-        far = (moved(relayed, ahead),)
+        far = (moved(relayed, [(i, j) for i, j in ahead if 2 <= i < j]),)
     else:
         straight = moved(kept[rows:], [(i, (i + 6) % (2 * blocks)) for i in spots])
         across = moved(sent[rows:], [(i, ((i ^ 1) + 6) % (2 * blocks)) for i in spots])

time: 44.6 us -> 41.7 us (0.935)
  the two profiles are of different devices: /device:TPU:0 before, /device:TPU:16 now
where the time goes in v7:
time: 41.7 us; the launch traced here: 41.5 us
  waiting for transfers between devices  17 us (41%)
  starting transfers between devices  11.6 us (28%)
  Pallas kernels  11.4 us (27%)
  local copies, waits for them, and re-layouts  1.3 us (3%)
    ppermute x7, waiting for transfers between devices, moved(): return lax.ppermute(block, SPOTS, pairs)  15.3 us
    ppermute x7, starting transfers between devices, moved(): return lax.ppermute(block, SPOTS, pairs)  9.76 us
    pallas_call x1, Pallas kernels, shards(): kernel_call(products_kernel, (message, message), [hbm] * 3, [pltpu.SMEM(s...  2.96 us
    pallas_call x1, Pallas kernels, shards(): kernel_call(tables_kernel, (shape((groups, 2, BLK, span), jnp.bfloat16),...  2.81 us
    ppermute x3, starting transfers between devices, shards(): lax.ppermute(power, 'mp', [(i, i ^ k) for i in range(peers)])  1.86 us
    ppermute x3, waiting for transfers between devices, shards(): lax.ppermute(power, 'mp', [(i, i ^ k) for i in range(peers)])  1.74 us
    pallas_call x1, Pallas kernels, shards(): kernel_call(near_kernel, (shape((2 * rows, width), jnp.float32), half_wid...  1.57 us
    pallas_call x1, Pallas kernels, shards(): kernel_call(functools.partial(far_kernel, short), (half_wide, half_shape,...  1.18 us
  transfers between devices with their start and end apart: 10, of which 7 were waited for; matrix products, arithmetic and copies ran while one was open for 3% of the time, Pallas kernels for 13%

profile of v7, /device:TPU:16, one launch (start us, length us, event | category | flops | bytes accessed | tf_op | source)
XLA Modules:
  0.0 41.5 jit_solution(15047447762795956650)
XLA Ops:
  0.0 0.0 copy-start.6
  0.0 0.0 copy-start.5
  0.0 0.0 copy-start.1
  0.0 0.0 copy-start.2
  0.0 3.0 %shard_map.73 = (bf16[144,1024]{1,0:T(8,128)(2,1)}, bf16[144,1024]{1,0:T(8,128)(2,1)}) custom-call(s32[32]{0:T(128)} %seq_ref.7, bf16[3,128,2048]{2,1,0:T(8,128)(2,1)} %bitcast.12, f32[3,3,2048]{2,1,0:T(4,128)} %w_ref.1), custom_call_target="tpu_custom_call" | custom-call | flops 5242880 | bytes 2097152 | tf_op jit(solution)/shard_map/pallas_call | solution.py:370
  3.0 1.6 %collective-permute-start = (bf16[144,1024]{1,0:T(8,128)(2,1)}, bf16[144,1024]{1,0:T(8,128)(2,1)S(1)}, u32[]{:S(2)}, u32[]{:S(2)}) collective-permute-start(bf16[144,1024]{1,0:T(8,128)(2,1)} %get-tuple-element.27.own_ref), channel_id=1, source_target_pairs={{0,8},{4,12},{8,16},{12,20},{16,24},{20,28},{24,0},{28,4},{1,9},{5... | collective-permute-start | bytes 884744 | tf_op jit(solution)/shard_map/ppermute | solution.py:20
  4.6 1.5 %collective-permute-start.1 = (bf16[144,1024]{1,0:T(8,128)(2,1)}, bf16[144,1024]{1,0:T(8,128)(2,1)S(1)}, u32[]{:S(2)}, u32[]{:S(2)}) collective-permute-start(bf16[144,1024]{1,0:T(8,128)(2,1)} %get-tuple-element.32), channel_id=1, source_target_pairs={{0,4},{4,0},{8,12},{12,8},{16,20},{20,16},{24,28},{28,24},{1,5},{5... | collective-permute-start | bytes 884744 | tf_op jit(solution)/shard_map/ppermute | solution.py:20
  6.1 1.1 %slice_bitcast_fusion = bf16[128,2048]{1,0:T(8,128)(2,1)S(1)} fusion(bf16[3,128,2048]{2,1,0:T(8,128)(2,1)} %bitcast.13), kind=kLoop, calls=%fused_computation | loop fusion | bytes 1048576 | tf_op jit(solution)/shard_map/squeeze | solution.py:392
  7.2 0.0 copy-start
  7.2 6.1 %collective-permute-done.1.pair_ref = bf16[144,1024]{1,0:T(8,128)(2,1)S(1)} collective-permute-done((bf16[144,1024]{1,0:T(8,128)(2,1)}, bf16[144,1024]{1,0:T(8,128)(2,1)S(1)}, u32[]{:S(2)}, u32[]{:S(2)}) %collective-permute-start.1) | collective-permute-done | bytes 294944 | tf_op jit(solution)/shard_map/ppermute | solution.py:20
  13.3 0.4 collective-permute-start.2
  13.7 1.6 %collective-permute-start.3 = (bf16[128,1024]{1,0:T(8,128)(2,1)S(1)}, bf16[128,1024]{1,0:T(8,128)(2,1)S(1)}, u32[]{:S(2)}, u32[]{:S(2)}) collective-permute-start(bf16[128,1024]{1,0:T(8,128)(2,1)S(1)} %get-tuple-element.34), channel_id=1, source_target_pairs={{0,4},{4,0},{8,12},{12,8},{16,20},{20,16},{24,28},{28,24},{1,5},{5... | collective-permute-start | bytes 786440 | tf_op jit(solution)/shard_map/ppermute | solution.py:20
  15.3 0.0 copy-done.6
  15.3 0.0 copy-start.3
  15.3 0.1 copy.8
  15.4 0.1 broadcast_in_dim.3
  15.5 0.0 copy-done.5
  15.5 0.0 copy-done.1
  15.5 0.0 copy-done.2
  15.5 2.8 %shard_map.74 = (bf16[8,2,128,768]{3,2,1,0:T(8,128)(2,1)S(1)}, bf16[8,128,256]{2,1,0:T(8,128)(2,1)S(1)}, f32[3,3,1024]{2,1,0:T(4,128)S(1)}) custom-call(s32[32]{0:T(128)S(1)} %copy-done.2, bf16[16,512]{1,0:T(8,128)(2,1)S(1)} %fusion.taps_ref, f32[3,3,2048]{2,1,0:T(4,128)S(1)} %copy-done.1), custom_call_target="tpu_custom_call" | custom-call | flops 20971520 | bytes 4194304 | tf_op jit(solution)/shard_map/pallas_call | solution.py:400
  18.3 0.0 collective-permute-done.back_own_ref.refs_0_
  18.3 2.3 %collective-permute-done.3.raw_ref = bf16[128,1024]{1,0:T(8,128)(2,1)S(1)} collective-permute-done((bf16[128,1024]{1,0:T(8,128)(2,1)S(1)}, bf16[128,1024]{1,0:T(8,128)(2,1)S(1)}, u32[]{:S(2)}, u32[]{:S(2)}) %collective-permute-start.3) | collective-permute-done | bytes 262176 | tf_op jit(solution)/shard_map/ppermute | solution.py:20
  20.7 0.2 collective-permute-done.2.back_pair_ref.refs_1_
  20.9 1.0 %shard_map.77 = bf16[144,1024]{1,0:T(8,128)(2,1)S(1)} custom-call(s32[32]{0:T(128)S(1)} %copy-done.2, bf16[8,128,256]{2,1,0:T(8,128)(2,1)S(1)} %get-tuple-element.45.next_ref, bf16[144,1024]{1,0:T(8,128)(2,1)S(1)} %collective-permute-done.back_own_ref.refs_0_, bf16[144,1024]{1,0:T(8,128)(2,1)S(1)} %collective-permute-done.2.back_pair_ref.refs_1_, ...), custom_call_target="tpu_custom_call" | custom-call | flops 67108864 | bytes 1048576 | tf_op jit(solution)/shard_map/pallas_call | solution.py:420
  21.8 2.6 %collective-permute-start.4 = (bf16[144,1024]{1,0:T(8,128)(2,1)S(1)}, bf16[144,1024]{1,0:T(8,128)(2,1)S(1)}, u32[]{:S(2)}, u32[]{:S(2)}) collective-permute-start(bf16[144,1024]{1,0:T(8,128)(2,1)S(1)} %shard_map.77), channel_id=1, source_target_pairs={{8,16},{12,20},{16,24},{20,28},{9,17},{13,21},{17,25},{21,29},{10,... | collective-permute-start | bytes 884744 | tf_op jit(solution)/shard_map/ppermute | solution.py:20
  24.4 0.0 copy-done
  24.4 0.9 %shard_map.76.qpair_ref = f32[128,1024]{1,0:T(8,128)S(1)} custom-call(s32[32]{0:T(128)S(1)} %copy-done.2, bf16[128,1024]{1,0:T(8,128)(2,1)S(1)} %collective-permute-done.3.raw_ref, bf16[144,1024]{1,0:T(8,128)(2,1)S(1)} %copy-done, bf16[144,1024]{1,0:T(8,128)(2,1)S(1)} %collective-permute-done.back_own_ref.refs_0_, f32[3,3,1024]{2,1,0:T(4,128)S(1)} %get-tuple-element.40.w_ref), custom_call_target="tpu_custom_call" | custom-call | flops 1310720 | bytes 1048576 | tf_op jit(solution)/shard_map/pallas_call | solution.py:444
  25.3 0.0 copy-done.3
  25.3 1.6 %shard_map.75 = (f32[256,1024]{1,0:T(8,128)S(1)}, f32[128,1024]{1,0:T(8,128)S(1)}, f32[3,8,128]{2,1,0:T(8,128)S(1)}) custom-call(s32[32]{0:T(128)S(1)} %copy-done.2, bf16[8,2,128,768]{3,2,1,0:T(8,128)(2,1)S(1)} %get-tuple-element.35.table_ref, bf16[144,1024]{1,0:T(8,128)(2,1)S(1)} %copy-done, bf16[144,1024]{1,0:T(8,128)(2,1)S(1)} %collective-permute-done.1.pair_ref, ...), custom_call_target="tpu_custom_call" | custom-call | flops 167772160 | bytes 2097152 | tf_op jit(solution)/shard_map/pallas_call | solution.py:435
  26.9 3.6 %collective-permute-done.4.refs_2_ = bf16[144,1024]{1,0:T(8,128)(2,1)S(1)} collective-permute-done((bf16[144,1024]{1,0:T(8,128)(2,1)S(1)}, bf16[144,1024]{1,0:T(8,128)(2,1)S(1)}, u32[]{:S(2)}, u32[]{:S(2)}) %collective-permute-start.4) | collective-permute-done | bytes 294944 | tf_op jit(solution)/shard_map/ppermute | solution.py:20
  30.5 0.0 copy-start.4
  30.5 1.2 %shard_map.78 = (f32[128,1024]{1,0:T(8,128)S(1)}, bf16[128,1024]{1,0:T(8,128)(2,1)S(1)}, f32[1,256]{1,0:T(1,128)S(1)}) custom-call(bf16[8,2,128,768]{3,2,1,0:T(8,128)(2,1)S(1)} %get-tuple-element.35.table_ref, f32[256,1024]{1,0:T(8,128)S(1)} %get-tuple-element.41.acc_ref, f32[128,1024]{1,0:T(8,128)S(1)} %get-tuple-element.42.qown_ref, ...), custom_call_target="tpu_custom_call" | custom-call | flops 167772160 | bytes 3145728 | tf_op jit(solution)/shard_map/pallas_call | solution.py:453
  31.6 1.6 %collective-permute-start.9 = (bf16[128,1024]{1,0:T(8,128)(2,1)S(1)}, bf16[128,1024]{1,0:T(8,128)(2,1)S(1)}, u32[]{:S(2)}, u32[]{:S(2)}) collective-permute-start(bf16[128,1024]{1,0:T(8,128)(2,1)S(1)} %get-tuple-element.48), channel_id=1, source_target_pairs={{0,4},{4,0},{8,12},{12,8},{16,20},{20,16},{24,28},{28,24},{1,5},{5... | collective-permute-start | bytes 786440 | tf_op jit(solution)/shard_map/ppermute | solution.py:20
  33.2 0.0 collective-permute-start.7
  33.2 1.5 %collective-permute-start.6 = (f32[1,256]{1,0:T(1,128)S(1)}, f32[1,256]{1,0:T(1,128)S(1)}, u32[]{:S(2)}, u32[]{:S(2)}) collective-permute-start(f32[1,256]{1,0:T(1,128)S(1)} %get-tuple-element.46), channel_id=1, source_target_pairs={{0,2},{1,3},{2,0},{3,1},{4,6},{5,7},{6,4},{7,5},{8,10},{9,11},{10,... | collective-permute-start | bytes 3080 | tf_op jit(solution)/shard_map/ppermute | solution.py:464
  34.7 0.3 collective-permute-start.5
  35.0 1.1 %collective-permute-done.7 = f32[1,256]{1,0:T(1,128)S(1)} collective-permute-done((f32[1,256]{1,0:T(1,128)S(1)}, f32[1,256]{1,0:T(1,128)S(1)}, u32[]{:S(2)}, u32[]{:S(2)}) %collective-permute-start.7) | collective-permute-done | bytes 1056 | tf_op jit(solution)/shard_map/ppermute | solution.py:464
  36.2 0.6 %collective-permute-done.6 = f32[1,256]{1,0:T(1,128)S(1)} collective-permute-done((f32[1,256]{1,0:T(1,128)S(1)}, f32[1,256]{1,0:T(1,128)S(1)}, u32[]{:S(2)}, u32[]{:S(2)}) %collective-permute-start.6) | collective-permute-done | bytes 1056 | tf_op jit(solution)/shard_map/ppermute | solution.py:464
  36.8 0.0 collective-permute-done.5
  36.8 0.6 %collective-permute-start.8 = (f32[1,256]{1,0:T(1,128)S(1)}, f32[1,256]{1,0:T(1,128)S(1)}, u32[]{:S(2)}, u32[]{:S(2)}) collective-permute-start(f32[1,256]{1,0:T(1,128)S(1)} %add_add_fusion.power_ref), channel_id=1, source_target_pairs={{0,4},{4,0},{8,12},{12,8},{16,20},{20,16},{24,28},{28,24},{1,5},{5... | collective-permute-start | bytes 3080 | tf_op jit(solution)/shard_map/ppermute | solution.py:20
  37.4 3.1 %collective-permute-done.8.power_got_ref = f32[1,256]{1,0:T(1,128)S(1)} collective-permute-done((f32[1,256]{1,0:T(1,128)S(1)}, f32[1,256]{1,0:T(1,128)S(1)}, u32[]{:S(2)}, u32[]{:S(2)}) %collective-permute-start.8) | collective-permute-done | bytes 1056 | tf_op jit(solution)/shard_map/ppermute | solution.py:20
  40.4 0.0 collective-permute-done.9.got_ref
  40.4 0.0 copy-done.4
  40.4 1.0 %shard_map.79 = bf16[128,2048]{1,0:T(8,128)(2,1)} custom-call(f32[1,256]{1,0:T(1,128)S(1)} %add_add_fusion.power_ref, f32[1,256]{1,0:T(1,128)S(1)} %collective-permute-done.8.power_got_ref, f32[128,1024]{1,0:T(8,128)S(1)} %get-tuple-element.47.kept_ref, bf16[128,1024]{1,0:T(8,128)(2,1)S(1)} %collective-permute-done.9.got_ref, f32[1,2048]{1,0:T(1,128)S(1)} %bitcast.11), custom_call_target="tpu_custom_call" | custom-call | flops 1048576 | bytes 1310720 | tf_op jit(solution)/shard_map/pallas_call | solution.py:466
  (4 shorter events, 0.1 us)
Async XLA Ops:
  0.0 15.3 %copy-start.6 = (s32[16,4]{0,1:T(4,128)S(1)}, s32[16,4]{0,1:T(4,128)}, u32[]{:S(2)}) copy-start(s32[16,4]{0,1:T(4,128)} %param.10) | copy-start | bytes 772
  0.0 15.5 %copy-start.5 = (f32[16,512]{1,0:T(8,128)S(1)}, f32[16,512]{1,0:T(8,128)}, u32[]{:S(2)}) copy-start(f32[16,512]{1,0:T(8,128)} %param.9) | copy-start | bytes 98308
  0.0 15.5 %copy-start.1 = (f32[3,3,2048]{2,1,0:T(4,128)S(1)}, f32[3,3,2048]{2,1,0:T(4,128)}, u32[]{:S(2)}) copy-start(f32[3,3,2048]{2,1,0:T(4,128)} %w_ref.1) | copy-start | bytes 221188
  0.0 15.5 %copy-start.2 = (s32[32]{0:T(128)S(1)}, s32[32]{0:T(128)}, u32[]{:S(2)}) copy-start(s32[32]{0:T(128)} %seq_ref.7) | copy-start | bytes 388
  3.0 15.3 %collective-permute-start = (bf16[144,1024]{1,0:T(8,128)(2,1)}, bf16[144,1024]{1,0:T(8,128)(2,1)S(1)}, u32[]{:S(2)}, u32[]{:S(2)}) collective-permute-start(bf16[144,1024]{1,0:T(8,128)(2,1)} %get-tuple-element.27.own_ref), channel_id=1, source_target_pairs={{0,8},{4,12},{8,16},{12,20},{16,24},{20,28},{24,0},{28,4},{1,9},{5... | collective-permute-start | bytes 884744 | tf_op jit(solution)/shard_map/ppermute | solution.py:20
  4.6 8.7 %collective-permute-start.1 = (bf16[144,1024]{1,0:T(8,128)(2,1)}, bf16[144,1024]{1,0:T(8,128)(2,1)S(1)}, u32[]{:S(2)}, u32[]{:S(2)}) collective-permute-start(bf16[144,1024]{1,0:T(8,128)(2,1)} %get-tuple-element.32), channel_id=1, source_target_pairs={{0,4},{4,0},{8,12},{12,8},{16,20},{20,16},{24,28},{28,24},{1,5},{5... | collective-permute-start | bytes 884744 | tf_op jit(solution)/shard_map/ppermute | solution.py:20
  7.2 17.2 %copy-start = (bf16[144,1024]{1,0:T(8,128)(2,1)S(1)}, bf16[144,1024]{1,0:T(8,128)(2,1)}, u32[]{:S(2)}) copy-start(bf16[144,1024]{1,0:T(8,128)(2,1)} %get-tuple-element.27.own_ref) | copy-start | bytes 884740
  13.3 7.6 %collective-permute-start.2 = (bf16[144,1024]{1,0:T(8,128)(2,1)S(1)}, bf16[144,1024]{1,0:T(8,128)(2,1)S(1)}, u32[]{:S(2)}, u32[]{:S(2)}) collective-permute-start(bf16[144,1024]{1,0:T(8,128)(2,1)S(1)} %collective-permute-done.1.pair_ref), channel_id=1, source_target_pairs={{0,8},{4,12},{8,16},{12,20},{16,24},{20,28},{24,0},{28,4},{1,9},{5... | collective-permute-start | bytes 884744 | tf_op jit(solution)/shard_map/ppermute | solution.py:20
  13.7 7.0 %collective-permute-start.3 = (bf16[128,1024]{1,0:T(8,128)(2,1)S(1)}, bf16[128,1024]{1,0:T(8,128)(2,1)S(1)}, u32[]{:S(2)}, u32[]{:S(2)}) collective-permute-start(bf16[128,1024]{1,0:T(8,128)(2,1)S(1)} %get-tuple-element.34), channel_id=1, source_target_pairs={{0,4},{4,0},{8,12},{12,8},{16,20},{20,16},{24,28},{28,24},{1,5},{5... | collective-permute-start | bytes 786440 | tf_op jit(solution)/shard_map/ppermute | solution.py:20
  15.3 10.0 %copy-start.3 = (f32[2048]{0:T(1024)S(1)}, f32[2048]{0:T(1024)}, u32[]{:S(2)}) copy-start(f32[2048]{0:T(1024)} %param.11) | copy-start | bytes 24580
  21.8 8.6 %collective-permute-start.4 = (bf16[144,1024]{1,0:T(8,128)(2,1)S(1)}, bf16[144,1024]{1,0:T(8,128)(2,1)S(1)}, u32[]{:S(2)}, u32[]{:S(2)}) collective-permute-start(bf16[144,1024]{1,0:T(8,128)(2,1)S(1)} %shard_map.77), channel_id=1, source_target_pairs={{8,16},{12,20},{16,24},{20,28},{9,17},{13,21},{17,25},{21,29},{10,... | collective-permute-start | bytes 884744 | tf_op jit(solution)/shard_map/ppermute | solution.py:20
  30.5 10.0 %copy-start.4 = (f32[2048]{0:T(1024)S(1)}, f32[2048]{0:T(1024)}, u32[]{:S(2)}) copy-start(f32[2048]{0:T(1024)} %param.12) | copy-start | bytes 24580
  31.6 8.8 %collective-permute-start.9 = (bf16[128,1024]{1,0:T(8,128)(2,1)S(1)}, bf16[128,1024]{1,0:T(8,128)(2,1)S(1)}, u32[]{:S(2)}, u32[]{:S(2)}) collective-permute-start(bf16[128,1024]{1,0:T(8,128)(2,1)S(1)} %get-tuple-element.48), channel_id=1, source_target_pairs={{0,4},{4,0},{8,12},{12,8},{16,20},{20,16},{24,28},{28,24},{1,5},{5... | collective-permute-start | bytes 786440 | tf_op jit(solution)/shard_map/ppermute | solution.py:20
  33.2 3.0 %collective-permute-start.7 = (f32[1,256]{1,0:T(1,128)S(1)}, f32[1,256]{1,0:T(1,128)S(1)}, u32[]{:S(2)}, u32[]{:S(2)}) collective-permute-start(f32[1,256]{1,0:T(1,128)S(1)} %get-tuple-element.46), channel_id=1, source_target_pairs={{0,3},{1,2},{2,1},{3,0},{4,7},{5,6},{6,5},{7,4},{8,11},{9,10},{10,... | collective-permute-start | bytes 3080 | tf_op jit(solution)/shard_map/ppermute | solution.py:464
  33.2 3.6 %collective-permute-start.6 = (f32[1,256]{1,0:T(1,128)S(1)}, f32[1,256]{1,0:T(1,128)S(1)}, u32[]{:S(2)}, u32[]{:S(2)}) collective-permute-start(f32[1,256]{1,0:T(1,128)S(1)} %get-tuple-element.46), channel_id=1, source_target_pairs={{0,2},{1,3},{2,0},{3,1},{4,6},{5,7},{6,4},{7,5},{8,10},{9,11},{10,... | collective-permute-start | bytes 3080 | tf_op jit(solution)/shard_map/ppermute | solution.py:464
  34.7 2.1 %collective-permute-start.5 = (f32[1,256]{1,0:T(1,128)S(1)}, f32[1,256]{1,0:T(1,128)S(1)}, u32[]{:S(2)}, u32[]{:S(2)}) collective-permute-start(f32[1,256]{1,0:T(1,128)S(1)} %get-tuple-element.46), channel_id=1, source_target_pairs={{0,1},{1,0},{2,3},{3,2},{4,5},{5,4},{6,7},{7,6},{8,9},{9,8},{10,11... | collective-permute-start | bytes 3080 | tf_op jit(solution)/shard_map/ppermute | solution.py:464
  36.8 3.6 %collective-permute-start.8 = (f32[1,256]{1,0:T(1,128)S(1)}, f32[1,256]{1,0:T(1,128)S(1)}, u32[]{:S(2)}, u32[]{:S(2)}) collective-permute-start(f32[1,256]{1,0:T(1,128)S(1)} %add_add_fusion.power_ref), channel_id=1, source_target_pairs={{0,4},{4,0},{8,12},{12,8},{16,20},{20,16},{24,28},{28,24},{1,5},{5... | collective-permute-start | bytes 3080 | tf_op jit(solution)/shard_map/ppermute | solution.py:20

commit v8 on v5

--- a/solution.py
+++ b/solution.py
@@ -63,9 +63,8 @@
     )
 
 
-def products_kernel(
-    seq_hbm, panels_hbm, w_hbm, sent_ref, kept_ref, seq_ref, kv_ref, q_ref, w_ref, x_ref, m1_ref, m2_ref, sems
-):
+def products_kernel(seq_hbm, panels_hbm, w_hbm, kept_ref, *refs):
+    *sent_refs, seq_ref, kv_ref, q_ref, w_ref, x_ref, m1_ref, m2_ref, sems = refs
     width = kept_ref.shape[1]
     rows = kv_ref.shape[2]
     pieces = kv_ref.shape[0]
@@ -91,10 +90,10 @@
     loads[2 + pieces].wait()
     for p in range(pieces):
         loads[1 + p].wait()
-        out_ref, at = (kept_ref, keep_at) if p < pieces // 2 else (sent_ref, send_at)
+        out_ref, at = (kept_ref, keep_at) if p < pieces // 2 else (sent_refs[p - pieces // 2], send_at)
         for c in range(0, piece, GROUP):
             base = (p % (pieces // 2)) * piece + c
-            there = slice(base, base + GROUP)
+            there = slice(base, base + GROUP) if p < pieces // 2 else slice(c, c + GROUP)
             lanes = pl.ds(pl.multiple_of(at + base, GROUP), GROUP)
             slot = (c // GROUP) % (x_ref.shape[0] // 2) * 2
             heads, tails, made = [], [], []
@@ -119,7 +118,7 @@
     return [1.0 - mark.astype(jnp.float32) for mark in boundaries(seq_ref, t)]
 
 
-def first_rows(now, ahead, w_ref, marks, spot):
+def first_rows(now, ahead, w_ref, marks, spot, lanes=slice(None)):
     m1, m2 = [mark[:, spot : spot + 1] for mark in marks]
     top = lax.broadcasted_iota(jnp.int32, now.shape, 0) == 0
     made = []
@@ -127,7 +126,7 @@
         x0 = pltpu.roll(now, (8 - 2 * i) % 8, 0) if i else now
         x1 = jnp.where(top, pltpu.roll(ahead, 3 - 2 * i, 0), pltpu.roll(now, (9 - 2 * i) % 8, 0))
         x2 = pltpu.roll(ahead, 4 - 2 * i, 0)
-        w = w_ref[1 + i]
+        w = w_ref[1 + i, :, lanes]
         made.append(w[0:1] * x0 + w[1:2] * x1 * m1 + w[2:3] * x2 * m2)
     return made[0] * made[1]
 
@@ -185,29 +184,36 @@
     lax.fori_loop(0, groups, one, 0)
 
 
-def fill(win_ref, extra_ref, spot, message):
-    win_ref[pl.ds(pl.multiple_of(spot * BLK, BLK), BLK), :] = message[:BLK]
-    extra_ref[spot] = message[BLK:].astype(jnp.float32)
-
-
-def relay_kernel(seq_ref, next_ref, back_own_ref, back_pair_ref, w_ref, out_ref, win_ref, extra_ref):
-    groups = next_ref.shape[0]
-    width = groups * GROUP
-    half = lax.axis_index("half")
-    fill(win_ref, extra_ref, half, back_own_ref)
+def fill(win_ref, extra_ref, spot, *pieces):
+    at = 0
+    for piece in pieces:
+        lanes = slice(at, at + piece.shape[1])
+        win_ref[pl.ds(pl.multiple_of(spot * BLK, BLK), BLK), lanes] = piece[:BLK]
+        extra_ref[spot, :, lanes] = piece[BLK:].astype(jnp.float32)
+        at += piece.shape[1]
+
+
+def relay_kernel(piece, seq_ref, next_ref, back_own_ref, back_pair_ref, w_ref, out_ref, win_ref, extra_ref):
+    width = out_ref.shape[1]
+    half = lax.axis_index("half")
+    lanes = slice(piece * width, (piece + 1) * width)
+    fill(win_ref, extra_ref, half, back_own_ref.at[:, lanes])
     fill(win_ref, extra_ref, 1 - half, back_pair_ref)
     marks = edge_marks(seq_ref)
-    rows = first_rows(extra_ref[1, :8], extra_ref[0, :8], w_ref, marks, 3)
+    rows = first_rows(extra_ref[1, :8], extra_ref[0, :8], w_ref, marks, 3, lanes)
     put_first_rows(win_ref, BLK, rows)
     out_ref[BLK:] = extra_ref[1].astype(out_ref.dtype)
     summed = reaches_past(seq_ref, lax.axis_index("blk") + 1)
 
     @pl.when(summed)
     def _():
-        for g in range(groups):
-            lanes = slice(g * GROUP, (g + 1) * GROUP)
-            total = jnp.dot(next_ref[g], win_ref[:, lanes], preferred_element_type=jnp.float32)
-            out_ref[:BLK, lanes] = total.astype(out_ref.dtype)
+        for c in range(0, width, GROUP):
+            total = jnp.dot(
+                next_ref[(piece * width + c) // GROUP],
+                win_ref[:, c : c + GROUP],
+                preferred_element_type=jnp.float32,
+            )
+            out_ref[:BLK, c : c + GROUP] = total.astype(out_ref.dtype)
 
     @pl.when(jnp.logical_not(summed))
     def _():
@@ -228,15 +234,17 @@
 
 
 def near_kernel(
-    seq_ref, table_ref, own_ref, pair_ref, back_own_ref, back_pair_ref, qkept_ref, w_ref, bias_ref,
+    seq_ref, table_ref, own_ref, back_own_ref, pair_a_ref, pair_b_ref, back_a_ref, back_b_ref, qkept_ref, w_ref, bias_ref,
     acc_ref, q_ref, marks_ref, win_ref, extra_ref, x_ref, m1_ref, m2_ref,
 ):
     groups = table_ref.shape[0]
     width = groups * GROUP
     half = lax.axis_index("half")
     block = lax.axis_index("blk")
-    for spot, message in ((half, back_own_ref), (1 - half, back_pair_ref), (2 + half, own_ref), (3 - half, pair_ref)):
-        fill(win_ref, extra_ref, spot, message)
+    fill(win_ref, extra_ref, half, back_own_ref)
+    fill(win_ref, extra_ref, 1 - half, back_a_ref, back_b_ref)
+    fill(win_ref, extra_ref, 2 + half, own_ref)
+    fill(win_ref, extra_ref, 3 - half, pair_a_ref, pair_b_ref)
     marks = edge_marks(seq_ref)
     marks_ref[0], marks_ref[1] = marks
     marks_ref[2] = jnp.full((8, GROUP), reaches_past(seq_ref, block).astype(jnp.float32))
@@ -276,19 +284,19 @@
     width = groups * GROUP
     half = lax.axis_index("half")
     marks = [marks_ref[0], marks_ref[1]]
-    back_own_ref, back_pair_ref, far_ref, *others = messages
+    back_own_ref, back_a_ref, back_b_ref, *far_refs = messages
     low = 1 if short else 0
     fill(win_ref, extra_ref, 2 + half, back_own_ref)
-    fill(win_ref, extra_ref, 3 - half, back_pair_ref)
+    fill(win_ref, extra_ref, 3 - half, back_a_ref, back_b_ref)
     if short:
         summed = marks_ref[2, 0:1, 0:1]
-        payload = far_ref[:BLK].astype(jnp.float32)
+        fill(win_ref, extra_ref, 1, *far_refs)
+        payload = win_ref[BLK : 2 * BLK, :].astype(jnp.float32)
         win_ref[BLK : 2 * BLK, :] = (payload * (1.0 - summed)).astype(win_ref.dtype)
-        extra_ref[1] = far_ref[BLK:].astype(jnp.float32)
     else:
-        fill(win_ref, extra_ref, half, far_ref)
-        fill(win_ref, extra_ref, 1 - half, others[0])
-        ahead = others[1][...].astype(jnp.float32)[:8]
+        fill(win_ref, extra_ref, half, far_refs[0])
+        fill(win_ref, extra_ref, 1 - half, far_refs[1], far_refs[2])
+        ahead = far_refs[3][...].astype(jnp.float32)[:8]
         put_first_rows(win_ref, 0, first_rows(extra_ref[0, :8], ahead, w_ref, marks, 0))
         rows = first_rows(extra_ref[1, :8], extra_ref[0, :8], w_ref, marks, 1)
         put_first_rows(win_ref, BLK, rows)
@@ -306,7 +314,9 @@
             )
             if short:
                 weight = summed * (part == 0).astype(jnp.float32)
-                filtered = filtered + weight * far_ref[:BLK, lanes].astype(jnp.float32)
+                at_far = g * GROUP % far_refs[0].shape[1]
+                far_ref = far_refs[g * GROUP // far_refs[0].shape[1]]
+                filtered = filtered + weight * far_ref[:BLK, at_far : at_far + GROUP].astype(jnp.float32)
             gated = q_ref[:, lanes] * filtered
             squares = squares + gated * gated
             out_ref[:, lanes] = gated.astype(out_ref.dtype)
@@ -360,17 +370,17 @@
     spots = range(2 * blocks)
     to_pair = [(i, i ^ 1) for i in spots]
     ahead = [(i, (i + 2) % (2 * blocks)) for i in spots]
-    ahead_pair = [(i, ((i ^ 1) + 2) % (2 * blocks)) for i in spots]
 
     panels = jnp.transpose(projected, (1, 0, 2))
     message = shape((rows + 16, width), jnp.bfloat16)
+    small = shape((rows + 16, width // 2), jnp.bfloat16)
     hbm = pl.BlockSpec(memory_space=pltpu.HBM)
     pieces = 4
     row_mask = pltpu.VMEM((rows, GROUP), jnp.float32)
 
-    sent, kept = kernel_call(
+    kept, *sent = kernel_call(
         products_kernel,
-        (message, message),
+        (message, small, small),
         [hbm] * 3,
         [
             pltpu.SMEM(seq_lengths.shape, jnp.int32),
@@ -388,14 +398,10 @@
     )(seq_lengths, panels, short_weight)
 
     back_own = moved(kept, ahead)
-    back_pair = moved(sent, ahead_pair)
-    filter_taps, query, _ = lax.optimization_barrier((filter_taps, panels[0], kept))
-    half = lax.axis_index("half")
-    qkept = lax.dynamic_slice_in_dim(query, half * width, width, 1)
-    qsent = lax.dynamic_slice_in_dim(query, (1 - half) * width, width, 1)
+    pair = [moved(piece, to_pair) for piece in sent]
+
+    filter_taps, _ = lax.optimization_barrier((filter_taps, kept))
     scaled = (filter_taps * jnp.repeat(tap_blocks.astype(jnp.float32), BLK, axis=1)).astype(jnp.bfloat16)
-    scaled, sent_late = lax.optimization_barrier((scaled, sent))
-    pair = moved(sent_late, to_pair)
     span = taps + 2 * BLK
     table, table_next, w_half = kernel_call(
         tables_kernel,
@@ -409,8 +415,13 @@
         40 * groups * BLK * taps,
         8 * groups * BLK * taps,
     )(seq_lengths, scaled, short_weight)
-    table, table_next, back_own = lax.optimization_barrier((table, table_next, back_own))
-    table, back_pair, qsent, qkept = lax.optimization_barrier((table, back_pair, qsent, qkept))
+    table, table_next, pair[0] = lax.optimization_barrier((table, table_next, pair[0]))
+    back_pair = [moved(piece, ahead) for piece in pair]
+
+    half = lax.axis_index("half")
+    query, pair[0] = lax.optimization_barrier((panels[0], pair[0]))
+    qkept = lax.dynamic_slice_in_dim(query, half * width, width, 1)
+    qsent = lax.dynamic_slice_in_dim(query, (1 - half) * width, width, 1)
     qgot = moved(qsent, to_pair)
 
     window = pltpu.VMEM((4 * rows, width), jnp.bfloat16)
@@ -418,29 +429,33 @@
     shifted = pltpu.VMEM((2, rows + 8, GROUP), jnp.float32)
     short = whole_tokens // 2 <= 4 * BLK
     if short:
-        relayed = kernel_call(
-            relay_kernel,
-            message,
-            [SMEM] + [VMEM] * 4,
-            [pltpu.VMEM((2 * rows, width), jnp.bfloat16), pltpu.VMEM((2, 16, width), jnp.float32)],
-            2 * 2 * rows * BLK * width,
-            8 * rows * width,
-        )(seq_lengths, table_next, back_own, back_pair, w_half)
-        far = (moved(relayed, ahead),)
+        onward = [(i, i if i < 2 else i + 2 if i + 2 < 2 * blocks else 2 + i % 2) for i in spots]
+        far = []
+        for piece in range(2):
+            relayed = kernel_call(
+                functools.partial(relay_kernel, piece),
+                small,
+                [SMEM] + [VMEM] * 4,
+                [pltpu.VMEM((2 * rows, width // 2), jnp.bfloat16), pltpu.VMEM((2, 16, width // 2), jnp.float32)],
+                2 * rows * BLK * width,
+                4 * rows * width,
+            )(seq_lengths, table_next, back_own, back_pair[piece], w_half)
+            far.append(moved(relayed, onward))
     else:
+        across = jnp.concatenate([piece[rows:] for piece in sent], 1)
+        across = moved(across, [(i, ((i ^ 1) + 6) % (2 * blocks)) for i in spots])
         straight = moved(kept[rows:], [(i, (i + 6) % (2 * blocks)) for i in spots])
-        across = moved(sent[rows:], [(i, ((i ^ 1) + 6) % (2 * blocks)) for i in spots])
         deep = jnp.where(half == 1, straight, across)
-        far = (moved(back_own, ahead), moved(back_pair, ahead), deep)
+        far = [moved(piece, ahead) for piece in (back_own, *back_pair)] + [deep]
 
     acc, qown, marks = kernel_call(
         near_kernel,
         (shape((2 * rows, width), jnp.float32), half_wide, shape((3, 8, GROUP), jnp.float32)),
-        [SMEM] + [VMEM] * 8,
+        [SMEM] + [VMEM] * 10,
         [window, extras, shifted, row_mask, row_mask],
         2 * 5 * rows * BLK * width,
         16 * rows * width,
-    )(seq_lengths, table, kept, pair, back_own, back_pair, qkept, w_half, skip_bias.reshape(1, -1))
+    )(seq_lengths, table, kept, back_own, *pair, *back_pair, qkept, w_half, skip_bias.reshape(1, -1))
 
     qpair = kernel_call(
         pair_gate_kernel,
@@ -454,11 +469,11 @@
     done, send, power = kernel_call(
         functools.partial(far_kernel, short),
         (half_wide, half_shape, shape((1, 2 * rows), jnp.float32)),
-        [VMEM] * (8 + len(far)),
+        [VMEM] * (9 + len(far)),
         [window, extras],
         2 * 5 * rows * BLK * width,
         24 * rows * width,
-    )(table, acc, qown, qpair, w_half, marks, back_own, back_pair, *far)
+    )(table, acc, qown, qpair, w_half, marks, back_own, *back_pair, *far)
 
     back = moved(send, to_pair)
     peers = lax.axis_size("mp")

time: 43.5 us -> 42.7 us (0.982)
  the two profiles are of different devices: /device:TPU:0 before, /device:TPU:8 now
where the time goes in v8:
time: 42.7 us; the launch traced here: 42.6 us
  starting transfers between devices  19 us (44%)
  Pallas kernels  12.1 us (28%)
  waiting for transfers between devices  10.1 us (24%)
  local copies, waits for them, and re-layouts  1.31 us (3%)
    ppermute x10, starting transfers between devices, moved(): return lax.ppermute(block, SPOTS, pairs)  16.8 us
    ppermute x10, waiting for transfers between devices, moved(): return lax.ppermute(block, SPOTS, pairs)  7.03 us
    ppermute x3, waiting for transfers between devices, shards(): lax.ppermute(power, 'mp', [(i, i ^ k) for i in range(peers)])  3.03 us
    pallas_call x1, Pallas kernels, shards(): kernel_call(products_kernel, (message, small, small), [hbm] * 3, [pltpu.S...  2.88 us
    pallas_call x1, Pallas kernels, shards(): kernel_call(tables_kernel, (shape((groups, 2, BLK, span), jnp.bfloat16),...  2.81 us
    ppermute x3, starting transfers between devices, shards(): lax.ppermute(power, 'mp', [(i, i ^ k) for i in range(peers)])  2.14 us
    pallas_call x2, Pallas kernels, shards(): kernel_call(functools.partial(relay_kernel, piece), small, [SMEM] + [VMEM...  1.77 us
    pallas_call x1, Pallas kernels, shards(): kernel_call(near_kernel, (shape((2 * rows, width), jnp.float32), half_wid...  1.55 us
  transfers between devices with their start and end apart: 13, of which 5 were waited for; matrix products, arithmetic and copies ran while one was open for 3% of the time, Pallas kernels for 16%

profile of v8, /device:TPU:8, one launch (start us, length us, event | category | flops | bytes accessed | tf_op | source)
XLA Modules:
  0.0 42.6 jit_solution(18103266375043925213)
XLA Ops:
  0.0 0.0 copy-start.2
  0.0 0.0 copy-start.6
  0.0 2.9 %shard_map.73 = (bf16[144,1024]{1,0:T(8,128)(2,1)}, bf16[144,512]{1,0:T(8,128)(2,1)}, bf16[144,512]{1,0:T(8,128)(2,1)}) custom-call(s32[32]{0:T(128)} %seq_ref.9, bf16[3,128,2048]{2,1,0:T(8,128)(2,1)} %bitcast.12, f32[3,3,2048]{2,1,0:T(4,128)} %w_ref.1), custom_call_target="tpu_custom_call" | custom-call | flops 5242880 | bytes 2097152 | tf_op jit(solution)/shard_map/pallas_call | solution.py:381
  2.9 1.6 %collective-permute-start = (bf16[144,512]{1,0:T(8,128)(2,1)}, bf16[144,512]{1,0:T(8,128)(2,1)S(1)}, u32[]{:S(2)}, u32[]{:S(2)}) collective-permute-start(bf16[144,512]{1,0:T(8,128)(2,1)} %get-tuple-element.27), channel_id=1, source_target_pairs={{0,4},{4,0},{8,12},{12,8},{16,20},{20,16},{24,28},{28,24},{1,5},{5... | collective-permute-start | bytes 442376 | tf_op jit(solution)/shard_map/ppermute | solution.py:20
  4.5 1.6 %collective-permute-start.1 = (bf16[144,1024]{1,0:T(8,128)(2,1)}, bf16[144,1024]{1,0:T(8,128)(2,1)S(1)}, u32[]{:S(2)}, u32[]{:S(2)}) collective-permute-start(bf16[144,1024]{1,0:T(8,128)(2,1)} %get-tuple-element.23.own_ref), channel_id=1, source_target_pairs={{0,8},{4,12},{8,16},{12,20},{16,24},{20,28},{24,0},{28,4},{1,9},{5... | collective-permute-start | bytes 884744 | tf_op jit(solution)/shard_map/ppermute | solution.py:20
  6.1 0.5 %collective-permute-start.2 = (bf16[144,512]{1,0:T(8,128)(2,1)}, bf16[144,512]{1,0:T(8,128)(2,1)S(1)}, u32[]{:S(2)}, u32[]{:S(2)}) collective-permute-start(bf16[144,512]{1,0:T(8,128)(2,1)} %get-tuple-element.31), channel_id=1, source_target_pairs={{0,4},{4,0},{8,12},{12,8},{16,20},{20,16},{24,28},{28,24},{1,5},{5... | collective-permute-start | bytes 442376 | tf_op jit(solution)/shard_map/ppermute | solution.py:20
  6.6 1.1 %slice_bitcast_fusion = bf16[128,2048]{1,0:T(8,128)(2,1)S(1)} fusion(bf16[3,128,2048]{2,1,0:T(8,128)(2,1)} %bitcast.13), kind=kLoop, calls=%fused_computation | loop fusion | bytes 1048576 | tf_op jit(solution)/shard_map/squeeze | solution.py:422
  7.7 0.0 copy-done.6
  7.7 0.1 copy.8
  7.8 0.1 broadcast_in_dim.3
  7.8 0.0 copy-done.5
  7.9 0.0 copy-done.2
  7.9 0.0 copy-done.1
  7.9 2.8 %shard_map.74 = (bf16[8,2,128,768]{3,2,1,0:T(8,128)(2,1)S(1)}, bf16[8,128,256]{2,1,0:T(8,128)(2,1)S(1)}, f32[3,3,1024]{2,1,0:T(4,128)S(1)}) custom-call(s32[32]{0:T(128)S(1)} %copy-done.2, bf16[16,512]{1,0:T(8,128)(2,1)S(1)} %fusion.taps_ref, f32[3,3,2048]{2,1,0:T(4,128)S(1)} %copy-done.1), custom_call_target="tpu_custom_call" | custom-call | flops 20971520 | bytes 4194304 | tf_op jit(solution)/shard_map/pallas_call | solution.py:406
  10.7 0.0 collective-permute-done.pair_a_ref
  10.7 0.0 copy-start
  10.7 0.0 copy-start.3
  10.7 1.6 %collective-permute-start.3 = (bf16[144,512]{1,0:T(8,128)(2,1)S(1)}, bf16[144,512]{1,0:T(8,128)(2,1)S(1)}, u32[]{:S(2)}, u32[]{:S(2)}) collective-permute-start(bf16[144,512]{1,0:T(8,128)(2,1)S(1)} %collective-permute-done.pair_a_ref), channel_id=1, source_target_pairs={{0,8},{4,12},{8,16},{12,20},{16,24},{20,28},{24,0},{28,4},{1,9},{5... | collective-permute-start | bytes 442376 | tf_op jit(solution)/shard_map/ppermute | solution.py:20
  12.4 0.0 collective-permute-done.2.pair_b_ref
  12.4 1.1 %collective-permute-start.4 = (bf16[144,512]{1,0:T(8,128)(2,1)S(1)}, bf16[144,512]{1,0:T(8,128)(2,1)S(1)}, u32[]{:S(2)}, u32[]{:S(2)}) collective-permute-start(bf16[144,512]{1,0:T(8,128)(2,1)S(1)} %collective-permute-done.2.pair_b_ref), channel_id=1, source_target_pairs={{0,8},{4,12},{8,16},{12,20},{16,24},{20,28},{24,0},{28,4},{1,9},{5... | collective-permute-start | bytes 442376 | tf_op jit(solution)/shard_map/ppermute | solution.py:20
  13.5 1.6 %collective-permute-start.5 = (bf16[128,1024]{1,0:T(8,128)(2,1)S(1)}, bf16[128,1024]{1,0:T(8,128)(2,1)S(1)}, u32[]{:S(2)}, u32[]{:S(2)}) collective-permute-start(bf16[128,1024]{1,0:T(8,128)(2,1)S(1)} %get-tuple-element.41), channel_id=1, source_target_pairs={{0,4},{4,0},{8,12},{12,8},{16,20},{20,16},{24,28},{28,24},{1,5},{5... | collective-permute-start | bytes 786440 | tf_op jit(solution)/shard_map/ppermute | solution.py:20
  15.1 2.5 %collective-permute-done.3.back_a_ref.back_pair_ref.refs_1_ = bf16[144,512]{1,0:T(8,128)(2,1)S(1)} collective-permute-done((bf16[144,512]{1,0:T(8,128)(2,1)S(1)}, bf16[144,512]{1,0:T(8,128)(2,1)S(1)}, u32[]{:S(2)}, u32[]{:S(2)}) %collective-permute-start.3) | collective-permute-done | bytes 147488 | tf_op jit(solution)/shard_map/ppermute | solution.py:20
  17.6 0.0 collective-permute-done.1.back_own_ref.refs_0_
  17.6 0.9 %shard_map.77 = bf16[144,512]{1,0:T(8,128)(2,1)S(1)} custom-call(s32[32]{0:T(128)S(1)} %copy-done.2, bf16[8,128,256]{2,1,0:T(8,128)(2,1)S(1)} %get-tuple-element.37.next_ref, bf16[144,1024]{1,0:T(8,128)(2,1)S(1)} %collective-permute-done.1.back_own_ref.refs_0_, bf16[144,512]{1,0:T(8,128)(2,1)S(1)} %collective-permute-done.3.back_a_ref.back_pair_ref.refs_1_, ...), custom_call_target="tpu_custom_call" | custom-call | flops 33554432 | bytes 524288 | tf_op jit(solution)/shard_map/pallas_call | solution.py:435
  18.5 3.3 %collective-permute-start.6 = (bf16[144,512]{1,0:T(8,128)(2,1)S(1)}, bf16[144,512]{1,0:T(8,128)(2,1)S(1)}, u32[]{:S(2)}, u32[]{:S(2)}) collective-permute-start(bf16[144,512]{1,0:T(8,128)(2,1)S(1)} %shard_map.77), channel_id=1, source_target_pairs={{0,0},{4,4},{8,16},{12,20},{16,24},{20,28},{24,8},{28,12},{1,1},{5... | collective-permute-start | bytes 442376 | tf_op jit(solution)/shard_map/ppermute | solution.py:20
  21.8 0.0 collective-permute-done.4.back_b_ref.back_pair_ref.refs_2_
  21.8 0.9 %shard_map.78 = bf16[144,512]{1,0:T(8,128)(2,1)S(1)} custom-call(s32[32]{0:T(128)S(1)} %copy-done.2, bf16[8,128,256]{2,1,0:T(8,128)(2,1)S(1)} %get-tuple-element.37.next_ref, bf16[144,1024]{1,0:T(8,128)(2,1)S(1)} %collective-permute-done.1.back_own_ref.refs_0_, bf16[144,512]{1,0:T(8,128)(2,1)S(1)} %collective-permute-done.4.back_b_ref.back_pair_ref.refs_2_, ...), custom_call_target="tpu_custom_call" | custom-call | flops 33554432 | bytes 524288 | tf_op jit(solution)/shard_map/pallas_call | solution.py:435
  22.7 3.5 %collective-permute-start.7 = (bf16[144,512]{1,0:T(8,128)(2,1)S(1)}, bf16[144,512]{1,0:T(8,128)(2,1)S(1)}, u32[]{:S(2)}, u32[]{:S(2)}) collective-permute-start(bf16[144,512]{1,0:T(8,128)(2,1)S(1)} %shard_map.78), channel_id=1, source_target_pairs={{0,0},{4,4},{8,16},{12,20},{16,24},{20,28},{24,8},{28,12},{1,1},{5... | collective-permute-start | bytes 442376 | tf_op jit(solution)/shard_map/ppermute | solution.py:20
  26.2 0.0 copy-done
  26.2 0.0 copy-done.3
  26.2 1.6 %shard_map.75 = (f32[256,1024]{1,0:T(8,128)S(1)}, f32[128,1024]{1,0:T(8,128)S(1)}, f32[3,8,128]{2,1,0:T(8,128)S(1)}) custom-call(s32[32]{0:T(128)S(1)} %copy-done.2, bf16[8,2,128,768]{3,2,1,0:T(8,128)(2,1)S(1)} %get-tuple-element.28.table_ref, bf16[144,1024]{1,0:T(8,128)(2,1)S(1)} %copy-done, ...), custom_call_target="tpu_custom_call" | custom-call | flops 167772160 | bytes 2097152 | tf_op jit(solution)/shard_map/pallas_call | solution.py:451
  27.7 0.0 collective-permute-done.5.raw_ref
  27.8 0.9 %shard_map.76.qpair_ref = f32[128,1024]{1,0:T(8,128)S(1)} custom-call(s32[32]{0:T(128)S(1)} %copy-done.2, bf16[128,1024]{1,0:T(8,128)(2,1)S(1)} %collective-permute-done.5.raw_ref, bf16[144,1024]{1,0:T(8,128)(2,1)S(1)} %copy-done, bf16[144,1024]{1,0:T(8,128)(2,1)S(1)} %collective-permute-done.1.back_own_ref.refs_0_, f32[3,3,1024]{2,1,0:T(4,128)S(1)} %get-tuple-element.33.w_ref), custom_call_target="tpu_custom_call" | custom-call | flops 1310720 | bytes 1048576 | tf_op jit(solution)/shard_map/pallas_call | solution.py:460
  28.6 0.0 collective-permute-done.6.refs_3_
  28.6 2.0 %collective-permute-done.7.refs_4_ = bf16[144,512]{1,0:T(8,128)(2,1)S(1)} collective-permute-done((bf16[144,512]{1,0:T(8,128)(2,1)S(1)}, bf16[144,512]{1,0:T(8,128)(2,1)S(1)}, u32[]{:S(2)}, u32[]{:S(2)}) %collective-permute-start.7) | collective-permute-done | bytes 147488 | tf_op jit(solution)/shard_map/ppermute | solution.py:20
  30.6 1.1 %shard_map.79 = (f32[128,1024]{1,0:T(8,128)S(1)}, bf16[128,1024]{1,0:T(8,128)(2,1)S(1)}, f32[1,256]{1,0:T(1,128)S(1)}) custom-call(bf16[8,2,128,768]{3,2,1,0:T(8,128)(2,1)S(1)} %get-tuple-element.28.table_ref, f32[256,1024]{1,0:T(8,128)S(1)} %get-tuple-element.34.acc_ref, f32[128,1024]{1,0:T(8,128)S(1)} %get-tuple-element.35.qown_ref, ...), custom_call_target="tpu_custom_call" | custom-call | flops 167772160 | bytes 3145728 | tf_op jit(solution)/shard_map/pallas_call | solution.py:469
  31.7 1.1 %collective-permute-start.12 = (bf16[128,1024]{1,0:T(8,128)(2,1)S(1)}, bf16[128,1024]{1,0:T(8,128)(2,1)S(1)}, u32[]{:S(2)}, u32[]{:S(2)}) collective-permute-start(bf16[128,1024]{1,0:T(8,128)(2,1)S(1)} %get-tuple-element.40), channel_id=1, source_target_pairs={{0,4},{4,0},{8,12},{12,8},{16,20},{20,16},{24,28},{28,24},{1,5},{5... | collective-permute-start | bytes 786440 | tf_op jit(solution)/shard_map/ppermute | solution.py:20
  32.8 0.0 collective-permute-start.10
  32.8 1.6 %collective-permute-start.8 = (f32[1,256]{1,0:T(1,128)S(1)}, f32[1,256]{1,0:T(1,128)S(1)}, u32[]{:S(2)}, u32[]{:S(2)}) collective-permute-start(f32[1,256]{1,0:T(1,128)S(1)} %get-tuple-element.38), channel_id=1, source_target_pairs={{0,1},{1,0},{2,3},{3,2},{4,5},{5,4},{6,7},{7,6},{8,9},{9,8},{10,11... | collective-permute-start | bytes 3080 | tf_op jit(solution)/shard_map/ppermute | solution.py:480
  34.4 0.5 %collective-permute-start.9 = (f32[1,256]{1,0:T(1,128)S(1)}, f32[1,256]{1,0:T(1,128)S(1)}, u32[]{:S(2)}, u32[]{:S(2)}) collective-permute-start(f32[1,256]{1,0:T(1,128)S(1)} %get-tuple-element.38), channel_id=1, source_target_pairs={{0,2},{1,3},{2,0},{3,1},{4,6},{5,7},{6,4},{7,5},{8,10},{9,11},{10,... | collective-permute-start | bytes 3080 | tf_op jit(solution)/shard_map/ppermute | solution.py:480
  35.0 0.9 %collective-permute-done.10 = f32[1,256]{1,0:T(1,128)S(1)} collective-permute-done((f32[1,256]{1,0:T(1,128)S(1)}, f32[1,256]{1,0:T(1,128)S(1)}, u32[]{:S(2)}, u32[]{:S(2)}) %collective-permute-start.10) | collective-permute-done | bytes 1056 | tf_op jit(solution)/shard_map/ppermute | solution.py:480
  35.8 0.0 collective-permute-done.8
  35.8 2.2 %collective-permute-done.9 = f32[1,256]{1,0:T(1,128)S(1)} collective-permute-done((f32[1,256]{1,0:T(1,128)S(1)}, f32[1,256]{1,0:T(1,128)S(1)}, u32[]{:S(2)}, u32[]{:S(2)}) %collective-permute-start.9) | collective-permute-done | bytes 1056 | tf_op jit(solution)/shard_map/ppermute | solution.py:480
  38.0 1.0 %collective-permute-start.11 = (f32[1,256]{1,0:T(1,128)S(1)}, f32[1,256]{1,0:T(1,128)S(1)}, u32[]{:S(2)}, u32[]{:S(2)}) collective-permute-start(f32[1,256]{1,0:T(1,128)S(1)} %add_add_fusion.power_ref), channel_id=1, source_target_pairs={{0,4},{4,0},{8,12},{12,8},{16,20},{20,16},{24,28},{28,24},{1,5},{5... | collective-permute-start | bytes 3080 | tf_op jit(solution)/shard_map/ppermute | solution.py:20
  39.0 2.6 %collective-permute-done.11.power_got_ref = f32[1,256]{1,0:T(1,128)S(1)} collective-permute-done((f32[1,256]{1,0:T(1,128)S(1)}, f32[1,256]{1,0:T(1,128)S(1)}, u32[]{:S(2)}, u32[]{:S(2)}) %collective-permute-start.11) | collective-permute-done | bytes 1056 | tf_op jit(solution)/shard_map/ppermute | solution.py:20
  41.6 0.0 collective-permute-done.12.got_ref
  41.6 0.0 copy-done.4
  41.6 1.0 %shard_map.80 = bf16[128,2048]{1,0:T(8,128)(2,1)} custom-call(f32[1,256]{1,0:T(1,128)S(1)} %add_add_fusion.power_ref, f32[1,256]{1,0:T(1,128)S(1)} %collective-permute-done.11.power_got_ref, f32[128,1024]{1,0:T(8,128)S(1)} %get-tuple-element.39.kept_ref, bf16[128,1024]{1,0:T(8,128)(2,1)S(1)} %collective-permute-done.12.got_ref, f32[1,2048]{1,0:T(1,128)S(1)} %bitcast.11), custom_call_target="tpu_custom_call" | custom-call | flops 1048576 | bytes 1310720 | tf_op jit(solution)/shard_map/pallas_call | solution.py:482
  (7 shorter events, 0.1 us)
Async XLA Ops:
  0.0 7.9 %copy-start.2 = (s32[32]{0:T(128)S(1)}, s32[32]{0:T(128)}, u32[]{:S(2)}) copy-start(s32[32]{0:T(128)} %seq_ref.9) | copy-start | bytes 388
  0.0 7.9 %copy-start.1 = (f32[3,3,2048]{2,1,0:T(4,128)S(1)}, f32[3,3,2048]{2,1,0:T(4,128)}, u32[]{:S(2)}) copy-start(f32[3,3,2048]{2,1,0:T(4,128)} %w_ref.1) | copy-start | bytes 221188
  0.0 7.8 %copy-start.5 = (f32[16,512]{1,0:T(8,128)S(1)}, f32[16,512]{1,0:T(8,128)}, u32[]{:S(2)}) copy-start(f32[16,512]{1,0:T(8,128)} %param.9) | copy-start | bytes 98308
  0.0 7.7 %copy-start.6 = (s32[16,4]{0,1:T(4,128)S(1)}, s32[16,4]{0,1:T(4,128)}, u32[]{:S(2)}) copy-start(s32[16,4]{0,1:T(4,128)} %param.10) | copy-start | bytes 772
  2.9 7.8 %collective-permute-start = (bf16[144,512]{1,0:T(8,128)(2,1)}, bf16[144,512]{1,0:T(8,128)(2,1)S(1)}, u32[]{:S(2)}, u32[]{:S(2)}) collective-permute-start(bf16[144,512]{1,0:T(8,128)(2,1)} %get-tuple-element.27), channel_id=1, source_target_pairs={{0,4},{4,0},{8,12},{12,8},{16,20},{20,16},{24,28},{28,24},{1,5},{5... | collective-permute-start | bytes 442376 | tf_op jit(solution)/shard_map/ppermute | solution.py:20
  4.5 13.1 %collective-permute-start.1 = (bf16[144,1024]{1,0:T(8,128)(2,1)}, bf16[144,1024]{1,0:T(8,128)(2,1)S(1)}, u32[]{:S(2)}, u32[]{:S(2)}) collective-permute-start(bf16[144,1024]{1,0:T(8,128)(2,1)} %get-tuple-element.23.own_ref), channel_id=1, source_target_pairs={{0,8},{4,12},{8,16},{12,20},{16,24},{20,28},{24,0},{28,4},{1,9},{5... | collective-permute-start | bytes 884744 | tf_op jit(solution)/shard_map/ppermute | solution.py:20
  6.1 6.3 %collective-permute-start.2 = (bf16[144,512]{1,0:T(8,128)(2,1)}, bf16[144,512]{1,0:T(8,128)(2,1)S(1)}, u32[]{:S(2)}, u32[]{:S(2)}) collective-permute-start(bf16[144,512]{1,0:T(8,128)(2,1)} %get-tuple-element.31), channel_id=1, source_target_pairs={{0,4},{4,0},{8,12},{12,8},{16,20},{20,16},{24,28},{28,24},{1,5},{5... | collective-permute-start | bytes 442376 | tf_op jit(solution)/shard_map/ppermute | solution.py:20
  10.7 15.4 %copy-start = (bf16[144,1024]{1,0:T(8,128)(2,1)S(1)}, bf16[144,1024]{1,0:T(8,128)(2,1)}, u32[]{:S(2)}) copy-start(bf16[144,1024]{1,0:T(8,128)(2,1)} %get-tuple-element.23.own_ref) | copy-start | bytes 884740
  10.7 15.4 %copy-start.3 = (f32[2048]{0:T(1024)S(1)}, f32[2048]{0:T(1024)}, u32[]{:S(2)}) copy-start(f32[2048]{0:T(1024)} %param.11) | copy-start | bytes 24580
  10.7 6.8 %collective-permute-start.3 = (bf16[144,512]{1,0:T(8,128)(2,1)S(1)}, bf16[144,512]{1,0:T(8,128)(2,1)S(1)}, u32[]{:S(2)}, u32[]{:S(2)}) collective-permute-start(bf16[144,512]{1,0:T(8,128)(2,1)S(1)} %collective-permute-done.pair_a_ref), channel_id=1, source_target_pairs={{0,8},{4,12},{8,16},{12,20},{16,24},{20,28},{24,0},{28,4},{1,9},{5... | collective-permute-start | bytes 442376 | tf_op jit(solution)/shard_map/ppermute | solution.py:20
  12.4 9.4 %collective-permute-start.4 = (bf16[144,512]{1,0:T(8,128)(2,1)S(1)}, bf16[144,512]{1,0:T(8,128)(2,1)S(1)}, u32[]{:S(2)}, u32[]{:S(2)}) collective-permute-start(bf16[144,512]{1,0:T(8,128)(2,1)S(1)} %collective-permute-done.2.pair_b_ref), channel_id=1, source_target_pairs={{0,8},{4,12},{8,16},{12,20},{16,24},{20,28},{24,0},{28,4},{1,9},{5... | collective-permute-start | bytes 442376 | tf_op jit(solution)/shard_map/ppermute | solution.py:20
  13.5 14.2 %collective-permute-start.5 = (bf16[128,1024]{1,0:T(8,128)(2,1)S(1)}, bf16[128,1024]{1,0:T(8,128)(2,1)S(1)}, u32[]{:S(2)}, u32[]{:S(2)}) collective-permute-start(bf16[128,1024]{1,0:T(8,128)(2,1)S(1)} %get-tuple-element.41), channel_id=1, source_target_pairs={{0,4},{4,0},{8,12},{12,8},{16,20},{20,16},{24,28},{28,24},{1,5},{5... | collective-permute-start | bytes 786440 | tf_op jit(solution)/shard_map/ppermute | solution.py:20
  18.5 10.2 %collective-permute-start.6 = (bf16[144,512]{1,0:T(8,128)(2,1)S(1)}, bf16[144,512]{1,0:T(8,128)(2,1)S(1)}, u32[]{:S(2)}, u32[]{:S(2)}) collective-permute-start(bf16[144,512]{1,0:T(8,128)(2,1)S(1)} %shard_map.77), channel_id=1, source_target_pairs={{0,0},{4,4},{8,16},{12,20},{16,24},{20,28},{24,8},{28,12},{1,1},{5... | collective-permute-start | bytes 442376 | tf_op jit(solution)/shard_map/ppermute | solution.py:20
  22.7 7.9 %collective-permute-start.7 = (bf16[144,512]{1,0:T(8,128)(2,1)S(1)}, bf16[144,512]{1,0:T(8,128)(2,1)S(1)}, u32[]{:S(2)}, u32[]{:S(2)}) collective-permute-start(bf16[144,512]{1,0:T(8,128)(2,1)S(1)} %shard_map.78), channel_id=1, source_target_pairs={{0,0},{4,4},{8,16},{12,20},{16,24},{20,28},{24,8},{28,12},{1,1},{5... | collective-permute-start | bytes 442376 | tf_op jit(solution)/shard_map/ppermute | solution.py:20
  30.6 11.0 %copy-start.4 = (f32[2048]{0:T(1024)S(1)}, f32[2048]{0:T(1024)}, u32[]{:S(2)}) copy-start(f32[2048]{0:T(1024)} %param.12) | copy-start | bytes 24580
  31.7 9.8 %collective-permute-start.12 = (bf16[128,1024]{1,0:T(8,128)(2,1)S(1)}, bf16[128,1024]{1,0:T(8,128)(2,1)S(1)}, u32[]{:S(2)}, u32[]{:S(2)}) collective-permute-start(bf16[128,1024]{1,0:T(8,128)(2,1)S(1)} %get-tuple-element.40), channel_id=1, source_target_pairs={{0,4},{4,0},{8,12},{12,8},{16,20},{20,16},{24,28},{28,24},{1,5},{5... | collective-permute-start | bytes 786440 | tf_op jit(solution)/shard_map/ppermute | solution.py:20
  32.8 3.0 %collective-permute-start.10 = (f32[1,256]{1,0:T(1,128)S(1)}, f32[1,256]{1,0:T(1,128)S(1)}, u32[]{:S(2)}, u32[]{:S(2)}) collective-permute-start(f32[1,256]{1,0:T(1,128)S(1)} %get-tuple-element.38), channel_id=1, source_target_pairs={{0,3},{1,2},{2,1},{3,0},{4,7},{5,6},{6,5},{7,4},{8,11},{9,10},{10,... | collective-permute-start | bytes 3080 | tf_op jit(solution)/shard_map/ppermute | solution.py:480
  32.8 3.0 %collective-permute-start.8 = (f32[1,256]{1,0:T(1,128)S(1)}, f32[1,256]{1,0:T(1,128)S(1)}, u32[]{:S(2)}, u32[]{:S(2)}) collective-permute-start(f32[1,256]{1,0:T(1,128)S(1)} %get-tuple-element.38), channel_id=1, source_target_pairs={{0,1},{1,0},{2,3},{3,2},{4,5},{5,4},{6,7},{7,6},{8,9},{9,8},{10,11... | collective-permute-start | bytes 3080 | tf_op jit(solution)/shard_map/ppermute | solution.py:480
  34.4 3.6 %collective-permute-start.9 = (f32[1,256]{1,0:T(1,128)S(1)}, f32[1,256]{1,0:T(1,128)S(1)}, u32[]{:S(2)}, u32[]{:S(2)}) collective-permute-start(f32[1,256]{1,0:T(1,128)S(1)} %get-tuple-element.38), channel_id=1, source_target_pairs={{0,2},{1,3},{2,0},{3,1},{4,6},{5,7},{6,4},{7,5},{8,10},{9,11},{10,... | collective-permute-start | bytes 3080 | tf_op jit(solution)/shard_map/ppermute | solution.py:480
  38.0 3.6 %collective-permute-start.11 = (f32[1,256]{1,0:T(1,128)S(1)}, f32[1,256]{1,0:T(1,128)S(1)}, u32[]{:S(2)}, u32[]{:S(2)}) collective-permute-start(f32[1,256]{1,0:T(1,128)S(1)} %add_add_fusion.power_ref), channel_id=1, source_target_pairs={{0,4},{4,0},{8,12},{12,8},{16,20},{20,16},{24,28},{28,24},{1,5},{5... | collective-permute-start | bytes 3080 | tf_op jit(solution)/shard_map/ppermute | solution.py:20

commit v9 on v8

--- a/solution.py
+++ b/solution.py
@@ -402,6 +402,7 @@
 
     filter_taps, _ = lax.optimization_barrier((filter_taps, kept))
     scaled = (filter_taps * jnp.repeat(tap_blocks.astype(jnp.float32), BLK, axis=1)).astype(jnp.bfloat16)
+    scaled, pair[0] = lax.optimization_barrier((scaled, pair[0]))
     span = taps + 2 * BLK
     table, table_next, w_half = kernel_call(
         tables_kernel,
@@ -415,13 +416,13 @@
         40 * groups * BLK * taps,
         8 * groups * BLK * taps,
     )(seq_lengths, scaled, short_weight)
-    table, table_next, pair[0] = lax.optimization_barrier((table, table_next, pair[0]))
+    table, table_next, pair[1] = lax.optimization_barrier((table, table_next, pair[1]))
     back_pair = [moved(piece, ahead) for piece in pair]
 
     half = lax.axis_index("half")
-    query, pair[0] = lax.optimization_barrier((panels[0], pair[0]))
-    qkept = lax.dynamic_slice_in_dim(query, half * width, width, 1)
-    qsent = lax.dynamic_slice_in_dim(query, (1 - half) * width, width, 1)
+    query, pair[1] = lax.optimization_barrier((panels, pair[1]))
+    qkept = lax.dynamic_slice(query, (0, 0, half * width), (1, rows, width))[0]
+    qsent = lax.dynamic_slice(query, (0, 0, (1 - half) * width), (1, rows, width))[0]
     qgot = moved(qsent, to_pair)
 
     window = pltpu.VMEM((4 * rows, width), jnp.bfloat16)
@@ -429,7 +430,6 @@
     shifted = pltpu.VMEM((2, rows + 8, GROUP), jnp.float32)
     short = whole_tokens // 2 <= 4 * BLK
     if short:
-        onward = [(i, i if i < 2 else i + 2 if i + 2 < 2 * blocks else 2 + i % 2) for i in spots]
         far = []
         for piece in range(2):
             relayed = kernel_call(
@@ -440,7 +440,7 @@
                 2 * rows * BLK * width,
                 4 * rows * width,
             )(seq_lengths, table_next, back_own, back_pair[piece], w_half)
-            far.append(moved(relayed, onward))
+            far.append(moved(relayed, ahead))
     else:
         across = jnp.concatenate([piece[rows:] for piece in sent], 1)
         across = moved(across, [(i, ((i ^ 1) + 6) % (2 * blocks)) for i in spots])

time: 42.7 us -> 43.5 us (1.019)
  the two profiles are of different devices: /device:TPU:8 before, /device:TPU:0 now
where the time goes in v9:
time: 43.5 us; the launch traced here: 43.4 us
  starting transfers between devices  16 us (37%)
  waiting for transfers between devices  14.3 us (33%)
  Pallas kernels  11.7 us (27%)
  local copies, waits for them, and re-layouts  1.26 us (3%)
    ppermute x10, starting transfers between devices, moved(): return lax.ppermute(block, SPOTS, pairs)  14.1 us
    ppermute x10, waiting for transfers between devices, moved(): return lax.ppermute(block, SPOTS, pairs)  12.6 us
    pallas_call x1, Pallas kernels, shards(): kernel_call(products_kernel, (message, small, small), [hbm] * 3, [pltpu.S...  2.88 us
    pallas_call x1, Pallas kernels, shards(): kernel_call(tables_kernel, (shape((groups, 2, BLK, span), jnp.bfloat16),...  2.81 us
    ppermute x3, starting transfers between devices, shards(): lax.ppermute(power, 'mp', [(i, i ^ k) for i in range(peers)])  1.86 us
    ppermute x3, waiting for transfers between devices, shards(): lax.ppermute(power, 'mp', [(i, i ^ k) for i in range(peers)])  1.74 us
    pallas_call x1, Pallas kernels, shards(): kernel_call(near_kernel, (shape((2 * rows, width), jnp.float32), half_wid...  1.55 us
    pallas_call x2, Pallas kernels, shards(): kernel_call(functools.partial(relay_kernel, piece), small, [SMEM] + [VMEM...  1.36 us
  transfers between devices with their start and end apart: 13, of which 7 were waited for; matrix products, arithmetic and copies ran while one was open for 3% of the time, Pallas kernels for 15%

profile of v9, /device:TPU:0, one launch (start us, length us, event | category | flops | bytes accessed | tf_op | source)
XLA Modules:
  0.0 43.4 jit_solution(15693600687796020938)
XLA Ops:
  0.0 0.0 copy-start.2
  0.0 0.0 copy-start.1
  0.0 2.9 %shard_map.73 = (bf16[144,1024]{1,0:T(8,128)(2,1)}, bf16[144,512]{1,0:T(8,128)(2,1)}, bf16[144,512]{1,0:T(8,128)(2,1)}) custom-call(s32[32]{0:T(128)} %seq_ref.9, bf16[3,128,2048]{2,1,0:T(8,128)(2,1)} %bitcast.14, f32[3,3,2048]{2,1,0:T(4,128)} %w_ref.1), custom_call_target="tpu_custom_call" | custom-call | flops 5242880 | bytes 2097152 | tf_op jit(solution)/shard_map/pallas_call | solution.py:381
  2.9 3.0 %collective-permute-start = (bf16[144,512]{1,0:T(8,128)(2,1)}, bf16[144,512]{1,0:T(8,128)(2,1)S(1)}, u32[]{:S(2)}, u32[]{:S(2)}) collective-permute-start(bf16[144,512]{1,0:T(8,128)(2,1)} %get-tuple-element.27), channel_id=1, source_target_pairs={{0,4},{4,0},{8,12},{12,8},{16,20},{20,16},{24,28},{28,24},{1,5},{5... | collective-permute-start | bytes 442376 | tf_op jit(solution)/shard_map/ppermute | solution.py:20
  5.9 0.1 collective-permute-start.1
  6.0 2.0 %collective-permute-start.2 = (bf16[144,1024]{1,0:T(8,128)(2,1)}, bf16[144,1024]{1,0:T(8,128)(2,1)S(1)}, u32[]{:S(2)}, u32[]{:S(2)}) collective-permute-start(bf16[144,1024]{1,0:T(8,128)(2,1)} %get-tuple-element.25.own_ref), channel_id=1, source_target_pairs={{0,8},{4,12},{8,16},{12,20},{16,24},{20,28},{24,0},{28,4},{1,9},{5... | collective-permute-start | bytes 884744 | tf_op jit(solution)/shard_map/ppermute | solution.py:20
  8.0 0.0 copy-done.6
  8.0 0.1 copy.8
  8.1 0.1 broadcast_in_dim.3
  8.2 0.0 copy-done.5
  8.2 2.6 %collective-permute-done.pair_a_ref = bf16[144,512]{1,0:T(8,128)(2,1)S(1)} collective-permute-done((bf16[144,512]{1,0:T(8,128)(2,1)}, bf16[144,512]{1,0:T(8,128)(2,1)S(1)}, u32[]{:S(2)}, u32[]{:S(2)}) %collective-permute-start) | collective-permute-done | bytes 147488 | tf_op jit(solution)/shard_map/ppermute | solution.py:20
  10.8 0.0 copy-done.2
  10.8 0.0 copy-done.1
  10.8 2.8 %shard_map.74 = (bf16[8,2,128,768]{3,2,1,0:T(8,128)(2,1)S(1)}, bf16[8,128,256]{2,1,0:T(8,128)(2,1)S(1)}, f32[3,3,1024]{2,1,0:T(4,128)S(1)}) custom-call(s32[32]{0:T(128)S(1)} %copy-done.2, bf16[16,512]{1,0:T(8,128)(2,1)S(1)} %fusion.taps_ref, f32[3,3,2048]{2,1,0:T(4,128)S(1)} %copy-done.1), custom_call_target="tpu_custom_call" | custom-call | flops 20971520 | bytes 4194304 | tf_op jit(solution)/shard_map/pallas_call | solution.py:407
  13.6 0.0 collective-permute-done.1.pair_b_ref
  13.7 0.0 copy-start
  13.7 0.0 copy-start.3
  13.7 2.2 %collective-permute-start.4 = (bf16[144,512]{1,0:T(8,128)(2,1)S(1)}, bf16[144,512]{1,0:T(8,128)(2,1)S(1)}, u32[]{:S(2)}, u32[]{:S(2)}) collective-permute-start(bf16[144,512]{1,0:T(8,128)(2,1)S(1)} %collective-permute-done.1.pair_b_ref), channel_id=1, source_target_pairs={{0,8},{4,12},{8,16},{12,20},{16,24},{20,28},{24,0},{28,4},{1,9},{5... | collective-permute-start | bytes 442376 | tf_op jit(solution)/shard_map/ppermute | solution.py:20
  15.8 1.6 %collective-permute-start.3 = (bf16[144,512]{1,0:T(8,128)(2,1)S(1)}, bf16[144,512]{1,0:T(8,128)(2,1)S(1)}, u32[]{:S(2)}, u32[]{:S(2)}) collective-permute-start(bf16[144,512]{1,0:T(8,128)(2,1)S(1)} %collective-permute-done.pair_a_ref), channel_id=1, source_target_pairs={{0,8},{4,12},{8,16},{12,20},{16,24},{20,28},{24,0},{28,4},{1,9},{5... | collective-permute-start | bytes 442376 | tf_op jit(solution)/shard_map/ppermute | solution.py:20
  17.4 1.1 %dynamic-slice_bitcast_fusion = (bf16[128,1024]{1,0:T(8,128)(2,1)S(1)}, bf16[128,1024]{1,0:T(8,128)(2,1)S(1)}) fusion(bf16[3,128,2048]{2,1,0:T(8,128)(2,1)} %bitcast.15, s32[]{:T(128)S(6)} %select_n.7, s32[]{:T(128)S(6)} %select_n.6), kind=kLoop, calls=%fused_computation | loop fusion | bytes 1048584 | tf_op jit(solution)/shard_map/squeeze | solution.py:425
  18.5 1.6 %collective-permute-start.5 = (bf16[128,1024]{1,0:T(8,128)(2,1)S(1)}, bf16[128,1024]{1,0:T(8,128)(2,1)S(1)}, u32[]{:S(2)}, u32[]{:S(2)}) collective-permute-start(bf16[128,1024]{1,0:T(8,128)(2,1)S(1)} %get-tuple-element.45), channel_id=1, source_target_pairs={{0,4},{4,0},{8,12},{12,8},{16,20},{20,16},{24,28},{28,24},{1,5},{5... | collective-permute-start | bytes 786440 | tf_op jit(solution)/shard_map/ppermute | solution.py:20
  20.1 0.0 collective-permute-done.2.back_own_ref.refs_0_
  20.1 3.1 %collective-permute-done.3.back_a_ref.back_pair_ref.refs_1_ = bf16[144,512]{1,0:T(8,128)(2,1)S(1)} collective-permute-done((bf16[144,512]{1,0:T(8,128)(2,1)S(1)}, bf16[144,512]{1,0:T(8,128)(2,1)S(1)}, u32[]{:S(2)}, u32[]{:S(2)}) %collective-permute-start.3) | collective-permute-done | bytes 147488 | tf_op jit(solution)/shard_map/ppermute | solution.py:20
  23.2 0.7 %shard_map.77 = bf16[144,512]{1,0:T(8,128)(2,1)S(1)} custom-call(s32[32]{0:T(128)S(1)} %copy-done.2, bf16[8,128,256]{2,1,0:T(8,128)(2,1)S(1)} %get-tuple-element.41.next_ref, bf16[144,1024]{1,0:T(8,128)(2,1)S(1)} %collective-permute-done.2.back_own_ref.refs_0_, bf16[144,512]{1,0:T(8,128)(2,1)S(1)} %collective-permute-done.3.back_a_ref.back_pair_ref.refs_1_, ...), custom_call_target="tpu_custom_call" | custom-call | flops 33554432 | bytes 524288 | tf_op jit(solution)/shard_map/pallas_call | solution.py:435
  23.8 0.1 collective-permute-start.6
  23.9 0.0 collective-permute-done.4.back_b_ref.back_pair_ref.refs_2_
  23.9 0.7 %shard_map.78 = bf16[144,512]{1,0:T(8,128)(2,1)S(1)} custom-call(s32[32]{0:T(128)S(1)} %copy-done.2, bf16[8,128,256]{2,1,0:T(8,128)(2,1)S(1)} %get-tuple-element.41.next_ref, bf16[144,1024]{1,0:T(8,128)(2,1)S(1)} %collective-permute-done.2.back_own_ref.refs_0_, bf16[144,512]{1,0:T(8,128)(2,1)S(1)} %collective-permute-done.4.back_b_ref.back_pair_ref.refs_2_, ...), custom_call_target="tpu_custom_call" | custom-call | flops 33554432 | bytes 524288 | tf_op jit(solution)/shard_map/pallas_call | solution.py:435
  24.6 1.5 %collective-permute-start.7 = (bf16[144,512]{1,0:T(8,128)(2,1)S(1)}, bf16[144,512]{1,0:T(8,128)(2,1)S(1)}, u32[]{:S(2)}, u32[]{:S(2)}) collective-permute-start(bf16[144,512]{1,0:T(8,128)(2,1)S(1)} %shard_map.78), channel_id=1, source_target_pairs={{0,8},{4,12},{8,16},{12,20},{16,24},{20,28},{24,0},{28,4},{1,9},{5... | collective-permute-start | bytes 442376 | tf_op jit(solution)/shard_map/ppermute | solution.py:20
  26.1 0.0 copy-done
  26.1 0.0 copy-done.3
  26.1 1.6 %shard_map.75 = (f32[256,1024]{1,0:T(8,128)S(1)}, f32[128,1024]{1,0:T(8,128)S(1)}, f32[3,8,128]{2,1,0:T(8,128)S(1)}) custom-call(s32[32]{0:T(128)S(1)} %copy-done.2, bf16[8,2,128,768]{3,2,1,0:T(8,128)(2,1)S(1)} %get-tuple-element.32.table_ref, bf16[144,1024]{1,0:T(8,128)(2,1)S(1)} %copy-done, ...), custom_call_target="tpu_custom_call" | custom-call | flops 167772160 | bytes 2097152 | tf_op jit(solution)/shard_map/pallas_call | solution.py:451
  27.7 0.0 collective-permute-done.5.raw_ref
  27.7 0.9 %shard_map.76.qpair_ref = f32[128,1024]{1,0:T(8,128)S(1)} custom-call(s32[32]{0:T(128)S(1)} %copy-done.2, bf16[128,1024]{1,0:T(8,128)(2,1)S(1)} %collective-permute-done.5.raw_ref, bf16[144,1024]{1,0:T(8,128)(2,1)S(1)} %copy-done, bf16[144,1024]{1,0:T(8,128)(2,1)S(1)} %collective-permute-done.2.back_own_ref.refs_0_, f32[3,3,1024]{2,1,0:T(4,128)S(1)} %get-tuple-element.37.w_ref), custom_call_target="tpu_custom_call" | custom-call | flops 1310720 | bytes 1048576 | tf_op jit(solution)/shard_map/pallas_call | solution.py:460
  28.5 2.3 %collective-permute-done.6.refs_3_ = bf16[144,512]{1,0:T(8,128)(2,1)S(1)} collective-permute-done((bf16[144,512]{1,0:T(8,128)(2,1)S(1)}, bf16[144,512]{1,0:T(8,128)(2,1)S(1)}, u32[]{:S(2)}, u32[]{:S(2)}) %collective-permute-start.6) | collective-permute-done | bytes 147488 | tf_op jit(solution)/shard_map/ppermute | solution.py:20
  30.8 1.6 %collective-permute-done.7.refs_4_ = bf16[144,512]{1,0:T(8,128)(2,1)S(1)} collective-permute-done((bf16[144,512]{1,0:T(8,128)(2,1)S(1)}, bf16[144,512]{1,0:T(8,128)(2,1)S(1)}, u32[]{:S(2)}, u32[]{:S(2)}) %collective-permute-start.7) | collective-permute-done | bytes 147488 | tf_op jit(solution)/shard_map/ppermute | solution.py:20
  32.4 1.1 %shard_map.79 = (f32[128,1024]{1,0:T(8,128)S(1)}, bf16[128,1024]{1,0:T(8,128)(2,1)S(1)}, f32[1,256]{1,0:T(1,128)S(1)}) custom-call(bf16[8,2,128,768]{3,2,1,0:T(8,128)(2,1)S(1)} %get-tuple-element.32.table_ref, f32[256,1024]{1,0:T(8,128)S(1)} %get-tuple-element.38.acc_ref, f32[128,1024]{1,0:T(8,128)S(1)} %get-tuple-element.39.qown_ref, ...), custom_call_target="tpu_custom_call" | custom-call | flops 167772160 | bytes 3145728 | tf_op jit(solution)/shard_map/pallas_call | solution.py:469
  33.5 1.5 %collective-permute-start.12 = (bf16[128,1024]{1,0:T(8,128)(2,1)S(1)}, bf16[128,1024]{1,0:T(8,128)(2,1)S(1)}, u32[]{:S(2)}, u32[]{:S(2)}) collective-permute-start(bf16[128,1024]{1,0:T(8,128)(2,1)S(1)} %get-tuple-element.44), channel_id=1, source_target_pairs={{0,4},{4,0},{8,12},{12,8},{16,20},{20,16},{24,28},{28,24},{1,5},{5... | collective-permute-start | bytes 786440 | tf_op jit(solution)/shard_map/ppermute | solution.py:20
  35.1 0.0 collective-permute-start.10
  35.1 1.5 %collective-permute-start.9 = (f32[1,256]{1,0:T(1,128)S(1)}, f32[1,256]{1,0:T(1,128)S(1)}, u32[]{:S(2)}, u32[]{:S(2)}) collective-permute-start(f32[1,256]{1,0:T(1,128)S(1)} %get-tuple-element.42), channel_id=1, source_target_pairs={{0,2},{1,3},{2,0},{3,1},{4,6},{5,7},{6,4},{7,5},{8,10},{9,11},{10,... | collective-permute-start | bytes 3080 | tf_op jit(solution)/shard_map/ppermute | solution.py:480
  36.6 0.3 collective-permute-start.8
  36.9 1.1 %collective-permute-done.10 = f32[1,256]{1,0:T(1,128)S(1)} collective-permute-done((f32[1,256]{1,0:T(1,128)S(1)}, f32[1,256]{1,0:T(1,128)S(1)}, u32[]{:S(2)}, u32[]{:S(2)}) %collective-permute-start.10) | collective-permute-done | bytes 1056 | tf_op jit(solution)/shard_map/ppermute | solution.py:480
  38.1 0.6 %collective-permute-done.9 = f32[1,256]{1,0:T(1,128)S(1)} collective-permute-done((f32[1,256]{1,0:T(1,128)S(1)}, f32[1,256]{1,0:T(1,128)S(1)}, u32[]{:S(2)}, u32[]{:S(2)}) %collective-permute-start.9) | collective-permute-done | bytes 1056 | tf_op jit(solution)/shard_map/ppermute | solution.py:480
  38.7 0.0 collective-permute-done.8
  38.7 0.6 %collective-permute-start.11 = (f32[1,256]{1,0:T(1,128)S(1)}, f32[1,256]{1,0:T(1,128)S(1)}, u32[]{:S(2)}, u32[]{:S(2)}) collective-permute-start(f32[1,256]{1,0:T(1,128)S(1)} %add_add_fusion.power_ref), channel_id=1, source_target_pairs={{0,4},{4,0},{8,12},{12,8},{16,20},{20,16},{24,28},{28,24},{1,5},{5... | collective-permute-start | bytes 3080 | tf_op jit(solution)/shard_map/ppermute | solution.py:20
  39.3 3.0 %collective-permute-done.11.power_got_ref = f32[1,256]{1,0:T(1,128)S(1)} collective-permute-done((f32[1,256]{1,0:T(1,128)S(1)}, f32[1,256]{1,0:T(1,128)S(1)}, u32[]{:S(2)}, u32[]{:S(2)}) %collective-permute-start.11) | collective-permute-done | bytes 1056 | tf_op jit(solution)/shard_map/ppermute | solution.py:20
  42.3 0.0 collective-permute-done.12.got_ref
  42.3 0.0 copy-done.4
  42.3 1.0 %shard_map.80 = bf16[128,2048]{1,0:T(8,128)(2,1)} custom-call(f32[1,256]{1,0:T(1,128)S(1)} %add_add_fusion.power_ref, f32[1,256]{1,0:T(1,128)S(1)} %collective-permute-done.11.power_got_ref, f32[128,1024]{1,0:T(8,128)S(1)} %get-tuple-element.43.kept_ref, bf16[128,1024]{1,0:T(8,128)(2,1)S(1)} %collective-permute-done.12.got_ref, f32[1,2048]{1,0:T(1,128)S(1)} %bitcast.13), custom_call_target="tpu_custom_call" | custom-call | flops 1048576 | bytes 1310720 | tf_op jit(solution)/shard_map/pallas_call | solution.py:482
  (6 shorter events, 0.0 us)
Async XLA Ops:
  0.0 10.8 %copy-start.2 = (s32[32]{0:T(128)S(1)}, s32[32]{0:T(128)}, u32[]{:S(2)}) copy-start(s32[32]{0:T(128)} %seq_ref.9) | copy-start | bytes 388
  0.0 10.8 %copy-start.1 = (f32[3,3,2048]{2,1,0:T(4,128)S(1)}, f32[3,3,2048]{2,1,0:T(4,128)}, u32[]{:S(2)}) copy-start(f32[3,3,2048]{2,1,0:T(4,128)} %w_ref.1) | copy-start | bytes 221188
  0.0 8.2 %copy-start.5 = (f32[16,512]{1,0:T(8,128)S(1)}, f32[16,512]{1,0:T(8,128)}, u32[]{:S(2)}) copy-start(f32[16,512]{1,0:T(8,128)} %param.9) | copy-start | bytes 98308
  0.0 8.0 %copy-start.6 = (s32[16,4]{0,1:T(4,128)S(1)}, s32[16,4]{0,1:T(4,128)}, u32[]{:S(2)}) copy-start(s32[16,4]{0,1:T(4,128)} %param.10) | copy-start | bytes 772
  2.9 7.9 %collective-permute-start = (bf16[144,512]{1,0:T(8,128)(2,1)}, bf16[144,512]{1,0:T(8,128)(2,1)S(1)}, u32[]{:S(2)}, u32[]{:S(2)}) collective-permute-start(bf16[144,512]{1,0:T(8,128)(2,1)} %get-tuple-element.27), channel_id=1, source_target_pairs={{0,4},{4,0},{8,12},{12,8},{16,20},{20,16},{24,28},{28,24},{1,5},{5... | collective-permute-start | bytes 442376 | tf_op jit(solution)/shard_map/ppermute | solution.py:20
  5.9 7.7 %collective-permute-start.1 = (bf16[144,512]{1,0:T(8,128)(2,1)}, bf16[144,512]{1,0:T(8,128)(2,1)S(1)}, u32[]{:S(2)}, u32[]{:S(2)}) collective-permute-start(bf16[144,512]{1,0:T(8,128)(2,1)} %get-tuple-element.31), channel_id=1, source_target_pairs={{0,4},{4,0},{8,12},{12,8},{16,20},{20,16},{24,28},{28,24},{1,5},{5... | collective-permute-start | bytes 442376 | tf_op jit(solution)/shard_map/ppermute | solution.py:20
  6.0 14.1 %collective-permute-start.2 = (bf16[144,1024]{1,0:T(8,128)(2,1)}, bf16[144,1024]{1,0:T(8,128)(2,1)S(1)}, u32[]{:S(2)}, u32[]{:S(2)}) collective-permute-start(bf16[144,1024]{1,0:T(8,128)(2,1)} %get-tuple-element.25.own_ref), channel_id=1, source_target_pairs={{0,8},{4,12},{8,16},{12,20},{16,24},{20,28},{24,0},{28,4},{1,9},{5... | collective-permute-start | bytes 884744 | tf_op jit(solution)/shard_map/ppermute | solution.py:20
  13.7 12.4 %copy-start = (bf16[144,1024]{1,0:T(8,128)(2,1)S(1)}, bf16[144,1024]{1,0:T(8,128)(2,1)}, u32[]{:S(2)}) copy-start(bf16[144,1024]{1,0:T(8,128)(2,1)} %get-tuple-element.25.own_ref) | copy-start | bytes 884740
  13.7 12.4 %copy-start.3 = (f32[2048]{0:T(1024)S(1)}, f32[2048]{0:T(1024)}, u32[]{:S(2)}) copy-start(f32[2048]{0:T(1024)} %param.11) | copy-start | bytes 24580
  13.7 10.2 %collective-permute-start.4 = (bf16[144,512]{1,0:T(8,128)(2,1)S(1)}, bf16[144,512]{1,0:T(8,128)(2,1)S(1)}, u32[]{:S(2)}, u32[]{:S(2)}) collective-permute-start(bf16[144,512]{1,0:T(8,128)(2,1)S(1)} %collective-permute-done.1.pair_b_ref), channel_id=1, source_target_pairs={{0,8},{4,12},{8,16},{12,20},{16,24},{20,28},{24,0},{28,4},{1,9},{5... | collective-permute-start | bytes 442376 | tf_op jit(solution)/shard_map/ppermute | solution.py:20
  15.8 7.3 %collective-permute-start.3 = (bf16[144,512]{1,0:T(8,128)(2,1)S(1)}, bf16[144,512]{1,0:T(8,128)(2,1)S(1)}, u32[]{:S(2)}, u32[]{:S(2)}) collective-permute-start(bf16[144,512]{1,0:T(8,128)(2,1)S(1)} %collective-permute-done.pair_a_ref), channel_id=1, source_target_pairs={{0,8},{4,12},{8,16},{12,20},{16,24},{20,28},{24,0},{28,4},{1,9},{5... | collective-permute-start | bytes 442376 | tf_op jit(solution)/shard_map/ppermute | solution.py:20
  18.5 9.2 %collective-permute-start.5 = (bf16[128,1024]{1,0:T(8,128)(2,1)S(1)}, bf16[128,1024]{1,0:T(8,128)(2,1)S(1)}, u32[]{:S(2)}, u32[]{:S(2)}) collective-permute-start(bf16[128,1024]{1,0:T(8,128)(2,1)S(1)} %get-tuple-element.45), channel_id=1, source_target_pairs={{0,4},{4,0},{8,12},{12,8},{16,20},{20,16},{24,28},{28,24},{1,5},{5... | collective-permute-start | bytes 786440 | tf_op jit(solution)/shard_map/ppermute | solution.py:20
  23.8 7.0 %collective-permute-start.6 = (bf16[144,512]{1,0:T(8,128)(2,1)S(1)}, bf16[144,512]{1,0:T(8,128)(2,1)S(1)}, u32[]{:S(2)}, u32[]{:S(2)}) collective-permute-start(bf16[144,512]{1,0:T(8,128)(2,1)S(1)} %shard_map.77), channel_id=1, source_target_pairs={{0,8},{4,12},{8,16},{12,20},{16,24},{20,28},{24,0},{28,4},{1,9},{5... | collective-permute-start | bytes 442376 | tf_op jit(solution)/shard_map/ppermute | solution.py:20
  24.6 7.8 %collective-permute-start.7 = (bf16[144,512]{1,0:T(8,128)(2,1)S(1)}, bf16[144,512]{1,0:T(8,128)(2,1)S(1)}, u32[]{:S(2)}, u32[]{:S(2)}) collective-permute-start(bf16[144,512]{1,0:T(8,128)(2,1)S(1)} %shard_map.78), channel_id=1, source_target_pairs={{0,8},{4,12},{8,16},{12,20},{16,24},{20,28},{24,0},{28,4},{1,9},{5... | collective-permute-start | bytes 442376 | tf_op jit(solution)/shard_map/ppermute | solution.py:20
  32.4 9.9 %copy-start.4 = (f32[2048]{0:T(1024)S(1)}, f32[2048]{0:T(1024)}, u32[]{:S(2)}) copy-start(f32[2048]{0:T(1024)} %param.12) | copy-start | bytes 24580
  33.5 8.8 %collective-permute-start.12 = (bf16[128,1024]{1,0:T(8,128)(2,1)S(1)}, bf16[128,1024]{1,0:T(8,128)(2,1)S(1)}, u32[]{:S(2)}, u32[]{:S(2)}) collective-permute-start(bf16[128,1024]{1,0:T(8,128)(2,1)S(1)} %get-tuple-element.44), channel_id=1, source_target_pairs={{0,4},{4,0},{8,12},{12,8},{16,20},{20,16},{24,28},{28,24},{1,5},{5... | collective-permute-start | bytes 786440 | tf_op jit(solution)/shard_map/ppermute | solution.py:20
  35.1 3.0 %collective-permute-start.10 = (f32[1,256]{1,0:T(1,128)S(1)}, f32[1,256]{1,0:T(1,128)S(1)}, u32[]{:S(2)}, u32[]{:S(2)}) collective-permute-start(f32[1,256]{1,0:T(1,128)S(1)} %get-tuple-element.42), channel_id=1, source_target_pairs={{0,3},{1,2},{2,1},{3,0},{4,7},{5,6},{6,5},{7,4},{8,11},{9,10},{10,... | collective-permute-start | bytes 3080 | tf_op jit(solution)/shard_map/ppermute | solution.py:480
  35.1 3.6 %collective-permute-start.9 = (f32[1,256]{1,0:T(1,128)S(1)}, f32[1,256]{1,0:T(1,128)S(1)}, u32[]{:S(2)}, u32[]{:S(2)}) collective-permute-start(f32[1,256]{1,0:T(1,128)S(1)} %get-tuple-element.42), channel_id=1, source_target_pairs={{0,2},{1,3},{2,0},{3,1},{4,6},{5,7},{6,4},{7,5},{8,10},{9,11},{10,... | collective-permute-start | bytes 3080 | tf_op jit(solution)/shard_map/ppermute | solution.py:480
  36.6 2.1 %collective-permute-start.8 = (f32[1,256]{1,0:T(1,128)S(1)}, f32[1,256]{1,0:T(1,128)S(1)}, u32[]{:S(2)}, u32[]{:S(2)}) collective-permute-start(f32[1,256]{1,0:T(1,128)S(1)} %get-tuple-element.42), channel_id=1, source_target_pairs={{0,1},{1,0},{2,3},{3,2},{4,5},{5,4},{6,7},{7,6},{8,9},{9,8},{10,11... | collective-permute-start | bytes 3080 | tf_op jit(solution)/shard_map/ppermute | solution.py:480
  38.7 3.6 %collective-permute-start.11 = (f32[1,256]{1,0:T(1,128)S(1)}, f32[1,256]{1,0:T(1,128)S(1)}, u32[]{:S(2)}, u32[]{:S(2)}) collective-permute-start(f32[1,256]{1,0:T(1,128)S(1)} %add_add_fusion.power_ref), channel_id=1, source_target_pairs={{0,4},{4,0},{8,12},{12,8},{16,20},{20,16},{24,28},{28,24},{1,5},{5... | collective-permute-start | bytes 3080 | tf_op jit(solution)/shard_map/ppermute | solution.py:20

commit v10 on v9

--- a/solution.py
+++ b/solution.py
@@ -402,7 +402,6 @@
 
     filter_taps, _ = lax.optimization_barrier((filter_taps, kept))
     scaled = (filter_taps * jnp.repeat(tap_blocks.astype(jnp.float32), BLK, axis=1)).astype(jnp.bfloat16)
-    scaled, pair[0] = lax.optimization_barrier((scaled, pair[0]))
     span = taps + 2 * BLK
     table, table_next, w_half = kernel_call(
         tables_kernel,
@@ -416,20 +415,22 @@
         40 * groups * BLK * taps,
         8 * groups * BLK * taps,
     )(seq_lengths, scaled, short_weight)
-    table, table_next, pair[1] = lax.optimization_barrier((table, table_next, pair[1]))
-    back_pair = [moved(piece, ahead) for piece in pair]
-
-    half = lax.axis_index("half")
-    query, pair[1] = lax.optimization_barrier((panels, pair[1]))
+    table, table_next, pair[0] = lax.optimization_barrier((table, table_next, pair[0]))
+
+    half = lax.axis_index("half")
+    query, _ = lax.optimization_barrier((panels, pair[0]))
     qkept = lax.dynamic_slice(query, (0, 0, half * width), (1, rows, width))[0]
     qsent = lax.dynamic_slice(query, (0, 0, (1 - half) * width), (1, rows, width))[0]
+    qkept, qsent, pair[1] = lax.optimization_barrier((qkept, qsent, pair[1]))
     qgot = moved(qsent, to_pair)
+    back_pair = [moved(piece, ahead) for piece in pair]
 
     window = pltpu.VMEM((4 * rows, width), jnp.bfloat16)
     extras = pltpu.VMEM((4, 16, width), jnp.float32)
     shifted = pltpu.VMEM((2, rows + 8, GROUP), jnp.float32)
     short = whole_tokens // 2 <= 4 * BLK
     if short:
+        onward = [(i, i ^ 1 if i < 2 else i + 2 if i + 2 < 2 * blocks else 2 + i % 2) for i in spots]
         far = []
         for piece in range(2):
             relayed = kernel_call(
@@ -440,7 +441,7 @@
                 2 * rows * BLK * width,
                 4 * rows * width,
             )(seq_lengths, table_next, back_own, back_pair[piece], w_half)
-            far.append(moved(relayed, ahead))
+            far.append(moved(relayed, onward))
     else:
         across = jnp.concatenate([piece[rows:] for piece in sent], 1)
         across = moved(across, [(i, ((i ^ 1) + 6) % (2 * blocks)) for i in spots])

time: 43.5 us -> 39.8 us (0.915)
  waiting for transfers between devices: 14.3 us -> 11.5 us
  starting transfers between devices: 16 us -> 15.1 us
    ppermute x10, waiting for transfers between devices: 12.6 us -> 9.77 us  [moved(): return lax.ppermute(block, SPOTS, pairs)]
    ppermute x10, starting transfers between devices: 14.1 us -> 13.2 us  [moved(): return lax.ppermute(block, SPOTS, pairs)]
  transfers between devices with their start and end apart: 13 -> 13, of which waited for: 7 -> 8; matrix products, arithmetic and copies ran while one was open for 3% -> 3% of each run, Pallas kernels for 15% -> 17%
where the time goes in v10:
time: 39.8 us; the launch traced here: 39.6 us
  starting transfers between devices  15.1 us (38%)
  Pallas kernels  11.6 us (29%)
  waiting for transfers between devices  11.5 us (29%)
  local copies, waits for them, and re-layouts  1.26 us (3%)
    ppermute x10, starting transfers between devices, moved(): return lax.ppermute(block, SPOTS, pairs)  13.2 us
    ppermute x10, waiting for transfers between devices, moved(): return lax.ppermute(block, SPOTS, pairs)  9.77 us
    pallas_call x1, Pallas kernels, shards(): kernel_call(products_kernel, (message, small, small), [hbm] * 3, [pltpu.S...  2.88 us
    pallas_call x1, Pallas kernels, shards(): kernel_call(tables_kernel, (shape((groups, 2, BLK, span), jnp.bfloat16),...  2.8 us
    ppermute x3, starting transfers between devices, shards(): lax.ppermute(power, 'mp', [(i, i ^ k) for i in range(peers)])  1.86 us
    ppermute x3, waiting for transfers between devices, shards(): lax.ppermute(power, 'mp', [(i, i ^ k) for i in range(peers)])  1.74 us
    pallas_call x1, Pallas kernels, shards(): kernel_call(near_kernel, (shape((2 * rows, width), jnp.float32), half_wid...  1.55 us
    pallas_call x2, Pallas kernels, shards(): kernel_call(functools.partial(relay_kernel, piece), small, [SMEM] + [VMEM...  1.36 us
  transfers between devices with their start and end apart: 13, of which 8 were waited for; matrix products, arithmetic and copies ran while one was open for 3% of the time, Pallas kernels for 17%

profile of v10, /device:TPU:0, one launch (start us, length us, event | category | flops | bytes accessed | tf_op | source)
XLA Modules:
  0.0 39.6 jit_solution(17450315444520668463)
XLA Ops:
  0.0 0.0 copy-start.2
  0.0 0.0 copy-start.1
  0.0 2.9 %shard_map.73 = (bf16[144,1024]{1,0:T(8,128)(2,1)}, bf16[144,512]{1,0:T(8,128)(2,1)}, bf16[144,512]{1,0:T(8,128)(2,1)}) custom-call(s32[32]{0:T(128)} %seq_ref.9, bf16[3,128,2048]{2,1,0:T(8,128)(2,1)} %bitcast.14, f32[3,3,2048]{2,1,0:T(4,128)} %w_ref.1), custom_call_target="tpu_custom_call" | custom-call | flops 5242880 | bytes 2097152 | tf_op jit(solution)/shard_map/pallas_call | solution.py:381
  2.9 3.0 %collective-permute-start = (bf16[144,512]{1,0:T(8,128)(2,1)}, bf16[144,512]{1,0:T(8,128)(2,1)S(1)}, u32[]{:S(2)}, u32[]{:S(2)}) collective-permute-start(bf16[144,512]{1,0:T(8,128)(2,1)} %get-tuple-element.29), channel_id=1, source_target_pairs={{0,4},{4,0},{8,12},{12,8},{16,20},{20,16},{24,28},{28,24},{1,5},{5... | collective-permute-start | bytes 442376 | tf_op jit(solution)/shard_map/ppermute | solution.py:20
  5.9 1.6 %collective-permute-start.1 = (bf16[144,1024]{1,0:T(8,128)(2,1)}, bf16[144,1024]{1,0:T(8,128)(2,1)S(1)}, u32[]{:S(2)}, u32[]{:S(2)}) collective-permute-start(bf16[144,1024]{1,0:T(8,128)(2,1)} %get-tuple-element.25.own_ref), channel_id=1, source_target_pairs={{0,8},{4,12},{8,16},{12,20},{16,24},{20,28},{24,0},{28,4},{1,9},{5... | collective-permute-start | bytes 884744 | tf_op jit(solution)/shard_map/ppermute | solution.py:20
  7.5 0.5 %collective-permute-start.2 = (bf16[144,512]{1,0:T(8,128)(2,1)}, bf16[144,512]{1,0:T(8,128)(2,1)S(1)}, u32[]{:S(2)}, u32[]{:S(2)}) collective-permute-start(bf16[144,512]{1,0:T(8,128)(2,1)} %get-tuple-element.33), channel_id=1, source_target_pairs={{0,4},{4,0},{8,12},{12,8},{16,20},{20,16},{24,28},{28,24},{1,5},{5... | collective-permute-start | bytes 442376 | tf_op jit(solution)/shard_map/ppermute | solution.py:20
  8.0 0.0 copy-done.6
  8.0 0.1 copy.8
  8.1 0.1 broadcast_in_dim.3
  8.2 0.0 copy-done.5
  8.2 0.0 copy-done.2
  8.2 0.0 copy-done.1
  8.2 2.8 %shard_map.74 = (bf16[8,2,128,768]{3,2,1,0:T(8,128)(2,1)S(1)}, bf16[8,128,256]{2,1,0:T(8,128)(2,1)S(1)}, f32[3,3,1024]{2,1,0:T(4,128)S(1)}) custom-call(s32[32]{0:T(128)S(1)} %copy-done.2, bf16[16,512]{1,0:T(8,128)(2,1)S(1)} %fusion.taps_ref, f32[3,3,2048]{2,1,0:T(4,128)S(1)} %copy-done.1), custom_call_target="tpu_custom_call" | custom-call | flops 20971520 | bytes 4194304 | tf_op jit(solution)/shard_map/pallas_call | solution.py:406
  11.1 0.0 collective-permute-done.pair_a_ref
  11.1 0.0 copy-start
  11.1 0.0 copy-start.3
  11.1 1.6 %collective-permute-start.3 = (bf16[144,512]{1,0:T(8,128)(2,1)S(1)}, bf16[144,512]{1,0:T(8,128)(2,1)S(1)}, u32[]{:S(2)}, u32[]{:S(2)}) collective-permute-start(bf16[144,512]{1,0:T(8,128)(2,1)S(1)} %collective-permute-done.pair_a_ref), channel_id=1, source_target_pairs={{0,8},{4,12},{8,16},{12,20},{16,24},{20,28},{24,0},{28,4},{1,9},{5... | collective-permute-start | bytes 442376 | tf_op jit(solution)/shard_map/ppermute | solution.py:20
  12.7 1.1 %dynamic-slice_bitcast_fusion = (bf16[128,1024]{1,0:T(8,128)(2,1)S(1)}, bf16[128,1024]{1,0:T(8,128)(2,1)S(1)}) fusion(bf16[3,128,2048]{2,1,0:T(8,128)(2,1)} %bitcast.15, s32[]{:T(128)S(6)} %select_n.7, s32[]{:T(128)S(6)} %select_n.6), kind=kLoop, calls=%fused_computation | loop fusion | bytes 1048584 | tf_op jit(solution)/shard_map/squeeze | solution.py:423
  13.8 0.0 collective-permute-done.2.pair_b_ref
  13.8 1.6 %collective-permute-start.4 = (bf16[144,512]{1,0:T(8,128)(2,1)S(1)}, bf16[144,512]{1,0:T(8,128)(2,1)S(1)}, u32[]{:S(2)}, u32[]{:S(2)}) collective-permute-start(bf16[144,512]{1,0:T(8,128)(2,1)S(1)} %collective-permute-done.2.pair_b_ref), channel_id=1, source_target_pairs={{0,8},{4,12},{8,16},{12,20},{16,24},{20,28},{24,0},{28,4},{1,9},{5... | collective-permute-start | bytes 442376 | tf_op jit(solution)/shard_map/ppermute | solution.py:20
  15.4 1.7 %collective-permute-start.5 = (bf16[128,1024]{1,0:T(8,128)(2,1)S(1)}, bf16[128,1024]{1,0:T(8,128)(2,1)S(1)}, u32[]{:S(2)}, u32[]{:S(2)}) collective-permute-start(bf16[128,1024]{1,0:T(8,128)(2,1)S(1)} %get-tuple-element.39), channel_id=1, source_target_pairs={{0,4},{4,0},{8,12},{12,8},{16,20},{20,16},{24,28},{28,24},{1,5},{5... | collective-permute-start | bytes 786440 | tf_op jit(solution)/shard_map/ppermute | solution.py:20
  17.2 0.7 %collective-permute-done.1.back_own_ref.refs_0_ = bf16[144,1024]{1,0:T(8,128)(2,1)S(1)} collective-permute-done((bf16[144,1024]{1,0:T(8,128)(2,1)}, bf16[144,1024]{1,0:T(8,128)(2,1)S(1)}, u32[]{:S(2)}, u32[]{:S(2)}) %collective-permute-start.1) | collective-permute-done | bytes 294944 | tf_op jit(solution)/shard_map/ppermute | solution.py:20
  17.9 3.2 %collective-permute-done.3.back_a_ref.back_pair_ref.refs_1_ = bf16[144,512]{1,0:T(8,128)(2,1)S(1)} collective-permute-done((bf16[144,512]{1,0:T(8,128)(2,1)S(1)}, bf16[144,512]{1,0:T(8,128)(2,1)S(1)}, u32[]{:S(2)}, u32[]{:S(2)}) %collective-permute-start.3) | collective-permute-done | bytes 147488 | tf_op jit(solution)/shard_map/ppermute | solution.py:20
  21.0 0.7 %shard_map.77 = bf16[144,512]{1,0:T(8,128)(2,1)S(1)} custom-call(s32[32]{0:T(128)S(1)} %copy-done.2, bf16[8,128,256]{2,1,0:T(8,128)(2,1)S(1)} %get-tuple-element.41.next_ref, bf16[144,1024]{1,0:T(8,128)(2,1)S(1)} %collective-permute-done.1.back_own_ref.refs_0_, bf16[144,512]{1,0:T(8,128)(2,1)S(1)} %collective-permute-done.3.back_a_ref.back_pair_ref.refs_1_, ...), custom_call_target="tpu_custom_call" | custom-call | flops 33554432 | bytes 524288 | tf_op jit(solution)/shard_map/pallas_call | solution.py:436
  21.7 0.5 %collective-permute-start.6 = (bf16[144,512]{1,0:T(8,128)(2,1)S(1)}, bf16[144,512]{1,0:T(8,128)(2,1)S(1)}, u32[]{:S(2)}, u32[]{:S(2)}) collective-permute-start(bf16[144,512]{1,0:T(8,128)(2,1)S(1)} %shard_map.77), channel_id=1, source_target_pairs={{0,4},{4,0},{8,16},{12,20},{16,24},{20,28},{24,8},{28,12},{1,5},{5... | collective-permute-start | bytes 442376 | tf_op jit(solution)/shard_map/ppermute | solution.py:20
  22.2 1.7 %collective-permute-done.4.back_b_ref.back_pair_ref.refs_2_ = bf16[144,512]{1,0:T(8,128)(2,1)S(1)} collective-permute-done((bf16[144,512]{1,0:T(8,128)(2,1)S(1)}, bf16[144,512]{1,0:T(8,128)(2,1)S(1)}, u32[]{:S(2)}, u32[]{:S(2)}) %collective-permute-start.4) | collective-permute-done | bytes 147488 | tf_op jit(solution)/shard_map/ppermute | solution.py:20
  23.9 0.7 %shard_map.78 = bf16[144,512]{1,0:T(8,128)(2,1)S(1)} custom-call(s32[32]{0:T(128)S(1)} %copy-done.2, bf16[8,128,256]{2,1,0:T(8,128)(2,1)S(1)} %get-tuple-element.41.next_ref, bf16[144,1024]{1,0:T(8,128)(2,1)S(1)} %collective-permute-done.1.back_own_ref.refs_0_, bf16[144,512]{1,0:T(8,128)(2,1)S(1)} %collective-permute-done.4.back_b_ref.back_pair_ref.refs_2_, ...), custom_call_target="tpu_custom_call" | custom-call | flops 33554432 | bytes 524288 | tf_op jit(solution)/shard_map/pallas_call | solution.py:436
  24.5 0.5 %collective-permute-start.7 = (bf16[144,512]{1,0:T(8,128)(2,1)S(1)}, bf16[144,512]{1,0:T(8,128)(2,1)S(1)}, u32[]{:S(2)}, u32[]{:S(2)}) collective-permute-start(bf16[144,512]{1,0:T(8,128)(2,1)S(1)} %shard_map.78), channel_id=1, source_target_pairs={{0,4},{4,0},{8,16},{12,20},{16,24},{20,28},{24,8},{28,12},{1,5},{5... | collective-permute-start | bytes 442376 | tf_op jit(solution)/shard_map/ppermute | solution.py:20
  25.0 0.0 copy-done
  25.0 0.0 copy-done.3
  25.0 1.5 %shard_map.75 = (f32[256,1024]{1,0:T(8,128)S(1)}, f32[128,1024]{1,0:T(8,128)S(1)}, f32[3,8,128]{2,1,0:T(8,128)S(1)}) custom-call(s32[32]{0:T(128)S(1)} %copy-done.2, bf16[8,2,128,768]{3,2,1,0:T(8,128)(2,1)S(1)} %get-tuple-element.30.table_ref, bf16[144,1024]{1,0:T(8,128)(2,1)S(1)} %copy-done, ...), custom_call_target="tpu_custom_call" | custom-call | flops 167772160 | bytes 2097152 | tf_op jit(solution)/shard_map/pallas_call | solution.py:452
  26.6 0.0 collective-permute-done.5.raw_ref
  26.6 0.9 %shard_map.76.qpair_ref = f32[128,1024]{1,0:T(8,128)S(1)} custom-call(s32[32]{0:T(128)S(1)} %copy-done.2, bf16[128,1024]{1,0:T(8,128)(2,1)S(1)} %collective-permute-done.5.raw_ref, bf16[144,1024]{1,0:T(8,128)(2,1)S(1)} %copy-done, bf16[144,1024]{1,0:T(8,128)(2,1)S(1)} %collective-permute-done.1.back_own_ref.refs_0_, f32[3,3,1024]{2,1,0:T(4,128)S(1)} %get-tuple-element.36.w_ref), custom_call_target="tpu_custom_call" | custom-call | flops 1310720 | bytes 1048576 | tf_op jit(solution)/shard_map/pallas_call | solution.py:461
  27.5 0.5 %collective-permute-done.6.refs_3_ = bf16[144,512]{1,0:T(8,128)(2,1)S(1)} collective-permute-done((bf16[144,512]{1,0:T(8,128)(2,1)S(1)}, bf16[144,512]{1,0:T(8,128)(2,1)S(1)}, u32[]{:S(2)}, u32[]{:S(2)}) %collective-permute-start.6) | collective-permute-done | bytes 147488 | tf_op jit(solution)/shard_map/ppermute | solution.py:20
  28.0 1.7 %collective-permute-done.7.refs_4_ = bf16[144,512]{1,0:T(8,128)(2,1)S(1)} collective-permute-done((bf16[144,512]{1,0:T(8,128)(2,1)S(1)}, bf16[144,512]{1,0:T(8,128)(2,1)S(1)}, u32[]{:S(2)}, u32[]{:S(2)}) %collective-permute-start.7) | collective-permute-done | bytes 147488 | tf_op jit(solution)/shard_map/ppermute | solution.py:20
  29.7 1.1 %shard_map.79 = (f32[128,1024]{1,0:T(8,128)S(1)}, bf16[128,1024]{1,0:T(8,128)(2,1)S(1)}, f32[1,256]{1,0:T(1,128)S(1)}) custom-call(bf16[8,2,128,768]{3,2,1,0:T(8,128)(2,1)S(1)} %get-tuple-element.30.table_ref, f32[256,1024]{1,0:T(8,128)S(1)} %get-tuple-element.37.acc_ref, f32[128,1024]{1,0:T(8,128)S(1)} %get-tuple-element.38.qown_ref, ...), custom_call_target="tpu_custom_call" | custom-call | flops 167772160 | bytes 3145728 | tf_op jit(solution)/shard_map/pallas_call | solution.py:470
  30.9 0.5 %collective-permute-start.12 = (bf16[128,1024]{1,0:T(8,128)(2,1)S(1)}, bf16[128,1024]{1,0:T(8,128)(2,1)S(1)}, u32[]{:S(2)}, u32[]{:S(2)}) collective-permute-start(bf16[128,1024]{1,0:T(8,128)(2,1)S(1)} %get-tuple-element.44), channel_id=1, source_target_pairs={{0,4},{4,0},{8,12},{12,8},{16,20},{20,16},{24,28},{28,24},{1,5},{5... | collective-permute-start | bytes 786440 | tf_op jit(solution)/shard_map/ppermute | solution.py:20
  31.3 0.0 collective-permute-start.10
  31.3 1.5 %collective-permute-start.9 = (f32[1,256]{1,0:T(1,128)S(1)}, f32[1,256]{1,0:T(1,128)S(1)}, u32[]{:S(2)}, u32[]{:S(2)}) collective-permute-start(f32[1,256]{1,0:T(1,128)S(1)} %get-tuple-element.42), channel_id=1, source_target_pairs={{0,2},{1,3},{2,0},{3,1},{4,6},{5,7},{6,4},{7,5},{8,10},{9,11},{10,... | collective-permute-start | bytes 3080 | tf_op jit(solution)/shard_map/ppermute | solution.py:481
  32.9 0.3 collective-permute-start.8
  33.2 1.1 %collective-permute-done.10 = f32[1,256]{1,0:T(1,128)S(1)} collective-permute-done((f32[1,256]{1,0:T(1,128)S(1)}, f32[1,256]{1,0:T(1,128)S(1)}, u32[]{:S(2)}, u32[]{:S(2)}) %collective-permute-start.10) | collective-permute-done | bytes 1056 | tf_op jit(solution)/shard_map/ppermute | solution.py:481
  34.3 0.6 %collective-permute-done.9 = f32[1,256]{1,0:T(1,128)S(1)} collective-permute-done((f32[1,256]{1,0:T(1,128)S(1)}, f32[1,256]{1,0:T(1,128)S(1)}, u32[]{:S(2)}, u32[]{:S(2)}) %collective-permute-start.9) | collective-permute-done | bytes 1056 | tf_op jit(solution)/shard_map/ppermute | solution.py:481
  34.9 0.0 collective-permute-done.8
  35.0 1.7 %collective-permute-start.11 = (f32[1,256]{1,0:T(1,128)S(1)}, f32[1,256]{1,0:T(1,128)S(1)}, u32[]{:S(2)}, u32[]{:S(2)}) collective-permute-start(f32[1,256]{1,0:T(1,128)S(1)} %add_add_fusion.power_ref), channel_id=1, source_target_pairs={{0,4},{4,0},{8,12},{12,8},{16,20},{20,16},{24,28},{28,24},{1,5},{5... | collective-permute-start | bytes 3080 | tf_op jit(solution)/shard_map/ppermute | solution.py:20
  36.6 2.0 %collective-permute-done.11.power_got_ref = f32[1,256]{1,0:T(1,128)S(1)} collective-permute-done((f32[1,256]{1,0:T(1,128)S(1)}, f32[1,256]{1,0:T(1,128)S(1)}, u32[]{:S(2)}, u32[]{:S(2)}) %collective-permute-start.11) | collective-permute-done | bytes 1056 | tf_op jit(solution)/shard_map/ppermute | solution.py:20
  38.6 0.0 collective-permute-done.12.got_ref
  38.6 0.0 copy-done.4
  38.6 1.0 %shard_map.80 = bf16[128,2048]{1,0:T(8,128)(2,1)} custom-call(f32[1,256]{1,0:T(1,128)S(1)} %add_add_fusion.power_ref, f32[1,256]{1,0:T(1,128)S(1)} %collective-permute-done.11.power_got_ref, f32[128,1024]{1,0:T(8,128)S(1)} %get-tuple-element.43.kept_ref, bf16[128,1024]{1,0:T(8,128)(2,1)S(1)} %collective-permute-done.12.got_ref, f32[1,2048]{1,0:T(1,128)S(1)} %bitcast.13), custom_call_target="tpu_custom_call" | custom-call | flops 1048576 | bytes 1310720 | tf_op jit(solution)/shard_map/pallas_call | solution.py:483
  (6 shorter events, 0.0 us)
Async XLA Ops:
  0.0 8.2 %copy-start.2 = (s32[32]{0:T(128)S(1)}, s32[32]{0:T(128)}, u32[]{:S(2)}) copy-start(s32[32]{0:T(128)} %seq_ref.9) | copy-start | bytes 388
  0.0 8.2 %copy-start.1 = (f32[3,3,2048]{2,1,0:T(4,128)S(1)}, f32[3,3,2048]{2,1,0:T(4,128)}, u32[]{:S(2)}) copy-start(f32[3,3,2048]{2,1,0:T(4,128)} %w_ref.1) | copy-start | bytes 221188
  0.0 8.2 %copy-start.5 = (f32[16,512]{1,0:T(8,128)S(1)}, f32[16,512]{1,0:T(8,128)}, u32[]{:S(2)}) copy-start(f32[16,512]{1,0:T(8,128)} %param.9) | copy-start | bytes 98308
  0.0 8.0 %copy-start.6 = (s32[16,4]{0,1:T(4,128)S(1)}, s32[16,4]{0,1:T(4,128)}, u32[]{:S(2)}) copy-start(s32[16,4]{0,1:T(4,128)} %param.10) | copy-start | bytes 772
  2.9 8.2 %collective-permute-start = (bf16[144,512]{1,0:T(8,128)(2,1)}, bf16[144,512]{1,0:T(8,128)(2,1)S(1)}, u32[]{:S(2)}, u32[]{:S(2)}) collective-permute-start(bf16[144,512]{1,0:T(8,128)(2,1)} %get-tuple-element.29), channel_id=1, source_target_pairs={{0,4},{4,0},{8,12},{12,8},{16,20},{20,16},{24,28},{28,24},{1,5},{5... | collective-permute-start | bytes 442376 | tf_op jit(solution)/shard_map/ppermute | solution.py:20
  5.9 11.9 %collective-permute-start.1 = (bf16[144,1024]{1,0:T(8,128)(2,1)}, bf16[144,1024]{1,0:T(8,128)(2,1)S(1)}, u32[]{:S(2)}, u32[]{:S(2)}) collective-permute-start(bf16[144,1024]{1,0:T(8,128)(2,1)} %get-tuple-element.25.own_ref), channel_id=1, source_target_pairs={{0,8},{4,12},{8,16},{12,20},{16,24},{20,28},{24,0},{28,4},{1,9},{5... | collective-permute-start | bytes 884744 | tf_op jit(solution)/shard_map/ppermute | solution.py:20
  7.5 6.3 %collective-permute-start.2 = (bf16[144,512]{1,0:T(8,128)(2,1)}, bf16[144,512]{1,0:T(8,128)(2,1)S(1)}, u32[]{:S(2)}, u32[]{:S(2)}) collective-permute-start(bf16[144,512]{1,0:T(8,128)(2,1)} %get-tuple-element.33), channel_id=1, source_target_pairs={{0,4},{4,0},{8,12},{12,8},{16,20},{20,16},{24,28},{28,24},{1,5},{5... | collective-permute-start | bytes 442376 | tf_op jit(solution)/shard_map/ppermute | solution.py:20
  11.1 14.0 %copy-start = (bf16[144,1024]{1,0:T(8,128)(2,1)S(1)}, bf16[144,1024]{1,0:T(8,128)(2,1)}, u32[]{:S(2)}) copy-start(bf16[144,1024]{1,0:T(8,128)(2,1)} %get-tuple-element.25.own_ref) | copy-start | bytes 884740
  11.1 14.0 %copy-start.3 = (f32[2048]{0:T(1024)S(1)}, f32[2048]{0:T(1024)}, u32[]{:S(2)}) copy-start(f32[2048]{0:T(1024)} %param.11) | copy-start | bytes 24580
  11.1 9.9 %collective-permute-start.3 = (bf16[144,512]{1,0:T(8,128)(2,1)S(1)}, bf16[144,512]{1,0:T(8,128)(2,1)S(1)}, u32[]{:S(2)}, u32[]{:S(2)}) collective-permute-start(bf16[144,512]{1,0:T(8,128)(2,1)S(1)} %collective-permute-done.pair_a_ref), channel_id=1, source_target_pairs={{0,8},{4,12},{8,16},{12,20},{16,24},{20,28},{24,0},{28,4},{1,9},{5... | collective-permute-start | bytes 442376 | tf_op jit(solution)/shard_map/ppermute | solution.py:20
  13.8 10.1 %collective-permute-start.4 = (bf16[144,512]{1,0:T(8,128)(2,1)S(1)}, bf16[144,512]{1,0:T(8,128)(2,1)S(1)}, u32[]{:S(2)}, u32[]{:S(2)}) collective-permute-start(bf16[144,512]{1,0:T(8,128)(2,1)S(1)} %collective-permute-done.2.pair_b_ref), channel_id=1, source_target_pairs={{0,8},{4,12},{8,16},{12,20},{16,24},{20,28},{24,0},{28,4},{1,9},{5... | collective-permute-start | bytes 442376 | tf_op jit(solution)/shard_map/ppermute | solution.py:20
  15.4 11.2 %collective-permute-start.5 = (bf16[128,1024]{1,0:T(8,128)(2,1)S(1)}, bf16[128,1024]{1,0:T(8,128)(2,1)S(1)}, u32[]{:S(2)}, u32[]{:S(2)}) collective-permute-start(bf16[128,1024]{1,0:T(8,128)(2,1)S(1)} %get-tuple-element.39), channel_id=1, source_target_pairs={{0,4},{4,0},{8,12},{12,8},{16,20},{20,16},{24,28},{28,24},{1,5},{5... | collective-permute-start | bytes 786440 | tf_op jit(solution)/shard_map/ppermute | solution.py:20
  21.7 6.3 %collective-permute-start.6 = (bf16[144,512]{1,0:T(8,128)(2,1)S(1)}, bf16[144,512]{1,0:T(8,128)(2,1)S(1)}, u32[]{:S(2)}, u32[]{:S(2)}) collective-permute-start(bf16[144,512]{1,0:T(8,128)(2,1)S(1)} %shard_map.77), channel_id=1, source_target_pairs={{0,4},{4,0},{8,16},{12,20},{16,24},{20,28},{24,8},{28,12},{1,5},{5... | collective-permute-start | bytes 442376 | tf_op jit(solution)/shard_map/ppermute | solution.py:20
  24.5 5.2 %collective-permute-start.7 = (bf16[144,512]{1,0:T(8,128)(2,1)S(1)}, bf16[144,512]{1,0:T(8,128)(2,1)S(1)}, u32[]{:S(2)}, u32[]{:S(2)}) collective-permute-start(bf16[144,512]{1,0:T(8,128)(2,1)S(1)} %shard_map.78), channel_id=1, source_target_pairs={{0,4},{4,0},{8,16},{12,20},{16,24},{20,28},{24,8},{28,12},{1,5},{5... | collective-permute-start | bytes 442376 | tf_op jit(solution)/shard_map/ppermute | solution.py:20
  29.7 8.9 %copy-start.4 = (f32[2048]{0:T(1024)S(1)}, f32[2048]{0:T(1024)}, u32[]{:S(2)}) copy-start(f32[2048]{0:T(1024)} %param.12) | copy-start | bytes 24580
  30.9 7.7 %collective-permute-start.12 = (bf16[128,1024]{1,0:T(8,128)(2,1)S(1)}, bf16[128,1024]{1,0:T(8,128)(2,1)S(1)}, u32[]{:S(2)}, u32[]{:S(2)}) collective-permute-start(bf16[128,1024]{1,0:T(8,128)(2,1)S(1)} %get-tuple-element.44), channel_id=1, source_target_pairs={{0,4},{4,0},{8,12},{12,8},{16,20},{20,16},{24,28},{28,24},{1,5},{5... | collective-permute-start | bytes 786440 | tf_op jit(solution)/shard_map/ppermute | solution.py:20
  31.3 3.0 %collective-permute-start.10 = (f32[1,256]{1,0:T(1,128)S(1)}, f32[1,256]{1,0:T(1,128)S(1)}, u32[]{:S(2)}, u32[]{:S(2)}) collective-permute-start(f32[1,256]{1,0:T(1,128)S(1)} %get-tuple-element.42), channel_id=1, source_target_pairs={{0,3},{1,2},{2,1},{3,0},{4,7},{5,6},{6,5},{7,4},{8,11},{9,10},{10,... | collective-permute-start | bytes 3080 | tf_op jit(solution)/shard_map/ppermute | solution.py:481
  31.3 3.6 %collective-permute-start.9 = (f32[1,256]{1,0:T(1,128)S(1)}, f32[1,256]{1,0:T(1,128)S(1)}, u32[]{:S(2)}, u32[]{:S(2)}) collective-permute-start(f32[1,256]{1,0:T(1,128)S(1)} %get-tuple-element.42), channel_id=1, source_target_pairs={{0,2},{1,3},{2,0},{3,1},{4,6},{5,7},{6,4},{7,5},{8,10},{9,11},{10,... | collective-permute-start | bytes 3080 | tf_op jit(solution)/shard_map/ppermute | solution.py:481
  32.9 2.1 %collective-permute-start.8 = (f32[1,256]{1,0:T(1,128)S(1)}, f32[1,256]{1,0:T(1,128)S(1)}, u32[]{:S(2)}, u32[]{:S(2)}) collective-permute-start(f32[1,256]{1,0:T(1,128)S(1)} %get-tuple-element.42), channel_id=1, source_target_pairs={{0,1},{1,0},{2,3},{3,2},{4,5},{5,4},{6,7},{7,6},{8,9},{9,8},{10,11... | collective-permute-start | bytes 3080 | tf_op jit(solution)/shard_map/ppermute | solution.py:481
  35.0 3.6 %collective-permute-start.11 = (f32[1,256]{1,0:T(1,128)S(1)}, f32[1,256]{1,0:T(1,128)S(1)}, u32[]{:S(2)}, u32[]{:S(2)}) collective-permute-start(f32[1,256]{1,0:T(1,128)S(1)} %add_add_fusion.power_ref), channel_id=1, source_target_pairs={{0,4},{4,0},{8,12},{12,8},{16,20},{20,16},{24,28},{28,24},{1,5},{5... | collective-permute-start | bytes 3080 | tf_op jit(solution)/shard_map/ppermute | solution.py:20

commit v11 on v10

--- a/solution.py
+++ b/solution.py
@@ -104,8 +104,10 @@
                 heads.append(x[0:2])
                 tails.append(x[rows - 2 :])
             out_ref[:rows, there] = (made[0] * made[1]).astype(out_ref.dtype)
-            tails.append(q_ref[:, lanes].astype(jnp.float32)[14:])
-            extra = jnp.concatenate(heads + tails + [jnp.zeros((6, GROUP), jnp.float32)], 0)
+            across = pl.ds(pl.multiple_of(keep_at + send_at - at + base, GROUP), GROUP)
+            for place in (lanes, across):
+                tails.append(q_ref[:, place].astype(jnp.float32)[14:])
+            extra = jnp.concatenate(heads + tails + [jnp.zeros((4, GROUP), jnp.float32)], 0)
             out_ref[rows:, there] = extra.astype(out_ref.dtype)
 
 
@@ -150,7 +152,7 @@
     return first - 2 * BLK - start > BLK
 
 
-def tables_kernel(seq_ref, taps_ref, w_ref, out_ref, next_ref, w_half_ref, rev_ref, m_ref):
+def tables_kernel(seq_ref, taps_ref, w_ref, out_ref, next_ref, w_half_ref, wq_ref, rev_ref, m_ref):
     groups = out_ref.shape[0]
     taps = taps_ref.shape[1]
     span = out_ref.shape[3]
@@ -158,6 +160,7 @@
     start = lax.axis_index("blk") * (2 * BLK)
     width = w_half_ref.shape[2]
     w_half_ref[...] = w_ref[:, :, pl.ds(pl.multiple_of(half * width, width), width)]
+    wq_ref[...] = w_ref[0]
     turn = lax.broadcasted_iota(jnp.int32, (taps, span), 0) + lax.broadcasted_iota(
         jnp.int32, (taps, span), 1
     )
@@ -220,22 +223,31 @@
         out_ref[:BLK] = win_ref[BLK:]
 
 
-def gate_rows(seq_ref, raw_ref, tail, w_ref, part, q_ref, x_ref, m1_ref, m2_ref):
-    width = raw_ref.shape[1]
-    row_masks(seq_ref, lax.axis_index("blk") * (2 * BLK) + part * BLK, m1_ref, m2_ref)
-    for c in range(0, width, GROUP):
-        lanes = slice(c, c + GROUP)
-        w = w_ref[0, :, lanes]
+def query_kernel(
+    seq_ref, raw_ref, pair_a_ref, pair_b_ref, back_a_ref, back_b_ref, w_ref, q_ref, x_ref, m1_ref, m2_ref
+):
+    piece = pair_a_ref.shape[1]
+    half = lax.axis_index("half")
+    row_masks(seq_ref, (lax.axis_index("blk") * 2 + half) * BLK, m1_ref, m2_ref)
+    for c in range(0, 4 * piece, GROUP):
+        turned = c // (2 * piece)
+        inside = c % (2 * piece)
+        at = jnp.where(half == turned, 0, 2 * piece) + inside
+        lanes = pl.ds(pl.multiple_of(at, GROUP), GROUP)
+        there = slice(inside % piece, inside % piece + GROUP)
+        pair_ref, back_ref = (pair_a_ref, back_a_ref) if inside < piece else (pair_b_ref, back_b_ref)
+        pair = pair_ref[BLK:, there].astype(jnp.float32)
+        back = back_ref[BLK:, there].astype(jnp.float32)
         x = raw_ref[:, lanes].astype(jnp.float32)
         slot = (c // GROUP) % 2
-        x_ref[slot, 6:8, :] = tail(lanes)
+        x_ref[slot, 6:8, :] = jnp.where(half == 1, pair, back)[8 + 2 * turned : 10 + 2 * turned]
         x_ref[slot, 8:, :] = x
-        q_ref[:, lanes] = feature(x, x_ref.at[slot], w, m1_ref, m2_ref)
+        q_ref[:, c : c + GROUP] = feature(x, x_ref.at[slot], w_ref[:, lanes], m1_ref, m2_ref)
 
 
 def near_kernel(
-    seq_ref, table_ref, own_ref, back_own_ref, pair_a_ref, pair_b_ref, back_a_ref, back_b_ref, qkept_ref, w_ref, bias_ref,
-    acc_ref, q_ref, marks_ref, win_ref, extra_ref, x_ref, m1_ref, m2_ref,
+    seq_ref, table_ref, own_ref, back_own_ref, pair_a_ref, pair_b_ref, back_a_ref, back_b_ref, w_ref, bias_ref,
+    acc_ref, marks_ref, win_ref, extra_ref,
 ):
     groups = table_ref.shape[0]
     width = groups * GROUP
@@ -262,88 +274,93 @@
             )
             here = win_ref[(2 + part) * BLK : (3 + part) * BLK, lanes].astype(jnp.float32)
             acc_ref[part * BLK : (part + 1) * BLK, lanes] = total + bias * here
-    gate_rows(
-        seq_ref, qkept_ref, lambda lanes: extra_ref[1 + half, 8:10, lanes], w_ref, half, q_ref, x_ref, m1_ref, m2_ref
-    )
-
-
-def pair_gate_kernel(seq_ref, raw_ref, own_ref, back_own_ref, w_ref, q_ref, x_ref, m1_ref, m2_ref):
-    half = lax.axis_index("half")
-
-    def tail(lanes):
-        back = back_own_ref[BLK:, lanes].astype(jnp.float32)
-        own = own_ref[BLK:, lanes].astype(jnp.float32)
-        return jnp.where(half == 1, back, own)[8:10]
-
-    gate_rows(seq_ref, raw_ref, tail, w_ref, 1 - half, q_ref, x_ref, m1_ref, m2_ref)
-
-
-def far_kernel(short, table_ref, acc_ref, qown_ref, qpair_ref, w_ref, marks_ref, *refs):
-    *messages, kept_ref, sent_ref, power_ref, win_ref, extra_ref = refs
-    groups = table_ref.shape[0]
-    width = groups * GROUP
-    half = lax.axis_index("half")
+
+
+def far_kernel(short, piece, table_ref, acc_ref, q_ref, w_ref, marks_ref, back_own_ref, back_pair_ref, *refs):
+    *far_refs, kept_ref, sent_ref, squares_ref, win_ref, extra_ref = refs
+    width = kept_ref.shape[1]
+    half = lax.axis_index("half")
+    lanes = slice(piece * width, (piece + 1) * width)
     marks = [marks_ref[0], marks_ref[1]]
-    back_own_ref, back_a_ref, back_b_ref, *far_refs = messages
     low = 1 if short else 0
-    fill(win_ref, extra_ref, 2 + half, back_own_ref)
-    fill(win_ref, extra_ref, 3 - half, back_a_ref, back_b_ref)
+    fill(win_ref, extra_ref, 2 + half, back_own_ref.at[:, lanes])
+    fill(win_ref, extra_ref, 3 - half, back_pair_ref)
     if short:
         summed = marks_ref[2, 0:1, 0:1]
-        fill(win_ref, extra_ref, 1, *far_refs)
+        fill(win_ref, extra_ref, 1, far_refs[0])
         payload = win_ref[BLK : 2 * BLK, :].astype(jnp.float32)
         win_ref[BLK : 2 * BLK, :] = (payload * (1.0 - summed)).astype(win_ref.dtype)
     else:
-        fill(win_ref, extra_ref, half, far_refs[0])
-        fill(win_ref, extra_ref, 1 - half, far_refs[1], far_refs[2])
-        ahead = far_refs[3][...].astype(jnp.float32)[:8]
-        put_first_rows(win_ref, 0, first_rows(extra_ref[0, :8], ahead, w_ref, marks, 0))
-        rows = first_rows(extra_ref[1, :8], extra_ref[0, :8], w_ref, marks, 1)
+        fill(win_ref, extra_ref, half, far_refs[0].at[:, lanes])
+        fill(win_ref, extra_ref, 1 - half, far_refs[1 + piece])
+        ahead = far_refs[3][:, lanes].astype(jnp.float32)[:8]
+        put_first_rows(win_ref, 0, first_rows(extra_ref[0, :8], ahead, w_ref, marks, 0, lanes))
+        rows = first_rows(extra_ref[1, :8], extra_ref[0, :8], w_ref, marks, 1, lanes)
         put_first_rows(win_ref, BLK, rows)
-    rows = first_rows(extra_ref[2, :8], extra_ref[1, :8], w_ref, marks, 2)
+    rows = first_rows(extra_ref[2, :8], extra_ref[1, :8], w_ref, marks, 2, lanes)
     put_first_rows(win_ref, 2 * BLK, rows)
-    for at, part, q_ref, out_ref in ((0, half, qown_ref, kept_ref), (BLK, 1 - half, qpair_ref, sent_ref)):
-        squares = jnp.zeros((BLK, GROUP), jnp.float32)
+    squares = jnp.zeros((BLK, GROUP), jnp.float32)
+    for part, own in ((1 - half, False), (half, True)):
         rows = pl.ds(pl.multiple_of(part * BLK, BLK), BLK)
-        for g in range(groups):
-            lanes = slice(g * GROUP, (g + 1) * GROUP)
-            filtered = acc_ref[rows, lanes] + jnp.dot(
-                table_ref[g, part, :, low * BLK : 3 * BLK],
-                win_ref[low * BLK : 3 * BLK, lanes],
+        for c in range(0, width, GROUP):
+            here = slice(c, c + GROUP)
+            whole = slice(piece * width + c, piece * width + c + GROUP)
+            filtered = acc_ref[rows, whole] + jnp.dot(
+                table_ref[(piece * width + c) // GROUP, part, :, low * BLK : 3 * BLK],
+                win_ref[low * BLK : 3 * BLK, here],
                 preferred_element_type=jnp.float32,
             )
             if short:
                 weight = summed * (part == 0).astype(jnp.float32)
-                at_far = g * GROUP % far_refs[0].shape[1]
-                far_ref = far_refs[g * GROUP // far_refs[0].shape[1]]
-                filtered = filtered + weight * far_ref[:BLK, at_far : at_far + GROUP].astype(jnp.float32)
-            gated = q_ref[:, lanes] * filtered
-            squares = squares + gated * gated
-            out_ref[:, lanes] = gated.astype(out_ref.dtype)
-        power_ref[:, at : at + BLK] = lax.dot_general(
-            jnp.ones((8, GROUP), jnp.float32),
-            squares,
-            (((1,), (1,)), ((), ())),
-            precision=lax.Precision.HIGHEST,
-            preferred_element_type=jnp.float32,
-        )[0:1]
-
-
-def norm_kernel(channels, power_ref, power_got_ref, kept_ref, got_ref, gain_ref, out_ref):
-    half = lax.axis_index("half")
-    width = kept_ref.shape[1]
-    power = power_ref[:, :BLK] + power_got_ref[:, BLK:]
+                filtered = filtered + weight * far_refs[0][:BLK, here].astype(jnp.float32)
+            if own:
+                gated = q_ref[:, whole] * filtered
+                kept_ref[:, here] = gated
+                squares = squares + gated * gated
+            else:
+                sent_ref[:, here] = filtered.astype(sent_ref.dtype)
+    squares_ref[...] = squares
+
+
+def gate_kernel(piece, q_ref, got_ref, gated_ref, squares_ref):
+    width = got_ref.shape[1]
+    squares = jnp.zeros((BLK, GROUP), jnp.float32)
+    for c in range(0, width, GROUP):
+        at = (2 + piece) * width + c
+        gated = q_ref[:, at : at + GROUP] * got_ref[:, c : c + GROUP].astype(jnp.float32)
+        gated_ref[:, c : c + GROUP] = gated
+        squares = squares + gated * gated
+    squares_ref[...] = squares
+
+
+def last_gate_kernel(piece, q_ref, got_ref, *refs):
+    *other_refs, gated_ref, power_ref, squares_ref = refs
+    gate_kernel(piece, q_ref, got_ref, gated_ref, squares_ref)
+    power_ref[...] = lax.dot_general(
+        jnp.ones((8, GROUP), jnp.float32),
+        sum([ref[...] for ref in other_refs], squares_ref[...]),
+        (((1,), (1,)), ((), ())),
+        precision=lax.Precision.HIGHEST,
+        preferred_element_type=jnp.float32,
+    )[0:1]
+
+
+def norm_kernel(channels, pieces, *refs):
+    part_refs, (*power_refs, gain_ref, out_ref) = refs[:pieces], refs[pieces:]
+    half = lax.axis_index("half")
+    width = part_refs[0].shape[1]
+    power = sum([ref[...] for ref in power_refs[1:]], power_refs[0][...])
     scale = lax.rsqrt(power / channels + norm_eps)
     diagonal = lax.broadcasted_iota(jnp.int32, (BLK, BLK), 0) == lax.broadcasted_iota(
         jnp.int32, (BLK, BLK), 1
     )
     column = jnp.sum(jnp.where(diagonal, scale, 0.0), axis=1, keepdims=True)
-    for which, part_ref in ((half, kept_ref), (1 - half, got_ref)):
+    for p, part_ref in enumerate(part_refs):
+        which = half if p < pieces // 2 else 1 - half
         for c in range(0, width, GROUP):
-            lanes = pl.ds(pl.multiple_of(which * width + c, GROUP), GROUP)
-            out_ref[:, lanes] = (
-                part_ref[:, c : c + GROUP].astype(jnp.float32) * column * gain_ref[:, lanes]
-            ).astype(out_ref.dtype)
+            at = (which * (pieces // 2) + p % (pieces // 2)) * width + c
+            lanes = pl.ds(pl.multiple_of(at, GROUP), GROUP)
+            out_ref[:, lanes] = (part_ref[:, c : c + GROUP] * column * gain_ref[:, lanes]).astype(out_ref.dtype)
 
 
 def kernel_call(body, outs, in_specs, scratch, flops, moved_bytes, vmem=24 << 20):
@@ -364,8 +381,9 @@
     groups = width // GROUP
     taps = filter_taps.shape[1]
     shape = jax.ShapeDtypeStruct
-    half_shape = shape((rows, width), jnp.bfloat16)
-    half_wide = shape((rows, width), jnp.float32)
+    piece_shape = shape((rows, width // 2), jnp.bfloat16)
+    piece_wide = shape((rows, width // 2), jnp.float32)
+    squares = shape((rows, GROUP), jnp.float32)
 
     spots = range(2 * blocks)
     to_pair = [(i, i ^ 1) for i in spots]
@@ -398,31 +416,28 @@
     )(seq_lengths, panels, short_weight)
 
     back_own = moved(kept, ahead)
-    pair = [moved(piece, to_pair) for piece in sent]
-
     filter_taps, _ = lax.optimization_barrier((filter_taps, kept))
     scaled = (filter_taps * jnp.repeat(tap_blocks.astype(jnp.float32), BLK, axis=1)).astype(jnp.bfloat16)
+    scaled, *sent = lax.optimization_barrier((scaled, *sent))
+    pair = [moved(piece, to_pair) for piece in sent]
     span = taps + 2 * BLK
-    table, table_next, w_half = kernel_call(
+    table, table_next, w_half, w_query = kernel_call(
         tables_kernel,
         (
             shape((groups, 2, BLK, span), jnp.bfloat16),
             shape((groups, BLK, 2 * BLK), jnp.bfloat16),
             shape((3, 3, width), jnp.float32),
+            shape((3, 2 * width), jnp.float32),
         ),
         [SMEM, VMEM, VMEM],
         [pltpu.VMEM((2 * groups, span), jnp.float32), pltpu.VMEM((3, BLK, span), jnp.float32)],
         40 * groups * BLK * taps,
         8 * groups * BLK * taps,
     )(seq_lengths, scaled, short_weight)
-    table, table_next, pair[0] = lax.optimization_barrier((table, table_next, pair[0]))
-
-    half = lax.axis_index("half")
-    query, _ = lax.optimization_barrier((panels, pair[0]))
-    qkept = lax.dynamic_slice(query, (0, 0, half * width), (1, rows, width))[0]
-    qsent = lax.dynamic_slice(query, (0, 0, (1 - half) * width), (1, rows, width))[0]
-    qkept, qsent, pair[1] = lax.optimization_barrier((qkept, qsent, pair[1]))
-    qgot = moved(qsent, to_pair)
+    table, table_next, pair[1] = lax.optimization_barrier((table, table_next, pair[1]))
+
+    query, _ = lax.optimization_barrier((panels, table_next))
+    query = query[0]
     back_pair = [moved(piece, ahead) for piece in pair]
 
     window = pltpu.VMEM((4 * rows, width), jnp.bfloat16)
@@ -446,48 +461,66 @@
         across = jnp.concatenate([piece[rows:] for piece in sent], 1)
         across = moved(across, [(i, ((i ^ 1) + 6) % (2 * blocks)) for i in spots])
         straight = moved(kept[rows:], [(i, (i + 6) % (2 * blocks)) for i in spots])
-        deep = jnp.where(half == 1, straight, across)
+        deep = jnp.where(lax.axis_index("half") == 1, straight, across)
         far = [moved(piece, ahead) for piece in (back_own, *back_pair)] + [deep]
 
-    acc, qown, marks = kernel_call(
+    acc, marks = kernel_call(
         near_kernel,
-        (shape((2 * rows, width), jnp.float32), half_wide, shape((3, 8, GROUP), jnp.float32)),
-        [SMEM] + [VMEM] * 10,
-        [window, extras, shifted, row_mask, row_mask],
+        (shape((2 * rows, width), jnp.float32), shape((3, 8, GROUP), jnp.float32)),
+        [SMEM] + [VMEM] * 9,
+        [window, extras],
         2 * 5 * rows * BLK * width,
         16 * rows * width,
-    )(seq_lengths, table, kept, back_own, *pair, *back_pair, qkept, w_half, skip_bias.reshape(1, -1))
-
-    qpair = kernel_call(
-        pair_gate_kernel,
-        half_wide,
-        [SMEM] + [VMEM] * 4,
-        [shifted, row_mask, row_mask],
-        10 * rows * width,
-        8 * rows * width,
-    )(seq_lengths, qgot, kept, back_own, w_half)
-
-    done, send, power = kernel_call(
-        functools.partial(far_kernel, short),
-        (half_wide, half_shape, shape((1, 2 * rows), jnp.float32)),
-        [VMEM] * (9 + len(far)),
-        [window, extras],
-        2 * 5 * rows * BLK * width,
-        24 * rows * width,
-    )(table, acc, qown, qpair, w_half, marks, back_own, *back_pair, *far)
-
-    back = moved(send, to_pair)
+    )(seq_lengths, table, kept, back_own, *pair, *back_pair, w_half, skip_bias.reshape(1, -1))
+
+    q = kernel_call(
+        query_kernel,
+        shape((rows, 2 * width), jnp.float32),
+        [SMEM] + [VMEM] * 6,
+        [pltpu.VMEM((2, rows + 8, GROUP), jnp.float32), row_mask, row_mask],
+        20 * rows * width,
+        12 * rows * width,
+    )(seq_lengths, query, *pair, *back_pair, w_query)
+
+    own, got, parts = [], [], []
+    for piece in range(2):
+        needed = far[piece : piece + 1] if short else far
+        if parts:
+            acc, _ = lax.optimization_barrier((acc, parts[0]))
+        done, send, part = kernel_call(
+            functools.partial(far_kernel, short, piece),
+            (piece_wide, piece_shape, squares),
+            [VMEM] * (7 + len(needed)),
+            [pltpu.VMEM((4 * rows, width // 2), jnp.bfloat16), pltpu.VMEM((4, 16, width // 2), jnp.float32)],
+            2 * 3 * rows * BLK * width,
+            12 * rows * width,
+        )(table, acc, q, w_half, marks, back_own, back_pair[piece], *needed)
+        own.append(done)
+        parts.append(part)
+        got.append(moved(send, to_pair))
+    first, part = kernel_call(
+        functools.partial(gate_kernel, 0), (piece_wide, squares), [VMEM] * 2, [], rows * width, 5 * rows * width
+    )(q, got[0])
+    second, power = kernel_call(
+        functools.partial(last_gate_kernel, 1),
+        (piece_wide, shape((1, rows), jnp.float32)),
+        [VMEM] * 5,
+        [pltpu.VMEM((rows, GROUP), jnp.float32)],
+        rows * width,
+        5 * rows * width,
+    )(q, got[1], *parts, part)
+
     peers = lax.axis_size("mp")
-    shares = [lax.ppermute(power, "mp", [(i, i ^ k) for i in range(peers)]) for k in range(1, peers)]
-    power = sum(shares, power)
+    powers = [power] + [lax.ppermute(power, "mp", [(i, i ^ k) for i in range(peers)]) for k in range(1, peers)]
+    results = (*own, first, second)
     return kernel_call(
-        functools.partial(norm_kernel, channels),
+        functools.partial(norm_kernel, channels, len(results)),
         shape((rows, 2 * width), jnp.bfloat16),
-        [VMEM] * 5,
+        [VMEM] * (len(results) + len(powers) + 1),
         [],
         8 * rows * width,
         10 * rows * width,
-    )(power, moved(power, to_pair), done, back, norm_gain.reshape(1, -1))
+    )(*results, *powers, norm_gain.reshape(1, -1))
 
 
 def solution(mesh):

time: 39.8 us -> 42.7 us (1.073)
  waiting for transfers between devices: 11.5 us -> 14.3 us
  starting transfers between devices: 15.1 us -> 14.2 us
  other arithmetic: 0.02 us -> 0.73 us
    ppermute x10 -> x9, waiting for transfers between devices: 9.77 us -> 12.6 us  [moved(): return lax.ppermute(block, SPOTS, pairs)]
    ppermute x10 -> x9, starting transfers between devices: 13.2 us -> 12.3 us  [moved(): return lax.ppermute(block, SPOTS, pairs)]
    convert_element_type x1, other arithmetic: 0.01 us -> 0.72 us  [shards(): tap_blocks.astype(jnp.float32)]
    pallas_call x4 -> x7, Pallas kernels: 4.6 us -> 4.61 us  [the longest x1 1.36 us: shards(): kernel_call(near_kernel, (shape((2 * rows, width), jnp.float32), shape((3...]
  transfers between devices with their start and end apart: 13 -> 12, of which waited for: 8 -> 7; matrix products, arithmetic and copies ran while one was open for 3% -> 3% of each run, Pallas kernels for 17% -> 18%
where the time goes in v11:
time: 42.7 us; the launch traced here: 42.3 us
  waiting for transfers between devices  14.3 us (33%)
  starting transfers between devices  14.2 us (33%)
  Pallas kernels  11.6 us (27%)
  local copies, waits for them, and re-layouts  1.27 us (3%)
  other arithmetic  0.73 us (2%)
    ppermute x9, waiting for transfers between devices, moved(): return lax.ppermute(block, SPOTS, pairs)  12.6 us
    ppermute x9, starting transfers between devices, moved(): return lax.ppermute(block, SPOTS, pairs)  12.3 us
    pallas_call x1, Pallas kernels, shards(): kernel_call(products_kernel, (message, small, small), [hbm] * 3, [pltpu.S...  2.81 us
    pallas_call x1, Pallas kernels, shards(): kernel_call(tables_kernel, (shape((groups, 2, BLK, span), jnp.bfloat16),...  2.8 us
    ppermute x3, starting transfers between devices, shards(): lax.ppermute(power, 'mp', [(i, i ^ k) for i in range(peers)])  1.89 us
    ppermute x3, waiting for transfers between devices, shards(): lax.ppermute(power, 'mp', [(i, i ^ k) for i in range(peers)])  1.71 us
    pallas_call x2, Pallas kernels, shards(): kernel_call(functools.partial(relay_kernel, piece), small, [SMEM] + [VMEM...  1.36 us
    pallas_call x1, Pallas kernels, shards(): kernel_call(near_kernel, (shape((2 * rows, width), jnp.float32), shape((3...  1.36 us
  transfers between devices with their start and end apart: 12, of which 7 were waited for; matrix products, arithmetic and copies ran while one was open for 3% of the time, Pallas kernels for 18%

profile of v11, /device:TPU:0, one launch (start us, length us, event | category | flops | bytes accessed | tf_op | source)
XLA Modules:
  0.0 42.3 jit_solution(3599355180823556767)
XLA Ops:
  0.0 0.0 copy-start.2
  0.0 0.7 %convert_element_type.6 = f32[16,4]{0,1:T(4,128)S(1)} convert(s32[16,4]{0,1:T(4,128)} %param.10) | non-fusion elementwise | flops 64 | bytes 512 | tf_op jit(solution)/shard_map/convert_element_type | solution.py:420
  0.7 0.1 copy.8
  0.8 2.8 %shard_map.73 = (bf16[144,1024]{1,0:T(8,128)(2,1)}, bf16[144,512]{1,0:T(8,128)(2,1)}, bf16[144,512]{1,0:T(8,128)(2,1)}) custom-call(s32[32]{0:T(128)} %seq_ref.9, bf16[3,128,2048]{2,1,0:T(8,128)(2,1)} %bitcast.12, f32[3,3,2048]{2,1,0:T(4,128)} %w_ref.1), custom_call_target="tpu_custom_call" | custom-call | flops 5242880 | bytes 2097152 | tf_op jit(solution)/shard_map/pallas_call | solution.py:399
  3.6 0.1 broadcast_in_dim.3
  3.7 0.0 copy-done.5
  3.7 3.0 %collective-permute-start.2 = (bf16[144,512]{1,0:T(8,128)(2,1)}, bf16[144,512]{1,0:T(8,128)(2,1)S(1)}, u32[]{:S(2)}, u32[]{:S(2)}) collective-permute-start(bf16[144,512]{1,0:T(8,128)(2,1)} %get-tuple-element.42), channel_id=1, source_target_pairs={{0,4},{4,0},{8,12},{12,8},{16,20},{20,16},{24,28},{28,24},{1,5},{5... | collective-permute-start | bytes 442376 | tf_op jit(solution)/shard_map/ppermute | solution.py:20
  6.8 1.6 %collective-permute-start.1 = (bf16[144,1024]{1,0:T(8,128)(2,1)}, bf16[144,1024]{1,0:T(8,128)(2,1)S(1)}, u32[]{:S(2)}, u32[]{:S(2)}) collective-permute-start(bf16[144,1024]{1,0:T(8,128)(2,1)} %get-tuple-element.33.own_ref), channel_id=1, source_target_pairs={{0,8},{4,12},{8,16},{12,20},{16,24},{20,28},{24,0},{28,4},{1,9},{5... | collective-permute-start | bytes 884744 | tf_op jit(solution)/shard_map/ppermute | solution.py:20
  8.4 0.5 %collective-permute-start = (bf16[144,512]{1,0:T(8,128)(2,1)}, bf16[144,512]{1,0:T(8,128)(2,1)S(1)}, u32[]{:S(2)}, u32[]{:S(2)}) collective-permute-start(bf16[144,512]{1,0:T(8,128)(2,1)} %get-tuple-element.40), channel_id=1, source_target_pairs={{0,4},{4,0},{8,12},{12,8},{16,20},{20,16},{24,28},{28,24},{1,5},{5... | collective-permute-start | bytes 442376 | tf_op jit(solution)/shard_map/ppermute | solution.py:20
  8.9 2.5 %collective-permute-done.2.pair_a_ref = bf16[144,512]{1,0:T(8,128)(2,1)S(1)} collective-permute-done((bf16[144,512]{1,0:T(8,128)(2,1)}, bf16[144,512]{1,0:T(8,128)(2,1)S(1)}, u32[]{:S(2)}, u32[]{:S(2)}) %collective-permute-start.2) | collective-permute-done | bytes 147488 | tf_op jit(solution)/shard_map/ppermute | solution.py:20
  11.3 1.9 %collective-permute-start.3 = (bf16[144,512]{1,0:T(8,128)(2,1)S(1)}, bf16[144,512]{1,0:T(8,128)(2,1)S(1)}, u32[]{:S(2)}, u32[]{:S(2)}) collective-permute-start(bf16[144,512]{1,0:T(8,128)(2,1)S(1)} %collective-permute-done.2.pair_a_ref), channel_id=1, source_target_pairs={{0,8},{4,12},{8,16},{12,20},{16,24},{20,28},{24,0},{28,4},{1,9},{5... | collective-permute-start | bytes 442376 | tf_op jit(solution)/shard_map/ppermute | solution.py:20
  13.2 0.0 copy-done.2
  13.2 0.0 copy-done
  13.2 2.8 %shard_map.74 = (bf16[8,2,128,768]{3,2,1,0:T(8,128)(2,1)S(1)}, bf16[8,128,256]{2,1,0:T(8,128)(2,1)S(1)}, f32[3,3,1024]{2,1,0:T(4,128)S(1)}, f32[3,2048]{1,0:T(4,128)S(1)}) custom-call(s32[32]{0:T(128)S(1)} %copy-done.2, bf16[16,512]{1,0:T(8,128)(2,1)S(1)} %fusion.taps_ref, f32[3,3,2048]{2,1,0:T(4,128)S(1)} %copy-done), custom_call_target="tpu_custom_call" | custom-call | flops 20971520 | bytes 4194304 | tf_op jit(solution)/shard_map/pallas_call | solution.py:424
  16.0 0.0 collective-permute-done.pair_b_ref
  16.0 1.6 %collective-permute-start.4 = (bf16[144,512]{1,0:T(8,128)(2,1)S(1)}, bf16[144,512]{1,0:T(8,128)(2,1)S(1)}, u32[]{:S(2)}, u32[]{:S(2)}) collective-permute-start(bf16[144,512]{1,0:T(8,128)(2,1)S(1)} %collective-permute-done.pair_b_ref), channel_id=1, source_target_pairs={{0,8},{4,12},{8,16},{12,20},{16,24},{20,28},{24,0},{28,4},{1,9},{5... | collective-permute-start | bytes 442376 | tf_op jit(solution)/shard_map/ppermute | solution.py:20
  17.7 4.2 %collective-permute-done.3.back_a_ref.back_pair_ref = bf16[144,512]{1,0:T(8,128)(2,1)S(1)} collective-permute-done((bf16[144,512]{1,0:T(8,128)(2,1)S(1)}, bf16[144,512]{1,0:T(8,128)(2,1)S(1)}, u32[]{:S(2)}, u32[]{:S(2)}) %collective-permute-start.3) | collective-permute-done | bytes 147488 | tf_op jit(solution)/shard_map/ppermute | solution.py:20
  21.9 0.0 collective-permute-done.1.back_own_ref
  21.9 0.7 %shard_map.77 = bf16[144,512]{1,0:T(8,128)(2,1)S(1)} custom-call(s32[32]{0:T(128)S(1)} %copy-done.2, bf16[8,128,256]{2,1,0:T(8,128)(2,1)S(1)} %get-tuple-element.46.next_ref, bf16[144,1024]{1,0:T(8,128)(2,1)S(1)} %collective-permute-done.1.back_own_ref, bf16[144,512]{1,0:T(8,128)(2,1)S(1)} %collective-permute-done.3.back_a_ref.back_pair_ref, ...), custom_call_target="tpu_custom_call" | custom-call | flops 33554432 | bytes 524288 | tf_op jit(solution)/shard_map/pallas_call | solution.py:451
  22.6 0.1 collective-permute-start.5
  22.6 2.1 %collective-permute-done.4.back_b_ref.back_pair_ref = bf16[144,512]{1,0:T(8,128)(2,1)S(1)} collective-permute-done((bf16[144,512]{1,0:T(8,128)(2,1)S(1)}, bf16[144,512]{1,0:T(8,128)(2,1)S(1)}, u32[]{:S(2)}, u32[]{:S(2)}) %collective-permute-start.4) | collective-permute-done | bytes 147488 | tf_op jit(solution)/shard_map/ppermute | solution.py:20
  24.7 0.7 %shard_map.79 = bf16[144,512]{1,0:T(8,128)(2,1)S(1)} custom-call(s32[32]{0:T(128)S(1)} %copy-done.2, bf16[8,128,256]{2,1,0:T(8,128)(2,1)S(1)} %get-tuple-element.46.next_ref, bf16[144,1024]{1,0:T(8,128)(2,1)S(1)} %collective-permute-done.1.back_own_ref, bf16[144,512]{1,0:T(8,128)(2,1)S(1)} %collective-permute-done.4.back_b_ref.back_pair_ref, ...), custom_call_target="tpu_custom_call" | custom-call | flops 33554432 | bytes 524288 | tf_op jit(solution)/shard_map/pallas_call | solution.py:451
  25.4 0.0 copy-start.1
  25.4 0.0 copy-start.3
  25.4 1.5 %collective-permute-start.6 = (bf16[144,512]{1,0:T(8,128)(2,1)S(1)}, bf16[144,512]{1,0:T(8,128)(2,1)S(1)}, u32[]{:S(2)}, u32[]{:S(2)}) collective-permute-start(bf16[144,512]{1,0:T(8,128)(2,1)S(1)} %shard_map.79), channel_id=1, source_target_pairs={{0,4},{4,0},{8,16},{12,20},{16,24},{20,28},{24,8},{28,12},{1,5},{5... | collective-permute-start | bytes 442376 | tf_op jit(solution)/shard_map/ppermute | solution.py:20
  26.9 1.1 %slice_bitcast_fusion.raw_ref = bf16[128,2048]{1,0:T(8,128)(2,1)S(1)} fusion(bf16[3,128,2048]{2,1,0:T(8,128)(2,1)} %bitcast.13), kind=kLoop, calls=%fused_computation | loop fusion | bytes 1048576 | tf_op jit(solution)/shard_map/squeeze | solution.py:440
  28.0 1.2 %shard_map.76.q_ref = f32[128,2048]{1,0:T(8,128)S(1)} custom-call(s32[32]{0:T(128)S(1)} %copy-done.2, bf16[128,2048]{1,0:T(8,128)(2,1)S(1)} %slice_bitcast_fusion.raw_ref, bf16[144,512]{1,0:T(8,128)(2,1)S(1)} %collective-permute-done.2.pair_a_ref, bf16[144,512]{1,0:T(8,128)(2,1)S(1)} %collective-permute-done.pair_b_ref, ...), custom_call_target="tpu_custom_call" | custom-call | flops 2621440 | bytes 1572864 | tf_op jit(solution)/shard_map/pallas_call | solution.py:476
  29.2 0.0 copy-done.1
  29.2 0.0 copy-done.3
  29.2 1.4 %shard_map.75 = (f32[256,1024]{1,0:T(8,128)S(1)}, f32[3,8,128]{2,1,0:T(8,128)S(1)}) custom-call(s32[32]{0:T(128)S(1)} %copy-done.2, bf16[8,2,128,768]{3,2,1,0:T(8,128)(2,1)S(1)} %get-tuple-element.41.table_ref, bf16[144,1024]{1,0:T(8,128)(2,1)S(1)} %copy-done.1, bf16[144,1024]{1,0:T(8,128)(2,1)S(1)} %collective-permute-done.1.back_own_ref, ...), custom_call_target="tpu_custom_call" | custom-call | flops 167772160 | bytes 2097152 | tf_op jit(solution)/shard_map/pallas_call | solution.py:467
  30.6 0.0 collective-permute-done.5.refs_0_
  30.6 0.4 shard_map.78
  31.0 0.6 %collective-permute-start.7 = (bf16[128,512]{1,0:T(8,128)(2,1)S(1)}, bf16[128,512]{1,0:T(8,128)(2,1)S(1)}, u32[]{:S(2)}, u32[]{:S(2)}) collective-permute-start(bf16[128,512]{1,0:T(8,128)(2,1)S(1)} %get-tuple-element.54), channel_id=1, source_target_pairs={{0,4},{4,0},{8,12},{12,8},{16,20},{20,16},{24,28},{28,24},{1,5},{5... | collective-permute-start | bytes 393224 | tf_op jit(solution)/shard_map/ppermute | solution.py:20
  31.6 0.0 collective-permute-done.6.refs_0_
  31.6 0.4 shard_map.80
  32.0 0.0 copy-start.4
  32.0 1.5 %collective-permute-start.8 = (bf16[128,512]{1,0:T(8,128)(2,1)S(1)}, bf16[128,512]{1,0:T(8,128)(2,1)S(1)}, u32[]{:S(2)}, u32[]{:S(2)}) collective-permute-start(bf16[128,512]{1,0:T(8,128)(2,1)S(1)} %get-tuple-element.56), channel_id=1, source_target_pairs={{0,4},{4,0},{8,12},{12,8},{16,20},{20,16},{24,28},{28,24},{1,5},{5... | collective-permute-start | bytes 393224 | tf_op jit(solution)/shard_map/ppermute | solution.py:20
  33.5 2.5 %collective-permute-done.7.got_ref = bf16[128,512]{1,0:T(8,128)(2,1)S(1)} collective-permute-done((bf16[128,512]{1,0:T(8,128)(2,1)S(1)}, bf16[128,512]{1,0:T(8,128)(2,1)S(1)}, u32[]{:S(2)}, u32[]{:S(2)}) %collective-permute-start.7) | collective-permute-done | bytes 131104 | tf_op jit(solution)/shard_map/ppermute | solution.py:20
  36.1 1.4 %collective-permute-done.8.got_ref = bf16[128,512]{1,0:T(8,128)(2,1)S(1)} collective-permute-done((bf16[128,512]{1,0:T(8,128)(2,1)S(1)}, bf16[128,512]{1,0:T(8,128)(2,1)S(1)}, u32[]{:S(2)}, u32[]{:S(2)}) %collective-permute-start.8) | collective-permute-done | bytes 131104 | tf_op jit(solution)/shard_map/ppermute | solution.py:20
  37.4 0.2 shard_map.82
  37.6 0.0 collective-permute-start.11
  37.6 1.6 %collective-permute-start.10 = (f32[1,128]{1,0:T(1,128)S(1)}, f32[1,128]{1,0:T(1,128)S(1)}, u32[]{:S(2)}, u32[]{:S(2)}) collective-permute-start(f32[1,128]{1,0:T(1,128)S(1)} %get-tuple-element.60.refs_4_), channel_id=1, source_target_pairs={{0,2},{1,3},{2,0},{3,1},{4,6},{5,7},{6,4},{7,5},{8,10},{9,11},{10,... | collective-permute-start | bytes 1544 | tf_op jit(solution)/shard_map/ppermute | solution.py:514
  39.2 0.3 collective-permute-start.9
  39.5 1.1 %collective-permute-done.11.refs_7_ = f32[1,128]{1,0:T(1,128)S(1)} collective-permute-done((f32[1,128]{1,0:T(1,128)S(1)}, f32[1,128]{1,0:T(1,128)S(1)}, u32[]{:S(2)}, u32[]{:S(2)}) %collective-permute-start.11) | collective-permute-done | bytes 544 | tf_op jit(solution)/shard_map/ppermute | solution.py:514
  40.6 0.6 %collective-permute-done.10.refs_6_ = f32[1,128]{1,0:T(1,128)S(1)} collective-permute-done((f32[1,128]{1,0:T(1,128)S(1)}, f32[1,128]{1,0:T(1,128)S(1)}, u32[]{:S(2)}, u32[]{:S(2)}) %collective-permute-start.10) | collective-permute-done | bytes 544 | tf_op jit(solution)/shard_map/ppermute | solution.py:514
  41.2 0.0 collective-permute-done.9.refs_5_
  41.2 0.0 copy-done.4
  41.2 1.0 %shard_map.83 = bf16[128,2048]{1,0:T(8,128)(2,1)} custom-call(f32[128,512]{1,0:T(8,128)S(1)} %get-tuple-element.50.refs_0_, f32[128,512]{1,0:T(8,128)S(1)} %get-tuple-element.53.refs_1_, f32[128,512]{1,0:T(8,128)S(1)} %get-tuple-element.55.refs_2_, f32[128,512]{1,0:T(8,128)S(1)} %get-tuple-element.59.refs_3_, f32[1,128]{1,0:T(1,128)S(1)} %get-tuple-element.60.refs_4_, ...), custom_call_target="tpu_custom_call" | custom-call | flops 1048576 | bytes 1310720 | tf_op jit(solution)/shard_map/pallas_call | solution.py:516
  (4 shorter events, 0.1 us)
Async XLA Ops:
  0.0 13.2 %copy-start.2 = (s32[32]{0:T(128)S(1)}, s32[32]{0:T(128)}, u32[]{:S(2)}) copy-start(s32[32]{0:T(128)} %seq_ref.9) | copy-start | bytes 388
  0.0 13.2 %copy-start = (f32[3,3,2048]{2,1,0:T(4,128)S(1)}, f32[3,3,2048]{2,1,0:T(4,128)}, u32[]{:S(2)}) copy-start(f32[3,3,2048]{2,1,0:T(4,128)} %w_ref.1) | copy-start | bytes 221188
  0.0 3.7 %copy-start.5 = (f32[16,512]{1,0:T(8,128)S(1)}, f32[16,512]{1,0:T(8,128)}, u32[]{:S(2)}) copy-start(f32[16,512]{1,0:T(8,128)} %param.9) | copy-start | bytes 98308
  3.7 7.6 %collective-permute-start.2 = (bf16[144,512]{1,0:T(8,128)(2,1)}, bf16[144,512]{1,0:T(8,128)(2,1)S(1)}, u32[]{:S(2)}, u32[]{:S(2)}) collective-permute-start(bf16[144,512]{1,0:T(8,128)(2,1)} %get-tuple-element.42), channel_id=1, source_target_pairs={{0,4},{4,0},{8,12},{12,8},{16,20},{20,16},{24,28},{28,24},{1,5},{5... | collective-permute-start | bytes 442376 | tf_op jit(solution)/shard_map/ppermute | solution.py:20
  6.8 15.1 %collective-permute-start.1 = (bf16[144,1024]{1,0:T(8,128)(2,1)}, bf16[144,1024]{1,0:T(8,128)(2,1)S(1)}, u32[]{:S(2)}, u32[]{:S(2)}) collective-permute-start(bf16[144,1024]{1,0:T(8,128)(2,1)} %get-tuple-element.33.own_ref), channel_id=1, source_target_pairs={{0,8},{4,12},{8,16},{12,20},{16,24},{20,28},{24,0},{28,4},{1,9},{5... | collective-permute-start | bytes 884744 | tf_op jit(solution)/shard_map/ppermute | solution.py:20
  8.4 7.7 %collective-permute-start = (bf16[144,512]{1,0:T(8,128)(2,1)}, bf16[144,512]{1,0:T(8,128)(2,1)S(1)}, u32[]{:S(2)}, u32[]{:S(2)}) collective-permute-start(bf16[144,512]{1,0:T(8,128)(2,1)} %get-tuple-element.40), channel_id=1, source_target_pairs={{0,4},{4,0},{8,12},{12,8},{16,20},{20,16},{24,28},{28,24},{1,5},{5... | collective-permute-start | bytes 442376 | tf_op jit(solution)/shard_map/ppermute | solution.py:20
  11.3 10.5 %collective-permute-start.3 = (bf16[144,512]{1,0:T(8,128)(2,1)S(1)}, bf16[144,512]{1,0:T(8,128)(2,1)S(1)}, u32[]{:S(2)}, u32[]{:S(2)}) collective-permute-start(bf16[144,512]{1,0:T(8,128)(2,1)S(1)} %collective-permute-done.2.pair_a_ref), channel_id=1, source_target_pairs={{0,8},{4,12},{8,16},{12,20},{16,24},{20,28},{24,0},{28,4},{1,9},{5... | collective-permute-start | bytes 442376 | tf_op jit(solution)/shard_map/ppermute | solution.py:20
  16.0 8.7 %collective-permute-start.4 = (bf16[144,512]{1,0:T(8,128)(2,1)S(1)}, bf16[144,512]{1,0:T(8,128)(2,1)S(1)}, u32[]{:S(2)}, u32[]{:S(2)}) collective-permute-start(bf16[144,512]{1,0:T(8,128)(2,1)S(1)} %collective-permute-done.pair_b_ref), channel_id=1, source_target_pairs={{0,8},{4,12},{8,16},{12,20},{16,24},{20,28},{24,0},{28,4},{1,9},{5... | collective-permute-start | bytes 442376 | tf_op jit(solution)/shard_map/ppermute | solution.py:20
  22.6 8.0 %collective-permute-start.5 = (bf16[144,512]{1,0:T(8,128)(2,1)S(1)}, bf16[144,512]{1,0:T(8,128)(2,1)S(1)}, u32[]{:S(2)}, u32[]{:S(2)}) collective-permute-start(bf16[144,512]{1,0:T(8,128)(2,1)S(1)} %shard_map.77), channel_id=1, source_target_pairs={{0,4},{4,0},{8,16},{12,20},{16,24},{20,28},{24,8},{28,12},{1,5},{5... | collective-permute-start | bytes 442376 | tf_op jit(solution)/shard_map/ppermute | solution.py:20
  25.4 3.8 %copy-start.1 = (bf16[144,1024]{1,0:T(8,128)(2,1)S(1)}, bf16[144,1024]{1,0:T(8,128)(2,1)}, u32[]{:S(2)}) copy-start(bf16[144,1024]{1,0:T(8,128)(2,1)} %get-tuple-element.33.own_ref) | copy-start | bytes 884740
  25.4 3.8 %copy-start.3 = (f32[2048]{0:T(1024)S(1)}, f32[2048]{0:T(1024)}, u32[]{:S(2)}) copy-start(f32[2048]{0:T(1024)} %param.11) | copy-start | bytes 24580
  25.4 6.2 %collective-permute-start.6 = (bf16[144,512]{1,0:T(8,128)(2,1)S(1)}, bf16[144,512]{1,0:T(8,128)(2,1)S(1)}, u32[]{:S(2)}, u32[]{:S(2)}) collective-permute-start(bf16[144,512]{1,0:T(8,128)(2,1)S(1)} %shard_map.79), channel_id=1, source_target_pairs={{0,4},{4,0},{8,16},{12,20},{16,24},{20,28},{24,8},{28,12},{1,5},{5... | collective-permute-start | bytes 442376 | tf_op jit(solution)/shard_map/ppermute | solution.py:20
  31.0 5.0 %collective-permute-start.7 = (bf16[128,512]{1,0:T(8,128)(2,1)S(1)}, bf16[128,512]{1,0:T(8,128)(2,1)S(1)}, u32[]{:S(2)}, u32[]{:S(2)}) collective-permute-start(bf16[128,512]{1,0:T(8,128)(2,1)S(1)} %get-tuple-element.54), channel_id=1, source_target_pairs={{0,4},{4,0},{8,12},{12,8},{16,20},{20,16},{24,28},{28,24},{1,5},{5... | collective-permute-start | bytes 393224 | tf_op jit(solution)/shard_map/ppermute | solution.py:20
  32.0 9.3 %copy-start.4 = (f32[2048]{0:T(1024)S(1)}, f32[2048]{0:T(1024)}, u32[]{:S(2)}) copy-start(f32[2048]{0:T(1024)} %param.12) | copy-start | bytes 24580
  32.0 5.4 %collective-permute-start.8 = (bf16[128,512]{1,0:T(8,128)(2,1)S(1)}, bf16[128,512]{1,0:T(8,128)(2,1)S(1)}, u32[]{:S(2)}, u32[]{:S(2)}) collective-permute-start(bf16[128,512]{1,0:T(8,128)(2,1)S(1)} %get-tuple-element.56), channel_id=1, source_target_pairs={{0,4},{4,0},{8,12},{12,8},{16,20},{20,16},{24,28},{28,24},{1,5},{5... | collective-permute-start | bytes 393224 | tf_op jit(solution)/shard_map/ppermute | solution.py:20
  37.6 3.0 %collective-permute-start.11 = (f32[1,128]{1,0:T(1,128)S(1)}, f32[1,128]{1,0:T(1,128)S(1)}, u32[]{:S(2)}, u32[]{:S(2)}) collective-permute-start(f32[1,128]{1,0:T(1,128)S(1)} %get-tuple-element.60.refs_4_), channel_id=1, source_target_pairs={{0,3},{1,2},{2,1},{3,0},{4,7},{5,6},{6,5},{7,4},{8,11},{9,10},{10,... | collective-permute-start | bytes 1544 | tf_op jit(solution)/shard_map/ppermute | solution.py:514
  37.6 3.6 %collective-permute-start.10 = (f32[1,128]{1,0:T(1,128)S(1)}, f32[1,128]{1,0:T(1,128)S(1)}, u32[]{:S(2)}, u32[]{:S(2)}) collective-permute-start(f32[1,128]{1,0:T(1,128)S(1)} %get-tuple-element.60.refs_4_), channel_id=1, source_target_pairs={{0,2},{1,3},{2,0},{3,1},{4,6},{5,7},{6,4},{7,5},{8,10},{9,11},{10,... | collective-permute-start | bytes 1544 | tf_op jit(solution)/shard_map/ppermute | solution.py:514
  39.2 2.1 %collective-permute-start.9 = (f32[1,128]{1,0:T(1,128)S(1)}, f32[1,128]{1,0:T(1,128)S(1)}, u32[]{:S(2)}, u32[]{:S(2)}) collective-permute-start(f32[1,128]{1,0:T(1,128)S(1)} %get-tuple-element.60.refs_4_), channel_id=1, source_target_pairs={{0,1},{1,0},{2,3},{3,2},{4,5},{5,4},{6,7},{7,6},{8,9},{9,8},{10,11... | collective-permute-start | bytes 1544 | tf_op jit(solution)/shard_map/ppermute | solution.py:514

commit v12 on v10

--- a/solution.py
+++ b/solution.py
@@ -96,17 +96,17 @@
             there = slice(base, base + GROUP) if p < pieces // 2 else slice(c, c + GROUP)
             lanes = pl.ds(pl.multiple_of(at + base, GROUP), GROUP)
             slot = (c // GROUP) % (x_ref.shape[0] // 2) * 2
-            heads, tails, made = [], [], []
+            raw, made = [], []
             for i in range(2):
                 x = kv_ref[p, i, :, c : c + GROUP].astype(jnp.float32)
                 x_ref[slot + i, 8:, :] = x
                 made.append(feature(x, x_ref.at[slot + i], w_ref[1 + i, :, lanes], m1_ref, m2_ref))
-                heads.append(x[0:2])
-                tails.append(x[rows - 2 :])
-            out_ref[:rows, there] = (made[0] * made[1]).astype(out_ref.dtype)
-            tails.append(q_ref[:, lanes].astype(jnp.float32)[14:])
-            extra = jnp.concatenate(heads + tails + [jnp.zeros((6, GROUP), jnp.float32)], 0)
-            out_ref[rows:, there] = extra.astype(out_ref.dtype)
+                raw.append(x)
+            product = made[0] * made[1]
+            top = jnp.where(lax.broadcasted_iota(jnp.int32, (8, GROUP), 0) < 2, raw[0][:8], product[:8])
+            out_ref[:rows, there] = jnp.concatenate([top, product[8:]], 0).astype(out_ref.dtype)
+            tails = [x[rows - 2 :] for x in raw] + [q_ref[:, lanes].astype(jnp.float32)[14:]]
+            out_ref[rows:, there] = jnp.concatenate([raw[1][0:2]] + tails, 0).astype(out_ref.dtype)
 
 
 def edge_marks(seq_ref):
@@ -120,12 +120,11 @@
 
 def first_rows(now, ahead, w_ref, marks, spot, lanes=slice(None)):
     m1, m2 = [mark[:, spot : spot + 1] for mark in marks]
-    top = lax.broadcasted_iota(jnp.int32, now.shape, 0) == 0
+    top = lax.broadcasted_iota(jnp.int32, ahead.shape, 0) == 0
     made = []
-    for i in range(2):
-        x0 = pltpu.roll(now, (8 - 2 * i) % 8, 0) if i else now
-        x1 = jnp.where(top, pltpu.roll(ahead, 3 - 2 * i, 0), pltpu.roll(now, (9 - 2 * i) % 8, 0))
-        x2 = pltpu.roll(ahead, 4 - 2 * i, 0)
+    for i, x0 in enumerate((now[8:], now[:8])):
+        x1 = jnp.where(top, pltpu.roll(ahead, 5 - 2 * i, 0), pltpu.roll(x0, 1, 0))
+        x2 = pltpu.roll(ahead, 6 - 2 * i, 0)
         w = w_ref[1 + i, :, lanes]
         made.append(w[0:1] * x0 + w[1:2] * x1 * m1 + w[2:3] * x2 * m2)
     return made[0] * made[1]
@@ -189,7 +188,8 @@
     for piece in pieces:
         lanes = slice(at, at + piece.shape[1])
         win_ref[pl.ds(pl.multiple_of(spot * BLK, BLK), BLK), lanes] = piece[:BLK]
-        extra_ref[spot, :, lanes] = piece[BLK:].astype(jnp.float32)
+        extra_ref[spot, :8, lanes] = piece[BLK:].astype(jnp.float32)
+        extra_ref[spot, 8:, lanes] = piece[:16].astype(jnp.float32)[:8]
         at += piece.shape[1]
 
 
@@ -200,9 +200,9 @@
     fill(win_ref, extra_ref, half, back_own_ref.at[:, lanes])
     fill(win_ref, extra_ref, 1 - half, back_pair_ref)
     marks = edge_marks(seq_ref)
-    rows = first_rows(extra_ref[1, :8], extra_ref[0, :8], w_ref, marks, 3, lanes)
-    put_first_rows(win_ref, BLK, rows)
-    out_ref[BLK:] = extra_ref[1].astype(out_ref.dtype)
+    put_first_rows(win_ref, 0, first_rows(extra_ref[0], jnp.zeros((8, width), jnp.float32), w_ref, marks, 2, lanes))
+    put_first_rows(win_ref, BLK, first_rows(extra_ref[1], extra_ref[0, :8], w_ref, marks, 3, lanes))
+    out_ref[BLK:] = extra_ref[1, :8].astype(out_ref.dtype)
     summed = reaches_past(seq_ref, lax.axis_index("blk") + 1)
 
     @pl.when(summed)
@@ -249,7 +249,7 @@
     marks_ref[0], marks_ref[1] = marks
     marks_ref[2] = jnp.full((8, GROUP), reaches_past(seq_ref, block).astype(jnp.float32))
     for spot in (1, 2, 3):
-        rows = first_rows(extra_ref[spot, :8], extra_ref[spot - 1, :8], w_ref, marks, spot + 2)
+        rows = first_rows(extra_ref[spot], extra_ref[spot - 1, :8], w_ref, marks, spot + 2)
         put_first_rows(win_ref, spot * BLK, rows)
     for g in range(groups):
         lanes = slice(g * GROUP, (g + 1) * GROUP)
@@ -263,7 +263,7 @@
             here = win_ref[(2 + part) * BLK : (3 + part) * BLK, lanes].astype(jnp.float32)
             acc_ref[part * BLK : (part + 1) * BLK, lanes] = total + bias * here
     gate_rows(
-        seq_ref, qkept_ref, lambda lanes: extra_ref[1 + half, 8:10, lanes], w_ref, half, q_ref, x_ref, m1_ref, m2_ref
+        seq_ref, qkept_ref, lambda lanes: extra_ref[1 + half, 6:8, lanes], w_ref, half, q_ref, x_ref, m1_ref, m2_ref
     )
 
 
@@ -273,7 +273,7 @@
     def tail(lanes):
         back = back_own_ref[BLK:, lanes].astype(jnp.float32)
         own = own_ref[BLK:, lanes].astype(jnp.float32)
-        return jnp.where(half == 1, back, own)[8:10]
+        return jnp.where(half == 1, back, own)[6:8]
 
     gate_rows(seq_ref, raw_ref, tail, w_ref, 1 - half, q_ref, x_ref, m1_ref, m2_ref)
 
@@ -296,11 +296,11 @@
     else:
         fill(win_ref, extra_ref, half, far_refs[0])
         fill(win_ref, extra_ref, 1 - half, far_refs[1], far_refs[2])
-        ahead = far_refs[3][...].astype(jnp.float32)[:8]
-        put_first_rows(win_ref, 0, first_rows(extra_ref[0, :8], ahead, w_ref, marks, 0))
-        rows = first_rows(extra_ref[1, :8], extra_ref[0, :8], w_ref, marks, 1)
+        ahead = far_refs[3][...].astype(jnp.float32)
+        put_first_rows(win_ref, 0, first_rows(extra_ref[0], ahead, w_ref, marks, 0))
+        rows = first_rows(extra_ref[1], extra_ref[0, :8], w_ref, marks, 1)
         put_first_rows(win_ref, BLK, rows)
-    rows = first_rows(extra_ref[2, :8], extra_ref[1, :8], w_ref, marks, 2)
+    rows = first_rows(extra_ref[2], extra_ref[1, :8], w_ref, marks, 2)
     put_first_rows(win_ref, 2 * BLK, rows)
     for at, part, q_ref, out_ref in ((0, half, qown_ref, kept_ref), (BLK, 1 - half, qpair_ref, sent_ref)):
         squares = jnp.zeros((BLK, GROUP), jnp.float32)
@@ -372,8 +372,8 @@
     ahead = [(i, (i + 2) % (2 * blocks)) for i in spots]
 
     panels = jnp.transpose(projected, (1, 0, 2))
-    message = shape((rows + 16, width), jnp.bfloat16)
-    small = shape((rows + 16, width // 2), jnp.bfloat16)
+    message = shape((rows + 8, width), jnp.bfloat16)
+    small = shape((rows + 8, width // 2), jnp.bfloat16)
     hbm = pl.BlockSpec(memory_space=pltpu.HBM)
     pieces = 4
     row_mask = pltpu.VMEM((rows, GROUP), jnp.float32)
@@ -418,7 +418,7 @@
     table, table_next, pair[0] = lax.optimization_barrier((table, table_next, pair[0]))
 
     half = lax.axis_index("half")
-    query, _ = lax.optimization_barrier((panels, pair[0]))
+    query, _, back_own = lax.optimization_barrier((panels, pair[0], back_own))
     qkept = lax.dynamic_slice(query, (0, 0, half * width), (1, rows, width))[0]
     qsent = lax.dynamic_slice(query, (0, 0, (1 - half) * width), (1, rows, width))[0]
     qkept, qsent, pair[1] = lax.optimization_barrier((qkept, qsent, pair[1]))

time: 39.8 us -> 41.1 us (1.033)
  starting transfers between devices: 15.1 us -> 16 us
    ppermute x10, starting transfers between devices: 13.2 us -> 14.2 us  [moved(): return lax.ppermute(block, SPOTS, pairs)]
  transfers between devices with their start and end apart: 13 -> 13, of which waited for: 8 -> 8; matrix products, arithmetic and copies ran while one was open for 3% -> 3% of each run, Pallas kernels for 17% -> 16%
where the time goes in v12:
time: 41.1 us; the launch traced here: 40.9 us
  starting transfers between devices  16 us (39%)
  waiting for transfers between devices  11.8 us (29%)
  Pallas kernels  11.7 us (28%)
  local copies, waits for them, and re-layouts  1.25 us (3%)
    ppermute x10, starting transfers between devices, moved(): return lax.ppermute(block, SPOTS, pairs)  14.2 us
    ppermute x10, waiting for transfers between devices, moved(): return lax.ppermute(block, SPOTS, pairs)  10.1 us
    pallas_call x1, Pallas kernels, shards(): kernel_call(products_kernel, (message, small, small), [hbm] * 3, [pltpu.S...  2.88 us
    pallas_call x1, Pallas kernels, shards(): kernel_call(tables_kernel, (shape((groups, 2, BLK, span), jnp.bfloat16),...  2.81 us
    ppermute x3, starting transfers between devices, shards(): lax.ppermute(power, 'mp', [(i, i ^ k) for i in range(peers)])  1.86 us
    ppermute x3, waiting for transfers between devices, shards(): lax.ppermute(power, 'mp', [(i, i ^ k) for i in range(peers)])  1.74 us
    pallas_call x1, Pallas kernels, shards(): kernel_call(near_kernel, (shape((2 * rows, width), jnp.float32), half_wid...  1.53 us
    pallas_call x2, Pallas kernels, shards(): kernel_call(functools.partial(relay_kernel, piece), small, [SMEM] + [VMEM...  1.37 us
  transfers between devices with their start and end apart: 13, of which 8 were waited for; matrix products, arithmetic and copies ran while one was open for 3% of the time, Pallas kernels for 16%

profile of v12, /device:TPU:0, one launch (start us, length us, event | category | flops | bytes accessed | tf_op | source)
XLA Modules:
  0.0 40.9 jit_solution(14244604687949124516)
XLA Ops:
  0.0 0.0 copy-start.2
  0.0 0.0 copy-start.5
  0.0 0.0 copy-start.6
  0.0 2.9 %shard_map.73 = (bf16[136,1024]{1,0:T(8,128)(2,1)}, bf16[136,512]{1,0:T(8,128)(2,1)}, bf16[136,512]{1,0:T(8,128)(2,1)}) custom-call(s32[32]{0:T(128)} %seq_ref.9, bf16[3,128,2048]{2,1,0:T(8,128)(2,1)} %bitcast.14, f32[3,3,2048]{2,1,0:T(4,128)} %w_ref.1), custom_call_target="tpu_custom_call" | custom-call | flops 5242880 | bytes 2097152 | tf_op jit(solution)/shard_map/pallas_call | solution.py:381
  2.9 3.1 %collective-permute-start.1 = (bf16[136,1024]{1,0:T(8,128)(2,1)}, bf16[136,1024]{1,0:T(8,128)(2,1)S(1)}, u32[]{:S(2)}, u32[]{:S(2)}) collective-permute-start(bf16[136,1024]{1,0:T(8,128)(2,1)} %get-tuple-element.26.own_ref), channel_id=1, source_target_pairs={{0,8},{4,12},{8,16},{12,20},{16,24},{20,28},{24,0},{28,4},{1,9},{5... | collective-permute-start | bytes 835592 | tf_op jit(solution)/shard_map/ppermute | solution.py:20
  6.0 1.5 %collective-permute-start = (bf16[136,512]{1,0:T(8,128)(2,1)}, bf16[136,512]{1,0:T(8,128)(2,1)S(1)}, u32[]{:S(2)}, u32[]{:S(2)}) collective-permute-start(bf16[136,512]{1,0:T(8,128)(2,1)} %get-tuple-element.30), channel_id=1, source_target_pairs={{0,4},{4,0},{8,12},{12,8},{16,20},{20,16},{24,28},{28,24},{1,5},{5... | collective-permute-start | bytes 417800 | tf_op jit(solution)/shard_map/ppermute | solution.py:20
  7.5 0.5 %collective-permute-start.2 = (bf16[136,512]{1,0:T(8,128)(2,1)}, bf16[136,512]{1,0:T(8,128)(2,1)S(1)}, u32[]{:S(2)}, u32[]{:S(2)}) collective-permute-start(bf16[136,512]{1,0:T(8,128)(2,1)} %get-tuple-element.35), channel_id=1, source_target_pairs={{0,4},{4,0},{8,12},{12,8},{16,20},{20,16},{24,28},{28,24},{1,5},{5... | collective-permute-start | bytes 417800 | tf_op jit(solution)/shard_map/ppermute | solution.py:20
  8.0 0.0 copy-done.6
  8.0 0.1 copy.8
  8.1 0.1 broadcast_in_dim.3
  8.2 0.0 copy-done.5
  8.2 0.0 copy-done.2
  8.2 0.0 copy-done.1
  8.2 2.8 %shard_map.74 = (bf16[8,2,128,768]{3,2,1,0:T(8,128)(2,1)S(1)}, bf16[8,128,256]{2,1,0:T(8,128)(2,1)S(1)}, f32[3,3,1024]{2,1,0:T(4,128)S(1)}) custom-call(s32[32]{0:T(128)S(1)} %copy-done.2, bf16[16,512]{1,0:T(8,128)(2,1)S(1)} %fusion.taps_ref, f32[3,3,2048]{2,1,0:T(4,128)S(1)} %copy-done.1), custom_call_target="tpu_custom_call" | custom-call | flops 20971520 | bytes 4194304 | tf_op jit(solution)/shard_map/pallas_call | solution.py:406
  11.0 1.7 %collective-permute-done.pair_a_ref = bf16[136,512]{1,0:T(8,128)(2,1)S(1)} collective-permute-done((bf16[136,512]{1,0:T(8,128)(2,1)}, bf16[136,512]{1,0:T(8,128)(2,1)S(1)}, u32[]{:S(2)}, u32[]{:S(2)}) %collective-permute-start) | collective-permute-done | bytes 139296 | tf_op jit(solution)/shard_map/ppermute | solution.py:20
  12.8 0.0 copy-start
  12.8 1.6 %collective-permute-start.3 = (bf16[136,512]{1,0:T(8,128)(2,1)S(1)}, bf16[136,512]{1,0:T(8,128)(2,1)S(1)}, u32[]{:S(2)}, u32[]{:S(2)}) collective-permute-start(bf16[136,512]{1,0:T(8,128)(2,1)S(1)} %collective-permute-done.pair_a_ref), channel_id=1, source_target_pairs={{0,8},{4,12},{8,16},{12,20},{16,24},{20,28},{24,0},{28,4},{1,9},{5... | collective-permute-start | bytes 417800 | tf_op jit(solution)/shard_map/ppermute | solution.py:20
  14.4 0.8 %collective-permute-done.1.back_own_ref.refs_0_ = bf16[136,1024]{1,0:T(8,128)(2,1)S(1)} collective-permute-done((bf16[136,1024]{1,0:T(8,128)(2,1)}, bf16[136,1024]{1,0:T(8,128)(2,1)S(1)}, u32[]{:S(2)}, u32[]{:S(2)}) %collective-permute-start.1) | collective-permute-done | bytes 278560 | tf_op jit(solution)/shard_map/ppermute | solution.py:20
  15.2 1.1 %dynamic-slice_bitcast_fusion = (bf16[128,1024]{1,0:T(8,128)(2,1)S(1)}, bf16[128,1024]{1,0:T(8,128)(2,1)S(1)}) fusion(bf16[3,128,2048]{2,1,0:T(8,128)(2,1)} %bitcast.15, s32[]{:T(128)S(6)} %select_n.7, s32[]{:T(128)S(6)} %select_n.6), kind=kLoop, calls=%fused_computation | loop fusion | bytes 1048584 | tf_op jit(solution)/shard_map/squeeze | solution.py:423
  16.2 0.0 collective-permute-done.2.pair_b_ref
  16.2 0.8 %collective-permute-start.4 = (bf16[136,512]{1,0:T(8,128)(2,1)S(1)}, bf16[136,512]{1,0:T(8,128)(2,1)S(1)}, u32[]{:S(2)}, u32[]{:S(2)}) collective-permute-start(bf16[136,512]{1,0:T(8,128)(2,1)S(1)} %collective-permute-done.2.pair_b_ref), channel_id=1, source_target_pairs={{0,8},{4,12},{8,16},{12,20},{16,24},{20,28},{24,0},{28,4},{1,9},{5... | collective-permute-start | bytes 417800 | tf_op jit(solution)/shard_map/ppermute | solution.py:20
  17.1 1.5 %collective-permute-start.5 = (bf16[128,1024]{1,0:T(8,128)(2,1)S(1)}, bf16[128,1024]{1,0:T(8,128)(2,1)S(1)}, u32[]{:S(2)}, u32[]{:S(2)}) collective-permute-start(bf16[128,1024]{1,0:T(8,128)(2,1)S(1)} %get-tuple-element.41), channel_id=1, source_target_pairs={{0,4},{4,0},{8,12},{12,8},{16,20},{20,16},{24,28},{28,24},{1,5},{5... | collective-permute-start | bytes 786440 | tf_op jit(solution)/shard_map/ppermute | solution.py:20
  18.6 1.0 %collective-permute-done.3.back_a_ref.back_pair_ref.refs_1_ = bf16[136,512]{1,0:T(8,128)(2,1)S(1)} collective-permute-done((bf16[136,512]{1,0:T(8,128)(2,1)S(1)}, bf16[136,512]{1,0:T(8,128)(2,1)S(1)}, u32[]{:S(2)}, u32[]{:S(2)}) %collective-permute-start.3) | collective-permute-done | bytes 139296 | tf_op jit(solution)/shard_map/ppermute | solution.py:20
  19.6 0.7 %shard_map.77 = bf16[136,512]{1,0:T(8,128)(2,1)S(1)} custom-call(s32[32]{0:T(128)S(1)} %copy-done.2, bf16[8,128,256]{2,1,0:T(8,128)(2,1)S(1)} %get-tuple-element.43.next_ref, bf16[136,1024]{1,0:T(8,128)(2,1)S(1)} %collective-permute-done.1.back_own_ref.refs_0_, bf16[136,512]{1,0:T(8,128)(2,1)S(1)} %collective-permute-done.3.back_a_ref.back_pair_ref.refs_1_, ...), custom_call_target="tpu_custom_call" | custom-call | flops 33554432 | bytes 524288 | tf_op jit(solution)/shard_map/pallas_call | solution.py:436
  20.3 1.7 %collective-permute-start.6 = (bf16[136,512]{1,0:T(8,128)(2,1)S(1)}, bf16[136,512]{1,0:T(8,128)(2,1)S(1)}, u32[]{:S(2)}, u32[]{:S(2)}) collective-permute-start(bf16[136,512]{1,0:T(8,128)(2,1)S(1)} %shard_map.77), channel_id=1, source_target_pairs={{0,4},{4,0},{8,16},{12,20},{16,24},{20,28},{24,8},{28,12},{1,5},{5... | collective-permute-start | bytes 417800 | tf_op jit(solution)/shard_map/ppermute | solution.py:20
  22.1 2.3 %collective-permute-done.4.back_b_ref.back_pair_ref.refs_2_ = bf16[136,512]{1,0:T(8,128)(2,1)S(1)} collective-permute-done((bf16[136,512]{1,0:T(8,128)(2,1)S(1)}, bf16[136,512]{1,0:T(8,128)(2,1)S(1)}, u32[]{:S(2)}, u32[]{:S(2)}) %collective-permute-start.4) | collective-permute-done | bytes 139296 | tf_op jit(solution)/shard_map/ppermute | solution.py:20
  24.4 0.7 %shard_map.78 = bf16[136,512]{1,0:T(8,128)(2,1)S(1)} custom-call(s32[32]{0:T(128)S(1)} %copy-done.2, bf16[8,128,256]{2,1,0:T(8,128)(2,1)S(1)} %get-tuple-element.43.next_ref, bf16[136,1024]{1,0:T(8,128)(2,1)S(1)} %collective-permute-done.1.back_own_ref.refs_0_, bf16[136,512]{1,0:T(8,128)(2,1)S(1)} %collective-permute-done.4.back_b_ref.back_pair_ref.refs_2_, ...), custom_call_target="tpu_custom_call" | custom-call | flops 33554432 | bytes 524288 | tf_op jit(solution)/shard_map/pallas_call | solution.py:436
  25.1 1.3 %collective-permute-start.7 = (bf16[136,512]{1,0:T(8,128)(2,1)S(1)}, bf16[136,512]{1,0:T(8,128)(2,1)S(1)}, u32[]{:S(2)}, u32[]{:S(2)}) collective-permute-start(bf16[136,512]{1,0:T(8,128)(2,1)S(1)} %shard_map.78), channel_id=1, source_target_pairs={{0,4},{4,0},{8,16},{12,20},{16,24},{20,28},{24,8},{28,12},{1,5},{5... | collective-permute-start | bytes 417800 | tf_op jit(solution)/shard_map/ppermute | solution.py:20
  26.4 0.0 copy-done
  26.4 0.0 copy-done.3
  26.4 1.5 %shard_map.75 = (f32[256,1024]{1,0:T(8,128)S(1)}, f32[128,1024]{1,0:T(8,128)S(1)}, f32[3,8,128]{2,1,0:T(8,128)S(1)}) custom-call(s32[32]{0:T(128)S(1)} %copy-done.2, bf16[8,2,128,768]{3,2,1,0:T(8,128)(2,1)S(1)} %get-tuple-element.31.table_ref, bf16[136,1024]{1,0:T(8,128)(2,1)S(1)} %copy-done, ...), custom_call_target="tpu_custom_call" | custom-call | flops 167772160 | bytes 2097152 | tf_op jit(solution)/shard_map/pallas_call | solution.py:452
  27.9 0.0 collective-permute-done.5.raw_ref
  27.9 0.9 %shard_map.76.qpair_ref = f32[128,1024]{1,0:T(8,128)S(1)} custom-call(s32[32]{0:T(128)S(1)} %copy-done.2, bf16[128,1024]{1,0:T(8,128)(2,1)S(1)} %collective-permute-done.5.raw_ref, bf16[136,1024]{1,0:T(8,128)(2,1)S(1)} %copy-done, bf16[136,1024]{1,0:T(8,128)(2,1)S(1)} %collective-permute-done.1.back_own_ref.refs_0_, f32[3,3,1024]{2,1,0:T(4,128)S(1)} %get-tuple-element.38.w_ref), custom_call_target="tpu_custom_call" | custom-call | flops 1310720 | bytes 1048576 | tf_op jit(solution)/shard_map/pallas_call | solution.py:461
  28.8 0.0 collective-permute-done.6.refs_3_
  28.8 1.4 %collective-permute-done.7.refs_4_ = bf16[136,512]{1,0:T(8,128)(2,1)S(1)} collective-permute-done((bf16[136,512]{1,0:T(8,128)(2,1)S(1)}, bf16[136,512]{1,0:T(8,128)(2,1)S(1)}, u32[]{:S(2)}, u32[]{:S(2)}) %collective-permute-start.7) | collective-permute-done | bytes 139296 | tf_op jit(solution)/shard_map/ppermute | solution.py:20
  30.2 1.2 %shard_map.79 = (f32[128,1024]{1,0:T(8,128)S(1)}, bf16[128,1024]{1,0:T(8,128)(2,1)S(1)}, f32[1,256]{1,0:T(1,128)S(1)}) custom-call(bf16[8,2,128,768]{3,2,1,0:T(8,128)(2,1)S(1)} %get-tuple-element.31.table_ref, f32[256,1024]{1,0:T(8,128)S(1)} %get-tuple-element.39.acc_ref, f32[128,1024]{1,0:T(8,128)S(1)} %get-tuple-element.40.qown_ref, ...), custom_call_target="tpu_custom_call" | custom-call | flops 167772160 | bytes 3145728 | tf_op jit(solution)/shard_map/pallas_call | solution.py:470
  31.4 1.3 %collective-permute-start.12 = (bf16[128,1024]{1,0:T(8,128)(2,1)S(1)}, bf16[128,1024]{1,0:T(8,128)(2,1)S(1)}, u32[]{:S(2)}, u32[]{:S(2)}) collective-permute-start(bf16[128,1024]{1,0:T(8,128)(2,1)S(1)} %get-tuple-element.46), channel_id=1, source_target_pairs={{0,4},{4,0},{8,12},{12,8},{16,20},{20,16},{24,28},{28,24},{1,5},{5... | collective-permute-start | bytes 786440 | tf_op jit(solution)/shard_map/ppermute | solution.py:20
  32.6 0.0 collective-permute-start.10
  32.6 1.5 %collective-permute-start.9 = (f32[1,256]{1,0:T(1,128)S(1)}, f32[1,256]{1,0:T(1,128)S(1)}, u32[]{:S(2)}, u32[]{:S(2)}) collective-permute-start(f32[1,256]{1,0:T(1,128)S(1)} %get-tuple-element.44), channel_id=1, source_target_pairs={{0,2},{1,3},{2,0},{3,1},{4,6},{5,7},{6,4},{7,5},{8,10},{9,11},{10,... | collective-permute-start | bytes 3080 | tf_op jit(solution)/shard_map/ppermute | solution.py:481
  34.2 0.3 collective-permute-start.8
  34.5 1.1 %collective-permute-done.10 = f32[1,256]{1,0:T(1,128)S(1)} collective-permute-done((f32[1,256]{1,0:T(1,128)S(1)}, f32[1,256]{1,0:T(1,128)S(1)}, u32[]{:S(2)}, u32[]{:S(2)}) %collective-permute-start.10) | collective-permute-done | bytes 1056 | tf_op jit(solution)/shard_map/ppermute | solution.py:481
  35.6 0.6 %collective-permute-done.9 = f32[1,256]{1,0:T(1,128)S(1)} collective-permute-done((f32[1,256]{1,0:T(1,128)S(1)}, f32[1,256]{1,0:T(1,128)S(1)}, u32[]{:S(2)}, u32[]{:S(2)}) %collective-permute-start.9) | collective-permute-done | bytes 1056 | tf_op jit(solution)/shard_map/ppermute | solution.py:481
  36.2 0.0 collective-permute-done.8
  36.2 0.9 %collective-permute-start.11 = (f32[1,256]{1,0:T(1,128)S(1)}, f32[1,256]{1,0:T(1,128)S(1)}, u32[]{:S(2)}, u32[]{:S(2)}) collective-permute-start(f32[1,256]{1,0:T(1,128)S(1)} %add_add_fusion.power_ref), channel_id=1, source_target_pairs={{0,4},{4,0},{8,12},{12,8},{16,20},{20,16},{24,28},{28,24},{1,5},{5... | collective-permute-start | bytes 3080 | tf_op jit(solution)/shard_map/ppermute | solution.py:20
  37.1 2.8 %collective-permute-done.11.power_got_ref = f32[1,256]{1,0:T(1,128)S(1)} collective-permute-done((f32[1,256]{1,0:T(1,128)S(1)}, f32[1,256]{1,0:T(1,128)S(1)}, u32[]{:S(2)}, u32[]{:S(2)}) %collective-permute-start.11) | collective-permute-done | bytes 1056 | tf_op jit(solution)/shard_map/ppermute | solution.py:20
  39.9 0.0 collective-permute-done.12.got_ref
  39.9 0.0 copy-done.4
  39.9 1.0 %shard_map.80 = bf16[128,2048]{1,0:T(8,128)(2,1)} custom-call(f32[1,256]{1,0:T(1,128)S(1)} %add_add_fusion.power_ref, f32[1,256]{1,0:T(1,128)S(1)} %collective-permute-done.11.power_got_ref, f32[128,1024]{1,0:T(8,128)S(1)} %get-tuple-element.45.kept_ref, bf16[128,1024]{1,0:T(8,128)(2,1)S(1)} %collective-permute-done.12.got_ref, f32[1,2048]{1,0:T(1,128)S(1)} %bitcast.13), custom_call_target="tpu_custom_call" | custom-call | flops 1048576 | bytes 1310720 | tf_op jit(solution)/shard_map/pallas_call | solution.py:483
  (6 shorter events, 0.0 us)
Async XLA Ops:
  0.0 8.2 %copy-start.2 = (s32[32]{0:T(128)S(1)}, s32[32]{0:T(128)}, u32[]{:S(2)}) copy-start(s32[32]{0:T(128)} %seq_ref.9) | copy-start | bytes 388
  0.0 8.2 %copy-start.1 = (f32[3,3,2048]{2,1,0:T(4,128)S(1)}, f32[3,3,2048]{2,1,0:T(4,128)}, u32[]{:S(2)}) copy-start(f32[3,3,2048]{2,1,0:T(4,128)} %w_ref.1) | copy-start | bytes 221188
  0.0 8.2 %copy-start.5 = (f32[16,512]{1,0:T(8,128)S(1)}, f32[16,512]{1,0:T(8,128)}, u32[]{:S(2)}) copy-start(f32[16,512]{1,0:T(8,128)} %param.9) | copy-start | bytes 98308
  0.0 8.0 %copy-start.6 = (s32[16,4]{0,1:T(4,128)S(1)}, s32[16,4]{0,1:T(4,128)}, u32[]{:S(2)}) copy-start(s32[16,4]{0,1:T(4,128)} %param.10) | copy-start | bytes 772
  2.9 12.3 %collective-permute-start.1 = (bf16[136,1024]{1,0:T(8,128)(2,1)}, bf16[136,1024]{1,0:T(8,128)(2,1)S(1)}, u32[]{:S(2)}, u32[]{:S(2)}) collective-permute-start(bf16[136,1024]{1,0:T(8,128)(2,1)} %get-tuple-element.26.own_ref), channel_id=1, source_target_pairs={{0,8},{4,12},{8,16},{12,20},{16,24},{20,28},{24,0},{28,4},{1,9},{5... | collective-permute-start | bytes 835592 | tf_op jit(solution)/shard_map/ppermute | solution.py:20
  6.0 6.8 %collective-permute-start = (bf16[136,512]{1,0:T(8,128)(2,1)}, bf16[136,512]{1,0:T(8,128)(2,1)S(1)}, u32[]{:S(2)}, u32[]{:S(2)}) collective-permute-start(bf16[136,512]{1,0:T(8,128)(2,1)} %get-tuple-element.30), channel_id=1, source_target_pairs={{0,4},{4,0},{8,12},{12,8},{16,20},{20,16},{24,28},{28,24},{1,5},{5... | collective-permute-start | bytes 417800 | tf_op jit(solution)/shard_map/ppermute | solution.py:20
  7.5 8.7 %collective-permute-start.2 = (bf16[136,512]{1,0:T(8,128)(2,1)}, bf16[136,512]{1,0:T(8,128)(2,1)S(1)}, u32[]{:S(2)}, u32[]{:S(2)}) collective-permute-start(bf16[136,512]{1,0:T(8,128)(2,1)} %get-tuple-element.35), channel_id=1, source_target_pairs={{0,4},{4,0},{8,12},{12,8},{16,20},{20,16},{24,28},{28,24},{1,5},{5... | collective-permute-start | bytes 417800 | tf_op jit(solution)/shard_map/ppermute | solution.py:20
  12.8 13.6 %copy-start = (bf16[136,1024]{1,0:T(8,128)(2,1)S(1)}, bf16[136,1024]{1,0:T(8,128)(2,1)}, u32[]{:S(2)}) copy-start(bf16[136,1024]{1,0:T(8,128)(2,1)} %get-tuple-element.26.own_ref) | copy-start | bytes 835588
  12.8 13.6 %copy-start.3 = (f32[2048]{0:T(1024)S(1)}, f32[2048]{0:T(1024)}, u32[]{:S(2)}) copy-start(f32[2048]{0:T(1024)} %param.11) | copy-start | bytes 24580
  12.8 6.9 %collective-permute-start.3 = (bf16[136,512]{1,0:T(8,128)(2,1)S(1)}, bf16[136,512]{1,0:T(8,128)(2,1)S(1)}, u32[]{:S(2)}, u32[]{:S(2)}) collective-permute-start(bf16[136,512]{1,0:T(8,128)(2,1)S(1)} %collective-permute-done.pair_a_ref), channel_id=1, source_target_pairs={{0,8},{4,12},{8,16},{12,20},{16,24},{20,28},{24,0},{28,4},{1,9},{5... | collective-permute-start | bytes 417800 | tf_op jit(solution)/shard_map/ppermute | solution.py:20
  16.2 8.2 %collective-permute-start.4 = (bf16[136,512]{1,0:T(8,128)(2,1)S(1)}, bf16[136,512]{1,0:T(8,128)(2,1)S(1)}, u32[]{:S(2)}, u32[]{:S(2)}) collective-permute-start(bf16[136,512]{1,0:T(8,128)(2,1)S(1)} %collective-permute-done.2.pair_b_ref), channel_id=1, source_target_pairs={{0,8},{4,12},{8,16},{12,20},{16,24},{20,28},{24,0},{28,4},{1,9},{5... | collective-permute-start | bytes 417800 | tf_op jit(solution)/shard_map/ppermute | solution.py:20
  17.1 10.8 %collective-permute-start.5 = (bf16[128,1024]{1,0:T(8,128)(2,1)S(1)}, bf16[128,1024]{1,0:T(8,128)(2,1)S(1)}, u32[]{:S(2)}, u32[]{:S(2)}) collective-permute-start(bf16[128,1024]{1,0:T(8,128)(2,1)S(1)} %get-tuple-element.41), channel_id=1, source_target_pairs={{0,4},{4,0},{8,12},{12,8},{16,20},{20,16},{24,28},{28,24},{1,5},{5... | collective-permute-start | bytes 786440 | tf_op jit(solution)/shard_map/ppermute | solution.py:20
  20.3 8.5 %collective-permute-start.6 = (bf16[136,512]{1,0:T(8,128)(2,1)S(1)}, bf16[136,512]{1,0:T(8,128)(2,1)S(1)}, u32[]{:S(2)}, u32[]{:S(2)}) collective-permute-start(bf16[136,512]{1,0:T(8,128)(2,1)S(1)} %shard_map.77), channel_id=1, source_target_pairs={{0,4},{4,0},{8,16},{12,20},{16,24},{20,28},{24,8},{28,12},{1,5},{5... | collective-permute-start | bytes 417800 | tf_op jit(solution)/shard_map/ppermute | solution.py:20
  25.1 5.1 %collective-permute-start.7 = (bf16[136,512]{1,0:T(8,128)(2,1)S(1)}, bf16[136,512]{1,0:T(8,128)(2,1)S(1)}, u32[]{:S(2)}, u32[]{:S(2)}) collective-permute-start(bf16[136,512]{1,0:T(8,128)(2,1)S(1)} %shard_map.78), channel_id=1, source_target_pairs={{0,4},{4,0},{8,16},{12,20},{16,24},{20,28},{24,8},{28,12},{1,5},{5... | collective-permute-start | bytes 417800 | tf_op jit(solution)/shard_map/ppermute | solution.py:20
  30.2 9.7 %copy-start.4 = (f32[2048]{0:T(1024)S(1)}, f32[2048]{0:T(1024)}, u32[]{:S(2)}) copy-start(f32[2048]{0:T(1024)} %param.12) | copy-start | bytes 24580
  31.4 8.5 %collective-permute-start.12 = (bf16[128,1024]{1,0:T(8,128)(2,1)S(1)}, bf16[128,1024]{1,0:T(8,128)(2,1)S(1)}, u32[]{:S(2)}, u32[]{:S(2)}) collective-permute-start(bf16[128,1024]{1,0:T(8,128)(2,1)S(1)} %get-tuple-element.46), channel_id=1, source_target_pairs={{0,4},{4,0},{8,12},{12,8},{16,20},{20,16},{24,28},{28,24},{1,5},{5... | collective-permute-start | bytes 786440 | tf_op jit(solution)/shard_map/ppermute | solution.py:20
  32.6 3.0 %collective-permute-start.10 = (f32[1,256]{1,0:T(1,128)S(1)}, f32[1,256]{1,0:T(1,128)S(1)}, u32[]{:S(2)}, u32[]{:S(2)}) collective-permute-start(f32[1,256]{1,0:T(1,128)S(1)} %get-tuple-element.44), channel_id=1, source_target_pairs={{0,3},{1,2},{2,1},{3,0},{4,7},{5,6},{6,5},{7,4},{8,11},{9,10},{10,... | collective-permute-start | bytes 3080 | tf_op jit(solution)/shard_map/ppermute | solution.py:481
  32.6 3.6 %collective-permute-start.9 = (f32[1,256]{1,0:T(1,128)S(1)}, f32[1,256]{1,0:T(1,128)S(1)}, u32[]{:S(2)}, u32[]{:S(2)}) collective-permute-start(f32[1,256]{1,0:T(1,128)S(1)} %get-tuple-element.44), channel_id=1, source_target_pairs={{0,2},{1,3},{2,0},{3,1},{4,6},{5,7},{6,4},{7,5},{8,10},{9,11},{10,... | collective-permute-start | bytes 3080 | tf_op jit(solution)/shard_map/ppermute | solution.py:481
  34.2 2.1 %collective-permute-start.8 = (f32[1,256]{1,0:T(1,128)S(1)}, f32[1,256]{1,0:T(1,128)S(1)}, u32[]{:S(2)}, u32[]{:S(2)}) collective-permute-start(f32[1,256]{1,0:T(1,128)S(1)} %get-tuple-element.44), channel_id=1, source_target_pairs={{0,1},{1,0},{2,3},{3,2},{4,5},{5,4},{6,7},{7,6},{8,9},{9,8},{10,11... | collective-permute-start | bytes 3080 | tf_op jit(solution)/shard_map/ppermute | solution.py:481
  36.2 3.6 %collective-permute-start.11 = (f32[1,256]{1,0:T(1,128)S(1)}, f32[1,256]{1,0:T(1,128)S(1)}, u32[]{:S(2)}, u32[]{:S(2)}) collective-permute-start(f32[1,256]{1,0:T(1,128)S(1)} %add_add_fusion.power_ref), channel_id=1, source_target_pairs={{0,4},{4,0},{8,12},{12,8},{16,20},{20,16},{24,28},{28,24},{1,5},{5... | collective-permute-start | bytes 3080 | tf_op jit(solution)/shard_map/ppermute | solution.py:20

commit v13 on v12

--- a/solution.py
+++ b/solution.py
@@ -418,7 +418,7 @@
     table, table_next, pair[0] = lax.optimization_barrier((table, table_next, pair[0]))
 
     half = lax.axis_index("half")
-    query, _, back_own = lax.optimization_barrier((panels, pair[0], back_own))
+    query, _ = lax.optimization_barrier((panels, pair[0]))
     qkept = lax.dynamic_slice(query, (0, 0, half * width), (1, rows, width))[0]
     qsent = lax.dynamic_slice(query, (0, 0, (1 - half) * width), (1, rows, width))[0]
     qkept, qsent, pair[1] = lax.optimization_barrier((qkept, qsent, pair[1]))

time: 41.1 us -> 39.2 us (0.954)
  starting transfers between devices: 16 us -> 15 us
  waiting for transfers between devices: 11.8 us -> 11 us
    ppermute x10, starting transfers between devices: 14.2 us -> 13.1 us  [moved(): return lax.ppermute(block, SPOTS, pairs)]
    ppermute x10, waiting for transfers between devices: 10.1 us -> 9.27 us  [moved(): return lax.ppermute(block, SPOTS, pairs)]
  transfers between devices with their start and end apart: 13 -> 13, of which waited for: 8 -> 8; matrix products, arithmetic and copies ran while one was open for 3% -> 3% of each run, Pallas kernels for 16% -> 17%
where the time goes in v13:
time: 39.2 us; the launch traced here: 39 us
  starting transfers between devices  15 us (38%)
  Pallas kernels  11.7 us (30%)
  waiting for transfers between devices  11 us (28%)
  local copies, waits for them, and re-layouts  1.26 us (3%)
    ppermute x10, starting transfers between devices, moved(): return lax.ppermute(block, SPOTS, pairs)  13.1 us
    ppermute x10, waiting for transfers between devices, moved(): return lax.ppermute(block, SPOTS, pairs)  9.27 us
    pallas_call x1, Pallas kernels, shards(): kernel_call(products_kernel, (message, small, small), [hbm] * 3, [pltpu.S...  2.88 us
    pallas_call x1, Pallas kernels, shards(): kernel_call(tables_kernel, (shape((groups, 2, BLK, span), jnp.bfloat16),...  2.8 us
    ppermute x3, starting transfers between devices, shards(): lax.ppermute(power, 'mp', [(i, i ^ k) for i in range(peers)])  1.86 us
    ppermute x3, waiting for transfers between devices, shards(): lax.ppermute(power, 'mp', [(i, i ^ k) for i in range(peers)])  1.74 us
    pallas_call x1, Pallas kernels, shards(): kernel_call(near_kernel, (shape((2 * rows, width), jnp.float32), half_wid...  1.53 us
    pallas_call x2, Pallas kernels, shards(): kernel_call(functools.partial(relay_kernel, piece), small, [SMEM] + [VMEM...  1.37 us
  transfers between devices with their start and end apart: 13, of which 8 were waited for; matrix products, arithmetic and copies ran while one was open for 3% of the time, Pallas kernels for 17%

profile of v13, /device:TPU:0, one launch (start us, length us, event | category | flops | bytes accessed | tf_op | source)
XLA Modules:
  0.0 39.0 jit_solution(566629593440710286)
XLA Ops:
  0.0 0.0 copy-start.2
  0.0 0.0 copy-start.1
  0.0 2.9 %shard_map.73 = (bf16[136,1024]{1,0:T(8,128)(2,1)}, bf16[136,512]{1,0:T(8,128)(2,1)}, bf16[136,512]{1,0:T(8,128)(2,1)}) custom-call(s32[32]{0:T(128)} %seq_ref.9, bf16[3,128,2048]{2,1,0:T(8,128)(2,1)} %bitcast.14, f32[3,3,2048]{2,1,0:T(4,128)} %w_ref.1), custom_call_target="tpu_custom_call" | custom-call | flops 5242880 | bytes 2097152 | tf_op jit(solution)/shard_map/pallas_call | solution.py:381
  2.9 3.0 %collective-permute-start = (bf16[136,512]{1,0:T(8,128)(2,1)}, bf16[136,512]{1,0:T(8,128)(2,1)S(1)}, u32[]{:S(2)}, u32[]{:S(2)}) collective-permute-start(bf16[136,512]{1,0:T(8,128)(2,1)} %get-tuple-element.29), channel_id=1, source_target_pairs={{0,4},{4,0},{8,12},{12,8},{16,20},{20,16},{24,28},{28,24},{1,5},{5... | collective-permute-start | bytes 417800 | tf_op jit(solution)/shard_map/ppermute | solution.py:20
  5.9 1.6 %collective-permute-start.1 = (bf16[136,1024]{1,0:T(8,128)(2,1)}, bf16[136,1024]{1,0:T(8,128)(2,1)S(1)}, u32[]{:S(2)}, u32[]{:S(2)}) collective-permute-start(bf16[136,1024]{1,0:T(8,128)(2,1)} %get-tuple-element.25.own_ref), channel_id=1, source_target_pairs={{0,8},{4,12},{8,16},{12,20},{16,24},{20,28},{24,0},{28,4},{1,9},{5... | collective-permute-start | bytes 835592 | tf_op jit(solution)/shard_map/ppermute | solution.py:20
  7.5 0.5 %collective-permute-start.2 = (bf16[136,512]{1,0:T(8,128)(2,1)}, bf16[136,512]{1,0:T(8,128)(2,1)S(1)}, u32[]{:S(2)}, u32[]{:S(2)}) collective-permute-start(bf16[136,512]{1,0:T(8,128)(2,1)} %get-tuple-element.33), channel_id=1, source_target_pairs={{0,4},{4,0},{8,12},{12,8},{16,20},{20,16},{24,28},{28,24},{1,5},{5... | collective-permute-start | bytes 417800 | tf_op jit(solution)/shard_map/ppermute | solution.py:20
  8.0 0.0 copy-done.6
  8.0 0.1 copy.8
  8.1 0.1 broadcast_in_dim.3
  8.2 0.0 copy-done.5
  8.2 0.0 copy-done.2
  8.2 0.0 copy-done.1
  8.2 2.8 %shard_map.74 = (bf16[8,2,128,768]{3,2,1,0:T(8,128)(2,1)S(1)}, bf16[8,128,256]{2,1,0:T(8,128)(2,1)S(1)}, f32[3,3,1024]{2,1,0:T(4,128)S(1)}) custom-call(s32[32]{0:T(128)S(1)} %copy-done.2, bf16[16,512]{1,0:T(8,128)(2,1)S(1)} %fusion.taps_ref, f32[3,3,2048]{2,1,0:T(4,128)S(1)} %copy-done.1), custom_call_target="tpu_custom_call" | custom-call | flops 20971520 | bytes 4194304 | tf_op jit(solution)/shard_map/pallas_call | solution.py:406
  11.1 0.0 collective-permute-done.pair_a_ref
  11.1 0.0 copy-start
  11.1 0.0 copy-start.3
  11.1 1.6 %collective-permute-start.3 = (bf16[136,512]{1,0:T(8,128)(2,1)S(1)}, bf16[136,512]{1,0:T(8,128)(2,1)S(1)}, u32[]{:S(2)}, u32[]{:S(2)}) collective-permute-start(bf16[136,512]{1,0:T(8,128)(2,1)S(1)} %collective-permute-done.pair_a_ref), channel_id=1, source_target_pairs={{0,8},{4,12},{8,16},{12,20},{16,24},{20,28},{24,0},{28,4},{1,9},{5... | collective-permute-start | bytes 417800 | tf_op jit(solution)/shard_map/ppermute | solution.py:20
  12.7 1.1 %dynamic-slice_bitcast_fusion = (bf16[128,1024]{1,0:T(8,128)(2,1)S(1)}, bf16[128,1024]{1,0:T(8,128)(2,1)S(1)}) fusion(bf16[3,128,2048]{2,1,0:T(8,128)(2,1)} %bitcast.15, s32[]{:T(128)S(6)} %select_n.7, s32[]{:T(128)S(6)} %select_n.6), kind=kLoop, calls=%fused_computation | loop fusion | bytes 1048584 | tf_op jit(solution)/shard_map/squeeze | solution.py:423
  13.8 0.0 collective-permute-done.2.pair_b_ref
  13.8 1.6 %collective-permute-start.4 = (bf16[136,512]{1,0:T(8,128)(2,1)S(1)}, bf16[136,512]{1,0:T(8,128)(2,1)S(1)}, u32[]{:S(2)}, u32[]{:S(2)}) collective-permute-start(bf16[136,512]{1,0:T(8,128)(2,1)S(1)} %collective-permute-done.2.pair_b_ref), channel_id=1, source_target_pairs={{0,8},{4,12},{8,16},{12,20},{16,24},{20,28},{24,0},{28,4},{1,9},{5... | collective-permute-start | bytes 417800 | tf_op jit(solution)/shard_map/ppermute | solution.py:20
  15.4 1.6 %collective-permute-start.5 = (bf16[128,1024]{1,0:T(8,128)(2,1)S(1)}, bf16[128,1024]{1,0:T(8,128)(2,1)S(1)}, u32[]{:S(2)}, u32[]{:S(2)}) collective-permute-start(bf16[128,1024]{1,0:T(8,128)(2,1)S(1)} %get-tuple-element.39), channel_id=1, source_target_pairs={{0,4},{4,0},{8,12},{12,8},{16,20},{20,16},{24,28},{28,24},{1,5},{5... | collective-permute-start | bytes 786440 | tf_op jit(solution)/shard_map/ppermute | solution.py:20
  17.0 0.5 %collective-permute-done.1.back_own_ref.refs_0_ = bf16[136,1024]{1,0:T(8,128)(2,1)S(1)} collective-permute-done((bf16[136,1024]{1,0:T(8,128)(2,1)}, bf16[136,1024]{1,0:T(8,128)(2,1)S(1)}, u32[]{:S(2)}, u32[]{:S(2)}) %collective-permute-start.1) | collective-permute-done | bytes 278560 | tf_op jit(solution)/shard_map/ppermute | solution.py:20
  17.5 3.0 %collective-permute-done.3.back_a_ref.back_pair_ref.refs_1_ = bf16[136,512]{1,0:T(8,128)(2,1)S(1)} collective-permute-done((bf16[136,512]{1,0:T(8,128)(2,1)S(1)}, bf16[136,512]{1,0:T(8,128)(2,1)S(1)}, u32[]{:S(2)}, u32[]{:S(2)}) %collective-permute-start.3) | collective-permute-done | bytes 139296 | tf_op jit(solution)/shard_map/ppermute | solution.py:20
  20.5 0.7 %shard_map.77 = bf16[136,512]{1,0:T(8,128)(2,1)S(1)} custom-call(s32[32]{0:T(128)S(1)} %copy-done.2, bf16[8,128,256]{2,1,0:T(8,128)(2,1)S(1)} %get-tuple-element.41.next_ref, bf16[136,1024]{1,0:T(8,128)(2,1)S(1)} %collective-permute-done.1.back_own_ref.refs_0_, bf16[136,512]{1,0:T(8,128)(2,1)S(1)} %collective-permute-done.3.back_a_ref.back_pair_ref.refs_1_, ...), custom_call_target="tpu_custom_call" | custom-call | flops 33554432 | bytes 524288 | tf_op jit(solution)/shard_map/pallas_call | solution.py:436
  21.2 0.4 collective-permute-start.6
  21.6 1.4 %collective-permute-done.4.back_b_ref.back_pair_ref.refs_2_ = bf16[136,512]{1,0:T(8,128)(2,1)S(1)} collective-permute-done((bf16[136,512]{1,0:T(8,128)(2,1)S(1)}, bf16[136,512]{1,0:T(8,128)(2,1)S(1)}, u32[]{:S(2)}, u32[]{:S(2)}) %collective-permute-start.4) | collective-permute-done | bytes 139296 | tf_op jit(solution)/shard_map/ppermute | solution.py:20
  23.0 0.7 %shard_map.78 = bf16[136,512]{1,0:T(8,128)(2,1)S(1)} custom-call(s32[32]{0:T(128)S(1)} %copy-done.2, bf16[8,128,256]{2,1,0:T(8,128)(2,1)S(1)} %get-tuple-element.41.next_ref, bf16[136,1024]{1,0:T(8,128)(2,1)S(1)} %collective-permute-done.1.back_own_ref.refs_0_, bf16[136,512]{1,0:T(8,128)(2,1)S(1)} %collective-permute-done.4.back_b_ref.back_pair_ref.refs_2_, ...), custom_call_target="tpu_custom_call" | custom-call | flops 33554432 | bytes 524288 | tf_op jit(solution)/shard_map/pallas_call | solution.py:436
  23.7 0.7 %collective-permute-start.7 = (bf16[136,512]{1,0:T(8,128)(2,1)S(1)}, bf16[136,512]{1,0:T(8,128)(2,1)S(1)}, u32[]{:S(2)}, u32[]{:S(2)}) collective-permute-start(bf16[136,512]{1,0:T(8,128)(2,1)S(1)} %shard_map.78), channel_id=1, source_target_pairs={{0,4},{4,0},{8,16},{12,20},{16,24},{20,28},{24,8},{28,12},{1,5},{5... | collective-permute-start | bytes 417800 | tf_op jit(solution)/shard_map/ppermute | solution.py:20
  24.3 0.0 copy-done
  24.3 0.0 copy-done.3
  24.3 1.5 %shard_map.75 = (f32[256,1024]{1,0:T(8,128)S(1)}, f32[128,1024]{1,0:T(8,128)S(1)}, f32[3,8,128]{2,1,0:T(8,128)S(1)}) custom-call(s32[32]{0:T(128)S(1)} %copy-done.2, bf16[8,2,128,768]{3,2,1,0:T(8,128)(2,1)S(1)} %get-tuple-element.30.table_ref, bf16[136,1024]{1,0:T(8,128)(2,1)S(1)} %copy-done, ...), custom_call_target="tpu_custom_call" | custom-call | flops 167772160 | bytes 2097152 | tf_op jit(solution)/shard_map/pallas_call | solution.py:452
  25.9 0.0 collective-permute-done.5.raw_ref
  25.9 0.9 %shard_map.76.qpair_ref = f32[128,1024]{1,0:T(8,128)S(1)} custom-call(s32[32]{0:T(128)S(1)} %copy-done.2, bf16[128,1024]{1,0:T(8,128)(2,1)S(1)} %collective-permute-done.5.raw_ref, bf16[136,1024]{1,0:T(8,128)(2,1)S(1)} %copy-done, bf16[136,1024]{1,0:T(8,128)(2,1)S(1)} %collective-permute-done.1.back_own_ref.refs_0_, f32[3,3,1024]{2,1,0:T(4,128)S(1)} %get-tuple-element.36.w_ref), custom_call_target="tpu_custom_call" | custom-call | flops 1310720 | bytes 1048576 | tf_op jit(solution)/shard_map/pallas_call | solution.py:461
  26.8 0.4 collective-permute-done.6.refs_3_
  27.1 1.6 %collective-permute-done.7.refs_4_ = bf16[136,512]{1,0:T(8,128)(2,1)S(1)} collective-permute-done((bf16[136,512]{1,0:T(8,128)(2,1)S(1)}, bf16[136,512]{1,0:T(8,128)(2,1)S(1)}, u32[]{:S(2)}, u32[]{:S(2)}) %collective-permute-start.7) | collective-permute-done | bytes 139296 | tf_op jit(solution)/shard_map/ppermute | solution.py:20
  28.8 1.2 %shard_map.79 = (f32[128,1024]{1,0:T(8,128)S(1)}, bf16[128,1024]{1,0:T(8,128)(2,1)S(1)}, f32[1,256]{1,0:T(1,128)S(1)}) custom-call(bf16[8,2,128,768]{3,2,1,0:T(8,128)(2,1)S(1)} %get-tuple-element.30.table_ref, f32[256,1024]{1,0:T(8,128)S(1)} %get-tuple-element.37.acc_ref, f32[128,1024]{1,0:T(8,128)S(1)} %get-tuple-element.38.qown_ref, ...), custom_call_target="tpu_custom_call" | custom-call | flops 167772160 | bytes 3145728 | tf_op jit(solution)/shard_map/pallas_call | solution.py:470
  29.9 0.8 %collective-permute-start.12 = (bf16[128,1024]{1,0:T(8,128)(2,1)S(1)}, bf16[128,1024]{1,0:T(8,128)(2,1)S(1)}, u32[]{:S(2)}, u32[]{:S(2)}) collective-permute-start(bf16[128,1024]{1,0:T(8,128)(2,1)S(1)} %get-tuple-element.44), channel_id=1, source_target_pairs={{0,4},{4,0},{8,12},{12,8},{16,20},{20,16},{24,28},{28,24},{1,5},{5... | collective-permute-start | bytes 786440 | tf_op jit(solution)/shard_map/ppermute | solution.py:20
  30.7 0.0 collective-permute-start.10
  30.7 1.5 %collective-permute-start.9 = (f32[1,256]{1,0:T(1,128)S(1)}, f32[1,256]{1,0:T(1,128)S(1)}, u32[]{:S(2)}, u32[]{:S(2)}) collective-permute-start(f32[1,256]{1,0:T(1,128)S(1)} %get-tuple-element.42), channel_id=1, source_target_pairs={{0,2},{1,3},{2,0},{3,1},{4,6},{5,7},{6,4},{7,5},{8,10},{9,11},{10,... | collective-permute-start | bytes 3080 | tf_op jit(solution)/shard_map/ppermute | solution.py:481
  32.3 0.3 collective-permute-start.8
  32.6 1.1 %collective-permute-done.10 = f32[1,256]{1,0:T(1,128)S(1)} collective-permute-done((f32[1,256]{1,0:T(1,128)S(1)}, f32[1,256]{1,0:T(1,128)S(1)}, u32[]{:S(2)}, u32[]{:S(2)}) %collective-permute-start.10) | collective-permute-done | bytes 1056 | tf_op jit(solution)/shard_map/ppermute | solution.py:481
  33.7 0.6 %collective-permute-done.9 = f32[1,256]{1,0:T(1,128)S(1)} collective-permute-done((f32[1,256]{1,0:T(1,128)S(1)}, f32[1,256]{1,0:T(1,128)S(1)}, u32[]{:S(2)}, u32[]{:S(2)}) %collective-permute-start.9) | collective-permute-done | bytes 1056 | tf_op jit(solution)/shard_map/ppermute | solution.py:481
  34.3 0.0 collective-permute-done.8
  34.4 1.3 %collective-permute-start.11 = (f32[1,256]{1,0:T(1,128)S(1)}, f32[1,256]{1,0:T(1,128)S(1)}, u32[]{:S(2)}, u32[]{:S(2)}) collective-permute-start(f32[1,256]{1,0:T(1,128)S(1)} %add_add_fusion.power_ref), channel_id=1, source_target_pairs={{0,4},{4,0},{8,12},{12,8},{16,20},{20,16},{24,28},{28,24},{1,5},{5... | collective-permute-start | bytes 3080 | tf_op jit(solution)/shard_map/ppermute | solution.py:20
  35.7 2.3 %collective-permute-done.11.power_got_ref = f32[1,256]{1,0:T(1,128)S(1)} collective-permute-done((f32[1,256]{1,0:T(1,128)S(1)}, f32[1,256]{1,0:T(1,128)S(1)}, u32[]{:S(2)}, u32[]{:S(2)}) %collective-permute-start.11) | collective-permute-done | bytes 1056 | tf_op jit(solution)/shard_map/ppermute | solution.py:20
  38.0 0.0 collective-permute-done.12.got_ref
  38.0 0.0 copy-done.4
  38.0 1.0 %shard_map.80 = bf16[128,2048]{1,0:T(8,128)(2,1)} custom-call(f32[1,256]{1,0:T(1,128)S(1)} %add_add_fusion.power_ref, f32[1,256]{1,0:T(1,128)S(1)} %collective-permute-done.11.power_got_ref, f32[128,1024]{1,0:T(8,128)S(1)} %get-tuple-element.43.kept_ref, bf16[128,1024]{1,0:T(8,128)(2,1)S(1)} %collective-permute-done.12.got_ref, f32[1,2048]{1,0:T(1,128)S(1)} %bitcast.13), custom_call_target="tpu_custom_call" | custom-call | flops 1048576 | bytes 1310720 | tf_op jit(solution)/shard_map/pallas_call | solution.py:483
  (6 shorter events, 0.0 us)
Async XLA Ops:
  0.0 8.2 %copy-start.2 = (s32[32]{0:T(128)S(1)}, s32[32]{0:T(128)}, u32[]{:S(2)}) copy-start(s32[32]{0:T(128)} %seq_ref.9) | copy-start | bytes 388
  0.0 8.2 %copy-start.1 = (f32[3,3,2048]{2,1,0:T(4,128)S(1)}, f32[3,3,2048]{2,1,0:T(4,128)}, u32[]{:S(2)}) copy-start(f32[3,3,2048]{2,1,0:T(4,128)} %w_ref.1) | copy-start | bytes 221188
  0.0 8.2 %copy-start.5 = (f32[16,512]{1,0:T(8,128)S(1)}, f32[16,512]{1,0:T(8,128)}, u32[]{:S(2)}) copy-start(f32[16,512]{1,0:T(8,128)} %param.9) | copy-start | bytes 98308
  0.0 8.0 %copy-start.6 = (s32[16,4]{0,1:T(4,128)S(1)}, s32[16,4]{0,1:T(4,128)}, u32[]{:S(2)}) copy-start(s32[16,4]{0,1:T(4,128)} %param.10) | copy-start | bytes 772
  2.9 8.2 %collective-permute-start = (bf16[136,512]{1,0:T(8,128)(2,1)}, bf16[136,512]{1,0:T(8,128)(2,1)S(1)}, u32[]{:S(2)}, u32[]{:S(2)}) collective-permute-start(bf16[136,512]{1,0:T(8,128)(2,1)} %get-tuple-element.29), channel_id=1, source_target_pairs={{0,4},{4,0},{8,12},{12,8},{16,20},{20,16},{24,28},{28,24},{1,5},{5... | collective-permute-start | bytes 417800 | tf_op jit(solution)/shard_map/ppermute | solution.py:20
  5.9 11.6 %collective-permute-start.1 = (bf16[136,1024]{1,0:T(8,128)(2,1)}, bf16[136,1024]{1,0:T(8,128)(2,1)S(1)}, u32[]{:S(2)}, u32[]{:S(2)}) collective-permute-start(bf16[136,1024]{1,0:T(8,128)(2,1)} %get-tuple-element.25.own_ref), channel_id=1, source_target_pairs={{0,8},{4,12},{8,16},{12,20},{16,24},{20,28},{24,0},{28,4},{1,9},{5... | collective-permute-start | bytes 835592 | tf_op jit(solution)/shard_map/ppermute | solution.py:20
  7.5 6.3 %collective-permute-start.2 = (bf16[136,512]{1,0:T(8,128)(2,1)}, bf16[136,512]{1,0:T(8,128)(2,1)S(1)}, u32[]{:S(2)}, u32[]{:S(2)}) collective-permute-start(bf16[136,512]{1,0:T(8,128)(2,1)} %get-tuple-element.33), channel_id=1, source_target_pairs={{0,4},{4,0},{8,12},{12,8},{16,20},{20,16},{24,28},{28,24},{1,5},{5... | collective-permute-start | bytes 417800 | tf_op jit(solution)/shard_map/ppermute | solution.py:20
  11.1 13.3 %copy-start = (bf16[136,1024]{1,0:T(8,128)(2,1)S(1)}, bf16[136,1024]{1,0:T(8,128)(2,1)}, u32[]{:S(2)}) copy-start(bf16[136,1024]{1,0:T(8,128)(2,1)} %get-tuple-element.25.own_ref) | copy-start | bytes 835588
  11.1 13.2 %copy-start.3 = (f32[2048]{0:T(1024)S(1)}, f32[2048]{0:T(1024)}, u32[]{:S(2)}) copy-start(f32[2048]{0:T(1024)} %param.11) | copy-start | bytes 24580
  11.1 9.4 %collective-permute-start.3 = (bf16[136,512]{1,0:T(8,128)(2,1)S(1)}, bf16[136,512]{1,0:T(8,128)(2,1)S(1)}, u32[]{:S(2)}, u32[]{:S(2)}) collective-permute-start(bf16[136,512]{1,0:T(8,128)(2,1)S(1)} %collective-permute-done.pair_a_ref), channel_id=1, source_target_pairs={{0,8},{4,12},{8,16},{12,20},{16,24},{20,28},{24,0},{28,4},{1,9},{5... | collective-permute-start | bytes 417800 | tf_op jit(solution)/shard_map/ppermute | solution.py:20
  13.8 9.2 %collective-permute-start.4 = (bf16[136,512]{1,0:T(8,128)(2,1)S(1)}, bf16[136,512]{1,0:T(8,128)(2,1)S(1)}, u32[]{:S(2)}, u32[]{:S(2)}) collective-permute-start(bf16[136,512]{1,0:T(8,128)(2,1)S(1)} %collective-permute-done.2.pair_b_ref), channel_id=1, source_target_pairs={{0,8},{4,12},{8,16},{12,20},{16,24},{20,28},{24,0},{28,4},{1,9},{5... | collective-permute-start | bytes 417800 | tf_op jit(solution)/shard_map/ppermute | solution.py:20
  15.4 10.4 %collective-permute-start.5 = (bf16[128,1024]{1,0:T(8,128)(2,1)S(1)}, bf16[128,1024]{1,0:T(8,128)(2,1)S(1)}, u32[]{:S(2)}, u32[]{:S(2)}) collective-permute-start(bf16[128,1024]{1,0:T(8,128)(2,1)S(1)} %get-tuple-element.39), channel_id=1, source_target_pairs={{0,4},{4,0},{8,12},{12,8},{16,20},{20,16},{24,28},{28,24},{1,5},{5... | collective-permute-start | bytes 786440 | tf_op jit(solution)/shard_map/ppermute | solution.py:20
  21.2 5.9 %collective-permute-start.6 = (bf16[136,512]{1,0:T(8,128)(2,1)S(1)}, bf16[136,512]{1,0:T(8,128)(2,1)S(1)}, u32[]{:S(2)}, u32[]{:S(2)}) collective-permute-start(bf16[136,512]{1,0:T(8,128)(2,1)S(1)} %shard_map.77), channel_id=1, source_target_pairs={{0,4},{4,0},{8,16},{12,20},{16,24},{20,28},{24,8},{28,12},{1,5},{5... | collective-permute-start | bytes 417800 | tf_op jit(solution)/shard_map/ppermute | solution.py:20
  23.7 5.1 %collective-permute-start.7 = (bf16[136,512]{1,0:T(8,128)(2,1)S(1)}, bf16[136,512]{1,0:T(8,128)(2,1)S(1)}, u32[]{:S(2)}, u32[]{:S(2)}) collective-permute-start(bf16[136,512]{1,0:T(8,128)(2,1)S(1)} %shard_map.78), channel_id=1, source_target_pairs={{0,4},{4,0},{8,16},{12,20},{16,24},{20,28},{24,8},{28,12},{1,5},{5... | collective-permute-start | bytes 417800 | tf_op jit(solution)/shard_map/ppermute | solution.py:20
  28.8 9.2 %copy-start.4 = (f32[2048]{0:T(1024)S(1)}, f32[2048]{0:T(1024)}, u32[]{:S(2)}) copy-start(f32[2048]{0:T(1024)} %param.12) | copy-start | bytes 24580
  29.9 8.1 %collective-permute-start.12 = (bf16[128,1024]{1,0:T(8,128)(2,1)S(1)}, bf16[128,1024]{1,0:T(8,128)(2,1)S(1)}, u32[]{:S(2)}, u32[]{:S(2)}) collective-permute-start(bf16[128,1024]{1,0:T(8,128)(2,1)S(1)} %get-tuple-element.44), channel_id=1, source_target_pairs={{0,4},{4,0},{8,12},{12,8},{16,20},{20,16},{24,28},{28,24},{1,5},{5... | collective-permute-start | bytes 786440 | tf_op jit(solution)/shard_map/ppermute | solution.py:20
  30.7 3.0 %collective-permute-start.10 = (f32[1,256]{1,0:T(1,128)S(1)}, f32[1,256]{1,0:T(1,128)S(1)}, u32[]{:S(2)}, u32[]{:S(2)}) collective-permute-start(f32[1,256]{1,0:T(1,128)S(1)} %get-tuple-element.42), channel_id=1, source_target_pairs={{0,3},{1,2},{2,1},{3,0},{4,7},{5,6},{6,5},{7,4},{8,11},{9,10},{10,... | collective-permute-start | bytes 3080 | tf_op jit(solution)/shard_map/ppermute | solution.py:481
  30.7 3.6 %collective-permute-start.9 = (f32[1,256]{1,0:T(1,128)S(1)}, f32[1,256]{1,0:T(1,128)S(1)}, u32[]{:S(2)}, u32[]{:S(2)}) collective-permute-start(f32[1,256]{1,0:T(1,128)S(1)} %get-tuple-element.42), channel_id=1, source_target_pairs={{0,2},{1,3},{2,0},{3,1},{4,6},{5,7},{6,4},{7,5},{8,10},{9,11},{10,... | collective-permute-start | bytes 3080 | tf_op jit(solution)/shard_map/ppermute | solution.py:481
  32.3 2.1 %collective-permute-start.8 = (f32[1,256]{1,0:T(1,128)S(1)}, f32[1,256]{1,0:T(1,128)S(1)}, u32[]{:S(2)}, u32[]{:S(2)}) collective-permute-start(f32[1,256]{1,0:T(1,128)S(1)} %get-tuple-element.42), channel_id=1, source_target_pairs={{0,1},{1,0},{2,3},{3,2},{4,5},{5,4},{6,7},{7,6},{8,9},{9,8},{10,11... | collective-permute-start | bytes 3080 | tf_op jit(solution)/shard_map/ppermute | solution.py:481
  34.4 3.6 %collective-permute-start.11 = (f32[1,256]{1,0:T(1,128)S(1)}, f32[1,256]{1,0:T(1,128)S(1)}, u32[]{:S(2)}, u32[]{:S(2)}) collective-permute-start(f32[1,256]{1,0:T(1,128)S(1)} %add_add_fusion.power_ref), channel_id=1, source_target_pairs={{0,4},{4,0},{8,12},{12,8},{16,20},{20,16},{24,28},{28,24},{1,5},{5... | collective-permute-start | bytes 3080 | tf_op jit(solution)/shard_map/ppermute | solution.py:20

commit v14 on v12

--- a/solution.py
+++ b/solution.py
@@ -398,7 +398,7 @@
     )(seq_lengths, panels, short_weight)
 
     back_own = moved(kept, ahead)
-    pair = [moved(piece, to_pair) for piece in sent]
+    pair = [moved(sent[0], to_pair)]
 
     filter_taps, _ = lax.optimization_barrier((filter_taps, kept))
     scaled = (filter_taps * jnp.repeat(tap_blocks.astype(jnp.float32), BLK, axis=1)).astype(jnp.bfloat16)
@@ -415,7 +415,8 @@
         40 * groups * BLK * taps,
         8 * groups * BLK * taps,
     )(seq_lengths, scaled, short_weight)
-    table, table_next, pair[0] = lax.optimization_barrier((table, table_next, pair[0]))
+    table, table_next, later = lax.optimization_barrier((table, table_next, sent[1]))
+    pair.append(moved(later, to_pair))
 
     half = lax.axis_index("half")
     query, _, back_own = lax.optimization_barrier((panels, pair[0], back_own))

time: 41.1 us -> 41.7 us (1.015)
  local copies, waits for them, and re-layouts: 1.25 us -> 3.97 us
  starting transfers between devices: 16 us -> 14.5 us
  waiting for transfers between devices: 11.8 us -> 10.8 us
    unnamed x14 -> x18, local copies, waits for them, and re-layouts: 0.03 us -> 2.74 us
    ppermute x10, starting transfers between devices: 14.2 us -> 12.6 us  [moved(): return lax.ppermute(block, SPOTS, pairs)]
    ppermute x10, waiting for transfers between devices: 10.1 us -> 9.03 us  [moved(): return lax.ppermute(block, SPOTS, pairs)]
    pallas_call x1, Pallas kernels: 1.53 us -> 2.01 us  [shards(): kernel_call(near_kernel, (shape((2 * rows, width), jnp.float32), half_wid...]
  transfers between devices with their start and end apart: 13 -> 13, of which waited for: 8 -> 9; matrix products, arithmetic and copies ran while one was open for 3% -> 3% of each run, Pallas kernels for 16% -> 17%
where the time goes in v14:
time: 41.7 us; the launch traced here: 41.5 us
  starting transfers between devices  14.5 us (35%)
  Pallas kernels  12.1 us (29%)
  waiting for transfers between devices  10.8 us (26%)
  local copies, waits for them, and re-layouts  3.97 us (10%)
    ppermute x10, starting transfers between devices, moved(): return lax.ppermute(block, SPOTS, pairs)  12.6 us
    ppermute x10, waiting for transfers between devices, moved(): return lax.ppermute(block, SPOTS, pairs)  9.03 us
    pallas_call x1, Pallas kernels, shards(): kernel_call(products_kernel, (message, small, small), [hbm] * 3, [pltpu.S...  2.83 us
    pallas_call x1, Pallas kernels, shards(): kernel_call(tables_kernel, (shape((groups, 2, BLK, span), jnp.bfloat16),...  2.81 us
    unnamed x18, local copies, waits for them, and re-layouts  2.74 us
    pallas_call x1, Pallas kernels, shards(): kernel_call(near_kernel, (shape((2 * rows, width), jnp.float32), half_wid...  2.01 us
    ppermute x3, starting transfers between devices, shards(): lax.ppermute(power, 'mp', [(i, i ^ k) for i in range(peers)])  1.86 us
    ppermute x3, waiting for transfers between devices, shards(): lax.ppermute(power, 'mp', [(i, i ^ k) for i in range(peers)])  1.74 us
  transfers between devices with their start and end apart: 13, of which 9 were waited for; matrix products, arithmetic and copies ran while one was open for 3% of the time, Pallas kernels for 17%

profile of v14, /device:TPU:0, one launch (start us, length us, event | category | flops | bytes accessed | tf_op | source)
XLA Modules:
  0.0 41.5 jit_solution(17324800715253650891)
XLA Ops:
  0.0 2.8 %shard_map.73 = (bf16[136,1024]{1,0:T(8,128)(2,1)}, bf16[136,512]{1,0:T(8,128)(2,1)}, bf16[136,512]{1,0:T(8,128)(2,1)}) custom-call(s32[32]{0:T(128)} %seq_ref.9, bf16[3,128,2048]{2,1,0:T(8,128)(2,1)} %bitcast.14, f32[3,3,2048]{2,1,0:T(4,128)} %w_ref.1), custom_call_target="tpu_custom_call" | custom-call | flops 5242880 | bytes 2097152 | tf_op jit(solution)/shard_map/pallas_call | solution.py:381
  2.8 3.1 %collective-permute-start.1 = (bf16[136,1024]{1,0:T(8,128)(2,1)}, bf16[136,1024]{1,0:T(8,128)(2,1)S(1)}, u32[]{:S(2)}, u32[]{:S(2)}) collective-permute-start(bf16[136,1024]{1,0:T(8,128)(2,1)} %get-tuple-element.26.own_ref), channel_id=1, source_target_pairs={{0,8},{4,12},{8,16},{12,20},{16,24},{20,28},{24,0},{28,4},{1,9},{5... | collective-permute-start | bytes 835592 | tf_op jit(solution)/shard_map/ppermute | solution.py:20
  5.9 1.5 %collective-permute-start = (bf16[136,512]{1,0:T(8,128)(2,1)}, bf16[136,512]{1,0:T(8,128)(2,1)}, u32[]{:S(2)}, u32[]{:S(2)}) collective-permute-start(bf16[136,512]{1,0:T(8,128)(2,1)} %get-tuple-element.32), channel_id=1, source_target_pairs={{0,4},{4,0},{8,12},{12,8},{16,20},{20,16},{24,28},{28,24},{1,5},{5... | collective-permute-start | bytes 417800 | tf_op jit(solution)/shard_map/ppermute | solution.py:20
  7.4 0.0 copy-done.8
  7.5 0.1 copy.8
  7.5 0.1 broadcast_in_dim.3
  7.6 0.0 copy-done.7
  7.6 0.0 copy-done.4
  7.6 0.0 copy-start.3
  7.7 0.9 %copy-done.3 = f32[3,3,2048]{2,1,0:T(4,128)S(1)} copy-done((f32[3,3,2048]{2,1,0:T(4,128)S(1)}, f32[3,3,2048]{2,1,0:T(4,128)}, u32[]{:S(2)}) %copy-start.3) | copy-done | bytes 73752
  8.5 2.8 %shard_map.74 = (bf16[8,2,128,768]{3,2,1,0:T(8,128)(2,1)S(1)}, bf16[8,128,256]{2,1,0:T(8,128)(2,1)S(1)}, f32[3,3,1024]{2,1,0:T(4,128)S(1)}) custom-call(s32[32]{0:T(128)S(1)} %copy-done.4, bf16[16,512]{1,0:T(8,128)(2,1)S(1)} %fusion.taps_ref, f32[3,3,2048]{2,1,0:T(4,128)S(1)} %copy-done.3), custom_call_target="tpu_custom_call" | custom-call | flops 20971520 | bytes 4194304 | tf_op jit(solution)/shard_map/pallas_call | solution.py:406
  11.4 0.0 copy-start
  11.4 0.8 %copy-done = bf16[8,128,256]{2,1,0:T(8,128)(2,1)} copy-done((bf16[8,128,256]{2,1,0:T(8,128)(2,1)}, bf16[8,128,256]{2,1,0:T(8,128)(2,1)S(1)}, u32[]{:S(2)}) %copy-start) | copy-done | bytes 524312
  12.2 0.5 %collective-permute-start.2 = (bf16[136,512]{1,0:T(8,128)(2,1)}, bf16[136,512]{1,0:T(8,128)(2,1)}, u32[]{:S(2)}, u32[]{:S(2)}) collective-permute-start(bf16[136,512]{1,0:T(8,128)(2,1)} %get-tuple-element.35), channel_id=1, source_target_pairs={{0,4},{4,0},{8,12},{12,8},{16,20},{20,16},{24,28},{28,24},{1,5},{5... | collective-permute-start | bytes 417800 | tf_op jit(solution)/shard_map/ppermute | solution.py:20
  12.7 0.0 collective-permute-done.pair_a_ref
  12.7 1.6 %collective-permute-start.3 = (bf16[136,512]{1,0:T(8,128)(2,1)}, bf16[136,512]{1,0:T(8,128)(2,1)S(1)}, u32[]{:S(2)}, u32[]{:S(2)}) collective-permute-start(bf16[136,512]{1,0:T(8,128)(2,1)} %collective-permute-done.pair_a_ref), channel_id=1, source_target_pairs={{0,8},{4,12},{8,16},{12,20},{16,24},{20,28},{24,0},{28,4},{1,9},{5... | collective-permute-start | bytes 417800 | tf_op jit(solution)/shard_map/ppermute | solution.py:20
  14.2 0.6 %collective-permute-done.1.back_own_ref.refs_0_ = bf16[136,1024]{1,0:T(8,128)(2,1)S(1)} collective-permute-done((bf16[136,1024]{1,0:T(8,128)(2,1)}, bf16[136,1024]{1,0:T(8,128)(2,1)S(1)}, u32[]{:S(2)}, u32[]{:S(2)}) %collective-permute-start.1) | collective-permute-done | bytes 278560 | tf_op jit(solution)/shard_map/ppermute | solution.py:20
  14.8 1.1 %dynamic-slice_bitcast_fusion = (bf16[128,1024]{1,0:T(8,128)(2,1)S(1)}, bf16[128,1024]{1,0:T(8,128)(2,1)S(1)}) fusion(bf16[3,128,2048]{2,1,0:T(8,128)(2,1)} %bitcast.15, s32[]{:T(128)S(6)} %select_n.7, s32[]{:T(128)S(6)} %select_n.6), kind=kLoop, calls=%fused_computation | loop fusion | bytes 1048584 | tf_op jit(solution)/shard_map/squeeze | solution.py:424
  15.9 1.6 %collective-permute-done.2.pair_b_ref = bf16[136,512]{1,0:T(8,128)(2,1)} collective-permute-done((bf16[136,512]{1,0:T(8,128)(2,1)}, bf16[136,512]{1,0:T(8,128)(2,1)}, u32[]{:S(2)}, u32[]{:S(2)}) %collective-permute-start.2) | collective-permute-done | bytes 139296 | tf_op jit(solution)/shard_map/ppermute | solution.py:20
  17.5 1.6 %collective-permute-start.4 = (bf16[136,512]{1,0:T(8,128)(2,1)}, bf16[136,512]{1,0:T(8,128)(2,1)S(1)}, u32[]{:S(2)}, u32[]{:S(2)}) collective-permute-start(bf16[136,512]{1,0:T(8,128)(2,1)} %collective-permute-done.2.pair_b_ref), channel_id=1, source_target_pairs={{0,8},{4,12},{8,16},{12,20},{16,24},{20,28},{24,0},{28,4},{1,9},{5... | collective-permute-start | bytes 417800 | tf_op jit(solution)/shard_map/ppermute | solution.py:20
  19.1 0.5 %collective-permute-start.5 = (bf16[128,1024]{1,0:T(8,128)(2,1)S(1)}, bf16[128,1024]{1,0:T(8,128)(2,1)S(1)}, u32[]{:S(2)}, u32[]{:S(2)}) collective-permute-start(bf16[128,1024]{1,0:T(8,128)(2,1)S(1)} %get-tuple-element.41), channel_id=1, source_target_pairs={{0,4},{4,0},{8,12},{12,8},{16,20},{20,16},{24,28},{28,24},{1,5},{5... | collective-permute-start | bytes 786440 | tf_op jit(solution)/shard_map/ppermute | solution.py:20
  19.6 0.1 collective-permute-done.3.back_a_ref.back_pair_ref.refs_1_
  19.7 1.0 %copy-done.1 = bf16[8,128,256]{2,1,0:T(8,128)(2,1)S(1)} copy-done((bf16[8,128,256]{2,1,0:T(8,128)(2,1)S(1)}, bf16[8,128,256]{2,1,0:T(8,128)(2,1)}, u32[]{:S(2)}) %copy-start.1) | copy-done | bytes 524312
  20.8 0.7 %shard_map.77 = bf16[136,512]{1,0:T(8,128)(2,1)S(1)} custom-call(s32[32]{0:T(128)S(1)} %copy-done.4, bf16[8,128,256]{2,1,0:T(8,128)(2,1)S(1)} %copy-done.1, bf16[136,1024]{1,0:T(8,128)(2,1)S(1)} %collective-permute-done.1.back_own_ref.refs_0_, bf16[136,512]{1,0:T(8,128)(2,1)S(1)} %collective-permute-done.3.back_a_ref.back_pair_ref.refs_1_, ...), custom_call_target="tpu_custom_call" | custom-call | flops 33554432 | bytes 524288 | tf_op jit(solution)/shard_map/pallas_call | solution.py:437
  21.5 1.7 %collective-permute-start.6 = (bf16[136,512]{1,0:T(8,128)(2,1)S(1)}, bf16[136,512]{1,0:T(8,128)(2,1)S(1)}, u32[]{:S(2)}, u32[]{:S(2)}) collective-permute-start(bf16[136,512]{1,0:T(8,128)(2,1)S(1)} %shard_map.77), channel_id=1, source_target_pairs={{0,4},{4,0},{8,16},{12,20},{16,24},{20,28},{24,8},{28,12},{1,5},{5... | collective-permute-start | bytes 417800 | tf_op jit(solution)/shard_map/ppermute | solution.py:20
  23.1 2.4 %collective-permute-done.4.back_b_ref.back_pair_ref.refs_2_ = bf16[136,512]{1,0:T(8,128)(2,1)S(1)} collective-permute-done((bf16[136,512]{1,0:T(8,128)(2,1)}, bf16[136,512]{1,0:T(8,128)(2,1)S(1)}, u32[]{:S(2)}, u32[]{:S(2)}) %collective-permute-start.4) | collective-permute-done | bytes 139296 | tf_op jit(solution)/shard_map/ppermute | solution.py:20
  25.6 0.7 %shard_map.78 = bf16[136,512]{1,0:T(8,128)(2,1)S(1)} custom-call(s32[32]{0:T(128)S(1)} %copy-done.4, bf16[8,128,256]{2,1,0:T(8,128)(2,1)S(1)} %copy-done.1, bf16[136,1024]{1,0:T(8,128)(2,1)S(1)} %collective-permute-done.1.back_own_ref.refs_0_, bf16[136,512]{1,0:T(8,128)(2,1)S(1)} %collective-permute-done.4.back_b_ref.back_pair_ref.refs_2_, ...), custom_call_target="tpu_custom_call" | custom-call | flops 33554432 | bytes 524288 | tf_op jit(solution)/shard_map/pallas_call | solution.py:437
  26.3 0.1 collective-permute-start.7
  26.3 0.0 copy-done.2
  26.3 0.0 copy-done.5
  26.4 2.0 %shard_map.75 = (f32[256,1024]{1,0:T(8,128)S(1)}, f32[128,1024]{1,0:T(8,128)S(1)}, f32[3,8,128]{2,1,0:T(8,128)S(1)}) custom-call(s32[32]{0:T(128)S(1)} %copy-done.4, bf16[8,2,128,768]{3,2,1,0:T(8,128)(2,1)S(1)} %get-tuple-element.31.table_ref, bf16[136,1024]{1,0:T(8,128)(2,1)S(1)} %copy-done.2, ...), custom_call_target="tpu_custom_call" | custom-call | flops 167772160 | bytes 2097152 | tf_op jit(solution)/shard_map/pallas_call | solution.py:453
  28.4 0.0 collective-permute-done.5.raw_ref
  28.4 0.9 %shard_map.76.qpair_ref = f32[128,1024]{1,0:T(8,128)S(1)} custom-call(s32[32]{0:T(128)S(1)} %copy-done.4, bf16[128,1024]{1,0:T(8,128)(2,1)S(1)} %collective-permute-done.5.raw_ref, bf16[136,1024]{1,0:T(8,128)(2,1)S(1)} %copy-done.2, bf16[136,1024]{1,0:T(8,128)(2,1)S(1)} %collective-permute-done.1.back_own_ref.refs_0_, f32[3,3,1024]{2,1,0:T(4,128)S(1)} %get-tuple-element.38.w_ref), custom_call_target="tpu_custom_call" | custom-call | flops 1310720 | bytes 1048576 | tf_op jit(solution)/shard_map/pallas_call | solution.py:462
  29.3 0.4 collective-permute-done.6.refs_3_
  29.6 1.7 %collective-permute-done.7.refs_4_ = bf16[136,512]{1,0:T(8,128)(2,1)S(1)} collective-permute-done((bf16[136,512]{1,0:T(8,128)(2,1)S(1)}, bf16[136,512]{1,0:T(8,128)(2,1)S(1)}, u32[]{:S(2)}, u32[]{:S(2)}) %collective-permute-start.7) | collective-permute-done | bytes 139296 | tf_op jit(solution)/shard_map/ppermute | solution.py:20
  31.4 1.2 %shard_map.79 = (f32[128,1024]{1,0:T(8,128)S(1)}, bf16[128,1024]{1,0:T(8,128)(2,1)S(1)}, f32[1,256]{1,0:T(1,128)S(1)}) custom-call(bf16[8,2,128,768]{3,2,1,0:T(8,128)(2,1)S(1)} %get-tuple-element.31.table_ref, f32[256,1024]{1,0:T(8,128)S(1)} %get-tuple-element.39.acc_ref, f32[128,1024]{1,0:T(8,128)S(1)} %get-tuple-element.40.qown_ref, ...), custom_call_target="tpu_custom_call" | custom-call | flops 167772160 | bytes 3145728 | tf_op jit(solution)/shard_map/pallas_call | solution.py:471
  32.6 0.6 %collective-permute-start.12 = (bf16[128,1024]{1,0:T(8,128)(2,1)S(1)}, bf16[128,1024]{1,0:T(8,128)(2,1)S(1)}, u32[]{:S(2)}, u32[]{:S(2)}) collective-permute-start(bf16[128,1024]{1,0:T(8,128)(2,1)S(1)} %get-tuple-element.46), channel_id=1, source_target_pairs={{0,4},{4,0},{8,12},{12,8},{16,20},{20,16},{24,28},{28,24},{1,5},{5... | collective-permute-start | bytes 786440 | tf_op jit(solution)/shard_map/ppermute | solution.py:20
  33.2 0.0 collective-permute-start.10
  33.2 1.5 %collective-permute-start.9 = (f32[1,256]{1,0:T(1,128)S(1)}, f32[1,256]{1,0:T(1,128)S(1)}, u32[]{:S(2)}, u32[]{:S(2)}) collective-permute-start(f32[1,256]{1,0:T(1,128)S(1)} %get-tuple-element.44), channel_id=1, source_target_pairs={{0,2},{1,3},{2,0},{3,1},{4,6},{5,7},{6,4},{7,5},{8,10},{9,11},{10,... | collective-permute-start | bytes 3080 | tf_op jit(solution)/shard_map/ppermute | solution.py:482
  34.7 0.3 collective-permute-start.8
  35.0 1.1 %collective-permute-done.10 = f32[1,256]{1,0:T(1,128)S(1)} collective-permute-done((f32[1,256]{1,0:T(1,128)S(1)}, f32[1,256]{1,0:T(1,128)S(1)}, u32[]{:S(2)}, u32[]{:S(2)}) %collective-permute-start.10) | collective-permute-done | bytes 1056 | tf_op jit(solution)/shard_map/ppermute | solution.py:482
  36.1 0.6 %collective-permute-done.9 = f32[1,256]{1,0:T(1,128)S(1)} collective-permute-done((f32[1,256]{1,0:T(1,128)S(1)}, f32[1,256]{1,0:T(1,128)S(1)}, u32[]{:S(2)}, u32[]{:S(2)}) %collective-permute-start.9) | collective-permute-done | bytes 1056 | tf_op jit(solution)/shard_map/ppermute | solution.py:482
  36.8 0.0 collective-permute-done.8
  36.8 1.5 %collective-permute-start.11 = (f32[1,256]{1,0:T(1,128)S(1)}, f32[1,256]{1,0:T(1,128)S(1)}, u32[]{:S(2)}, u32[]{:S(2)}) collective-permute-start(f32[1,256]{1,0:T(1,128)S(1)} %add_add_fusion.power_ref), channel_id=1, source_target_pairs={{0,4},{4,0},{8,12},{12,8},{16,20},{20,16},{24,28},{28,24},{1,5},{5... | collective-permute-start | bytes 3080 | tf_op jit(solution)/shard_map/ppermute | solution.py:20
  38.3 2.1 %collective-permute-done.11.power_got_ref = f32[1,256]{1,0:T(1,128)S(1)} collective-permute-done((f32[1,256]{1,0:T(1,128)S(1)}, f32[1,256]{1,0:T(1,128)S(1)}, u32[]{:S(2)}, u32[]{:S(2)}) %collective-permute-start.11) | collective-permute-done | bytes 1056 | tf_op jit(solution)/shard_map/ppermute | solution.py:20
  40.4 0.0 collective-permute-done.12.got_ref
  40.4 0.0 copy-done.6
  40.4 1.0 %shard_map.80 = bf16[128,2048]{1,0:T(8,128)(2,1)} custom-call(f32[1,256]{1,0:T(1,128)S(1)} %add_add_fusion.power_ref, f32[1,256]{1,0:T(1,128)S(1)} %collective-permute-done.11.power_got_ref, f32[128,1024]{1,0:T(8,128)S(1)} %get-tuple-element.45.kept_ref, bf16[128,1024]{1,0:T(8,128)(2,1)S(1)} %collective-permute-done.12.got_ref, f32[1,2048]{1,0:T(1,128)S(1)} %bitcast.13), custom_call_target="tpu_custom_call" | custom-call | flops 1048576 | bytes 1310720 | tf_op jit(solution)/shard_map/pallas_call | solution.py:484
  (10 shorter events, 0.0 us)
Async XLA Ops:
  0.0 7.6 %copy-start.4 = (s32[32]{0:T(128)S(1)}, s32[32]{0:T(128)}, u32[]{:S(2)}) copy-start(s32[32]{0:T(128)} %seq_ref.9) | copy-start | bytes 388
  0.0 7.6 %copy-start.7 = (f32[16,512]{1,0:T(8,128)S(1)}, f32[16,512]{1,0:T(8,128)}, u32[]{:S(2)}) copy-start(f32[16,512]{1,0:T(8,128)} %param.9) | copy-start | bytes 98308
  0.0 7.4 %copy-start.8 = (s32[16,4]{0,1:T(4,128)S(1)}, s32[16,4]{0,1:T(4,128)}, u32[]{:S(2)}) copy-start(s32[16,4]{0,1:T(4,128)} %param.10) | copy-start | bytes 772
  2.8 12.0 %collective-permute-start.1 = (bf16[136,1024]{1,0:T(8,128)(2,1)}, bf16[136,1024]{1,0:T(8,128)(2,1)S(1)}, u32[]{:S(2)}, u32[]{:S(2)}) collective-permute-start(bf16[136,1024]{1,0:T(8,128)(2,1)} %get-tuple-element.26.own_ref), channel_id=1, source_target_pairs={{0,8},{4,12},{8,16},{12,20},{16,24},{20,28},{24,0},{28,4},{1,9},{5... | collective-permute-start | bytes 835592 | tf_op jit(solution)/shard_map/ppermute | solution.py:20
  5.9 6.7 %collective-permute-start = (bf16[136,512]{1,0:T(8,128)(2,1)}, bf16[136,512]{1,0:T(8,128)(2,1)}, u32[]{:S(2)}, u32[]{:S(2)}) collective-permute-start(bf16[136,512]{1,0:T(8,128)(2,1)} %get-tuple-element.32), channel_id=1, source_target_pairs={{0,4},{4,0},{8,12},{12,8},{16,20},{20,16},{24,28},{28,24},{1,5},{5... | collective-permute-start | bytes 417800 | tf_op jit(solution)/shard_map/ppermute | solution.py:20
  7.6 0.9 %copy-start.3 = (f32[3,3,2048]{2,1,0:T(4,128)S(1)}, f32[3,3,2048]{2,1,0:T(4,128)}, u32[]{:S(2)}) copy-start(f32[3,3,2048]{2,1,0:T(4,128)} %w_ref.1) | copy-start | bytes 221188
  11.4 0.8 %copy-start = (bf16[8,128,256]{2,1,0:T(8,128)(2,1)}, bf16[8,128,256]{2,1,0:T(8,128)(2,1)S(1)}, u32[]{:S(2)}) copy-start(bf16[8,128,256]{2,1,0:T(8,128)(2,1)S(1)} %get-tuple-element.43.next_ref) | copy-start | bytes 1572868
  12.2 5.4 %collective-permute-start.2 = (bf16[136,512]{1,0:T(8,128)(2,1)}, bf16[136,512]{1,0:T(8,128)(2,1)}, u32[]{:S(2)}, u32[]{:S(2)}) collective-permute-start(bf16[136,512]{1,0:T(8,128)(2,1)} %get-tuple-element.35), channel_id=1, source_target_pairs={{0,4},{4,0},{8,12},{12,8},{16,20},{20,16},{24,28},{28,24},{1,5},{5... | collective-permute-start | bytes 417800 | tf_op jit(solution)/shard_map/ppermute | solution.py:20
  12.7 13.7 %copy-start.2 = (bf16[136,1024]{1,0:T(8,128)(2,1)S(1)}, bf16[136,1024]{1,0:T(8,128)(2,1)}, u32[]{:S(2)}) copy-start(bf16[136,1024]{1,0:T(8,128)(2,1)} %get-tuple-element.26.own_ref) | copy-start | bytes 835588
  12.7 13.7 %copy-start.5 = (f32[2048]{0:T(1024)S(1)}, f32[2048]{0:T(1024)}, u32[]{:S(2)}) copy-start(f32[2048]{0:T(1024)} %param.11) | copy-start | bytes 24580
  12.7 7.1 %collective-permute-start.3 = (bf16[136,512]{1,0:T(8,128)(2,1)}, bf16[136,512]{1,0:T(8,128)(2,1)S(1)}, u32[]{:S(2)}, u32[]{:S(2)}) collective-permute-start(bf16[136,512]{1,0:T(8,128)(2,1)} %collective-permute-done.pair_a_ref), channel_id=1, source_target_pairs={{0,8},{4,12},{8,16},{12,20},{16,24},{20,28},{24,0},{28,4},{1,9},{5... | collective-permute-start | bytes 417800 | tf_op jit(solution)/shard_map/ppermute | solution.py:20
  17.5 8.1 %collective-permute-start.4 = (bf16[136,512]{1,0:T(8,128)(2,1)}, bf16[136,512]{1,0:T(8,128)(2,1)S(1)}, u32[]{:S(2)}, u32[]{:S(2)}) collective-permute-start(bf16[136,512]{1,0:T(8,128)(2,1)} %collective-permute-done.2.pair_b_ref), channel_id=1, source_target_pairs={{0,8},{4,12},{8,16},{12,20},{16,24},{20,28},{24,0},{28,4},{1,9},{5... | collective-permute-start | bytes 417800 | tf_op jit(solution)/shard_map/ppermute | solution.py:20
  19.1 9.3 %collective-permute-start.5 = (bf16[128,1024]{1,0:T(8,128)(2,1)S(1)}, bf16[128,1024]{1,0:T(8,128)(2,1)S(1)}, u32[]{:S(2)}, u32[]{:S(2)}) collective-permute-start(bf16[128,1024]{1,0:T(8,128)(2,1)S(1)} %get-tuple-element.41), channel_id=1, source_target_pairs={{0,4},{4,0},{8,12},{12,8},{16,20},{20,16},{24,28},{28,24},{1,5},{5... | collective-permute-start | bytes 786440 | tf_op jit(solution)/shard_map/ppermute | solution.py:20
  19.7 1.0 %copy-start.1 = (bf16[8,128,256]{2,1,0:T(8,128)(2,1)S(1)}, bf16[8,128,256]{2,1,0:T(8,128)(2,1)}, u32[]{:S(2)}) copy-start(bf16[8,128,256]{2,1,0:T(8,128)(2,1)} %copy-done) | copy-start | bytes 1572868
  21.5 8.2 %collective-permute-start.6 = (bf16[136,512]{1,0:T(8,128)(2,1)S(1)}, bf16[136,512]{1,0:T(8,128)(2,1)S(1)}, u32[]{:S(2)}, u32[]{:S(2)}) collective-permute-start(bf16[136,512]{1,0:T(8,128)(2,1)S(1)} %shard_map.77), channel_id=1, source_target_pairs={{0,4},{4,0},{8,16},{12,20},{16,24},{20,28},{24,8},{28,12},{1,5},{5... | collective-permute-start | bytes 417800 | tf_op jit(solution)/shard_map/ppermute | solution.py:20
  26.3 5.1 %collective-permute-start.7 = (bf16[136,512]{1,0:T(8,128)(2,1)S(1)}, bf16[136,512]{1,0:T(8,128)(2,1)S(1)}, u32[]{:S(2)}, u32[]{:S(2)}) collective-permute-start(bf16[136,512]{1,0:T(8,128)(2,1)S(1)} %shard_map.78), channel_id=1, source_target_pairs={{0,4},{4,0},{8,16},{12,20},{16,24},{20,28},{24,8},{28,12},{1,5},{5... | collective-permute-start | bytes 417800 | tf_op jit(solution)/shard_map/ppermute | solution.py:20
  31.4 9.0 %copy-start.6 = (f32[2048]{0:T(1024)S(1)}, f32[2048]{0:T(1024)}, u32[]{:S(2)}) copy-start(f32[2048]{0:T(1024)} %param.12) | copy-start | bytes 24580
  32.6 7.9 %collective-permute-start.12 = (bf16[128,1024]{1,0:T(8,128)(2,1)S(1)}, bf16[128,1024]{1,0:T(8,128)(2,1)S(1)}, u32[]{:S(2)}, u32[]{:S(2)}) collective-permute-start(bf16[128,1024]{1,0:T(8,128)(2,1)S(1)} %get-tuple-element.46), channel_id=1, source_target_pairs={{0,4},{4,0},{8,12},{12,8},{16,20},{20,16},{24,28},{28,24},{1,5},{5... | collective-permute-start | bytes 786440 | tf_op jit(solution)/shard_map/ppermute | solution.py:20
  33.2 3.0 %collective-permute-start.10 = (f32[1,256]{1,0:T(1,128)S(1)}, f32[1,256]{1,0:T(1,128)S(1)}, u32[]{:S(2)}, u32[]{:S(2)}) collective-permute-start(f32[1,256]{1,0:T(1,128)S(1)} %get-tuple-element.44), channel_id=1, source_target_pairs={{0,3},{1,2},{2,1},{3,0},{4,7},{5,6},{6,5},{7,4},{8,11},{9,10},{10,... | collective-permute-start | bytes 3080 | tf_op jit(solution)/shard_map/ppermute | solution.py:482
  33.2 3.6 %collective-permute-start.9 = (f32[1,256]{1,0:T(1,128)S(1)}, f32[1,256]{1,0:T(1,128)S(1)}, u32[]{:S(2)}, u32[]{:S(2)}) collective-permute-start(f32[1,256]{1,0:T(1,128)S(1)} %get-tuple-element.44), channel_id=1, source_target_pairs={{0,2},{1,3},{2,0},{3,1},{4,6},{5,7},{6,4},{7,5},{8,10},{9,11},{10,... | collective-permute-start | bytes 3080 | tf_op jit(solution)/shard_map/ppermute | solution.py:482
  34.7 2.1 %collective-permute-start.8 = (f32[1,256]{1,0:T(1,128)S(1)}, f32[1,256]{1,0:T(1,128)S(1)}, u32[]{:S(2)}, u32[]{:S(2)}) collective-permute-start(f32[1,256]{1,0:T(1,128)S(1)} %get-tuple-element.44), channel_id=1, source_target_pairs={{0,1},{1,0},{2,3},{3,2},{4,5},{5,4},{6,7},{7,6},{8,9},{9,8},{10,11... | collective-permute-start | bytes 3080 | tf_op jit(solution)/shard_map/ppermute | solution.py:482
  36.8 3.6 %collective-permute-start.11 = (f32[1,256]{1,0:T(1,128)S(1)}, f32[1,256]{1,0:T(1,128)S(1)}, u32[]{:S(2)}, u32[]{:S(2)}) collective-permute-start(f32[1,256]{1,0:T(1,128)S(1)} %add_add_fusion.power_ref), channel_id=1, source_target_pairs={{0,4},{4,0},{8,12},{12,8},{16,20},{20,16},{24,28},{28,24},{1,5},{5... | collective-permute-start | bytes 3080 | tf_op jit(solution)/shard_map/ppermute | solution.py:20

commit v15 on v13

--- a/solution.py
+++ b/solution.py
@@ -149,12 +149,16 @@
     return first - 2 * BLK - start > BLK
 
 
-def tables_kernel(seq_ref, taps_ref, w_ref, out_ref, next_ref, w_half_ref, rev_ref, m_ref):
+def tables_kernel(seq_ref, taps_ref, w_ref, out_ref, next_ref, w_half_ref, marks_ref, rev_ref, m_ref):
     groups = out_ref.shape[0]
     taps = taps_ref.shape[1]
     span = out_ref.shape[3]
     half = lax.axis_index("half")
     start = lax.axis_index("blk") * (2 * BLK)
+    marks_ref[0], marks_ref[1] = edge_marks(seq_ref)
+    for ahead in range(2):
+        flag = reaches_past(seq_ref, lax.axis_index("blk") + ahead)
+        marks_ref[2 + ahead] = jnp.full((8, GROUP), flag.astype(jnp.float32))
     width = w_half_ref.shape[2]
     w_half_ref[...] = w_ref[:, :, pl.ds(pl.multiple_of(half * width, width), width)]
     turn = lax.broadcasted_iota(jnp.int32, (taps, span), 0) + lax.broadcasted_iota(
@@ -193,17 +197,17 @@
         at += piece.shape[1]
 
 
-def relay_kernel(piece, seq_ref, next_ref, back_own_ref, back_pair_ref, w_ref, out_ref, win_ref, extra_ref):
+def relay_kernel(piece, marks_ref, next_ref, back_own_ref, back_pair_ref, w_ref, out_ref, win_ref, extra_ref):
     width = out_ref.shape[1]
     half = lax.axis_index("half")
     lanes = slice(piece * width, (piece + 1) * width)
     fill(win_ref, extra_ref, half, back_own_ref.at[:, lanes])
     fill(win_ref, extra_ref, 1 - half, back_pair_ref)
-    marks = edge_marks(seq_ref)
+    marks = [marks_ref[0], marks_ref[1]]
     put_first_rows(win_ref, 0, first_rows(extra_ref[0], jnp.zeros((8, width), jnp.float32), w_ref, marks, 2, lanes))
     put_first_rows(win_ref, BLK, first_rows(extra_ref[1], extra_ref[0, :8], w_ref, marks, 3, lanes))
     out_ref[BLK:] = extra_ref[1, :8].astype(out_ref.dtype)
-    summed = reaches_past(seq_ref, lax.axis_index("blk") + 1)
+    summed = jnp.max(marks_ref[3]) > 0.5
 
     @pl.when(summed)
     def _():
@@ -234,20 +238,17 @@
 
 
 def near_kernel(
-    seq_ref, table_ref, own_ref, back_own_ref, pair_a_ref, pair_b_ref, back_a_ref, back_b_ref, qkept_ref, w_ref, bias_ref,
-    acc_ref, q_ref, marks_ref, win_ref, extra_ref, x_ref, m1_ref, m2_ref,
+    seq_ref, marks_ref, table_ref, own_ref, back_own_ref, pair_a_ref, pair_b_ref, back_a_ref, back_b_ref, qkept_ref, w_ref, bias_ref,
+    acc_ref, q_ref, win_ref, extra_ref, x_ref, m1_ref, m2_ref,
 ):
     groups = table_ref.shape[0]
     width = groups * GROUP
     half = lax.axis_index("half")
-    block = lax.axis_index("blk")
     fill(win_ref, extra_ref, half, back_own_ref)
     fill(win_ref, extra_ref, 1 - half, back_a_ref, back_b_ref)
     fill(win_ref, extra_ref, 2 + half, own_ref)
     fill(win_ref, extra_ref, 3 - half, pair_a_ref, pair_b_ref)
-    marks = edge_marks(seq_ref)
-    marks_ref[0], marks_ref[1] = marks
-    marks_ref[2] = jnp.full((8, GROUP), reaches_past(seq_ref, block).astype(jnp.float32))
+    marks = [marks_ref[0], marks_ref[1]]
     for spot in (1, 2, 3):
         rows = first_rows(extra_ref[spot], extra_ref[spot - 1, :8], w_ref, marks, spot + 2)
         put_first_rows(win_ref, spot * BLK, rows)
@@ -278,72 +279,86 @@
     gate_rows(seq_ref, raw_ref, tail, w_ref, 1 - half, q_ref, x_ref, m1_ref, m2_ref)
 
 
-def far_kernel(short, table_ref, acc_ref, qown_ref, qpair_ref, w_ref, marks_ref, *refs):
-    *messages, kept_ref, sent_ref, power_ref, win_ref, extra_ref = refs
-    groups = table_ref.shape[0]
-    width = groups * GROUP
-    half = lax.axis_index("half")
+def far_kernel(
+    short, piece, table_ref, acc_ref, qown_ref, qpair_ref, w_ref, marks_ref, back_own_ref, back_pair_ref, *refs
+):
+    *refs, kept_ref, sent_ref, total_ref, win_ref, extra_ref = refs
+    far_refs, before = refs[: len(refs) - 2 * piece], refs[len(refs) - 2 * piece :]
+    width = kept_ref.shape[1]
+    half = lax.axis_index("half")
+    lanes = slice(piece * width, (piece + 1) * width)
     marks = [marks_ref[0], marks_ref[1]]
-    back_own_ref, back_a_ref, back_b_ref, *far_refs = messages
     low = 1 if short else 0
-    fill(win_ref, extra_ref, 2 + half, back_own_ref)
-    fill(win_ref, extra_ref, 3 - half, back_a_ref, back_b_ref)
+
+    @pl.when(half == 0)
+    def _():
+        fill(win_ref, extra_ref, 2, back_own_ref.at[:, lanes])
+
+    @pl.when(half == 1)
+    def _():
+        fill(win_ref, extra_ref, 2, back_pair_ref)
+
     if short:
         summed = marks_ref[2, 0:1, 0:1]
-        fill(win_ref, extra_ref, 1, *far_refs)
+        fill(win_ref, extra_ref, 1, far_refs[0])
         payload = win_ref[BLK : 2 * BLK, :].astype(jnp.float32)
         win_ref[BLK : 2 * BLK, :] = (payload * (1.0 - summed)).astype(win_ref.dtype)
     else:
-        fill(win_ref, extra_ref, half, far_refs[0])
-        fill(win_ref, extra_ref, 1 - half, far_refs[1], far_refs[2])
-        ahead = far_refs[3][...].astype(jnp.float32)
-        put_first_rows(win_ref, 0, first_rows(extra_ref[0], ahead, w_ref, marks, 0))
-        rows = first_rows(extra_ref[1], extra_ref[0, :8], w_ref, marks, 1)
-        put_first_rows(win_ref, BLK, rows)
-    rows = first_rows(extra_ref[2], extra_ref[1, :8], w_ref, marks, 2)
-    put_first_rows(win_ref, 2 * BLK, rows)
-    for at, part, q_ref, out_ref in ((0, half, qown_ref, kept_ref), (BLK, 1 - half, qpair_ref, sent_ref)):
-        squares = jnp.zeros((BLK, GROUP), jnp.float32)
+        fill(win_ref, extra_ref, half, far_refs[0].at[:, lanes])
+        fill(win_ref, extra_ref, 1 - half, far_refs[1 + piece])
+        ahead = far_refs[3][:, lanes].astype(jnp.float32)
+        put_first_rows(win_ref, 0, first_rows(extra_ref[0], ahead, w_ref, marks, 0, lanes))
+        put_first_rows(win_ref, BLK, first_rows(extra_ref[1], extra_ref[0, :8], w_ref, marks, 1, lanes))
+    put_first_rows(win_ref, 2 * BLK, first_rows(extra_ref[2], extra_ref[1, :8], w_ref, marks, 2, lanes))
+    if before:
+        sent_ref[:, :width] = before[1][...]
+    for i, (part, q_ref, out_ref) in enumerate(((half, qown_ref, kept_ref), (1 - half, qpair_ref, sent_ref))):
+        part_sent = i == 1
+        squares = before[0][i] if before else jnp.zeros((BLK, GROUP), jnp.float32)
         rows = pl.ds(pl.multiple_of(part * BLK, BLK), BLK)
-        for g in range(groups):
-            lanes = slice(g * GROUP, (g + 1) * GROUP)
-            filtered = acc_ref[rows, lanes] + jnp.dot(
-                table_ref[g, part, :, low * BLK : 3 * BLK],
-                win_ref[low * BLK : 3 * BLK, lanes],
+        for c in range(0, width, GROUP):
+            here = slice(c, c + GROUP)
+            whole = slice(piece * width + c, piece * width + c + GROUP)
+            filtered = acc_ref[rows, whole] + jnp.dot(
+                table_ref[(piece * width + c) // GROUP, part, :, low * BLK : 3 * BLK],
+                win_ref[low * BLK : 3 * BLK, here],
                 preferred_element_type=jnp.float32,
             )
             if short:
                 weight = summed * (part == 0).astype(jnp.float32)
-                at_far = g * GROUP % far_refs[0].shape[1]
-                far_ref = far_refs[g * GROUP // far_refs[0].shape[1]]
-                filtered = filtered + weight * far_ref[:BLK, at_far : at_far + GROUP].astype(jnp.float32)
-            gated = q_ref[:, lanes] * filtered
+                filtered = filtered + weight * far_refs[0][:BLK, here].astype(jnp.float32)
+            gated = q_ref[:, whole] * filtered
             squares = squares + gated * gated
-            out_ref[:, lanes] = gated.astype(out_ref.dtype)
-        power_ref[:, at : at + BLK] = lax.dot_general(
-            jnp.ones((8, GROUP), jnp.float32),
-            squares,
-            (((1,), (1,)), ((), ())),
-            precision=lax.Precision.HIGHEST,
-            preferred_element_type=jnp.float32,
-        )[0:1]
-
-
-def norm_kernel(channels, power_ref, power_got_ref, kept_ref, got_ref, gain_ref, out_ref):
-    half = lax.axis_index("half")
-    width = kept_ref.shape[1]
+            out_ref[:, whole if before and part_sent else here] = gated.astype(out_ref.dtype)
+        if before:
+            total_ref[:, i * BLK : (i + 1) * BLK] = lax.dot_general(
+                jnp.ones((8, GROUP), jnp.float32),
+                squares,
+                (((1,), (1,)), ((), ())),
+                precision=lax.Precision.HIGHEST,
+                preferred_element_type=jnp.float32,
+            )[0:1]
+        else:
+            total_ref[i] = squares
+
+
+def norm_kernel(channels, power_ref, power_got_ref, *refs):
+    *kept_refs, got_ref, gain_ref, out_ref = refs
+    half = lax.axis_index("half")
     power = power_ref[:, :BLK] + power_got_ref[:, BLK:]
     scale = lax.rsqrt(power / channels + norm_eps)
     diagonal = lax.broadcasted_iota(jnp.int32, (BLK, BLK), 0) == lax.broadcasted_iota(
         jnp.int32, (BLK, BLK), 1
     )
     column = jnp.sum(jnp.where(diagonal, scale, 0.0), axis=1, keepdims=True)
-    for which, part_ref in ((half, kept_ref), (1 - half, got_ref)):
-        for c in range(0, width, GROUP):
-            lanes = pl.ds(pl.multiple_of(which * width + c, GROUP), GROUP)
-            out_ref[:, lanes] = (
-                part_ref[:, c : c + GROUP].astype(jnp.float32) * column * gain_ref[:, lanes]
-            ).astype(out_ref.dtype)
+    for at, refs in ((half, kept_refs), (1 - half, [got_ref])):
+        at = at * got_ref.shape[1]
+        for ref in refs:
+            for c in range(0, ref.shape[1], GROUP):
+                lanes = pl.ds(pl.multiple_of(at + c, GROUP), GROUP)
+                part = ref[:, c : c + GROUP].astype(jnp.float32)
+                out_ref[:, lanes] = (part * column * gain_ref[:, lanes]).astype(out_ref.dtype)
+            at = at + ref.shape[1]
 
 
 def kernel_call(body, outs, in_specs, scratch, flops, moved_bytes, vmem=24 << 20):
@@ -403,12 +418,13 @@
     filter_taps, _ = lax.optimization_barrier((filter_taps, kept))
     scaled = (filter_taps * jnp.repeat(tap_blocks.astype(jnp.float32), BLK, axis=1)).astype(jnp.bfloat16)
     span = taps + 2 * BLK
-    table, table_next, w_half = kernel_call(
+    table, table_next, w_half, marks = kernel_call(
         tables_kernel,
         (
             shape((groups, 2, BLK, span), jnp.bfloat16),
             shape((groups, BLK, 2 * BLK), jnp.bfloat16),
             shape((3, 3, width), jnp.float32),
+            shape((4, 8, GROUP), jnp.float32),
         ),
         [SMEM, VMEM, VMEM],
         [pltpu.VMEM((2 * groups, span), jnp.float32), pltpu.VMEM((3, BLK, span), jnp.float32)],
@@ -436,11 +452,11 @@
             relayed = kernel_call(
                 functools.partial(relay_kernel, piece),
                 small,
-                [SMEM] + [VMEM] * 4,
+                [VMEM] * 5,
                 [pltpu.VMEM((2 * rows, width // 2), jnp.bfloat16), pltpu.VMEM((2, 16, width // 2), jnp.float32)],
                 2 * rows * BLK * width,
                 4 * rows * width,
-            )(seq_lengths, table_next, back_own, back_pair[piece], w_half)
+            )(marks, table_next, back_own, back_pair[piece], w_half)
             far.append(moved(relayed, onward))
     else:
         across = jnp.concatenate([piece[rows:] for piece in sent], 1)
@@ -449,14 +465,14 @@
         deep = jnp.where(half == 1, straight, across)
         far = [moved(piece, ahead) for piece in (back_own, *back_pair)] + [deep]
 
-    acc, qown, marks = kernel_call(
+    acc, qown = kernel_call(
         near_kernel,
-        (shape((2 * rows, width), jnp.float32), half_wide, shape((3, 8, GROUP), jnp.float32)),
-        [SMEM] + [VMEM] * 10,
+        (shape((2 * rows, width), jnp.float32), half_wide),
+        [SMEM] + [VMEM] * 11,
         [window, extras, shifted, row_mask, row_mask],
         2 * 5 * rows * BLK * width,
         16 * rows * width,
-    )(seq_lengths, table, kept, back_own, *pair, *back_pair, qkept, w_half, skip_bias.reshape(1, -1))
+    )(seq_lengths, marks, table, kept, back_own, *pair, *back_pair, qkept, w_half, skip_bias.reshape(1, -1))
 
     qpair = kernel_call(
         pair_gate_kernel,
@@ -467,27 +483,36 @@
         8 * rows * width,
     )(seq_lengths, qgot, kept, back_own, w_half)
 
-    done, send, power = kernel_call(
-        functools.partial(far_kernel, short),
-        (half_wide, half_shape, shape((1, 2 * rows), jnp.float32)),
-        [VMEM] * (9 + len(far)),
-        [window, extras],
-        2 * 5 * rows * BLK * width,
-        24 * rows * width,
-    )(table, acc, qown, qpair, w_half, marks, back_own, *back_pair, *far)
-
+    done, power, send = [], None, None
+    for piece in range(2):
+        needed = far[piece : piece + 1] if short else far
+        before = [power, send] if piece else []
+        own, send, power = kernel_call(
+            functools.partial(far_kernel, short, piece),
+            (
+                shape((rows, width // 2), jnp.float32),
+                shape((rows, width if piece else width // 2), jnp.bfloat16),
+                shape((1, 2 * rows) if piece else (2, rows, GROUP), jnp.float32),
+            ),
+            [VMEM] * (8 + len(needed) + len(before)),
+            [pltpu.VMEM((3 * rows, width // 2), jnp.bfloat16), pltpu.VMEM((3, 16, width // 2), jnp.float32)],
+            2 * 3 * rows * BLK * width,
+            12 * rows * width,
+        )(table, acc, qown, qpair, w_half, marks, back_own, back_pair[piece], *needed, *before)
+        done.append(own)
     back = moved(send, to_pair)
+
     peers = lax.axis_size("mp")
     shares = [lax.ppermute(power, "mp", [(i, i ^ k) for i in range(peers)]) for k in range(1, peers)]
     power = sum(shares, power)
     return kernel_call(
         functools.partial(norm_kernel, channels),
         shape((rows, 2 * width), jnp.bfloat16),
-        [VMEM] * 5,
+        [VMEM] * 6,
         [],
         8 * rows * width,
         10 * rows * width,
-    )(power, moved(power, to_pair), done, back, norm_gain.reshape(1, -1))
+    )(power, moved(power, to_pair), *done, back, norm_gain.reshape(1, -1))
 
 
 def solution(mesh):

time: 39.2 us -> 38.8 us (0.990)
  Pallas kernels: 11.7 us -> 10.6 us
  waiting for transfers between devices: 11 us -> 12.1 us
  starting transfers between devices: 15 us -> 14.5 us
    pallas_call x3 -> x4, Pallas kernels: 2.53 us -> 1.38 us  [the longest x2 1.08 us: shards(): kernel_call(functools.partial(far_kernel, short, piece), (shape((rows, wi...]
    ppermute x10, waiting for transfers between devices: 9.27 us -> 10.4 us  [moved(): return lax.ppermute(block, SPOTS, pairs)]
    ppermute x10, starting transfers between devices: 13.1 us -> 12.7 us  [moved(): return lax.ppermute(block, SPOTS, pairs)]
  transfers between devices with their start and end apart: 13 -> 13, of which waited for: 8 -> 8; matrix products, arithmetic and copies ran while one was open for 3% -> 3% of each run, Pallas kernels for 17% -> 15%
where the time goes in v15:
time: 38.8 us; the launch traced here: 38.6 us
  starting transfers between devices  14.5 us (37%)
  waiting for transfers between devices  12.1 us (31%)
  Pallas kernels  10.6 us (27%)
  local copies, waits for them, and re-layouts  1.26 us (3%)
    ppermute x10, starting transfers between devices, moved(): return lax.ppermute(block, SPOTS, pairs)  12.7 us
    ppermute x10, waiting for transfers between devices, moved(): return lax.ppermute(block, SPOTS, pairs)  10.4 us
    pallas_call x1, Pallas kernels, shards(): kernel_call(products_kernel, (message, small, small), [hbm] * 3, [pltpu.S...  2.88 us
    pallas_call x1, Pallas kernels, shards(): kernel_call(tables_kernel, (shape((groups, 2, BLK, span), jnp.bfloat16),...  2.85 us
    ppermute x3, starting transfers between devices, shards(): lax.ppermute(power, 'mp', [(i, i ^ k) for i in range(peers)])  1.86 us
    ppermute x3, waiting for transfers between devices, shards(): lax.ppermute(power, 'mp', [(i, i ^ k) for i in range(peers)])  1.74 us
    pallas_call x1, Pallas kernels, shards(): kernel_call(near_kernel, (shape((2 * rows, width), jnp.float32), half_wid...  1.52 us
    pallas_call x2, Pallas kernels, shards(): kernel_call(functools.partial(far_kernel, short, piece), (shape((rows, wi...  1.08 us
  transfers between devices with their start and end apart: 13, of which 8 were waited for; matrix products, arithmetic and copies ran while one was open for 3% of the time, Pallas kernels for 15%

profile of v15, /device:TPU:0, one launch (start us, length us, event | category | flops | bytes accessed | tf_op | source)
XLA Modules:
  0.0 38.6 jit_solution(2595165659636867145)
XLA Ops:
  0.0 0.0 copy-start.2
  0.0 2.9 %shard_map.73 = (bf16[136,1024]{1,0:T(8,128)(2,1)}, bf16[136,512]{1,0:T(8,128)(2,1)}, bf16[136,512]{1,0:T(8,128)(2,1)}) custom-call(s32[32]{0:T(128)} %seq_ref.5, bf16[3,128,2048]{2,1,0:T(8,128)(2,1)} %bitcast.14, f32[3,3,2048]{2,1,0:T(4,128)} %w_ref.1), custom_call_target="tpu_custom_call" | custom-call | flops 5242880 | bytes 2097152 | tf_op jit(solution)/shard_map/pallas_call | solution.py:396
  2.9 3.0 %collective-permute-start = (bf16[136,512]{1,0:T(8,128)(2,1)}, bf16[136,512]{1,0:T(8,128)(2,1)S(1)}, u32[]{:S(2)}, u32[]{:S(2)}) collective-permute-start(bf16[136,512]{1,0:T(8,128)(2,1)} %get-tuple-element.32), channel_id=1, source_target_pairs={{0,4},{4,0},{8,12},{12,8},{16,20},{20,16},{24,28},{28,24},{1,5},{5... | collective-permute-start | bytes 417800 | tf_op jit(solution)/shard_map/ppermute | solution.py:20
  5.9 1.6 %collective-permute-start.1 = (bf16[136,1024]{1,0:T(8,128)(2,1)}, bf16[136,1024]{1,0:T(8,128)(2,1)S(1)}, u32[]{:S(2)}, u32[]{:S(2)}) collective-permute-start(bf16[136,1024]{1,0:T(8,128)(2,1)} %get-tuple-element.28.own_ref), channel_id=1, source_target_pairs={{0,8},{4,12},{8,16},{12,20},{16,24},{20,28},{24,0},{28,4},{1,9},{5... | collective-permute-start | bytes 835592 | tf_op jit(solution)/shard_map/ppermute | solution.py:20
  7.5 0.5 %collective-permute-start.2 = (bf16[136,512]{1,0:T(8,128)(2,1)}, bf16[136,512]{1,0:T(8,128)(2,1)S(1)}, u32[]{:S(2)}, u32[]{:S(2)}) collective-permute-start(bf16[136,512]{1,0:T(8,128)(2,1)} %get-tuple-element.37), channel_id=1, source_target_pairs={{0,4},{4,0},{8,12},{12,8},{16,20},{20,16},{24,28},{28,24},{1,5},{5... | collective-permute-start | bytes 417800 | tf_op jit(solution)/shard_map/ppermute | solution.py:20
  8.0 0.0 copy-done.6
  8.0 0.1 copy.8
  8.1 0.1 broadcast_in_dim.3
  8.2 0.0 copy-done.5
  8.2 0.0 copy-done.2
  8.2 0.0 copy-done.1
  8.2 2.9 %shard_map.74 = (bf16[8,2,128,768]{3,2,1,0:T(8,128)(2,1)S(1)}, bf16[8,128,256]{2,1,0:T(8,128)(2,1)S(1)}, f32[3,3,1024]{2,1,0:T(4,128)S(1)}, f32[4,8,128]{2,1,0:T(8,128)S(1)}) custom-call(s32[32]{0:T(128)S(1)} %copy-done.2, bf16[16,512]{1,0:T(8,128)(2,1)S(1)} %fusion.taps_ref, f32[3,3,2048]{2,1,0:T(4,128)S(1)} %copy-done.1), custom_call_target="tpu_custom_call" | custom-call | flops 20971520 | bytes 4194304 | tf_op jit(solution)/shard_map/pallas_call | solution.py:421
  11.1 0.0 collective-permute-done.pair_a_ref
  11.1 0.0 copy-start
  11.1 0.0 copy-start.3
  11.1 1.6 %collective-permute-start.3 = (bf16[136,512]{1,0:T(8,128)(2,1)S(1)}, bf16[136,512]{1,0:T(8,128)(2,1)S(1)}, u32[]{:S(2)}, u32[]{:S(2)}) collective-permute-start(bf16[136,512]{1,0:T(8,128)(2,1)S(1)} %collective-permute-done.pair_a_ref), channel_id=1, source_target_pairs={{0,8},{4,12},{8,16},{12,20},{16,24},{20,28},{24,0},{28,4},{1,9},{5... | collective-permute-start | bytes 417800 | tf_op jit(solution)/shard_map/ppermute | solution.py:20
  12.8 1.1 %dynamic-slice_bitcast_fusion = (bf16[128,1024]{1,0:T(8,128)(2,1)S(1)}, bf16[128,1024]{1,0:T(8,128)(2,1)S(1)}) fusion(bf16[3,128,2048]{2,1,0:T(8,128)(2,1)} %bitcast.15, s32[]{:T(128)S(6)} %select_n.7, s32[]{:T(128)S(6)} %select_n.6), kind=kLoop, calls=%fused_computation | loop fusion | bytes 1048584 | tf_op jit(solution)/shard_map/squeeze | solution.py:439
  13.8 0.0 collective-permute-done.2.pair_b_ref
  13.8 1.6 %collective-permute-start.4 = (bf16[136,512]{1,0:T(8,128)(2,1)S(1)}, bf16[136,512]{1,0:T(8,128)(2,1)S(1)}, u32[]{:S(2)}, u32[]{:S(2)}) collective-permute-start(bf16[136,512]{1,0:T(8,128)(2,1)S(1)} %collective-permute-done.2.pair_b_ref), channel_id=1, source_target_pairs={{0,8},{4,12},{8,16},{12,20},{16,24},{20,28},{24,0},{28,4},{1,9},{5... | collective-permute-start | bytes 417800 | tf_op jit(solution)/shard_map/ppermute | solution.py:20
  15.5 1.5 %collective-permute-start.5 = (bf16[128,1024]{1,0:T(8,128)(2,1)S(1)}, bf16[128,1024]{1,0:T(8,128)(2,1)S(1)}, u32[]{:S(2)}, u32[]{:S(2)}) collective-permute-start(bf16[128,1024]{1,0:T(8,128)(2,1)S(1)} %get-tuple-element.43), channel_id=1, source_target_pairs={{0,4},{4,0},{8,12},{12,8},{16,20},{20,16},{24,28},{28,24},{1,5},{5... | collective-permute-start | bytes 786440 | tf_op jit(solution)/shard_map/ppermute | solution.py:20
  17.0 0.5 %collective-permute-done.1.back_own_ref = bf16[136,1024]{1,0:T(8,128)(2,1)S(1)} collective-permute-done((bf16[136,1024]{1,0:T(8,128)(2,1)}, bf16[136,1024]{1,0:T(8,128)(2,1)S(1)}, u32[]{:S(2)}, u32[]{:S(2)}) %collective-permute-start.1) | collective-permute-done | bytes 278560 | tf_op jit(solution)/shard_map/ppermute | solution.py:20
  17.5 3.0 %collective-permute-done.3.back_a_ref.back_pair_ref = bf16[136,512]{1,0:T(8,128)(2,1)S(1)} collective-permute-done((bf16[136,512]{1,0:T(8,128)(2,1)S(1)}, bf16[136,512]{1,0:T(8,128)(2,1)S(1)}, u32[]{:S(2)}, u32[]{:S(2)}) %collective-permute-start.3) | collective-permute-done | bytes 139296 | tf_op jit(solution)/shard_map/ppermute | solution.py:20
  20.5 0.1 shard_map.78
  20.7 0.3 collective-permute-start.7
  21.0 2.5 %collective-permute-done.4.back_b_ref.back_pair_ref = bf16[136,512]{1,0:T(8,128)(2,1)S(1)} collective-permute-done((bf16[136,512]{1,0:T(8,128)(2,1)S(1)}, bf16[136,512]{1,0:T(8,128)(2,1)S(1)}, u32[]{:S(2)}, u32[]{:S(2)}) %collective-permute-start.4) | collective-permute-done | bytes 139296 | tf_op jit(solution)/shard_map/ppermute | solution.py:20
  23.5 0.1 shard_map.77
  23.6 0.3 collective-permute-start.6
  24.0 0.0 copy-done
  24.0 0.0 copy-done.3
  24.0 1.5 %shard_map.75 = (f32[256,1024]{1,0:T(8,128)S(1)}, f32[128,1024]{1,0:T(8,128)S(1)}) custom-call(s32[32]{0:T(128)S(1)} %copy-done.2, f32[4,8,128]{2,1,0:T(8,128)S(1)} %get-tuple-element.34.marks_ref, bf16[8,2,128,768]{3,2,1,0:T(8,128)(2,1)S(1)} %get-tuple-element.33.table_ref, bf16[136,1024]{1,0:T(8,128)(2,1)S(1)} %copy-done, ...), custom_call_target="tpu_custom_call" | custom-call | flops 167772160 | bytes 2097152 | tf_op jit(solution)/shard_map/pallas_call | solution.py:468
  25.5 0.0 collective-permute-done.5.raw_ref
  25.5 0.9 %shard_map.76.qpair_ref = f32[128,1024]{1,0:T(8,128)S(1)} custom-call(s32[32]{0:T(128)S(1)} %copy-done.2, bf16[128,1024]{1,0:T(8,128)(2,1)S(1)} %collective-permute-done.5.raw_ref, bf16[136,1024]{1,0:T(8,128)(2,1)S(1)} %copy-done, bf16[136,1024]{1,0:T(8,128)(2,1)S(1)} %collective-permute-done.1.back_own_ref, f32[3,3,1024]{2,1,0:T(4,128)S(1)} %get-tuple-element.40.w_ref), custom_call_target="tpu_custom_call" | custom-call | flops 1310720 | bytes 1048576 | tf_op jit(solution)/shard_map/pallas_call | solution.py:477
  26.4 0.2 collective-permute-done.7.refs_0_
  26.6 0.4 %shard_map.79 = (f32[128,512]{1,0:T(8,128)S(1)}, bf16[128,512]{1,0:T(8,128)(2,1)S(1)}, f32[2,128,128]{2,1,0:T(8,128)S(1)}) custom-call(bf16[8,2,128,768]{3,2,1,0:T(8,128)(2,1)S(1)} %get-tuple-element.33.table_ref, f32[256,1024]{1,0:T(8,128)S(1)} %get-tuple-element.41.acc_ref, f32[128,1024]{1,0:T(8,128)S(1)} %get-tuple-element.42.qown_ref, ...), custom_call_target="tpu_custom_call" | custom-call | flops 100663296 | bytes 1572864 | tf_op jit(solution)/shard_map/pallas_call | solution.py:490
  27.0 1.8 %collective-permute-done.6.refs_0_ = bf16[136,512]{1,0:T(8,128)(2,1)S(1)} collective-permute-done((bf16[136,512]{1,0:T(8,128)(2,1)S(1)}, bf16[136,512]{1,0:T(8,128)(2,1)S(1)}, u32[]{:S(2)}, u32[]{:S(2)}) %collective-permute-start.6) | collective-permute-done | bytes 139296 | tf_op jit(solution)/shard_map/ppermute | solution.py:20
  28.8 0.7 %shard_map.80 = (f32[128,512]{1,0:T(8,128)S(1)}, bf16[128,1024]{1,0:T(8,128)(2,1)S(1)}, f32[1,256]{1,0:T(1,128)S(1)}) custom-call(bf16[8,2,128,768]{3,2,1,0:T(8,128)(2,1)S(1)} %get-tuple-element.33.table_ref, f32[256,1024]{1,0:T(8,128)S(1)} %get-tuple-element.41.acc_ref, f32[128,1024]{1,0:T(8,128)S(1)} %get-tuple-element.42.qown_ref, ...), custom_call_target="tpu_custom_call" | custom-call | flops 100663296 | bytes 1572864 | tf_op jit(solution)/shard_map/pallas_call | solution.py:490
  29.4 0.9 %collective-permute-start.12 = (bf16[128,1024]{1,0:T(8,128)(2,1)S(1)}, bf16[128,1024]{1,0:T(8,128)(2,1)S(1)}, u32[]{:S(2)}, u32[]{:S(2)}) collective-permute-start(bf16[128,1024]{1,0:T(8,128)(2,1)S(1)} %get-tuple-element.50), channel_id=1, source_target_pairs={{0,4},{4,0},{8,12},{12,8},{16,20},{20,16},{24,28},{28,24},{1,5},{5... | collective-permute-start | bytes 786440 | tf_op jit(solution)/shard_map/ppermute | solution.py:20
  30.3 0.0 collective-permute-start.10
  30.3 1.5 %collective-permute-start.9 = (f32[1,256]{1,0:T(1,128)S(1)}, f32[1,256]{1,0:T(1,128)S(1)}, u32[]{:S(2)}, u32[]{:S(2)}) collective-permute-start(f32[1,256]{1,0:T(1,128)S(1)} %get-tuple-element.47), channel_id=1, source_target_pairs={{0,2},{1,3},{2,0},{3,1},{4,6},{5,7},{6,4},{7,5},{8,10},{9,11},{10,... | collective-permute-start | bytes 3080 | tf_op jit(solution)/shard_map/ppermute | solution.py:506
  31.8 0.3 collective-permute-start.8
  32.2 1.1 %collective-permute-done.10 = f32[1,256]{1,0:T(1,128)S(1)} collective-permute-done((f32[1,256]{1,0:T(1,128)S(1)}, f32[1,256]{1,0:T(1,128)S(1)}, u32[]{:S(2)}, u32[]{:S(2)}) %collective-permute-start.10) | collective-permute-done | bytes 1056 | tf_op jit(solution)/shard_map/ppermute | solution.py:506
  33.3 0.6 %collective-permute-done.9 = f32[1,256]{1,0:T(1,128)S(1)} collective-permute-done((f32[1,256]{1,0:T(1,128)S(1)}, f32[1,256]{1,0:T(1,128)S(1)}, u32[]{:S(2)}, u32[]{:S(2)}) %collective-permute-start.9) | collective-permute-done | bytes 1056 | tf_op jit(solution)/shard_map/ppermute | solution.py:506
  33.9 0.0 collective-permute-done.8
  33.9 1.2 %collective-permute-start.11 = (f32[1,256]{1,0:T(1,128)S(1)}, f32[1,256]{1,0:T(1,128)S(1)}, u32[]{:S(2)}, u32[]{:S(2)}) collective-permute-start(f32[1,256]{1,0:T(1,128)S(1)} %add_add_fusion.power_ref), channel_id=1, source_target_pairs={{0,4},{4,0},{8,12},{12,8},{16,20},{20,16},{24,28},{28,24},{1,5},{5... | collective-permute-start | bytes 3080 | tf_op jit(solution)/shard_map/ppermute | solution.py:20
  35.2 2.4 %collective-permute-done.11.power_got_ref = f32[1,256]{1,0:T(1,128)S(1)} collective-permute-done((f32[1,256]{1,0:T(1,128)S(1)}, f32[1,256]{1,0:T(1,128)S(1)}, u32[]{:S(2)}, u32[]{:S(2)}) %collective-permute-start.11) | collective-permute-done | bytes 1056 | tf_op jit(solution)/shard_map/ppermute | solution.py:20
  37.6 0.0 collective-permute-done.12.refs_2_
  37.6 0.0 copy-done.4
  37.6 1.0 %shard_map.81 = bf16[128,2048]{1,0:T(8,128)(2,1)} custom-call(f32[1,256]{1,0:T(1,128)S(1)} %add_add_fusion.power_ref, f32[1,256]{1,0:T(1,128)S(1)} %collective-permute-done.11.power_got_ref, f32[128,512]{1,0:T(8,128)S(1)} %get-tuple-element.48.refs_0_, f32[128,512]{1,0:T(8,128)S(1)} %get-tuple-element.49.refs_1_, ...), custom_call_target="tpu_custom_call" | custom-call | flops 1048576 | bytes 1310720 | tf_op jit(solution)/shard_map/pallas_call | solution.py:508
  (7 shorter events, 0.0 us)
Async XLA Ops:
  0.0 8.2 %copy-start.2 = (s32[32]{0:T(128)S(1)}, s32[32]{0:T(128)}, u32[]{:S(2)}) copy-start(s32[32]{0:T(128)} %seq_ref.5) | copy-start | bytes 388
  0.0 8.2 %copy-start.1 = (f32[3,3,2048]{2,1,0:T(4,128)S(1)}, f32[3,3,2048]{2,1,0:T(4,128)}, u32[]{:S(2)}) copy-start(f32[3,3,2048]{2,1,0:T(4,128)} %w_ref.1) | copy-start | bytes 221188
  0.0 8.2 %copy-start.5 = (f32[16,512]{1,0:T(8,128)S(1)}, f32[16,512]{1,0:T(8,128)}, u32[]{:S(2)}) copy-start(f32[16,512]{1,0:T(8,128)} %param.9) | copy-start | bytes 98308
  0.0 8.0 %copy-start.6 = (s32[16,4]{0,1:T(4,128)S(1)}, s32[16,4]{0,1:T(4,128)}, u32[]{:S(2)}) copy-start(s32[16,4]{0,1:T(4,128)} %param.10) | copy-start | bytes 772
  2.9 8.2 %collective-permute-start = (bf16[136,512]{1,0:T(8,128)(2,1)}, bf16[136,512]{1,0:T(8,128)(2,1)S(1)}, u32[]{:S(2)}, u32[]{:S(2)}) collective-permute-start(bf16[136,512]{1,0:T(8,128)(2,1)} %get-tuple-element.32), channel_id=1, source_target_pairs={{0,4},{4,0},{8,12},{12,8},{16,20},{20,16},{24,28},{28,24},{1,5},{5... | collective-permute-start | bytes 417800 | tf_op jit(solution)/shard_map/ppermute | solution.py:20
  5.9 11.6 %collective-permute-start.1 = (bf16[136,1024]{1,0:T(8,128)(2,1)}, bf16[136,1024]{1,0:T(8,128)(2,1)S(1)}, u32[]{:S(2)}, u32[]{:S(2)}) collective-permute-start(bf16[136,1024]{1,0:T(8,128)(2,1)} %get-tuple-element.28.own_ref), channel_id=1, source_target_pairs={{0,8},{4,12},{8,16},{12,20},{16,24},{20,28},{24,0},{28,4},{1,9},{5... | collective-permute-start | bytes 835592 | tf_op jit(solution)/shard_map/ppermute | solution.py:20
  7.5 6.3 %collective-permute-start.2 = (bf16[136,512]{1,0:T(8,128)(2,1)}, bf16[136,512]{1,0:T(8,128)(2,1)S(1)}, u32[]{:S(2)}, u32[]{:S(2)}) collective-permute-start(bf16[136,512]{1,0:T(8,128)(2,1)} %get-tuple-element.37), channel_id=1, source_target_pairs={{0,4},{4,0},{8,12},{12,8},{16,20},{20,16},{24,28},{28,24},{1,5},{5... | collective-permute-start | bytes 417800 | tf_op jit(solution)/shard_map/ppermute | solution.py:20
  11.1 12.9 %copy-start = (bf16[136,1024]{1,0:T(8,128)(2,1)S(1)}, bf16[136,1024]{1,0:T(8,128)(2,1)}, u32[]{:S(2)}) copy-start(bf16[136,1024]{1,0:T(8,128)(2,1)} %get-tuple-element.28.own_ref) | copy-start | bytes 835588
  11.1 12.9 %copy-start.3 = (f32[2048]{0:T(1024)S(1)}, f32[2048]{0:T(1024)}, u32[]{:S(2)}) copy-start(f32[2048]{0:T(1024)} %param.11) | copy-start | bytes 24580
  11.1 9.4 %collective-permute-start.3 = (bf16[136,512]{1,0:T(8,128)(2,1)S(1)}, bf16[136,512]{1,0:T(8,128)(2,1)S(1)}, u32[]{:S(2)}, u32[]{:S(2)}) collective-permute-start(bf16[136,512]{1,0:T(8,128)(2,1)S(1)} %collective-permute-done.pair_a_ref), channel_id=1, source_target_pairs={{0,8},{4,12},{8,16},{12,20},{16,24},{20,28},{24,0},{28,4},{1,9},{5... | collective-permute-start | bytes 417800 | tf_op jit(solution)/shard_map/ppermute | solution.py:20
  13.8 9.6 %collective-permute-start.4 = (bf16[136,512]{1,0:T(8,128)(2,1)S(1)}, bf16[136,512]{1,0:T(8,128)(2,1)S(1)}, u32[]{:S(2)}, u32[]{:S(2)}) collective-permute-start(bf16[136,512]{1,0:T(8,128)(2,1)S(1)} %collective-permute-done.2.pair_b_ref), channel_id=1, source_target_pairs={{0,8},{4,12},{8,16},{12,20},{16,24},{20,28},{24,0},{28,4},{1,9},{5... | collective-permute-start | bytes 417800 | tf_op jit(solution)/shard_map/ppermute | solution.py:20
  15.5 10.0 %collective-permute-start.5 = (bf16[128,1024]{1,0:T(8,128)(2,1)S(1)}, bf16[128,1024]{1,0:T(8,128)(2,1)S(1)}, u32[]{:S(2)}, u32[]{:S(2)}) collective-permute-start(bf16[128,1024]{1,0:T(8,128)(2,1)S(1)} %get-tuple-element.43), channel_id=1, source_target_pairs={{0,4},{4,0},{8,12},{12,8},{16,20},{20,16},{24,28},{28,24},{1,5},{5... | collective-permute-start | bytes 786440 | tf_op jit(solution)/shard_map/ppermute | solution.py:20
  20.7 5.9 %collective-permute-start.7 = (bf16[136,512]{1,0:T(8,128)(2,1)S(1)}, bf16[136,512]{1,0:T(8,128)(2,1)S(1)}, u32[]{:S(2)}, u32[]{:S(2)}) collective-permute-start(bf16[136,512]{1,0:T(8,128)(2,1)S(1)} %shard_map.78), channel_id=1, source_target_pairs={{0,4},{4,0},{8,16},{12,20},{16,24},{20,28},{24,8},{28,12},{1,5},{5... | collective-permute-start | bytes 417800 | tf_op jit(solution)/shard_map/ppermute | solution.py:20
  23.6 5.1 %collective-permute-start.6 = (bf16[136,512]{1,0:T(8,128)(2,1)S(1)}, bf16[136,512]{1,0:T(8,128)(2,1)S(1)}, u32[]{:S(2)}, u32[]{:S(2)}) collective-permute-start(bf16[136,512]{1,0:T(8,128)(2,1)S(1)} %shard_map.77), channel_id=1, source_target_pairs={{0,4},{4,0},{8,16},{12,20},{16,24},{20,28},{24,8},{28,12},{1,5},{5... | collective-permute-start | bytes 417800 | tf_op jit(solution)/shard_map/ppermute | solution.py:20
  28.8 8.8 %copy-start.4 = (f32[2048]{0:T(1024)S(1)}, f32[2048]{0:T(1024)}, u32[]{:S(2)}) copy-start(f32[2048]{0:T(1024)} %param.12) | copy-start | bytes 24580
  29.4 8.1 %collective-permute-start.12 = (bf16[128,1024]{1,0:T(8,128)(2,1)S(1)}, bf16[128,1024]{1,0:T(8,128)(2,1)S(1)}, u32[]{:S(2)}, u32[]{:S(2)}) collective-permute-start(bf16[128,1024]{1,0:T(8,128)(2,1)S(1)} %get-tuple-element.50), channel_id=1, source_target_pairs={{0,4},{4,0},{8,12},{12,8},{16,20},{20,16},{24,28},{28,24},{1,5},{5... | collective-permute-start | bytes 786440 | tf_op jit(solution)/shard_map/ppermute | solution.py:20
  30.3 3.0 %collective-permute-start.10 = (f32[1,256]{1,0:T(1,128)S(1)}, f32[1,256]{1,0:T(1,128)S(1)}, u32[]{:S(2)}, u32[]{:S(2)}) collective-permute-start(f32[1,256]{1,0:T(1,128)S(1)} %get-tuple-element.47), channel_id=1, source_target_pairs={{0,3},{1,2},{2,1},{3,0},{4,7},{5,6},{6,5},{7,4},{8,11},{9,10},{10,... | collective-permute-start | bytes 3080 | tf_op jit(solution)/shard_map/ppermute | solution.py:506
  30.3 3.6 %collective-permute-start.9 = (f32[1,256]{1,0:T(1,128)S(1)}, f32[1,256]{1,0:T(1,128)S(1)}, u32[]{:S(2)}, u32[]{:S(2)}) collective-permute-start(f32[1,256]{1,0:T(1,128)S(1)} %get-tuple-element.47), channel_id=1, source_target_pairs={{0,2},{1,3},{2,0},{3,1},{4,6},{5,7},{6,4},{7,5},{8,10},{9,11},{10,... | collective-permute-start | bytes 3080 | tf_op jit(solution)/shard_map/ppermute | solution.py:506
  31.8 2.1 %collective-permute-start.8 = (f32[1,256]{1,0:T(1,128)S(1)}, f32[1,256]{1,0:T(1,128)S(1)}, u32[]{:S(2)}, u32[]{:S(2)}) collective-permute-start(f32[1,256]{1,0:T(1,128)S(1)} %get-tuple-element.47), channel_id=1, source_target_pairs={{0,1},{1,0},{2,3},{3,2},{4,5},{5,4},{6,7},{7,6},{8,9},{9,8},{10,11... | collective-permute-start | bytes 3080 | tf_op jit(solution)/shard_map/ppermute | solution.py:506
  33.9 3.6 %collective-permute-start.11 = (f32[1,256]{1,0:T(1,128)S(1)}, f32[1,256]{1,0:T(1,128)S(1)}, u32[]{:S(2)}, u32[]{:S(2)}) collective-permute-start(f32[1,256]{1,0:T(1,128)S(1)} %add_add_fusion.power_ref), channel_id=1, source_target_pairs={{0,4},{4,0},{8,12},{12,8},{16,20},{20,16},{24,28},{28,24},{1,5},{5... | collective-permute-start | bytes 3080 | tf_op jit(solution)/shard_map/ppermute | solution.py:20

commit v16 on v15

--- a/solution.py
+++ b/solution.py
@@ -32,14 +32,20 @@
     return first, first | second
 
 
-def row_masks(seq_ref, start, m1_ref, m2_ref):
-    rows = lax.broadcasted_iota(jnp.int32, (BLK, GROUP), 0)
-    diagonal = rows == lax.broadcasted_iota(jnp.int32, (BLK, GROUP), 1)
-    marks = boundaries(seq_ref, start + lax.broadcasted_iota(jnp.int32, (8, GROUP), 1))
-    for mark, m_ref in zip(marks, (m1_ref, m2_ref)):
-        keep = 1.0 - mark.astype(jnp.float32)[0:1]
+def row_masks(lengths_ref, start, m1_ref, m2_ref):
+    count = lengths_ref.shape[1]
+    square = (count, count)
+    upto = lax.broadcasted_iota(jnp.int32, square, 1) <= lax.broadcasted_iota(jnp.int32, square, 0)
+    lengths = jnp.broadcast_to(lengths_ref[...].astype(jnp.float32), square)
+    ends = jnp.sum(jnp.where(upto, lengths, 0.0), axis=1, keepdims=True)
+    t = (start + lax.broadcasted_iota(jnp.int32, (count, BLK), 1)).astype(jnp.float32)
+    opens = (t == ends) | (t == 0.0)
+    after = opens | (t - 1.0 == ends) | (t == 1.0)
+    diagonal = lax.broadcasted_iota(jnp.int32, (BLK, BLK), 0) == lax.broadcasted_iota(jnp.int32, (BLK, BLK), 1)
+    for mark, m_ref in ((opens, m1_ref), (after, m2_ref)):
+        keep = 1.0 - jnp.max(mark.astype(jnp.float32), axis=0, keepdims=True)
         column = jnp.sum(jnp.where(diagonal, keep, 0.0), axis=1, keepdims=True)
-        m_ref[...] = jnp.broadcast_to(column, (BLK, GROUP))
+        m_ref[...] = jnp.broadcast_to(column, m_ref.shape)
 
 
 def counted(seq_ref, t):
@@ -63,8 +69,9 @@
     )
 
 
-def products_kernel(seq_hbm, panels_hbm, w_hbm, kept_ref, *refs):
-    *sent_refs, seq_ref, kv_ref, q_ref, w_ref, x_ref, m1_ref, m2_ref, sems = refs
+def products_kernel(seq_hbm, panels_hbm, w_hbm, *refs):
+    outs, (kept_ref, *sent_refs), refs = refs[:3], refs[3:6], refs[6:]
+    seq_ref, kv_ref, q_ref, w_ref, x_ref, m1_ref, m2_ref, sems = refs
     width = kept_ref.shape[1]
     rows = kv_ref.shape[2]
     pieces = kv_ref.shape[0]
@@ -88,6 +95,7 @@
     row_masks(seq_ref, shard * rows, m1_ref, m2_ref)
     loads[1 + pieces].wait()
     loads[2 + pieces].wait()
+    stores = []
     for p in range(pieces):
         loads[1 + p].wait()
         out_ref, at = (kept_ref, keep_at) if p < pieces // 2 else (sent_refs[p - pieces // 2], send_at)
@@ -107,6 +115,12 @@
             out_ref[:rows, there] = jnp.concatenate([top, product[8:]], 0).astype(out_ref.dtype)
             tails = [x[rows - 2 :] for x in raw] + [q_ref[:, lanes].astype(jnp.float32)[14:]]
             out_ref[rows:, there] = jnp.concatenate([raw[1][0:2]] + tails, 0).astype(out_ref.dtype)
+        if p >= pieces // 2 - 1:
+            done = p - pieces // 2 + 1
+            stores.append(pltpu.make_async_copy(out_ref, outs[done], sems.at[3 + pieces + done]))
+            stores[-1].start()
+    for store in stores:
+        store.wait()
 
 
 def edge_marks(seq_ref):
@@ -361,12 +375,12 @@
             at = at + ref.shape[1]
 
 
-def kernel_call(body, outs, in_specs, scratch, flops, moved_bytes, vmem=24 << 20):
+def kernel_call(body, outs, in_specs, scratch, flops, moved_bytes, vmem=24 << 20, out_space=VMEM):
     return pl.pallas_call(
         body,
         out_shape=outs,
         in_specs=in_specs,
-        out_specs=jax.tree.map(lambda _: VMEM, outs),
+        out_specs=jax.tree.map(lambda _: out_space, outs),
         scratch_shapes=scratch,
         compiler_params=pltpu.CompilerParams(vmem_limit_bytes=vmem),
         cost_estimate=pl.CostEstimate(flops=flops, bytes_accessed=moved_bytes, transcendentals=0),
@@ -391,6 +405,7 @@
     small = shape((rows + 8, width // 2), jnp.bfloat16)
     hbm = pl.BlockSpec(memory_space=pltpu.HBM)
     pieces = 4
+    lengths = seq_lengths.reshape(1, -1)
     row_mask = pltpu.VMEM((rows, GROUP), jnp.float32)
 
     kept, *sent = kernel_call(
@@ -398,19 +413,23 @@
         (message, small, small),
         [hbm] * 3,
         [
-            pltpu.SMEM(seq_lengths.shape, jnp.int32),
+            pltpu.VMEM(message.shape, message.dtype),
+            pltpu.VMEM(small.shape, small.dtype),
+            pltpu.VMEM(small.shape, small.dtype),
+            pltpu.VMEM(lengths.shape, jnp.int32),
             pltpu.VMEM((pieces, 2, rows, 2 * width // pieces), jnp.bfloat16),
             pltpu.VMEM((16, 2 * width), jnp.bfloat16),
             pltpu.VMEM(short_weight.shape, jnp.float32),
             pltpu.VMEM((4, rows + 8, GROUP), jnp.float32),
             row_mask,
             row_mask,
-            pltpu.SemaphoreType.DMA((3 + pieces,)),
+            pltpu.SemaphoreType.DMA((6 + pieces,)),
         ],
         40 * rows * width,
         16 * rows * width,
         60 << 20,
-    )(seq_lengths, panels, short_weight)
+        hbm,
+    )(lengths, panels, short_weight)
 
     back_own = moved(kept, ahead)
     pair = [moved(piece, to_pair) for piece in sent]
@@ -468,20 +487,20 @@
     acc, qown = kernel_call(
         near_kernel,
         (shape((2 * rows, width), jnp.float32), half_wide),
-        [SMEM] + [VMEM] * 11,
+        [VMEM] * 12,
         [window, extras, shifted, row_mask, row_mask],
         2 * 5 * rows * BLK * width,
         16 * rows * width,
-    )(seq_lengths, marks, table, kept, back_own, *pair, *back_pair, qkept, w_half, skip_bias.reshape(1, -1))
+    )(lengths, marks, table, kept, back_own, *pair, *back_pair, qkept, w_half, skip_bias.reshape(1, -1))
 
     qpair = kernel_call(
         pair_gate_kernel,
         half_wide,
-        [SMEM] + [VMEM] * 4,
+        [VMEM] * 5,
         [shifted, row_mask, row_mask],
         10 * rows * width,
         8 * rows * width,
-    )(seq_lengths, qgot, kept, back_own, w_half)
+    )(lengths, qgot, kept, back_own, w_half)
 
     done, power, send = [], None, None
     for piece in range(2):

time: 38.8 us -> 38.8 us (level)
  Pallas kernels: 10.6 us -> 9.52 us
  waiting for transfers between devices: 12.1 us -> 13 us
    ppermute x10, waiting for transfers between devices: 10.4 us -> 11.2 us  [moved(): return lax.ppermute(block, SPOTS, pairs)]
    pallas_call x1, Pallas kernels: 1.52 us -> 0.97 us  [shards(): kernel_call(near_kernel, (shape((2 * rows, width), jnp.float32), half_wid...]
    pallas_call x2, Pallas kernels: 3.75 us -> 3.29 us  [the longest x1 2.91 us: shards(): kernel_call(products_kernel, (message, small, small), [hbm] * 3, [pltpu.V...]
  transfers between devices with their start and end apart: 13 -> 13, of which waited for: 8 -> 8; matrix products, arithmetic and copies ran while one was open for 3% -> 3% of each run, Pallas kernels for 15% -> 13%
where the time goes in v16:
time: 38.8 us; the launch traced here: 38.6 us
  starting transfers between devices  14.7 us (38%)
  waiting for transfers between devices  13 us (34%)
  Pallas kernels  9.52 us (25%)
  local copies, waits for them, and re-layouts  1.26 us (3%)
    ppermute x10, starting transfers between devices, moved(): return lax.ppermute(block, SPOTS, pairs)  12.9 us
    ppermute x10, waiting for transfers between devices, moved(): return lax.ppermute(block, SPOTS, pairs)  11.2 us
    pallas_call x1, Pallas kernels, shards(): kernel_call(products_kernel, (message, small, small), [hbm] * 3, [pltpu.V...  2.91 us
    pallas_call x1, Pallas kernels, shards(): kernel_call(tables_kernel, (shape((groups, 2, BLK, span), jnp.bfloat16),...  2.85 us
    ppermute x3, starting transfers between devices, shards(): lax.ppermute(power, 'mp', [(i, i ^ k) for i in range(peers)])  1.86 us
    ppermute x3, waiting for transfers between devices, shards(): lax.ppermute(power, 'mp', [(i, i ^ k) for i in range(peers)])  1.74 us
    pallas_call x2, Pallas kernels, shards(): kernel_call(functools.partial(far_kernel, short, piece), (shape((rows, wi...  1.07 us
    squeeze x1, local copies, waits for them, and re-layouts, shards(): lax.dynamic_slice(query, (0, 0, (1 - half) * width), (1, rows, width))[0]  1.06 us
  transfers between devices with their start and end apart: 13, of which 8 were waited for; matrix products, arithmetic and copies ran while one was open for 3% of the time, Pallas kernels for 13%

profile of v16, /device:TPU:0, one launch (start us, length us, event | category | flops | bytes accessed | tf_op | source)
XLA Modules:
  0.0 38.6 jit_solution(12804721031143466020)
XLA Ops:
  0.0 0.0 copy-start.2
  0.0 2.9 %shard_map.73 = (bf16[136,1024]{1,0:T(8,128)(2,1)}, bf16[136,512]{1,0:T(8,128)(2,1)}, bf16[136,512]{1,0:T(8,128)(2,1)}) custom-call(s32[1,32]{1,0:T(1,128)} %bitcast.13, bf16[3,128,2048]{2,1,0:T(8,128)(2,1)} %bitcast.18, f32[3,3,2048]{2,1,0:T(4,128)} %w_ref.1), custom_call_target="tpu_custom_call" | custom-call | flops 5242880 | bytes 2097152 | tf_op jit(solution)/shard_map/pallas_call | solution.py:411
  2.9 3.0 %collective-permute-start = (bf16[136,512]{1,0:T(8,128)(2,1)}, bf16[136,512]{1,0:T(8,128)(2,1)S(1)}, u32[]{:S(2)}, u32[]{:S(2)}) collective-permute-start(bf16[136,512]{1,0:T(8,128)(2,1)} %get-tuple-element.32), channel_id=1, source_target_pairs={{0,4},{4,0},{8,12},{12,8},{16,20},{20,16},{24,28},{28,24},{1,5},{5... | collective-permute-start | bytes 417800 | tf_op jit(solution)/shard_map/ppermute | solution.py:20
  6.0 1.6 %collective-permute-start.1 = (bf16[136,1024]{1,0:T(8,128)(2,1)}, bf16[136,1024]{1,0:T(8,128)(2,1)S(1)}, u32[]{:S(2)}, u32[]{:S(2)}) collective-permute-start(bf16[136,1024]{1,0:T(8,128)(2,1)} %get-tuple-element.28.own_ref), channel_id=1, source_target_pairs={{0,8},{4,12},{8,16},{12,20},{16,24},{20,28},{24,0},{28,4},{1,9},{5... | collective-permute-start | bytes 835592 | tf_op jit(solution)/shard_map/ppermute | solution.py:20
  7.6 0.5 %collective-permute-start.2 = (bf16[136,512]{1,0:T(8,128)(2,1)}, bf16[136,512]{1,0:T(8,128)(2,1)S(1)}, u32[]{:S(2)}, u32[]{:S(2)}) collective-permute-start(bf16[136,512]{1,0:T(8,128)(2,1)} %get-tuple-element.37), channel_id=1, source_target_pairs={{0,4},{4,0},{8,12},{12,8},{16,20},{20,16},{24,28},{28,24},{1,5},{5... | collective-permute-start | bytes 417800 | tf_op jit(solution)/shard_map/ppermute | solution.py:20
  8.1 0.0 copy-done.6
  8.1 0.1 copy.8
  8.2 0.1 broadcast_in_dim.3
  8.2 0.0 copy-done.5
  8.3 0.0 copy-done.2
  8.3 0.0 copy-done.1
  8.3 2.9 %shard_map.74 = (bf16[8,2,128,768]{3,2,1,0:T(8,128)(2,1)S(1)}, bf16[8,128,256]{2,1,0:T(8,128)(2,1)S(1)}, f32[3,3,1024]{2,1,0:T(4,128)S(1)}, f32[4,8,128]{2,1,0:T(8,128)S(1)}) custom-call(s32[32]{0:T(128)S(1)} %copy-done.2, bf16[16,512]{1,0:T(8,128)(2,1)S(1)} %fusion.taps_ref, f32[3,3,2048]{2,1,0:T(4,128)S(1)} %copy-done.1), custom_call_target="tpu_custom_call" | custom-call | flops 20971520 | bytes 4194304 | tf_op jit(solution)/shard_map/pallas_call | solution.py:440
  11.1 0.0 collective-permute-done.pair_a_ref
  11.1 0.0 copy-start
  11.2 0.0 copy-start.3
  11.2 1.6 %collective-permute-start.3 = (bf16[136,512]{1,0:T(8,128)(2,1)S(1)}, bf16[136,512]{1,0:T(8,128)(2,1)S(1)}, u32[]{:S(2)}, u32[]{:S(2)}) collective-permute-start(bf16[136,512]{1,0:T(8,128)(2,1)S(1)} %collective-permute-done.pair_a_ref), channel_id=1, source_target_pairs={{0,8},{4,12},{8,16},{12,20},{16,24},{20,28},{24,0},{28,4},{1,9},{5... | collective-permute-start | bytes 417800 | tf_op jit(solution)/shard_map/ppermute | solution.py:20
  12.8 1.1 %dynamic-slice_bitcast_fusion = (bf16[128,1024]{1,0:T(8,128)(2,1)S(1)}, bf16[128,1024]{1,0:T(8,128)(2,1)S(1)}) fusion(bf16[3,128,2048]{2,1,0:T(8,128)(2,1)} %bitcast.19, s32[]{:T(128)S(6)} %select_n.7, s32[]{:T(128)S(6)} %select_n.6), kind=kLoop, calls=%fused_computation | loop fusion | bytes 1048584 | tf_op jit(solution)/shard_map/squeeze | solution.py:458
  13.9 0.0 collective-permute-done.2.pair_b_ref
  13.9 1.6 %collective-permute-start.4 = (bf16[136,512]{1,0:T(8,128)(2,1)S(1)}, bf16[136,512]{1,0:T(8,128)(2,1)S(1)}, u32[]{:S(2)}, u32[]{:S(2)}) collective-permute-start(bf16[136,512]{1,0:T(8,128)(2,1)S(1)} %collective-permute-done.2.pair_b_ref), channel_id=1, source_target_pairs={{0,8},{4,12},{8,16},{12,20},{16,24},{20,28},{24,0},{28,4},{1,9},{5... | collective-permute-start | bytes 417800 | tf_op jit(solution)/shard_map/ppermute | solution.py:20
  15.5 1.5 %collective-permute-start.5 = (bf16[128,1024]{1,0:T(8,128)(2,1)S(1)}, bf16[128,1024]{1,0:T(8,128)(2,1)S(1)}, u32[]{:S(2)}, u32[]{:S(2)}) collective-permute-start(bf16[128,1024]{1,0:T(8,128)(2,1)S(1)} %get-tuple-element.43), channel_id=1, source_target_pairs={{0,4},{4,0},{8,12},{12,8},{16,20},{20,16},{24,28},{28,24},{1,5},{5... | collective-permute-start | bytes 786440 | tf_op jit(solution)/shard_map/ppermute | solution.py:20
  17.0 0.5 %collective-permute-done.1.back_own_ref = bf16[136,1024]{1,0:T(8,128)(2,1)S(1)} collective-permute-done((bf16[136,1024]{1,0:T(8,128)(2,1)}, bf16[136,1024]{1,0:T(8,128)(2,1)S(1)}, u32[]{:S(2)}, u32[]{:S(2)}) %collective-permute-start.1) | collective-permute-done | bytes 278560 | tf_op jit(solution)/shard_map/ppermute | solution.py:20
  17.6 3.0 %collective-permute-done.3.back_a_ref.back_pair_ref = bf16[136,512]{1,0:T(8,128)(2,1)S(1)} collective-permute-done((bf16[136,512]{1,0:T(8,128)(2,1)S(1)}, bf16[136,512]{1,0:T(8,128)(2,1)S(1)}, u32[]{:S(2)}, u32[]{:S(2)}) %collective-permute-start.3) | collective-permute-done | bytes 139296 | tf_op jit(solution)/shard_map/ppermute | solution.py:20
  20.5 0.1 shard_map.78
  20.7 0.3 collective-permute-start.7
  21.0 2.3 %collective-permute-done.4.back_b_ref.back_pair_ref = bf16[136,512]{1,0:T(8,128)(2,1)S(1)} collective-permute-done((bf16[136,512]{1,0:T(8,128)(2,1)S(1)}, bf16[136,512]{1,0:T(8,128)(2,1)S(1)}, u32[]{:S(2)}, u32[]{:S(2)}) %collective-permute-start.4) | collective-permute-done | bytes 139296 | tf_op jit(solution)/shard_map/ppermute | solution.py:20
  23.4 0.1 shard_map.77
  23.5 0.5 %collective-permute-start.6 = (bf16[136,512]{1,0:T(8,128)(2,1)S(1)}, bf16[136,512]{1,0:T(8,128)(2,1)S(1)}, u32[]{:S(2)}, u32[]{:S(2)}) collective-permute-start(bf16[136,512]{1,0:T(8,128)(2,1)S(1)} %shard_map.77), channel_id=1, source_target_pairs={{0,4},{4,0},{8,16},{12,20},{16,24},{20,28},{24,8},{28,12},{1,5},{5... | collective-permute-start | bytes 417800 | tf_op jit(solution)/shard_map/ppermute | solution.py:20
  24.0 0.0 copy-done
  24.0 0.0 copy-done.3
  24.0 1.0 %shard_map.75 = (f32[256,1024]{1,0:T(8,128)S(1)}, f32[128,1024]{1,0:T(8,128)S(1)}) custom-call(s32[1,32]{1,0:T(1,128)S(1)} %bitcast.14, f32[4,8,128]{2,1,0:T(8,128)S(1)} %get-tuple-element.34.marks_ref, bf16[8,2,128,768]{3,2,1,0:T(8,128)(2,1)S(1)} %get-tuple-element.33.table_ref, bf16[136,1024]{1,0:T(8,128)(2,1)S(1)} %copy-done, ...), custom_call_target="tpu_custom_call" | custom-call | flops 167772160 | bytes 2097152 | tf_op jit(solution)/shard_map/pallas_call | solution.py:487
  25.0 0.0 collective-permute-done.5.raw_ref
  25.0 0.4 shard_map.76.qpair_ref
  25.4 1.2 %collective-permute-done.7.refs_0_ = bf16[136,512]{1,0:T(8,128)(2,1)S(1)} collective-permute-done((bf16[136,512]{1,0:T(8,128)(2,1)S(1)}, bf16[136,512]{1,0:T(8,128)(2,1)S(1)}, u32[]{:S(2)}, u32[]{:S(2)}) %collective-permute-start.7) | collective-permute-done | bytes 139296 | tf_op jit(solution)/shard_map/ppermute | solution.py:20
  26.6 0.4 %shard_map.79 = (f32[128,512]{1,0:T(8,128)S(1)}, bf16[128,512]{1,0:T(8,128)(2,1)S(1)}, f32[2,128,128]{2,1,0:T(8,128)S(1)}) custom-call(bf16[8,2,128,768]{3,2,1,0:T(8,128)(2,1)S(1)} %get-tuple-element.33.table_ref, f32[256,1024]{1,0:T(8,128)S(1)} %get-tuple-element.41.acc_ref, f32[128,1024]{1,0:T(8,128)S(1)} %get-tuple-element.42.qown_ref, ...), custom_call_target="tpu_custom_call" | custom-call | flops 100663296 | bytes 1572864 | tf_op jit(solution)/shard_map/pallas_call | solution.py:509
  27.0 1.6 %collective-permute-done.6.refs_0_ = bf16[136,512]{1,0:T(8,128)(2,1)S(1)} collective-permute-done((bf16[136,512]{1,0:T(8,128)(2,1)S(1)}, bf16[136,512]{1,0:T(8,128)(2,1)S(1)}, u32[]{:S(2)}, u32[]{:S(2)}) %collective-permute-start.6) | collective-permute-done | bytes 139296 | tf_op jit(solution)/shard_map/ppermute | solution.py:20
  28.6 0.7 %shard_map.80 = (f32[128,512]{1,0:T(8,128)S(1)}, bf16[128,1024]{1,0:T(8,128)(2,1)S(1)}, f32[1,256]{1,0:T(1,128)S(1)}) custom-call(bf16[8,2,128,768]{3,2,1,0:T(8,128)(2,1)S(1)} %get-tuple-element.33.table_ref, f32[256,1024]{1,0:T(8,128)S(1)} %get-tuple-element.41.acc_ref, f32[128,1024]{1,0:T(8,128)S(1)} %get-tuple-element.42.qown_ref, ...), custom_call_target="tpu_custom_call" | custom-call | flops 100663296 | bytes 1572864 | tf_op jit(solution)/shard_map/pallas_call | solution.py:509
  29.3 1.1 %collective-permute-start.12 = (bf16[128,1024]{1,0:T(8,128)(2,1)S(1)}, bf16[128,1024]{1,0:T(8,128)(2,1)S(1)}, u32[]{:S(2)}, u32[]{:S(2)}) collective-permute-start(bf16[128,1024]{1,0:T(8,128)(2,1)S(1)} %get-tuple-element.50), channel_id=1, source_target_pairs={{0,4},{4,0},{8,12},{12,8},{16,20},{20,16},{24,28},{28,24},{1,5},{5... | collective-permute-start | bytes 786440 | tf_op jit(solution)/shard_map/ppermute | solution.py:20
  30.4 0.0 collective-permute-start.10
  30.4 1.5 %collective-permute-start.9 = (f32[1,256]{1,0:T(1,128)S(1)}, f32[1,256]{1,0:T(1,128)S(1)}, u32[]{:S(2)}, u32[]{:S(2)}) collective-permute-start(f32[1,256]{1,0:T(1,128)S(1)} %get-tuple-element.47), channel_id=1, source_target_pairs={{0,2},{1,3},{2,0},{3,1},{4,6},{5,7},{6,4},{7,5},{8,10},{9,11},{10,... | collective-permute-start | bytes 3080 | tf_op jit(solution)/shard_map/ppermute | solution.py:525
  31.9 0.3 collective-permute-start.8
  32.2 1.1 %collective-permute-done.10 = f32[1,256]{1,0:T(1,128)S(1)} collective-permute-done((f32[1,256]{1,0:T(1,128)S(1)}, f32[1,256]{1,0:T(1,128)S(1)}, u32[]{:S(2)}, u32[]{:S(2)}) %collective-permute-start.10) | collective-permute-done | bytes 1056 | tf_op jit(solution)/shard_map/ppermute | solution.py:525
  33.3 0.6 %collective-permute-done.9 = f32[1,256]{1,0:T(1,128)S(1)} collective-permute-done((f32[1,256]{1,0:T(1,128)S(1)}, f32[1,256]{1,0:T(1,128)S(1)}, u32[]{:S(2)}, u32[]{:S(2)}) %collective-permute-start.9) | collective-permute-done | bytes 1056 | tf_op jit(solution)/shard_map/ppermute | solution.py:525
  34.0 0.0 collective-permute-done.8
  34.0 1.1 %collective-permute-start.11 = (f32[1,256]{1,0:T(1,128)S(1)}, f32[1,256]{1,0:T(1,128)S(1)}, u32[]{:S(2)}, u32[]{:S(2)}) collective-permute-start(f32[1,256]{1,0:T(1,128)S(1)} %add_add_fusion.power_ref), channel_id=1, source_target_pairs={{0,4},{4,0},{8,12},{12,8},{16,20},{20,16},{24,28},{28,24},{1,5},{5... | collective-permute-start | bytes 3080 | tf_op jit(solution)/shard_map/ppermute | solution.py:20
  35.0 2.6 %collective-permute-done.11.power_got_ref = f32[1,256]{1,0:T(1,128)S(1)} collective-permute-done((f32[1,256]{1,0:T(1,128)S(1)}, f32[1,256]{1,0:T(1,128)S(1)}, u32[]{:S(2)}, u32[]{:S(2)}) %collective-permute-start.11) | collective-permute-done | bytes 1056 | tf_op jit(solution)/shard_map/ppermute | solution.py:20
  37.6 0.0 collective-permute-done.12.refs_2_
  37.6 0.0 copy-done.4
  37.6 1.0 %shard_map.81 = bf16[128,2048]{1,0:T(8,128)(2,1)} custom-call(f32[1,256]{1,0:T(1,128)S(1)} %add_add_fusion.power_ref, f32[1,256]{1,0:T(1,128)S(1)} %collective-permute-done.11.power_got_ref, f32[128,512]{1,0:T(8,128)S(1)} %get-tuple-element.48.refs_0_, f32[128,512]{1,0:T(8,128)S(1)} %get-tuple-element.49.refs_1_, ...), custom_call_target="tpu_custom_call" | custom-call | flops 1048576 | bytes 1310720 | tf_op jit(solution)/shard_map/pallas_call | solution.py:527
  (7 shorter events, 0.0 us)
Async XLA Ops:
  0.0 8.3 %copy-start.2 = (s32[32]{0:T(128)S(1)}, s32[32]{0:T(128)}, u32[]{:S(2)}) copy-start(s32[32]{0:T(128)} %seq_ref.1) | copy-start | bytes 388
  0.0 8.3 %copy-start.1 = (f32[3,3,2048]{2,1,0:T(4,128)S(1)}, f32[3,3,2048]{2,1,0:T(4,128)}, u32[]{:S(2)}) copy-start(f32[3,3,2048]{2,1,0:T(4,128)} %w_ref.1) | copy-start | bytes 221188
  0.0 8.2 %copy-start.5 = (f32[16,512]{1,0:T(8,128)S(1)}, f32[16,512]{1,0:T(8,128)}, u32[]{:S(2)}) copy-start(f32[16,512]{1,0:T(8,128)} %param.9) | copy-start | bytes 98308
  0.0 8.1 %copy-start.6 = (s32[16,4]{0,1:T(4,128)S(1)}, s32[16,4]{0,1:T(4,128)}, u32[]{:S(2)}) copy-start(s32[16,4]{0,1:T(4,128)} %param.10) | copy-start | bytes 772
  2.9 8.2 %collective-permute-start = (bf16[136,512]{1,0:T(8,128)(2,1)}, bf16[136,512]{1,0:T(8,128)(2,1)S(1)}, u32[]{:S(2)}, u32[]{:S(2)}) collective-permute-start(bf16[136,512]{1,0:T(8,128)(2,1)} %get-tuple-element.32), channel_id=1, source_target_pairs={{0,4},{4,0},{8,12},{12,8},{16,20},{20,16},{24,28},{28,24},{1,5},{5... | collective-permute-start | bytes 417800 | tf_op jit(solution)/shard_map/ppermute | solution.py:20
  6.0 11.6 %collective-permute-start.1 = (bf16[136,1024]{1,0:T(8,128)(2,1)}, bf16[136,1024]{1,0:T(8,128)(2,1)S(1)}, u32[]{:S(2)}, u32[]{:S(2)}) collective-permute-start(bf16[136,1024]{1,0:T(8,128)(2,1)} %get-tuple-element.28.own_ref), channel_id=1, source_target_pairs={{0,8},{4,12},{8,16},{12,20},{16,24},{20,28},{24,0},{28,4},{1,9},{5... | collective-permute-start | bytes 835592 | tf_op jit(solution)/shard_map/ppermute | solution.py:20
  7.6 6.3 %collective-permute-start.2 = (bf16[136,512]{1,0:T(8,128)(2,1)}, bf16[136,512]{1,0:T(8,128)(2,1)S(1)}, u32[]{:S(2)}, u32[]{:S(2)}) collective-permute-start(bf16[136,512]{1,0:T(8,128)(2,1)} %get-tuple-element.37), channel_id=1, source_target_pairs={{0,4},{4,0},{8,12},{12,8},{16,20},{20,16},{24,28},{28,24},{1,5},{5... | collective-permute-start | bytes 417800 | tf_op jit(solution)/shard_map/ppermute | solution.py:20
  11.1 12.9 %copy-start = (bf16[136,1024]{1,0:T(8,128)(2,1)S(1)}, bf16[136,1024]{1,0:T(8,128)(2,1)}, u32[]{:S(2)}) copy-start(bf16[136,1024]{1,0:T(8,128)(2,1)} %get-tuple-element.28.own_ref) | copy-start | bytes 835588
  11.2 12.9 %copy-start.3 = (f32[2048]{0:T(1024)S(1)}, f32[2048]{0:T(1024)}, u32[]{:S(2)}) copy-start(f32[2048]{0:T(1024)} %param.11) | copy-start | bytes 24580
  11.2 9.4 %collective-permute-start.3 = (bf16[136,512]{1,0:T(8,128)(2,1)S(1)}, bf16[136,512]{1,0:T(8,128)(2,1)S(1)}, u32[]{:S(2)}, u32[]{:S(2)}) collective-permute-start(bf16[136,512]{1,0:T(8,128)(2,1)S(1)} %collective-permute-done.pair_a_ref), channel_id=1, source_target_pairs={{0,8},{4,12},{8,16},{12,20},{16,24},{20,28},{24,0},{28,4},{1,9},{5... | collective-permute-start | bytes 417800 | tf_op jit(solution)/shard_map/ppermute | solution.py:20
  13.9 9.5 %collective-permute-start.4 = (bf16[136,512]{1,0:T(8,128)(2,1)S(1)}, bf16[136,512]{1,0:T(8,128)(2,1)S(1)}, u32[]{:S(2)}, u32[]{:S(2)}) collective-permute-start(bf16[136,512]{1,0:T(8,128)(2,1)S(1)} %collective-permute-done.2.pair_b_ref), channel_id=1, source_target_pairs={{0,8},{4,12},{8,16},{12,20},{16,24},{20,28},{24,0},{28,4},{1,9},{5... | collective-permute-start | bytes 417800 | tf_op jit(solution)/shard_map/ppermute | solution.py:20
  15.5 9.5 %collective-permute-start.5 = (bf16[128,1024]{1,0:T(8,128)(2,1)S(1)}, bf16[128,1024]{1,0:T(8,128)(2,1)S(1)}, u32[]{:S(2)}, u32[]{:S(2)}) collective-permute-start(bf16[128,1024]{1,0:T(8,128)(2,1)S(1)} %get-tuple-element.43), channel_id=1, source_target_pairs={{0,4},{4,0},{8,12},{12,8},{16,20},{20,16},{24,28},{28,24},{1,5},{5... | collective-permute-start | bytes 786440 | tf_op jit(solution)/shard_map/ppermute | solution.py:20
  20.7 5.9 %collective-permute-start.7 = (bf16[136,512]{1,0:T(8,128)(2,1)S(1)}, bf16[136,512]{1,0:T(8,128)(2,1)S(1)}, u32[]{:S(2)}, u32[]{:S(2)}) collective-permute-start(bf16[136,512]{1,0:T(8,128)(2,1)S(1)} %shard_map.78), channel_id=1, source_target_pairs={{0,4},{4,0},{8,16},{12,20},{16,24},{20,28},{24,8},{28,12},{1,5},{5... | collective-permute-start | bytes 417800 | tf_op jit(solution)/shard_map/ppermute | solution.py:20
  23.5 5.1 %collective-permute-start.6 = (bf16[136,512]{1,0:T(8,128)(2,1)S(1)}, bf16[136,512]{1,0:T(8,128)(2,1)S(1)}, u32[]{:S(2)}, u32[]{:S(2)}) collective-permute-start(bf16[136,512]{1,0:T(8,128)(2,1)S(1)} %shard_map.77), channel_id=1, source_target_pairs={{0,4},{4,0},{8,16},{12,20},{16,24},{20,28},{24,8},{28,12},{1,5},{5... | collective-permute-start | bytes 417800 | tf_op jit(solution)/shard_map/ppermute | solution.py:20
  28.6 9.0 %copy-start.4 = (f32[2048]{0:T(1024)S(1)}, f32[2048]{0:T(1024)}, u32[]{:S(2)}) copy-start(f32[2048]{0:T(1024)} %param.12) | copy-start | bytes 24580
  29.3 8.3 %collective-permute-start.12 = (bf16[128,1024]{1,0:T(8,128)(2,1)S(1)}, bf16[128,1024]{1,0:T(8,128)(2,1)S(1)}, u32[]{:S(2)}, u32[]{:S(2)}) collective-permute-start(bf16[128,1024]{1,0:T(8,128)(2,1)S(1)} %get-tuple-element.50), channel_id=1, source_target_pairs={{0,4},{4,0},{8,12},{12,8},{16,20},{20,16},{24,28},{28,24},{1,5},{5... | collective-permute-start | bytes 786440 | tf_op jit(solution)/shard_map/ppermute | solution.py:20
  30.4 3.0 %collective-permute-start.10 = (f32[1,256]{1,0:T(1,128)S(1)}, f32[1,256]{1,0:T(1,128)S(1)}, u32[]{:S(2)}, u32[]{:S(2)}) collective-permute-start(f32[1,256]{1,0:T(1,128)S(1)} %get-tuple-element.47), channel_id=1, source_target_pairs={{0,3},{1,2},{2,1},{3,0},{4,7},{5,6},{6,5},{7,4},{8,11},{9,10},{10,... | collective-permute-start | bytes 3080 | tf_op jit(solution)/shard_map/ppermute | solution.py:525
  30.4 3.6 %collective-permute-start.9 = (f32[1,256]{1,0:T(1,128)S(1)}, f32[1,256]{1,0:T(1,128)S(1)}, u32[]{:S(2)}, u32[]{:S(2)}) collective-permute-start(f32[1,256]{1,0:T(1,128)S(1)} %get-tuple-element.47), channel_id=1, source_target_pairs={{0,2},{1,3},{2,0},{3,1},{4,6},{5,7},{6,4},{7,5},{8,10},{9,11},{10,... | collective-permute-start | bytes 3080 | tf_op jit(solution)/shard_map/ppermute | solution.py:525
  31.9 2.1 %collective-permute-start.8 = (f32[1,256]{1,0:T(1,128)S(1)}, f32[1,256]{1,0:T(1,128)S(1)}, u32[]{:S(2)}, u32[]{:S(2)}) collective-permute-start(f32[1,256]{1,0:T(1,128)S(1)} %get-tuple-element.47), channel_id=1, source_target_pairs={{0,1},{1,0},{2,3},{3,2},{4,5},{5,4},{6,7},{7,6},{8,9},{9,8},{10,11... | collective-permute-start | bytes 3080 | tf_op jit(solution)/shard_map/ppermute | solution.py:525
  34.0 3.6 %collective-permute-start.11 = (f32[1,256]{1,0:T(1,128)S(1)}, f32[1,256]{1,0:T(1,128)S(1)}, u32[]{:S(2)}, u32[]{:S(2)}) collective-permute-start(f32[1,256]{1,0:T(1,128)S(1)} %add_add_fusion.power_ref), channel_id=1, source_target_pairs={{0,4},{4,0},{8,12},{12,8},{16,20},{20,16},{24,28},{28,24},{1,5},{5... | collective-permute-start | bytes 3080 | tf_op jit(solution)/shard_map/ppermute | solution.py:20

commit v17 on v16

--- a/solution.py
+++ b/solution.py
@@ -32,7 +32,7 @@
     return first, first | second
 
 
-def row_masks(lengths_ref, start, m1_ref, m2_ref):
+def mask_columns(lengths_ref, start):
     count = lengths_ref.shape[1]
     square = (count, count)
     upto = lax.broadcasted_iota(jnp.int32, square, 1) <= lax.broadcasted_iota(jnp.int32, square, 0)
@@ -42,9 +42,15 @@
     opens = (t == ends) | (t == 0.0)
     after = opens | (t - 1.0 == ends) | (t == 1.0)
     diagonal = lax.broadcasted_iota(jnp.int32, (BLK, BLK), 0) == lax.broadcasted_iota(jnp.int32, (BLK, BLK), 1)
-    for mark, m_ref in ((opens, m1_ref), (after, m2_ref)):
+    columns = []
+    for mark in (opens, after):
         keep = 1.0 - jnp.max(mark.astype(jnp.float32), axis=0, keepdims=True)
-        column = jnp.sum(jnp.where(diagonal, keep, 0.0), axis=1, keepdims=True)
+        columns.append(jnp.sum(jnp.where(diagonal, keep, 0.0), axis=1, keepdims=True))
+    return columns
+
+
+def row_masks(lengths_ref, start, m1_ref, m2_ref):
+    for column, m_ref in zip(mask_columns(lengths_ref, start), (m1_ref, m2_ref)):
         m_ref[...] = jnp.broadcast_to(column, m_ref.shape)
 
 
@@ -71,7 +77,7 @@
 
 def products_kernel(seq_hbm, panels_hbm, w_hbm, *refs):
     outs, (kept_ref, *sent_refs), refs = refs[:3], refs[3:6], refs[6:]
-    seq_ref, kv_ref, q_ref, w_ref, x_ref, m1_ref, m2_ref, sems = refs
+    seq_ref, kv_ref, q_ref, w_ref, shift_ref, sems = refs
     width = kept_ref.shape[1]
     rows = kv_ref.shape[2]
     pieces = kv_ref.shape[0]
@@ -90,28 +96,31 @@
     loads.append(pltpu.make_async_copy(panels_hbm.at[0, rows - 16 :, :], q_ref, sems.at[2 + pieces]))
     for load in loads:
         load.start()
-    x_ref[:, 0:8, :] = jnp.zeros((x_ref.shape[0], 8, GROUP), jnp.float32)
     loads[0].wait()
-    row_masks(seq_ref, shard * rows, m1_ref, m2_ref)
+    place = lax.broadcasted_iota(jnp.int32, (rows, rows), 0) - lax.broadcasted_iota(jnp.int32, (rows, rows), 1)
+    for j, column in enumerate(mask_columns(seq_ref, shard * rows)):
+        shift_ref[j * rows : (j + 1) * rows, :] = jnp.where(place == j + 1, column, 0.0).astype(shift_ref.dtype)
     loads[1 + pieces].wait()
     loads[2 + pieces].wait()
     stores = []
     for p in range(pieces):
         loads[1 + p].wait()
         out_ref, at = (kept_ref, keep_at) if p < pieces // 2 else (sent_refs[p - pieces // 2], send_at)
-        for c in range(0, piece, GROUP):
+        step = 2 * GROUP
+        for c in range(0, piece, step):
             base = (p % (pieces // 2)) * piece + c
-            there = slice(base, base + GROUP) if p < pieces // 2 else slice(c, c + GROUP)
-            lanes = pl.ds(pl.multiple_of(at + base, GROUP), GROUP)
-            slot = (c // GROUP) % (x_ref.shape[0] // 2) * 2
+            there = slice(base, base + step) if p < pieces // 2 else slice(c, c + step)
+            lanes = pl.ds(pl.multiple_of(at + base, step), step)
             raw, made = [], []
             for i in range(2):
-                x = kv_ref[p, i, :, c : c + GROUP].astype(jnp.float32)
-                x_ref[slot + i, 8:, :] = x
-                made.append(feature(x, x_ref.at[slot + i], w_ref[1 + i, :, lanes], m1_ref, m2_ref))
+                x = kv_ref[p, i, :, c : c + step]
+                moved_rows = jnp.dot(shift_ref[...], x, preferred_element_type=jnp.float32)
+                w = w_ref[1 + i, :, lanes]
+                x = x.astype(jnp.float32)
+                made.append(w[0:1] * x + w[1:2] * moved_rows[:rows] + w[2:3] * moved_rows[rows:])
                 raw.append(x)
             product = made[0] * made[1]
-            top = jnp.where(lax.broadcasted_iota(jnp.int32, (8, GROUP), 0) < 2, raw[0][:8], product[:8])
+            top = jnp.where(lax.broadcasted_iota(jnp.int32, (8, step), 0) < 2, raw[0][:8], product[:8])
             out_ref[:rows, there] = jnp.concatenate([top, product[8:]], 0).astype(out_ref.dtype)
             tails = [x[rows - 2 :] for x in raw] + [q_ref[:, lanes].astype(jnp.float32)[14:]]
             out_ref[rows:, there] = jnp.concatenate([raw[1][0:2]] + tails, 0).astype(out_ref.dtype)
@@ -420,9 +429,7 @@
             pltpu.VMEM((pieces, 2, rows, 2 * width // pieces), jnp.bfloat16),
             pltpu.VMEM((16, 2 * width), jnp.bfloat16),
             pltpu.VMEM(short_weight.shape, jnp.float32),
-            pltpu.VMEM((4, rows + 8, GROUP), jnp.float32),
-            row_mask,
-            row_mask,
+            pltpu.VMEM((2 * rows, rows), jnp.bfloat16),
             pltpu.SemaphoreType.DMA((6 + pieces,)),
         ],
         40 * rows * width,

time: 38.8 us -> 39.1 us (level)
  no operation moved by 1% of the time
where the time goes in v17:
time: 39.1 us; the launch traced here: 39 us
  starting transfers between devices  14.5 us (37%)
  waiting for transfers between devices  13.2 us (34%)
  Pallas kernels  9.83 us (25%)
  local copies, waits for them, and re-layouts  1.26 us (3%)
    ppermute x10, starting transfers between devices, moved(): return lax.ppermute(block, SPOTS, pairs)  12.7 us
    ppermute x10, waiting for transfers between devices, moved(): return lax.ppermute(block, SPOTS, pairs)  11.4 us
    pallas_call x1, Pallas kernels, shards(): kernel_call(products_kernel, (message, small, small), [hbm] * 3, [pltpu.V...  3.22 us
    pallas_call x1, Pallas kernels, shards(): kernel_call(tables_kernel, (shape((groups, 2, BLK, span), jnp.bfloat16),...  2.85 us
    ppermute x3, starting transfers between devices, shards(): lax.ppermute(power, 'mp', [(i, i ^ k) for i in range(peers)])  1.86 us
    ppermute x3, waiting for transfers between devices, shards(): lax.ppermute(power, 'mp', [(i, i ^ k) for i in range(peers)])  1.74 us
    pallas_call x2, Pallas kernels, shards(): kernel_call(functools.partial(far_kernel, short, piece), (shape((rows, wi...  1.07 us
    squeeze x1, local copies, waits for them, and re-layouts, shards(): lax.dynamic_slice(query, (0, 0, (1 - half) * width), (1, rows, width))[0]  1.06 us
  transfers between devices with their start and end apart: 13, of which 8 were waited for; matrix products, arithmetic and copies ran while one was open for 3% of the time, Pallas kernels for 13%

profile of v17, /device:TPU:0, one launch (start us, length us, event | category | flops | bytes accessed | tf_op | source)
XLA Modules:
  0.0 39.0 jit_solution(10284247877621432100)
XLA Ops:
  0.0 0.0 copy-start.2
  0.0 3.2 %shard_map.73 = (bf16[136,1024]{1,0:T(8,128)(2,1)}, bf16[136,512]{1,0:T(8,128)(2,1)}, bf16[136,512]{1,0:T(8,128)(2,1)}) custom-call(s32[1,32]{1,0:T(1,128)} %bitcast.13, bf16[3,128,2048]{2,1,0:T(8,128)(2,1)} %bitcast.18, f32[3,3,2048]{2,1,0:T(4,128)} %w_ref.1), custom_call_target="tpu_custom_call" | custom-call | flops 5242880 | bytes 2097152 | tf_op jit(solution)/shard_map/pallas_call | solution.py:420
  3.2 3.0 %collective-permute-start = (bf16[136,512]{1,0:T(8,128)(2,1)}, bf16[136,512]{1,0:T(8,128)(2,1)S(1)}, u32[]{:S(2)}, u32[]{:S(2)}) collective-permute-start(bf16[136,512]{1,0:T(8,128)(2,1)} %get-tuple-element.32), channel_id=1, source_target_pairs={{0,4},{4,0},{8,12},{12,8},{16,20},{20,16},{24,28},{28,24},{1,5},{5... | collective-permute-start | bytes 417800 | tf_op jit(solution)/shard_map/ppermute | solution.py:20
  6.3 1.6 %collective-permute-start.1 = (bf16[136,1024]{1,0:T(8,128)(2,1)}, bf16[136,1024]{1,0:T(8,128)(2,1)S(1)}, u32[]{:S(2)}, u32[]{:S(2)}) collective-permute-start(bf16[136,1024]{1,0:T(8,128)(2,1)} %get-tuple-element.28.own_ref), channel_id=1, source_target_pairs={{0,8},{4,12},{8,16},{12,20},{16,24},{20,28},{24,0},{28,4},{1,9},{5... | collective-permute-start | bytes 835592 | tf_op jit(solution)/shard_map/ppermute | solution.py:20
  7.9 0.5 %collective-permute-start.2 = (bf16[136,512]{1,0:T(8,128)(2,1)}, bf16[136,512]{1,0:T(8,128)(2,1)S(1)}, u32[]{:S(2)}, u32[]{:S(2)}) collective-permute-start(bf16[136,512]{1,0:T(8,128)(2,1)} %get-tuple-element.37), channel_id=1, source_target_pairs={{0,4},{4,0},{8,12},{12,8},{16,20},{20,16},{24,28},{28,24},{1,5},{5... | collective-permute-start | bytes 417800 | tf_op jit(solution)/shard_map/ppermute | solution.py:20
  8.4 0.0 copy-done.6
  8.4 0.1 copy.8
  8.5 0.1 broadcast_in_dim.3
  8.5 0.0 copy-done.5
  8.6 0.0 copy-done.2
  8.6 0.0 copy-done.1
  8.6 2.9 %shard_map.74 = (bf16[8,2,128,768]{3,2,1,0:T(8,128)(2,1)S(1)}, bf16[8,128,256]{2,1,0:T(8,128)(2,1)S(1)}, f32[3,3,1024]{2,1,0:T(4,128)S(1)}, f32[4,8,128]{2,1,0:T(8,128)S(1)}) custom-call(s32[32]{0:T(128)S(1)} %copy-done.2, bf16[16,512]{1,0:T(8,128)(2,1)S(1)} %fusion.taps_ref, f32[3,3,2048]{2,1,0:T(4,128)S(1)} %copy-done.1), custom_call_target="tpu_custom_call" | custom-call | flops 20971520 | bytes 4194304 | tf_op jit(solution)/shard_map/pallas_call | solution.py:447
  11.4 0.0 collective-permute-done.pair_a_ref
  11.5 0.0 copy-start
  11.5 0.0 copy-start.3
  11.5 1.6 %collective-permute-start.3 = (bf16[136,512]{1,0:T(8,128)(2,1)S(1)}, bf16[136,512]{1,0:T(8,128)(2,1)S(1)}, u32[]{:S(2)}, u32[]{:S(2)}) collective-permute-start(bf16[136,512]{1,0:T(8,128)(2,1)S(1)} %collective-permute-done.pair_a_ref), channel_id=1, source_target_pairs={{0,8},{4,12},{8,16},{12,20},{16,24},{20,28},{24,0},{28,4},{1,9},{5... | collective-permute-start | bytes 417800 | tf_op jit(solution)/shard_map/ppermute | solution.py:20
  13.1 1.1 %dynamic-slice_bitcast_fusion = (bf16[128,1024]{1,0:T(8,128)(2,1)S(1)}, bf16[128,1024]{1,0:T(8,128)(2,1)S(1)}) fusion(bf16[3,128,2048]{2,1,0:T(8,128)(2,1)} %bitcast.19, s32[]{:T(128)S(6)} %select_n.7, s32[]{:T(128)S(6)} %select_n.6), kind=kLoop, calls=%fused_computation | loop fusion | bytes 1048584 | tf_op jit(solution)/shard_map/squeeze | solution.py:465
  14.2 0.0 collective-permute-done.2.pair_b_ref
  14.2 1.6 %collective-permute-start.4 = (bf16[136,512]{1,0:T(8,128)(2,1)S(1)}, bf16[136,512]{1,0:T(8,128)(2,1)S(1)}, u32[]{:S(2)}, u32[]{:S(2)}) collective-permute-start(bf16[136,512]{1,0:T(8,128)(2,1)S(1)} %collective-permute-done.2.pair_b_ref), channel_id=1, source_target_pairs={{0,8},{4,12},{8,16},{12,20},{16,24},{20,28},{24,0},{28,4},{1,9},{5... | collective-permute-start | bytes 417800 | tf_op jit(solution)/shard_map/ppermute | solution.py:20
  15.8 1.5 %collective-permute-start.5 = (bf16[128,1024]{1,0:T(8,128)(2,1)S(1)}, bf16[128,1024]{1,0:T(8,128)(2,1)S(1)}, u32[]{:S(2)}, u32[]{:S(2)}) collective-permute-start(bf16[128,1024]{1,0:T(8,128)(2,1)S(1)} %get-tuple-element.43), channel_id=1, source_target_pairs={{0,4},{4,0},{8,12},{12,8},{16,20},{20,16},{24,28},{28,24},{1,5},{5... | collective-permute-start | bytes 786440 | tf_op jit(solution)/shard_map/ppermute | solution.py:20
  17.3 0.5 %collective-permute-done.1.back_own_ref = bf16[136,1024]{1,0:T(8,128)(2,1)S(1)} collective-permute-done((bf16[136,1024]{1,0:T(8,128)(2,1)}, bf16[136,1024]{1,0:T(8,128)(2,1)S(1)}, u32[]{:S(2)}, u32[]{:S(2)}) %collective-permute-start.1) | collective-permute-done | bytes 278560 | tf_op jit(solution)/shard_map/ppermute | solution.py:20
  17.9 3.0 %collective-permute-done.3.back_a_ref.back_pair_ref = bf16[136,512]{1,0:T(8,128)(2,1)S(1)} collective-permute-done((bf16[136,512]{1,0:T(8,128)(2,1)S(1)}, bf16[136,512]{1,0:T(8,128)(2,1)S(1)}, u32[]{:S(2)}, u32[]{:S(2)}) %collective-permute-start.3) | collective-permute-done | bytes 139296 | tf_op jit(solution)/shard_map/ppermute | solution.py:20
  20.9 0.1 shard_map.78
  21.0 0.3 collective-permute-start.7
  21.3 2.5 %collective-permute-done.4.back_b_ref.back_pair_ref = bf16[136,512]{1,0:T(8,128)(2,1)S(1)} collective-permute-done((bf16[136,512]{1,0:T(8,128)(2,1)S(1)}, bf16[136,512]{1,0:T(8,128)(2,1)S(1)}, u32[]{:S(2)}, u32[]{:S(2)}) %collective-permute-start.4) | collective-permute-done | bytes 139296 | tf_op jit(solution)/shard_map/ppermute | solution.py:20
  23.8 0.1 shard_map.77
  24.0 0.3 collective-permute-start.6
  24.3 0.0 copy-done
  24.3 0.0 copy-done.3
  24.3 1.0 %shard_map.75 = (f32[256,1024]{1,0:T(8,128)S(1)}, f32[128,1024]{1,0:T(8,128)S(1)}) custom-call(s32[1,32]{1,0:T(1,128)S(1)} %bitcast.14, f32[4,8,128]{2,1,0:T(8,128)S(1)} %get-tuple-element.34.marks_ref, bf16[8,2,128,768]{3,2,1,0:T(8,128)(2,1)S(1)} %get-tuple-element.33.table_ref, bf16[136,1024]{1,0:T(8,128)(2,1)S(1)} %copy-done, ...), custom_call_target="tpu_custom_call" | custom-call | flops 167772160 | bytes 2097152 | tf_op jit(solution)/shard_map/pallas_call | solution.py:494
  25.3 0.0 collective-permute-done.5.raw_ref
  25.3 0.4 shard_map.76.qpair_ref
  25.7 1.2 %collective-permute-done.7.refs_0_ = bf16[136,512]{1,0:T(8,128)(2,1)S(1)} collective-permute-done((bf16[136,512]{1,0:T(8,128)(2,1)S(1)}, bf16[136,512]{1,0:T(8,128)(2,1)S(1)}, u32[]{:S(2)}, u32[]{:S(2)}) %collective-permute-start.7) | collective-permute-done | bytes 139296 | tf_op jit(solution)/shard_map/ppermute | solution.py:20
  26.9 0.4 %shard_map.79 = (f32[128,512]{1,0:T(8,128)S(1)}, bf16[128,512]{1,0:T(8,128)(2,1)S(1)}, f32[2,128,128]{2,1,0:T(8,128)S(1)}) custom-call(bf16[8,2,128,768]{3,2,1,0:T(8,128)(2,1)S(1)} %get-tuple-element.33.table_ref, f32[256,1024]{1,0:T(8,128)S(1)} %get-tuple-element.41.acc_ref, f32[128,1024]{1,0:T(8,128)S(1)} %get-tuple-element.42.qown_ref, ...), custom_call_target="tpu_custom_call" | custom-call | flops 100663296 | bytes 1572864 | tf_op jit(solution)/shard_map/pallas_call | solution.py:516
  27.3 1.8 %collective-permute-done.6.refs_0_ = bf16[136,512]{1,0:T(8,128)(2,1)S(1)} collective-permute-done((bf16[136,512]{1,0:T(8,128)(2,1)S(1)}, bf16[136,512]{1,0:T(8,128)(2,1)S(1)}, u32[]{:S(2)}, u32[]{:S(2)}) %collective-permute-start.6) | collective-permute-done | bytes 139296 | tf_op jit(solution)/shard_map/ppermute | solution.py:20
  29.1 0.7 %shard_map.80 = (f32[128,512]{1,0:T(8,128)S(1)}, bf16[128,1024]{1,0:T(8,128)(2,1)S(1)}, f32[1,256]{1,0:T(1,128)S(1)}) custom-call(bf16[8,2,128,768]{3,2,1,0:T(8,128)(2,1)S(1)} %get-tuple-element.33.table_ref, f32[256,1024]{1,0:T(8,128)S(1)} %get-tuple-element.41.acc_ref, f32[128,1024]{1,0:T(8,128)S(1)} %get-tuple-element.42.qown_ref, ...), custom_call_target="tpu_custom_call" | custom-call | flops 100663296 | bytes 1572864 | tf_op jit(solution)/shard_map/pallas_call | solution.py:516
  29.8 0.9 %collective-permute-start.12 = (bf16[128,1024]{1,0:T(8,128)(2,1)S(1)}, bf16[128,1024]{1,0:T(8,128)(2,1)S(1)}, u32[]{:S(2)}, u32[]{:S(2)}) collective-permute-start(bf16[128,1024]{1,0:T(8,128)(2,1)S(1)} %get-tuple-element.50), channel_id=1, source_target_pairs={{0,4},{4,0},{8,12},{12,8},{16,20},{20,16},{24,28},{28,24},{1,5},{5... | collective-permute-start | bytes 786440 | tf_op jit(solution)/shard_map/ppermute | solution.py:20
  30.7 0.0 collective-permute-start.10
  30.7 1.5 %collective-permute-start.9 = (f32[1,256]{1,0:T(1,128)S(1)}, f32[1,256]{1,0:T(1,128)S(1)}, u32[]{:S(2)}, u32[]{:S(2)}) collective-permute-start(f32[1,256]{1,0:T(1,128)S(1)} %get-tuple-element.47), channel_id=1, source_target_pairs={{0,2},{1,3},{2,0},{3,1},{4,6},{5,7},{6,4},{7,5},{8,10},{9,11},{10,... | collective-permute-start | bytes 3080 | tf_op jit(solution)/shard_map/ppermute | solution.py:532
  32.2 0.3 collective-permute-start.8
  32.5 1.1 %collective-permute-done.10 = f32[1,256]{1,0:T(1,128)S(1)} collective-permute-done((f32[1,256]{1,0:T(1,128)S(1)}, f32[1,256]{1,0:T(1,128)S(1)}, u32[]{:S(2)}, u32[]{:S(2)}) %collective-permute-start.10) | collective-permute-done | bytes 1056 | tf_op jit(solution)/shard_map/ppermute | solution.py:532
  33.7 0.6 %collective-permute-done.9 = f32[1,256]{1,0:T(1,128)S(1)} collective-permute-done((f32[1,256]{1,0:T(1,128)S(1)}, f32[1,256]{1,0:T(1,128)S(1)}, u32[]{:S(2)}, u32[]{:S(2)}) %collective-permute-start.9) | collective-permute-done | bytes 1056 | tf_op jit(solution)/shard_map/ppermute | solution.py:532
  34.3 0.0 collective-permute-done.8
  34.3 1.2 %collective-permute-start.11 = (f32[1,256]{1,0:T(1,128)S(1)}, f32[1,256]{1,0:T(1,128)S(1)}, u32[]{:S(2)}, u32[]{:S(2)}) collective-permute-start(f32[1,256]{1,0:T(1,128)S(1)} %add_add_fusion.power_ref), channel_id=1, source_target_pairs={{0,4},{4,0},{8,12},{12,8},{16,20},{20,16},{24,28},{28,24},{1,5},{5... | collective-permute-start | bytes 3080 | tf_op jit(solution)/shard_map/ppermute | solution.py:20
  35.5 2.4 %collective-permute-done.11.power_got_ref = f32[1,256]{1,0:T(1,128)S(1)} collective-permute-done((f32[1,256]{1,0:T(1,128)S(1)}, f32[1,256]{1,0:T(1,128)S(1)}, u32[]{:S(2)}, u32[]{:S(2)}) %collective-permute-start.11) | collective-permute-done | bytes 1056 | tf_op jit(solution)/shard_map/ppermute | solution.py:20
  37.9 0.0 collective-permute-done.12.refs_2_
  37.9 0.0 copy-done.4
  37.9 1.0 %shard_map.81 = bf16[128,2048]{1,0:T(8,128)(2,1)} custom-call(f32[1,256]{1,0:T(1,128)S(1)} %add_add_fusion.power_ref, f32[1,256]{1,0:T(1,128)S(1)} %collective-permute-done.11.power_got_ref, f32[128,512]{1,0:T(8,128)S(1)} %get-tuple-element.48.refs_0_, f32[128,512]{1,0:T(8,128)S(1)} %get-tuple-element.49.refs_1_, ...), custom_call_target="tpu_custom_call" | custom-call | flops 1048576 | bytes 1310720 | tf_op jit(solution)/shard_map/pallas_call | solution.py:534
  (7 shorter events, 0.0 us)
Async XLA Ops:
  0.0 8.6 %copy-start.2 = (s32[32]{0:T(128)S(1)}, s32[32]{0:T(128)}, u32[]{:S(2)}) copy-start(s32[32]{0:T(128)} %seq_ref.1) | copy-start | bytes 388
  0.0 8.6 %copy-start.1 = (f32[3,3,2048]{2,1,0:T(4,128)S(1)}, f32[3,3,2048]{2,1,0:T(4,128)}, u32[]{:S(2)}) copy-start(f32[3,3,2048]{2,1,0:T(4,128)} %w_ref.1) | copy-start | bytes 221188
  0.0 8.5 %copy-start.5 = (f32[16,512]{1,0:T(8,128)S(1)}, f32[16,512]{1,0:T(8,128)}, u32[]{:S(2)}) copy-start(f32[16,512]{1,0:T(8,128)} %param.9) | copy-start | bytes 98308
  0.0 8.4 %copy-start.6 = (s32[16,4]{0,1:T(4,128)S(1)}, s32[16,4]{0,1:T(4,128)}, u32[]{:S(2)}) copy-start(s32[16,4]{0,1:T(4,128)} %param.10) | copy-start | bytes 772
  3.2 8.2 %collective-permute-start = (bf16[136,512]{1,0:T(8,128)(2,1)}, bf16[136,512]{1,0:T(8,128)(2,1)S(1)}, u32[]{:S(2)}, u32[]{:S(2)}) collective-permute-start(bf16[136,512]{1,0:T(8,128)(2,1)} %get-tuple-element.32), channel_id=1, source_target_pairs={{0,4},{4,0},{8,12},{12,8},{16,20},{20,16},{24,28},{28,24},{1,5},{5... | collective-permute-start | bytes 417800 | tf_op jit(solution)/shard_map/ppermute | solution.py:20
  6.3 11.6 %collective-permute-start.1 = (bf16[136,1024]{1,0:T(8,128)(2,1)}, bf16[136,1024]{1,0:T(8,128)(2,1)S(1)}, u32[]{:S(2)}, u32[]{:S(2)}) collective-permute-start(bf16[136,1024]{1,0:T(8,128)(2,1)} %get-tuple-element.28.own_ref), channel_id=1, source_target_pairs={{0,8},{4,12},{8,16},{12,20},{16,24},{20,28},{24,0},{28,4},{1,9},{5... | collective-permute-start | bytes 835592 | tf_op jit(solution)/shard_map/ppermute | solution.py:20
  7.9 6.3 %collective-permute-start.2 = (bf16[136,512]{1,0:T(8,128)(2,1)}, bf16[136,512]{1,0:T(8,128)(2,1)S(1)}, u32[]{:S(2)}, u32[]{:S(2)}) collective-permute-start(bf16[136,512]{1,0:T(8,128)(2,1)} %get-tuple-element.37), channel_id=1, source_target_pairs={{0,4},{4,0},{8,12},{12,8},{16,20},{20,16},{24,28},{28,24},{1,5},{5... | collective-permute-start | bytes 417800 | tf_op jit(solution)/shard_map/ppermute | solution.py:20
  11.5 12.9 %copy-start = (bf16[136,1024]{1,0:T(8,128)(2,1)S(1)}, bf16[136,1024]{1,0:T(8,128)(2,1)}, u32[]{:S(2)}) copy-start(bf16[136,1024]{1,0:T(8,128)(2,1)} %get-tuple-element.28.own_ref) | copy-start | bytes 835588
  11.5 12.9 %copy-start.3 = (f32[2048]{0:T(1024)S(1)}, f32[2048]{0:T(1024)}, u32[]{:S(2)}) copy-start(f32[2048]{0:T(1024)} %param.11) | copy-start | bytes 24580
  11.5 9.4 %collective-permute-start.3 = (bf16[136,512]{1,0:T(8,128)(2,1)S(1)}, bf16[136,512]{1,0:T(8,128)(2,1)S(1)}, u32[]{:S(2)}, u32[]{:S(2)}) collective-permute-start(bf16[136,512]{1,0:T(8,128)(2,1)S(1)} %collective-permute-done.pair_a_ref), channel_id=1, source_target_pairs={{0,8},{4,12},{8,16},{12,20},{16,24},{20,28},{24,0},{28,4},{1,9},{5... | collective-permute-start | bytes 417800 | tf_op jit(solution)/shard_map/ppermute | solution.py:20
  14.2 9.7 %collective-permute-start.4 = (bf16[136,512]{1,0:T(8,128)(2,1)S(1)}, bf16[136,512]{1,0:T(8,128)(2,1)S(1)}, u32[]{:S(2)}, u32[]{:S(2)}) collective-permute-start(bf16[136,512]{1,0:T(8,128)(2,1)S(1)} %collective-permute-done.2.pair_b_ref), channel_id=1, source_target_pairs={{0,8},{4,12},{8,16},{12,20},{16,24},{20,28},{24,0},{28,4},{1,9},{5... | collective-permute-start | bytes 417800 | tf_op jit(solution)/shard_map/ppermute | solution.py:20
  15.8 9.5 %collective-permute-start.5 = (bf16[128,1024]{1,0:T(8,128)(2,1)S(1)}, bf16[128,1024]{1,0:T(8,128)(2,1)S(1)}, u32[]{:S(2)}, u32[]{:S(2)}) collective-permute-start(bf16[128,1024]{1,0:T(8,128)(2,1)S(1)} %get-tuple-element.43), channel_id=1, source_target_pairs={{0,4},{4,0},{8,12},{12,8},{16,20},{20,16},{24,28},{28,24},{1,5},{5... | collective-permute-start | bytes 786440 | tf_op jit(solution)/shard_map/ppermute | solution.py:20
  21.0 5.9 %collective-permute-start.7 = (bf16[136,512]{1,0:T(8,128)(2,1)S(1)}, bf16[136,512]{1,0:T(8,128)(2,1)S(1)}, u32[]{:S(2)}, u32[]{:S(2)}) collective-permute-start(bf16[136,512]{1,0:T(8,128)(2,1)S(1)} %shard_map.78), channel_id=1, source_target_pairs={{0,4},{4,0},{8,16},{12,20},{16,24},{20,28},{24,8},{28,12},{1,5},{5... | collective-permute-start | bytes 417800 | tf_op jit(solution)/shard_map/ppermute | solution.py:20
  24.0 5.1 %collective-permute-start.6 = (bf16[136,512]{1,0:T(8,128)(2,1)S(1)}, bf16[136,512]{1,0:T(8,128)(2,1)S(1)}, u32[]{:S(2)}, u32[]{:S(2)}) collective-permute-start(bf16[136,512]{1,0:T(8,128)(2,1)S(1)} %shard_map.77), channel_id=1, source_target_pairs={{0,4},{4,0},{8,16},{12,20},{16,24},{20,28},{24,8},{28,12},{1,5},{5... | collective-permute-start | bytes 417800 | tf_op jit(solution)/shard_map/ppermute | solution.py:20
  29.1 8.8 %copy-start.4 = (f32[2048]{0:T(1024)S(1)}, f32[2048]{0:T(1024)}, u32[]{:S(2)}) copy-start(f32[2048]{0:T(1024)} %param.12) | copy-start | bytes 24580
  29.8 8.1 %collective-permute-start.12 = (bf16[128,1024]{1,0:T(8,128)(2,1)S(1)}, bf16[128,1024]{1,0:T(8,128)(2,1)S(1)}, u32[]{:S(2)}, u32[]{:S(2)}) collective-permute-start(bf16[128,1024]{1,0:T(8,128)(2,1)S(1)} %get-tuple-element.50), channel_id=1, source_target_pairs={{0,4},{4,0},{8,12},{12,8},{16,20},{20,16},{24,28},{28,24},{1,5},{5... | collective-permute-start | bytes 786440 | tf_op jit(solution)/shard_map/ppermute | solution.py:20
  30.7 3.0 %collective-permute-start.10 = (f32[1,256]{1,0:T(1,128)S(1)}, f32[1,256]{1,0:T(1,128)S(1)}, u32[]{:S(2)}, u32[]{:S(2)}) collective-permute-start(f32[1,256]{1,0:T(1,128)S(1)} %get-tuple-element.47), channel_id=1, source_target_pairs={{0,3},{1,2},{2,1},{3,0},{4,7},{5,6},{6,5},{7,4},{8,11},{9,10},{10,... | collective-permute-start | bytes 3080 | tf_op jit(solution)/shard_map/ppermute | solution.py:532
  30.7 3.6 %collective-permute-start.9 = (f32[1,256]{1,0:T(1,128)S(1)}, f32[1,256]{1,0:T(1,128)S(1)}, u32[]{:S(2)}, u32[]{:S(2)}) collective-permute-start(f32[1,256]{1,0:T(1,128)S(1)} %get-tuple-element.47), channel_id=1, source_target_pairs={{0,2},{1,3},{2,0},{3,1},{4,6},{5,7},{6,4},{7,5},{8,10},{9,11},{10,... | collective-permute-start | bytes 3080 | tf_op jit(solution)/shard_map/ppermute | solution.py:532
  32.2 2.1 %collective-permute-start.8 = (f32[1,256]{1,0:T(1,128)S(1)}, f32[1,256]{1,0:T(1,128)S(1)}, u32[]{:S(2)}, u32[]{:S(2)}) collective-permute-start(f32[1,256]{1,0:T(1,128)S(1)} %get-tuple-element.47), channel_id=1, source_target_pairs={{0,1},{1,0},{2,3},{3,2},{4,5},{5,4},{6,7},{7,6},{8,9},{9,8},{10,11... | collective-permute-start | bytes 3080 | tf_op jit(solution)/shard_map/ppermute | solution.py:532
  34.3 3.6 %collective-permute-start.11 = (f32[1,256]{1,0:T(1,128)S(1)}, f32[1,256]{1,0:T(1,128)S(1)}, u32[]{:S(2)}, u32[]{:S(2)}) collective-permute-start(f32[1,256]{1,0:T(1,128)S(1)} %add_add_fusion.power_ref), channel_id=1, source_target_pairs={{0,4},{4,0},{8,12},{12,8},{16,20},{20,16},{24,28},{28,24},{1,5},{5... | collective-permute-start | bytes 3080 | tf_op jit(solution)/shard_map/ppermute | solution.py:20

commit v18 on v16

--- a/solution.py
+++ b/solution.py
@@ -70,7 +70,7 @@
 
 
 def products_kernel(seq_hbm, panels_hbm, w_hbm, *refs):
-    outs, (kept_ref, *sent_refs), refs = refs[:3], refs[3:6], refs[6:]
+    (kept_ref, *sent_refs), refs = refs[:3], refs[3:]
     seq_ref, kv_ref, q_ref, w_ref, x_ref, m1_ref, m2_ref, sems = refs
     width = kept_ref.shape[1]
     rows = kv_ref.shape[2]
@@ -95,7 +95,6 @@
     row_masks(seq_ref, shard * rows, m1_ref, m2_ref)
     loads[1 + pieces].wait()
     loads[2 + pieces].wait()
-    stores = []
     for p in range(pieces):
         loads[1 + p].wait()
         out_ref, at = (kept_ref, keep_at) if p < pieces // 2 else (sent_refs[p - pieces // 2], send_at)
@@ -115,12 +114,6 @@
             out_ref[:rows, there] = jnp.concatenate([top, product[8:]], 0).astype(out_ref.dtype)
             tails = [x[rows - 2 :] for x in raw] + [q_ref[:, lanes].astype(jnp.float32)[14:]]
             out_ref[rows:, there] = jnp.concatenate([raw[1][0:2]] + tails, 0).astype(out_ref.dtype)
-        if p >= pieces // 2 - 1:
-            done = p - pieces // 2 + 1
-            stores.append(pltpu.make_async_copy(out_ref, outs[done], sems.at[3 + pieces + done]))
-            stores[-1].start()
-    for store in stores:
-        store.wait()
 
 
 def edge_marks(seq_ref):
@@ -375,14 +368,14 @@
             at = at + ref.shape[1]
 
 
-def kernel_call(body, outs, in_specs, scratch, flops, moved_bytes, vmem=24 << 20, out_space=VMEM):
+def kernel_call(body, outs, in_specs, scratch, flops, moved_bytes):
     return pl.pallas_call(
         body,
         out_shape=outs,
         in_specs=in_specs,
-        out_specs=jax.tree.map(lambda _: out_space, outs),
+        out_specs=jax.tree.map(lambda _: VMEM, outs),
         scratch_shapes=scratch,
-        compiler_params=pltpu.CompilerParams(vmem_limit_bytes=vmem),
+        compiler_params=pltpu.CompilerParams(vmem_limit_bytes=24 << 20),
         cost_estimate=pl.CostEstimate(flops=flops, bytes_accessed=moved_bytes, transcendentals=0),
     )
 
@@ -413,9 +406,6 @@
         (message, small, small),
         [hbm] * 3,
         [
-            pltpu.VMEM(message.shape, message.dtype),
-            pltpu.VMEM(small.shape, small.dtype),
-            pltpu.VMEM(small.shape, small.dtype),
             pltpu.VMEM(lengths.shape, jnp.int32),
             pltpu.VMEM((pieces, 2, rows, 2 * width // pieces), jnp.bfloat16),
             pltpu.VMEM((16, 2 * width), jnp.bfloat16),
@@ -423,13 +413,11 @@
             pltpu.VMEM((4, rows + 8, GROUP), jnp.float32),
             row_mask,
             row_mask,
-            pltpu.SemaphoreType.DMA((6 + pieces,)),
+            pltpu.SemaphoreType.DMA((3 + pieces,)),
         ],
         40 * rows * width,
         16 * rows * width,
-        60 << 20,
-        hbm,
-    )(lengths, panels, short_weight)
+    )(*[pltpu.with_memory_space_constraint(a, pltpu.HBM) for a in (lengths, panels, short_weight)])
 
     back_own = moved(kept, ahead)
     pair = [moved(piece, to_pair) for piece in sent]

time: 38.8 us -> 38.1 us (0.982)
  Pallas kernels: 9.52 us -> 8.86 us
  starting transfers between devices: 14.7 us -> 15.2 us
  waiting for transfers between devices: 13 us -> 12.5 us
    pallas_call x1, Pallas kernels: 2.91 us -> 2.23 us  [shards(): kernel_call(products_kernel, (message, small, small), [hbm] * 3, [pltpu.V...]
    ppermute x10, waiting for transfers between devices: 11.2 us -> 10.7 us  [moved(): return lax.ppermute(block, SPOTS, pairs)]
    ppermute x10, starting transfers between devices: 12.9 us -> 13.4 us  [moved(): return lax.ppermute(block, SPOTS, pairs)]
where the time goes in v18:
time: 38.1 us; the launch traced here: 38 us
  starting transfers between devices  15.2 us (40%)
  waiting for transfers between devices  12.5 us (33%)
  Pallas kernels  8.86 us (23%)
  local copies, waits for them, and re-layouts  1.25 us (3%)
    ppermute x10, starting transfers between devices, moved(): return lax.ppermute(block, SPOTS, pairs)  13.4 us
    ppermute x10, waiting for transfers between devices, moved(): return lax.ppermute(block, SPOTS, pairs)  10.7 us
    pallas_call x1, Pallas kernels, shards(): kernel_call(tables_kernel, (shape((groups, 2, BLK, span), jnp.bfloat16),...  2.85 us
    pallas_call x1, Pallas kernels, shards(): kernel_call(products_kernel, (message, small, small), [hbm] * 3, [pltpu.V...  2.23 us
    ppermute x3, starting transfers between devices, shards(): lax.ppermute(power, 'mp', [(i, i ^ k) for i in range(peers)])  1.86 us
    ppermute x3, waiting for transfers between devices, shards(): lax.ppermute(power, 'mp', [(i, i ^ k) for i in range(peers)])  1.74 us
    pallas_call x2, Pallas kernels, shards(): kernel_call(functools.partial(far_kernel, short, piece), (shape((rows, wi...  1.08 us
    squeeze x1, local copies, waits for them, and re-layouts, shards(): lax.dynamic_slice(query, (0, 0, (1 - half) * width), (1, rows, width))[0]  1.06 us
  transfers between devices with their start and end apart: 13, of which 8 were waited for; matrix products, arithmetic and copies ran while one was open for 3% of the time, Pallas kernels for 13%

profile of v18, /device:TPU:0, one launch (start us, length us, event | category | flops | bytes accessed | tf_op | source)
XLA Modules:
  0.0 38.0 jit_solution(10760377051001445146)
XLA Ops:
  0.0 0.0 copy-start.1
  0.0 0.0 copy-start
  0.0 0.0 copy-start.4
  0.0 2.2 %shard_map.73 = (bf16[136,1024]{1,0:T(8,128)(2,1)S(1)}, bf16[136,512]{1,0:T(8,128)(2,1)S(1)}, bf16[136,512]{1,0:T(8,128)(2,1)S(1)}) custom-call(s32[1,32]{1,0:T(1,128)} %bitcast.13, bf16[3,128,2048]{2,1,0:T(8,128)(2,1)} %bitcast.18, f32[3,3,2048]{2,1,0:T(4,128)} %w_ref.1), custom_call_target="tpu_custom_call" | custom-call | flops 5242880 | bytes 2097152 | tf_op jit(solution)/shard_map/pallas_call | solution.py:404
  2.3 3.0 %collective-permute-start = (bf16[136,512]{1,0:T(8,128)(2,1)S(1)}, bf16[136,512]{1,0:T(8,128)(2,1)S(1)}, u32[]{:S(2)}, u32[]{:S(2)}) collective-permute-start(bf16[136,512]{1,0:T(8,128)(2,1)S(1)} %get-tuple-element.32), channel_id=1, source_target_pairs={{0,4},{4,0},{8,12},{12,8},{16,20},{20,16},{24,28},{28,24},{1,5},{5... | collective-permute-start | bytes 417800 | tf_op jit(solution)/shard_map/ppermute | solution.py:20
  5.3 1.6 %collective-permute-start.1 = (bf16[136,1024]{1,0:T(8,128)(2,1)S(1)}, bf16[136,1024]{1,0:T(8,128)(2,1)S(1)}, u32[]{:S(2)}, u32[]{:S(2)}) collective-permute-start(bf16[136,1024]{1,0:T(8,128)(2,1)S(1)} %get-tuple-element.28.own_ref), channel_id=1, source_target_pairs={{0,8},{4,12},{8,16},{12,20},{16,24},{20,28},{24,0},{28,4},{1,9},{5... | collective-permute-start | bytes 835592 | tf_op jit(solution)/shard_map/ppermute | solution.py:20
  6.9 0.5 %collective-permute-start.2 = (bf16[136,512]{1,0:T(8,128)(2,1)S(1)}, bf16[136,512]{1,0:T(8,128)(2,1)S(1)}, u32[]{:S(2)}, u32[]{:S(2)}) collective-permute-start(bf16[136,512]{1,0:T(8,128)(2,1)S(1)} %get-tuple-element.37), channel_id=1, source_target_pairs={{0,4},{4,0},{8,12},{12,8},{16,20},{20,16},{24,28},{28,24},{1,5},{5... | collective-permute-start | bytes 417800 | tf_op jit(solution)/shard_map/ppermute | solution.py:20
  7.4 0.0 copy-done.5
  7.4 0.1 copy.8
  7.5 0.1 broadcast_in_dim.3
  7.5 0.0 copy-done.4
  7.6 0.0 copy-done.1
  7.6 0.0 copy-done
  7.6 2.9 %shard_map.74 = (bf16[8,2,128,768]{3,2,1,0:T(8,128)(2,1)S(1)}, bf16[8,128,256]{2,1,0:T(8,128)(2,1)S(1)}, f32[3,3,1024]{2,1,0:T(4,128)S(1)}, f32[4,8,128]{2,1,0:T(8,128)S(1)}) custom-call(s32[32]{0:T(128)S(1)} %copy-done.1, bf16[16,512]{1,0:T(8,128)(2,1)S(1)} %fusion.taps_ref, f32[3,3,2048]{2,1,0:T(4,128)S(1)} %copy-done), custom_call_target="tpu_custom_call" | custom-call | flops 20971520 | bytes 4194304 | tf_op jit(solution)/shard_map/pallas_call | solution.py:428
  10.5 0.0 collective-permute-done.pair_a_ref
  10.5 0.0 copy-start.2
  10.5 1.6 %collective-permute-start.3 = (bf16[136,512]{1,0:T(8,128)(2,1)S(1)}, bf16[136,512]{1,0:T(8,128)(2,1)S(1)}, u32[]{:S(2)}, u32[]{:S(2)}) collective-permute-start(bf16[136,512]{1,0:T(8,128)(2,1)S(1)} %collective-permute-done.pair_a_ref), channel_id=1, source_target_pairs={{0,8},{4,12},{8,16},{12,20},{16,24},{20,28},{24,0},{28,4},{1,9},{5... | collective-permute-start | bytes 417800 | tf_op jit(solution)/shard_map/ppermute | solution.py:20
  12.1 1.1 %dynamic-slice_bitcast_fusion = (bf16[128,1024]{1,0:T(8,128)(2,1)S(1)}, bf16[128,1024]{1,0:T(8,128)(2,1)S(1)}) fusion(bf16[3,128,2048]{2,1,0:T(8,128)(2,1)} %bitcast.19, s32[]{:T(128)S(6)} %select_n.7, s32[]{:T(128)S(6)} %select_n.6), kind=kLoop, calls=%fused_computation | loop fusion | bytes 1048584 | tf_op jit(solution)/shard_map/squeeze | solution.py:446
  13.2 0.0 collective-permute-done.2.pair_b_ref
  13.2 1.6 %collective-permute-start.4 = (bf16[136,512]{1,0:T(8,128)(2,1)S(1)}, bf16[136,512]{1,0:T(8,128)(2,1)S(1)}, u32[]{:S(2)}, u32[]{:S(2)}) collective-permute-start(bf16[136,512]{1,0:T(8,128)(2,1)S(1)} %collective-permute-done.2.pair_b_ref), channel_id=1, source_target_pairs={{0,8},{4,12},{8,16},{12,20},{16,24},{20,28},{24,0},{28,4},{1,9},{5... | collective-permute-start | bytes 417800 | tf_op jit(solution)/shard_map/ppermute | solution.py:20
  14.8 1.5 %collective-permute-start.5 = (bf16[128,1024]{1,0:T(8,128)(2,1)S(1)}, bf16[128,1024]{1,0:T(8,128)(2,1)S(1)}, u32[]{:S(2)}, u32[]{:S(2)}) collective-permute-start(bf16[128,1024]{1,0:T(8,128)(2,1)S(1)} %get-tuple-element.43), channel_id=1, source_target_pairs={{0,4},{4,0},{8,12},{12,8},{16,20},{20,16},{24,28},{28,24},{1,5},{5... | collective-permute-start | bytes 786440 | tf_op jit(solution)/shard_map/ppermute | solution.py:20
  16.3 0.2 collective-permute-done.1.back_own_ref
  16.6 3.0 %collective-permute-done.3.back_a_ref.back_pair_ref = bf16[136,512]{1,0:T(8,128)(2,1)S(1)} collective-permute-done((bf16[136,512]{1,0:T(8,128)(2,1)S(1)}, bf16[136,512]{1,0:T(8,128)(2,1)S(1)}, u32[]{:S(2)}, u32[]{:S(2)}) %collective-permute-start.3) | collective-permute-done | bytes 139296 | tf_op jit(solution)/shard_map/ppermute | solution.py:20
  19.5 0.1 shard_map.78
  19.7 0.5 %collective-permute-start.7 = (bf16[136,512]{1,0:T(8,128)(2,1)S(1)}, bf16[136,512]{1,0:T(8,128)(2,1)S(1)}, u32[]{:S(2)}, u32[]{:S(2)}) collective-permute-start(bf16[136,512]{1,0:T(8,128)(2,1)S(1)} %shard_map.78), channel_id=1, source_target_pairs={{0,4},{4,0},{8,16},{12,20},{16,24},{20,28},{24,8},{28,12},{1,5},{5... | collective-permute-start | bytes 417800 | tf_op jit(solution)/shard_map/ppermute | solution.py:20
  20.2 2.2 %collective-permute-done.4.back_b_ref.back_pair_ref = bf16[136,512]{1,0:T(8,128)(2,1)S(1)} collective-permute-done((bf16[136,512]{1,0:T(8,128)(2,1)S(1)}, bf16[136,512]{1,0:T(8,128)(2,1)S(1)}, u32[]{:S(2)}, u32[]{:S(2)}) %collective-permute-start.4) | collective-permute-done | bytes 139296 | tf_op jit(solution)/shard_map/ppermute | solution.py:20
  22.4 0.1 shard_map.77
  22.6 0.8 %collective-permute-start.6 = (bf16[136,512]{1,0:T(8,128)(2,1)S(1)}, bf16[136,512]{1,0:T(8,128)(2,1)S(1)}, u32[]{:S(2)}, u32[]{:S(2)}) collective-permute-start(bf16[136,512]{1,0:T(8,128)(2,1)S(1)} %shard_map.77), channel_id=1, source_target_pairs={{0,4},{4,0},{8,16},{12,20},{16,24},{20,28},{24,8},{28,12},{1,5},{5... | collective-permute-start | bytes 417800 | tf_op jit(solution)/shard_map/ppermute | solution.py:20
  23.4 0.0 copy-done.2
  23.4 1.0 %shard_map.75 = (f32[256,1024]{1,0:T(8,128)S(1)}, f32[128,1024]{1,0:T(8,128)S(1)}) custom-call(s32[1,32]{1,0:T(1,128)S(1)} %bitcast.14, f32[4,8,128]{2,1,0:T(8,128)S(1)} %get-tuple-element.34.marks_ref, bf16[8,2,128,768]{3,2,1,0:T(8,128)(2,1)S(1)} %get-tuple-element.33.table_ref, bf16[136,1024]{1,0:T(8,128)(2,1)S(1)} %get-tuple-element.28.own_ref, ...), custom_call_target="tpu_custom_call" | custom-call | flops 167772160 | bytes 2097152 | tf_op jit(solution)/shard_map/pallas_call | solution.py:475
  24.4 0.0 collective-permute-done.5.raw_ref
  24.4 0.4 shard_map.76.qpair_ref
  24.8 1.2 %collective-permute-done.7.refs_0_ = bf16[136,512]{1,0:T(8,128)(2,1)S(1)} collective-permute-done((bf16[136,512]{1,0:T(8,128)(2,1)S(1)}, bf16[136,512]{1,0:T(8,128)(2,1)S(1)}, u32[]{:S(2)}, u32[]{:S(2)}) %collective-permute-start.7) | collective-permute-done | bytes 139296 | tf_op jit(solution)/shard_map/ppermute | solution.py:20
  25.9 0.4 %shard_map.79 = (f32[128,512]{1,0:T(8,128)S(1)}, bf16[128,512]{1,0:T(8,128)(2,1)S(1)}, f32[2,128,128]{2,1,0:T(8,128)S(1)}) custom-call(bf16[8,2,128,768]{3,2,1,0:T(8,128)(2,1)S(1)} %get-tuple-element.33.table_ref, f32[256,1024]{1,0:T(8,128)S(1)} %get-tuple-element.41.acc_ref, f32[128,1024]{1,0:T(8,128)S(1)} %get-tuple-element.42.qown_ref, ...), custom_call_target="tpu_custom_call" | custom-call | flops 100663296 | bytes 1572864 | tf_op jit(solution)/shard_map/pallas_call | solution.py:497
  26.3 1.3 %collective-permute-done.6.refs_0_ = bf16[136,512]{1,0:T(8,128)(2,1)S(1)} collective-permute-done((bf16[136,512]{1,0:T(8,128)(2,1)S(1)}, bf16[136,512]{1,0:T(8,128)(2,1)S(1)}, u32[]{:S(2)}, u32[]{:S(2)}) %collective-permute-start.6) | collective-permute-done | bytes 139296 | tf_op jit(solution)/shard_map/ppermute | solution.py:20
  27.7 0.7 %shard_map.80 = (f32[128,512]{1,0:T(8,128)S(1)}, bf16[128,1024]{1,0:T(8,128)(2,1)S(1)}, f32[1,256]{1,0:T(1,128)S(1)}) custom-call(bf16[8,2,128,768]{3,2,1,0:T(8,128)(2,1)S(1)} %get-tuple-element.33.table_ref, f32[256,1024]{1,0:T(8,128)S(1)} %get-tuple-element.41.acc_ref, f32[128,1024]{1,0:T(8,128)S(1)} %get-tuple-element.42.qown_ref, ...), custom_call_target="tpu_custom_call" | custom-call | flops 100663296 | bytes 1572864 | tf_op jit(solution)/shard_map/pallas_call | solution.py:497
  28.4 1.3 %collective-permute-start.12 = (bf16[128,1024]{1,0:T(8,128)(2,1)S(1)}, bf16[128,1024]{1,0:T(8,128)(2,1)S(1)}, u32[]{:S(2)}, u32[]{:S(2)}) collective-permute-start(bf16[128,1024]{1,0:T(8,128)(2,1)S(1)} %get-tuple-element.50), channel_id=1, source_target_pairs={{0,4},{4,0},{8,12},{12,8},{16,20},{20,16},{24,28},{28,24},{1,5},{5... | collective-permute-start | bytes 786440 | tf_op jit(solution)/shard_map/ppermute | solution.py:20
  29.7 0.0 collective-permute-start.10
  29.7 1.5 %collective-permute-start.9 = (f32[1,256]{1,0:T(1,128)S(1)}, f32[1,256]{1,0:T(1,128)S(1)}, u32[]{:S(2)}, u32[]{:S(2)}) collective-permute-start(f32[1,256]{1,0:T(1,128)S(1)} %get-tuple-element.47), channel_id=1, source_target_pairs={{0,2},{1,3},{2,0},{3,1},{4,6},{5,7},{6,4},{7,5},{8,10},{9,11},{10,... | collective-permute-start | bytes 3080 | tf_op jit(solution)/shard_map/ppermute | solution.py:513
  31.2 0.3 collective-permute-start.8
  31.5 1.1 %collective-permute-done.10 = f32[1,256]{1,0:T(1,128)S(1)} collective-permute-done((f32[1,256]{1,0:T(1,128)S(1)}, f32[1,256]{1,0:T(1,128)S(1)}, u32[]{:S(2)}, u32[]{:S(2)}) %collective-permute-start.10) | collective-permute-done | bytes 1056 | tf_op jit(solution)/shard_map/ppermute | solution.py:513
  32.7 0.6 %collective-permute-done.9 = f32[1,256]{1,0:T(1,128)S(1)} collective-permute-done((f32[1,256]{1,0:T(1,128)S(1)}, f32[1,256]{1,0:T(1,128)S(1)}, u32[]{:S(2)}, u32[]{:S(2)}) %collective-permute-start.9) | collective-permute-done | bytes 1056 | tf_op jit(solution)/shard_map/ppermute | solution.py:513
  33.3 0.0 collective-permute-done.8
  33.3 0.8 %collective-permute-start.11 = (f32[1,256]{1,0:T(1,128)S(1)}, f32[1,256]{1,0:T(1,128)S(1)}, u32[]{:S(2)}, u32[]{:S(2)}) collective-permute-start(f32[1,256]{1,0:T(1,128)S(1)} %add_add_fusion.power_ref), channel_id=1, source_target_pairs={{0,4},{4,0},{8,12},{12,8},{16,20},{20,16},{24,28},{28,24},{1,5},{5... | collective-permute-start | bytes 3080 | tf_op jit(solution)/shard_map/ppermute | solution.py:20
  34.1 2.8 %collective-permute-done.11.power_got_ref = f32[1,256]{1,0:T(1,128)S(1)} collective-permute-done((f32[1,256]{1,0:T(1,128)S(1)}, f32[1,256]{1,0:T(1,128)S(1)}, u32[]{:S(2)}, u32[]{:S(2)}) %collective-permute-start.11) | collective-permute-done | bytes 1056 | tf_op jit(solution)/shard_map/ppermute | solution.py:20
  36.9 0.0 collective-permute-done.12.refs_2_
  36.9 0.0 copy-done.3
  36.9 1.0 %shard_map.81 = bf16[128,2048]{1,0:T(8,128)(2,1)} custom-call(f32[1,256]{1,0:T(1,128)S(1)} %add_add_fusion.power_ref, f32[1,256]{1,0:T(1,128)S(1)} %collective-permute-done.11.power_got_ref, f32[128,512]{1,0:T(8,128)S(1)} %get-tuple-element.48.refs_0_, f32[128,512]{1,0:T(8,128)S(1)} %get-tuple-element.49.refs_1_, ...), custom_call_target="tpu_custom_call" | custom-call | flops 1048576 | bytes 1310720 | tf_op jit(solution)/shard_map/pallas_call | solution.py:515
  (5 shorter events, 0.0 us)
Async XLA Ops:
  0.0 7.6 %copy-start.1 = (s32[32]{0:T(128)S(1)}, s32[32]{0:T(128)}, u32[]{:S(2)}) copy-start(s32[32]{0:T(128)} %seq_ref.1) | copy-start | bytes 388
  0.0 7.6 %copy-start = (f32[3,3,2048]{2,1,0:T(4,128)S(1)}, f32[3,3,2048]{2,1,0:T(4,128)}, u32[]{:S(2)}) copy-start(f32[3,3,2048]{2,1,0:T(4,128)} %w_ref.1) | copy-start | bytes 221188
  0.0 7.5 %copy-start.4 = (f32[16,512]{1,0:T(8,128)S(1)}, f32[16,512]{1,0:T(8,128)}, u32[]{:S(2)}) copy-start(f32[16,512]{1,0:T(8,128)} %param.9) | copy-start | bytes 98308
  0.0 7.4 %copy-start.5 = (s32[16,4]{0,1:T(4,128)S(1)}, s32[16,4]{0,1:T(4,128)}, u32[]{:S(2)}) copy-start(s32[16,4]{0,1:T(4,128)} %param.10) | copy-start | bytes 772
  2.3 8.2 %collective-permute-start = (bf16[136,512]{1,0:T(8,128)(2,1)S(1)}, bf16[136,512]{1,0:T(8,128)(2,1)S(1)}, u32[]{:S(2)}, u32[]{:S(2)}) collective-permute-start(bf16[136,512]{1,0:T(8,128)(2,1)S(1)} %get-tuple-element.32), channel_id=1, source_target_pairs={{0,4},{4,0},{8,12},{12,8},{16,20},{20,16},{24,28},{28,24},{1,5},{5... | collective-permute-start | bytes 417800 | tf_op jit(solution)/shard_map/ppermute | solution.py:20
  5.3 11.3 %collective-permute-start.1 = (bf16[136,1024]{1,0:T(8,128)(2,1)S(1)}, bf16[136,1024]{1,0:T(8,128)(2,1)S(1)}, u32[]{:S(2)}, u32[]{:S(2)}) collective-permute-start(bf16[136,1024]{1,0:T(8,128)(2,1)S(1)} %get-tuple-element.28.own_ref), channel_id=1, source_target_pairs={{0,8},{4,12},{8,16},{12,20},{16,24},{20,28},{24,0},{28,4},{1,9},{5... | collective-permute-start | bytes 835592 | tf_op jit(solution)/shard_map/ppermute | solution.py:20
  6.9 6.3 %collective-permute-start.2 = (bf16[136,512]{1,0:T(8,128)(2,1)S(1)}, bf16[136,512]{1,0:T(8,128)(2,1)S(1)}, u32[]{:S(2)}, u32[]{:S(2)}) collective-permute-start(bf16[136,512]{1,0:T(8,128)(2,1)S(1)} %get-tuple-element.37), channel_id=1, source_target_pairs={{0,4},{4,0},{8,12},{12,8},{16,20},{20,16},{24,28},{28,24},{1,5},{5... | collective-permute-start | bytes 417800 | tf_op jit(solution)/shard_map/ppermute | solution.py:20
  10.5 12.9 %copy-start.2 = (f32[2048]{0:T(1024)S(1)}, f32[2048]{0:T(1024)}, u32[]{:S(2)}) copy-start(f32[2048]{0:T(1024)} %param.11) | copy-start | bytes 24580
  10.5 9.1 %collective-permute-start.3 = (bf16[136,512]{1,0:T(8,128)(2,1)S(1)}, bf16[136,512]{1,0:T(8,128)(2,1)S(1)}, u32[]{:S(2)}, u32[]{:S(2)}) collective-permute-start(bf16[136,512]{1,0:T(8,128)(2,1)S(1)} %collective-permute-done.pair_a_ref), channel_id=1, source_target_pairs={{0,8},{4,12},{8,16},{12,20},{16,24},{20,28},{24,0},{28,4},{1,9},{5... | collective-permute-start | bytes 417800 | tf_op jit(solution)/shard_map/ppermute | solution.py:20
  13.2 9.2 %collective-permute-start.4 = (bf16[136,512]{1,0:T(8,128)(2,1)S(1)}, bf16[136,512]{1,0:T(8,128)(2,1)S(1)}, u32[]{:S(2)}, u32[]{:S(2)}) collective-permute-start(bf16[136,512]{1,0:T(8,128)(2,1)S(1)} %collective-permute-done.2.pair_b_ref), channel_id=1, source_target_pairs={{0,8},{4,12},{8,16},{12,20},{16,24},{20,28},{24,0},{28,4},{1,9},{5... | collective-permute-start | bytes 417800 | tf_op jit(solution)/shard_map/ppermute | solution.py:20
  14.8 9.6 %collective-permute-start.5 = (bf16[128,1024]{1,0:T(8,128)(2,1)S(1)}, bf16[128,1024]{1,0:T(8,128)(2,1)S(1)}, u32[]{:S(2)}, u32[]{:S(2)}) collective-permute-start(bf16[128,1024]{1,0:T(8,128)(2,1)S(1)} %get-tuple-element.43), channel_id=1, source_target_pairs={{0,4},{4,0},{8,12},{12,8},{16,20},{20,16},{24,28},{28,24},{1,5},{5... | collective-permute-start | bytes 786440 | tf_op jit(solution)/shard_map/ppermute | solution.py:20
  19.7 6.2 %collective-permute-start.7 = (bf16[136,512]{1,0:T(8,128)(2,1)S(1)}, bf16[136,512]{1,0:T(8,128)(2,1)S(1)}, u32[]{:S(2)}, u32[]{:S(2)}) collective-permute-start(bf16[136,512]{1,0:T(8,128)(2,1)S(1)} %shard_map.78), channel_id=1, source_target_pairs={{0,4},{4,0},{8,16},{12,20},{16,24},{20,28},{24,8},{28,12},{1,5},{5... | collective-permute-start | bytes 417800 | tf_op jit(solution)/shard_map/ppermute | solution.py:20
  22.6 5.1 %collective-permute-start.6 = (bf16[136,512]{1,0:T(8,128)(2,1)S(1)}, bf16[136,512]{1,0:T(8,128)(2,1)S(1)}, u32[]{:S(2)}, u32[]{:S(2)}) collective-permute-start(bf16[136,512]{1,0:T(8,128)(2,1)S(1)} %shard_map.77), channel_id=1, source_target_pairs={{0,4},{4,0},{8,16},{12,20},{16,24},{20,28},{24,8},{28,12},{1,5},{5... | collective-permute-start | bytes 417800 | tf_op jit(solution)/shard_map/ppermute | solution.py:20
  27.7 9.2 %copy-start.3 = (f32[2048]{0:T(1024)S(1)}, f32[2048]{0:T(1024)}, u32[]{:S(2)}) copy-start(f32[2048]{0:T(1024)} %param.12) | copy-start | bytes 24580
  28.4 8.5 %collective-permute-start.12 = (bf16[128,1024]{1,0:T(8,128)(2,1)S(1)}, bf16[128,1024]{1,0:T(8,128)(2,1)S(1)}, u32[]{:S(2)}, u32[]{:S(2)}) collective-permute-start(bf16[128,1024]{1,0:T(8,128)(2,1)S(1)} %get-tuple-element.50), channel_id=1, source_target_pairs={{0,4},{4,0},{8,12},{12,8},{16,20},{20,16},{24,28},{28,24},{1,5},{5... | collective-permute-start | bytes 786440 | tf_op jit(solution)/shard_map/ppermute | solution.py:20
  29.7 3.0 %collective-permute-start.10 = (f32[1,256]{1,0:T(1,128)S(1)}, f32[1,256]{1,0:T(1,128)S(1)}, u32[]{:S(2)}, u32[]{:S(2)}) collective-permute-start(f32[1,256]{1,0:T(1,128)S(1)} %get-tuple-element.47), channel_id=1, source_target_pairs={{0,3},{1,2},{2,1},{3,0},{4,7},{5,6},{6,5},{7,4},{8,11},{9,10},{10,... | collective-permute-start | bytes 3080 | tf_op jit(solution)/shard_map/ppermute | solution.py:513
  29.7 3.6 %collective-permute-start.9 = (f32[1,256]{1,0:T(1,128)S(1)}, f32[1,256]{1,0:T(1,128)S(1)}, u32[]{:S(2)}, u32[]{:S(2)}) collective-permute-start(f32[1,256]{1,0:T(1,128)S(1)} %get-tuple-element.47), channel_id=1, source_target_pairs={{0,2},{1,3},{2,0},{3,1},{4,6},{5,7},{6,4},{7,5},{8,10},{9,11},{10,... | collective-permute-start | bytes 3080 | tf_op jit(solution)/shard_map/ppermute | solution.py:513
  31.2 2.1 %collective-permute-start.8 = (f32[1,256]{1,0:T(1,128)S(1)}, f32[1,256]{1,0:T(1,128)S(1)}, u32[]{:S(2)}, u32[]{:S(2)}) collective-permute-start(f32[1,256]{1,0:T(1,128)S(1)} %get-tuple-element.47), channel_id=1, source_target_pairs={{0,1},{1,0},{2,3},{3,2},{4,5},{5,4},{6,7},{7,6},{8,9},{9,8},{10,11... | collective-permute-start | bytes 3080 | tf_op jit(solution)/shard_map/ppermute | solution.py:513
  33.3 3.6 %collective-permute-start.11 = (f32[1,256]{1,0:T(1,128)S(1)}, f32[1,256]{1,0:T(1,128)S(1)}, u32[]{:S(2)}, u32[]{:S(2)}) collective-permute-start(f32[1,256]{1,0:T(1,128)S(1)} %add_add_fusion.power_ref), channel_id=1, source_target_pairs={{0,4},{4,0},{8,12},{12,8},{16,20},{20,16},{24,28},{28,24},{1,5},{5... | collective-permute-start | bytes 3080 | tf_op jit(solution)/shard_map/ppermute | solution.py:20

commit v19 on v18

--- a/solution.py
+++ b/solution.py
@@ -446,7 +446,7 @@
     qsent = lax.dynamic_slice(query, (0, 0, (1 - half) * width), (1, rows, width))[0]
     qkept, qsent, pair[1] = lax.optimization_barrier((qkept, qsent, pair[1]))
     qgot = moved(qsent, to_pair)
-    back_pair = [moved(piece, ahead) for piece in pair]
+    back_pair = [moved(pair[0], ahead), moved(pair[1], [(i, j) for i, j in ahead if i < j])]
 
     window = pltpu.VMEM((4 * rows, width), jnp.bfloat16)
     extras = pltpu.VMEM((4, 16, width), jnp.float32)

time: 38.1 us -> 40.1 us (1.052)
  starting transfers between devices: 15.2 us -> 18.1 us
  waiting for transfers between devices: 12.5 us -> 11.6 us
    ppermute x10, starting transfers between devices: 13.4 us -> 16.2 us  [moved(): return lax.ppermute(block, SPOTS, pairs)]
    ppermute x10, waiting for transfers between devices: 10.7 us -> 9.84 us  [moved(): return lax.ppermute(block, SPOTS, pairs)]
  transfers between devices with their start and end apart: 13 -> 13, of which waited for: 8 -> 7; matrix products, arithmetic and copies ran while one was open for 3% -> 3% of each run, Pallas kernels for 13% -> 12%
where the time goes in v19:
time: 40.1 us; the launch traced here: 39.9 us
  starting transfers between devices  18.1 us (45%)
  waiting for transfers between devices  11.6 us (29%)
  Pallas kernels  8.85 us (22%)
  local copies, waits for them, and re-layouts  1.25 us (3%)
    ppermute x10, starting transfers between devices, moved(): return lax.ppermute(block, SPOTS, pairs)  16.2 us
    ppermute x10, waiting for transfers between devices, moved(): return lax.ppermute(block, SPOTS, pairs)  9.84 us
    pallas_call x1, Pallas kernels, shards(): kernel_call(tables_kernel, (shape((groups, 2, BLK, span), jnp.bfloat16),...  2.85 us
    pallas_call x1, Pallas kernels, shards(): kernel_call(products_kernel, (message, small, small), [hbm] * 3, [pltpu.V...  2.23 us
    ppermute x3, starting transfers between devices, shards(): lax.ppermute(power, 'mp', [(i, i ^ k) for i in range(peers)])  1.86 us
    ppermute x3, waiting for transfers between devices, shards(): lax.ppermute(power, 'mp', [(i, i ^ k) for i in range(peers)])  1.74 us
    pallas_call x2, Pallas kernels, shards(): kernel_call(functools.partial(far_kernel, short, piece), (shape((rows, wi...  1.08 us
    squeeze x1, local copies, waits for them, and re-layouts, shards(): lax.dynamic_slice(query, (0, 0, (1 - half) * width), (1, rows, width))[0]  1.06 us
  transfers between devices with their start and end apart: 13, of which 7 were waited for; matrix products, arithmetic and copies ran while one was open for 3% of the time, Pallas kernels for 12%

profile of v19, /device:TPU:0, one launch (start us, length us, event | category | flops | bytes accessed | tf_op | source)
XLA Modules:
  0.0 39.9 jit_solution(7401610723800387423)
XLA Ops:
  0.0 0.0 copy-start.1
  0.0 0.0 copy-start
  0.0 0.0 copy-start.4
  0.0 2.2 %shard_map.73 = (bf16[136,1024]{1,0:T(8,128)(2,1)S(1)}, bf16[136,512]{1,0:T(8,128)(2,1)S(1)}, bf16[136,512]{1,0:T(8,128)(2,1)S(1)}) custom-call(s32[1,32]{1,0:T(1,128)} %bitcast.13, bf16[3,128,2048]{2,1,0:T(8,128)(2,1)} %bitcast.18, f32[3,3,2048]{2,1,0:T(4,128)} %w_ref.1), custom_call_target="tpu_custom_call" | custom-call | flops 5242880 | bytes 2097152 | tf_op jit(solution)/shard_map/pallas_call | solution.py:404
  2.3 3.0 %collective-permute-start = (bf16[136,512]{1,0:T(8,128)(2,1)S(1)}, bf16[136,512]{1,0:T(8,128)(2,1)S(1)}, u32[]{:S(2)}, u32[]{:S(2)}) collective-permute-start(bf16[136,512]{1,0:T(8,128)(2,1)S(1)} %get-tuple-element.32), channel_id=1, source_target_pairs={{0,4},{4,0},{8,12},{12,8},{16,20},{20,16},{24,28},{28,24},{1,5},{5... | collective-permute-start | bytes 417800 | tf_op jit(solution)/shard_map/ppermute | solution.py:20
  5.3 1.6 %collective-permute-start.1 = (bf16[136,1024]{1,0:T(8,128)(2,1)S(1)}, bf16[136,1024]{1,0:T(8,128)(2,1)S(1)}, u32[]{:S(2)}, u32[]{:S(2)}) collective-permute-start(bf16[136,1024]{1,0:T(8,128)(2,1)S(1)} %get-tuple-element.28.own_ref), channel_id=1, source_target_pairs={{0,8},{4,12},{8,16},{12,20},{16,24},{20,28},{24,0},{28,4},{1,9},{5... | collective-permute-start | bytes 835592 | tf_op jit(solution)/shard_map/ppermute | solution.py:20
  6.9 0.5 %collective-permute-start.2 = (bf16[136,512]{1,0:T(8,128)(2,1)S(1)}, bf16[136,512]{1,0:T(8,128)(2,1)S(1)}, u32[]{:S(2)}, u32[]{:S(2)}) collective-permute-start(bf16[136,512]{1,0:T(8,128)(2,1)S(1)} %get-tuple-element.37), channel_id=1, source_target_pairs={{0,4},{4,0},{8,12},{12,8},{16,20},{20,16},{24,28},{28,24},{1,5},{5... | collective-permute-start | bytes 417800 | tf_op jit(solution)/shard_map/ppermute | solution.py:20
  7.4 0.0 copy-done.5
  7.4 0.1 copy.8
  7.5 0.1 broadcast_in_dim.3
  7.5 0.0 copy-done.4
  7.6 0.0 copy-done.1
  7.6 0.0 copy-done
  7.6 2.9 %shard_map.74 = (bf16[8,2,128,768]{3,2,1,0:T(8,128)(2,1)S(1)}, bf16[8,128,256]{2,1,0:T(8,128)(2,1)S(1)}, f32[3,3,1024]{2,1,0:T(4,128)S(1)}, f32[4,8,128]{2,1,0:T(8,128)S(1)}) custom-call(s32[32]{0:T(128)S(1)} %copy-done.1, bf16[16,512]{1,0:T(8,128)(2,1)S(1)} %fusion.taps_ref, f32[3,3,2048]{2,1,0:T(4,128)S(1)} %copy-done), custom_call_target="tpu_custom_call" | custom-call | flops 20971520 | bytes 4194304 | tf_op jit(solution)/shard_map/pallas_call | solution.py:428
  10.5 0.0 collective-permute-done.pair_a_ref
  10.5 0.0 copy-start.2
  10.5 1.6 %collective-permute-start.3 = (bf16[136,512]{1,0:T(8,128)(2,1)S(1)}, bf16[136,512]{1,0:T(8,128)(2,1)S(1)}, u32[]{:S(2)}, u32[]{:S(2)}) collective-permute-start(bf16[136,512]{1,0:T(8,128)(2,1)S(1)} %collective-permute-done.pair_a_ref), channel_id=1, source_target_pairs={{0,8},{4,12},{8,16},{12,20},{16,24},{20,28},{24,0},{28,4},{1,9},{5... | collective-permute-start | bytes 417800 | tf_op jit(solution)/shard_map/ppermute | solution.py:20
  12.1 1.1 %dynamic-slice_bitcast_fusion = (bf16[128,1024]{1,0:T(8,128)(2,1)S(1)}, bf16[128,1024]{1,0:T(8,128)(2,1)S(1)}) fusion(bf16[3,128,2048]{2,1,0:T(8,128)(2,1)} %bitcast.19, s32[]{:T(128)S(6)} %select_n.7, s32[]{:T(128)S(6)} %select_n.6), kind=kLoop, calls=%fused_computation | loop fusion | bytes 1048584 | tf_op jit(solution)/shard_map/squeeze | solution.py:446
  13.2 0.0 collective-permute-done.2.pair_b_ref
  13.2 3.5 %collective-permute-start.4 = (bf16[136,512]{1,0:T(8,128)(2,1)S(1)}, bf16[136,512]{1,0:T(8,128)(2,1)S(1)}, u32[]{:S(2)}, u32[]{:S(2)}) collective-permute-start(bf16[136,512]{1,0:T(8,128)(2,1)S(1)} %collective-permute-done.2.pair_b_ref), channel_id=1, source_target_pairs={{0,8},{4,12},{8,16},{12,20},{16,24},{20,28},{1,9},{5,13},{9,17},{1... | collective-permute-start | bytes 417800 | tf_op jit(solution)/shard_map/ppermute | solution.py:20
  16.7 1.6 %collective-permute-start.5 = (bf16[128,1024]{1,0:T(8,128)(2,1)S(1)}, bf16[128,1024]{1,0:T(8,128)(2,1)S(1)}, u32[]{:S(2)}, u32[]{:S(2)}) collective-permute-start(bf16[128,1024]{1,0:T(8,128)(2,1)S(1)} %get-tuple-element.43), channel_id=1, source_target_pairs={{0,4},{4,0},{8,12},{12,8},{16,20},{20,16},{24,28},{28,24},{1,5},{5... | collective-permute-start | bytes 786440 | tf_op jit(solution)/shard_map/ppermute | solution.py:20
  18.3 0.0 collective-permute-done.1.back_own_ref
  18.3 0.0 collective-permute-done.3.back_a_ref.back_pair_ref
  18.3 0.2 shard_map.78
  18.4 0.7 %collective-permute-start.7 = (bf16[136,512]{1,0:T(8,128)(2,1)S(1)}, bf16[136,512]{1,0:T(8,128)(2,1)S(1)}, u32[]{:S(2)}, u32[]{:S(2)}) collective-permute-start(bf16[136,512]{1,0:T(8,128)(2,1)S(1)} %shard_map.78), channel_id=1, source_target_pairs={{0,4},{4,0},{8,16},{12,20},{16,24},{20,28},{24,8},{28,12},{1,5},{5... | collective-permute-start | bytes 417800 | tf_op jit(solution)/shard_map/ppermute | solution.py:20
  19.1 0.1 collective-permute-done.4.back_b_ref.back_pair_ref
  19.3 0.1 shard_map.77
  19.4 1.6 %collective-permute-start.6 = (bf16[136,512]{1,0:T(8,128)(2,1)S(1)}, bf16[136,512]{1,0:T(8,128)(2,1)S(1)}, u32[]{:S(2)}, u32[]{:S(2)}) collective-permute-start(bf16[136,512]{1,0:T(8,128)(2,1)S(1)} %shard_map.77), channel_id=1, source_target_pairs={{0,4},{4,0},{8,16},{12,20},{16,24},{20,28},{24,8},{28,12},{1,5},{5... | collective-permute-start | bytes 417800 | tf_op jit(solution)/shard_map/ppermute | solution.py:20
  21.0 0.0 copy-done.2
  21.0 1.0 %shard_map.75 = (f32[256,1024]{1,0:T(8,128)S(1)}, f32[128,1024]{1,0:T(8,128)S(1)}) custom-call(s32[1,32]{1,0:T(1,128)S(1)} %bitcast.14, f32[4,8,128]{2,1,0:T(8,128)S(1)} %get-tuple-element.34.marks_ref, bf16[8,2,128,768]{3,2,1,0:T(8,128)(2,1)S(1)} %get-tuple-element.33.table_ref, bf16[136,1024]{1,0:T(8,128)(2,1)S(1)} %get-tuple-element.28.own_ref, ...), custom_call_target="tpu_custom_call" | custom-call | flops 167772160 | bytes 2097152 | tf_op jit(solution)/shard_map/pallas_call | solution.py:475
  22.0 4.0 %collective-permute-done.5.raw_ref = bf16[128,1024]{1,0:T(8,128)(2,1)S(1)} collective-permute-done((bf16[128,1024]{1,0:T(8,128)(2,1)S(1)}, bf16[128,1024]{1,0:T(8,128)(2,1)S(1)}, u32[]{:S(2)}, u32[]{:S(2)}) %collective-permute-start.5) | collective-permute-done | bytes 262176 | tf_op jit(solution)/shard_map/ppermute | solution.py:20
  26.0 0.4 shard_map.76.qpair_ref
  26.4 1.5 %collective-permute-done.7.refs_0_ = bf16[136,512]{1,0:T(8,128)(2,1)S(1)} collective-permute-done((bf16[136,512]{1,0:T(8,128)(2,1)S(1)}, bf16[136,512]{1,0:T(8,128)(2,1)S(1)}, u32[]{:S(2)}, u32[]{:S(2)}) %collective-permute-start.7) | collective-permute-done | bytes 139296 | tf_op jit(solution)/shard_map/ppermute | solution.py:20
  27.9 0.4 shard_map.79
  28.3 1.1 %collective-permute-done.6.refs_0_ = bf16[136,512]{1,0:T(8,128)(2,1)S(1)} collective-permute-done((bf16[136,512]{1,0:T(8,128)(2,1)S(1)}, bf16[136,512]{1,0:T(8,128)(2,1)S(1)}, u32[]{:S(2)}, u32[]{:S(2)}) %collective-permute-start.6) | collective-permute-done | bytes 139296 | tf_op jit(solution)/shard_map/ppermute | solution.py:20
  29.4 0.7 %shard_map.80 = (f32[128,512]{1,0:T(8,128)S(1)}, bf16[128,1024]{1,0:T(8,128)(2,1)S(1)}, f32[1,256]{1,0:T(1,128)S(1)}) custom-call(bf16[8,2,128,768]{3,2,1,0:T(8,128)(2,1)S(1)} %get-tuple-element.33.table_ref, f32[256,1024]{1,0:T(8,128)S(1)} %get-tuple-element.41.acc_ref, f32[128,1024]{1,0:T(8,128)S(1)} %get-tuple-element.42.qown_ref, ...), custom_call_target="tpu_custom_call" | custom-call | flops 100663296 | bytes 1572864 | tf_op jit(solution)/shard_map/pallas_call | solution.py:497
  30.1 1.5 %collective-permute-start.12 = (bf16[128,1024]{1,0:T(8,128)(2,1)S(1)}, bf16[128,1024]{1,0:T(8,128)(2,1)S(1)}, u32[]{:S(2)}, u32[]{:S(2)}) collective-permute-start(bf16[128,1024]{1,0:T(8,128)(2,1)S(1)} %get-tuple-element.50), channel_id=1, source_target_pairs={{0,4},{4,0},{8,12},{12,8},{16,20},{20,16},{24,28},{28,24},{1,5},{5... | collective-permute-start | bytes 786440 | tf_op jit(solution)/shard_map/ppermute | solution.py:20
  31.6 0.0 collective-permute-start.10
  31.6 1.5 %collective-permute-start.9 = (f32[1,256]{1,0:T(1,128)S(1)}, f32[1,256]{1,0:T(1,128)S(1)}, u32[]{:S(2)}, u32[]{:S(2)}) collective-permute-start(f32[1,256]{1,0:T(1,128)S(1)} %get-tuple-element.47), channel_id=1, source_target_pairs={{0,2},{1,3},{2,0},{3,1},{4,6},{5,7},{6,4},{7,5},{8,10},{9,11},{10,... | collective-permute-start | bytes 3080 | tf_op jit(solution)/shard_map/ppermute | solution.py:513
  33.1 0.3 collective-permute-start.8
  33.5 1.1 %collective-permute-done.10 = f32[1,256]{1,0:T(1,128)S(1)} collective-permute-done((f32[1,256]{1,0:T(1,128)S(1)}, f32[1,256]{1,0:T(1,128)S(1)}, u32[]{:S(2)}, u32[]{:S(2)}) %collective-permute-start.10) | collective-permute-done | bytes 1056 | tf_op jit(solution)/shard_map/ppermute | solution.py:513
  34.6 0.6 %collective-permute-done.9 = f32[1,256]{1,0:T(1,128)S(1)} collective-permute-done((f32[1,256]{1,0:T(1,128)S(1)}, f32[1,256]{1,0:T(1,128)S(1)}, u32[]{:S(2)}, u32[]{:S(2)}) %collective-permute-start.9) | collective-permute-done | bytes 1056 | tf_op jit(solution)/shard_map/ppermute | solution.py:513
  35.2 0.0 collective-permute-done.8
  35.2 0.6 %collective-permute-start.11 = (f32[1,256]{1,0:T(1,128)S(1)}, f32[1,256]{1,0:T(1,128)S(1)}, u32[]{:S(2)}, u32[]{:S(2)}) collective-permute-start(f32[1,256]{1,0:T(1,128)S(1)} %add_add_fusion.power_ref), channel_id=1, source_target_pairs={{0,4},{4,0},{8,12},{12,8},{16,20},{20,16},{24,28},{28,24},{1,5},{5... | collective-permute-start | bytes 3080 | tf_op jit(solution)/shard_map/ppermute | solution.py:20
  35.8 3.1 %collective-permute-done.11.power_got_ref = f32[1,256]{1,0:T(1,128)S(1)} collective-permute-done((f32[1,256]{1,0:T(1,128)S(1)}, f32[1,256]{1,0:T(1,128)S(1)}, u32[]{:S(2)}, u32[]{:S(2)}) %collective-permute-start.11) | collective-permute-done | bytes 1056 | tf_op jit(solution)/shard_map/ppermute | solution.py:20
  38.9 0.0 collective-permute-done.12.refs_2_
  38.9 0.0 copy-done.3
  38.9 1.0 %shard_map.81 = bf16[128,2048]{1,0:T(8,128)(2,1)} custom-call(f32[1,256]{1,0:T(1,128)S(1)} %add_add_fusion.power_ref, f32[1,256]{1,0:T(1,128)S(1)} %collective-permute-done.11.power_got_ref, f32[128,512]{1,0:T(8,128)S(1)} %get-tuple-element.48.refs_0_, f32[128,512]{1,0:T(8,128)S(1)} %get-tuple-element.49.refs_1_, ...), custom_call_target="tpu_custom_call" | custom-call | flops 1048576 | bytes 1310720 | tf_op jit(solution)/shard_map/pallas_call | solution.py:515
  (5 shorter events, 0.0 us)
Async XLA Ops:
  0.0 7.6 %copy-start.1 = (s32[32]{0:T(128)S(1)}, s32[32]{0:T(128)}, u32[]{:S(2)}) copy-start(s32[32]{0:T(128)} %seq_ref.1) | copy-start | bytes 388
  0.0 7.6 %copy-start = (f32[3,3,2048]{2,1,0:T(4,128)S(1)}, f32[3,3,2048]{2,1,0:T(4,128)}, u32[]{:S(2)}) copy-start(f32[3,3,2048]{2,1,0:T(4,128)} %w_ref.1) | copy-start | bytes 221188
  0.0 7.5 %copy-start.4 = (f32[16,512]{1,0:T(8,128)S(1)}, f32[16,512]{1,0:T(8,128)}, u32[]{:S(2)}) copy-start(f32[16,512]{1,0:T(8,128)} %param.9) | copy-start | bytes 98308
  0.0 7.4 %copy-start.5 = (s32[16,4]{0,1:T(4,128)S(1)}, s32[16,4]{0,1:T(4,128)}, u32[]{:S(2)}) copy-start(s32[16,4]{0,1:T(4,128)} %param.10) | copy-start | bytes 772
  2.3 8.2 %collective-permute-start = (bf16[136,512]{1,0:T(8,128)(2,1)S(1)}, bf16[136,512]{1,0:T(8,128)(2,1)S(1)}, u32[]{:S(2)}, u32[]{:S(2)}) collective-permute-start(bf16[136,512]{1,0:T(8,128)(2,1)S(1)} %get-tuple-element.32), channel_id=1, source_target_pairs={{0,4},{4,0},{8,12},{12,8},{16,20},{20,16},{24,28},{28,24},{1,5},{5... | collective-permute-start | bytes 417800 | tf_op jit(solution)/shard_map/ppermute | solution.py:20
  5.3 13.0 %collective-permute-start.1 = (bf16[136,1024]{1,0:T(8,128)(2,1)S(1)}, bf16[136,1024]{1,0:T(8,128)(2,1)S(1)}, u32[]{:S(2)}, u32[]{:S(2)}) collective-permute-start(bf16[136,1024]{1,0:T(8,128)(2,1)S(1)} %get-tuple-element.28.own_ref), channel_id=1, source_target_pairs={{0,8},{4,12},{8,16},{12,20},{16,24},{20,28},{24,0},{28,4},{1,9},{5... | collective-permute-start | bytes 835592 | tf_op jit(solution)/shard_map/ppermute | solution.py:20
  6.9 6.3 %collective-permute-start.2 = (bf16[136,512]{1,0:T(8,128)(2,1)S(1)}, bf16[136,512]{1,0:T(8,128)(2,1)S(1)}, u32[]{:S(2)}, u32[]{:S(2)}) collective-permute-start(bf16[136,512]{1,0:T(8,128)(2,1)S(1)} %get-tuple-element.37), channel_id=1, source_target_pairs={{0,4},{4,0},{8,12},{12,8},{16,20},{20,16},{24,28},{28,24},{1,5},{5... | collective-permute-start | bytes 417800 | tf_op jit(solution)/shard_map/ppermute | solution.py:20
  10.5 10.5 %copy-start.2 = (f32[2048]{0:T(1024)S(1)}, f32[2048]{0:T(1024)}, u32[]{:S(2)}) copy-start(f32[2048]{0:T(1024)} %param.11) | copy-start | bytes 24580
  10.5 7.8 %collective-permute-start.3 = (bf16[136,512]{1,0:T(8,128)(2,1)S(1)}, bf16[136,512]{1,0:T(8,128)(2,1)S(1)}, u32[]{:S(2)}, u32[]{:S(2)}) collective-permute-start(bf16[136,512]{1,0:T(8,128)(2,1)S(1)} %collective-permute-done.pair_a_ref), channel_id=1, source_target_pairs={{0,8},{4,12},{8,16},{12,20},{16,24},{20,28},{24,0},{28,4},{1,9},{5... | collective-permute-start | bytes 417800 | tf_op jit(solution)/shard_map/ppermute | solution.py:20
  13.2 6.1 %collective-permute-start.4 = (bf16[136,512]{1,0:T(8,128)(2,1)S(1)}, bf16[136,512]{1,0:T(8,128)(2,1)S(1)}, u32[]{:S(2)}, u32[]{:S(2)}) collective-permute-start(bf16[136,512]{1,0:T(8,128)(2,1)S(1)} %collective-permute-done.2.pair_b_ref), channel_id=1, source_target_pairs={{0,8},{4,12},{8,16},{12,20},{16,24},{20,28},{1,9},{5,13},{9,17},{1... | collective-permute-start | bytes 417800 | tf_op jit(solution)/shard_map/ppermute | solution.py:20
  16.7 9.3 %collective-permute-start.5 = (bf16[128,1024]{1,0:T(8,128)(2,1)S(1)}, bf16[128,1024]{1,0:T(8,128)(2,1)S(1)}, u32[]{:S(2)}, u32[]{:S(2)}) collective-permute-start(bf16[128,1024]{1,0:T(8,128)(2,1)S(1)} %get-tuple-element.43), channel_id=1, source_target_pairs={{0,4},{4,0},{8,12},{12,8},{16,20},{20,16},{24,28},{28,24},{1,5},{5... | collective-permute-start | bytes 786440 | tf_op jit(solution)/shard_map/ppermute | solution.py:20
  18.4 9.4 %collective-permute-start.7 = (bf16[136,512]{1,0:T(8,128)(2,1)S(1)}, bf16[136,512]{1,0:T(8,128)(2,1)S(1)}, u32[]{:S(2)}, u32[]{:S(2)}) collective-permute-start(bf16[136,512]{1,0:T(8,128)(2,1)S(1)} %shard_map.78), channel_id=1, source_target_pairs={{0,4},{4,0},{8,16},{12,20},{16,24},{20,28},{24,8},{28,12},{1,5},{5... | collective-permute-start | bytes 417800 | tf_op jit(solution)/shard_map/ppermute | solution.py:20
  19.4 10.0 %collective-permute-start.6 = (bf16[136,512]{1,0:T(8,128)(2,1)S(1)}, bf16[136,512]{1,0:T(8,128)(2,1)S(1)}, u32[]{:S(2)}, u32[]{:S(2)}) collective-permute-start(bf16[136,512]{1,0:T(8,128)(2,1)S(1)} %shard_map.77), channel_id=1, source_target_pairs={{0,4},{4,0},{8,16},{12,20},{16,24},{20,28},{24,8},{28,12},{1,5},{5... | collective-permute-start | bytes 417800 | tf_op jit(solution)/shard_map/ppermute | solution.py:20
  29.4 9.5 %copy-start.3 = (f32[2048]{0:T(1024)S(1)}, f32[2048]{0:T(1024)}, u32[]{:S(2)}) copy-start(f32[2048]{0:T(1024)} %param.12) | copy-start | bytes 24580
  30.1 8.8 %collective-permute-start.12 = (bf16[128,1024]{1,0:T(8,128)(2,1)S(1)}, bf16[128,1024]{1,0:T(8,128)(2,1)S(1)}, u32[]{:S(2)}, u32[]{:S(2)}) collective-permute-start(bf16[128,1024]{1,0:T(8,128)(2,1)S(1)} %get-tuple-element.50), channel_id=1, source_target_pairs={{0,4},{4,0},{8,12},{12,8},{16,20},{20,16},{24,28},{28,24},{1,5},{5... | collective-permute-start | bytes 786440 | tf_op jit(solution)/shard_map/ppermute | solution.py:20
  31.6 3.0 %collective-permute-start.10 = (f32[1,256]{1,0:T(1,128)S(1)}, f32[1,256]{1,0:T(1,128)S(1)}, u32[]{:S(2)}, u32[]{:S(2)}) collective-permute-start(f32[1,256]{1,0:T(1,128)S(1)} %get-tuple-element.47), channel_id=1, source_target_pairs={{0,3},{1,2},{2,1},{3,0},{4,7},{5,6},{6,5},{7,4},{8,11},{9,10},{10,... | collective-permute-start | bytes 3080 | tf_op jit(solution)/shard_map/ppermute | solution.py:513
  31.6 3.6 %collective-permute-start.9 = (f32[1,256]{1,0:T(1,128)S(1)}, f32[1,256]{1,0:T(1,128)S(1)}, u32[]{:S(2)}, u32[]{:S(2)}) collective-permute-start(f32[1,256]{1,0:T(1,128)S(1)} %get-tuple-element.47), channel_id=1, source_target_pairs={{0,2},{1,3},{2,0},{3,1},{4,6},{5,7},{6,4},{7,5},{8,10},{9,11},{10,... | collective-permute-start | bytes 3080 | tf_op jit(solution)/shard_map/ppermute | solution.py:513
  33.1 2.1 %collective-permute-start.8 = (f32[1,256]{1,0:T(1,128)S(1)}, f32[1,256]{1,0:T(1,128)S(1)}, u32[]{:S(2)}, u32[]{:S(2)}) collective-permute-start(f32[1,256]{1,0:T(1,128)S(1)} %get-tuple-element.47), channel_id=1, source_target_pairs={{0,1},{1,0},{2,3},{3,2},{4,5},{5,4},{6,7},{7,6},{8,9},{9,8},{10,11... | collective-permute-start | bytes 3080 | tf_op jit(solution)/shard_map/ppermute | solution.py:513
  35.2 3.6 %collective-permute-start.11 = (f32[1,256]{1,0:T(1,128)S(1)}, f32[1,256]{1,0:T(1,128)S(1)}, u32[]{:S(2)}, u32[]{:S(2)}) collective-permute-start(f32[1,256]{1,0:T(1,128)S(1)} %add_add_fusion.power_ref), channel_id=1, source_target_pairs={{0,4},{4,0},{8,12},{12,8},{16,20},{20,16},{24,28},{28,24},{1,5},{5... | collective-permute-start | bytes 3080 | tf_op jit(solution)/shard_map/ppermute | solution.py:20

commit v20 on v19

--- a/solution.py
+++ b/solution.py
@@ -204,7 +204,13 @@
         at += piece.shape[1]
 
 
-def relay_kernel(piece, marks_ref, next_ref, back_own_ref, back_pair_ref, w_ref, out_ref, win_ref, extra_ref):
+def relay_kernel(piece, marks_ref, next_ref, back_own_ref, w_ref, *refs):
+    *ways, out_ref, back_pair_ref, win_ref, extra_ref = refs
+    for i, way in enumerate(ways):
+        @pl.when((lax.axis_index("blk") + i) % len(ways) == 0)
+        def _():
+            back_pair_ref[...] = way[...]
+
     width = out_ref.shape[1]
     half = lax.axis_index("half")
     lanes = slice(piece * width, (piece + 1) * width)
@@ -380,6 +386,15 @@
     )
 
 
+def matching(blocks, first):
+    pairs = []
+    for i in range(2 * blocks):
+        block = i // 2
+        partner = block + 1 if (block - first) % 2 == 0 else block - 1
+        pairs.append((i, 2 * partner + i % 2 if 0 <= partner < blocks else i ^ 1))
+    return pairs
+
+
 def shards(blocks, whole_tokens, channels, projected, short_weight, filter_taps, tap_blocks, skip_bias, norm_gain, seq_lengths):
     rows = projected.shape[0]
     width = projected.shape[2] // 2
@@ -446,7 +461,7 @@
     qsent = lax.dynamic_slice(query, (0, 0, (1 - half) * width), (1, rows, width))[0]
     qkept, qsent, pair[1] = lax.optimization_barrier((qkept, qsent, pair[1]))
     qgot = moved(qsent, to_pair)
-    back_pair = [moved(pair[0], ahead), moved(pair[1], [(i, j) for i, j in ahead if i < j])]
+    back_pair = [[moved(pair[0], ahead)], [moved(pair[1], matching(blocks, first)) for first in (1, 0)]]
 
     window = pltpu.VMEM((4 * rows, width), jnp.bfloat16)
     extras = pltpu.VMEM((4, 16, width), jnp.float32)
@@ -456,16 +471,17 @@
         onward = [(i, i ^ 1 if i < 2 else i + 2 if i + 2 < 2 * blocks else 2 + i % 2) for i in spots]
         far = []
         for piece in range(2):
-            relayed = kernel_call(
+            relayed, back_pair[piece] = kernel_call(
                 functools.partial(relay_kernel, piece),
-                small,
-                [VMEM] * 5,
+                (small, small),
+                [VMEM] * (4 + len(back_pair[piece])),
                 [pltpu.VMEM((2 * rows, width // 2), jnp.bfloat16), pltpu.VMEM((2, 16, width // 2), jnp.float32)],
                 2 * rows * BLK * width,
                 4 * rows * width,
-            )(marks, table_next, back_own, back_pair[piece], w_half)
+            )(marks, table_next, back_own, w_half, *back_pair[piece])
             far.append(moved(relayed, onward))
     else:
+        back_pair = [moved(piece, ahead) for piece in pair]
         across = jnp.concatenate([piece[rows:] for piece in sent], 1)
         across = moved(across, [(i, ((i ^ 1) + 6) % (2 * blocks)) for i in spots])
         straight = moved(kept[rows:], [(i, (i + 6) % (2 * blocks)) for i in spots])

time: 40.1 us -> 40.1 us (level)
  starting transfers between devices: 18.1 us -> 15.9 us
  waiting for transfers between devices: 11.6 us -> 13.7 us
    ppermute x10 -> x11, waiting for transfers between devices: 9.84 us -> 12 us  [moved(): return lax.ppermute(block, SPOTS, pairs)]
    ppermute x10 -> x11, starting transfers between devices: 16.2 us -> 14 us  [moved(): return lax.ppermute(block, SPOTS, pairs)]
  transfers between devices with their start and end apart: 13 -> 14, of which waited for: 7 -> 8; matrix products, arithmetic and copies ran while one was open for 3% -> 3% of each run, Pallas kernels for 12% -> 12%
where the time goes in v20:
time: 40.1 us; the launch traced here: 39.9 us
  starting transfers between devices  15.9 us (40%)
  waiting for transfers between devices  13.7 us (34%)
  Pallas kernels  8.86 us (22%)
  local copies, waits for them, and re-layouts  1.25 us (3%)
    ppermute x11, starting transfers between devices, moved(): return lax.ppermute(block, SPOTS, pairs)  14 us
    ppermute x11, waiting for transfers between devices, moved(): return lax.ppermute(block, SPOTS, pairs)  12 us
    pallas_call x1, Pallas kernels, shards(): kernel_call(tables_kernel, (shape((groups, 2, BLK, span), jnp.bfloat16),...  2.85 us
    pallas_call x1, Pallas kernels, shards(): kernel_call(products_kernel, (message, small, small), [hbm] * 3, [pltpu.V...  2.23 us
    ppermute x3, starting transfers between devices, shards(): lax.ppermute(power, 'mp', [(i, i ^ k) for i in range(peers)])  1.86 us
    ppermute x3, waiting for transfers between devices, shards(): lax.ppermute(power, 'mp', [(i, i ^ k) for i in range(peers)])  1.74 us
    pallas_call x2, Pallas kernels, shards(): kernel_call(functools.partial(far_kernel, short, piece), (shape((rows, wi...  1.08 us
    squeeze x1, local copies, waits for them, and re-layouts, shards(): lax.dynamic_slice(query, (0, 0, (1 - half) * width), (1, rows, width))[0]  1.06 us
  transfers between devices with their start and end apart: 14, of which 8 were waited for; matrix products, arithmetic and copies ran while one was open for 3% of the time, Pallas kernels for 12%

profile of v20, /device:TPU:0, one launch (start us, length us, event | category | flops | bytes accessed | tf_op | source)
XLA Modules:
  0.0 39.9 jit_solution(11920993492765677180)
XLA Ops:
  0.0 0.0 copy-start.1
  0.0 2.2 %shard_map.73 = (bf16[136,1024]{1,0:T(8,128)(2,1)S(1)}, bf16[136,512]{1,0:T(8,128)(2,1)S(1)}, bf16[136,512]{1,0:T(8,128)(2,1)S(1)}) custom-call(s32[1,32]{1,0:T(1,128)} %bitcast.13, bf16[3,128,2048]{2,1,0:T(8,128)(2,1)} %bitcast.18, f32[3,3,2048]{2,1,0:T(4,128)} %w_ref.1), custom_call_target="tpu_custom_call" | custom-call | flops 5242880 | bytes 2097152 | tf_op jit(solution)/shard_map/pallas_call | solution.py:419
  2.3 3.0 %collective-permute-start = (bf16[136,512]{1,0:T(8,128)(2,1)S(1)}, bf16[136,512]{1,0:T(8,128)(2,1)S(1)}, u32[]{:S(2)}, u32[]{:S(2)}) collective-permute-start(bf16[136,512]{1,0:T(8,128)(2,1)S(1)} %get-tuple-element.36), channel_id=1, source_target_pairs={{0,4},{4,0},{8,12},{12,8},{16,20},{20,16},{24,28},{28,24},{1,5},{5... | collective-permute-start | bytes 417800 | tf_op jit(solution)/shard_map/ppermute | solution.py:20
  5.3 1.6 %collective-permute-start.1 = (bf16[136,1024]{1,0:T(8,128)(2,1)S(1)}, bf16[136,1024]{1,0:T(8,128)(2,1)S(1)}, u32[]{:S(2)}, u32[]{:S(2)}) collective-permute-start(bf16[136,1024]{1,0:T(8,128)(2,1)S(1)} %get-tuple-element.32.own_ref), channel_id=1, source_target_pairs={{0,8},{4,12},{8,16},{12,20},{16,24},{20,28},{24,0},{28,4},{1,9},{5... | collective-permute-start | bytes 835592 | tf_op jit(solution)/shard_map/ppermute | solution.py:20
  6.9 0.5 %collective-permute-start.2 = (bf16[136,512]{1,0:T(8,128)(2,1)S(1)}, bf16[136,512]{1,0:T(8,128)(2,1)S(1)}, u32[]{:S(2)}, u32[]{:S(2)}) collective-permute-start(bf16[136,512]{1,0:T(8,128)(2,1)S(1)} %get-tuple-element.41), channel_id=1, source_target_pairs={{0,4},{4,0},{8,12},{12,8},{16,20},{20,16},{24,28},{28,24},{1,5},{5... | collective-permute-start | bytes 417800 | tf_op jit(solution)/shard_map/ppermute | solution.py:20
  7.4 0.0 copy-done.5
  7.4 0.1 copy.8
  7.5 0.1 broadcast_in_dim.3
  7.5 0.0 copy-done.4
  7.6 0.0 copy-done.1
  7.6 0.0 copy-done
  7.6 2.9 %shard_map.74 = (bf16[8,2,128,768]{3,2,1,0:T(8,128)(2,1)S(1)}, bf16[8,128,256]{2,1,0:T(8,128)(2,1)S(1)}, f32[3,3,1024]{2,1,0:T(4,128)S(1)}, f32[4,8,128]{2,1,0:T(8,128)S(1)}) custom-call(s32[32]{0:T(128)S(1)} %copy-done.1, bf16[16,512]{1,0:T(8,128)(2,1)S(1)} %fusion.taps_ref, f32[3,3,2048]{2,1,0:T(4,128)S(1)} %copy-done), custom_call_target="tpu_custom_call" | custom-call | flops 20971520 | bytes 4194304 | tf_op jit(solution)/shard_map/pallas_call | solution.py:443
  10.5 0.0 collective-permute-done.pair_a_ref
  10.5 0.0 copy-start.2
  10.5 1.6 %collective-permute-start.3 = (bf16[136,512]{1,0:T(8,128)(2,1)S(1)}, bf16[136,512]{1,0:T(8,128)(2,1)S(1)}, u32[]{:S(2)}, u32[]{:S(2)}) collective-permute-start(bf16[136,512]{1,0:T(8,128)(2,1)S(1)} %collective-permute-done.pair_a_ref), channel_id=1, source_target_pairs={{0,8},{4,12},{8,16},{12,20},{16,24},{20,28},{24,0},{28,4},{1,9},{5... | collective-permute-start | bytes 417800 | tf_op jit(solution)/shard_map/ppermute | solution.py:20
  12.1 1.1 %dynamic-slice_bitcast_fusion = (bf16[128,1024]{1,0:T(8,128)(2,1)S(1)}, bf16[128,1024]{1,0:T(8,128)(2,1)S(1)}) fusion(bf16[3,128,2048]{2,1,0:T(8,128)(2,1)} %bitcast.19, s32[]{:T(128)S(6)} %select_n.7, s32[]{:T(128)S(6)} %select_n.6), kind=kLoop, calls=%fused_computation | loop fusion | bytes 1048584 | tf_op jit(solution)/shard_map/squeeze | solution.py:461
  13.2 0.0 collective-permute-done.2.pair_b_ref
  13.2 1.6 %collective-permute-start.4 = (bf16[136,512]{1,0:T(8,128)(2,1)S(1)}, bf16[136,512]{1,0:T(8,128)(2,1)S(1)}, u32[]{:S(2)}, u32[]{:S(2)}) collective-permute-start(bf16[136,512]{1,0:T(8,128)(2,1)S(1)} %collective-permute-done.2.pair_b_ref), channel_id=1, source_target_pairs={{0,4},{4,0},{8,16},{12,20},{16,8},{20,12},{24,28},{28,24},{1,5},{5... | collective-permute-start | bytes 417800 | tf_op jit(solution)/shard_map/ppermute | solution.py:20
  14.8 1.4 %collective-permute-start.5 = (bf16[136,512]{1,0:T(8,128)(2,1)S(1)}, bf16[136,512]{1,0:T(8,128)(2,1)S(1)}, u32[]{:S(2)}, u32[]{:S(2)}) collective-permute-start(bf16[136,512]{1,0:T(8,128)(2,1)S(1)} %collective-permute-done.2.pair_b_ref), channel_id=1, source_target_pairs={{0,8},{4,12},{8,0},{12,4},{16,24},{20,28},{24,16},{28,20},{1,9},{5... | collective-permute-start | bytes 417800 | tf_op jit(solution)/shard_map/ppermute | solution.py:20
  16.2 1.5 %collective-permute-start.6 = (bf16[128,1024]{1,0:T(8,128)(2,1)S(1)}, bf16[128,1024]{1,0:T(8,128)(2,1)S(1)}, u32[]{:S(2)}, u32[]{:S(2)}) collective-permute-start(bf16[128,1024]{1,0:T(8,128)(2,1)S(1)} %get-tuple-element.50), channel_id=1, source_target_pairs={{0,4},{4,0},{8,12},{12,8},{16,20},{20,16},{24,28},{28,24},{1,5},{5... | collective-permute-start | bytes 786440 | tf_op jit(solution)/shard_map/ppermute | solution.py:20
  17.7 0.0 collective-permute-done.1.back_own_ref
  17.7 1.8 %collective-permute-done.3.refs_0_ = bf16[136,512]{1,0:T(8,128)(2,1)S(1)} collective-permute-done((bf16[136,512]{1,0:T(8,128)(2,1)S(1)}, bf16[136,512]{1,0:T(8,128)(2,1)S(1)}, u32[]{:S(2)}, u32[]{:S(2)}) %collective-permute-start.3) | collective-permute-done | bytes 139296 | tf_op jit(solution)/shard_map/ppermute | solution.py:20
  19.5 0.1 shard_map.75
  19.7 0.1 collective-permute-start.8
  19.8 0.0 collective-permute-done.4.refs_0_
  19.8 1.5 %collective-permute-done.5.refs_1_ = bf16[136,512]{1,0:T(8,128)(2,1)S(1)} collective-permute-done((bf16[136,512]{1,0:T(8,128)(2,1)S(1)}, bf16[136,512]{1,0:T(8,128)(2,1)S(1)}, u32[]{:S(2)}, u32[]{:S(2)}) %collective-permute-start.5) | collective-permute-done | bytes 139296 | tf_op jit(solution)/shard_map/ppermute | solution.py:20
  21.3 0.2 shard_map.76
  21.4 0.6 %collective-permute-start.7 = (bf16[136,512]{1,0:T(8,128)(2,1)S(1)}, bf16[136,512]{1,0:T(8,128)(2,1)S(1)}, u32[]{:S(2)}, u32[]{:S(2)}) collective-permute-start(bf16[136,512]{1,0:T(8,128)(2,1)S(1)} %get-tuple-element.51), channel_id=1, source_target_pairs={{0,4},{4,0},{8,16},{12,20},{16,24},{20,28},{24,8},{28,12},{1,5},{5... | collective-permute-start | bytes 417800 | tf_op jit(solution)/shard_map/ppermute | solution.py:20
  22.0 0.0 copy-done.2
  22.0 1.0 %shard_map.77 = (f32[256,1024]{1,0:T(8,128)S(1)}, f32[128,1024]{1,0:T(8,128)S(1)}) custom-call(s32[1,32]{1,0:T(1,128)S(1)} %bitcast.14, f32[4,8,128]{2,1,0:T(8,128)S(1)} %get-tuple-element.38.marks_ref, bf16[8,2,128,768]{3,2,1,0:T(8,128)(2,1)S(1)} %get-tuple-element.37.table_ref, bf16[136,1024]{1,0:T(8,128)(2,1)S(1)} %get-tuple-element.32.own_ref, ...), custom_call_target="tpu_custom_call" | custom-call | flops 167772160 | bytes 2097152 | tf_op jit(solution)/shard_map/pallas_call | solution.py:491
  23.0 2.5 %collective-permute-done.6.raw_ref = bf16[128,1024]{1,0:T(8,128)(2,1)S(1)} collective-permute-done((bf16[128,1024]{1,0:T(8,128)(2,1)S(1)}, bf16[128,1024]{1,0:T(8,128)(2,1)S(1)}, u32[]{:S(2)}, u32[]{:S(2)}) %collective-permute-start.6) | collective-permute-done | bytes 262176 | tf_op jit(solution)/shard_map/ppermute | solution.py:20
  25.5 0.4 shard_map.78.qpair_ref
  25.8 1.9 %collective-permute-done.8.refs_0_ = bf16[136,512]{1,0:T(8,128)(2,1)S(1)} collective-permute-done((bf16[136,512]{1,0:T(8,128)(2,1)S(1)}, bf16[136,512]{1,0:T(8,128)(2,1)S(1)}, u32[]{:S(2)}, u32[]{:S(2)}) %collective-permute-start.8) | collective-permute-done | bytes 139296 | tf_op jit(solution)/shard_map/ppermute | solution.py:20
  27.7 0.4 shard_map.79
  28.1 1.1 %collective-permute-done.7.refs_0_ = bf16[136,512]{1,0:T(8,128)(2,1)S(1)} collective-permute-done((bf16[136,512]{1,0:T(8,128)(2,1)S(1)}, bf16[136,512]{1,0:T(8,128)(2,1)S(1)}, u32[]{:S(2)}, u32[]{:S(2)}) %collective-permute-start.7) | collective-permute-done | bytes 139296 | tf_op jit(solution)/shard_map/ppermute | solution.py:20
  29.2 0.7 %shard_map.80 = (f32[128,512]{1,0:T(8,128)S(1)}, bf16[128,1024]{1,0:T(8,128)(2,1)S(1)}, f32[1,256]{1,0:T(1,128)S(1)}) custom-call(bf16[8,2,128,768]{3,2,1,0:T(8,128)(2,1)S(1)} %get-tuple-element.37.table_ref, f32[256,1024]{1,0:T(8,128)S(1)} %get-tuple-element.48.acc_ref, f32[128,1024]{1,0:T(8,128)S(1)} %get-tuple-element.49.qown_ref, ...), custom_call_target="tpu_custom_call" | custom-call | flops 100663296 | bytes 1572864 | tf_op jit(solution)/shard_map/pallas_call | solution.py:513
  29.9 1.7 %collective-permute-start.13 = (bf16[128,1024]{1,0:T(8,128)(2,1)S(1)}, bf16[128,1024]{1,0:T(8,128)(2,1)S(1)}, u32[]{:S(2)}, u32[]{:S(2)}) collective-permute-start(bf16[128,1024]{1,0:T(8,128)(2,1)S(1)} %get-tuple-element.58), channel_id=1, source_target_pairs={{0,4},{4,0},{8,12},{12,8},{16,20},{20,16},{24,28},{28,24},{1,5},{5... | collective-permute-start | bytes 786440 | tf_op jit(solution)/shard_map/ppermute | solution.py:20
  31.6 0.0 collective-permute-start.11
  31.6 1.5 %collective-permute-start.10 = (f32[1,256]{1,0:T(1,128)S(1)}, f32[1,256]{1,0:T(1,128)S(1)}, u32[]{:S(2)}, u32[]{:S(2)}) collective-permute-start(f32[1,256]{1,0:T(1,128)S(1)} %get-tuple-element.55), channel_id=1, source_target_pairs={{0,2},{1,3},{2,0},{3,1},{4,6},{5,7},{6,4},{7,5},{8,10},{9,11},{10,... | collective-permute-start | bytes 3080 | tf_op jit(solution)/shard_map/ppermute | solution.py:529
  33.2 0.3 collective-permute-start.9
  33.5 1.1 %collective-permute-done.11 = f32[1,256]{1,0:T(1,128)S(1)} collective-permute-done((f32[1,256]{1,0:T(1,128)S(1)}, f32[1,256]{1,0:T(1,128)S(1)}, u32[]{:S(2)}, u32[]{:S(2)}) %collective-permute-start.11) | collective-permute-done | bytes 1056 | tf_op jit(solution)/shard_map/ppermute | solution.py:529
  34.6 0.6 %collective-permute-done.10 = f32[1,256]{1,0:T(1,128)S(1)} collective-permute-done((f32[1,256]{1,0:T(1,128)S(1)}, f32[1,256]{1,0:T(1,128)S(1)}, u32[]{:S(2)}, u32[]{:S(2)}) %collective-permute-start.10) | collective-permute-done | bytes 1056 | tf_op jit(solution)/shard_map/ppermute | solution.py:529
  35.2 0.0 collective-permute-done.9
  35.2 0.4 %collective-permute-start.12 = (f32[1,256]{1,0:T(1,128)S(1)}, f32[1,256]{1,0:T(1,128)S(1)}, u32[]{:S(2)}, u32[]{:S(2)}) collective-permute-start(f32[1,256]{1,0:T(1,128)S(1)} %add_add_fusion.power_ref), channel_id=1, source_target_pairs={{0,4},{4,0},{8,12},{12,8},{16,20},{20,16},{24,28},{28,24},{1,5},{5... | collective-permute-start | bytes 3080 | tf_op jit(solution)/shard_map/ppermute | solution.py:20
  35.7 3.2 %collective-permute-done.12.power_got_ref = f32[1,256]{1,0:T(1,128)S(1)} collective-permute-done((f32[1,256]{1,0:T(1,128)S(1)}, f32[1,256]{1,0:T(1,128)S(1)}, u32[]{:S(2)}, u32[]{:S(2)}) %collective-permute-start.12) | collective-permute-done | bytes 1056 | tf_op jit(solution)/shard_map/ppermute | solution.py:20
  38.9 0.0 collective-permute-done.13.refs_2_
  38.9 0.0 copy-done.3
  38.9 1.0 %shard_map.81 = bf16[128,2048]{1,0:T(8,128)(2,1)} custom-call(f32[1,256]{1,0:T(1,128)S(1)} %add_add_fusion.power_ref, f32[1,256]{1,0:T(1,128)S(1)} %collective-permute-done.12.power_got_ref, f32[128,512]{1,0:T(8,128)S(1)} %get-tuple-element.56.refs_0_, f32[128,512]{1,0:T(8,128)S(1)} %get-tuple-element.57.refs_1_, ...), custom_call_target="tpu_custom_call" | custom-call | flops 1048576 | bytes 1310720 | tf_op jit(solution)/shard_map/pallas_call | solution.py:531
  (7 shorter events, 0.0 us)
Async XLA Ops:
  0.0 7.6 %copy-start.1 = (s32[32]{0:T(128)S(1)}, s32[32]{0:T(128)}, u32[]{:S(2)}) copy-start(s32[32]{0:T(128)} %seq_ref.1) | copy-start | bytes 388
  0.0 7.6 %copy-start = (f32[3,3,2048]{2,1,0:T(4,128)S(1)}, f32[3,3,2048]{2,1,0:T(4,128)}, u32[]{:S(2)}) copy-start(f32[3,3,2048]{2,1,0:T(4,128)} %w_ref.1) | copy-start | bytes 221188
  0.0 7.5 %copy-start.4 = (f32[16,512]{1,0:T(8,128)S(1)}, f32[16,512]{1,0:T(8,128)}, u32[]{:S(2)}) copy-start(f32[16,512]{1,0:T(8,128)} %param.9) | copy-start | bytes 98308
  0.0 7.4 %copy-start.5 = (s32[16,4]{0,1:T(4,128)S(1)}, s32[16,4]{0,1:T(4,128)}, u32[]{:S(2)}) copy-start(s32[16,4]{0,1:T(4,128)} %param.10) | copy-start | bytes 772
  2.3 8.2 %collective-permute-start = (bf16[136,512]{1,0:T(8,128)(2,1)S(1)}, bf16[136,512]{1,0:T(8,128)(2,1)S(1)}, u32[]{:S(2)}, u32[]{:S(2)}) collective-permute-start(bf16[136,512]{1,0:T(8,128)(2,1)S(1)} %get-tuple-element.36), channel_id=1, source_target_pairs={{0,4},{4,0},{8,12},{12,8},{16,20},{20,16},{24,28},{28,24},{1,5},{5... | collective-permute-start | bytes 417800 | tf_op jit(solution)/shard_map/ppermute | solution.py:20
  5.3 12.4 %collective-permute-start.1 = (bf16[136,1024]{1,0:T(8,128)(2,1)S(1)}, bf16[136,1024]{1,0:T(8,128)(2,1)S(1)}, u32[]{:S(2)}, u32[]{:S(2)}) collective-permute-start(bf16[136,1024]{1,0:T(8,128)(2,1)S(1)} %get-tuple-element.32.own_ref), channel_id=1, source_target_pairs={{0,8},{4,12},{8,16},{12,20},{16,24},{20,28},{24,0},{28,4},{1,9},{5... | collective-permute-start | bytes 835592 | tf_op jit(solution)/shard_map/ppermute | solution.py:20
  6.9 6.3 %collective-permute-start.2 = (bf16[136,512]{1,0:T(8,128)(2,1)S(1)}, bf16[136,512]{1,0:T(8,128)(2,1)S(1)}, u32[]{:S(2)}, u32[]{:S(2)}) collective-permute-start(bf16[136,512]{1,0:T(8,128)(2,1)S(1)} %get-tuple-element.41), channel_id=1, source_target_pairs={{0,4},{4,0},{8,12},{12,8},{16,20},{20,16},{24,28},{28,24},{1,5},{5... | collective-permute-start | bytes 417800 | tf_op jit(solution)/shard_map/ppermute | solution.py:20
  10.5 11.5 %copy-start.2 = (f32[2048]{0:T(1024)S(1)}, f32[2048]{0:T(1024)}, u32[]{:S(2)}) copy-start(f32[2048]{0:T(1024)} %param.11) | copy-start | bytes 24580
  10.5 9.1 %collective-permute-start.3 = (bf16[136,512]{1,0:T(8,128)(2,1)S(1)}, bf16[136,512]{1,0:T(8,128)(2,1)S(1)}, u32[]{:S(2)}, u32[]{:S(2)}) collective-permute-start(bf16[136,512]{1,0:T(8,128)(2,1)S(1)} %collective-permute-done.pair_a_ref), channel_id=1, source_target_pairs={{0,8},{4,12},{8,16},{12,20},{16,24},{20,28},{24,0},{28,4},{1,9},{5... | collective-permute-start | bytes 417800 | tf_op jit(solution)/shard_map/ppermute | solution.py:20
  13.2 6.6 %collective-permute-start.4 = (bf16[136,512]{1,0:T(8,128)(2,1)S(1)}, bf16[136,512]{1,0:T(8,128)(2,1)S(1)}, u32[]{:S(2)}, u32[]{:S(2)}) collective-permute-start(bf16[136,512]{1,0:T(8,128)(2,1)S(1)} %collective-permute-done.2.pair_b_ref), channel_id=1, source_target_pairs={{0,4},{4,0},{8,16},{12,20},{16,8},{20,12},{24,28},{28,24},{1,5},{5... | collective-permute-start | bytes 417800 | tf_op jit(solution)/shard_map/ppermute | solution.py:20
  14.8 6.5 %collective-permute-start.5 = (bf16[136,512]{1,0:T(8,128)(2,1)S(1)}, bf16[136,512]{1,0:T(8,128)(2,1)S(1)}, u32[]{:S(2)}, u32[]{:S(2)}) collective-permute-start(bf16[136,512]{1,0:T(8,128)(2,1)S(1)} %collective-permute-done.2.pair_b_ref), channel_id=1, source_target_pairs={{0,8},{4,12},{8,0},{12,4},{16,24},{20,28},{24,16},{28,20},{1,9},{5... | collective-permute-start | bytes 417800 | tf_op jit(solution)/shard_map/ppermute | solution.py:20
  16.2 9.2 %collective-permute-start.6 = (bf16[128,1024]{1,0:T(8,128)(2,1)S(1)}, bf16[128,1024]{1,0:T(8,128)(2,1)S(1)}, u32[]{:S(2)}, u32[]{:S(2)}) collective-permute-start(bf16[128,1024]{1,0:T(8,128)(2,1)S(1)} %get-tuple-element.50), channel_id=1, source_target_pairs={{0,4},{4,0},{8,12},{12,8},{16,20},{20,16},{24,28},{28,24},{1,5},{5... | collective-permute-start | bytes 786440 | tf_op jit(solution)/shard_map/ppermute | solution.py:20
  19.7 8.0 %collective-permute-start.8 = (bf16[136,512]{1,0:T(8,128)(2,1)S(1)}, bf16[136,512]{1,0:T(8,128)(2,1)S(1)}, u32[]{:S(2)}, u32[]{:S(2)}) collective-permute-start(bf16[136,512]{1,0:T(8,128)(2,1)S(1)} %get-tuple-element.52), channel_id=1, source_target_pairs={{0,4},{4,0},{8,16},{12,20},{16,24},{20,28},{24,8},{28,12},{1,5},{5... | collective-permute-start | bytes 417800 | tf_op jit(solution)/shard_map/ppermute | solution.py:20
  21.4 7.8 %collective-permute-start.7 = (bf16[136,512]{1,0:T(8,128)(2,1)S(1)}, bf16[136,512]{1,0:T(8,128)(2,1)S(1)}, u32[]{:S(2)}, u32[]{:S(2)}) collective-permute-start(bf16[136,512]{1,0:T(8,128)(2,1)S(1)} %get-tuple-element.51), channel_id=1, source_target_pairs={{0,4},{4,0},{8,16},{12,20},{16,24},{20,28},{24,8},{28,12},{1,5},{5... | collective-permute-start | bytes 417800 | tf_op jit(solution)/shard_map/ppermute | solution.py:20
  29.2 9.6 %copy-start.3 = (f32[2048]{0:T(1024)S(1)}, f32[2048]{0:T(1024)}, u32[]{:S(2)}) copy-start(f32[2048]{0:T(1024)} %param.12) | copy-start | bytes 24580
  29.9 9.0 %collective-permute-start.13 = (bf16[128,1024]{1,0:T(8,128)(2,1)S(1)}, bf16[128,1024]{1,0:T(8,128)(2,1)S(1)}, u32[]{:S(2)}, u32[]{:S(2)}) collective-permute-start(bf16[128,1024]{1,0:T(8,128)(2,1)S(1)} %get-tuple-element.58), channel_id=1, source_target_pairs={{0,4},{4,0},{8,12},{12,8},{16,20},{20,16},{24,28},{28,24},{1,5},{5... | collective-permute-start | bytes 786440 | tf_op jit(solution)/shard_map/ppermute | solution.py:20
  31.6 3.0 %collective-permute-start.11 = (f32[1,256]{1,0:T(1,128)S(1)}, f32[1,256]{1,0:T(1,128)S(1)}, u32[]{:S(2)}, u32[]{:S(2)}) collective-permute-start(f32[1,256]{1,0:T(1,128)S(1)} %get-tuple-element.55), channel_id=1, source_target_pairs={{0,3},{1,2},{2,1},{3,0},{4,7},{5,6},{6,5},{7,4},{8,11},{9,10},{10,... | collective-permute-start | bytes 3080 | tf_op jit(solution)/shard_map/ppermute | solution.py:529
  31.6 3.6 %collective-permute-start.10 = (f32[1,256]{1,0:T(1,128)S(1)}, f32[1,256]{1,0:T(1,128)S(1)}, u32[]{:S(2)}, u32[]{:S(2)}) collective-permute-start(f32[1,256]{1,0:T(1,128)S(1)} %get-tuple-element.55), channel_id=1, source_target_pairs={{0,2},{1,3},{2,0},{3,1},{4,6},{5,7},{6,4},{7,5},{8,10},{9,11},{10,... | collective-permute-start | bytes 3080 | tf_op jit(solution)/shard_map/ppermute | solution.py:529
  33.2 2.1 %collective-permute-start.9 = (f32[1,256]{1,0:T(1,128)S(1)}, f32[1,256]{1,0:T(1,128)S(1)}, u32[]{:S(2)}, u32[]{:S(2)}) collective-permute-start(f32[1,256]{1,0:T(1,128)S(1)} %get-tuple-element.55), channel_id=1, source_target_pairs={{0,1},{1,0},{2,3},{3,2},{4,5},{5,4},{6,7},{7,6},{8,9},{9,8},{10,11... | collective-permute-start | bytes 3080 | tf_op jit(solution)/shard_map/ppermute | solution.py:529
  35.2 3.6 %collective-permute-start.12 = (f32[1,256]{1,0:T(1,128)S(1)}, f32[1,256]{1,0:T(1,128)S(1)}, u32[]{:S(2)}, u32[]{:S(2)}) collective-permute-start(f32[1,256]{1,0:T(1,128)S(1)} %add_add_fusion.power_ref), channel_id=1, source_target_pairs={{0,4},{4,0},{8,12},{12,8},{16,20},{20,16},{24,28},{28,24},{1,5},{5... | collective-permute-start | bytes 3080 | tf_op jit(solution)/shard_map/ppermute | solution.py:20

commit v21 on v20

--- a/solution.py
+++ b/solution.py
@@ -17,7 +17,9 @@
 
 
 def moved(block, pairs):
-    return lax.ppermute(block, SPOTS, pairs)
+    peers = lax.axis_size("mp")
+    whole = [(i * peers + m, j * peers + (m if i != j else m ^ 1)) for i, j in pairs for m in range(peers)]
+    return lax.ppermute(block, SPOTS + ("mp",), whole)
 
 
 def boundaries(seq_ref, t):
@@ -391,7 +393,7 @@
     for i in range(2 * blocks):
         block = i // 2
         partner = block + 1 if (block - first) % 2 == 0 else block - 1
-        pairs.append((i, 2 * partner + i % 2 if 0 <= partner < blocks else i ^ 1))
+        pairs.append((i, 2 * partner + i % 2 if 0 <= partner < blocks else i))
     return pairs
 
 
@@ -468,7 +470,7 @@
     shifted = pltpu.VMEM((2, rows + 8, GROUP), jnp.float32)
     short = whole_tokens // 2 <= 4 * BLK
     if short:
-        onward = [(i, i ^ 1 if i < 2 else i + 2 if i + 2 < 2 * blocks else 2 + i % 2) for i in spots]
+        onward = [(i, i if i < 2 else i + 2 if i + 2 < 2 * blocks else 2 + i % 2) for i in spots]
         far = []
         for piece in range(2):
             relayed, back_pair[piece] = kernel_call(

time: 40.1 us -> 36.1 us (0.900)
  the two profiles are of different devices: /device:TPU:0 before, /device:TPU:10 now
where the time goes in v21:
time: 36.1 us; the launch traced here: 36 us
  starting transfers between devices  15 us (42%)
  waiting for transfers between devices  10.6 us (29%)
  Pallas kernels  8.88 us (25%)
  local copies, waits for them, and re-layouts  1.25 us (3%)
    ppermute x11, starting transfers between devices, moved(): return lax.ppermute(block, SPOTS + ('mp',), whole)  13.2 us
    ppermute x11, waiting for transfers between devices, moved(): return lax.ppermute(block, SPOTS + ('mp',), whole)  8.86 us
    pallas_call x1, Pallas kernels, shards(): kernel_call(tables_kernel, (shape((groups, 2, BLK, span), jnp.bfloat16),...  2.85 us
    pallas_call x1, Pallas kernels, shards(): kernel_call(products_kernel, (message, small, small), [hbm] * 3, [pltpu.V...  2.24 us
    ppermute x3, starting transfers between devices, shards(): lax.ppermute(power, 'mp', [(i, i ^ k) for i in range(peers)])  1.86 us
    ppermute x3, waiting for transfers between devices, shards(): lax.ppermute(power, 'mp', [(i, i ^ k) for i in range(peers)])  1.74 us
    pallas_call x2, Pallas kernels, shards(): kernel_call(functools.partial(far_kernel, short, piece), (shape((rows, wi...  1.1 us
    squeeze x1, local copies, waits for them, and re-layouts, shards(): lax.dynamic_slice(query, (0, 0, (1 - half) * width), (1, rows, width))[0]  1.06 us
  transfers between devices with their start and end apart: 14, of which 6 were waited for; matrix products, arithmetic and copies ran while one was open for 3% of the time, Pallas kernels for 14%

profile of v21, /device:TPU:10, one launch (start us, length us, event | category | flops | bytes accessed | tf_op | source)
XLA Modules:
  0.0 36.0 jit_solution(2661461477695862574)
XLA Ops:
  0.0 0.0 copy-start.5
  0.0 2.2 %shard_map.73 = (bf16[136,1024]{1,0:T(8,128)(2,1)S(1)}, bf16[136,512]{1,0:T(8,128)(2,1)S(1)}, bf16[136,512]{1,0:T(8,128)(2,1)S(1)}) custom-call(s32[1,32]{1,0:T(1,128)} %bitcast.13, bf16[3,128,2048]{2,1,0:T(8,128)(2,1)} %bitcast.18, f32[3,3,2048]{2,1,0:T(4,128)} %w_ref.1), custom_call_target="tpu_custom_call" | custom-call | flops 5242880 | bytes 2097152 | tf_op jit(solution)/shard_map/pallas_call | solution.py:421
  2.3 1.6 %collective-permute-start = (bf16[136,512]{1,0:T(8,128)(2,1)S(1)}, bf16[136,512]{1,0:T(8,128)(2,1)S(1)}, u32[]{:S(2)}, u32[]{:S(2)}) collective-permute-start(bf16[136,512]{1,0:T(8,128)(2,1)S(1)} %get-tuple-element.36), channel_id=1, source_target_pairs={{0,4},{1,5},{2,6},{3,7},{4,0},{5,1},{6,2},{7,3},{8,12},{9,13},{10,... | collective-permute-start | bytes 417800 | tf_op jit(solution)/shard_map/ppermute | solution.py:22
  3.8 1.6 %collective-permute-start.1 = (bf16[136,1024]{1,0:T(8,128)(2,1)S(1)}, bf16[136,1024]{1,0:T(8,128)(2,1)S(1)}, u32[]{:S(2)}, u32[]{:S(2)}) collective-permute-start(bf16[136,1024]{1,0:T(8,128)(2,1)S(1)} %get-tuple-element.32.own_ref), channel_id=1, source_target_pairs={{0,8},{1,9},{2,10},{3,11},{4,12},{5,13},{6,14},{7,15},{8,16},{9,17... | collective-permute-start | bytes 835592 | tf_op jit(solution)/shard_map/ppermute | solution.py:22
  5.4 0.5 %collective-permute-start.2 = (bf16[136,512]{1,0:T(8,128)(2,1)S(1)}, bf16[136,512]{1,0:T(8,128)(2,1)S(1)}, u32[]{:S(2)}, u32[]{:S(2)}) collective-permute-start(bf16[136,512]{1,0:T(8,128)(2,1)S(1)} %get-tuple-element.41), channel_id=1, source_target_pairs={{0,4},{1,5},{2,6},{3,7},{4,0},{5,1},{6,2},{7,3},{8,12},{9,13},{10,... | collective-permute-start | bytes 417800 | tf_op jit(solution)/shard_map/ppermute | solution.py:22
  5.9 0.0 copy-done.5
  5.9 0.1 copy.8
  6.0 0.1 broadcast_in_dim.3
  6.1 0.0 copy-done.4
  6.1 0.0 copy-done.1
  6.1 0.0 copy-done
  6.2 2.9 %shard_map.74 = (bf16[8,2,128,768]{3,2,1,0:T(8,128)(2,1)S(1)}, bf16[8,128,256]{2,1,0:T(8,128)(2,1)S(1)}, f32[3,3,1024]{2,1,0:T(4,128)S(1)}, f32[4,8,128]{2,1,0:T(8,128)S(1)}) custom-call(s32[32]{0:T(128)S(1)} %copy-done.1, bf16[16,512]{1,0:T(8,128)(2,1)S(1)} %fusion.taps_ref, f32[3,3,2048]{2,1,0:T(4,128)S(1)} %copy-done), custom_call_target="tpu_custom_call" | custom-call | flops 20971520 | bytes 4194304 | tf_op jit(solution)/shard_map/pallas_call | solution.py:445
  9.0 0.0 collective-permute-done.pair_a_ref
  9.0 0.0 copy-start.2
  9.0 1.6 %collective-permute-start.3 = (bf16[136,512]{1,0:T(8,128)(2,1)S(1)}, bf16[136,512]{1,0:T(8,128)(2,1)S(1)}, u32[]{:S(2)}, u32[]{:S(2)}) collective-permute-start(bf16[136,512]{1,0:T(8,128)(2,1)S(1)} %collective-permute-done.pair_a_ref), channel_id=1, source_target_pairs={{0,8},{1,9},{2,10},{3,11},{4,12},{5,13},{6,14},{7,15},{8,16},{9,17... | collective-permute-start | bytes 417800 | tf_op jit(solution)/shard_map/ppermute | solution.py:22
  10.7 1.1 %dynamic-slice_bitcast_fusion = (bf16[128,1024]{1,0:T(8,128)(2,1)S(1)}, bf16[128,1024]{1,0:T(8,128)(2,1)S(1)}) fusion(bf16[3,128,2048]{2,1,0:T(8,128)(2,1)} %bitcast.19, s32[]{:T(128)S(6)} %select_n.7, s32[]{:T(128)S(6)} %select_n.6), kind=kLoop, calls=%fused_computation | loop fusion | bytes 1048584 | tf_op jit(solution)/shard_map/squeeze | solution.py:463
  11.7 0.0 collective-permute-done.2.pair_b_ref
  11.7 1.4 %collective-permute-start.4 = (bf16[136,512]{1,0:T(8,128)(2,1)S(1)}, bf16[136,512]{1,0:T(8,128)(2,1)S(1)}, u32[]{:S(2)}, u32[]{:S(2)}) collective-permute-start(bf16[136,512]{1,0:T(8,128)(2,1)S(1)} %collective-permute-done.2.pair_b_ref), channel_id=1, source_target_pairs={{0,1},{1,0},{2,3},{3,2},{4,5},{5,4},{6,7},{7,6},{8,16},{9,17},{10,... | collective-permute-start | bytes 417800 | tf_op jit(solution)/shard_map/ppermute | solution.py:22
  13.2 0.0 collective-permute-start.5
  13.2 1.5 %collective-permute-start.6 = (bf16[128,1024]{1,0:T(8,128)(2,1)S(1)}, bf16[128,1024]{1,0:T(8,128)(2,1)S(1)}, u32[]{:S(2)}, u32[]{:S(2)}) collective-permute-start(bf16[128,1024]{1,0:T(8,128)(2,1)S(1)} %get-tuple-element.50), channel_id=1, source_target_pairs={{0,4},{1,5},{2,6},{3,7},{4,0},{5,1},{6,2},{7,3},{8,12},{9,13},{10,... | collective-permute-start | bytes 786440 | tf_op jit(solution)/shard_map/ppermute | solution.py:22
  14.7 0.0 collective-permute-done.1.back_own_ref
  14.7 1.5 %collective-permute-done.3.refs_0_ = bf16[136,512]{1,0:T(8,128)(2,1)S(1)} collective-permute-done((bf16[136,512]{1,0:T(8,128)(2,1)S(1)}, bf16[136,512]{1,0:T(8,128)(2,1)S(1)}, u32[]{:S(2)}, u32[]{:S(2)}) %collective-permute-start.3) | collective-permute-done | bytes 139296 | tf_op jit(solution)/shard_map/ppermute | solution.py:22
  16.2 0.1 shard_map.75
  16.3 1.8 %collective-permute-start.8 = (bf16[136,512]{1,0:T(8,128)(2,1)S(1)}, bf16[136,512]{1,0:T(8,128)(2,1)S(1)}, u32[]{:S(2)}, u32[]{:S(2)}) collective-permute-start(bf16[136,512]{1,0:T(8,128)(2,1)S(1)} %get-tuple-element.52), channel_id=1, source_target_pairs={{0,1},{1,0},{2,3},{3,2},{4,5},{5,4},{6,7},{7,6},{8,16},{9,17},{10,... | collective-permute-start | bytes 417800 | tf_op jit(solution)/shard_map/ppermute | solution.py:22
  18.2 1.7 %collective-permute-done.4.refs_0_ = bf16[136,512]{1,0:T(8,128)(2,1)S(1)} collective-permute-done((bf16[136,512]{1,0:T(8,128)(2,1)S(1)}, bf16[136,512]{1,0:T(8,128)(2,1)S(1)}, u32[]{:S(2)}, u32[]{:S(2)}) %collective-permute-start.4) | collective-permute-done | bytes 139296 | tf_op jit(solution)/shard_map/ppermute | solution.py:22
  19.8 0.0 collective-permute-done.5.refs_1_
  19.8 0.2 shard_map.76
  20.0 1.0 %collective-permute-start.7 = (bf16[136,512]{1,0:T(8,128)(2,1)S(1)}, bf16[136,512]{1,0:T(8,128)(2,1)S(1)}, u32[]{:S(2)}, u32[]{:S(2)}) collective-permute-start(bf16[136,512]{1,0:T(8,128)(2,1)S(1)} %get-tuple-element.51), channel_id=1, source_target_pairs={{0,1},{1,0},{2,3},{3,2},{4,5},{5,4},{6,7},{7,6},{8,16},{9,17},{10,... | collective-permute-start | bytes 417800 | tf_op jit(solution)/shard_map/ppermute | solution.py:22
  21.0 0.0 copy-done.2
  21.0 1.0 %shard_map.77 = (f32[256,1024]{1,0:T(8,128)S(1)}, f32[128,1024]{1,0:T(8,128)S(1)}) custom-call(s32[1,32]{1,0:T(1,128)S(1)} %bitcast.14, f32[4,8,128]{2,1,0:T(8,128)S(1)} %get-tuple-element.38.marks_ref, bf16[8,2,128,768]{3,2,1,0:T(8,128)(2,1)S(1)} %get-tuple-element.37.table_ref, bf16[136,1024]{1,0:T(8,128)(2,1)S(1)} %get-tuple-element.32.own_ref, ...), custom_call_target="tpu_custom_call" | custom-call | flops 167772160 | bytes 2097152 | tf_op jit(solution)/shard_map/pallas_call | solution.py:493
  22.0 0.0 collective-permute-done.6.raw_ref
  22.0 0.4 %shard_map.78.qpair_ref = f32[128,1024]{1,0:T(8,128)S(1)} custom-call(s32[1,32]{1,0:T(1,128)S(1)} %bitcast.15, bf16[128,1024]{1,0:T(8,128)(2,1)S(1)} %collective-permute-done.6.raw_ref, bf16[136,1024]{1,0:T(8,128)(2,1)S(1)} %get-tuple-element.32.own_ref, bf16[136,1024]{1,0:T(8,128)(2,1)S(1)} %collective-permute-done.1.back_own_ref, ...), custom_call_target="tpu_custom_call" | custom-call | flops 1310720 | bytes 1048576 | tf_op jit(solution)/shard_map/pallas_call | solution.py:502
  22.3 0.0 collective-permute-done.8.refs_0_
  22.4 0.4 %shard_map.79 = (f32[128,512]{1,0:T(8,128)S(1)}, bf16[128,512]{1,0:T(8,128)(2,1)S(1)}, f32[2,128,128]{2,1,0:T(8,128)S(1)}) custom-call(bf16[8,2,128,768]{3,2,1,0:T(8,128)(2,1)S(1)} %get-tuple-element.37.table_ref, f32[256,1024]{1,0:T(8,128)S(1)} %get-tuple-element.48.acc_ref, f32[128,1024]{1,0:T(8,128)S(1)} %get-tuple-element.49.qown_ref, ...), custom_call_target="tpu_custom_call" | custom-call | flops 100663296 | bytes 1572864 | tf_op jit(solution)/shard_map/pallas_call | solution.py:515
  22.8 3.2 %collective-permute-done.7.refs_0_ = bf16[136,512]{1,0:T(8,128)(2,1)S(1)} collective-permute-done((bf16[136,512]{1,0:T(8,128)(2,1)S(1)}, bf16[136,512]{1,0:T(8,128)(2,1)S(1)}, u32[]{:S(2)}, u32[]{:S(2)}) %collective-permute-start.7) | collective-permute-done | bytes 139296 | tf_op jit(solution)/shard_map/ppermute | solution.py:22
  26.0 0.7 %shard_map.80 = (f32[128,512]{1,0:T(8,128)S(1)}, bf16[128,1024]{1,0:T(8,128)(2,1)S(1)}, f32[1,256]{1,0:T(1,128)S(1)}) custom-call(bf16[8,2,128,768]{3,2,1,0:T(8,128)(2,1)S(1)} %get-tuple-element.37.table_ref, f32[256,1024]{1,0:T(8,128)S(1)} %get-tuple-element.48.acc_ref, f32[128,1024]{1,0:T(8,128)S(1)} %get-tuple-element.49.qown_ref, ...), custom_call_target="tpu_custom_call" | custom-call | flops 100663296 | bytes 1572864 | tf_op jit(solution)/shard_map/pallas_call | solution.py:515
  26.7 1.0 %collective-permute-start.13 = (bf16[128,1024]{1,0:T(8,128)(2,1)S(1)}, bf16[128,1024]{1,0:T(8,128)(2,1)S(1)}, u32[]{:S(2)}, u32[]{:S(2)}) collective-permute-start(bf16[128,1024]{1,0:T(8,128)(2,1)S(1)} %get-tuple-element.58), channel_id=1, source_target_pairs={{0,4},{1,5},{2,6},{3,7},{4,0},{5,1},{6,2},{7,3},{8,12},{9,13},{10,... | collective-permute-start | bytes 786440 | tf_op jit(solution)/shard_map/ppermute | solution.py:22
  27.7 0.0 collective-permute-start.11
  27.7 0.6 %collective-permute-start.10 = (f32[1,256]{1,0:T(1,128)S(1)}, f32[1,256]{1,0:T(1,128)S(1)}, u32[]{:S(2)}, u32[]{:S(2)}) collective-permute-start(f32[1,256]{1,0:T(1,128)S(1)} %get-tuple-element.55), channel_id=1, source_target_pairs={{0,2},{1,3},{2,0},{3,1},{4,6},{5,7},{6,4},{7,5},{8,10},{9,11},{10,... | collective-permute-start | bytes 3080 | tf_op jit(solution)/shard_map/ppermute | solution.py:531
  28.2 1.3 %collective-permute-start.9 = (f32[1,256]{1,0:T(1,128)S(1)}, f32[1,256]{1,0:T(1,128)S(1)}, u32[]{:S(2)}, u32[]{:S(2)}) collective-permute-start(f32[1,256]{1,0:T(1,128)S(1)} %get-tuple-element.55), channel_id=1, source_target_pairs={{0,1},{1,0},{2,3},{3,2},{4,5},{5,4},{6,7},{7,6},{8,9},{9,8},{10,11... | collective-permute-start | bytes 3080 | tf_op jit(solution)/shard_map/ppermute | solution.py:531
  29.5 1.1 %collective-permute-done.11 = f32[1,256]{1,0:T(1,128)S(1)} collective-permute-done((f32[1,256]{1,0:T(1,128)S(1)}, f32[1,256]{1,0:T(1,128)S(1)}, u32[]{:S(2)}, u32[]{:S(2)}) %collective-permute-start.11) | collective-permute-done | bytes 1056 | tf_op jit(solution)/shard_map/ppermute | solution.py:531
  30.7 0.6 %collective-permute-done.10 = f32[1,256]{1,0:T(1,128)S(1)} collective-permute-done((f32[1,256]{1,0:T(1,128)S(1)}, f32[1,256]{1,0:T(1,128)S(1)}, u32[]{:S(2)}, u32[]{:S(2)}) %collective-permute-start.10) | collective-permute-done | bytes 1056 | tf_op jit(solution)/shard_map/ppermute | solution.py:531
  31.3 0.0 collective-permute-done.9
  31.3 1.1 %collective-permute-start.12 = (f32[1,256]{1,0:T(1,128)S(1)}, f32[1,256]{1,0:T(1,128)S(1)}, u32[]{:S(2)}, u32[]{:S(2)}) collective-permute-start(f32[1,256]{1,0:T(1,128)S(1)} %add_add_fusion.power_ref), channel_id=1, source_target_pairs={{0,4},{1,5},{2,6},{3,7},{4,0},{5,1},{6,2},{7,3},{8,12},{9,13},{10,... | collective-permute-start | bytes 3080 | tf_op jit(solution)/shard_map/ppermute | solution.py:22
  32.4 2.5 %collective-permute-done.12.power_got_ref = f32[1,256]{1,0:T(1,128)S(1)} collective-permute-done((f32[1,256]{1,0:T(1,128)S(1)}, f32[1,256]{1,0:T(1,128)S(1)}, u32[]{:S(2)}, u32[]{:S(2)}) %collective-permute-start.12) | collective-permute-done | bytes 1056 | tf_op jit(solution)/shard_map/ppermute | solution.py:22
  34.9 0.0 collective-permute-done.13.refs_2_
  34.9 0.0 copy-done.3
  34.9 1.0 %shard_map.81 = bf16[128,2048]{1,0:T(8,128)(2,1)} custom-call(f32[1,256]{1,0:T(1,128)S(1)} %add_add_fusion.power_ref, f32[1,256]{1,0:T(1,128)S(1)} %collective-permute-done.12.power_got_ref, f32[128,512]{1,0:T(8,128)S(1)} %get-tuple-element.56.refs_0_, f32[128,512]{1,0:T(8,128)S(1)} %get-tuple-element.57.refs_1_, ...), custom_call_target="tpu_custom_call" | custom-call | flops 1048576 | bytes 1310720 | tf_op jit(solution)/shard_map/pallas_call | solution.py:533
  (7 shorter events, 0.0 us)
Async XLA Ops:
  0.0 6.1 %copy-start.1 = (s32[32]{0:T(128)S(1)}, s32[32]{0:T(128)}, u32[]{:S(2)}) copy-start(s32[32]{0:T(128)} %seq_ref.1) | copy-start | bytes 388
  0.0 6.1 %copy-start = (f32[3,3,2048]{2,1,0:T(4,128)S(1)}, f32[3,3,2048]{2,1,0:T(4,128)}, u32[]{:S(2)}) copy-start(f32[3,3,2048]{2,1,0:T(4,128)} %w_ref.1) | copy-start | bytes 221188
  0.0 6.1 %copy-start.4 = (f32[16,512]{1,0:T(8,128)S(1)}, f32[16,512]{1,0:T(8,128)}, u32[]{:S(2)}) copy-start(f32[16,512]{1,0:T(8,128)} %param.9) | copy-start | bytes 98308
  0.0 5.9 %copy-start.5 = (s32[16,4]{0,1:T(4,128)S(1)}, s32[16,4]{0,1:T(4,128)}, u32[]{:S(2)}) copy-start(s32[16,4]{0,1:T(4,128)} %param.10) | copy-start | bytes 772
  2.3 6.8 %collective-permute-start = (bf16[136,512]{1,0:T(8,128)(2,1)S(1)}, bf16[136,512]{1,0:T(8,128)(2,1)S(1)}, u32[]{:S(2)}, u32[]{:S(2)}) collective-permute-start(bf16[136,512]{1,0:T(8,128)(2,1)S(1)} %get-tuple-element.36), channel_id=1, source_target_pairs={{0,4},{1,5},{2,6},{3,7},{4,0},{5,1},{6,2},{7,3},{8,12},{9,13},{10,... | collective-permute-start | bytes 417800 | tf_op jit(solution)/shard_map/ppermute | solution.py:22
  3.8 10.9 %collective-permute-start.1 = (bf16[136,1024]{1,0:T(8,128)(2,1)S(1)}, bf16[136,1024]{1,0:T(8,128)(2,1)S(1)}, u32[]{:S(2)}, u32[]{:S(2)}) collective-permute-start(bf16[136,1024]{1,0:T(8,128)(2,1)S(1)} %get-tuple-element.32.own_ref), channel_id=1, source_target_pairs={{0,8},{1,9},{2,10},{3,11},{4,12},{5,13},{6,14},{7,15},{8,16},{9,17... | collective-permute-start | bytes 835592 | tf_op jit(solution)/shard_map/ppermute | solution.py:22
  5.4 6.3 %collective-permute-start.2 = (bf16[136,512]{1,0:T(8,128)(2,1)S(1)}, bf16[136,512]{1,0:T(8,128)(2,1)S(1)}, u32[]{:S(2)}, u32[]{:S(2)}) collective-permute-start(bf16[136,512]{1,0:T(8,128)(2,1)S(1)} %get-tuple-element.41), channel_id=1, source_target_pairs={{0,4},{1,5},{2,6},{3,7},{4,0},{5,1},{6,2},{7,3},{8,12},{9,13},{10,... | collective-permute-start | bytes 417800 | tf_op jit(solution)/shard_map/ppermute | solution.py:22
  9.0 11.9 %copy-start.2 = (f32[2048]{0:T(1024)S(1)}, f32[2048]{0:T(1024)}, u32[]{:S(2)}) copy-start(f32[2048]{0:T(1024)} %param.11) | copy-start | bytes 24580
  9.0 7.1 %collective-permute-start.3 = (bf16[136,512]{1,0:T(8,128)(2,1)S(1)}, bf16[136,512]{1,0:T(8,128)(2,1)S(1)}, u32[]{:S(2)}, u32[]{:S(2)}) collective-permute-start(bf16[136,512]{1,0:T(8,128)(2,1)S(1)} %collective-permute-done.pair_a_ref), channel_id=1, source_target_pairs={{0,8},{1,9},{2,10},{3,11},{4,12},{5,13},{6,14},{7,15},{8,16},{9,17... | collective-permute-start | bytes 417800 | tf_op jit(solution)/shard_map/ppermute | solution.py:22
  11.7 8.1 %collective-permute-start.4 = (bf16[136,512]{1,0:T(8,128)(2,1)S(1)}, bf16[136,512]{1,0:T(8,128)(2,1)S(1)}, u32[]{:S(2)}, u32[]{:S(2)}) collective-permute-start(bf16[136,512]{1,0:T(8,128)(2,1)S(1)} %collective-permute-done.2.pair_b_ref), channel_id=1, source_target_pairs={{0,1},{1,0},{2,3},{3,2},{4,5},{5,4},{6,7},{7,6},{8,16},{9,17},{10,... | collective-permute-start | bytes 417800 | tf_op jit(solution)/shard_map/ppermute | solution.py:22
  13.2 6.6 %collective-permute-start.5 = (bf16[136,512]{1,0:T(8,128)(2,1)S(1)}, bf16[136,512]{1,0:T(8,128)(2,1)S(1)}, u32[]{:S(2)}, u32[]{:S(2)}) collective-permute-start(bf16[136,512]{1,0:T(8,128)(2,1)S(1)} %collective-permute-done.2.pair_b_ref), channel_id=1, source_target_pairs={{0,8},{1,9},{2,10},{3,11},{4,12},{5,13},{6,14},{7,15},{8,0},{9,1},... | collective-permute-start | bytes 417800 | tf_op jit(solution)/shard_map/ppermute | solution.py:22
  13.2 8.8 %collective-permute-start.6 = (bf16[128,1024]{1,0:T(8,128)(2,1)S(1)}, bf16[128,1024]{1,0:T(8,128)(2,1)S(1)}, u32[]{:S(2)}, u32[]{:S(2)}) collective-permute-start(bf16[128,1024]{1,0:T(8,128)(2,1)S(1)} %get-tuple-element.50), channel_id=1, source_target_pairs={{0,4},{1,5},{2,6},{3,7},{4,0},{5,1},{6,2},{7,3},{8,12},{9,13},{10,... | collective-permute-start | bytes 786440 | tf_op jit(solution)/shard_map/ppermute | solution.py:22
  16.3 6.0 %collective-permute-start.8 = (bf16[136,512]{1,0:T(8,128)(2,1)S(1)}, bf16[136,512]{1,0:T(8,128)(2,1)S(1)}, u32[]{:S(2)}, u32[]{:S(2)}) collective-permute-start(bf16[136,512]{1,0:T(8,128)(2,1)S(1)} %get-tuple-element.52), channel_id=1, source_target_pairs={{0,1},{1,0},{2,3},{3,2},{4,5},{5,4},{6,7},{7,6},{8,16},{9,17},{10,... | collective-permute-start | bytes 417800 | tf_op jit(solution)/shard_map/ppermute | solution.py:22
  20.0 6.0 %collective-permute-start.7 = (bf16[136,512]{1,0:T(8,128)(2,1)S(1)}, bf16[136,512]{1,0:T(8,128)(2,1)S(1)}, u32[]{:S(2)}, u32[]{:S(2)}) collective-permute-start(bf16[136,512]{1,0:T(8,128)(2,1)S(1)} %get-tuple-element.51), channel_id=1, source_target_pairs={{0,1},{1,0},{2,3},{3,2},{4,5},{5,4},{6,7},{7,6},{8,16},{9,17},{10,... | collective-permute-start | bytes 417800 | tf_op jit(solution)/shard_map/ppermute | solution.py:22
  26.0 8.9 %copy-start.3 = (f32[2048]{0:T(1024)S(1)}, f32[2048]{0:T(1024)}, u32[]{:S(2)}) copy-start(f32[2048]{0:T(1024)} %param.12) | copy-start | bytes 24580
  26.7 8.2 %collective-permute-start.13 = (bf16[128,1024]{1,0:T(8,128)(2,1)S(1)}, bf16[128,1024]{1,0:T(8,128)(2,1)S(1)}, u32[]{:S(2)}, u32[]{:S(2)}) collective-permute-start(bf16[128,1024]{1,0:T(8,128)(2,1)S(1)} %get-tuple-element.58), channel_id=1, source_target_pairs={{0,4},{1,5},{2,6},{3,7},{4,0},{5,1},{6,2},{7,3},{8,12},{9,13},{10,... | collective-permute-start | bytes 786440 | tf_op jit(solution)/shard_map/ppermute | solution.py:22
  27.7 3.0 %collective-permute-start.11 = (f32[1,256]{1,0:T(1,128)S(1)}, f32[1,256]{1,0:T(1,128)S(1)}, u32[]{:S(2)}, u32[]{:S(2)}) collective-permute-start(f32[1,256]{1,0:T(1,128)S(1)} %get-tuple-element.55), channel_id=1, source_target_pairs={{0,3},{1,2},{2,1},{3,0},{4,7},{5,6},{6,5},{7,4},{8,11},{9,10},{10,... | collective-permute-start | bytes 3080 | tf_op jit(solution)/shard_map/ppermute | solution.py:531
  27.7 3.6 %collective-permute-start.10 = (f32[1,256]{1,0:T(1,128)S(1)}, f32[1,256]{1,0:T(1,128)S(1)}, u32[]{:S(2)}, u32[]{:S(2)}) collective-permute-start(f32[1,256]{1,0:T(1,128)S(1)} %get-tuple-element.55), channel_id=1, source_target_pairs={{0,2},{1,3},{2,0},{3,1},{4,6},{5,7},{6,4},{7,5},{8,10},{9,11},{10,... | collective-permute-start | bytes 3080 | tf_op jit(solution)/shard_map/ppermute | solution.py:531
  28.2 3.0 %collective-permute-start.9 = (f32[1,256]{1,0:T(1,128)S(1)}, f32[1,256]{1,0:T(1,128)S(1)}, u32[]{:S(2)}, u32[]{:S(2)}) collective-permute-start(f32[1,256]{1,0:T(1,128)S(1)} %get-tuple-element.55), channel_id=1, source_target_pairs={{0,1},{1,0},{2,3},{3,2},{4,5},{5,4},{6,7},{7,6},{8,9},{9,8},{10,11... | collective-permute-start | bytes 3080 | tf_op jit(solution)/shard_map/ppermute | solution.py:531
  31.3 3.6 %collective-permute-start.12 = (f32[1,256]{1,0:T(1,128)S(1)}, f32[1,256]{1,0:T(1,128)S(1)}, u32[]{:S(2)}, u32[]{:S(2)}) collective-permute-start(f32[1,256]{1,0:T(1,128)S(1)} %add_add_fusion.power_ref), channel_id=1, source_target_pairs={{0,4},{1,5},{2,6},{3,7},{4,0},{5,1},{6,2},{7,3},{8,12},{9,13},{10,... | collective-permute-start | bytes 3080 | tf_op jit(solution)/shard_map/ppermute | solution.py:22

commit v22 on v21

--- a/solution.py
+++ b/solution.py
@@ -315,8 +315,13 @@
 
     if short:
         summed = marks_ref[2, 0:1, 0:1]
-        fill(win_ref, extra_ref, 1, far_refs[0])
+        for i, way in enumerate(far_refs):
+            @pl.when((lax.axis_index("blk") + i) % len(far_refs) == 0)
+            def _():
+                fill(win_ref, extra_ref, 1, way)
+
         payload = win_ref[BLK : 2 * BLK, :].astype(jnp.float32)
+        win_ref[:BLK, :] = (payload * summed).astype(win_ref.dtype)
         win_ref[BLK : 2 * BLK, :] = (payload * (1.0 - summed)).astype(win_ref.dtype)
     else:
         fill(win_ref, extra_ref, half, far_refs[0].at[:, lanes])
@@ -340,8 +345,8 @@
                 preferred_element_type=jnp.float32,
             )
             if short:
-                weight = summed * (part == 0).astype(jnp.float32)
-                filtered = filtered + weight * far_refs[0][:BLK, here].astype(jnp.float32)
+                weight = (part == 0).astype(jnp.float32)
+                filtered = filtered + weight * win_ref[:BLK, here].astype(jnp.float32)
             gated = q_ref[:, whole] * filtered
             squares = squares + gated * gated
             out_ref[:, whole if before and part_sent else here] = gated.astype(out_ref.dtype)
@@ -471,6 +476,7 @@
     short = whole_tokens // 2 <= 4 * BLK
     if short:
         onward = [(i, i if i < 2 else i + 2 if i + 2 < 2 * blocks else 2 + i % 2) for i in spots]
+        linked = [[(i, j if min(i, j) >= 2 else i) for i, j in matching(blocks, first)] for first in (1, 0)]
         far = []
         for piece in range(2):
             relayed, back_pair[piece] = kernel_call(
@@ -481,7 +487,7 @@
                 2 * rows * BLK * width,
                 4 * rows * width,
             )(marks, table_next, back_own, w_half, *back_pair[piece])
-            far.append(moved(relayed, onward))
+            far.append([moved(relayed, way) for way in (linked if piece else [onward])])
     else:
         back_pair = [moved(piece, ahead) for piece in pair]
         across = jnp.concatenate([piece[rows:] for piece in sent], 1)
@@ -510,7 +516,7 @@
 
     done, power, send = [], None, None
     for piece in range(2):
-        needed = far[piece : piece + 1] if short else far
+        needed = far[piece] if short else far
         before = [power, send] if piece else []
         own, send, power = kernel_call(
             functools.partial(far_kernel, short, piece),

time: 36.1 us -> 37.5 us (1.039)
  the two profiles are of different devices: /device:TPU:10 before, /device:TPU:16 now
where the time goes in v22:
time: 37.5 us; the launch traced here: 37.4 us
  starting transfers between devices  14.3 us (38%)
  waiting for transfers between devices  12.7 us (34%)
  Pallas kernels  8.93 us (24%)
  local copies, waits for them, and re-layouts  1.25 us (3%)
    ppermute x12, starting transfers between devices, moved(): return lax.ppermute(block, SPOTS + ('mp',), whole)  12.4 us
    ppermute x12, waiting for transfers between devices, moved(): return lax.ppermute(block, SPOTS + ('mp',), whole)  10.1 us
    pallas_call x1, Pallas kernels, shards(): kernel_call(tables_kernel, (shape((groups, 2, BLK, span), jnp.bfloat16),...  2.85 us
    ppermute x3, waiting for transfers between devices, shards(): lax.ppermute(power, 'mp', [(i, i ^ k) for i in range(peers)])  2.63 us
    pallas_call x1, Pallas kernels, shards(): kernel_call(products_kernel, (message, small, small), [hbm] * 3, [pltpu.V...  2.24 us
    ppermute x3, starting transfers between devices, shards(): lax.ppermute(power, 'mp', [(i, i ^ k) for i in range(peers)])  1.86 us
    pallas_call x2, Pallas kernels, shards(): kernel_call(functools.partial(far_kernel, short, piece), (shape((rows, wi...  1.15 us
    squeeze x1, local copies, waits for them, and re-layouts, shards(): lax.dynamic_slice(query, (0, 0, (1 - half) * width), (1, rows, width))[0]  1.06 us
  transfers between devices with their start and end apart: 15, of which 7 were waited for; matrix products, arithmetic and copies ran while one was open for 3% of the time, Pallas kernels for 13%

profile of v22, /device:TPU:16, one launch (start us, length us, event | category | flops | bytes accessed | tf_op | source)
XLA Modules:
  0.0 37.4 jit_solution(919136002206091277)
XLA Ops:
  0.0 0.0 copy-start.5
  0.0 2.2 %shard_map.73 = (bf16[136,1024]{1,0:T(8,128)(2,1)S(1)}, bf16[136,512]{1,0:T(8,128)(2,1)S(1)}, bf16[136,512]{1,0:T(8,128)(2,1)S(1)}) custom-call(s32[1,32]{1,0:T(1,128)} %bitcast.13, bf16[3,128,2048]{2,1,0:T(8,128)(2,1)} %bitcast.18, f32[3,3,2048]{2,1,0:T(4,128)} %w_ref.1), custom_call_target="tpu_custom_call" | custom-call | flops 5242880 | bytes 2097152 | tf_op jit(solution)/shard_map/pallas_call | solution.py:426
  2.3 1.6 %collective-permute-start = (bf16[136,512]{1,0:T(8,128)(2,1)S(1)}, bf16[136,512]{1,0:T(8,128)(2,1)S(1)}, u32[]{:S(2)}, u32[]{:S(2)}) collective-permute-start(bf16[136,512]{1,0:T(8,128)(2,1)S(1)} %get-tuple-element.36), channel_id=1, source_target_pairs={{0,4},{1,5},{2,6},{3,7},{4,0},{5,1},{6,2},{7,3},{8,12},{9,13},{10,... | collective-permute-start | bytes 417800 | tf_op jit(solution)/shard_map/ppermute | solution.py:22
  3.8 0.5 %collective-permute-start.2 = (bf16[136,512]{1,0:T(8,128)(2,1)S(1)}, bf16[136,512]{1,0:T(8,128)(2,1)S(1)}, u32[]{:S(2)}, u32[]{:S(2)}) collective-permute-start(bf16[136,512]{1,0:T(8,128)(2,1)S(1)} %get-tuple-element.41), channel_id=1, source_target_pairs={{0,4},{1,5},{2,6},{3,7},{4,0},{5,1},{6,2},{7,3},{8,12},{9,13},{10,... | collective-permute-start | bytes 417800 | tf_op jit(solution)/shard_map/ppermute | solution.py:22
  4.4 1.6 %collective-permute-start.1 = (bf16[136,1024]{1,0:T(8,128)(2,1)S(1)}, bf16[136,1024]{1,0:T(8,128)(2,1)S(1)}, u32[]{:S(2)}, u32[]{:S(2)}) collective-permute-start(bf16[136,1024]{1,0:T(8,128)(2,1)S(1)} %get-tuple-element.32.own_ref), channel_id=1, source_target_pairs={{0,8},{1,9},{2,10},{3,11},{4,12},{5,13},{6,14},{7,15},{8,16},{9,17... | collective-permute-start | bytes 835592 | tf_op jit(solution)/shard_map/ppermute | solution.py:22
  5.9 0.0 copy-done.5
  5.9 0.1 copy.8
  6.0 0.1 broadcast_in_dim.3
  6.1 0.0 copy-done.4
  6.1 0.0 copy-done.1
  6.1 0.0 copy-done
  6.2 2.9 %shard_map.74 = (bf16[8,2,128,768]{3,2,1,0:T(8,128)(2,1)S(1)}, bf16[8,128,256]{2,1,0:T(8,128)(2,1)S(1)}, f32[3,3,1024]{2,1,0:T(4,128)S(1)}, f32[4,8,128]{2,1,0:T(8,128)S(1)}) custom-call(s32[32]{0:T(128)S(1)} %copy-done.1, bf16[16,512]{1,0:T(8,128)(2,1)S(1)} %fusion.taps_ref, f32[3,3,2048]{2,1,0:T(4,128)S(1)} %copy-done), custom_call_target="tpu_custom_call" | custom-call | flops 20971520 | bytes 4194304 | tf_op jit(solution)/shard_map/pallas_call | solution.py:450
  9.0 0.0 collective-permute-done.pair_a_ref
  9.0 0.0 copy-start.2
  9.0 1.4 %collective-permute-start.3 = (bf16[136,512]{1,0:T(8,128)(2,1)S(1)}, bf16[136,512]{1,0:T(8,128)(2,1)S(1)}, u32[]{:S(2)}, u32[]{:S(2)}) collective-permute-start(bf16[136,512]{1,0:T(8,128)(2,1)S(1)} %collective-permute-done.pair_a_ref), channel_id=1, source_target_pairs={{0,8},{1,9},{2,10},{3,11},{4,12},{5,13},{6,14},{7,15},{8,16},{9,17... | collective-permute-start | bytes 417800 | tf_op jit(solution)/shard_map/ppermute | solution.py:22
  10.5 1.1 %dynamic-slice_bitcast_fusion = (bf16[128,1024]{1,0:T(8,128)(2,1)S(1)}, bf16[128,1024]{1,0:T(8,128)(2,1)S(1)}) fusion(bf16[3,128,2048]{2,1,0:T(8,128)(2,1)} %bitcast.19, s32[]{:T(128)S(6)} %select_n.7, s32[]{:T(128)S(6)} %select_n.6), kind=kLoop, calls=%fused_computation | loop fusion | bytes 1048584 | tf_op jit(solution)/shard_map/squeeze | solution.py:468
  11.5 0.0 collective-permute-done.2.pair_b_ref
  11.5 0.7 %collective-permute-start.4 = (bf16[136,512]{1,0:T(8,128)(2,1)S(1)}, bf16[136,512]{1,0:T(8,128)(2,1)S(1)}, u32[]{:S(2)}, u32[]{:S(2)}) collective-permute-start(bf16[136,512]{1,0:T(8,128)(2,1)S(1)} %collective-permute-done.2.pair_b_ref), channel_id=1, source_target_pairs={{0,1},{1,0},{2,3},{3,2},{4,5},{5,4},{6,7},{7,6},{8,16},{9,17},{10,... | collective-permute-start | bytes 417800 | tf_op jit(solution)/shard_map/ppermute | solution.py:22
  12.3 0.0 collective-permute-start.5
  12.3 1.5 %collective-permute-start.6 = (bf16[128,1024]{1,0:T(8,128)(2,1)S(1)}, bf16[128,1024]{1,0:T(8,128)(2,1)S(1)}, u32[]{:S(2)}, u32[]{:S(2)}) collective-permute-start(bf16[128,1024]{1,0:T(8,128)(2,1)S(1)} %get-tuple-element.50), channel_id=1, source_target_pairs={{0,4},{1,5},{2,6},{3,7},{4,0},{5,1},{6,2},{7,3},{8,12},{9,13},{10,... | collective-permute-start | bytes 786440 | tf_op jit(solution)/shard_map/ppermute | solution.py:22
  13.8 0.0 collective-permute-done.1.back_own_ref
  13.8 2.8 %collective-permute-done.3.refs_0_ = bf16[136,512]{1,0:T(8,128)(2,1)S(1)} collective-permute-done((bf16[136,512]{1,0:T(8,128)(2,1)S(1)}, bf16[136,512]{1,0:T(8,128)(2,1)S(1)}, u32[]{:S(2)}, u32[]{:S(2)}) %collective-permute-start.3) | collective-permute-done | bytes 139296 | tf_op jit(solution)/shard_map/ppermute | solution.py:22
  16.6 0.1 shard_map.75
  16.8 1.5 %collective-permute-start.9 = (bf16[136,512]{1,0:T(8,128)(2,1)S(1)}, bf16[136,512]{1,0:T(8,128)(2,1)S(1)}, u32[]{:S(2)}, u32[]{:S(2)}) collective-permute-start(bf16[136,512]{1,0:T(8,128)(2,1)S(1)} %get-tuple-element.52), channel_id=1, source_target_pairs={{0,1},{1,0},{2,3},{3,2},{4,5},{5,4},{6,7},{7,6},{8,16},{9,17},{10,... | collective-permute-start | bytes 417800 | tf_op jit(solution)/shard_map/ppermute | solution.py:22
  18.2 1.4 %collective-permute-done.4.refs_0_ = bf16[136,512]{1,0:T(8,128)(2,1)S(1)} collective-permute-done((bf16[136,512]{1,0:T(8,128)(2,1)S(1)}, bf16[136,512]{1,0:T(8,128)(2,1)S(1)}, u32[]{:S(2)}, u32[]{:S(2)}) %collective-permute-start.4) | collective-permute-done | bytes 139296 | tf_op jit(solution)/shard_map/ppermute | solution.py:22
  19.6 0.0 collective-permute-done.5.refs_1_
  19.6 0.2 shard_map.76
  19.8 1.2 %collective-permute-start.7 = (bf16[136,512]{1,0:T(8,128)(2,1)S(1)}, bf16[136,512]{1,0:T(8,128)(2,1)S(1)}, u32[]{:S(2)}, u32[]{:S(2)}) collective-permute-start(bf16[136,512]{1,0:T(8,128)(2,1)S(1)} %get-tuple-element.51), channel_id=1, source_target_pairs={{0,1},{1,0},{2,3},{3,2},{4,5},{5,4},{6,7},{7,6},{8,16},{9,17},{10,... | collective-permute-start | bytes 417800 | tf_op jit(solution)/shard_map/ppermute | solution.py:22
  21.0 0.4 collective-permute-start.8
  21.3 1.0 %shard_map.77 = (f32[256,1024]{1,0:T(8,128)S(1)}, f32[128,1024]{1,0:T(8,128)S(1)}) custom-call(s32[1,32]{1,0:T(1,128)S(1)} %bitcast.14, f32[4,8,128]{2,1,0:T(8,128)S(1)} %get-tuple-element.38.marks_ref, bf16[8,2,128,768]{3,2,1,0:T(8,128)(2,1)S(1)} %get-tuple-element.37.table_ref, bf16[136,1024]{1,0:T(8,128)(2,1)S(1)} %get-tuple-element.32.own_ref, ...), custom_call_target="tpu_custom_call" | custom-call | flops 167772160 | bytes 2097152 | tf_op jit(solution)/shard_map/pallas_call | solution.py:499
  22.3 0.0 collective-permute-done.6.raw_ref
  22.3 0.4 shard_map.78.qpair_ref
  22.7 0.0 collective-permute-done.9.refs_0_
  22.7 0.4 %shard_map.79 = (f32[128,512]{1,0:T(8,128)S(1)}, bf16[128,512]{1,0:T(8,128)(2,1)S(1)}, f32[2,128,128]{2,1,0:T(8,128)S(1)}) custom-call(bf16[8,2,128,768]{3,2,1,0:T(8,128)(2,1)S(1)} %get-tuple-element.37.table_ref, f32[256,1024]{1,0:T(8,128)S(1)} %get-tuple-element.48.acc_ref, f32[128,1024]{1,0:T(8,128)S(1)} %get-tuple-element.49.qown_ref, ...), custom_call_target="tpu_custom_call" | custom-call | flops 100663296 | bytes 1572864 | tf_op jit(solution)/shard_map/pallas_call | solution.py:521
  23.1 1.8 %collective-permute-done.7.refs_0_ = bf16[136,512]{1,0:T(8,128)(2,1)S(1)} collective-permute-done((bf16[136,512]{1,0:T(8,128)(2,1)S(1)}, bf16[136,512]{1,0:T(8,128)(2,1)S(1)}, u32[]{:S(2)}, u32[]{:S(2)}) %collective-permute-start.7) | collective-permute-done | bytes 139296 | tf_op jit(solution)/shard_map/ppermute | solution.py:22
  24.9 1.1 %collective-permute-done.8.refs_1_ = bf16[136,512]{1,0:T(8,128)(2,1)S(1)} collective-permute-done((bf16[136,512]{1,0:T(8,128)(2,1)S(1)}, bf16[136,512]{1,0:T(8,128)(2,1)S(1)}, u32[]{:S(2)}, u32[]{:S(2)}) %collective-permute-start.8) | collective-permute-done | bytes 139296 | tf_op jit(solution)/shard_map/ppermute | solution.py:22
  26.0 0.7 %shard_map.80 = (f32[128,512]{1,0:T(8,128)S(1)}, bf16[128,1024]{1,0:T(8,128)(2,1)S(1)}, f32[1,256]{1,0:T(1,128)S(1)}) custom-call(bf16[8,2,128,768]{3,2,1,0:T(8,128)(2,1)S(1)} %get-tuple-element.37.table_ref, f32[256,1024]{1,0:T(8,128)S(1)} %get-tuple-element.48.acc_ref, f32[128,1024]{1,0:T(8,128)S(1)} %get-tuple-element.49.qown_ref, ...), custom_call_target="tpu_custom_call" | custom-call | flops 100663296 | bytes 1572864 | tf_op jit(solution)/shard_map/pallas_call | solution.py:521
  26.8 1.5 %collective-permute-start.14 = (bf16[128,1024]{1,0:T(8,128)(2,1)S(1)}, bf16[128,1024]{1,0:T(8,128)(2,1)S(1)}, u32[]{:S(2)}, u32[]{:S(2)}) collective-permute-start(bf16[128,1024]{1,0:T(8,128)(2,1)S(1)} %get-tuple-element.58), channel_id=1, source_target_pairs={{0,4},{1,5},{2,6},{3,7},{4,0},{5,1},{6,2},{7,3},{8,12},{9,13},{10,... | collective-permute-start | bytes 786440 | tf_op jit(solution)/shard_map/ppermute | solution.py:22
  28.3 0.0 collective-permute-start.10
  28.3 1.5 %collective-permute-start.11 = (f32[1,256]{1,0:T(1,128)S(1)}, f32[1,256]{1,0:T(1,128)S(1)}, u32[]{:S(2)}, u32[]{:S(2)}) collective-permute-start(f32[1,256]{1,0:T(1,128)S(1)} %get-tuple-element.55), channel_id=1, source_target_pairs={{0,2},{1,3},{2,0},{3,1},{4,6},{5,7},{6,4},{7,5},{8,10},{9,11},{10,... | collective-permute-start | bytes 3080 | tf_op jit(solution)/shard_map/ppermute | solution.py:537
  29.8 0.4 collective-permute-start.12
  30.1 0.0 collective-permute-done.10
  30.1 1.7 %collective-permute-done.11 = f32[1,256]{1,0:T(1,128)S(1)} collective-permute-done((f32[1,256]{1,0:T(1,128)S(1)}, f32[1,256]{1,0:T(1,128)S(1)}, u32[]{:S(2)}, u32[]{:S(2)}) %collective-permute-start.11) | collective-permute-done | bytes 1056 | tf_op jit(solution)/shard_map/ppermute | solution.py:537
  31.9 0.9 %collective-permute-done.12 = f32[1,256]{1,0:T(1,128)S(1)} collective-permute-done((f32[1,256]{1,0:T(1,128)S(1)}, f32[1,256]{1,0:T(1,128)S(1)}, u32[]{:S(2)}, u32[]{:S(2)}) %collective-permute-start.12) | collective-permute-done | bytes 1056 | tf_op jit(solution)/shard_map/ppermute | solution.py:537
  32.8 0.5 %collective-permute-start.13 = (f32[1,256]{1,0:T(1,128)S(1)}, f32[1,256]{1,0:T(1,128)S(1)}, u32[]{:S(2)}, u32[]{:S(2)}) collective-permute-start(f32[1,256]{1,0:T(1,128)S(1)} %add_add_fusion.power_ref), channel_id=1, source_target_pairs={{0,4},{1,5},{2,6},{3,7},{4,0},{5,1},{6,2},{7,3},{8,12},{9,13},{10,... | collective-permute-start | bytes 3080 | tf_op jit(solution)/shard_map/ppermute | solution.py:22
  33.3 3.1 %collective-permute-done.13.power_got_ref = f32[1,256]{1,0:T(1,128)S(1)} collective-permute-done((f32[1,256]{1,0:T(1,128)S(1)}, f32[1,256]{1,0:T(1,128)S(1)}, u32[]{:S(2)}, u32[]{:S(2)}) %collective-permute-start.13) | collective-permute-done | bytes 1056 | tf_op jit(solution)/shard_map/ppermute | solution.py:22
  36.3 0.0 collective-permute-done.14.refs_2_
  36.4 1.0 %shard_map.81 = bf16[128,2048]{1,0:T(8,128)(2,1)} custom-call(f32[1,256]{1,0:T(1,128)S(1)} %add_add_fusion.power_ref, f32[1,256]{1,0:T(1,128)S(1)} %collective-permute-done.13.power_got_ref, f32[128,512]{1,0:T(8,128)S(1)} %get-tuple-element.56.refs_0_, f32[128,512]{1,0:T(8,128)S(1)} %get-tuple-element.57.refs_1_, ...), custom_call_target="tpu_custom_call" | custom-call | flops 1048576 | bytes 1310720 | tf_op jit(solution)/shard_map/pallas_call | solution.py:539
  (9 shorter events, 0.0 us)
Async XLA Ops:
  0.0 6.1 %copy-start.1 = (s32[32]{0:T(128)S(1)}, s32[32]{0:T(128)}, u32[]{:S(2)}) copy-start(s32[32]{0:T(128)} %seq_ref.1) | copy-start | bytes 388
  0.0 6.1 %copy-start = (f32[3,3,2048]{2,1,0:T(4,128)S(1)}, f32[3,3,2048]{2,1,0:T(4,128)}, u32[]{:S(2)}) copy-start(f32[3,3,2048]{2,1,0:T(4,128)} %w_ref.1) | copy-start | bytes 221188
  0.0 6.1 %copy-start.4 = (f32[16,512]{1,0:T(8,128)S(1)}, f32[16,512]{1,0:T(8,128)}, u32[]{:S(2)}) copy-start(f32[16,512]{1,0:T(8,128)} %param.9) | copy-start | bytes 98308
  0.0 5.9 %copy-start.5 = (s32[16,4]{0,1:T(4,128)S(1)}, s32[16,4]{0,1:T(4,128)}, u32[]{:S(2)}) copy-start(s32[16,4]{0,1:T(4,128)} %param.10) | copy-start | bytes 772
  2.3 6.8 %collective-permute-start = (bf16[136,512]{1,0:T(8,128)(2,1)S(1)}, bf16[136,512]{1,0:T(8,128)(2,1)S(1)}, u32[]{:S(2)}, u32[]{:S(2)}) collective-permute-start(bf16[136,512]{1,0:T(8,128)(2,1)S(1)} %get-tuple-element.36), channel_id=1, source_target_pairs={{0,4},{1,5},{2,6},{3,7},{4,0},{5,1},{6,2},{7,3},{8,12},{9,13},{10,... | collective-permute-start | bytes 417800 | tf_op jit(solution)/shard_map/ppermute | solution.py:22
  3.8 7.7 %collective-permute-start.2 = (bf16[136,512]{1,0:T(8,128)(2,1)S(1)}, bf16[136,512]{1,0:T(8,128)(2,1)S(1)}, u32[]{:S(2)}, u32[]{:S(2)}) collective-permute-start(bf16[136,512]{1,0:T(8,128)(2,1)S(1)} %get-tuple-element.41), channel_id=1, source_target_pairs={{0,4},{1,5},{2,6},{3,7},{4,0},{5,1},{6,2},{7,3},{8,12},{9,13},{10,... | collective-permute-start | bytes 417800 | tf_op jit(solution)/shard_map/ppermute | solution.py:22
  4.4 9.5 %collective-permute-start.1 = (bf16[136,1024]{1,0:T(8,128)(2,1)S(1)}, bf16[136,1024]{1,0:T(8,128)(2,1)S(1)}, u32[]{:S(2)}, u32[]{:S(2)}) collective-permute-start(bf16[136,1024]{1,0:T(8,128)(2,1)S(1)} %get-tuple-element.32.own_ref), channel_id=1, source_target_pairs={{0,8},{1,9},{2,10},{3,11},{4,12},{5,13},{6,14},{7,15},{8,16},{9,17... | collective-permute-start | bytes 835592 | tf_op jit(solution)/shard_map/ppermute | solution.py:22
  9.0 12.3 %copy-start.2 = (f32[2048]{0:T(1024)S(1)}, f32[2048]{0:T(1024)}, u32[]{:S(2)}) copy-start(f32[2048]{0:T(1024)} %param.11) | copy-start | bytes 24580
  9.0 7.6 %collective-permute-start.3 = (bf16[136,512]{1,0:T(8,128)(2,1)S(1)}, bf16[136,512]{1,0:T(8,128)(2,1)S(1)}, u32[]{:S(2)}, u32[]{:S(2)}) collective-permute-start(bf16[136,512]{1,0:T(8,128)(2,1)S(1)} %collective-permute-done.pair_a_ref), channel_id=1, source_target_pairs={{0,8},{1,9},{2,10},{3,11},{4,12},{5,13},{6,14},{7,15},{8,16},{9,17... | collective-permute-start | bytes 417800 | tf_op jit(solution)/shard_map/ppermute | solution.py:22
  11.5 8.1 %collective-permute-start.4 = (bf16[136,512]{1,0:T(8,128)(2,1)S(1)}, bf16[136,512]{1,0:T(8,128)(2,1)S(1)}, u32[]{:S(2)}, u32[]{:S(2)}) collective-permute-start(bf16[136,512]{1,0:T(8,128)(2,1)S(1)} %collective-permute-done.2.pair_b_ref), channel_id=1, source_target_pairs={{0,1},{1,0},{2,3},{3,2},{4,5},{5,4},{6,7},{7,6},{8,16},{9,17},{10,... | collective-permute-start | bytes 417800 | tf_op jit(solution)/shard_map/ppermute | solution.py:22
  12.3 7.4 %collective-permute-start.5 = (bf16[136,512]{1,0:T(8,128)(2,1)S(1)}, bf16[136,512]{1,0:T(8,128)(2,1)S(1)}, u32[]{:S(2)}, u32[]{:S(2)}) collective-permute-start(bf16[136,512]{1,0:T(8,128)(2,1)S(1)} %collective-permute-done.2.pair_b_ref), channel_id=1, source_target_pairs={{0,8},{1,9},{2,10},{3,11},{4,12},{5,13},{6,14},{7,15},{8,0},{9,1},... | collective-permute-start | bytes 417800 | tf_op jit(solution)/shard_map/ppermute | solution.py:22
  12.3 10.0 %collective-permute-start.6 = (bf16[128,1024]{1,0:T(8,128)(2,1)S(1)}, bf16[128,1024]{1,0:T(8,128)(2,1)S(1)}, u32[]{:S(2)}, u32[]{:S(2)}) collective-permute-start(bf16[128,1024]{1,0:T(8,128)(2,1)S(1)} %get-tuple-element.50), channel_id=1, source_target_pairs={{0,4},{1,5},{2,6},{3,7},{4,0},{5,1},{6,2},{7,3},{8,12},{9,13},{10,... | collective-permute-start | bytes 786440 | tf_op jit(solution)/shard_map/ppermute | solution.py:22
  16.8 5.9 %collective-permute-start.9 = (bf16[136,512]{1,0:T(8,128)(2,1)S(1)}, bf16[136,512]{1,0:T(8,128)(2,1)S(1)}, u32[]{:S(2)}, u32[]{:S(2)}) collective-permute-start(bf16[136,512]{1,0:T(8,128)(2,1)S(1)} %get-tuple-element.52), channel_id=1, source_target_pairs={{0,1},{1,0},{2,3},{3,2},{4,5},{5,4},{6,7},{7,6},{8,16},{9,17},{10,... | collective-permute-start | bytes 417800 | tf_op jit(solution)/shard_map/ppermute | solution.py:22
  19.8 5.1 %collective-permute-start.7 = (bf16[136,512]{1,0:T(8,128)(2,1)S(1)}, bf16[136,512]{1,0:T(8,128)(2,1)S(1)}, u32[]{:S(2)}, u32[]{:S(2)}) collective-permute-start(bf16[136,512]{1,0:T(8,128)(2,1)S(1)} %get-tuple-element.51), channel_id=1, source_target_pairs={{0,1},{1,0},{2,3},{3,2},{4,5},{5,4},{6,7},{7,6},{8,16},{9,17},{10,... | collective-permute-start | bytes 417800 | tf_op jit(solution)/shard_map/ppermute | solution.py:22
  21.0 5.1 %collective-permute-start.8 = (bf16[136,512]{1,0:T(8,128)(2,1)S(1)}, bf16[136,512]{1,0:T(8,128)(2,1)S(1)}, u32[]{:S(2)}, u32[]{:S(2)}) collective-permute-start(bf16[136,512]{1,0:T(8,128)(2,1)S(1)} %get-tuple-element.51), channel_id=1, source_target_pairs={{0,1},{1,0},{2,3},{3,2},{4,5},{5,4},{6,7},{7,6},{8,9},{9,8},{10,11... | collective-permute-start | bytes 417800 | tf_op jit(solution)/shard_map/ppermute | solution.py:22
  26.0 10.3 %copy-start.3 = (f32[2048]{0:T(1024)S(1)}, f32[2048]{0:T(1024)}, u32[]{:S(2)}) copy-start(f32[2048]{0:T(1024)} %param.12) | copy-start | bytes 24580
  26.8 9.6 %collective-permute-start.14 = (bf16[128,1024]{1,0:T(8,128)(2,1)S(1)}, bf16[128,1024]{1,0:T(8,128)(2,1)S(1)}, u32[]{:S(2)}, u32[]{:S(2)}) collective-permute-start(bf16[128,1024]{1,0:T(8,128)(2,1)S(1)} %get-tuple-element.58), channel_id=1, source_target_pairs={{0,4},{1,5},{2,6},{3,7},{4,0},{5,1},{6,2},{7,3},{8,12},{9,13},{10,... | collective-permute-start | bytes 786440 | tf_op jit(solution)/shard_map/ppermute | solution.py:22
  28.3 1.9 %collective-permute-start.10 = (f32[1,256]{1,0:T(1,128)S(1)}, f32[1,256]{1,0:T(1,128)S(1)}, u32[]{:S(2)}, u32[]{:S(2)}) collective-permute-start(f32[1,256]{1,0:T(1,128)S(1)} %get-tuple-element.55), channel_id=1, source_target_pairs={{0,1},{1,0},{2,3},{3,2},{4,5},{5,4},{6,7},{7,6},{8,9},{9,8},{10,11... | collective-permute-start | bytes 3080 | tf_op jit(solution)/shard_map/ppermute | solution.py:537
  28.3 3.6 %collective-permute-start.11 = (f32[1,256]{1,0:T(1,128)S(1)}, f32[1,256]{1,0:T(1,128)S(1)}, u32[]{:S(2)}, u32[]{:S(2)}) collective-permute-start(f32[1,256]{1,0:T(1,128)S(1)} %get-tuple-element.55), channel_id=1, source_target_pairs={{0,2},{1,3},{2,0},{3,1},{4,6},{5,7},{6,4},{7,5},{8,10},{9,11},{10,... | collective-permute-start | bytes 3080 | tf_op jit(solution)/shard_map/ppermute | solution.py:537
  29.8 3.0 %collective-permute-start.12 = (f32[1,256]{1,0:T(1,128)S(1)}, f32[1,256]{1,0:T(1,128)S(1)}, u32[]{:S(2)}, u32[]{:S(2)}) collective-permute-start(f32[1,256]{1,0:T(1,128)S(1)} %get-tuple-element.55), channel_id=1, source_target_pairs={{0,3},{1,2},{2,1},{3,0},{4,7},{5,6},{6,5},{7,4},{8,11},{9,10},{10,... | collective-permute-start | bytes 3080 | tf_op jit(solution)/shard_map/ppermute | solution.py:537
  32.8 3.6 %collective-permute-start.13 = (f32[1,256]{1,0:T(1,128)S(1)}, f32[1,256]{1,0:T(1,128)S(1)}, u32[]{:S(2)}, u32[]{:S(2)}) collective-permute-start(f32[1,256]{1,0:T(1,128)S(1)} %add_add_fusion.power_ref), channel_id=1, source_target_pairs={{0,4},{1,5},{2,6},{3,7},{4,0},{5,1},{6,2},{7,3},{8,12},{9,13},{10,... | collective-permute-start | bytes 3080 | tf_op jit(solution)/shard_map/ppermute | solution.py:22

commit v23 on v21

--- a/solution.py
+++ b/solution.py
@@ -346,19 +346,17 @@
             squares = squares + gated * gated
             out_ref[:, whole if before and part_sent else here] = gated.astype(out_ref.dtype)
         if before:
-            total_ref[:, i * BLK : (i + 1) * BLK] = lax.dot_general(
-                jnp.ones((8, GROUP), jnp.float32),
-                squares,
-                (((1,), (1,)), ((), ())),
-                precision=lax.Precision.HIGHEST,
-                preferred_element_type=jnp.float32,
-            )[0:1]
+            place = lax.broadcasted_iota(jnp.int32, (BLK, BLK), 0) - lax.broadcasted_iota(jnp.int32, (BLK, BLK), 1)
+            column = jnp.sum(squares, axis=1, keepdims=True)
+            total_ref[:, i * BLK : (i + 1) * BLK] = jnp.sum(
+                jnp.where(place == 0, column, 0.0), axis=0, keepdims=True
+            )
         else:
             total_ref[i] = squares
 
 
 def norm_kernel(channels, power_ref, power_got_ref, *refs):
-    *kept_refs, got_ref, gain_ref, out_ref = refs
+    *kept_refs, got_ref, gain_ref, out_hbm, out_ref, sems = refs
     half = lax.axis_index("half")
     power = power_ref[:, :BLK] + power_got_ref[:, BLK:]
     scale = lax.rsqrt(power / channels + norm_eps)
@@ -366,6 +364,8 @@
         jnp.int32, (BLK, BLK), 1
     )
     column = jnp.sum(jnp.where(diagonal, scale, 0.0), axis=1, keepdims=True)
+    piece = kept_refs[0].shape[1]
+    stores = []
     for at, refs in ((half, kept_refs), (1 - half, [got_ref])):
         at = at * got_ref.shape[1]
         for ref in refs:
@@ -373,15 +373,23 @@
                 lanes = pl.ds(pl.multiple_of(at + c, GROUP), GROUP)
                 part = ref[:, c : c + GROUP].astype(jnp.float32)
                 out_ref[:, lanes] = (part * column * gain_ref[:, lanes]).astype(out_ref.dtype)
+                if (c + GROUP) % piece == 0:
+                    ready = pl.ds(pl.multiple_of(at + c + GROUP - piece, piece), piece)
+                    stores.append(
+                        pltpu.make_async_copy(out_ref.at[:, ready], out_hbm.at[:, ready], sems.at[len(stores)])
+                    )
+                    stores[-1].start()
             at = at + ref.shape[1]
-
-
-def kernel_call(body, outs, in_specs, scratch, flops, moved_bytes):
+    for store in stores:
+        store.wait()
+
+
+def kernel_call(body, outs, in_specs, scratch, flops, moved_bytes, out_space=VMEM):
     return pl.pallas_call(
         body,
         out_shape=outs,
         in_specs=in_specs,
-        out_specs=jax.tree.map(lambda _: VMEM, outs),
+        out_specs=jax.tree.map(lambda _: out_space, outs),
         scratch_shapes=scratch,
         compiler_params=pltpu.CompilerParams(vmem_limit_bytes=24 << 20),
         cost_estimate=pl.CostEstimate(flops=flops, bytes_accessed=moved_bytes, transcendentals=0),
@@ -534,9 +542,10 @@
         functools.partial(norm_kernel, channels),
         shape((rows, 2 * width), jnp.bfloat16),
         [VMEM] * 6,
-        [],
+        [pltpu.VMEM((rows, 2 * width), jnp.bfloat16), pltpu.SemaphoreType.DMA((4,))],
         8 * rows * width,
         10 * rows * width,
+        hbm,
     )(power, moved(power, to_pair), *done, back, norm_gain.reshape(1, -1))
 
 

time: 36.1 us -> 35.9 us (level)
  the two profiles are of different devices: /device:TPU:10 before, /device:TPU:8 now
where the time goes in v23:
time: 35.9 us; the launch traced here: 35.7 us
  starting transfers between devices  14.9 us (42%)
  waiting for transfers between devices  10.8 us (30%)
  Pallas kernels  8.63 us (24%)
  local copies, waits for them, and re-layouts  1.25 us (3%)
    ppermute x11, starting transfers between devices, moved(): return lax.ppermute(block, SPOTS + ('mp',), whole)  13 us
    ppermute x11, waiting for transfers between devices, moved(): return lax.ppermute(block, SPOTS + ('mp',), whole)  9.06 us
    pallas_call x1, Pallas kernels, shards(): kernel_call(tables_kernel, (shape((groups, 2, BLK, span), jnp.bfloat16),...  2.85 us
    pallas_call x1, Pallas kernels, shards(): kernel_call(products_kernel, (message, small, small), [hbm] * 3, [pltpu.V...  2.24 us
    ppermute x3, starting transfers between devices, shards(): lax.ppermute(power, 'mp', [(i, i ^ k) for i in range(peers)])  1.86 us
    ppermute x3, waiting for transfers between devices, shards(): lax.ppermute(power, 'mp', [(i, i ^ k) for i in range(peers)])  1.74 us
    squeeze x1, local copies, waits for them, and re-layouts, shards(): lax.dynamic_slice(query, (0, 0, (1 - half) * width), (1, rows, width))[0]  1.06 us
    pallas_call x1, Pallas kernels, shards(): kernel_call(functools.partial(norm_kernel, channels), shape((rows, 2 * wi...  0.99 us
  transfers between devices with their start and end apart: 14, of which 6 were waited for; matrix products, arithmetic and copies ran while one was open for 3% of the time, Pallas kernels for 14%

profile of v23, /device:TPU:8, one launch (start us, length us, event | category | flops | bytes accessed | tf_op | source)
XLA Modules:
  0.0 35.7 jit_solution(1070931936187349547)
XLA Ops:
  0.0 0.0 copy-start.5
  0.0 2.2 %shard_map.73 = (bf16[136,1024]{1,0:T(8,128)(2,1)S(1)}, bf16[136,512]{1,0:T(8,128)(2,1)S(1)}, bf16[136,512]{1,0:T(8,128)(2,1)S(1)}) custom-call(s32[1,32]{1,0:T(1,128)} %bitcast.13, bf16[3,128,2048]{2,1,0:T(8,128)(2,1)} %bitcast.18, f32[3,3,2048]{2,1,0:T(4,128)} %w_ref.1), custom_call_target="tpu_custom_call" | custom-call | flops 5242880 | bytes 2097152 | tf_op jit(solution)/shard_map/pallas_call | solution.py:429
  2.3 1.6 %collective-permute-start = (bf16[136,512]{1,0:T(8,128)(2,1)S(1)}, bf16[136,512]{1,0:T(8,128)(2,1)S(1)}, u32[]{:S(2)}, u32[]{:S(2)}) collective-permute-start(bf16[136,512]{1,0:T(8,128)(2,1)S(1)} %get-tuple-element.36), channel_id=1, source_target_pairs={{0,4},{1,5},{2,6},{3,7},{4,0},{5,1},{6,2},{7,3},{8,12},{9,13},{10,... | collective-permute-start | bytes 417800 | tf_op jit(solution)/shard_map/ppermute | solution.py:22
  3.8 1.6 %collective-permute-start.1 = (bf16[136,1024]{1,0:T(8,128)(2,1)S(1)}, bf16[136,1024]{1,0:T(8,128)(2,1)S(1)}, u32[]{:S(2)}, u32[]{:S(2)}) collective-permute-start(bf16[136,1024]{1,0:T(8,128)(2,1)S(1)} %get-tuple-element.32.own_ref), channel_id=1, source_target_pairs={{0,8},{1,9},{2,10},{3,11},{4,12},{5,13},{6,14},{7,15},{8,16},{9,17... | collective-permute-start | bytes 835592 | tf_op jit(solution)/shard_map/ppermute | solution.py:22
  5.4 0.5 %collective-permute-start.2 = (bf16[136,512]{1,0:T(8,128)(2,1)S(1)}, bf16[136,512]{1,0:T(8,128)(2,1)S(1)}, u32[]{:S(2)}, u32[]{:S(2)}) collective-permute-start(bf16[136,512]{1,0:T(8,128)(2,1)S(1)} %get-tuple-element.41), channel_id=1, source_target_pairs={{0,4},{1,5},{2,6},{3,7},{4,0},{5,1},{6,2},{7,3},{8,12},{9,13},{10,... | collective-permute-start | bytes 417800 | tf_op jit(solution)/shard_map/ppermute | solution.py:22
  5.9 0.0 copy-done.5
  5.9 0.1 copy.8
  6.0 0.1 broadcast_in_dim.3
  6.1 0.0 copy-done.4
  6.1 0.0 copy-done.1
  6.1 0.0 copy-done
  6.2 2.9 %shard_map.74 = (bf16[8,2,128,768]{3,2,1,0:T(8,128)(2,1)S(1)}, bf16[8,128,256]{2,1,0:T(8,128)(2,1)S(1)}, f32[3,3,1024]{2,1,0:T(4,128)S(1)}, f32[4,8,128]{2,1,0:T(8,128)S(1)}) custom-call(s32[32]{0:T(128)S(1)} %copy-done.1, bf16[16,512]{1,0:T(8,128)(2,1)S(1)} %fusion.taps_ref, f32[3,3,2048]{2,1,0:T(4,128)S(1)} %copy-done), custom_call_target="tpu_custom_call" | custom-call | flops 20971520 | bytes 4194304 | tf_op jit(solution)/shard_map/pallas_call | solution.py:453
  9.0 0.0 collective-permute-done.pair_a_ref
  9.0 0.0 copy-start.2
  9.0 1.6 %collective-permute-start.3 = (bf16[136,512]{1,0:T(8,128)(2,1)S(1)}, bf16[136,512]{1,0:T(8,128)(2,1)S(1)}, u32[]{:S(2)}, u32[]{:S(2)}) collective-permute-start(bf16[136,512]{1,0:T(8,128)(2,1)S(1)} %collective-permute-done.pair_a_ref), channel_id=1, source_target_pairs={{0,8},{1,9},{2,10},{3,11},{4,12},{5,13},{6,14},{7,15},{8,16},{9,17... | collective-permute-start | bytes 417800 | tf_op jit(solution)/shard_map/ppermute | solution.py:22
  10.7 1.1 %dynamic-slice_bitcast_fusion = (bf16[128,1024]{1,0:T(8,128)(2,1)S(1)}, bf16[128,1024]{1,0:T(8,128)(2,1)S(1)}) fusion(bf16[3,128,2048]{2,1,0:T(8,128)(2,1)} %bitcast.19, s32[]{:T(128)S(6)} %select_n.7, s32[]{:T(128)S(6)} %select_n.6), kind=kLoop, calls=%fused_computation | loop fusion | bytes 1048584 | tf_op jit(solution)/shard_map/squeeze | solution.py:471
  11.7 0.0 collective-permute-done.2.pair_b_ref
  11.7 1.4 %collective-permute-start.4 = (bf16[136,512]{1,0:T(8,128)(2,1)S(1)}, bf16[136,512]{1,0:T(8,128)(2,1)S(1)}, u32[]{:S(2)}, u32[]{:S(2)}) collective-permute-start(bf16[136,512]{1,0:T(8,128)(2,1)S(1)} %collective-permute-done.2.pair_b_ref), channel_id=1, source_target_pairs={{0,1},{1,0},{2,3},{3,2},{4,5},{5,4},{6,7},{7,6},{8,16},{9,17},{10,... | collective-permute-start | bytes 417800 | tf_op jit(solution)/shard_map/ppermute | solution.py:22
  13.2 0.0 collective-permute-start.5
  13.2 1.5 %collective-permute-start.6 = (bf16[128,1024]{1,0:T(8,128)(2,1)S(1)}, bf16[128,1024]{1,0:T(8,128)(2,1)S(1)}, u32[]{:S(2)}, u32[]{:S(2)}) collective-permute-start(bf16[128,1024]{1,0:T(8,128)(2,1)S(1)} %get-tuple-element.50), channel_id=1, source_target_pairs={{0,4},{1,5},{2,6},{3,7},{4,0},{5,1},{6,2},{7,3},{8,12},{9,13},{10,... | collective-permute-start | bytes 786440 | tf_op jit(solution)/shard_map/ppermute | solution.py:22
  14.7 0.0 collective-permute-done.1.back_own_ref
  14.7 1.5 %collective-permute-done.3.refs_0_ = bf16[136,512]{1,0:T(8,128)(2,1)S(1)} collective-permute-done((bf16[136,512]{1,0:T(8,128)(2,1)S(1)}, bf16[136,512]{1,0:T(8,128)(2,1)S(1)}, u32[]{:S(2)}, u32[]{:S(2)}) %collective-permute-start.3) | collective-permute-done | bytes 139296 | tf_op jit(solution)/shard_map/ppermute | solution.py:22
  16.2 0.1 shard_map.75
  16.3 1.6 %collective-permute-start.8 = (bf16[136,512]{1,0:T(8,128)(2,1)S(1)}, bf16[136,512]{1,0:T(8,128)(2,1)S(1)}, u32[]{:S(2)}, u32[]{:S(2)}) collective-permute-start(bf16[136,512]{1,0:T(8,128)(2,1)S(1)} %get-tuple-element.52), channel_id=1, source_target_pairs={{0,1},{1,0},{2,3},{3,2},{4,5},{5,4},{6,7},{7,6},{8,16},{9,17},{10,... | collective-permute-start | bytes 417800 | tf_op jit(solution)/shard_map/ppermute | solution.py:22
  18.0 1.9 %collective-permute-done.4.refs_0_ = bf16[136,512]{1,0:T(8,128)(2,1)S(1)} collective-permute-done((bf16[136,512]{1,0:T(8,128)(2,1)S(1)}, bf16[136,512]{1,0:T(8,128)(2,1)S(1)}, u32[]{:S(2)}, u32[]{:S(2)}) %collective-permute-start.4) | collective-permute-done | bytes 139296 | tf_op jit(solution)/shard_map/ppermute | solution.py:22
  19.8 0.0 collective-permute-done.5.refs_1_
  19.8 0.2 shard_map.76
  20.0 1.0 %collective-permute-start.7 = (bf16[136,512]{1,0:T(8,128)(2,1)S(1)}, bf16[136,512]{1,0:T(8,128)(2,1)S(1)}, u32[]{:S(2)}, u32[]{:S(2)}) collective-permute-start(bf16[136,512]{1,0:T(8,128)(2,1)S(1)} %get-tuple-element.51), channel_id=1, source_target_pairs={{0,1},{1,0},{2,3},{3,2},{4,5},{5,4},{6,7},{7,6},{8,16},{9,17},{10,... | collective-permute-start | bytes 417800 | tf_op jit(solution)/shard_map/ppermute | solution.py:22
  21.0 0.0 copy-done.2
  21.0 1.0 %shard_map.77 = (f32[256,1024]{1,0:T(8,128)S(1)}, f32[128,1024]{1,0:T(8,128)S(1)}) custom-call(s32[1,32]{1,0:T(1,128)S(1)} %bitcast.14, f32[4,8,128]{2,1,0:T(8,128)S(1)} %get-tuple-element.38.marks_ref, bf16[8,2,128,768]{3,2,1,0:T(8,128)(2,1)S(1)} %get-tuple-element.37.table_ref, bf16[136,1024]{1,0:T(8,128)(2,1)S(1)} %get-tuple-element.32.own_ref, ...), custom_call_target="tpu_custom_call" | custom-call | flops 167772160 | bytes 2097152 | tf_op jit(solution)/shard_map/pallas_call | solution.py:501
  21.9 0.0 collective-permute-done.6.raw_ref
  22.0 0.4 %shard_map.78.qpair_ref = f32[128,1024]{1,0:T(8,128)S(1)} custom-call(s32[1,32]{1,0:T(1,128)S(1)} %bitcast.15, bf16[128,1024]{1,0:T(8,128)(2,1)S(1)} %collective-permute-done.6.raw_ref, bf16[136,1024]{1,0:T(8,128)(2,1)S(1)} %get-tuple-element.32.own_ref, bf16[136,1024]{1,0:T(8,128)(2,1)S(1)} %collective-permute-done.1.back_own_ref, ...), custom_call_target="tpu_custom_call" | custom-call | flops 1310720 | bytes 1048576 | tf_op jit(solution)/shard_map/pallas_call | solution.py:510
  22.3 0.0 collective-permute-done.8.refs_0_
  22.4 0.4 %shard_map.79 = (f32[128,512]{1,0:T(8,128)S(1)}, bf16[128,512]{1,0:T(8,128)(2,1)S(1)}, f32[2,128,128]{2,1,0:T(8,128)S(1)}) custom-call(bf16[8,2,128,768]{3,2,1,0:T(8,128)(2,1)S(1)} %get-tuple-element.37.table_ref, f32[256,1024]{1,0:T(8,128)S(1)} %get-tuple-element.48.acc_ref, f32[128,1024]{1,0:T(8,128)S(1)} %get-tuple-element.49.qown_ref, ...), custom_call_target="tpu_custom_call" | custom-call | flops 100663296 | bytes 1572864 | tf_op jit(solution)/shard_map/pallas_call | solution.py:523
  22.8 3.2 %collective-permute-done.7.refs_0_ = bf16[136,512]{1,0:T(8,128)(2,1)S(1)} collective-permute-done((bf16[136,512]{1,0:T(8,128)(2,1)S(1)}, bf16[136,512]{1,0:T(8,128)(2,1)S(1)}, u32[]{:S(2)}, u32[]{:S(2)}) %collective-permute-start.7) | collective-permute-done | bytes 139296 | tf_op jit(solution)/shard_map/ppermute | solution.py:22
  26.0 0.5 %shard_map.80 = (f32[128,512]{1,0:T(8,128)S(1)}, bf16[128,1024]{1,0:T(8,128)(2,1)S(1)}, f32[1,256]{1,0:T(1,128)S(1)}) custom-call(bf16[8,2,128,768]{3,2,1,0:T(8,128)(2,1)S(1)} %get-tuple-element.37.table_ref, f32[256,1024]{1,0:T(8,128)S(1)} %get-tuple-element.48.acc_ref, f32[128,1024]{1,0:T(8,128)S(1)} %get-tuple-element.49.qown_ref, ...), custom_call_target="tpu_custom_call" | custom-call | flops 100663296 | bytes 1572864 | tf_op jit(solution)/shard_map/pallas_call | solution.py:523
  26.5 1.0 %collective-permute-start.13 = (bf16[128,1024]{1,0:T(8,128)(2,1)S(1)}, bf16[128,1024]{1,0:T(8,128)(2,1)S(1)}, u32[]{:S(2)}, u32[]{:S(2)}) collective-permute-start(bf16[128,1024]{1,0:T(8,128)(2,1)S(1)} %get-tuple-element.58), channel_id=1, source_target_pairs={{0,4},{1,5},{2,6},{3,7},{4,0},{5,1},{6,2},{7,3},{8,12},{9,13},{10,... | collective-permute-start | bytes 786440 | tf_op jit(solution)/shard_map/ppermute | solution.py:22
  27.5 0.0 collective-permute-start.11
  27.5 1.5 %collective-permute-start.10 = (f32[1,256]{1,0:T(1,128)S(1)}, f32[1,256]{1,0:T(1,128)S(1)}, u32[]{:S(2)}, u32[]{:S(2)}) collective-permute-start(f32[1,256]{1,0:T(1,128)S(1)} %get-tuple-element.55), channel_id=1, source_target_pairs={{0,2},{1,3},{2,0},{3,1},{4,6},{5,7},{6,4},{7,5},{8,10},{9,11},{10,... | collective-permute-start | bytes 3080 | tf_op jit(solution)/shard_map/ppermute | solution.py:539
  29.0 0.3 collective-permute-start.9
  29.4 1.1 %collective-permute-done.11 = f32[1,256]{1,0:T(1,128)S(1)} collective-permute-done((f32[1,256]{1,0:T(1,128)S(1)}, f32[1,256]{1,0:T(1,128)S(1)}, u32[]{:S(2)}, u32[]{:S(2)}) %collective-permute-start.11) | collective-permute-done | bytes 1056 | tf_op jit(solution)/shard_map/ppermute | solution.py:539
  30.5 0.6 %collective-permute-done.10 = f32[1,256]{1,0:T(1,128)S(1)} collective-permute-done((f32[1,256]{1,0:T(1,128)S(1)}, f32[1,256]{1,0:T(1,128)S(1)}, u32[]{:S(2)}, u32[]{:S(2)}) %collective-permute-start.10) | collective-permute-done | bytes 1056 | tf_op jit(solution)/shard_map/ppermute | solution.py:539
  31.1 0.0 collective-permute-done.9
  31.1 1.1 %collective-permute-start.12 = (f32[1,256]{1,0:T(1,128)S(1)}, f32[1,256]{1,0:T(1,128)S(1)}, u32[]{:S(2)}, u32[]{:S(2)}) collective-permute-start(f32[1,256]{1,0:T(1,128)S(1)} %add_add_fusion.power_ref), channel_id=1, source_target_pairs={{0,4},{1,5},{2,6},{3,7},{4,0},{5,1},{6,2},{7,3},{8,12},{9,13},{10,... | collective-permute-start | bytes 3080 | tf_op jit(solution)/shard_map/ppermute | solution.py:22
  32.2 2.5 %collective-permute-done.12.power_got_ref = f32[1,256]{1,0:T(1,128)S(1)} collective-permute-done((f32[1,256]{1,0:T(1,128)S(1)}, f32[1,256]{1,0:T(1,128)S(1)}, u32[]{:S(2)}, u32[]{:S(2)}) %collective-permute-start.12) | collective-permute-done | bytes 1056 | tf_op jit(solution)/shard_map/ppermute | solution.py:22
  34.7 0.0 collective-permute-done.13.refs_2_
  34.7 0.0 copy-done.3
  34.8 1.0 %shard_map.81 = bf16[128,2048]{1,0:T(8,128)(2,1)} custom-call(f32[1,256]{1,0:T(1,128)S(1)} %add_add_fusion.power_ref, f32[1,256]{1,0:T(1,128)S(1)} %collective-permute-done.12.power_got_ref, f32[128,512]{1,0:T(8,128)S(1)} %get-tuple-element.56.refs_0_, f32[128,512]{1,0:T(8,128)S(1)} %get-tuple-element.57.refs_1_, ...), custom_call_target="tpu_custom_call" | custom-call | flops 1048576 | bytes 1310720 | tf_op jit(solution)/shard_map/pallas_call | solution.py:541
  (7 shorter events, 0.0 us)
Async XLA Ops:
  0.0 6.1 %copy-start.1 = (s32[32]{0:T(128)S(1)}, s32[32]{0:T(128)}, u32[]{:S(2)}) copy-start(s32[32]{0:T(128)} %seq_ref.1) | copy-start | bytes 388
  0.0 6.1 %copy-start = (f32[3,3,2048]{2,1,0:T(4,128)S(1)}, f32[3,3,2048]{2,1,0:T(4,128)}, u32[]{:S(2)}) copy-start(f32[3,3,2048]{2,1,0:T(4,128)} %w_ref.1) | copy-start | bytes 221188
  0.0 6.1 %copy-start.4 = (f32[16,512]{1,0:T(8,128)S(1)}, f32[16,512]{1,0:T(8,128)}, u32[]{:S(2)}) copy-start(f32[16,512]{1,0:T(8,128)} %param.9) | copy-start | bytes 98308
  0.0 5.9 %copy-start.5 = (s32[16,4]{0,1:T(4,128)S(1)}, s32[16,4]{0,1:T(4,128)}, u32[]{:S(2)}) copy-start(s32[16,4]{0,1:T(4,128)} %param.10) | copy-start | bytes 772
  2.3 6.8 %collective-permute-start = (bf16[136,512]{1,0:T(8,128)(2,1)S(1)}, bf16[136,512]{1,0:T(8,128)(2,1)S(1)}, u32[]{:S(2)}, u32[]{:S(2)}) collective-permute-start(bf16[136,512]{1,0:T(8,128)(2,1)S(1)} %get-tuple-element.36), channel_id=1, source_target_pairs={{0,4},{1,5},{2,6},{3,7},{4,0},{5,1},{6,2},{7,3},{8,12},{9,13},{10,... | collective-permute-start | bytes 417800 | tf_op jit(solution)/shard_map/ppermute | solution.py:22
  3.8 10.9 %collective-permute-start.1 = (bf16[136,1024]{1,0:T(8,128)(2,1)S(1)}, bf16[136,1024]{1,0:T(8,128)(2,1)S(1)}, u32[]{:S(2)}, u32[]{:S(2)}) collective-permute-start(bf16[136,1024]{1,0:T(8,128)(2,1)S(1)} %get-tuple-element.32.own_ref), channel_id=1, source_target_pairs={{0,8},{1,9},{2,10},{3,11},{4,12},{5,13},{6,14},{7,15},{8,16},{9,17... | collective-permute-start | bytes 835592 | tf_op jit(solution)/shard_map/ppermute | solution.py:22
  5.4 6.3 %collective-permute-start.2 = (bf16[136,512]{1,0:T(8,128)(2,1)S(1)}, bf16[136,512]{1,0:T(8,128)(2,1)S(1)}, u32[]{:S(2)}, u32[]{:S(2)}) collective-permute-start(bf16[136,512]{1,0:T(8,128)(2,1)S(1)} %get-tuple-element.41), channel_id=1, source_target_pairs={{0,4},{1,5},{2,6},{3,7},{4,0},{5,1},{6,2},{7,3},{8,12},{9,13},{10,... | collective-permute-start | bytes 417800 | tf_op jit(solution)/shard_map/ppermute | solution.py:22
  9.0 11.9 %copy-start.2 = (f32[2048]{0:T(1024)S(1)}, f32[2048]{0:T(1024)}, u32[]{:S(2)}) copy-start(f32[2048]{0:T(1024)} %param.11) | copy-start | bytes 24580
  9.0 7.1 %collective-permute-start.3 = (bf16[136,512]{1,0:T(8,128)(2,1)S(1)}, bf16[136,512]{1,0:T(8,128)(2,1)S(1)}, u32[]{:S(2)}, u32[]{:S(2)}) collective-permute-start(bf16[136,512]{1,0:T(8,128)(2,1)S(1)} %collective-permute-done.pair_a_ref), channel_id=1, source_target_pairs={{0,8},{1,9},{2,10},{3,11},{4,12},{5,13},{6,14},{7,15},{8,16},{9,17... | collective-permute-start | bytes 417800 | tf_op jit(solution)/shard_map/ppermute | solution.py:22
  11.7 8.1 %collective-permute-start.4 = (bf16[136,512]{1,0:T(8,128)(2,1)S(1)}, bf16[136,512]{1,0:T(8,128)(2,1)S(1)}, u32[]{:S(2)}, u32[]{:S(2)}) collective-permute-start(bf16[136,512]{1,0:T(8,128)(2,1)S(1)} %collective-permute-done.2.pair_b_ref), channel_id=1, source_target_pairs={{0,1},{1,0},{2,3},{3,2},{4,5},{5,4},{6,7},{7,6},{8,16},{9,17},{10,... | collective-permute-start | bytes 417800 | tf_op jit(solution)/shard_map/ppermute | solution.py:22
  13.2 6.6 %collective-permute-start.5 = (bf16[136,512]{1,0:T(8,128)(2,1)S(1)}, bf16[136,512]{1,0:T(8,128)(2,1)S(1)}, u32[]{:S(2)}, u32[]{:S(2)}) collective-permute-start(bf16[136,512]{1,0:T(8,128)(2,1)S(1)} %collective-permute-done.2.pair_b_ref), channel_id=1, source_target_pairs={{0,8},{1,9},{2,10},{3,11},{4,12},{5,13},{6,14},{7,15},{8,0},{9,1},... | collective-permute-start | bytes 417800 | tf_op jit(solution)/shard_map/ppermute | solution.py:22
  13.2 8.8 %collective-permute-start.6 = (bf16[128,1024]{1,0:T(8,128)(2,1)S(1)}, bf16[128,1024]{1,0:T(8,128)(2,1)S(1)}, u32[]{:S(2)}, u32[]{:S(2)}) collective-permute-start(bf16[128,1024]{1,0:T(8,128)(2,1)S(1)} %get-tuple-element.50), channel_id=1, source_target_pairs={{0,4},{1,5},{2,6},{3,7},{4,0},{5,1},{6,2},{7,3},{8,12},{9,13},{10,... | collective-permute-start | bytes 786440 | tf_op jit(solution)/shard_map/ppermute | solution.py:22
  16.3 6.0 %collective-permute-start.8 = (bf16[136,512]{1,0:T(8,128)(2,1)S(1)}, bf16[136,512]{1,0:T(8,128)(2,1)S(1)}, u32[]{:S(2)}, u32[]{:S(2)}) collective-permute-start(bf16[136,512]{1,0:T(8,128)(2,1)S(1)} %get-tuple-element.52), channel_id=1, source_target_pairs={{0,1},{1,0},{2,3},{3,2},{4,5},{5,4},{6,7},{7,6},{8,16},{9,17},{10,... | collective-permute-start | bytes 417800 | tf_op jit(solution)/shard_map/ppermute | solution.py:22
  20.0 6.0 %collective-permute-start.7 = (bf16[136,512]{1,0:T(8,128)(2,1)S(1)}, bf16[136,512]{1,0:T(8,128)(2,1)S(1)}, u32[]{:S(2)}, u32[]{:S(2)}) collective-permute-start(bf16[136,512]{1,0:T(8,128)(2,1)S(1)} %get-tuple-element.51), channel_id=1, source_target_pairs={{0,1},{1,0},{2,3},{3,2},{4,5},{5,4},{6,7},{7,6},{8,16},{9,17},{10,... | collective-permute-start | bytes 417800 | tf_op jit(solution)/shard_map/ppermute | solution.py:22
  26.0 8.8 %copy-start.3 = (f32[2048]{0:T(1024)S(1)}, f32[2048]{0:T(1024)}, u32[]{:S(2)}) copy-start(f32[2048]{0:T(1024)} %param.12) | copy-start | bytes 24580
  26.5 8.3 %collective-permute-start.13 = (bf16[128,1024]{1,0:T(8,128)(2,1)S(1)}, bf16[128,1024]{1,0:T(8,128)(2,1)S(1)}, u32[]{:S(2)}, u32[]{:S(2)}) collective-permute-start(bf16[128,1024]{1,0:T(8,128)(2,1)S(1)} %get-tuple-element.58), channel_id=1, source_target_pairs={{0,4},{1,5},{2,6},{3,7},{4,0},{5,1},{6,2},{7,3},{8,12},{9,13},{10,... | collective-permute-start | bytes 786440 | tf_op jit(solution)/shard_map/ppermute | solution.py:22
  27.5 3.0 %collective-permute-start.11 = (f32[1,256]{1,0:T(1,128)S(1)}, f32[1,256]{1,0:T(1,128)S(1)}, u32[]{:S(2)}, u32[]{:S(2)}) collective-permute-start(f32[1,256]{1,0:T(1,128)S(1)} %get-tuple-element.55), channel_id=1, source_target_pairs={{0,3},{1,2},{2,1},{3,0},{4,7},{5,6},{6,5},{7,4},{8,11},{9,10},{10,... | collective-permute-start | bytes 3080 | tf_op jit(solution)/shard_map/ppermute | solution.py:539
  27.5 3.6 %collective-permute-start.10 = (f32[1,256]{1,0:T(1,128)S(1)}, f32[1,256]{1,0:T(1,128)S(1)}, u32[]{:S(2)}, u32[]{:S(2)}) collective-permute-start(f32[1,256]{1,0:T(1,128)S(1)} %get-tuple-element.55), channel_id=1, source_target_pairs={{0,2},{1,3},{2,0},{3,1},{4,6},{5,7},{6,4},{7,5},{8,10},{9,11},{10,... | collective-permute-start | bytes 3080 | tf_op jit(solution)/shard_map/ppermute | solution.py:539
  29.0 2.1 %collective-permute-start.9 = (f32[1,256]{1,0:T(1,128)S(1)}, f32[1,256]{1,0:T(1,128)S(1)}, u32[]{:S(2)}, u32[]{:S(2)}) collective-permute-start(f32[1,256]{1,0:T(1,128)S(1)} %get-tuple-element.55), channel_id=1, source_target_pairs={{0,1},{1,0},{2,3},{3,2},{4,5},{5,4},{6,7},{7,6},{8,9},{9,8},{10,11... | collective-permute-start | bytes 3080 | tf_op jit(solution)/shard_map/ppermute | solution.py:539
  31.1 3.6 %collective-permute-start.12 = (f32[1,256]{1,0:T(1,128)S(1)}, f32[1,256]{1,0:T(1,128)S(1)}, u32[]{:S(2)}, u32[]{:S(2)}) collective-permute-start(f32[1,256]{1,0:T(1,128)S(1)} %add_add_fusion.power_ref), channel_id=1, source_target_pairs={{0,4},{1,5},{2,6},{3,7},{4,0},{5,1},{6,2},{7,3},{8,12},{9,13},{10,... | collective-permute-start | bytes 3080 | tf_op jit(solution)/shard_map/ppermute | solution.py:22

commit v24 on v23

--- a/solution.py
+++ b/solution.py
@@ -209,7 +209,7 @@
 def relay_kernel(piece, marks_ref, next_ref, back_own_ref, w_ref, *refs):
     *ways, out_ref, back_pair_ref, win_ref, extra_ref = refs
     for i, way in enumerate(ways):
-        @pl.when((lax.axis_index("blk") + i) % len(ways) == 0)
+        @pl.when((lax.axis_index("blk") + i) % len(ways) == len(ways) - 1)
         def _():
             back_pair_ref[...] = way[...]
 
@@ -471,7 +471,8 @@
     qsent = lax.dynamic_slice(query, (0, 0, (1 - half) * width), (1, rows, width))[0]
     qkept, qsent, pair[1] = lax.optimization_barrier((qkept, qsent, pair[1]))
     qgot = moved(qsent, to_pair)
-    back_pair = [[moved(pair[0], ahead)], [moved(pair[1], matching(blocks, first)) for first in (1, 0)]]
+    by_odd = moved(pair[1], matching(blocks, 0))
+    back_pair = [[moved(pair[0], ahead)], [by_odd, moved(pair[1], matching(blocks, 1))]]
 
     window = pltpu.VMEM((4 * rows, width), jnp.bfloat16)
     extras = pltpu.VMEM((4, 16, width), jnp.float32)

time: 35.9 us -> 36.1 us (level)
  waiting for transfers between devices: 10.8 us -> 10.4 us
  Pallas kernels: 8.63 us -> 9.01 us
    pallas_call x2, Pallas kernels: 0.3 us -> 0.7 us  [shards(): kernel_call(functools.partial(relay_kernel, piece), (small, small), [VMEM...]
    ppermute x11, waiting for transfers between devices: 9.06 us -> 8.67 us  [moved(): return lax.ppermute(block, SPOTS + ('mp',), whole)]
  transfers between devices with their start and end apart: 14 -> 14, of which waited for: 6 -> 7; matrix products, arithmetic and copies ran while one was open for 3% -> 3% of each run, Pallas kernels for 14% -> 15%
where the time goes in v24:
time: 36.1 us
  starting transfers between devices  15.2 us (42%)
  waiting for transfers between devices  10.4 us (29%)
  Pallas kernels  9.01 us (25%)
  local copies, waits for them, and re-layouts  1.25 us (3%)
    ppermute x11, starting transfers between devices, moved(): return lax.ppermute(block, SPOTS + ('mp',), whole)  13.4 us
    ppermute x11, waiting for transfers between devices, moved(): return lax.ppermute(block, SPOTS + ('mp',), whole)  8.67 us
    pallas_call x1, Pallas kernels, shards(): kernel_call(tables_kernel, (shape((groups, 2, BLK, span), jnp.bfloat16),...  2.85 us
    pallas_call x1, Pallas kernels, shards(): kernel_call(products_kernel, (message, small, small), [hbm] * 3, [pltpu.V...  2.24 us
    ppermute x3, starting transfers between devices, shards(): lax.ppermute(power, 'mp', [(i, i ^ k) for i in range(peers)])  1.86 us
    ppermute x3, waiting for transfers between devices, shards(): lax.ppermute(power, 'mp', [(i, i ^ k) for i in range(peers)])  1.74 us
    squeeze x1, local copies, waits for them, and re-layouts, shards(): lax.dynamic_slice(query, (0, 0, (1 - half) * width), (1, rows, width))[0]  1.06 us
    pallas_call x1, Pallas kernels, shards(): kernel_call(functools.partial(norm_kernel, channels), shape((rows, 2 * wi...  0.99 us
  transfers between devices with their start and end apart: 14, of which 7 were waited for; matrix products, arithmetic and copies ran while one was open for 3% of the time, Pallas kernels for 15%

profile of v24, /device:TPU:8, one launch (start us, length us, event | category | flops | bytes accessed | tf_op | source)
XLA Modules:
  0.0 36.1 jit_solution(13210553103806205957)
XLA Ops:
  0.0 0.0 copy-start.5
  0.0 2.2 %shard_map.73 = (bf16[136,1024]{1,0:T(8,128)(2,1)S(1)}, bf16[136,512]{1,0:T(8,128)(2,1)S(1)}, bf16[136,512]{1,0:T(8,128)(2,1)S(1)}) custom-call(s32[1,32]{1,0:T(1,128)} %bitcast.13, bf16[3,128,2048]{2,1,0:T(8,128)(2,1)} %bitcast.18, f32[3,3,2048]{2,1,0:T(4,128)} %w_ref.1), custom_call_target="tpu_custom_call" | custom-call | flops 5242880 | bytes 2097152 | tf_op jit(solution)/shard_map/pallas_call | solution.py:429
  2.3 1.6 %collective-permute-start = (bf16[136,512]{1,0:T(8,128)(2,1)S(1)}, bf16[136,512]{1,0:T(8,128)(2,1)S(1)}, u32[]{:S(2)}, u32[]{:S(2)}) collective-permute-start(bf16[136,512]{1,0:T(8,128)(2,1)S(1)} %get-tuple-element.36), channel_id=1, source_target_pairs={{0,4},{1,5},{2,6},{3,7},{4,0},{5,1},{6,2},{7,3},{8,12},{9,13},{10,... | collective-permute-start | bytes 417800 | tf_op jit(solution)/shard_map/ppermute | solution.py:22
  3.8 1.6 %collective-permute-start.1 = (bf16[136,1024]{1,0:T(8,128)(2,1)S(1)}, bf16[136,1024]{1,0:T(8,128)(2,1)S(1)}, u32[]{:S(2)}, u32[]{:S(2)}) collective-permute-start(bf16[136,1024]{1,0:T(8,128)(2,1)S(1)} %get-tuple-element.32.own_ref), channel_id=1, source_target_pairs={{0,8},{1,9},{2,10},{3,11},{4,12},{5,13},{6,14},{7,15},{8,16},{9,17... | collective-permute-start | bytes 835592 | tf_op jit(solution)/shard_map/ppermute | solution.py:22
  5.4 0.5 %collective-permute-start.2 = (bf16[136,512]{1,0:T(8,128)(2,1)S(1)}, bf16[136,512]{1,0:T(8,128)(2,1)S(1)}, u32[]{:S(2)}, u32[]{:S(2)}) collective-permute-start(bf16[136,512]{1,0:T(8,128)(2,1)S(1)} %get-tuple-element.41), channel_id=1, source_target_pairs={{0,4},{1,5},{2,6},{3,7},{4,0},{5,1},{6,2},{7,3},{8,12},{9,13},{10,... | collective-permute-start | bytes 417800 | tf_op jit(solution)/shard_map/ppermute | solution.py:22
  5.9 0.0 copy-done.5
  5.9 0.1 copy.8
  6.0 0.1 broadcast_in_dim.3
  6.1 0.0 copy-done.4
  6.1 0.0 copy-done.1
  6.1 0.0 copy-done
  6.2 2.9 %shard_map.74 = (bf16[8,2,128,768]{3,2,1,0:T(8,128)(2,1)S(1)}, bf16[8,128,256]{2,1,0:T(8,128)(2,1)S(1)}, f32[3,3,1024]{2,1,0:T(4,128)S(1)}, f32[4,8,128]{2,1,0:T(8,128)S(1)}) custom-call(s32[32]{0:T(128)S(1)} %copy-done.1, bf16[16,512]{1,0:T(8,128)(2,1)S(1)} %fusion.taps_ref, f32[3,3,2048]{2,1,0:T(4,128)S(1)} %copy-done), custom_call_target="tpu_custom_call" | custom-call | flops 20971520 | bytes 4194304 | tf_op jit(solution)/shard_map/pallas_call | solution.py:453
  9.0 0.0 collective-permute-done.pair_a_ref
  9.0 0.0 copy-start.2
  9.0 1.6 %collective-permute-start.3 = (bf16[136,512]{1,0:T(8,128)(2,1)S(1)}, bf16[136,512]{1,0:T(8,128)(2,1)S(1)}, u32[]{:S(2)}, u32[]{:S(2)}) collective-permute-start(bf16[136,512]{1,0:T(8,128)(2,1)S(1)} %collective-permute-done.pair_a_ref), channel_id=1, source_target_pairs={{0,8},{1,9},{2,10},{3,11},{4,12},{5,13},{6,14},{7,15},{8,16},{9,17... | collective-permute-start | bytes 417800 | tf_op jit(solution)/shard_map/ppermute | solution.py:22
  10.7 1.1 %dynamic-slice_bitcast_fusion = (bf16[128,1024]{1,0:T(8,128)(2,1)S(1)}, bf16[128,1024]{1,0:T(8,128)(2,1)S(1)}) fusion(bf16[3,128,2048]{2,1,0:T(8,128)(2,1)} %bitcast.19, s32[]{:T(128)S(6)} %select_n.7, s32[]{:T(128)S(6)} %select_n.6), kind=kLoop, calls=%fused_computation | loop fusion | bytes 1048584 | tf_op jit(solution)/shard_map/squeeze | solution.py:471
  11.7 0.0 collective-permute-done.2.pair_b_ref
  11.7 0.5 %collective-permute-start.4 = (bf16[136,512]{1,0:T(8,128)(2,1)S(1)}, bf16[136,512]{1,0:T(8,128)(2,1)S(1)}, u32[]{:S(2)}, u32[]{:S(2)}) collective-permute-start(bf16[136,512]{1,0:T(8,128)(2,1)S(1)} %collective-permute-done.2.pair_b_ref), channel_id=1, source_target_pairs={{0,8},{1,9},{2,10},{3,11},{4,12},{5,13},{6,14},{7,15},{8,0},{9,1},... | collective-permute-start | bytes 417800 | tf_op jit(solution)/shard_map/ppermute | solution.py:22
  12.3 1.6 %collective-permute-start.5 = (bf16[136,512]{1,0:T(8,128)(2,1)S(1)}, bf16[136,512]{1,0:T(8,128)(2,1)S(1)}, u32[]{:S(2)}, u32[]{:S(2)}) collective-permute-start(bf16[136,512]{1,0:T(8,128)(2,1)S(1)} %collective-permute-done.2.pair_b_ref), channel_id=1, source_target_pairs={{0,1},{1,0},{2,3},{3,2},{4,5},{5,4},{6,7},{7,6},{8,16},{9,17},{10,... | collective-permute-start | bytes 417800 | tf_op jit(solution)/shard_map/ppermute | solution.py:22
  13.9 1.5 %collective-permute-start.6 = (bf16[128,1024]{1,0:T(8,128)(2,1)S(1)}, bf16[128,1024]{1,0:T(8,128)(2,1)S(1)}, u32[]{:S(2)}, u32[]{:S(2)}) collective-permute-start(bf16[128,1024]{1,0:T(8,128)(2,1)S(1)} %get-tuple-element.50), channel_id=1, source_target_pairs={{0,4},{1,5},{2,6},{3,7},{4,0},{5,1},{6,2},{7,3},{8,12},{9,13},{10,... | collective-permute-start | bytes 786440 | tf_op jit(solution)/shard_map/ppermute | solution.py:22
  15.4 0.0 collective-permute-done.1.back_own_ref
  15.4 0.8 %collective-permute-done.3.refs_0_ = bf16[136,512]{1,0:T(8,128)(2,1)S(1)} collective-permute-done((bf16[136,512]{1,0:T(8,128)(2,1)S(1)}, bf16[136,512]{1,0:T(8,128)(2,1)S(1)}, u32[]{:S(2)}, u32[]{:S(2)}) %collective-permute-start.3) | collective-permute-done | bytes 139296 | tf_op jit(solution)/shard_map/ppermute | solution.py:22
  16.2 0.3 shard_map.75
  16.5 1.4 %collective-permute-start.8 = (bf16[136,512]{1,0:T(8,128)(2,1)S(1)}, bf16[136,512]{1,0:T(8,128)(2,1)S(1)}, u32[]{:S(2)}, u32[]{:S(2)}) collective-permute-start(bf16[136,512]{1,0:T(8,128)(2,1)S(1)} %get-tuple-element.52), channel_id=1, source_target_pairs={{0,1},{1,0},{2,3},{3,2},{4,5},{5,4},{6,7},{7,6},{8,16},{9,17},{10,... | collective-permute-start | bytes 417800 | tf_op jit(solution)/shard_map/ppermute | solution.py:22
  18.0 0.0 collective-permute-done.4.refs_0_
  18.0 1.8 %collective-permute-done.5.refs_1_ = bf16[136,512]{1,0:T(8,128)(2,1)S(1)} collective-permute-done((bf16[136,512]{1,0:T(8,128)(2,1)S(1)}, bf16[136,512]{1,0:T(8,128)(2,1)S(1)}, u32[]{:S(2)}, u32[]{:S(2)}) %collective-permute-start.5) | collective-permute-done | bytes 139296 | tf_op jit(solution)/shard_map/ppermute | solution.py:22
  19.8 0.4 shard_map.76
  20.1 0.8 %collective-permute-start.7 = (bf16[136,512]{1,0:T(8,128)(2,1)S(1)}, bf16[136,512]{1,0:T(8,128)(2,1)S(1)}, u32[]{:S(2)}, u32[]{:S(2)}) collective-permute-start(bf16[136,512]{1,0:T(8,128)(2,1)S(1)} %get-tuple-element.51), channel_id=1, source_target_pairs={{0,1},{1,0},{2,3},{3,2},{4,5},{5,4},{6,7},{7,6},{8,16},{9,17},{10,... | collective-permute-start | bytes 417800 | tf_op jit(solution)/shard_map/ppermute | solution.py:22
  20.9 0.0 copy-done.2
  20.9 1.0 %shard_map.77 = (f32[256,1024]{1,0:T(8,128)S(1)}, f32[128,1024]{1,0:T(8,128)S(1)}) custom-call(s32[1,32]{1,0:T(1,128)S(1)} %bitcast.14, f32[4,8,128]{2,1,0:T(8,128)S(1)} %get-tuple-element.38.marks_ref, bf16[8,2,128,768]{3,2,1,0:T(8,128)(2,1)S(1)} %get-tuple-element.37.table_ref, bf16[136,1024]{1,0:T(8,128)(2,1)S(1)} %get-tuple-element.32.own_ref, ...), custom_call_target="tpu_custom_call" | custom-call | flops 167772160 | bytes 2097152 | tf_op jit(solution)/shard_map/pallas_call | solution.py:502
  21.9 0.0 collective-permute-done.6.raw_ref
  21.9 0.4 %shard_map.78.qpair_ref = f32[128,1024]{1,0:T(8,128)S(1)} custom-call(s32[1,32]{1,0:T(1,128)S(1)} %bitcast.15, bf16[128,1024]{1,0:T(8,128)(2,1)S(1)} %collective-permute-done.6.raw_ref, bf16[136,1024]{1,0:T(8,128)(2,1)S(1)} %get-tuple-element.32.own_ref, bf16[136,1024]{1,0:T(8,128)(2,1)S(1)} %collective-permute-done.1.back_own_ref, ...), custom_call_target="tpu_custom_call" | custom-call | flops 1310720 | bytes 1048576 | tf_op jit(solution)/shard_map/pallas_call | solution.py:511
  22.3 0.4 %collective-permute-done.8.refs_0_ = bf16[136,512]{1,0:T(8,128)(2,1)S(1)} collective-permute-done((bf16[136,512]{1,0:T(8,128)(2,1)S(1)}, bf16[136,512]{1,0:T(8,128)(2,1)S(1)}, u32[]{:S(2)}, u32[]{:S(2)}) %collective-permute-start.8) | collective-permute-done | bytes 139296 | tf_op jit(solution)/shard_map/ppermute | solution.py:22
  22.7 0.4 %shard_map.79 = (f32[128,512]{1,0:T(8,128)S(1)}, bf16[128,512]{1,0:T(8,128)(2,1)S(1)}, f32[2,128,128]{2,1,0:T(8,128)S(1)}) custom-call(bf16[8,2,128,768]{3,2,1,0:T(8,128)(2,1)S(1)} %get-tuple-element.37.table_ref, f32[256,1024]{1,0:T(8,128)S(1)} %get-tuple-element.48.acc_ref, f32[128,1024]{1,0:T(8,128)S(1)} %get-tuple-element.49.qown_ref, ...), custom_call_target="tpu_custom_call" | custom-call | flops 100663296 | bytes 1572864 | tf_op jit(solution)/shard_map/pallas_call | solution.py:524
  23.1 3.0 %collective-permute-done.7.refs_0_ = bf16[136,512]{1,0:T(8,128)(2,1)S(1)} collective-permute-done((bf16[136,512]{1,0:T(8,128)(2,1)S(1)}, bf16[136,512]{1,0:T(8,128)(2,1)S(1)}, u32[]{:S(2)}, u32[]{:S(2)}) %collective-permute-start.7) | collective-permute-done | bytes 139296 | tf_op jit(solution)/shard_map/ppermute | solution.py:22
  26.1 0.5 %shard_map.80 = (f32[128,512]{1,0:T(8,128)S(1)}, bf16[128,1024]{1,0:T(8,128)(2,1)S(1)}, f32[1,256]{1,0:T(1,128)S(1)}) custom-call(bf16[8,2,128,768]{3,2,1,0:T(8,128)(2,1)S(1)} %get-tuple-element.37.table_ref, f32[256,1024]{1,0:T(8,128)S(1)} %get-tuple-element.48.acc_ref, f32[128,1024]{1,0:T(8,128)S(1)} %get-tuple-element.49.qown_ref, ...), custom_call_target="tpu_custom_call" | custom-call | flops 100663296 | bytes 1572864 | tf_op jit(solution)/shard_map/pallas_call | solution.py:524
  26.6 1.2 %collective-permute-start.13 = (bf16[128,1024]{1,0:T(8,128)(2,1)S(1)}, bf16[128,1024]{1,0:T(8,128)(2,1)S(1)}, u32[]{:S(2)}, u32[]{:S(2)}) collective-permute-start(bf16[128,1024]{1,0:T(8,128)(2,1)S(1)} %get-tuple-element.58), channel_id=1, source_target_pairs={{0,4},{1,5},{2,6},{3,7},{4,0},{5,1},{6,2},{7,3},{8,12},{9,13},{10,... | collective-permute-start | bytes 786440 | tf_op jit(solution)/shard_map/ppermute | solution.py:22
  27.8 0.0 collective-permute-start.11
  27.8 1.5 %collective-permute-start.10 = (f32[1,256]{1,0:T(1,128)S(1)}, f32[1,256]{1,0:T(1,128)S(1)}, u32[]{:S(2)}, u32[]{:S(2)}) collective-permute-start(f32[1,256]{1,0:T(1,128)S(1)} %get-tuple-element.55), channel_id=1, source_target_pairs={{0,2},{1,3},{2,0},{3,1},{4,6},{5,7},{6,4},{7,5},{8,10},{9,11},{10,... | collective-permute-start | bytes 3080 | tf_op jit(solution)/shard_map/ppermute | solution.py:540
  29.3 0.3 collective-permute-start.9
  29.7 1.1 %collective-permute-done.11 = f32[1,256]{1,0:T(1,128)S(1)} collective-permute-done((f32[1,256]{1,0:T(1,128)S(1)}, f32[1,256]{1,0:T(1,128)S(1)}, u32[]{:S(2)}, u32[]{:S(2)}) %collective-permute-start.11) | collective-permute-done | bytes 1056 | tf_op jit(solution)/shard_map/ppermute | solution.py:540
  30.8 0.6 %collective-permute-done.10 = f32[1,256]{1,0:T(1,128)S(1)} collective-permute-done((f32[1,256]{1,0:T(1,128)S(1)}, f32[1,256]{1,0:T(1,128)S(1)}, u32[]{:S(2)}, u32[]{:S(2)}) %collective-permute-start.10) | collective-permute-done | bytes 1056 | tf_op jit(solution)/shard_map/ppermute | solution.py:540
  31.4 0.0 collective-permute-done.9
  31.4 0.9 %collective-permute-start.12 = (f32[1,256]{1,0:T(1,128)S(1)}, f32[1,256]{1,0:T(1,128)S(1)}, u32[]{:S(2)}, u32[]{:S(2)}) collective-permute-start(f32[1,256]{1,0:T(1,128)S(1)} %add_add_fusion.power_ref), channel_id=1, source_target_pairs={{0,4},{1,5},{2,6},{3,7},{4,0},{5,1},{6,2},{7,3},{8,12},{9,13},{10,... | collective-permute-start | bytes 3080 | tf_op jit(solution)/shard_map/ppermute | solution.py:22
  32.4 2.7 %collective-permute-done.12.power_got_ref = f32[1,256]{1,0:T(1,128)S(1)} collective-permute-done((f32[1,256]{1,0:T(1,128)S(1)}, f32[1,256]{1,0:T(1,128)S(1)}, u32[]{:S(2)}, u32[]{:S(2)}) %collective-permute-start.12) | collective-permute-done | bytes 1056 | tf_op jit(solution)/shard_map/ppermute | solution.py:22
  35.1 0.0 collective-permute-done.13.refs_2_
  35.1 0.0 copy-done.3
  35.1 1.0 %shard_map.81 = bf16[128,2048]{1,0:T(8,128)(2,1)} custom-call(f32[1,256]{1,0:T(1,128)S(1)} %add_add_fusion.power_ref, f32[1,256]{1,0:T(1,128)S(1)} %collective-permute-done.12.power_got_ref, f32[128,512]{1,0:T(8,128)S(1)} %get-tuple-element.56.refs_0_, f32[128,512]{1,0:T(8,128)S(1)} %get-tuple-element.57.refs_1_, ...), custom_call_target="tpu_custom_call" | custom-call | flops 1048576 | bytes 1310720 | tf_op jit(solution)/shard_map/pallas_call | solution.py:542
  (7 shorter events, 0.0 us)
Async XLA Ops:
  0.0 6.1 %copy-start.1 = (s32[32]{0:T(128)S(1)}, s32[32]{0:T(128)}, u32[]{:S(2)}) copy-start(s32[32]{0:T(128)} %seq_ref.1) | copy-start | bytes 388
  0.0 6.1 %copy-start = (f32[3,3,2048]{2,1,0:T(4,128)S(1)}, f32[3,3,2048]{2,1,0:T(4,128)}, u32[]{:S(2)}) copy-start(f32[3,3,2048]{2,1,0:T(4,128)} %w_ref.1) | copy-start | bytes 221188
  0.0 6.1 %copy-start.4 = (f32[16,512]{1,0:T(8,128)S(1)}, f32[16,512]{1,0:T(8,128)}, u32[]{:S(2)}) copy-start(f32[16,512]{1,0:T(8,128)} %param.9) | copy-start | bytes 98308
  0.0 5.9 %copy-start.5 = (s32[16,4]{0,1:T(4,128)S(1)}, s32[16,4]{0,1:T(4,128)}, u32[]{:S(2)}) copy-start(s32[16,4]{0,1:T(4,128)} %param.10) | copy-start | bytes 772
  2.3 6.8 %collective-permute-start = (bf16[136,512]{1,0:T(8,128)(2,1)S(1)}, bf16[136,512]{1,0:T(8,128)(2,1)S(1)}, u32[]{:S(2)}, u32[]{:S(2)}) collective-permute-start(bf16[136,512]{1,0:T(8,128)(2,1)S(1)} %get-tuple-element.36), channel_id=1, source_target_pairs={{0,4},{1,5},{2,6},{3,7},{4,0},{5,1},{6,2},{7,3},{8,12},{9,13},{10,... | collective-permute-start | bytes 417800 | tf_op jit(solution)/shard_map/ppermute | solution.py:22
  3.8 11.6 %collective-permute-start.1 = (bf16[136,1024]{1,0:T(8,128)(2,1)S(1)}, bf16[136,1024]{1,0:T(8,128)(2,1)S(1)}, u32[]{:S(2)}, u32[]{:S(2)}) collective-permute-start(bf16[136,1024]{1,0:T(8,128)(2,1)S(1)} %get-tuple-element.32.own_ref), channel_id=1, source_target_pairs={{0,8},{1,9},{2,10},{3,11},{4,12},{5,13},{6,14},{7,15},{8,16},{9,17... | collective-permute-start | bytes 835592 | tf_op jit(solution)/shard_map/ppermute | solution.py:22
  5.4 6.3 %collective-permute-start.2 = (bf16[136,512]{1,0:T(8,128)(2,1)S(1)}, bf16[136,512]{1,0:T(8,128)(2,1)S(1)}, u32[]{:S(2)}, u32[]{:S(2)}) collective-permute-start(bf16[136,512]{1,0:T(8,128)(2,1)S(1)} %get-tuple-element.41), channel_id=1, source_target_pairs={{0,4},{1,5},{2,6},{3,7},{4,0},{5,1},{6,2},{7,3},{8,12},{9,13},{10,... | collective-permute-start | bytes 417800 | tf_op jit(solution)/shard_map/ppermute | solution.py:22
  9.0 11.9 %copy-start.2 = (f32[2048]{0:T(1024)S(1)}, f32[2048]{0:T(1024)}, u32[]{:S(2)}) copy-start(f32[2048]{0:T(1024)} %param.11) | copy-start | bytes 24580
  9.0 7.1 %collective-permute-start.3 = (bf16[136,512]{1,0:T(8,128)(2,1)S(1)}, bf16[136,512]{1,0:T(8,128)(2,1)S(1)}, u32[]{:S(2)}, u32[]{:S(2)}) collective-permute-start(bf16[136,512]{1,0:T(8,128)(2,1)S(1)} %collective-permute-done.pair_a_ref), channel_id=1, source_target_pairs={{0,8},{1,9},{2,10},{3,11},{4,12},{5,13},{6,14},{7,15},{8,16},{9,17... | collective-permute-start | bytes 417800 | tf_op jit(solution)/shard_map/ppermute | solution.py:22
  11.7 6.2 %collective-permute-start.4 = (bf16[136,512]{1,0:T(8,128)(2,1)S(1)}, bf16[136,512]{1,0:T(8,128)(2,1)S(1)}, u32[]{:S(2)}, u32[]{:S(2)}) collective-permute-start(bf16[136,512]{1,0:T(8,128)(2,1)S(1)} %collective-permute-done.2.pair_b_ref), channel_id=1, source_target_pairs={{0,8},{1,9},{2,10},{3,11},{4,12},{5,13},{6,14},{7,15},{8,0},{9,1},... | collective-permute-start | bytes 417800 | tf_op jit(solution)/shard_map/ppermute | solution.py:22
  12.3 7.5 %collective-permute-start.5 = (bf16[136,512]{1,0:T(8,128)(2,1)S(1)}, bf16[136,512]{1,0:T(8,128)(2,1)S(1)}, u32[]{:S(2)}, u32[]{:S(2)}) collective-permute-start(bf16[136,512]{1,0:T(8,128)(2,1)S(1)} %collective-permute-done.2.pair_b_ref), channel_id=1, source_target_pairs={{0,1},{1,0},{2,3},{3,2},{4,5},{5,4},{6,7},{7,6},{8,16},{9,17},{10,... | collective-permute-start | bytes 417800 | tf_op jit(solution)/shard_map/ppermute | solution.py:22
  13.9 8.1 %collective-permute-start.6 = (bf16[128,1024]{1,0:T(8,128)(2,1)S(1)}, bf16[128,1024]{1,0:T(8,128)(2,1)S(1)}, u32[]{:S(2)}, u32[]{:S(2)}) collective-permute-start(bf16[128,1024]{1,0:T(8,128)(2,1)S(1)} %get-tuple-element.50), channel_id=1, source_target_pairs={{0,4},{1,5},{2,6},{3,7},{4,0},{5,1},{6,2},{7,3},{8,12},{9,13},{10,... | collective-permute-start | bytes 786440 | tf_op jit(solution)/shard_map/ppermute | solution.py:22
  16.5 6.2 %collective-permute-start.8 = (bf16[136,512]{1,0:T(8,128)(2,1)S(1)}, bf16[136,512]{1,0:T(8,128)(2,1)S(1)}, u32[]{:S(2)}, u32[]{:S(2)}) collective-permute-start(bf16[136,512]{1,0:T(8,128)(2,1)S(1)} %get-tuple-element.52), channel_id=1, source_target_pairs={{0,1},{1,0},{2,3},{3,2},{4,5},{5,4},{6,7},{7,6},{8,16},{9,17},{10,... | collective-permute-start | bytes 417800 | tf_op jit(solution)/shard_map/ppermute | solution.py:22
  20.1 6.0 %collective-permute-start.7 = (bf16[136,512]{1,0:T(8,128)(2,1)S(1)}, bf16[136,512]{1,0:T(8,128)(2,1)S(1)}, u32[]{:S(2)}, u32[]{:S(2)}) collective-permute-start(bf16[136,512]{1,0:T(8,128)(2,1)S(1)} %get-tuple-element.51), channel_id=1, source_target_pairs={{0,1},{1,0},{2,3},{3,2},{4,5},{5,4},{6,7},{7,6},{8,16},{9,17},{10,... | collective-permute-start | bytes 417800 | tf_op jit(solution)/shard_map/ppermute | solution.py:22
  26.1 8.9 %copy-start.3 = (f32[2048]{0:T(1024)S(1)}, f32[2048]{0:T(1024)}, u32[]{:S(2)}) copy-start(f32[2048]{0:T(1024)} %param.12) | copy-start | bytes 24580
  26.6 8.5 %collective-permute-start.13 = (bf16[128,1024]{1,0:T(8,128)(2,1)S(1)}, bf16[128,1024]{1,0:T(8,128)(2,1)S(1)}, u32[]{:S(2)}, u32[]{:S(2)}) collective-permute-start(bf16[128,1024]{1,0:T(8,128)(2,1)S(1)} %get-tuple-element.58), channel_id=1, source_target_pairs={{0,4},{1,5},{2,6},{3,7},{4,0},{5,1},{6,2},{7,3},{8,12},{9,13},{10,... | collective-permute-start | bytes 786440 | tf_op jit(solution)/shard_map/ppermute | solution.py:22
  27.8 3.0 %collective-permute-start.11 = (f32[1,256]{1,0:T(1,128)S(1)}, f32[1,256]{1,0:T(1,128)S(1)}, u32[]{:S(2)}, u32[]{:S(2)}) collective-permute-start(f32[1,256]{1,0:T(1,128)S(1)} %get-tuple-element.55), channel_id=1, source_target_pairs={{0,3},{1,2},{2,1},{3,0},{4,7},{5,6},{6,5},{7,4},{8,11},{9,10},{10,... | collective-permute-start | bytes 3080 | tf_op jit(solution)/shard_map/ppermute | solution.py:540
  27.8 3.6 %collective-permute-start.10 = (f32[1,256]{1,0:T(1,128)S(1)}, f32[1,256]{1,0:T(1,128)S(1)}, u32[]{:S(2)}, u32[]{:S(2)}) collective-permute-start(f32[1,256]{1,0:T(1,128)S(1)} %get-tuple-element.55), channel_id=1, source_target_pairs={{0,2},{1,3},{2,0},{3,1},{4,6},{5,7},{6,4},{7,5},{8,10},{9,11},{10,... | collective-permute-start | bytes 3080 | tf_op jit(solution)/shard_map/ppermute | solution.py:540
  29.3 2.1 %collective-permute-start.9 = (f32[1,256]{1,0:T(1,128)S(1)}, f32[1,256]{1,0:T(1,128)S(1)}, u32[]{:S(2)}, u32[]{:S(2)}) collective-permute-start(f32[1,256]{1,0:T(1,128)S(1)} %get-tuple-element.55), channel_id=1, source_target_pairs={{0,1},{1,0},{2,3},{3,2},{4,5},{5,4},{6,7},{7,6},{8,9},{9,8},{10,11... | collective-permute-start | bytes 3080 | tf_op jit(solution)/shard_map/ppermute | solution.py:540
  31.4 3.6 %collective-permute-start.12 = (f32[1,256]{1,0:T(1,128)S(1)}, f32[1,256]{1,0:T(1,128)S(1)}, u32[]{:S(2)}, u32[]{:S(2)}) collective-permute-start(f32[1,256]{1,0:T(1,128)S(1)} %add_add_fusion.power_ref), channel_id=1, source_target_pairs={{0,4},{1,5},{2,6},{3,7},{4,0},{5,1},{6,2},{7,3},{8,12},{9,13},{10,... | collective-permute-start | bytes 3080 | tf_op jit(solution)/shard_map/ppermute | solution.py:22

commit v25 on v23

--- a/solution.py
+++ b/solution.py
@@ -466,10 +466,10 @@
     table, table_next, pair[0] = lax.optimization_barrier((table, table_next, pair[0]))
 
     half = lax.axis_index("half")
-    query, _ = lax.optimization_barrier((panels, pair[0]))
+    query, _ = lax.optimization_barrier((panels, kept))
     qkept = lax.dynamic_slice(query, (0, 0, half * width), (1, rows, width))[0]
     qsent = lax.dynamic_slice(query, (0, 0, (1 - half) * width), (1, rows, width))[0]
-    qkept, qsent, pair[1] = lax.optimization_barrier((qkept, qsent, pair[1]))
+    table_next, qkept, qsent = lax.optimization_barrier((table_next, qkept, qsent))
     qgot = moved(qsent, to_pair)
     back_pair = [[moved(pair[0], ahead)], [moved(pair[1], matching(blocks, first)) for first in (1, 0)]]
 

time: 35.9 us -> 36 us (level)
  the two profiles are of different devices: /device:TPU:8 before, /device:TPU:14 now
where the time goes in v25:
time: 36 us; the launch traced here: 35.9 us
  starting transfers between devices  14.4 us (40%)
  waiting for transfers between devices  11 us (31%)
  Pallas kernels  9.03 us (25%)
  local copies, waits for them, and re-layouts  1.25 us (3%)
    ppermute x11, starting transfers between devices, moved(): return lax.ppermute(block, SPOTS + ('mp',), whole)  12.6 us
    ppermute x11, waiting for transfers between devices, moved(): return lax.ppermute(block, SPOTS + ('mp',), whole)  9.25 us
    pallas_call x1, Pallas kernels, shards(): kernel_call(tables_kernel, (shape((groups, 2, BLK, span), jnp.bfloat16),...  2.85 us
    pallas_call x1, Pallas kernels, shards(): kernel_call(products_kernel, (message, small, small), [hbm] * 3, [pltpu.V...  2.24 us
    ppermute x3, starting transfers between devices, shards(): lax.ppermute(power, 'mp', [(i, i ^ k) for i in range(peers)])  1.86 us
    ppermute x3, waiting for transfers between devices, shards(): lax.ppermute(power, 'mp', [(i, i ^ k) for i in range(peers)])  1.74 us
    squeeze x1, local copies, waits for them, and re-layouts, shards(): lax.dynamic_slice(query, (0, 0, (1 - half) * width), (1, rows, width))[0]  1.06 us
    pallas_call x1, Pallas kernels, shards(): kernel_call(functools.partial(norm_kernel, channels), shape((rows, 2 * wi...  0.99 us
  transfers between devices with their start and end apart: 14, of which 8 were waited for; matrix products, arithmetic and copies ran while one was open for 3% of the time, Pallas kernels for 15%

profile of v25, /device:TPU:14, one launch (start us, length us, event | category | flops | bytes accessed | tf_op | source)
XLA Modules:
  0.0 35.9 jit_solution(17516123731568256)
XLA Ops:
  0.0 0.0 copy-start.5
  0.0 2.2 %shard_map.73 = (bf16[136,1024]{1,0:T(8,128)(2,1)S(1)}, bf16[136,512]{1,0:T(8,128)(2,1)S(1)}, bf16[136,512]{1,0:T(8,128)(2,1)S(1)}) custom-call(s32[1,32]{1,0:T(1,128)} %bitcast.13, bf16[3,128,2048]{2,1,0:T(8,128)(2,1)} %bitcast.18, f32[3,3,2048]{2,1,0:T(4,128)} %w_ref.1), custom_call_target="tpu_custom_call" | custom-call | flops 5242880 | bytes 2097152 | tf_op jit(solution)/shard_map/pallas_call | solution.py:429
  2.3 0.6 %collective-permute-start = (bf16[136,512]{1,0:T(8,128)(2,1)S(1)}, bf16[136,512]{1,0:T(8,128)(2,1)S(1)}, u32[]{:S(2)}, u32[]{:S(2)}) collective-permute-start(bf16[136,512]{1,0:T(8,128)(2,1)S(1)} %get-tuple-element.36), channel_id=1, source_target_pairs={{0,4},{1,5},{2,6},{3,7},{4,0},{5,1},{6,2},{7,3},{8,12},{9,13},{10,... | collective-permute-start | bytes 417800 | tf_op jit(solution)/shard_map/ppermute | solution.py:22
  2.8 1.6 %collective-permute-start.1 = (bf16[136,1024]{1,0:T(8,128)(2,1)S(1)}, bf16[136,1024]{1,0:T(8,128)(2,1)S(1)}, u32[]{:S(2)}, u32[]{:S(2)}) collective-permute-start(bf16[136,1024]{1,0:T(8,128)(2,1)S(1)} %get-tuple-element.32.own_ref), channel_id=1, source_target_pairs={{0,8},{1,9},{2,10},{3,11},{4,12},{5,13},{6,14},{7,15},{8,16},{9,17... | collective-permute-start | bytes 835592 | tf_op jit(solution)/shard_map/ppermute | solution.py:22
  4.4 1.5 %collective-permute-start.2 = (bf16[136,512]{1,0:T(8,128)(2,1)S(1)}, bf16[136,512]{1,0:T(8,128)(2,1)S(1)}, u32[]{:S(2)}, u32[]{:S(2)}) collective-permute-start(bf16[136,512]{1,0:T(8,128)(2,1)S(1)} %get-tuple-element.40), channel_id=1, source_target_pairs={{0,4},{1,5},{2,6},{3,7},{4,0},{5,1},{6,2},{7,3},{8,12},{9,13},{10,... | collective-permute-start | bytes 417800 | tf_op jit(solution)/shard_map/ppermute | solution.py:22
  5.9 0.0 copy-done.5
  5.9 0.1 copy.8
  6.0 0.1 broadcast_in_dim.3
  6.1 0.0 copy-done.4
  6.1 0.0 copy-done.1
  6.1 0.0 copy-done
  6.2 2.9 %shard_map.74 = (bf16[8,2,128,768]{3,2,1,0:T(8,128)(2,1)S(1)}, bf16[8,128,256]{2,1,0:T(8,128)(2,1)S(1)}, f32[3,3,1024]{2,1,0:T(4,128)S(1)}, f32[4,8,128]{2,1,0:T(8,128)S(1)}) custom-call(s32[32]{0:T(128)S(1)} %copy-done.1, bf16[16,512]{1,0:T(8,128)(2,1)S(1)} %fusion.taps_ref, f32[3,3,2048]{2,1,0:T(4,128)S(1)} %copy-done), custom_call_target="tpu_custom_call" | custom-call | flops 20971520 | bytes 4194304 | tf_op jit(solution)/shard_map/pallas_call | solution.py:453
  9.0 0.0 collective-permute-done.pair_a_ref
  9.0 0.0 copy-start.2
  9.0 1.6 %collective-permute-start.3 = (bf16[136,512]{1,0:T(8,128)(2,1)S(1)}, bf16[136,512]{1,0:T(8,128)(2,1)S(1)}, u32[]{:S(2)}, u32[]{:S(2)}) collective-permute-start(bf16[136,512]{1,0:T(8,128)(2,1)S(1)} %collective-permute-done.pair_a_ref), channel_id=1, source_target_pairs={{0,8},{1,9},{2,10},{3,11},{4,12},{5,13},{6,14},{7,15},{8,16},{9,17... | collective-permute-start | bytes 417800 | tf_op jit(solution)/shard_map/ppermute | solution.py:22
  10.7 0.1 collective-permute-done.2.pair_b_ref
  10.7 1.6 %collective-permute-start.4 = (bf16[136,512]{1,0:T(8,128)(2,1)S(1)}, bf16[136,512]{1,0:T(8,128)(2,1)S(1)}, u32[]{:S(2)}, u32[]{:S(2)}) collective-permute-start(bf16[136,512]{1,0:T(8,128)(2,1)S(1)} %collective-permute-done.2.pair_b_ref), channel_id=1, source_target_pairs={{0,1},{1,0},{2,3},{3,2},{4,5},{5,4},{6,7},{7,6},{8,16},{9,17},{10,... | collective-permute-start | bytes 417800 | tf_op jit(solution)/shard_map/ppermute | solution.py:22
  12.3 0.0 collective-permute-start.5
  12.3 1.1 %dynamic-slice_bitcast_fusion = (bf16[128,1024]{1,0:T(8,128)(2,1)S(1)}, bf16[128,1024]{1,0:T(8,128)(2,1)S(1)}) fusion(bf16[3,128,2048]{2,1,0:T(8,128)(2,1)} %bitcast.19, s32[]{:T(128)S(6)} %select_n.7, s32[]{:T(128)S(6)} %select_n.6), kind=kLoop, calls=%fused_computation | loop fusion | bytes 1048584 | tf_op jit(solution)/shard_map/squeeze | solution.py:471
  13.4 0.6 %collective-permute-start.6 = (bf16[128,1024]{1,0:T(8,128)(2,1)S(1)}, bf16[128,1024]{1,0:T(8,128)(2,1)S(1)}, u32[]{:S(2)}, u32[]{:S(2)}) collective-permute-start(bf16[128,1024]{1,0:T(8,128)(2,1)S(1)} %get-tuple-element.50), channel_id=1, source_target_pairs={{0,4},{1,5},{2,6},{3,7},{4,0},{5,1},{6,2},{7,3},{8,12},{9,13},{10,... | collective-permute-start | bytes 786440 | tf_op jit(solution)/shard_map/ppermute | solution.py:22
  13.9 0.0 collective-permute-done.1.back_own_ref
  13.9 0.8 %collective-permute-done.3.refs_0_ = bf16[136,512]{1,0:T(8,128)(2,1)S(1)} collective-permute-done((bf16[136,512]{1,0:T(8,128)(2,1)S(1)}, bf16[136,512]{1,0:T(8,128)(2,1)S(1)}, u32[]{:S(2)}, u32[]{:S(2)}) %collective-permute-start.3) | collective-permute-done | bytes 139296 | tf_op jit(solution)/shard_map/ppermute | solution.py:22
  14.7 0.3 shard_map.75
  15.1 2.1 %collective-permute-start.8 = (bf16[136,512]{1,0:T(8,128)(2,1)S(1)}, bf16[136,512]{1,0:T(8,128)(2,1)S(1)}, u32[]{:S(2)}, u32[]{:S(2)}) collective-permute-start(bf16[136,512]{1,0:T(8,128)(2,1)S(1)} %get-tuple-element.52), channel_id=1, source_target_pairs={{0,1},{1,0},{2,3},{3,2},{4,5},{5,4},{6,7},{7,6},{8,16},{9,17},{10,... | collective-permute-start | bytes 417800 | tf_op jit(solution)/shard_map/ppermute | solution.py:22
  17.2 1.2 %collective-permute-done.4.refs_0_ = bf16[136,512]{1,0:T(8,128)(2,1)S(1)} collective-permute-done((bf16[136,512]{1,0:T(8,128)(2,1)S(1)}, bf16[136,512]{1,0:T(8,128)(2,1)S(1)}, u32[]{:S(2)}, u32[]{:S(2)}) %collective-permute-start.4) | collective-permute-done | bytes 139296 | tf_op jit(solution)/shard_map/ppermute | solution.py:22
  18.5 0.0 collective-permute-done.5.refs_1_
  18.5 0.3 shard_map.76
  18.8 0.7 %collective-permute-start.7 = (bf16[136,512]{1,0:T(8,128)(2,1)S(1)}, bf16[136,512]{1,0:T(8,128)(2,1)S(1)}, u32[]{:S(2)}, u32[]{:S(2)}) collective-permute-start(bf16[136,512]{1,0:T(8,128)(2,1)S(1)} %get-tuple-element.51), channel_id=1, source_target_pairs={{0,1},{1,0},{2,3},{3,2},{4,5},{5,4},{6,7},{7,6},{8,16},{9,17},{10,... | collective-permute-start | bytes 417800 | tf_op jit(solution)/shard_map/ppermute | solution.py:22
  19.5 0.0 copy-done.2
  19.5 1.0 %shard_map.77 = (f32[256,1024]{1,0:T(8,128)S(1)}, f32[128,1024]{1,0:T(8,128)S(1)}) custom-call(s32[1,32]{1,0:T(1,128)S(1)} %bitcast.14, f32[4,8,128]{2,1,0:T(8,128)S(1)} %get-tuple-element.38.marks_ref, bf16[8,2,128,768]{3,2,1,0:T(8,128)(2,1)S(1)} %get-tuple-element.37.table_ref, bf16[136,1024]{1,0:T(8,128)(2,1)S(1)} %get-tuple-element.32.own_ref, ...), custom_call_target="tpu_custom_call" | custom-call | flops 167772160 | bytes 2097152 | tf_op jit(solution)/shard_map/pallas_call | solution.py:501
  20.5 0.2 collective-permute-done.6.raw_ref
  20.7 0.4 %shard_map.78.qpair_ref = f32[128,1024]{1,0:T(8,128)S(1)} custom-call(s32[1,32]{1,0:T(1,128)S(1)} %bitcast.15, bf16[128,1024]{1,0:T(8,128)(2,1)S(1)} %collective-permute-done.6.raw_ref, bf16[136,1024]{1,0:T(8,128)(2,1)S(1)} %get-tuple-element.32.own_ref, bf16[136,1024]{1,0:T(8,128)(2,1)S(1)} %collective-permute-done.1.back_own_ref, ...), custom_call_target="tpu_custom_call" | custom-call | flops 1310720 | bytes 1048576 | tf_op jit(solution)/shard_map/pallas_call | solution.py:510
  21.1 0.0 collective-permute-done.8.refs_0_
  21.1 0.4 %shard_map.79 = (f32[128,512]{1,0:T(8,128)S(1)}, bf16[128,512]{1,0:T(8,128)(2,1)S(1)}, f32[2,128,128]{2,1,0:T(8,128)S(1)}) custom-call(bf16[8,2,128,768]{3,2,1,0:T(8,128)(2,1)S(1)} %get-tuple-element.37.table_ref, f32[256,1024]{1,0:T(8,128)S(1)} %get-tuple-element.48.acc_ref, f32[128,1024]{1,0:T(8,128)S(1)} %get-tuple-element.49.qown_ref, ...), custom_call_target="tpu_custom_call" | custom-call | flops 100663296 | bytes 1572864 | tf_op jit(solution)/shard_map/pallas_call | solution.py:523
  21.6 3.5 %collective-permute-done.7.refs_0_ = bf16[136,512]{1,0:T(8,128)(2,1)S(1)} collective-permute-done((bf16[136,512]{1,0:T(8,128)(2,1)S(1)}, bf16[136,512]{1,0:T(8,128)(2,1)S(1)}, u32[]{:S(2)}, u32[]{:S(2)}) %collective-permute-start.7) | collective-permute-done | bytes 139296 | tf_op jit(solution)/shard_map/ppermute | solution.py:22
  25.1 0.5 %shard_map.80 = (f32[128,512]{1,0:T(8,128)S(1)}, bf16[128,1024]{1,0:T(8,128)(2,1)S(1)}, f32[1,256]{1,0:T(1,128)S(1)}) custom-call(bf16[8,2,128,768]{3,2,1,0:T(8,128)(2,1)S(1)} %get-tuple-element.37.table_ref, f32[256,1024]{1,0:T(8,128)S(1)} %get-tuple-element.48.acc_ref, f32[128,1024]{1,0:T(8,128)S(1)} %get-tuple-element.49.qown_ref, ...), custom_call_target="tpu_custom_call" | custom-call | flops 100663296 | bytes 1572864 | tf_op jit(solution)/shard_map/pallas_call | solution.py:523
  25.5 2.1 %collective-permute-start.13 = (bf16[128,1024]{1,0:T(8,128)(2,1)S(1)}, bf16[128,1024]{1,0:T(8,128)(2,1)S(1)}, u32[]{:S(2)}, u32[]{:S(2)}) collective-permute-start(bf16[128,1024]{1,0:T(8,128)(2,1)S(1)} %get-tuple-element.58), channel_id=1, source_target_pairs={{0,4},{1,5},{2,6},{3,7},{4,0},{5,1},{6,2},{7,3},{8,12},{9,13},{10,... | collective-permute-start | bytes 786440 | tf_op jit(solution)/shard_map/ppermute | solution.py:22
  27.6 0.0 collective-permute-start.11
  27.6 0.6 %collective-permute-start.10 = (f32[1,256]{1,0:T(1,128)S(1)}, f32[1,256]{1,0:T(1,128)S(1)}, u32[]{:S(2)}, u32[]{:S(2)}) collective-permute-start(f32[1,256]{1,0:T(1,128)S(1)} %get-tuple-element.55), channel_id=1, source_target_pairs={{0,2},{1,3},{2,0},{3,1},{4,6},{5,7},{6,4},{7,5},{8,10},{9,11},{10,... | collective-permute-start | bytes 3080 | tf_op jit(solution)/shard_map/ppermute | solution.py:539
  28.2 1.3 %collective-permute-start.9 = (f32[1,256]{1,0:T(1,128)S(1)}, f32[1,256]{1,0:T(1,128)S(1)}, u32[]{:S(2)}, u32[]{:S(2)}) collective-permute-start(f32[1,256]{1,0:T(1,128)S(1)} %get-tuple-element.55), channel_id=1, source_target_pairs={{0,1},{1,0},{2,3},{3,2},{4,5},{5,4},{6,7},{7,6},{8,9},{9,8},{10,11... | collective-permute-start | bytes 3080 | tf_op jit(solution)/shard_map/ppermute | solution.py:539
  29.5 1.1 %collective-permute-done.11 = f32[1,256]{1,0:T(1,128)S(1)} collective-permute-done((f32[1,256]{1,0:T(1,128)S(1)}, f32[1,256]{1,0:T(1,128)S(1)}, u32[]{:S(2)}, u32[]{:S(2)}) %collective-permute-start.11) | collective-permute-done | bytes 1056 | tf_op jit(solution)/shard_map/ppermute | solution.py:539
  30.6 0.6 %collective-permute-done.10 = f32[1,256]{1,0:T(1,128)S(1)} collective-permute-done((f32[1,256]{1,0:T(1,128)S(1)}, f32[1,256]{1,0:T(1,128)S(1)}, u32[]{:S(2)}, u32[]{:S(2)}) %collective-permute-start.10) | collective-permute-done | bytes 1056 | tf_op jit(solution)/shard_map/ppermute | solution.py:539
  31.2 0.0 collective-permute-done.9
  31.2 0.2 collective-permute-start.12
  31.4 3.4 %collective-permute-done.12.power_got_ref = f32[1,256]{1,0:T(1,128)S(1)} collective-permute-done((f32[1,256]{1,0:T(1,128)S(1)}, f32[1,256]{1,0:T(1,128)S(1)}, u32[]{:S(2)}, u32[]{:S(2)}) %collective-permute-start.12) | collective-permute-done | bytes 1056 | tf_op jit(solution)/shard_map/ppermute | solution.py:22
  34.9 0.0 collective-permute-done.13.refs_2_
  34.9 0.0 copy-done.3
  34.9 1.0 %shard_map.81 = bf16[128,2048]{1,0:T(8,128)(2,1)} custom-call(f32[1,256]{1,0:T(1,128)S(1)} %add_add_fusion.power_ref, f32[1,256]{1,0:T(1,128)S(1)} %collective-permute-done.12.power_got_ref, f32[128,512]{1,0:T(8,128)S(1)} %get-tuple-element.56.refs_0_, f32[128,512]{1,0:T(8,128)S(1)} %get-tuple-element.57.refs_1_, ...), custom_call_target="tpu_custom_call" | custom-call | flops 1048576 | bytes 1310720 | tf_op jit(solution)/shard_map/pallas_call | solution.py:541
  (7 shorter events, 0.0 us)
Async XLA Ops:
  0.0 6.1 %copy-start.1 = (s32[32]{0:T(128)S(1)}, s32[32]{0:T(128)}, u32[]{:S(2)}) copy-start(s32[32]{0:T(128)} %seq_ref.1) | copy-start | bytes 388
  0.0 6.1 %copy-start = (f32[3,3,2048]{2,1,0:T(4,128)S(1)}, f32[3,3,2048]{2,1,0:T(4,128)}, u32[]{:S(2)}) copy-start(f32[3,3,2048]{2,1,0:T(4,128)} %w_ref.1) | copy-start | bytes 221188
  0.0 6.1 %copy-start.4 = (f32[16,512]{1,0:T(8,128)S(1)}, f32[16,512]{1,0:T(8,128)}, u32[]{:S(2)}) copy-start(f32[16,512]{1,0:T(8,128)} %param.9) | copy-start | bytes 98308
  0.0 5.9 %copy-start.5 = (s32[16,4]{0,1:T(4,128)S(1)}, s32[16,4]{0,1:T(4,128)}, u32[]{:S(2)}) copy-start(s32[16,4]{0,1:T(4,128)} %param.10) | copy-start | bytes 772
  2.3 6.8 %collective-permute-start = (bf16[136,512]{1,0:T(8,128)(2,1)S(1)}, bf16[136,512]{1,0:T(8,128)(2,1)S(1)}, u32[]{:S(2)}, u32[]{:S(2)}) collective-permute-start(bf16[136,512]{1,0:T(8,128)(2,1)S(1)} %get-tuple-element.36), channel_id=1, source_target_pairs={{0,4},{1,5},{2,6},{3,7},{4,0},{5,1},{6,2},{7,3},{8,12},{9,13},{10,... | collective-permute-start | bytes 417800 | tf_op jit(solution)/shard_map/ppermute | solution.py:22
  2.8 11.1 %collective-permute-start.1 = (bf16[136,1024]{1,0:T(8,128)(2,1)S(1)}, bf16[136,1024]{1,0:T(8,128)(2,1)S(1)}, u32[]{:S(2)}, u32[]{:S(2)}) collective-permute-start(bf16[136,1024]{1,0:T(8,128)(2,1)S(1)} %get-tuple-element.32.own_ref), channel_id=1, source_target_pairs={{0,8},{1,9},{2,10},{3,11},{4,12},{5,13},{6,14},{7,15},{8,16},{9,17... | collective-permute-start | bytes 835592 | tf_op jit(solution)/shard_map/ppermute | solution.py:22
  4.4 6.3 %collective-permute-start.2 = (bf16[136,512]{1,0:T(8,128)(2,1)S(1)}, bf16[136,512]{1,0:T(8,128)(2,1)S(1)}, u32[]{:S(2)}, u32[]{:S(2)}) collective-permute-start(bf16[136,512]{1,0:T(8,128)(2,1)S(1)} %get-tuple-element.40), channel_id=1, source_target_pairs={{0,4},{1,5},{2,6},{3,7},{4,0},{5,1},{6,2},{7,3},{8,12},{9,13},{10,... | collective-permute-start | bytes 417800 | tf_op jit(solution)/shard_map/ppermute | solution.py:22
  9.0 10.5 %copy-start.2 = (f32[2048]{0:T(1024)S(1)}, f32[2048]{0:T(1024)}, u32[]{:S(2)}) copy-start(f32[2048]{0:T(1024)} %param.11) | copy-start | bytes 24580
  9.0 5.7 %collective-permute-start.3 = (bf16[136,512]{1,0:T(8,128)(2,1)S(1)}, bf16[136,512]{1,0:T(8,128)(2,1)S(1)}, u32[]{:S(2)}, u32[]{:S(2)}) collective-permute-start(bf16[136,512]{1,0:T(8,128)(2,1)S(1)} %collective-permute-done.pair_a_ref), channel_id=1, source_target_pairs={{0,8},{1,9},{2,10},{3,11},{4,12},{5,13},{6,14},{7,15},{8,16},{9,17... | collective-permute-start | bytes 417800 | tf_op jit(solution)/shard_map/ppermute | solution.py:22
  10.7 7.7 %collective-permute-start.4 = (bf16[136,512]{1,0:T(8,128)(2,1)S(1)}, bf16[136,512]{1,0:T(8,128)(2,1)S(1)}, u32[]{:S(2)}, u32[]{:S(2)}) collective-permute-start(bf16[136,512]{1,0:T(8,128)(2,1)S(1)} %collective-permute-done.2.pair_b_ref), channel_id=1, source_target_pairs={{0,1},{1,0},{2,3},{3,2},{4,5},{5,4},{6,7},{7,6},{8,16},{9,17},{10,... | collective-permute-start | bytes 417800 | tf_op jit(solution)/shard_map/ppermute | solution.py:22
  12.3 6.2 %collective-permute-start.5 = (bf16[136,512]{1,0:T(8,128)(2,1)S(1)}, bf16[136,512]{1,0:T(8,128)(2,1)S(1)}, u32[]{:S(2)}, u32[]{:S(2)}) collective-permute-start(bf16[136,512]{1,0:T(8,128)(2,1)S(1)} %collective-permute-done.2.pair_b_ref), channel_id=1, source_target_pairs={{0,8},{1,9},{2,10},{3,11},{4,12},{5,13},{6,14},{7,15},{8,0},{9,1},... | collective-permute-start | bytes 417800 | tf_op jit(solution)/shard_map/ppermute | solution.py:22
  13.4 7.4 %collective-permute-start.6 = (bf16[128,1024]{1,0:T(8,128)(2,1)S(1)}, bf16[128,1024]{1,0:T(8,128)(2,1)S(1)}, u32[]{:S(2)}, u32[]{:S(2)}) collective-permute-start(bf16[128,1024]{1,0:T(8,128)(2,1)S(1)} %get-tuple-element.50), channel_id=1, source_target_pairs={{0,4},{1,5},{2,6},{3,7},{4,0},{5,1},{6,2},{7,3},{8,12},{9,13},{10,... | collective-permute-start | bytes 786440 | tf_op jit(solution)/shard_map/ppermute | solution.py:22
  15.1 6.1 %collective-permute-start.8 = (bf16[136,512]{1,0:T(8,128)(2,1)S(1)}, bf16[136,512]{1,0:T(8,128)(2,1)S(1)}, u32[]{:S(2)}, u32[]{:S(2)}) collective-permute-start(bf16[136,512]{1,0:T(8,128)(2,1)S(1)} %get-tuple-element.52), channel_id=1, source_target_pairs={{0,1},{1,0},{2,3},{3,2},{4,5},{5,4},{6,7},{7,6},{8,16},{9,17},{10,... | collective-permute-start | bytes 417800 | tf_op jit(solution)/shard_map/ppermute | solution.py:22
  18.8 6.2 %collective-permute-start.7 = (bf16[136,512]{1,0:T(8,128)(2,1)S(1)}, bf16[136,512]{1,0:T(8,128)(2,1)S(1)}, u32[]{:S(2)}, u32[]{:S(2)}) collective-permute-start(bf16[136,512]{1,0:T(8,128)(2,1)S(1)} %get-tuple-element.51), channel_id=1, source_target_pairs={{0,1},{1,0},{2,3},{3,2},{4,5},{5,4},{6,7},{7,6},{8,16},{9,17},{10,... | collective-permute-start | bytes 417800 | tf_op jit(solution)/shard_map/ppermute | solution.py:22
  25.1 9.8 %copy-start.3 = (f32[2048]{0:T(1024)S(1)}, f32[2048]{0:T(1024)}, u32[]{:S(2)}) copy-start(f32[2048]{0:T(1024)} %param.12) | copy-start | bytes 24580
  25.5 9.3 %collective-permute-start.13 = (bf16[128,1024]{1,0:T(8,128)(2,1)S(1)}, bf16[128,1024]{1,0:T(8,128)(2,1)S(1)}, u32[]{:S(2)}, u32[]{:S(2)}) collective-permute-start(bf16[128,1024]{1,0:T(8,128)(2,1)S(1)} %get-tuple-element.58), channel_id=1, source_target_pairs={{0,4},{1,5},{2,6},{3,7},{4,0},{5,1},{6,2},{7,3},{8,12},{9,13},{10,... | collective-permute-start | bytes 786440 | tf_op jit(solution)/shard_map/ppermute | solution.py:22
  27.6 3.0 %collective-permute-start.11 = (f32[1,256]{1,0:T(1,128)S(1)}, f32[1,256]{1,0:T(1,128)S(1)}, u32[]{:S(2)}, u32[]{:S(2)}) collective-permute-start(f32[1,256]{1,0:T(1,128)S(1)} %get-tuple-element.55), channel_id=1, source_target_pairs={{0,3},{1,2},{2,1},{3,0},{4,7},{5,6},{6,5},{7,4},{8,11},{9,10},{10,... | collective-permute-start | bytes 3080 | tf_op jit(solution)/shard_map/ppermute | solution.py:539
  27.6 3.6 %collective-permute-start.10 = (f32[1,256]{1,0:T(1,128)S(1)}, f32[1,256]{1,0:T(1,128)S(1)}, u32[]{:S(2)}, u32[]{:S(2)}) collective-permute-start(f32[1,256]{1,0:T(1,128)S(1)} %get-tuple-element.55), channel_id=1, source_target_pairs={{0,2},{1,3},{2,0},{3,1},{4,6},{5,7},{6,4},{7,5},{8,10},{9,11},{10,... | collective-permute-start | bytes 3080 | tf_op jit(solution)/shard_map/ppermute | solution.py:539
  28.2 3.0 %collective-permute-start.9 = (f32[1,256]{1,0:T(1,128)S(1)}, f32[1,256]{1,0:T(1,128)S(1)}, u32[]{:S(2)}, u32[]{:S(2)}) collective-permute-start(f32[1,256]{1,0:T(1,128)S(1)} %get-tuple-element.55), channel_id=1, source_target_pairs={{0,1},{1,0},{2,3},{3,2},{4,5},{5,4},{6,7},{7,6},{8,9},{9,8},{10,11... | collective-permute-start | bytes 3080 | tf_op jit(solution)/shard_map/ppermute | solution.py:539
  31.2 3.6 %collective-permute-start.12 = (f32[1,256]{1,0:T(1,128)S(1)}, f32[1,256]{1,0:T(1,128)S(1)}, u32[]{:S(2)}, u32[]{:S(2)}) collective-permute-start(f32[1,256]{1,0:T(1,128)S(1)} %add_add_fusion.power_ref), channel_id=1, source_target_pairs={{0,4},{1,5},{2,6},{3,7},{4,0},{5,1},{6,2},{7,3},{8,12},{9,13},{10,... | collective-permute-start | bytes 3080 | tf_op jit(solution)/shard_map/ppermute | solution.py:22
